TPU v7x, 32 devices: a whole 2x2x4 slice. The times are simulated.
32 devices in a mesh: band: 2 (over x), feed: 16 (over z, y, core).
Axes of the slice: x: 2, y: 2, z: 4, core: 2. Of those that a mesh axis runs over, the one named last changes fastest.
Arguments:
- samples: int32 [8192, 16, 519], P(('band', 'feed')), parts along dimension 0, may hold values from 0 to 255
- gains: int32 [2, 32, 4096], P(None, 'band', 'feed'), parts along dimension 1, may hold values from -2048 to 2047
- feed_slot: int32 [4096], replicated, may hold values from 0 to 4095, each once
Outputs:
- visibility: float32 [8192, 2, 4096], P(('band', 'feed')), parts along dimension 0
There are 2 independent parts, one for each index of `band`. A program takes and returns all parts, laid end to end along the dimension named above; an argument that names none is the same for every part. Nothing has to cross between parts.
Inputs may be any that keep to these rules, and one draw needn't show every extreme that they name: `samples`: each word is 16 times the in-phase level plus the quadrature level, both offset by 8. `feed_slot`: every slot appears once.
All inputs are finite; a program needn't handle non-finite values.
Results may differ from a plain program's by a relative error of at most 0.0026.
Values may be sent and summed in bfloat16 or wider, within the bound.
No kernel may reach another device: no remote copies, remote signals or barrier semaphores. Data moves between devices by JAX's collectives and lax.ppermute only.
A program may use at most 128 MiB of HBM per device.

v0:
```python
import math

import jax
import jax.numpy as jnp
from jax import lax
from jax.sharding import PartitionSpec as P

CH = 16
TAPS = 8
SPECTRA = 512
ROWS = 256


def filter_taps():
    length = TAPS * CH
    place = jnp.arange(length).astype(jnp.float32)
    window = 0.5 - 0.5 * jnp.cos(2.0 * math.pi * place / (length - 1))
    return (jnp.sinc((place - 0.5 * (length - 1)) / CH) * window).reshape(TAPS, CH)


def dft_table():
    index = jnp.arange(CH, dtype=jnp.int32)
    phase = index[:, None] * index[None, :] % CH
    angle = phase.astype(jnp.float32) * (2.0 * math.pi / CH)
    cosine = jnp.cos(angle) / math.sqrt(CH)
    sine = jnp.sin(angle) / math.sqrt(CH)
    upper = jnp.stack([cosine, sine], axis=1)
    lower = jnp.stack([-sine, cosine], axis=1)
    return jnp.stack([upper, lower], axis=0)


def channelize(words, scales, blocks):
    inphase = (words // 16 - 8).astype(jnp.float32) * 0.125
    quadrature = (words % 16 - 8).astype(jnp.float32) * 0.125
    voltage = jnp.stack([inphase, quadrature], axis=1)
    taps = filter_taps()
    count = words.shape[2] - TAPS + 1
    filtered = taps[0][None, None, :, None] * voltage[:, :, :, 0:count]
    for tap in range(1, TAPS):
        filtered = filtered + taps[tap][None, None, :, None] * voltage[:, :, :, tap : tap + count]
    split = filtered.reshape(filtered.shape[0], 2, CH, blocks, count // blocks)
    channels = jnp.einsum("pcqk,nqkat->canpt", dft_table(), split, precision=lax.Precision.HIGHEST)
    gain = scales.astype(jnp.float32) * (1.0 / 2048.0)
    gain_real = gain[0][:, None, :, None]
    gain_imag = gain[1][:, None, :, None]
    real = channels[:, :, :, 0]
    imag = channels[:, :, :, 1]
    weighted = jnp.stack(
        [gain_real * real - gain_imag * imag, gain_real * imag + gain_imag * real], axis=3
    )
    return weighted.astype(jnp.bfloat16)


def sky_order(moved, feed_slot):
    flat = moved.reshape(moved.shape[1], moved.shape[2] * moved.shape[3])
    return jnp.take(flat, feed_slot, axis=0)[None]


def correlate(stacked, first):
    feed_rows = lax.dynamic_slice_in_dim(stacked, first, ROWS, 1)
    middle = stacked.shape[2] // 2
    turned = jnp.concatenate([feed_rows[:, :, middle:], -feed_rows[:, :, :middle]], axis=2)
    left_side = jnp.stack([feed_rows, turned], axis=2)
    return jnp.einsum("mrok,mjk->roj", left_side, stacked, preferred_element_type=jnp.float32)


def body(samples, gains, feed_slot):
    groups = lax.axis_size("feed") // CH
    position = lax.axis_index("feed")
    first = position % groups * ROWS
    spectra = channelize(samples, gains, 1)
    copies = jnp.broadcast_to(spectra, (CH, groups) + spectra.shape[2:])
    outgoing = copies.reshape((CH * groups,) + spectra.shape[2:])
    moved = lax.all_to_all(outgoing, "feed", split_axis=0, concat_axis=1, tiled=True)
    total = correlate(sky_order(moved, feed_slot), first)
    return total * (1.0 / SPECTRA)


def solution(mesh):
    return jax.shard_map(
        body,
        mesh=mesh,
        in_specs=(P(("band", "feed"), None, None), P(None, "band", "feed"), P()),
        out_specs=P(("band", "feed"), None, None),
        check_vma=False,
    )
```

profile of v0, /device:TPU:13, one launch (start us, length us, event | category | flops | bytes accessed | tf_op | source)
XLA Modules:
  0.0 385.7 jit_solution(17009220216554379644)
XLA Ops:
  0.0 0.1 sine_multiply_fusion
  0.1 0.1 fusion.58
  0.2 0.1 fusion.68
  0.3 14.5 %fusion.30 = (f32[256,1,16,519]{0,2,3,1:T(8,128)}, f32[256,1,16,519]{0,2,3,1:T(8,128)}) fusion(s32[256,16,519]{0,1,2:T(8,128)} %param.3), kind=kLoop, calls=%fused_computation.52 | loop fusion | flops 53145600 | bytes 25509888 | tf_op jit(solution)/shard_map/stack | solution.py:35
  14.8 49.6 %fusion.4 = f32[256,2,16,512,1]{0,2,3,1,4:T(8,128)} fusion(f32[256,1,16,519]{0,2,3,1:T(8,128)} %get-tuple-element.6, f32[256,1,16,519]{0,2,3,1:T(8,128)} %get-tuple-element.5, f32[16]{0:T(128)S(1)} %get-tuple-element.16, f32[16]{0:T(128)S(1)} %get-tuple-element.17, f32[16]{0:T(128)S(1)} %get-tuple-element.18, f32[16]{0:T(128)S(1)} %get-tuple-element.19, ...), kind=kLoop, calls=%fused_computation.19 | loop fusion | flops 96468992 | bytes 33784320 | tf_op jit(solution)/shard_map/add | solution.py:40
  64.3 0.0 copy-start.1
  64.3 20.3 %copy.33 = f32[256,2,16,512,1]{3,2,1,4,0:T(8,128)} copy(f32[256,2,16,512,1]{0,2,3,1,4:T(8,128)} %fusion.4) | data formatting | bytes 33554432 | tf_op jit(solution)/shard_map/add | solution.py:40
  84.6 0.0 copy-done.1
  84.6 0.1 copy.22
  84.7 0.1 copy.25
  84.9 19.7 %convolution_bitcast_fusion = f32[16,1,256,2,512]{4,0,3,2,1:T(8,128)S(1)} fusion(f32[256,2,16,512,1]{3,2,1,4,0:T(8,128)} %copy.33, f32[1,16,2,16]{3,1,2,0:T(8,128)S(1)} %get-tuple-element.14, f32[1,16,2,16]{3,1,2,0:T(8,128)S(1)} %get-tuple-element.13), kind=kOutput, calls=%fused_computation.44 | convolution fusion | flops 1610613760 | bytes 33558528 | tf_op jit(solution)/shard_map/pcqk,nqkat->canpt/dot_general | solution.py:42
  104.5 1.8 fusion.42
  106.3 3.6 fusion.43
  109.9 6.3 %pad_maximum_fusion.1 = bf16[16,256,2,512]{3,0,1,2:T(8,128)(2,1)} fusion(bf16[16,256,1,512]{3,0,1,2:T(8,128)(2,1)} %fusion.43, bf16[16,256,1,512]{3,0,1,2:T(8,128)(2,1)S(1)} %fusion.42), kind=kLoop, calls=%fused_computation.56 | loop fusion | flops 4194304 | bytes 16777216 | tf_op jit(solution)/shard_map/stack | solution.py:48
  116.2 11.4 %copy.29 = bf16[16,256,2,512]{3,1,2,0:T(8,128)(2,1)} copy(bf16[16,256,2,512]{3,0,1,2:T(8,128)(2,1)} %pad_maximum_fusion.1) | data formatting | bytes 16777216 | tf_op jit(solution)/shard_map/stack | solution.py:48
  127.6 0.0 copy-start
  127.6 6.7 %all-to-all-start = ((bf16[16,256,2,512]{3,1,2,0:T(8,128)(2,1)}), bf16[16,256,2,512]{3,1,2,0:T(8,128)(2,1)}, u32[]{:S(2)}, u32[]{:S(2)}) async-start(bf16[16,256,2,512]{3,1,2,0:T(8,128)(2,1)} %copy.29), calls=%async_computation | async-start | bytes 16777216 | tf_op jit(solution)/shard_map/all_to_all | solution.py:74
  134.3 0.0 copy-done
  134.3 182.3 %all-to-all-done = bf16[16,256,2,512]{3,1,2,0:T(8,128)(2,1)} async-done(((bf16[16,256,2,512]{3,1,2,0:T(8,128)(2,1)}), bf16[16,256,2,512]{3,1,2,0:T(8,128)(2,1)}, u32[]{:S(2)}, u32[]{:S(2)}) %all-to-all-start) | async-done | bytes 8388640 | tf_op jit(solution)/shard_map/all_to_all | solution.py:74
  316.6 16.2 %copy.37 = bf16[16,256,2,512]{3,2,1,0:T(2,128)(2,1)} copy(bf16[16,256,2,512]{3,1,2,0:T(8,128)(2,1)} %all-to-all-done) | data formatting | bytes 16777216 | tf_op jit(solution)/shard_map/reshape | solution.py:55
  332.9 9.3 %copy.40 = bf16[512,8,2,512]{3,1,2,0:T(8,128)(2,1)} copy(bf16[512,8,2,512]{3,2,1,0:T(2,128)(2,1)} %bitcast.85) | data formatting | bytes 16777216
  342.2 25.2 %gather_fusion = bf16[4096,1024]{1,0:T(8,128)(2,1)} fusion(bf16[4096,1024]{1,0:T(8,128)(2,1)} %bitcast.84, s32[4096]{0:T(1024)S(1)} %fusion.51), kind=kCustom, calls=%fused_computation | custom fusion | bytes 16793600 | tf_op jit(solution)/shard_map/jit(_take)/gather | solution.py:56
  367.4 1.2 fusion.47
  368.6 0.1 maximum_bitcast_fusion.2
  368.7 7.2 %fusion.38 = f32[256,2,4096]{2,0,1:T(8,128)S(1)} fusion(bf16[4096,1024]{1,0:T(8,128)(2,1)} %gather_fusion, pred[4096]{0:T(1024)(128)(4,1)S(1)} %compare_and_fusion, bf16[1,256,1,1024]{3,1,2,0:T(8,128)(2,1)S(1)} %maximum_bitcast_fusion.2, bf16[1,256,1,1024]{3,1,2,0:T(8,128)(2,1)S(1)} %get-tuple-element.7), kind=kOutput, calls=%fused_computation.67 | convolution fusion | flops 4301783040 | bytes 17829888 | tf_op jit(solution)/shard_map/mrok,mjk->roj/dot_general | solution.py:64
  375.9 9.8 %copy.32 = f32[256,2,4096]{2,1,0:T(2,128)} copy(f32[256,2,4096]{2,0,1:T(8,128)S(1)} %fusion.38) | data formatting | bytes 16777216 | tf_op jit(solution)/shard_map/mul | solution.py:76
  (8 shorter events, 0.1 us)
Async XLA Ops:
  64.3 20.3 %copy-start.1 = (s32[2,16,256]{2,1,0:T(8,128)S(1)}, s32[2,16,256]{2,1,0:T(8,128)}, u32[]{:S(2)}) copy-start(s32[2,16,256]{2,1,0:T(8,128)} %param.4) | copy-start | bytes 98308
  127.6 6.7 %copy-start = (s32[4096]{0:T(1024)S(1)}, s32[4096]{0:T(1024)}, u32[]{:S(2)}) copy-start(s32[4096]{0:T(1024)} %param.5) | copy-start | bytes 49156
  127.6 189.0 %all-to-all-start = ((bf16[16,256,2,512]{3,1,2,0:T(8,128)(2,1)}), bf16[16,256,2,512]{3,1,2,0:T(8,128)(2,1)}, u32[]{:S(2)}, u32[]{:S(2)}) async-start(bf16[16,256,2,512]{3,1,2,0:T(8,128)(2,1)} %copy.29), calls=%async_computation | async-start | bytes 16777216 | tf_op jit(solution)/shard_map/all_to_all | solution.py:74
where the time goes:
time: 387 us; the launch traced here: 386 us
  waiting for transfers between devices  182 us (47%)
  local copies, waits for them, and re-layouts  92.5 us (24%)
  other arithmetic  77.2 us (20%)
  matrix products  26.9 us (7%)
  starting transfers between devices  6.69 us (2%)
    all_to_all x1, waiting for transfers between devices, body(): lax.all_to_all(outgoing, 'feed', split_axis=0, concat_axis=1, tiled=True)  182 us
    add x1, other arithmetic, channelize(): filtered + taps[tap][None, None, :, None] * voltage[:, :, :, tap:tap + co...  49.6 us
    gather x1, local copies, waits for them, and re-layouts, sky_order(): return jnp.take(flat, feed_slot, axis=0)[None]  25.2 us
    add x1, local copies, waits for them, and re-layouts, channelize(): filtered + taps[tap][None, None, :, None] * voltage[:, :, :, tap:tap + co...  20.3 us
    dot_general x1, matrix products, channelize(): jnp.einsum('pcqk,nqkat->canpt', dft_table(), split, precision=lax.Precisi...  19.7 us
    reshape x1, local copies, waits for them, and re-layouts, sky_order(): flat = moved.reshape(moved.shape[1], moved.shape[2] * moved.shape[3])  16.2 us
    another operation x1, other arithmetic, channelize(): voltage = jnp.stack([inphase, quadrature], axis=1)  14.5 us
    another operation x3, other arithmetic, channelize(): jnp.stack([gain_real * real - gain_imag * imag, gain_real * imag + gain_i...  11.7 us
  transfers between devices with their start and end apart: 1, of which 1 were waited for; matrix products, arithmetic and copies ran while one was open for 0% of the time, Pallas kernels for 0%

commit v1 on v0

v1 whole, which is shorter than its diff:
```python
import functools
import math

import jax
import jax.numpy as jnp
import numpy as np
from jax import lax
from jax.experimental import pallas as pl
from jax.experimental.pallas import tpu as pltpu
from jax.sharding import PartitionSpec as P

TAPS = 8
ROWS = 256
LANES = 128


def filter_taps(ch):
    length = TAPS * ch
    place = np.arange(length, dtype=np.float64)
    window = 0.5 - 0.5 * np.cos(2.0 * math.pi * place / (length - 1))
    return (np.sinc((place - 0.5 * (length - 1)) / ch) * window).reshape(TAPS, ch)


def twiddle(value, turn):
    real, imag = value
    if turn == 0:
        return value
    if turn == 0.25:
        return imag, -real
    half = math.sqrt(0.5)
    if turn == 0.125:
        return half * (real + imag), half * (imag - real)
    if turn == 0.375:
        return half * (imag - real), -half * (real + imag)
    c, s = math.cos(2.0 * math.pi * turn), math.sin(2.0 * math.pi * turn)
    return c * real + s * imag, c * imag - s * real


def fft(values):
    count = len(values)
    if count == 1:
        return values
    even, odd = fft(values[0::2]), fft(values[1::2])
    low, high = [], []
    for index in range(count // 2):
        real, imag = twiddle(odd[index], index / count)
        low.append((even[index][0] + real, even[index][1] + imag))
        high.append((even[index][0] - real, even[index][1] - imag))
    return low + high


def channel_kernel(taps, *refs):
    *samples_refs, gains_ref, out_ref, filtered = refs
    ch, block, width = out_ref.shape
    spectra = width // 2
    padded = len(samples_refs) * LANES
    for k in range(ch):
        words = jnp.concatenate(
            [ref[pl.ds(k, block, stride=ch), :] for ref in samples_refs], axis=1
        )
        levels = ((words >> 4) - 8, (words & 15) - 8)
        for part in range(2):
            value = levels[part].astype(jnp.float32)
            shifted = [value] + [pltpu.roll(value, padded - t, 1) for t in range(1, TAPS // 2)]
            near = float(taps[0, k]) * shifted[0]
            far = float(taps[TAPS // 2, k]) * shifted[0]
            for t in range(1, TAPS // 2):
                near = near + float(taps[t, k]) * shifted[t]
                far = far + float(taps[t + TAPS // 2, k]) * shifted[t]
            total = near + pltpu.roll(far, padded - TAPS // 2, 1)
            filtered[2 * k + part] = total[:, :spectra]
    for row in range(0, block, 8):
        gains = gains_ref[row : row + 8, :]
        for lane in range(0, spectra, LANES):
            spot = (slice(row, row + 8), slice(lane, lane + LANES))
            values = [(filtered[2 * k][spot], filtered[2 * k + 1][spot]) for k in range(ch)]
            for c, (real, imag) in enumerate(fft(values)):
                gain_real = gains[:, c : c + 1]
                gain_imag = gains[:, ch + c : ch + c + 1]
                out_ref[c, row : row + 8, lane : lane + LANES] = (
                    gain_real * real - gain_imag * imag
                ).astype(out_ref.dtype)
                out_ref[c, row : row + 8, spectra + lane : spectra + lane + LANES] = (
                    gain_real * imag + gain_imag * real
                ).astype(out_ref.dtype)


def channelize(samples, gains):
    count, ch, frames = samples.shape
    spectra = frames - TAPS + 1
    block = 16
    pieces = pl.cdiv(frames, LANES)
    scale = 0.125 / math.sqrt(ch) / 2048.0
    taps = (filter_taps(ch) * scale).astype(np.float32)
    return pl.pallas_call(
        functools.partial(channel_kernel, taps),
        grid=(count // block,),
        in_specs=[
            pl.BlockSpec((block * ch, LANES), functools.partial(lambda piece, i: (i, piece), piece))
            for piece in range(pieces)
        ]
        + [pl.BlockSpec((block, 2 * ch), lambda i: (i, 0))],
        out_specs=pl.BlockSpec((ch, block, 2 * spectra), lambda i: (0, i, 0)),
        out_shape=jax.ShapeDtypeStruct((ch, count, 2 * spectra), jnp.bfloat16),
        scratch_shapes=[pltpu.VMEM((2 * ch, block, spectra), jnp.float32)],
        compiler_params=pltpu.CompilerParams(vmem_limit_bytes=32 << 20),
        name="channelize",
    )(*[samples.reshape(count * ch, frames)] * pieces, gains)


def correlate_kernel(scale, slot_ref, row_ref, data_ref, out_ref, products, tile):
    feeds, width = data_ref.shape
    spectra = width // 2
    rows = row_ref.shape[0]
    pieces = 2 * rows // LANES
    step = 256
    picked = jnp.zeros((rows, width), jnp.float32)
    for first in range(0, feeds, 512):
        place = lax.broadcasted_iota(jnp.int32, (rows, 512), 1) + first
        choice = jnp.where(row_ref[...] == place, 1.0, 0.0).astype(jnp.bfloat16)
        picked = picked + jnp.dot(
            choice, data_ref[first : first + 512, :], preferred_element_type=jnp.float32
        )
    left = jnp.concatenate(
        [
            picked,
            jnp.concatenate([picked[:, spectra:], -picked[:, :spectra]], axis=1),
        ],
        axis=0,
    ).astype(jnp.bfloat16)

    @pl.loop(0, feeds // step)
    def _(i):
        first = pl.multiple_of(i * step, step)
        result = lax.dot_general(
            data_ref[pl.ds(first, step), :],
            left,
            (((1,), (1,)), ((), ())),
            preferred_element_type=jnp.float32,
        )
        for piece in range(pieces):
            products[pl.ds(first * pieces + piece, step, stride=pieces), :] = (
                result[:, piece * LANES : (piece + 1) * LANES] * scale
            )

    lines = 2 * (feeds // LANES)

    @pl.loop(0, feeds // LANES)
    def _(j):
        @pl.loop(0, LANES, unroll=16)
        def _(i):
            slot = slot_ref[j * LANES + i]
            tile[pl.ds(pl.multiple_of(i * pieces, pieces), pieces), :] = products[
                pl.ds(pl.multiple_of(slot * pieces, pieces), pieces), :
            ]

        for piece in range(pieces):
            part, first = divmod(piece * LANES, rows)
            turned = tile[pl.ds(piece, LANES, stride=pieces), :].T
            out_ref[pl.ds(first * lines + 2 * j + part, LANES, stride=lines), :] = turned


def correlate(data, feed_slot, first, rows):
    feeds, width = data.shape
    row_slots = lax.dynamic_slice_in_dim(feed_slot, first, rows, 0).reshape(rows, 1)
    lines = 2 * (feeds // LANES)
    out = pl.pallas_call(
        functools.partial(correlate_kernel, 2.0 / width),
        in_specs=[
            pl.BlockSpec(memory_space=pltpu.SMEM),
            pl.BlockSpec(memory_space=pltpu.VMEM),
            pl.BlockSpec(memory_space=pltpu.VMEM),
        ],
        out_specs=pl.BlockSpec(memory_space=pltpu.VMEM),
        out_shape=jax.ShapeDtypeStruct((rows * lines, LANES), jnp.float32),
        scratch_shapes=[
            pltpu.VMEM((feeds * 2 * rows // LANES, LANES), jnp.float32),
            pltpu.VMEM((LANES * 2 * rows // LANES, LANES), jnp.float32),
        ],
        compiler_params=pltpu.CompilerParams(vmem_limit_bytes=48 << 20),
        name="correlate",
    )(feed_slot, row_slots, data)
    out = out.reshape(rows, feeds // LANES, 2, LANES)
    return jnp.transpose(out, (0, 2, 1, 3)).reshape(rows, 2, feeds)


def body(samples, gains, feed_slot):
    count, ch, _ = samples.shape
    groups = lax.axis_size("feed") // ch
    first = lax.axis_index("feed") % groups * ROWS
    scales = jnp.transpose(gains, (2, 0, 1)).reshape(count, 2 * ch).astype(jnp.float32)
    spectra = channelize(samples, scales)
    width = spectra.shape[2]
    outgoing = jnp.broadcast_to(spectra[:, None], (ch, groups, count, width))
    outgoing = outgoing.reshape(ch * groups, count, width)
    moved = lax.all_to_all(outgoing, "feed", split_axis=0, concat_axis=0, tiled=True)
    return correlate(moved.reshape(-1, width), feed_slot, first, ROWS)


def solution(mesh):
    return jax.shard_map(
        body,
        mesh=mesh,
        in_specs=(P(("band", "feed"), None, None), P(None, "band", "feed"), P()),
        out_specs=P(("band", "feed"), None, None),
        check_vma=False,
    )
```

time: 387 us -> 302 us (0.78)
  Pallas kernels: 0 us -> 93.3 us
  other arithmetic: 77.2 us -> 0.01 us
  local copies, waits for them, and re-layouts: 92.5 us -> 19.8 us
  matrix products: 26.9 us -> 0 us
    pallas_call x0 -> x2, Pallas kernels: none -> 93.3 us  [the longest x1 59.4 us: channelize(): pl.pallas_call(functools.partial(channel_kernel, taps), grid=(count // bl...]
    add x1 -> x0, other arithmetic: 49.6 us -> none  [channelize(): filtered + taps[tap][None, None, :, None] * voltage[:, :, :, tap:tap + co...]
    another operation x7 -> x0, other arithmetic: 27.4 us -> none  [the longest x1 14.5 us: channelize(): voltage = jnp.stack([inphase, quadrature], axis=1)]
    dot_general x2 -> x0, matrix products: 26.9 us -> none  [the longest x1 19.7 us: channelize(): jnp.einsum('pcqk,nqkat->canpt', dft_table(), split, precision=lax.Precisi...]
    gather x1 -> x0, local copies, waits for them, and re-layouts: 25.2 us -> none  [sky_order(): return jnp.take(flat, feed_slot, axis=0)[None]]
    add x1 -> x0, local copies, waits for them, and re-layouts: 20.3 us -> none  [channelize(): filtered + taps[tap][None, None, :, None] * voltage[:, :, :, tap:tap + co...]
    reshape x1, local copies, waits for them, and re-layouts: 16.2 us -> 0.13 us  [correlate(): lax.dynamic_slice_in_dim(feed_slot, first, rows, 0).reshape(rows, 1)]
    another operation x2 -> x0, local copies, waits for them, and re-layouts: 11.4 us -> none  [the longest x1 11.4 us: channelize(): jnp.stack([gain_real * real - gain_imag * imag, gain_real * imag + gain_i...]
where the time goes in v1:
time: 302 us
  waiting for transfers between devices  182 us (60%)
  Pallas kernels  93.3 us (31%)
  local copies, waits for them, and re-layouts  19.8 us (7%)
  starting transfers between devices  6.69 us (2%)
    all_to_all x1, waiting for transfers between devices, body(): lax.all_to_all(outgoing, 'feed', split_axis=0, concat_axis=0, tiled=True)  182 us
    pallas_call x1, Pallas kernels, channelize(): pl.pallas_call(functools.partial(channel_kernel, taps), grid=(count // bl...  59.4 us
    pallas_call x1, Pallas kernels, correlate(): pl.pallas_call(functools.partial(correlate_kernel, 2.0 / width), in_specs...  33.8 us
    unnamed x9, local copies, waits for them, and re-layouts  19.5 us
    all_to_all x1, starting transfers between devices, body(): lax.all_to_all(outgoing, 'feed', split_axis=0, concat_axis=0, tiled=True)  6.69 us
  transfers between devices with their start and end apart: 1, of which 1 were waited for; matrix products, arithmetic and copies ran while one was open for 0% of the time, Pallas kernels for 0%

profile of v1, /device:TPU:13, one launch (start us, length us, event | category | flops | bytes accessed | tf_op | source)
XLA Modules:
  0.0 302.0 jit_solution(7164842034655441613)
XLA Ops:
  0.0 0.0 copy-start.3
  0.0 12.1 %copy.7 = s32[256,16,519]{2,1,0:T(8,128)} copy(s32[256,16,519]{0,1,2:T(8,128)} %param.3) | data formatting | bytes 17006592 | tf_op args[0]
  12.1 0.0 copy-done.3
  12.2 0.1 copy.8.refs_5_
  12.3 0.0 copy-start
  12.3 4.0 %copy-done = s32[256,16,519]{2,1,0:T(8,128)S(1)} copy-done((s32[256,16,519]{2,1,0:T(8,128)S(1)}, s32[256,16,519]{2,1,0:T(8,128)}, u32[]{:S(2)}) %copy-start) | copy-done | bytes 8503320
  16.2 59.4 %channelize.1 = bf16[16,256,1024]{2,1,0:T(8,128)(2,1)S(1)} custom-call(s32[4096,519]{1,0:T(8,128)S(1)} %bitcast.11, s32[4096,519]{1,0:T(8,128)S(1)} %bitcast.12, s32[4096,519]{1,0:T(8,128)S(1)} %bitcast.13, s32[4096,519]{1,0:T(8,128)S(1)} %bitcast.14, s32[4096,519]{1,0:T(8,128)S(1)} %bitcast.15, f32[256,32]{1,0:T(8,128)S(1)} %copy.8.refs_5_), custom_call_target="tpu_custom_call" | custom-call | tf_op jit(solution)/shard_map/channelize/pallas_call | solution.py:95
  75.7 0.0 copy-start.1
  75.7 3.4 %copy-done.1 = bf16[16,256,1024]{2,1,0:T(8,128)(2,1)} copy-done((bf16[16,256,1024]{2,1,0:T(8,128)(2,1)}, bf16[16,256,1024]{2,1,0:T(8,128)(2,1)S(1)}, u32[]{:S(2)}) %copy-start.1) | copy-done | bytes 8388632
  79.1 0.0 slice-start
  79.1 0.0 copy-start.2
  79.1 6.7 %all-to-all-start = ((bf16[16,256,1024]{2,1,0:T(8,128)(2,1)}), bf16[16,256,1024]{2,1,0:T(8,128)(2,1)}, u32[]{:S(2)}, u32[]{:S(2)}) async-start(bf16[16,256,1024]{2,1,0:T(8,128)(2,1)} %copy-done.1), calls=%async_computation | async-start | bytes 16777216 | tf_op jit(solution)/shard_map/all_to_all | solution.py:196
  85.8 0.0 slice-done
  85.8 0.1 copy.9.row_ref
  85.9 182.2 %all-to-all-done = bf16[16,256,1024]{2,1,0:T(8,128)(2,1)} async-done(((bf16[16,256,1024]{2,1,0:T(8,128)(2,1)}), bf16[16,256,1024]{2,1,0:T(8,128)(2,1)}, u32[]{:S(2)}, u32[]{:S(2)}) %all-to-all-start) | async-done | bytes 8388640 | tf_op jit(solution)/shard_map/all_to_all | solution.py:196
  268.1 0.0 copy-done.2
  268.1 33.8 %correlate.1 = f32[16384,128]{1,0:T(8,128)} custom-call(s32[4096]{0:T(1024)S(1)} %copy-done.2, s32[256,1]{1,0:T(8,128)S(1)} %copy.9.row_ref, bf16[4096,1024]{1,0:T(8,128)(2,1)} %bitcast.4.data_ref), custom_call_target="tpu_custom_call" | custom-call | tf_op jit(solution)/shard_map/correlate/pallas_call | solution.py:167
  (1 shorter events, 0.0 us)
Async XLA Ops:
  0.0 12.1 %copy-start.3 = (s32[2,16,256]{2,1,0:T(8,128)S(1)}, s32[2,16,256]{2,1,0:T(8,128)}, u32[]{:S(2)}) copy-start(s32[2,16,256]{2,1,0:T(8,128)} %param.4) | copy-start | bytes 98308
  12.3 4.0 %copy-start = (s32[256,16,519]{2,1,0:T(8,128)S(1)}, s32[256,16,519]{2,1,0:T(8,128)}, u32[]{:S(2)}) copy-start(s32[256,16,519]{2,1,0:T(8,128)} %copy.7) | copy-start | bytes 25509892
  75.7 3.4 %copy-start.1 = (bf16[16,256,1024]{2,1,0:T(8,128)(2,1)}, bf16[16,256,1024]{2,1,0:T(8,128)(2,1)S(1)}, u32[]{:S(2)}) copy-start(bf16[16,256,1024]{2,1,0:T(8,128)(2,1)S(1)} %channelize.1) | copy-start | bytes 25165828
  79.1 6.7 %slice-start = ((s32[4096]{0:T(1024)}), s32[256]{0:T(256)S(1)}, s32[]{:S(2)}) async-start(s32[4096]{0:T(1024)} %slot_ref.1), calls=%async_computation.1 | async-start | bytes 2048 | tf_op jit(solution)/shard_map/dynamic_slice | solution.py:165
  79.1 189.0 %copy-start.2 = (s32[4096]{0:T(1024)S(1)}, s32[4096]{0:T(1024)}, u32[]{:S(2)}) copy-start(s32[4096]{0:T(1024)} %slot_ref.1) | copy-start | bytes 49156
  79.1 189.0 %all-to-all-start = ((bf16[16,256,1024]{2,1,0:T(8,128)(2,1)}), bf16[16,256,1024]{2,1,0:T(8,128)(2,1)}, u32[]{:S(2)}, u32[]{:S(2)}) async-start(bf16[16,256,1024]{2,1,0:T(8,128)(2,1)} %copy-done.1), calls=%async_computation | async-start | bytes 16777216 | tf_op jit(solution)/shard_map/all_to_all | solution.py:196

commit v2 on v1

--- a/solution.py
+++ b/solution.py
@@ -184,7 +184,7 @@
     return jnp.transpose(out, (0, 2, 1, 3)).reshape(rows, 2, feeds)
 
 
-def body(samples, gains, feed_slot):
+def through_spectra(samples, gains, feed_slot):
     count, ch, _ = samples.shape
     groups = lax.axis_size("feed") // ch
     first = lax.axis_index("feed") % groups * ROWS
@@ -197,6 +197,311 @@
     return correlate(moved.reshape(-1, width), feed_slot, first, ROWS)
 
 
+STEP = 8
+SPAN = 16
+STEPS = 8
+RANGE = 14
+
+
+def filter_weights(ch):
+    taps = filter_taps(ch) * (0.125 / math.sqrt(ch) / 2048.0)
+    weights = np.zeros((ch, 2, STEP, 2, SPAN, ch))
+    angle = 2.0 * math.pi * (np.arange(ch)[:, None] * np.arange(ch)[None, :] % ch) / ch
+    for spectrum in range(STEP):
+        for t in range(TAPS):
+            cosine, sine = taps[t] * np.cos(angle), taps[t] * np.sin(angle)
+            weights[:, 0, spectrum, 0, spectrum + t] = cosine
+            weights[:, 0, spectrum, 1, spectrum + t] = sine
+            weights[:, 1, spectrum, 0, spectrum + t] = -sine
+            weights[:, 1, spectrum, 1, spectrum + t] = cosine
+    weights = weights.reshape(ch * 2 * STEP, 2, SPAN * ch)
+    high = weights.astype(jnp.bfloat16)
+    low = (weights - high.astype(np.float64)).astype(jnp.bfloat16)
+    return np.stack([high[:, 0], high[:, 1], low[:, 0], low[:, 1]])
+
+
+def spectra_of(weights_ref, levels, gains, ch, store):
+    count = levels[0].shape[1]
+    for b in range(STEPS):
+        spot = slice(b * STEP * ch, b * STEP * ch + SPAN * ch)
+        total = None
+        for part in range(2):
+            slab = levels[part][spot]
+            for split in range(2):
+                term = jnp.dot(weights_ref[2 * split + part], slab, preferred_element_type=jnp.float32)
+                total = term if total is None else total + term
+        for c in range(ch):
+            real = total[c * 2 * STEP : c * 2 * STEP + STEP]
+            imag = total[c * 2 * STEP + STEP : (c + 1) * 2 * STEP]
+            gain_real, gain_imag = gains[c : c + 1], gains[ch + c : ch + c + 1]
+            store(b, c, gain_real * real - gain_imag * imag, gain_real * imag + gain_imag * real)
+
+
+def levels_of(words):
+    return [
+        ((words >> 4) - 8).astype(jnp.float32).astype(jnp.bfloat16),
+        ((words & 15) - 8).astype(jnp.float32).astype(jnp.bfloat16),
+    ]
+
+
+def own_kernel(main_ref, next_ref, gains_ref, weights_ref, out_ref):
+    ch = out_ref.shape[0]
+    words = jnp.concatenate([main_ref[...], next_ref[...]], axis=0)
+
+    def store(b, c, real, imag):
+        out_ref[c, b * 2 * STEP : (b + 1) * 2 * STEP, :] = jnp.concatenate([real, imag], axis=0).astype(
+            out_ref.dtype
+        )
+
+    spectra_of(weights_ref, levels_of(words), gains_ref[...], ch, store)
+
+
+def own_spectra(words, gains, weights, ch, spectra):
+    count = words.shape[1]
+    main = STEPS * STEP * ch
+    return pl.pallas_call(
+        own_kernel,
+        grid=(spectra // (STEPS * STEP),),
+        in_specs=[
+            pl.BlockSpec((main, count), lambda i: (i, 0)),
+            pl.BlockSpec((STEP * ch, count), lambda i: ((i + 1) * STEPS, 0)),
+            pl.BlockSpec(gains.shape, lambda i: (0, 0)),
+            pl.BlockSpec(weights.shape, lambda i: (0, 0, 0)),
+        ],
+        out_specs=pl.BlockSpec((ch, 2 * STEPS * STEP, count), lambda i: (0, i, 0)),
+        out_shape=jax.ShapeDtypeStruct((ch, 2 * spectra, count), jnp.bfloat16),
+        compiler_params=pltpu.CompilerParams(vmem_limit_bytes=40 << 20),
+        name="own_spectra",
+    )(words, words, gains, weights)
+
+
+def select_kernel(last_rows, slots_ref, words_ref, parts_ref, *outs):
+    step = pl.program_id(0)
+    count = words_ref.shape[1]
+    words = words_ref[...].astype(jnp.float32).astype(jnp.bfloat16)
+    for index, out_ref in enumerate(outs):
+        rows = out_ref.shape[1]
+        place = lax.broadcasted_iota(jnp.int32, (count, rows), 0)
+        choice = jnp.where(slots_ref[index : index + 1, :] == place, 1.0, 0.0).astype(jnp.bfloat16)
+        out_ref[...] = jnp.dot(words, choice, preferred_element_type=jnp.float32).astype(out_ref.dtype)
+
+        @pl.when(step == pl.num_programs(0) - 1)
+        def _():
+            extra = parts_ref.shape[0]
+            out_ref[last_rows : last_rows + extra, :] = jnp.dot(
+                parts_ref[...], choice, preferred_element_type=jnp.float32
+            ).astype(out_ref.dtype)
+            left = out_ref.shape[0] - last_rows - extra
+            out_ref[last_rows + extra :, :] = jnp.zeros((left, rows), out_ref.dtype)
+
+
+def select_rows(words, gains, slots, total):
+    lines, count = words.shape
+    pieces, rows = slots.shape
+    block = total // STEPS
+    parts = jnp.concatenate([gains >> 4, gains & 15], axis=0).astype(jnp.bfloat16)
+    return pl.pallas_call(
+        functools.partial(select_kernel, lines - (STEPS - 1) * block),
+        grid=(STEPS,),
+        in_specs=[
+            pl.BlockSpec((pieces, rows), lambda i: (0, 0)),
+            pl.BlockSpec((block, count), lambda i: (i, 0)),
+            pl.BlockSpec(parts.shape, lambda i: (0, 0)),
+        ],
+        out_specs=[pl.BlockSpec((block, rows), lambda i: (i, 0))] * pieces,
+        out_shape=[jax.ShapeDtypeStruct((total, rows), jnp.bfloat16)] * pieces,
+        compiler_params=pltpu.CompilerParams(vmem_limit_bytes=24 << 20),
+        name="select_rows",
+    )(slots, words, parts)
+
+
+def swap(value, bit):
+    pairs = [(index, index ^ bit) for index in range(lax.axis_size("feed"))]
+    return lax.ppermute(value, "feed", pairs)
+
+
+def side(bit):
+    return lax.axis_index("feed") // bit % 2
+
+
+def reduce_half(value, bit):
+    size = value.shape[0] // 2
+    keep = lax.dynamic_slice_in_dim(value, side(bit) * size, size, 0)
+    send = lax.dynamic_slice_in_dim(value, (1 - side(bit)) * size, size, 0)
+    return keep + swap(send, bit)
+
+
+def gather_half(value, bit, buffer):
+    size = value.shape[0]
+    other = swap(value, bit)
+    buffer = lax.dynamic_update_slice_in_dim(buffer, value, side(bit) * size, 0)
+    return lax.dynamic_update_slice_in_dim(buffer, other, (1 - side(bit)) * size, 0)
+
+
+def sum_over_feed(value):
+    half = reduce_half(value, 1)
+    size = half.shape[0] // 2
+    left, right = half[:size], half[size:]
+    left_1, right_1 = reduce_half(left, 2), reduce_half(right, 4)
+    left_2, right_2 = reduce_half(left_1, 4), reduce_half(right_1, 2)
+    left_3, right_3 = left_2 + swap(left_2, 8), right_2 + swap(right_2, 8)
+    left_1, right_1 = gather_half(left_3, 4, left_1), gather_half(right_3, 2, right_1)
+    left, right = gather_half(left_1, 2, left), gather_half(right_1, 4, right)
+    return gather_half(jnp.concatenate([left, right], axis=0), 1, value)
+
+
+def rows_kernel(main_ref, next_ref, parts_ref, weights_ref, own_ref, out_ref, left):
+    step = pl.program_id(0)
+    steps = pl.num_programs(0) // 2
+    ch = left.shape[0]
+    rows = main_ref.shape[1]
+
+    @pl.when(step < steps)
+    def _():
+        words = jnp.concatenate([main_ref[...], next_ref[...]], axis=0).astype(jnp.float32).astype(jnp.int32)
+        parts = parts_ref[...].astype(jnp.float32)
+        gains = parts[: 2 * ch] * 16.0 + parts[2 * ch :]
+
+        def store(b, c, real, imag):
+            spot = pl.ds(pl.multiple_of(step * (2 * STEPS * STEP), 2 * STEPS * STEP) + b * 2 * STEP, 2 * STEP)
+            left[c, spot, :rows] = jnp.concatenate([real, imag], axis=0).astype(left.dtype)
+            left[c, spot, rows:] = jnp.concatenate([imag, -real], axis=0).astype(left.dtype)
+
+        spectra_of(weights_ref, levels_of(words), gains, ch, store)
+
+    @pl.when(step >= steps)
+    def _():
+        each = own_ref.shape[0]
+        for index in range(each):
+            products = lax.dot_general(
+                own_ref[index],
+                left[(step - steps) * each + index],
+                (((0,), (0,)), ((), ())),
+                preferred_element_type=jnp.float32,
+            )
+            count = products.shape[0]
+            largest = jnp.maximum(jnp.max(jnp.abs(products), axis=0, keepdims=True), 2.0**-60)
+            power = jnp.floor(jnp.log2(largest))
+            coded = jnp.clip(jnp.round(products * jnp.exp2(RANGE - power)), -32767.0, 32767.0)
+            out_ref[index, :count, :] = coded.astype(jnp.int32).astype(jnp.int16)
+            line = jnp.broadcast_to(power, (out_ref.shape[1] - count, power.shape[1]))
+            out_ref[index, count:, :] = line.astype(jnp.int32).astype(jnp.int16)
+
+
+def row_products(words, own, weights, lines):
+    ch, width, count = own.shape
+    rows = words.shape[1]
+    main = STEPS * STEP * ch
+    steps = width // (2 * STEPS * STEP)
+    each = ch // steps
+    parts = words[lines : lines + 4 * ch]
+    return pl.pallas_call(
+        rows_kernel,
+        grid=(2 * steps,),
+        in_specs=[
+            pl.BlockSpec((main, rows), lambda i: (jnp.minimum(i, steps - 1), 0)),
+            pl.BlockSpec((STEP * ch, rows), lambda i: ((jnp.minimum(i, steps - 1) + 1) * STEPS, 0)),
+            pl.BlockSpec(parts.shape, lambda i: (0, 0)),
+            pl.BlockSpec(weights.shape, lambda i: (0, 0, 0)),
+            pl.BlockSpec((each, width, count), lambda i: (jnp.maximum(i - steps, 0), 0, 0)),
+        ],
+        out_specs=pl.BlockSpec((each, count + 16, 2 * rows), lambda i: (jnp.maximum(i - steps, 0), 0, 0)),
+        out_shape=jax.ShapeDtypeStruct((ch, count + 16, 2 * rows), jnp.int16),
+        scratch_shapes=[pltpu.VMEM((ch, width, 2 * rows), jnp.bfloat16)],
+        compiler_params=pltpu.CompilerParams(vmem_limit_bytes=40 << 20),
+        name="row_products",
+    )(words, words, parts, weights, own)
+
+
+def finish_kernel(scale, slot_ref, coded_ref, *refs):
+    out_ref, products, tile = refs[-3:]
+    step = pl.program_id(0)
+    sources, lines, width = coded_ref.shape
+    count = lines - 16
+    pieces = width // LANES
+    feeds = sources * count
+    columns = 2 * (feeds // LANES)
+    for source in range(sources):
+        power = coded_ref[source, count : count + 16, :][:1].astype(jnp.float32)
+        values = coded_ref[source, :count, :].astype(jnp.float32) * (jnp.exp2(power - RANGE) * scale)
+        for piece in range(pieces):
+            products[pl.ds(source * count * pieces + piece, count, stride=pieces), :] = values[
+                :, piece * LANES : (piece + 1) * LANES
+            ]
+
+    @pl.loop(0, feeds // LANES)
+    def _(j):
+        @pl.loop(0, LANES, unroll=16)
+        def _(i):
+            slot = slot_ref[j * LANES + i]
+            tile[pl.ds(pl.multiple_of(i * pieces, pieces), pieces), :] = products[
+                pl.ds(pl.multiple_of(slot * pieces, pieces), pieces), :
+            ]
+
+        for piece in range(pieces):
+            turned = tile[pl.ds(piece, LANES, stride=pieces), :].T
+            out_ref[pl.ds(2 * j + piece, LANES, stride=columns), :] = turned
+
+
+def finish(coded, feed_slot, index, pieces, scale, before):
+    sources, lines, width = coded.shape
+    rows = width // 2
+    feeds = sources * (lines - 16)
+    columns = 2 * (feeds // LANES)
+    earlier = [] if before is None else [before]
+    return pl.pallas_call(
+        functools.partial(finish_kernel, scale),
+        grid=(1,),
+        in_specs=[
+            pl.BlockSpec(memory_space=pltpu.SMEM),
+            pl.BlockSpec(coded.shape, lambda i: (0, 0, 0)),
+        ]
+        + [pl.BlockSpec(memory_space=pl.ANY)] * len(earlier),
+        out_specs=pl.BlockSpec((rows * columns, LANES), lambda i: (index, 0)),
+        out_shape=jax.ShapeDtypeStruct((pieces * rows * columns, LANES), jnp.float32),
+        scratch_shapes=[
+            pltpu.VMEM((feeds * width // LANES, LANES), jnp.float32),
+            pltpu.VMEM((width, LANES), jnp.float32),
+        ],
+        input_output_aliases={2: 0} if earlier else {},
+        compiler_params=pltpu.CompilerParams(vmem_limit_bytes=40 << 20),
+        name="finish",
+    )(feed_slot, coded, *earlier)
+
+
+def through_rows(samples, gains, feed_slot):
+    count, ch, frames = samples.shape
+    spectra = frames - TAPS + 1
+    pieces = ROWS // LANES
+    lines = frames * ch
+    unit = 16 * STEPS * 2
+    total = pl.cdiv(lines + 4 * ch, unit) * unit
+    words = jnp.transpose(samples, (2, 1, 0)).reshape(lines, count)
+    scales = gains.reshape(2 * ch, count)
+    weights = jnp.asarray(filter_weights(ch))
+    slots = (feed_slot[:ROWS] - lax.axis_index("feed") * count).reshape(pieces, LANES)
+    picked = select_rows(words, scales, slots, total)
+    own = own_spectra(words, scales.astype(jnp.float32), weights, ch, spectra)
+    out = None
+    for index in range(pieces):
+        rows = sum_over_feed(picked[index])
+        coded = row_products(rows, own, weights, lines)
+        moved = lax.all_to_all(coded, "feed", split_axis=0, concat_axis=0, tiled=True)
+        out = finish(moved, feed_slot, index, pieces, 1.0 / spectra, out)
+    feeds = feed_slot.shape[0]
+    out = out.reshape(ROWS, feeds // LANES, 2, LANES)
+    return jnp.transpose(out, (0, 2, 1, 3)).reshape(ROWS, 2, feeds)
+
+
+def body(samples, gains, feed_slot):
+    count, ch, frames = samples.shape
+    spectra = frames - TAPS + 1
+    even = count % LANES == 0 and spectra % (STEPS * STEP) == 0 and ch % STEPS == 0
+    if lax.axis_size("feed") == ch == 16 and even:
+        return through_rows(samples, gains, feed_slot)
+    return through_spectra(samples, gains, feed_slot)
+
+
 def solution(mesh):
     return jax.shard_map(
         body,

time: 302 us -> 266 us (0.88)
  waiting for transfers between devices: 182 us -> 115 us
  starting transfers between devices: 6.69 us -> 47.4 us
  Pallas kernels: 93.3 us -> 78.7 us
  other arithmetic: 0.01 us -> 11.1 us
  local copies, waits for them, and re-layouts: 19.8 us -> 13 us
    all_to_all x1 -> x2, waiting for transfers between devices: 182 us -> 34.7 us  [through_rows(): lax.all_to_all(coded, 'feed', split_axis=0, concat_axis=0, tiled=True)]
    ppermute x0 -> x24, waiting for transfers between devices: none -> 80 us  [swap(): return lax.ppermute(value, 'feed', pairs)]
    ppermute x0 -> x24, starting transfers between devices: none -> 36 us  [swap(): return lax.ppermute(value, 'feed', pairs)]
    pallas_call x2 -> x6, Pallas kernels: 93.3 us -> 78.7 us  [the longest x2 31.3 us: finish(): pl.pallas_call(functools.partial(finish_kernel, scale), grid=(1,), in_spe...]
    unnamed x9 -> x22, local copies, waits for them, and re-layouts: 19.5 us -> 6.24 us
    add x0 -> x10, other arithmetic: none -> 6.17 us  [reduce_half(): return keep + swap(send, bit)]
    all_to_all x1 -> x2, starting transfers between devices: 6.69 us -> 11.3 us  [through_rows(): lax.all_to_all(coded, 'feed', split_axis=0, concat_axis=0, tiled=True)]
    dynamic_update_slice x0 -> x14, local copies, waits for them, and re-layouts: none -> 3.68 us  [the longest x10 1.85 us: gather_half(): lax.dynamic_update_slice_in_dim(buffer, other, (1 - side(bit)) * size, 0)]
  transfers between devices with their start and end apart: 1 -> 26, of which waited for: 1 -> 13; matrix products, arithmetic and copies ran while one was open for 0% -> 6% of each run, Pallas kernels for 0% -> 22%
where the time goes in v2:
time: 266 us; the launch traced here: 265 us
  waiting for transfers between devices  115 us (43%)
  Pallas kernels  78.7 us (30%)
  starting transfers between devices  47.4 us (18%)
  local copies, waits for them, and re-layouts  13 us (5%)
  other arithmetic  11.1 us (4%)
    ppermute x24, waiting for transfers between devices, swap(): return lax.ppermute(value, 'feed', pairs)  80 us
    ppermute x24, starting transfers between devices, swap(): return lax.ppermute(value, 'feed', pairs)  36 us
    all_to_all x2, waiting for transfers between devices, through_rows(): lax.all_to_all(coded, 'feed', split_axis=0, concat_axis=0, tiled=True)  34.7 us
    pallas_call x2, Pallas kernels, finish(): pl.pallas_call(functools.partial(finish_kernel, scale), grid=(1,), in_spe...  31.3 us
    pallas_call x2, Pallas kernels, row_products(): pl.pallas_call(rows_kernel, grid=(2 * steps,), in_specs=[pl.BlockSpec((ma...  29.8 us
    pallas_call x1, Pallas kernels, own_spectra(): pl.pallas_call(own_kernel, grid=(spectra // (STEPS * STEP),), in_specs=[p...  12.4 us
    all_to_all x2, starting transfers between devices, through_rows(): lax.all_to_all(coded, 'feed', split_axis=0, concat_axis=0, tiled=True)  11.3 us
    unnamed x22, local copies, waits for them, and re-layouts  6.24 us
  transfers between devices with their start and end apart: 26, of which 13 were waited for; matrix products, arithmetic and copies ran while one was open for 6% of the time, Pallas kernels for 22%

profile of v2, /device:TPU:13, one launch (start us, length us, event | category | flops | bytes accessed | tf_op | source)
XLA Modules:
  0.0 265.3 jit_solution(7891831448389210182)
XLA Ops:
  0.0 0.8 fusion.2
  0.9 0.7 subtract_bitcast_fusion.slots_ref
  1.6 3.4 %copy-done = s32[256,16,519]{0,1,2:T(8,128)S(1)} copy-done((s32[256,16,519]{0,1,2:T(8,128)S(1)}, s32[256,16,519]{0,1,2:T(8,128)}, u32[]{:S(2)}) %copy-start) | copy-done | bytes 8503320
  5.0 5.2 %select_rows.1 = (bf16[8448,128]{1,0:T(8,128)(2,1)S(1)}, bf16[8448,128]{1,0:T(8,128)(2,1)S(1)}) custom-call(s32[2,128]{1,0:T(2,128)S(1)} %subtract_bitcast_fusion.slots_ref, s32[8304,256]{1,0:T(8,128)S(1)} %bitcast.15, bf16[64,256]{1,0:T(8,128)(2,1)S(1)} %pad_maximum_fusion.2.parts_ref), custom_call_target="tpu_custom_call" | custom-call | tf_op jit(solution)/shard_map/select_rows/pallas_call | solution.py:303
  10.1 1.1 constant_dynamic-slice_fusion.4
  11.9 1.0 constant_dynamic-slice_fusion.9
  12.9 12.4 %own_spectra.1.own_ref = bf16[16,1024,256]{2,1,0:T(8,128)(2,1)S(1)} custom-call(s32[8304,256]{1,0:T(8,128)} %bitcast.13, s32[8304,256]{1,0:T(8,128)} %bitcast.14, f32[32,256]{1,0:T(8,128)S(1)} %bitcast.16, bf16[4,256,256]{2,1,0:T(8,128)(2,1)S(1)} %copy-done.7), custom_call_target="tpu_custom_call" | custom-call | tf_op jit(solution)/shard_map/own_spectra/pallas_call | solution.py:262
  25.4 2.3 dynamic-slice_add_fusion
  28.3 1.8 dynamic-slice_add_fusion.1
  30.2 1.2 collective-permute-start.6
  31.4 1.3 collective-permute-start.1
  32.7 2.7 %collective-permute-done.18 = bf16[1056,128]{1,0:T(8,128)(2,1)S(1)} collective-permute-done((bf16[1056,128]{1,0:T(8,128)(2,1)S(1)}, bf16[1056,128]{1,0:T(8,128)(2,1)S(1)}, u32[]{:S(2)}, u32[]{:S(2)}) %collective-permute-start.18) | collective-permute-done | bytes 270368 | tf_op jit(solution)/shard_map/ppermute | solution.py:320
  36.0 0.9 collective-permute-start.14
  36.9 7.3 %collective-permute-done.19 = bf16[528,128]{1,0:T(8,128)(2,1)S(1)} collective-permute-done((bf16[528,128]{1,0:T(8,128)(2,1)S(1)}, bf16[528,128]{1,0:T(8,128)(2,1)S(1)}, u32[]{:S(2)}, u32[]{:S(2)}) %collective-permute-start.19) | collective-permute-done | bytes 135200 | tf_op jit(solution)/shard_map/ppermute | solution.py:320
  44.2 2.4 collective-permute-start.20
  46.7 2.3 collective-permute-done.20
  49.1 6.1 %collective-permute-start.21 = (bf16[528,128]{1,0:T(8,128)(2,1)S(1)}, bf16[528,128]{1,0:T(8,128)(2,1)S(1)}, u32[]{:S(2)}, u32[]{:S(2)}) collective-permute-start(bf16[528,128]{1,0:T(8,128)(2,1)S(1)} %get-tuple-element.12), channel_id=1, source_target_pairs={{0,2},{1,3},{2,0},{3,1},{4,6},{5,7},{6,4},{7,5},{8,10},{9,11},{10,... | collective-permute-start | bytes 405512 | tf_op jit(solution)/shard_map/ppermute | solution.py:320
  55.2 2.1 collective-permute-done.15
  57.4 2.6 collective-permute-start.16
  60.0 1.0 collective-permute-start.22
  61.0 1.6 collective-permute-done.16
  62.7 1.1 collective-permute-start.17
  63.8 4.2 %collective-permute-done.22 = bf16[1056,128]{1,0:T(8,128)(2,1)S(1)} collective-permute-done((bf16[1056,128]{1,0:T(8,128)(2,1)S(1)}, bf16[1056,128]{1,0:T(8,128)(2,1)S(1)}, u32[]{:S(2)}, u32[]{:S(2)}) %collective-permute-start.22) | collective-permute-done | bytes 270368 | tf_op jit(solution)/shard_map/ppermute | solution.py:320
  68.6 4.1 %collective-permute-start.23 = (bf16[4224,128]{1,0:T(8,128)(2,1)S(1)}, bf16[4224,128]{1,0:T(8,128)(2,1)S(1)}, u32[]{:S(2)}, u32[]{:S(2)}) collective-permute-start(bf16[4224,128]{1,0:T(8,128)(2,1)S(1)} %get-tuple-element.17), channel_id=1, source_target_pairs={{0,1},{1,0},{2,3},{3,2},{4,5},{5,4},{6,7},{7,6},{8,9},{9,8},{10,11... | collective-permute-start | bytes 3244040 | tf_op jit(solution)/shard_map/ppermute | solution.py:320
  74.0 1.8 collective-permute-start.2
  75.8 2.4 collective-permute-done.7
  78.2 0.7 dynamic-slice_add_fusion.8
  78.9 3.0 %collective-permute-start.8 = (bf16[528,128]{1,0:T(8,128)(2,1)}, bf16[528,128]{1,0:T(8,128)(2,1)}, u32[]{:S(2)}, u32[]{:S(2)}) collective-permute-start(bf16[528,128]{1,0:T(8,128)(2,1)} %dynamic-slice_add_fusion.8), channel_id=1, source_target_pairs={{0,8},{1,9},{2,10},{3,11},{4,12},{5,13},{6,14},{7,15},{8,0},{9,1},... | collective-permute-start | bytes 405512 | tf_op jit(solution)/shard_map/ppermute | solution.py:320
  82.0 14.9 %row_products.3 = s16[16,272,256]{2,1,0:T(8,128)(2,1)S(1)} custom-call(bf16[8448,128]{1,0:T(8,128)(2,1)S(1)} %constant_dynamic-update-slice_fusion.main_ref.next_ref, bf16[8448,128]{1,0:T(8,128)(2,1)S(1)} %constant_dynamic-update-slice_fusion.main_ref.next_ref, bf16[64,128]{1,0:T(8,128)(2,1)S(1)} %slice.41.parts_ref, bf16[4,256,256]{2,1,0:T(8,128)(2,1)S(1)} %copy-done.7, ...), custom_call_target="tpu_custom_call" | custom-call | tf_op jit(solution)/shard_map/row_products/pallas_call | solution.py:398
  97.0 1.4 copy-done.5
  98.4 4.9 %all-to-all-start.1 = ((s16[16,272,256]{2,1,0:T(8,128)(2,1)}), s16[16,272,256]{2,1,0:T(8,128)(2,1)}, u32[]{:S(2)}, u32[]{:S(2)}) async-start(s16[16,272,256]{2,1,0:T(8,128)(2,1)} %copy-done.5), calls=%async_computation.1 | async-start | bytes 4456448 | tf_op jit(solution)/shard_map/all_to_all | solution.py:489
  103.2 1.0 dynamic-slice_add_fusion.9
  104.2 2.2 collective-permute-start.3
  106.4 1.7 constant_dynamic-update-slice_fusion.15
  108.3 48.7 %collective-permute-done.3 = bf16[528,128]{1,0:T(8,128)(2,1)S(1)} collective-permute-done((bf16[528,128]{1,0:T(8,128)(2,1)S(1)}, bf16[528,128]{1,0:T(8,128)(2,1)S(1)}, u32[]{:S(2)}, u32[]{:S(2)}) %collective-permute-start.3) | collective-permute-done | bytes 135200 | tf_op jit(solution)/shard_map/ppermute | solution.py:320
  157.1 3.3 %collective-permute-start.4 = (bf16[528,128]{1,0:T(8,128)(2,1)S(1)}, bf16[528,128]{1,0:T(8,128)(2,1)S(1)}, u32[]{:S(2)}, u32[]{:S(2)}) collective-permute-start(bf16[528,128]{1,0:T(8,128)(2,1)S(1)} %get-tuple-element.14), channel_id=1, source_target_pairs={{0,4},{1,5},{2,6},{3,7},{4,0},{5,1},{6,2},{7,3},{8,12},{9,13},{10,... | collective-permute-start | bytes 405512 | tf_op jit(solution)/shard_map/ppermute | solution.py:320
  161.2 1.7 constant_dynamic-update-slice_fusion.13
  163.9 5.4 %collective-permute-done.10 = bf16[1056,128]{1,0:T(8,128)(2,1)S(1)} collective-permute-done((bf16[1056,128]{1,0:T(8,128)(2,1)}, bf16[1056,128]{1,0:T(8,128)(2,1)S(1)}, u32[]{:S(2)}, u32[]{:S(2)}) %collective-permute-start.10) | collective-permute-done | bytes 270368 | tf_op jit(solution)/shard_map/ppermute | solution.py:320
  169.3 0.7 constant_dynamic-update-slice_fusion.12
  170.1 1.3 pad_maximum_fusion
  171.4 2.6 collective-permute-start.11
  174.0 2.3 collective-permute-done.11
  176.5 14.9 %row_products.2 = s16[16,272,256]{2,1,0:T(8,128)(2,1)S(1)} custom-call(bf16[8448,128]{1,0:T(8,128)(2,1)S(1)} %constant_dynamic-update-slice_fusion.10.main_ref.next_ref, bf16[8448,128]{1,0:T(8,128)(2,1)S(1)} %constant_dynamic-update-slice_fusion.10.main_ref.next_ref, bf16[64,128]{1,0:T(8,128)(2,1)S(1)} %slice.38.parts_ref, ...), custom_call_target="tpu_custom_call" | custom-call | tf_op jit(solution)/shard_map/row_products/pallas_call | solution.py:398
  191.4 1.4 copy-done.6
  192.8 6.4 %all-to-all-start = ((s16[16,272,256]{2,1,0:T(8,128)(2,1)}), s16[16,272,256]{2,1,0:T(8,128)(2,1)}, u32[]{:S(2)}, u32[]{:S(2)}) async-start(s16[16,272,256]{2,1,0:T(8,128)(2,1)} %copy-done.6), calls=%async_computation | async-start | bytes 4456448 | tf_op jit(solution)/shard_map/all_to_all | solution.py:489
  199.3 15.7 %finish.2.refs_0_ = f32[16384,128]{1,0:T(8,128)} custom-call(s32[4096]{0:T(1024)S(1)} %copy-done.8, s16[16,272,256]{2,1,0:T(8,128)(2,1)} %all-to-all-done.1.coded_ref), custom_call_target="tpu_custom_call" | custom-call | tf_op jit(solution)/shard_map/finish/pallas_call | solution.py:452
  214.9 34.7 %all-to-all-done.coded_ref = s16[16,272,256]{2,1,0:T(8,128)(2,1)} async-done(((s16[16,272,256]{2,1,0:T(8,128)(2,1)}), s16[16,272,256]{2,1,0:T(8,128)(2,1)}, u32[]{:S(2)}, u32[]{:S(2)}) %all-to-all-start) | async-done | bytes 2228256 | tf_op jit(solution)/shard_map/all_to_all | solution.py:489
  249.6 15.7 %finish.3 = f32[16384,128]{1,0:T(8,128)} custom-call(s32[4096]{0:T(1024)S(1)} %copy-done.8, s16[16,272,256]{2,1,0:T(8,128)(2,1)} %all-to-all-done.coded_ref, f32[16384,128]{1,0:T(8,128)} %finish.2.refs_0_), custom_call_target="tpu_custom_call", output_to_operand_aliasing={{}: (2, {})} | custom-call | tf_op jit(solution)/shard_map/finish/pallas_call | solution.py:452
  (79 shorter events, 6.6 us)
Async XLA Ops:
  1.6 3.4 %copy-start = (s32[256,16,519]{0,1,2:T(8,128)S(1)}, s32[256,16,519]{0,1,2:T(8,128)}, u32[]{:S(2)}) copy-start(s32[256,16,519]{0,1,2:T(8,128)} %param.4) | copy-start | bytes 25509892
  10.1 2.8 %copy-start.3 = (bf16[8448,128]{1,0:T(8,128)(2,1)}, bf16[8448,128]{1,0:T(8,128)(2,1)S(1)}, u32[]{:S(2)}) copy-start(bf16[8448,128]{1,0:T(8,128)(2,1)S(1)} %get-tuple-element.8) | copy-start | bytes 6488068
  10.1 2.8 %copy-start.7 = (bf16[4,256,256]{2,1,0:T(8,128)(2,1)S(1)}, bf16[4,256,256]{2,1,0:T(8,128)(2,1)}, u32[]{:S(2)}) copy-start(bf16[4,256,256]{2,1,0:T(8,128)(2,1)} %constant.222.clone.weights_ref) | copy-start | bytes 1572868
  11.2 14.1 %collective-permute-start.12 = (bf16[4224,128]{1,0:T(8,128)(2,1)}, bf16[4224,128]{1,0:T(8,128)(2,1)}, u32[]{:S(2)}, u32[]{:S(2)}) collective-permute-start(bf16[4224,128]{1,0:T(8,128)(2,1)} %constant_dynamic-slice_fusion.4), channel_id=1, source_target_pairs={{0,1},{1,0},{2,3},{3,2},{4,5},{5,4},{6,7},{7,6},{8,9},{9,8},{10,11... | collective-permute-start | bytes 3244040 | tf_op jit(solution)/shard_map/ppermute | solution.py:320
  12.9 15.3 %collective-permute-start = (bf16[4224,128]{1,0:T(8,128)(2,1)}, bf16[4224,128]{1,0:T(8,128)(2,1)}, u32[]{:S(2)}, u32[]{:S(2)}) collective-permute-start(bf16[4224,128]{1,0:T(8,128)(2,1)} %constant_dynamic-slice_fusion.9), channel_id=1, source_target_pairs={{0,1},{1,0},{2,3},{3,2},{4,5},{5,4},{6,7},{7,6},{8,9},{9,8},{10,11... | collective-permute-start | bytes 3244040 | tf_op jit(solution)/shard_map/ppermute | solution.py:320
  12.9 12.4 %copy-start.4 = (bf16[8448,128]{1,0:T(8,128)(2,1)S(1)}, bf16[8448,128]{1,0:T(8,128)(2,1)}, u32[]{:S(2)}) copy-start(bf16[8448,128]{1,0:T(8,128)(2,1)} %copy-done.3) | copy-start | bytes 6488068
  25.3 56.7 %copy-start.1 = (bf16[16,1024,256]{2,1,0:T(8,128)(2,1)}, bf16[16,1024,256]{2,1,0:T(8,128)(2,1)S(1)}, u32[]{:S(2)}) copy-start(bf16[16,1024,256]{2,1,0:T(8,128)(2,1)S(1)} %own_spectra.1.own_ref) | copy-start | bytes 25165828
  27.8 7.6 %collective-permute-start.18 = (bf16[1056,128]{1,0:T(8,128)(2,1)S(1)}, bf16[1056,128]{1,0:T(8,128)(2,1)S(1)}, u32[]{:S(2)}, u32[]{:S(2)}) collective-permute-start(bf16[1056,128]{1,0:T(8,128)(2,1)S(1)} %constant_dynamic-slice_fusion.1), channel_id=1, source_target_pairs={{0,4},{1,5},{2,6},{3,7},{4,0},{5,1},{6,2},{7,3},{8,12},{9,13},{10,... | collective-permute-start | bytes 811016 | tf_op jit(solution)/shard_map/ppermute | solution.py:320
  28.1 7.8 %collective-permute-start.13 = (bf16[1056,128]{1,0:T(8,128)(2,1)S(1)}, bf16[1056,128]{1,0:T(8,128)(2,1)S(1)}, u32[]{:S(2)}, u32[]{:S(2)}) collective-permute-start(bf16[1056,128]{1,0:T(8,128)(2,1)S(1)} %constant_dynamic-slice_fusion.3), channel_id=1, source_target_pairs={{0,2},{1,3},{2,0},{3,1},{4,6},{5,7},{6,4},{7,5},{8,10},{9,11},{10,... | collective-permute-start | bytes 811016 | tf_op jit(solution)/shard_map/ppermute | solution.py:320
  30.1 42.6 %copy-start.9 = (bf16[2112,128]{1,0:T(8,128)(2,1)}, bf16[2112,128]{1,0:T(8,128)(2,1)S(1)}, u32[]{:S(2)}) copy-start(bf16[2112,128]{1,0:T(8,128)(2,1)S(1)} %get-tuple-element.24) | copy-start | bytes 1622020
  30.2 42.5 %collective-permute-start.6 = (bf16[1056,128]{1,0:T(8,128)(2,1)S(1)}, bf16[1056,128]{1,0:T(8,128)(2,1)S(1)}, u32[]{:S(2)}, u32[]{:S(2)}) collective-permute-start(bf16[1056,128]{1,0:T(8,128)(2,1)S(1)} %constant_dynamic-slice_fusion.6), channel_id=1, source_target_pairs={{0,4},{1,5},{2,6},{3,7},{4,0},{5,1},{6,2},{7,3},{8,12},{9,13},{10,... | collective-permute-start | bytes 811016 | tf_op jit(solution)/shard_map/ppermute | solution.py:320
  31.4 41.8 %collective-permute-start.1 = (bf16[1056,128]{1,0:T(8,128)(2,1)S(1)}, bf16[1056,128]{1,0:T(8,128)(2,1)S(1)}, u32[]{:S(2)}, u32[]{:S(2)}) collective-permute-start(bf16[1056,128]{1,0:T(8,128)(2,1)S(1)} %constant_dynamic-slice_fusion.8), channel_id=1, source_target_pairs={{0,2},{1,3},{2,0},{3,1},{4,6},{5,7},{6,4},{7,5},{8,10},{9,11},{10,... | collective-permute-start | bytes 811016 | tf_op jit(solution)/shard_map/ppermute | solution.py:320
  35.6 8.6 %collective-permute-start.19 = (bf16[528,128]{1,0:T(8,128)(2,1)S(1)}, bf16[528,128]{1,0:T(8,128)(2,1)S(1)}, u32[]{:S(2)}, u32[]{:S(2)}) collective-permute-start(bf16[528,128]{1,0:T(8,128)(2,1)S(1)} %constant_dynamic-slice_fusion), channel_id=1, source_target_pairs={{0,2},{1,3},{2,0},{3,1},{4,6},{5,7},{6,4},{7,5},{8,10},{9,11},{10,... | collective-permute-start | bytes 405512 | tf_op jit(solution)/shard_map/ppermute | solution.py:320
  36.0 10.5 %collective-permute-start.14 = (bf16[528,128]{1,0:T(8,128)(2,1)S(1)}, bf16[528,128]{1,0:T(8,128)(2,1)S(1)}, u32[]{:S(2)}, u32[]{:S(2)}) collective-permute-start(bf16[528,128]{1,0:T(8,128)(2,1)S(1)} %constant_dynamic-slice_fusion.2), channel_id=1, source_target_pairs={{0,4},{1,5},{2,6},{3,7},{4,0},{5,1},{6,2},{7,3},{8,12},{9,13},{10,... | collective-permute-start | bytes 405512 | tf_op jit(solution)/shard_map/ppermute | solution.py:320
  44.2 4.9 %collective-permute-start.20 = (bf16[528,128]{1,0:T(8,128)(2,1)S(1)}, bf16[528,128]{1,0:T(8,128)(2,1)S(1)}, u32[]{:S(2)}, u32[]{:S(2)}) collective-permute-start(bf16[528,128]{1,0:T(8,128)(2,1)S(1)} %dynamic-slice_add_fusion.6), channel_id=1, source_target_pairs={{0,8},{1,9},{2,10},{3,11},{4,12},{5,13},{6,14},{7,15},{8,0},{9,1},... | collective-permute-start | bytes 405512 | tf_op jit(solution)/shard_map/ppermute | solution.py:320
  46.6 10.7 %collective-permute-start.15 = (bf16[528,128]{1,0:T(8,128)(2,1)S(1)}, bf16[528,128]{1,0:T(8,128)(2,1)S(1)}, u32[]{:S(2)}, u32[]{:S(2)}) collective-permute-start(bf16[528,128]{1,0:T(8,128)(2,1)S(1)} %dynamic-slice_add_fusion.7), channel_id=1, source_target_pairs={{0,8},{1,9},{2,10},{3,11},{4,12},{5,13},{6,14},{7,15},{8,0},{9,1},... | collective-permute-start | bytes 405512 | tf_op jit(solution)/shard_map/ppermute | solution.py:320
  49.1 10.8 %collective-permute-start.21 = (bf16[528,128]{1,0:T(8,128)(2,1)S(1)}, bf16[528,128]{1,0:T(8,128)(2,1)S(1)}, u32[]{:S(2)}, u32[]{:S(2)}) collective-permute-start(bf16[528,128]{1,0:T(8,128)(2,1)S(1)} %get-tuple-element.12), channel_id=1, source_target_pairs={{0,2},{1,3},{2,0},{3,1},{4,6},{5,7},{6,4},{7,5},{8,10},{9,11},{10,... | collective-permute-start | bytes 405512 | tf_op jit(solution)/shard_map/ppermute | solution.py:320
  57.4 5.3 %collective-permute-start.16 = (bf16[528,128]{1,0:T(8,128)(2,1)S(1)}, bf16[528,128]{1,0:T(8,128)(2,1)S(1)}, u32[]{:S(2)}, u32[]{:S(2)}) collective-permute-start(bf16[528,128]{1,0:T(8,128)(2,1)S(1)} %get-tuple-element.10), channel_id=1, source_target_pairs={{0,4},{1,5},{2,6},{3,7},{4,0},{5,1},{6,2},{7,3},{8,12},{9,13},{10,... | collective-permute-start | bytes 405512 | tf_op jit(solution)/shard_map/ppermute | solution.py:320
  60.0 8.1 %collective-permute-start.22 = (bf16[1056,128]{1,0:T(8,128)(2,1)S(1)}, bf16[1056,128]{1,0:T(8,128)(2,1)S(1)}, u32[]{:S(2)}, u32[]{:S(2)}) collective-permute-start(bf16[1056,128]{1,0:T(8,128)(2,1)S(1)} %constant_dynamic-update-slice_fusion.4), channel_id=1, source_target_pairs={{0,4},{1,5},{2,6},{3,7},{4,0},{5,1},{6,2},{7,3},{8,12},{9,13},{10,... | collective-permute-start | bytes 811016 | tf_op jit(solution)/shard_map/ppermute | solution.py:320
  62.7 5.7 %collective-permute-start.17 = (bf16[1056,128]{1,0:T(8,128)(2,1)S(1)}, bf16[1056,128]{1,0:T(8,128)(2,1)S(1)}, u32[]{:S(2)}, u32[]{:S(2)}) collective-permute-start(bf16[1056,128]{1,0:T(8,128)(2,1)S(1)} %constant_dynamic-update-slice_fusion.8), channel_id=1, source_target_pairs={{0,2},{1,3},{2,0},{3,1},{4,6},{5,7},{6,4},{7,5},{8,10},{9,11},{10,... | collective-permute-start | bytes 811016 | tf_op jit(solution)/shard_map/ppermute | solution.py:320
  68.6 13.2 %collective-permute-start.23 = (bf16[4224,128]{1,0:T(8,128)(2,1)S(1)}, bf16[4224,128]{1,0:T(8,128)(2,1)S(1)}, u32[]{:S(2)}, u32[]{:S(2)}) collective-permute-start(bf16[4224,128]{1,0:T(8,128)(2,1)S(1)} %get-tuple-element.17), channel_id=1, source_target_pairs={{0,1},{1,0},{2,3},{3,2},{4,5},{5,4},{6,7},{7,6},{8,9},{9,8},{10,11... | collective-permute-start | bytes 3244040 | tf_op jit(solution)/shard_map/ppermute | solution.py:320
  72.8 9.1 %copy-start.10 = (bf16[1056,128]{1,0:T(8,128)(2,1)}, bf16[1056,128]{1,0:T(8,128)(2,1)S(1)}, u32[]{:S(2)}) copy-start(bf16[1056,128]{1,0:T(8,128)(2,1)S(1)} %dynamic-slice_add_fusion.4) | copy-start | bytes 811012
  72.8 5.3 %collective-permute-start.7 = (bf16[528,128]{1,0:T(8,128)(2,1)S(1)}, bf16[528,128]{1,0:T(8,128)(2,1)S(1)}, u32[]{:S(2)}, u32[]{:S(2)}) collective-permute-start(bf16[528,128]{1,0:T(8,128)(2,1)S(1)} %constant_dynamic-slice_fusion.5), channel_id=1, source_target_pairs={{0,2},{1,3},{2,0},{3,1},{4,6},{5,7},{6,4},{7,5},{8,10},{9,11},{10,... | collective-permute-start | bytes 405512 | tf_op jit(solution)/shard_map/ppermute | solution.py:320
  74.0 29.2 %collective-permute-start.2 = (bf16[528,128]{1,0:T(8,128)(2,1)}, bf16[528,128]{1,0:T(8,128)(2,1)}, u32[]{:S(2)}, u32[]{:S(2)}) collective-permute-start(bf16[528,128]{1,0:T(8,128)(2,1)} %constant_dynamic-slice_fusion.7), channel_id=1, source_target_pairs={{0,4},{1,5},{2,6},{3,7},{4,0},{5,1},{6,2},{7,3},{8,12},{9,13},{10,... | collective-permute-start | bytes 405512 | tf_op jit(solution)/shard_map/ppermute | solution.py:320
  78.9 27.5 %collective-permute-start.8 = (bf16[528,128]{1,0:T(8,128)(2,1)}, bf16[528,128]{1,0:T(8,128)(2,1)}, u32[]{:S(2)}, u32[]{:S(2)}) collective-permute-start(bf16[528,128]{1,0:T(8,128)(2,1)} %dynamic-slice_add_fusion.8), channel_id=1, source_target_pairs={{0,8},{1,9},{2,10},{3,11},{4,12},{5,13},{6,14},{7,15},{8,0},{9,1},... | collective-permute-start | bytes 405512 | tf_op jit(solution)/shard_map/ppermute | solution.py:320
  96.9 1.4 copy-start.5
  98.4 94.4 %all-to-all-start.1 = ((s16[16,272,256]{2,1,0:T(8,128)(2,1)}), s16[16,272,256]{2,1,0:T(8,128)(2,1)}, u32[]{:S(2)}, u32[]{:S(2)}) async-start(s16[16,272,256]{2,1,0:T(8,128)(2,1)} %copy-done.5), calls=%async_computation.1 | async-start | bytes 4456448 | tf_op jit(solution)/shard_map/all_to_all | solution.py:489
  104.2 52.9 %collective-permute-start.3 = (bf16[528,128]{1,0:T(8,128)(2,1)S(1)}, bf16[528,128]{1,0:T(8,128)(2,1)S(1)}, u32[]{:S(2)}, u32[]{:S(2)}) collective-permute-start(bf16[528,128]{1,0:T(8,128)(2,1)S(1)} %dynamic-slice_add_fusion.9), channel_id=1, source_target_pairs={{0,8},{1,9},{2,10},{3,11},{4,12},{5,13},{6,14},{7,15},{8,0},{9,1},... | collective-permute-start | bytes 405512 | tf_op jit(solution)/shard_map/ppermute | solution.py:320
  108.1 52.4 %collective-permute-start.9 = (bf16[528,128]{1,0:T(8,128)(2,1)S(1)}, bf16[528,128]{1,0:T(8,128)(2,1)S(1)}, u32[]{:S(2)}, u32[]{:S(2)}) collective-permute-start(bf16[528,128]{1,0:T(8,128)(2,1)S(1)} %get-tuple-element.16), channel_id=1, source_target_pairs={{0,2},{1,3},{2,0},{3,1},{4,6},{5,7},{6,4},{7,5},{8,10},{9,11},{10,... | collective-permute-start | bytes 405512 | tf_op jit(solution)/shard_map/ppermute | solution.py:320
  157.1 19.4 %copy-start.2 = (bf16[16,1024,256]{2,1,0:T(8,128)(2,1)S(1)}, bf16[16,1024,256]{2,1,0:T(8,128)(2,1)}, u32[]{:S(2)}) copy-start(bf16[16,1024,256]{2,1,0:T(8,128)(2,1)} %copy-done.1) | copy-start | bytes 25165828
  157.1 6.4 %collective-permute-start.4 = (bf16[528,128]{1,0:T(8,128)(2,1)S(1)}, bf16[528,128]{1,0:T(8,128)(2,1)S(1)}, u32[]{:S(2)}, u32[]{:S(2)}) collective-permute-start(bf16[528,128]{1,0:T(8,128)(2,1)S(1)} %get-tuple-element.14), channel_id=1, source_target_pairs={{0,4},{1,5},{2,6},{3,7},{4,0},{5,1},{6,2},{7,3},{8,12},{9,13},{10,... | collective-permute-start | bytes 405512 | tf_op jit(solution)/shard_map/ppermute | solution.py:320
  161.1 8.1 %collective-permute-start.10 = (bf16[1056,128]{1,0:T(8,128)(2,1)}, bf16[1056,128]{1,0:T(8,128)(2,1)S(1)}, u32[]{:S(2)}, u32[]{:S(2)}) collective-permute-start(bf16[1056,128]{1,0:T(8,128)(2,1)} %constant_dynamic-update-slice_fusion.14), channel_id=1, source_target_pairs={{0,4},{1,5},{2,6},{3,7},{4,0},{5,1},{6,2},{7,3},{8,12},{9,13},{10,... | collective-permute-start | bytes 811016 | tf_op jit(solution)/shard_map/ppermute | solution.py:320
  163.6 6.4 %collective-permute-start.5 = (bf16[1056,128]{1,0:T(8,128)(2,1)S(1)}, bf16[1056,128]{1,0:T(8,128)(2,1)S(1)}, u32[]{:S(2)}, u32[]{:S(2)}) collective-permute-start(bf16[1056,128]{1,0:T(8,128)(2,1)S(1)} %constant_dynamic-update-slice_fusion.18), channel_id=1, source_target_pairs={{0,2},{1,3},{2,0},{3,1},{4,6},{5,7},{6,4},{7,5},{8,10},{9,11},{10,... | collective-permute-start | bytes 811016 | tf_op jit(solution)/shard_map/ppermute | solution.py:320
  171.4 4.9 %collective-permute-start.11 = (bf16[4224,128]{1,0:T(8,128)(2,1)S(1)}, bf16[4224,128]{1,0:T(8,128)(2,1)S(1)}, u32[]{:S(2)}, u32[]{:S(2)}) collective-permute-start(bf16[4224,128]{1,0:T(8,128)(2,1)S(1)} %get-tuple-element.21), channel_id=1, source_target_pairs={{0,1},{1,0},{2,3},{3,2},{4,5},{5,4},{6,7},{7,6},{8,9},{9,8},{10,11... | collective-permute-start | bytes 3244040 | tf_op jit(solution)/shard_map/ppermute | solution.py:320
  191.4 1.4 copy-start.6
  192.8 6.5 %copy-start.8 = (s32[4096]{0:T(1024)S(1)}, s32[4096]{0:T(1024)}, u32[]{:S(2)}) copy-start(s32[4096]{0:T(1024)} %slot_ref.3) | copy-start | bytes 49156
  192.8 56.8 %all-to-all-start = ((s16[16,272,256]{2,1,0:T(8,128)(2,1)}), s16[16,272,256]{2,1,0:T(8,128)(2,1)}, u32[]{:S(2)}, u32[]{:S(2)}) async-start(s16[16,272,256]{2,1,0:T(8,128)(2,1)} %copy-done.6), calls=%async_computation | async-start | bytes 4456448 | tf_op jit(solution)/shard_map/all_to_all | solution.py:489

commit v3 on v2

--- a/solution.py
+++ b/solution.py
@@ -275,41 +275,39 @@
     )(words, words, gains, weights)
 
 
-def select_kernel(last_rows, slots_ref, words_ref, parts_ref, *outs):
+def select_kernel(last_rows, slots_ref, words_ref, parts_ref, out_ref):
     step = pl.program_id(0)
-    count = words_ref.shape[1]
+    count, rows = words_ref.shape[1], out_ref.shape[1]
     words = words_ref[...].astype(jnp.float32).astype(jnp.bfloat16)
-    for index, out_ref in enumerate(outs):
-        rows = out_ref.shape[1]
-        place = lax.broadcasted_iota(jnp.int32, (count, rows), 0)
-        choice = jnp.where(slots_ref[index : index + 1, :] == place, 1.0, 0.0).astype(jnp.bfloat16)
-        out_ref[...] = jnp.dot(words, choice, preferred_element_type=jnp.float32).astype(out_ref.dtype)
-
-        @pl.when(step == pl.num_programs(0) - 1)
-        def _():
-            extra = parts_ref.shape[0]
-            out_ref[last_rows : last_rows + extra, :] = jnp.dot(
-                parts_ref[...], choice, preferred_element_type=jnp.float32
-            ).astype(out_ref.dtype)
-            left = out_ref.shape[0] - last_rows - extra
-            out_ref[last_rows + extra :, :] = jnp.zeros((left, rows), out_ref.dtype)
+    place = lax.broadcasted_iota(jnp.int32, (count, rows), 0)
+    choice = jnp.where(slots_ref[...] == place, 1.0, 0.0).astype(jnp.bfloat16)
+    out_ref[...] = jnp.dot(words, choice, preferred_element_type=jnp.float32).astype(out_ref.dtype)
+
+    @pl.when(step == pl.num_programs(0) - 1)
+    def _():
+        extra = parts_ref.shape[0]
+        out_ref[last_rows : last_rows + extra, :] = jnp.dot(
+            parts_ref[...], choice, preferred_element_type=jnp.float32
+        ).astype(out_ref.dtype)
+        left = out_ref.shape[0] - last_rows - extra
+        out_ref[last_rows + extra :, :] = jnp.zeros((left, rows), out_ref.dtype)
 
 
 def select_rows(words, gains, slots, total):
     lines, count = words.shape
-    pieces, rows = slots.shape
+    rows = slots.shape[1]
     block = total // STEPS
     parts = jnp.concatenate([gains >> 4, gains & 15], axis=0).astype(jnp.bfloat16)
     return pl.pallas_call(
         functools.partial(select_kernel, lines - (STEPS - 1) * block),
         grid=(STEPS,),
         in_specs=[
-            pl.BlockSpec((pieces, rows), lambda i: (0, 0)),
+            pl.BlockSpec((1, rows), lambda i: (0, 0)),
             pl.BlockSpec((block, count), lambda i: (i, 0)),
             pl.BlockSpec(parts.shape, lambda i: (0, 0)),
         ],
-        out_specs=[pl.BlockSpec((block, rows), lambda i: (i, 0))] * pieces,
-        out_shape=[jax.ShapeDtypeStruct((total, rows), jnp.bfloat16)] * pieces,
+        out_specs=pl.BlockSpec((block, rows), lambda i: (i, 0)),
+        out_shape=jax.ShapeDtypeStruct((total, rows), jnp.bfloat16),
         compiler_params=pltpu.CompilerParams(vmem_limit_bytes=24 << 20),
         name="select_rows",
     )(slots, words, parts)
@@ -388,20 +386,19 @@
             out_ref[index, count:, :] = line.astype(jnp.int32).astype(jnp.int16)
 
 
-def row_products(words, own, weights, lines):
+def row_products(words, parts, own, weights, index):
     ch, width, count = own.shape
-    rows = words.shape[1]
+    rows = LANES
     main = STEPS * STEP * ch
     steps = width // (2 * STEPS * STEP)
     each = ch // steps
-    parts = words[lines : lines + 4 * ch]
     return pl.pallas_call(
         rows_kernel,
         grid=(2 * steps,),
         in_specs=[
-            pl.BlockSpec((main, rows), lambda i: (jnp.minimum(i, steps - 1), 0)),
-            pl.BlockSpec((STEP * ch, rows), lambda i: ((jnp.minimum(i, steps - 1) + 1) * STEPS, 0)),
-            pl.BlockSpec(parts.shape, lambda i: (0, 0)),
+            pl.BlockSpec((main, rows), lambda i: (jnp.minimum(i, steps - 1), index)),
+            pl.BlockSpec((STEP * ch, rows), lambda i: ((jnp.minimum(i, steps - 1) + 1) * STEPS, index)),
+            pl.BlockSpec((parts.shape[0], rows), lambda i: (0, index)),
             pl.BlockSpec(weights.shape, lambda i: (0, 0, 0)),
             pl.BlockSpec((each, width, count), lambda i: (jnp.maximum(i - steps, 0), 0, 0)),
         ],
@@ -479,13 +476,14 @@
     words = jnp.transpose(samples, (2, 1, 0)).reshape(lines, count)
     scales = gains.reshape(2 * ch, count)
     weights = jnp.asarray(filter_weights(ch))
-    slots = (feed_slot[:ROWS] - lax.axis_index("feed") * count).reshape(pieces, LANES)
+    slots = (feed_slot[:ROWS] - lax.axis_index("feed") * count).reshape(1, ROWS)
     picked = select_rows(words, scales, slots, total)
     own = own_spectra(words, scales.astype(jnp.float32), weights, ch, spectra)
+    rows = sum_over_feed(picked)
+    parts = rows[lines : lines + 4 * ch]
     out = None
     for index in range(pieces):
-        rows = sum_over_feed(picked[index])
-        coded = row_products(rows, own, weights, lines)
+        coded = row_products(rows, parts, own, weights, index)
         moved = lax.all_to_all(coded, "feed", split_axis=0, concat_axis=0, tiled=True)
         out = finish(moved, feed_slot, index, pieces, 1.0 / spectra, out)
     feeds = feed_slot.shape[0]

time: 266 us -> 259 us (0.974)
  starting transfers between devices: 47.4 us -> 19.2 us
  waiting for transfers between devices: 115 us -> 127 us
  Pallas kernels: 78.7 us -> 86.7 us
  local copies, waits for them, and re-layouts: 13 us -> 18.2 us
  other arithmetic: 11.1 us -> 6.93 us
    ppermute x24 -> x12, starting transfers between devices: 36 us -> 7.47 us  [swap(): return lax.ppermute(value, 'feed', pairs)]
    all_to_all x2, waiting for transfers between devices: 34.7 us -> 62.8 us  [through_rows(): lax.all_to_all(coded, 'feed', split_axis=0, concat_axis=0, tiled=True)]
    ppermute x24 -> x12, waiting for transfers between devices: 80 us -> 63.7 us  [swap(): return lax.ppermute(value, 'feed', pairs)]
    pallas_call x2, Pallas kernels: 29.8 us -> 41.3 us  [row_products(): pl.pallas_call(rows_kernel, grid=(2 * steps,), in_specs=[pl.BlockSpec((ma...]
    unnamed x22 -> x18, local copies, waits for them, and re-layouts: 6.24 us -> 12.2 us
    add x10 -> x5, other arithmetic: 6.17 us -> 3.66 us  [reduce_half(): return keep + swap(send, bit)]
  transfers between devices with their start and end apart: 26 -> 14, of which waited for: 13 -> 10; matrix products, arithmetic and copies ran while one was open for 6% -> 1% of each run, Pallas kernels for 22% -> 19%
where the time goes in v3:
time: 259 us; the launch traced here: 258 us
  waiting for transfers between devices  127 us (49%)
  Pallas kernels  86.7 us (33%)
  starting transfers between devices  19.2 us (7%)
  local copies, waits for them, and re-layouts  18.2 us (7%)
  other arithmetic  6.93 us (3%)
    ppermute x12, waiting for transfers between devices, swap(): return lax.ppermute(value, 'feed', pairs)  63.7 us
    all_to_all x2, waiting for transfers between devices, through_rows(): lax.all_to_all(coded, 'feed', split_axis=0, concat_axis=0, tiled=True)  62.8 us
    pallas_call x2, Pallas kernels, row_products(): pl.pallas_call(rows_kernel, grid=(2 * steps,), in_specs=[pl.BlockSpec((ma...  41.3 us
    pallas_call x2, Pallas kernels, finish(): pl.pallas_call(functools.partial(finish_kernel, scale), grid=(1,), in_spe...  30.5 us
    pallas_call x1, Pallas kernels, own_spectra(): pl.pallas_call(own_kernel, grid=(spectra // (STEPS * STEP),), in_specs=[p...  12.2 us
    unnamed x18, local copies, waits for them, and re-layouts  12.2 us
    all_to_all x2, starting transfers between devices, through_rows(): lax.all_to_all(coded, 'feed', split_axis=0, concat_axis=0, tiled=True)  11.7 us
    ppermute x12, starting transfers between devices, swap(): return lax.ppermute(value, 'feed', pairs)  7.47 us
  transfers between devices with their start and end apart: 14, of which 10 were waited for; matrix products, arithmetic and copies ran while one was open for 1% of the time, Pallas kernels for 19%

profile of v3, /device:TPU:13, one launch (start us, length us, event | category | flops | bytes accessed | tf_op | source)
XLA Modules:
  0.0 257.7 jit_solution(14567641939151331718)
XLA Ops:
  0.0 0.8 fusion.1
  0.9 0.7 slice_subtract_fusion
  1.6 3.4 %copy-done.3 = s32[256,16,519]{0,1,2:T(8,128)S(1)} copy-done((s32[256,16,519]{0,1,2:T(8,128)S(1)}, s32[256,16,519]{0,1,2:T(8,128)}, u32[]{:S(2)}) %copy-start.3) | copy-done | bytes 8503320
  5.0 2.6 %select_rows.1 = bf16[8448,256]{1,0:T(8,128)(2,1)S(1)} custom-call(s32[1,256]{1,0:T(1,128)S(1)} %bitcast.18, s32[8304,256]{1,0:T(8,128)S(1)} %bitcast.16, bf16[64,256]{1,0:T(8,128)(2,1)S(1)} %pad_maximum_fusion.1.parts_ref), custom_call_target="tpu_custom_call" | custom-call | tf_op jit(solution)/shard_map/select_rows/pallas_call | solution.py:301
  7.6 1.6 constant_dynamic-slice_fusion.4
  9.2 1.1 copy-done
  10.3 0.7 collective-permute-start
  11.0 4.1 %collective-permute-done = bf16[4224,256]{1,0:T(8,128)(2,1)S(1)} collective-permute-done((bf16[4224,256]{1,0:T(8,128)(2,1)}, bf16[4224,256]{1,0:T(8,128)(2,1)S(1)}, u32[]{:S(2)}, u32[]{:S(2)}) %collective-permute-start) | collective-permute-done | bytes 2162720 | tf_op jit(solution)/shard_map/ppermute | solution.py:318
  15.1 2.2 dynamic-slice_add_fusion
  17.2 1.1 fusion
  18.4 1.1 constant_dynamic-slice_fusion.1
  19.5 0.2 collective-permute-start.6
  19.7 0.1 collective-permute-start.1
  19.9 13.1 %collective-permute-done.6 = bf16[1056,256]{1,0:T(8,128)(2,1)S(1)} collective-permute-done((bf16[1056,256]{1,0:T(8,128)(2,1)S(1)}, bf16[1056,256]{1,0:T(8,128)(2,1)S(1)}, u32[]{:S(2)}, u32[]{:S(2)}) %collective-permute-start.6) | collective-permute-done | bytes 540704 | tf_op jit(solution)/shard_map/ppermute | solution.py:318
  33.0 1.2 dynamic-slice_add_fusion.1
  34.3 0.2 collective-permute-start.7
  34.5 0.1 dynamic-slice_add_fusion.2
  34.7 0.4 collective-permute-start.2
  35.1 6.0 %collective-permute-done.7 = bf16[528,256]{1,0:T(8,128)(2,1)S(1)} collective-permute-done((bf16[528,256]{1,0:T(8,128)(2,1)S(1)}, bf16[528,256]{1,0:T(8,128)(2,1)S(1)}, u32[]{:S(2)}, u32[]{:S(2)}) %collective-permute-start.7) | collective-permute-done | bytes 270368 | tf_op jit(solution)/shard_map/ppermute | solution.py:318
  41.2 2.4 collective-permute-start.8
  43.6 0.1 dynamic-slice_add_fusion.4
  43.6 0.1 collective-permute-start.3
  43.8 17.4 %collective-permute-done.8 = bf16[528,256]{1,0:T(8,128)(2,1)S(1)} collective-permute-done((bf16[528,256]{1,0:T(8,128)(2,1)S(1)}, bf16[528,256]{1,0:T(8,128)(2,1)S(1)}, u32[]{:S(2)}, u32[]{:S(2)}) %collective-permute-start.8) | collective-permute-done | bytes 270368 | tf_op jit(solution)/shard_map/ppermute | solution.py:318
  61.2 0.1 constant_dynamic-update-slice_fusion.5
  61.2 0.4 collective-permute-start.9
  61.6 5.4 %collective-permute-done.3 = bf16[528,256]{1,0:T(8,128)(2,1)S(1)} collective-permute-done((bf16[528,256]{1,0:T(8,128)(2,1)S(1)}, bf16[528,256]{1,0:T(8,128)(2,1)S(1)}, u32[]{:S(2)}, u32[]{:S(2)}) %collective-permute-start.3) | collective-permute-done | bytes 270368 | tf_op jit(solution)/shard_map/ppermute | solution.py:318
  67.0 0.1 collective-permute-start.4
  67.2 1.6 collective-permute-done.9
  68.9 5.8 %collective-permute-done.4 = bf16[528,256]{1,0:T(8,128)(2,1)S(1)} collective-permute-done((bf16[528,256]{1,0:T(8,128)(2,1)S(1)}, bf16[528,256]{1,0:T(8,128)(2,1)S(1)}, u32[]{:S(2)}, u32[]{:S(2)}) %collective-permute-start.4) | collective-permute-done | bytes 270368 | tf_op jit(solution)/shard_map/ppermute | solution.py:318
  74.7 0.4 collective-permute-start.5
  75.0 0.8 constant_dynamic-update-slice_fusion.3
  75.9 10.3 %collective-permute-done.10 = bf16[1056,256]{1,0:T(8,128)(2,1)S(1)} collective-permute-done((bf16[1056,256]{1,0:T(8,128)(2,1)S(1)}, bf16[1056,256]{1,0:T(8,128)(2,1)S(1)}, u32[]{:S(2)}, u32[]{:S(2)}) %collective-permute-start.10) | collective-permute-done | bytes 540704 | tf_op jit(solution)/shard_map/ppermute | solution.py:318
  86.2 0.8 constant_dynamic-update-slice_fusion.2
  87.2 1.6 pad_maximum_fusion
  88.8 2.4 collective-permute-start.11
  91.2 12.2 %own_spectra.1.own_ref = bf16[16,1024,256]{2,1,0:T(8,128)(2,1)S(1)} custom-call(s32[8304,256]{1,0:T(8,128)} %bitcast.14, s32[8304,256]{1,0:T(8,128)} %bitcast.15, f32[32,256]{1,0:T(8,128)S(1)} %bitcast.17, bf16[4,256,256]{2,1,0:T(8,128)(2,1)S(1)} %copy-done.5), custom_call_target="tpu_custom_call" | custom-call | tf_op jit(solution)/shard_map/own_spectra/pallas_call | solution.py:262
  103.4 3.4 %copy-done.4 = bf16[16,1024,256]{2,1,0:T(8,128)(2,1)} copy-done((bf16[16,1024,256]{2,1,0:T(8,128)(2,1)}, bf16[16,1024,256]{2,1,0:T(8,128)(2,1)S(1)}, u32[]{:S(2)}) %copy-start.4) | copy-done | bytes 8388632
  106.8 0.3 constant_dynamic-update-slice_fusion.main_ref.next_ref
  107.1 20.7 %row_products.3 = s16[16,272,256]{2,1,0:T(8,128)(2,1)} custom-call(bf16[8448,256]{1,0:T(8,128)(2,1)S(1)} %constant_dynamic-update-slice_fusion.main_ref.next_ref, bf16[8448,256]{1,0:T(8,128)(2,1)S(1)} %constant_dynamic-update-slice_fusion.main_ref.next_ref, bf16[64,256]{1,0:T(8,128)(2,1)S(1)} %slice.18.parts_ref, bf16[4,256,256]{2,1,0:T(8,128)(2,1)S(1)} %copy-done.5, ...), custom_call_target="tpu_custom_call" | custom-call | tf_op jit(solution)/shard_map/row_products/pallas_call | solution.py:395
  127.8 2.0 copy-done.1
  129.8 6.8 %all-to-all-start.1 = ((s16[16,272,256]{2,1,0:T(8,128)(2,1)}), s16[16,272,256]{2,1,0:T(8,128)(2,1)S(1)}, u32[]{:S(2)}, u32[]{:S(2)}) async-start(s16[16,272,256]{2,1,0:T(8,128)(2,1)} %row_products.3), calls=%async_computation.1 | async-start | bytes 4456448 | tf_op jit(solution)/shard_map/all_to_all | solution.py:487
  136.6 2.2 copy-done.2
  138.8 20.6 %row_products.2 = s16[16,272,256]{2,1,0:T(8,128)(2,1)} custom-call(bf16[8448,256]{1,0:T(8,128)(2,1)S(1)} %copy-done.2, bf16[8448,256]{1,0:T(8,128)(2,1)S(1)} %copy-done.2, bf16[64,256]{1,0:T(8,128)(2,1)S(1)} %slice.18.parts_ref, bf16[4,256,256]{2,1,0:T(8,128)(2,1)S(1)} %copy-done.5, bf16[16,1024,256]{2,1,0:T(8,128)(2,1)} %copy-done.4), custom_call_target="tpu_custom_call" | custom-call | tf_op jit(solution)/shard_map/row_products/pallas_call | solution.py:395
  159.5 27.4 %all-to-all-done.1.coded_ref = s16[16,272,256]{2,1,0:T(8,128)(2,1)S(1)} async-done(((s16[16,272,256]{2,1,0:T(8,128)(2,1)}), s16[16,272,256]{2,1,0:T(8,128)(2,1)S(1)}, u32[]{:S(2)}, u32[]{:S(2)}) %all-to-all-start.1) | async-done | bytes 2228256 | tf_op jit(solution)/shard_map/all_to_all | solution.py:487
  186.8 4.9 %all-to-all-start = ((s16[16,272,256]{2,1,0:T(8,128)(2,1)}), s16[16,272,256]{2,1,0:T(8,128)(2,1)}, u32[]{:S(2)}, u32[]{:S(2)}) async-start(s16[16,272,256]{2,1,0:T(8,128)(2,1)} %row_products.2), calls=%async_computation | async-start | bytes 4456448 | tf_op jit(solution)/shard_map/all_to_all | solution.py:487
  191.7 14.8 %finish.2.refs_0_ = f32[16384,128]{1,0:T(8,128)} custom-call(s32[4096]{0:T(1024)S(1)} %copy-done.6, s16[16,272,256]{2,1,0:T(8,128)(2,1)S(1)} %all-to-all-done.1.coded_ref), custom_call_target="tpu_custom_call" | custom-call | tf_op jit(solution)/shard_map/finish/pallas_call | solution.py:449
  206.6 35.5 %all-to-all-done.coded_ref = s16[16,272,256]{2,1,0:T(8,128)(2,1)} async-done(((s16[16,272,256]{2,1,0:T(8,128)(2,1)}), s16[16,272,256]{2,1,0:T(8,128)(2,1)}, u32[]{:S(2)}, u32[]{:S(2)}) %all-to-all-start) | async-done | bytes 2228256 | tf_op jit(solution)/shard_map/all_to_all | solution.py:487
  242.1 15.7 %finish.3 = f32[16384,128]{1,0:T(8,128)} custom-call(s32[4096]{0:T(1024)S(1)} %copy-done.6, s16[16,272,256]{2,1,0:T(8,128)(2,1)} %all-to-all-done.coded_ref, f32[16384,128]{1,0:T(8,128)} %finish.2.refs_0_), custom_call_target="tpu_custom_call", output_to_operand_aliasing={{}: (2, {})} | custom-call | tf_op jit(solution)/shard_map/finish/pallas_call | solution.py:449
  (30 shorter events, 0.5 us)
Async XLA Ops:
  1.6 3.4 %copy-start.3 = (s32[256,16,519]{0,1,2:T(8,128)S(1)}, s32[256,16,519]{0,1,2:T(8,128)}, u32[]{:S(2)}) copy-start(s32[256,16,519]{0,1,2:T(8,128)} %param.4) | copy-start | bytes 25509892
  7.6 2.7 %copy-start = (bf16[8448,256]{1,0:T(8,128)(2,1)}, bf16[8448,256]{1,0:T(8,128)(2,1)S(1)}, u32[]{:S(2)}) copy-start(bf16[8448,256]{1,0:T(8,128)(2,1)S(1)} %select_rows.1) | copy-start | bytes 12976132
  10.3 4.8 %collective-permute-start = (bf16[4224,256]{1,0:T(8,128)(2,1)}, bf16[4224,256]{1,0:T(8,128)(2,1)S(1)}, u32[]{:S(2)}, u32[]{:S(2)}) collective-permute-start(bf16[4224,256]{1,0:T(8,128)(2,1)} %constant_dynamic-slice_fusion.4), channel_id=1, source_target_pairs={{0,1},{1,0},{2,3},{3,2},{4,5},{5,4},{6,7},{7,6},{8,9},{9,8},{10,11... | collective-permute-start | bytes 6488072 | tf_op jit(solution)/shard_map/ppermute | solution.py:318
  19.5 13.6 %collective-permute-start.6 = (bf16[1056,256]{1,0:T(8,128)(2,1)S(1)}, bf16[1056,256]{1,0:T(8,128)(2,1)S(1)}, u32[]{:S(2)}, u32[]{:S(2)}) collective-permute-start(bf16[1056,256]{1,0:T(8,128)(2,1)S(1)} %constant_dynamic-slice_fusion.1), channel_id=1, source_target_pairs={{0,4},{1,5},{2,6},{3,7},{4,0},{5,1},{6,2},{7,3},{8,12},{9,13},{10,... | collective-permute-start | bytes 1622024 | tf_op jit(solution)/shard_map/ppermute | solution.py:318
  19.7 14.8 %collective-permute-start.1 = (bf16[1056,256]{1,0:T(8,128)(2,1)S(1)}, bf16[1056,256]{1,0:T(8,128)(2,1)S(1)}, u32[]{:S(2)}, u32[]{:S(2)}) collective-permute-start(bf16[1056,256]{1,0:T(8,128)(2,1)S(1)} %constant_dynamic-slice_fusion.3), channel_id=1, source_target_pairs={{0,2},{1,3},{2,0},{3,1},{4,6},{5,7},{6,4},{7,5},{8,10},{9,11},{10,... | collective-permute-start | bytes 1622024 | tf_op jit(solution)/shard_map/ppermute | solution.py:318
  33.0 54.1 %slice-start = ((s8[4325376]{0:T(1024)(128)(4,1)}), s8[131072]{0:T(1024)(128)(4,1)S(1)}, s32[]{:S(2)}) async-start(s8[4325376]{0:T(1024)(128)(4,1)} %bitcast.12), calls=%async_computation.2 | async-start | bytes 262144
  34.3 6.8 %collective-permute-start.7 = (bf16[528,256]{1,0:T(8,128)(2,1)S(1)}, bf16[528,256]{1,0:T(8,128)(2,1)S(1)}, u32[]{:S(2)}, u32[]{:S(2)}) collective-permute-start(bf16[528,256]{1,0:T(8,128)(2,1)S(1)} %constant_dynamic-slice_fusion), channel_id=1, source_target_pairs={{0,2},{1,3},{2,0},{3,1},{4,6},{5,7},{6,4},{7,5},{8,10},{9,11},{10,... | collective-permute-start | bytes 811016 | tf_op jit(solution)/shard_map/ppermute | solution.py:318
  34.7 8.9 %collective-permute-start.2 = (bf16[528,256]{1,0:T(8,128)(2,1)S(1)}, bf16[528,256]{1,0:T(8,128)(2,1)S(1)}, u32[]{:S(2)}, u32[]{:S(2)}) collective-permute-start(bf16[528,256]{1,0:T(8,128)(2,1)S(1)} %constant_dynamic-slice_fusion.2), channel_id=1, source_target_pairs={{0,4},{1,5},{2,6},{3,7},{4,0},{5,1},{6,2},{7,3},{8,12},{9,13},{10,... | collective-permute-start | bytes 811016 | tf_op jit(solution)/shard_map/ppermute | solution.py:318
  41.2 20.0 %collective-permute-start.8 = (bf16[528,256]{1,0:T(8,128)(2,1)S(1)}, bf16[528,256]{1,0:T(8,128)(2,1)S(1)}, u32[]{:S(2)}, u32[]{:S(2)}) collective-permute-start(bf16[528,256]{1,0:T(8,128)(2,1)S(1)} %dynamic-slice_add_fusion.3), channel_id=1, source_target_pairs={{0,8},{1,9},{2,10},{3,11},{4,12},{5,13},{6,14},{7,15},{8,0},{9,1},... | collective-permute-start | bytes 811016 | tf_op jit(solution)/shard_map/ppermute | solution.py:318
  43.6 43.5 %slice-start.1 = ((s8[4325376]{0:T(1024)(128)(4,1)}), s8[4194304]{0:T(1024)(128)(4,1)S(1)}, s32[]{:S(2)}) async-start(s8[4325376]{0:T(1024)(128)(4,1)} %bitcast.12), calls=%async_computation.3 | async-start | bytes 8388608
  43.6 23.3 %collective-permute-start.3 = (bf16[528,256]{1,0:T(8,128)(2,1)S(1)}, bf16[528,256]{1,0:T(8,128)(2,1)S(1)}, u32[]{:S(2)}, u32[]{:S(2)}) collective-permute-start(bf16[528,256]{1,0:T(8,128)(2,1)S(1)} %dynamic-slice_add_fusion.4), channel_id=1, source_target_pairs={{0,8},{1,9},{2,10},{3,11},{4,12},{5,13},{6,14},{7,15},{8,0},{9,1},... | collective-permute-start | bytes 811016 | tf_op jit(solution)/shard_map/ppermute | solution.py:318
  61.2 7.5 %collective-permute-start.9 = (bf16[528,256]{1,0:T(8,128)(2,1)S(1)}, bf16[528,256]{1,0:T(8,128)(2,1)S(1)}, u32[]{:S(2)}, u32[]{:S(2)}) collective-permute-start(bf16[528,256]{1,0:T(8,128)(2,1)S(1)} %get-tuple-element.8), channel_id=1, source_target_pairs={{0,2},{1,3},{2,0},{3,1},{4,6},{5,7},{6,4},{7,5},{8,10},{9,11},{10,... | collective-permute-start | bytes 811016 | tf_op jit(solution)/shard_map/ppermute | solution.py:318
  67.0 7.6 %collective-permute-start.4 = (bf16[528,256]{1,0:T(8,128)(2,1)S(1)}, bf16[528,256]{1,0:T(8,128)(2,1)S(1)}, u32[]{:S(2)}, u32[]{:S(2)}) collective-permute-start(bf16[528,256]{1,0:T(8,128)(2,1)S(1)} %get-tuple-element.6), channel_id=1, source_target_pairs={{0,4},{1,5},{2,6},{3,7},{4,0},{5,1},{6,2},{7,3},{8,12},{9,13},{10,... | collective-permute-start | bytes 811016 | tf_op jit(solution)/shard_map/ppermute | solution.py:318
  68.8 17.5 %collective-permute-start.10 = (bf16[1056,256]{1,0:T(8,128)(2,1)S(1)}, bf16[1056,256]{1,0:T(8,128)(2,1)S(1)}, u32[]{:S(2)}, u32[]{:S(2)}) collective-permute-start(bf16[1056,256]{1,0:T(8,128)(2,1)S(1)} %constant_dynamic-update-slice_fusion.4), channel_id=1, source_target_pairs={{0,4},{1,5},{2,6},{3,7},{4,0},{5,1},{6,2},{7,3},{8,12},{9,13},{10,... | collective-permute-start | bytes 1622024 | tf_op jit(solution)/shard_map/ppermute | solution.py:318
  74.7 12.4 %collective-permute-start.5 = (bf16[1056,256]{1,0:T(8,128)(2,1)S(1)}, bf16[1056,256]{1,0:T(8,128)(2,1)S(1)}, u32[]{:S(2)}, u32[]{:S(2)}) collective-permute-start(bf16[1056,256]{1,0:T(8,128)(2,1)S(1)} %constant_dynamic-update-slice_fusion.8), channel_id=1, source_target_pairs={{0,2},{1,3},{2,0},{3,1},{4,6},{5,7},{6,4},{7,5},{8,10},{9,11},{10,... | collective-permute-start | bytes 1622024 | tf_op jit(solution)/shard_map/ppermute | solution.py:318
  87.2 4.0 %copy-start.5 = (bf16[4,256,256]{2,1,0:T(8,128)(2,1)S(1)}, bf16[4,256,256]{2,1,0:T(8,128)(2,1)}, u32[]{:S(2)}) copy-start(bf16[4,256,256]{2,1,0:T(8,128)(2,1)} %constant.142.clone.weights_ref) | copy-start | bytes 1572868
  88.8 18.0 %collective-permute-start.11 = (bf16[4224,256]{1,0:T(8,128)(2,1)S(1)}, bf16[4224,256]{1,0:T(8,128)(2,1)S(1)}, u32[]{:S(2)}, u32[]{:S(2)}) collective-permute-start(bf16[4224,256]{1,0:T(8,128)(2,1)S(1)} %get-tuple-element.9), channel_id=1, source_target_pairs={{0,1},{1,0},{2,3},{3,2},{4,5},{5,4},{6,7},{7,6},{8,9},{9,8},{10,11... | collective-permute-start | bytes 6488072 | tf_op jit(solution)/shard_map/ppermute | solution.py:318
  103.4 3.4 %copy-start.4 = (bf16[16,1024,256]{2,1,0:T(8,128)(2,1)}, bf16[16,1024,256]{2,1,0:T(8,128)(2,1)S(1)}, u32[]{:S(2)}) copy-start(bf16[16,1024,256]{2,1,0:T(8,128)(2,1)S(1)} %own_spectra.1.own_ref) | copy-start | bytes 25165828
  127.8 2.0 copy-start.1
  129.8 57.0 %all-to-all-start.1 = ((s16[16,272,256]{2,1,0:T(8,128)(2,1)}), s16[16,272,256]{2,1,0:T(8,128)(2,1)S(1)}, u32[]{:S(2)}, u32[]{:S(2)}) async-start(s16[16,272,256]{2,1,0:T(8,128)(2,1)} %row_products.3), calls=%async_computation.1 | async-start | bytes 4456448 | tf_op jit(solution)/shard_map/all_to_all | solution.py:487
  136.6 2.2 copy-start.2
  159.5 32.3 %copy-start.6 = (s32[4096]{0:T(1024)S(1)}, s32[4096]{0:T(1024)}, u32[]{:S(2)}) copy-start(s32[4096]{0:T(1024)} %slot_ref.3) | copy-start | bytes 49156
  186.8 55.2 %all-to-all-start = ((s16[16,272,256]{2,1,0:T(8,128)(2,1)}), s16[16,272,256]{2,1,0:T(8,128)(2,1)}, u32[]{:S(2)}, u32[]{:S(2)}) async-start(s16[16,272,256]{2,1,0:T(8,128)(2,1)} %row_products.2), calls=%async_computation | async-start | bytes 4456448 | tf_op jit(solution)/shard_map/all_to_all | solution.py:487

commit v4 on v3

--- a/solution.py
+++ b/solution.py
@@ -222,19 +222,27 @@
 
 def spectra_of(weights_ref, levels, gains, ch, store):
     count = levels[0].shape[1]
-    for b in range(STEPS):
-        spot = slice(b * STEP * ch, b * STEP * ch + SPAN * ch)
+    beside = max(1, 256 // count)
+    for first in range(0, STEPS, beside):
         total = None
         for part in range(2):
-            slab = levels[part][spot]
+            slabs = [levels[part][b * STEP * ch : (b * STEP + SPAN) * ch] for b in range(first, first + beside)]
+            slab = jnp.concatenate(slabs, axis=1) if beside > 1 else slabs[0]
             for split in range(2):
                 term = jnp.dot(weights_ref[2 * split + part], slab, preferred_element_type=jnp.float32)
                 total = term if total is None else total + term
-        for c in range(ch):
-            real = total[c * 2 * STEP : c * 2 * STEP + STEP]
-            imag = total[c * 2 * STEP + STEP : (c + 1) * 2 * STEP]
-            gain_real, gain_imag = gains[c : c + 1], gains[ch + c : ch + c + 1]
-            store(b, c, gain_real * real - gain_imag * imag, gain_real * imag + gain_imag * real)
+        for index in range(beside):
+            mine = total[:, index * count : (index + 1) * count]
+            for c in range(ch):
+                real = mine[c * 2 * STEP : c * 2 * STEP + STEP]
+                imag = mine[c * 2 * STEP + STEP : (c + 1) * 2 * STEP]
+                gain_real, gain_imag = gains[c : c + 1], gains[ch + c : ch + c + 1]
+                store(
+                    first + index,
+                    c,
+                    gain_real * real - gain_imag * imag,
+                    gain_real * imag + gain_imag * real,
+                )
 
 
 def levels_of(words):
@@ -244,16 +252,16 @@
     ]
 
 
-def own_kernel(main_ref, next_ref, gains_ref, weights_ref, out_ref):
+def own_kernel(main_ref, next_ref, gains_ref, weights_ref, out_ref, held):
     ch = out_ref.shape[0]
     words = jnp.concatenate([main_ref[...], next_ref[...]], axis=0)
 
     def store(b, c, real, imag):
-        out_ref[c, b * 2 * STEP : (b + 1) * 2 * STEP, :] = jnp.concatenate([real, imag], axis=0).astype(
-            out_ref.dtype
-        )
+        held[c, b * 2 * STEP : (b + 1) * 2 * STEP, :] = jnp.concatenate([real, imag], axis=0).astype(held.dtype)
 
     spectra_of(weights_ref, levels_of(words), gains_ref[...], ch, store)
+    for c in range(ch):
+        out_ref[c] = held[c].T
 
 
 def own_spectra(words, gains, weights, ch, spectra):
@@ -268,9 +276,15 @@
             pl.BlockSpec(gains.shape, lambda i: (0, 0)),
             pl.BlockSpec(weights.shape, lambda i: (0, 0, 0)),
         ],
-        out_specs=pl.BlockSpec((ch, 2 * STEPS * STEP, count), lambda i: (0, i, 0)),
-        out_shape=jax.ShapeDtypeStruct((ch, 2 * spectra, count), jnp.bfloat16),
+        out_specs=pl.BlockSpec((ch, count, 2 * STEPS * STEP), lambda i: (0, 0, i)),
+        out_shape=jax.ShapeDtypeStruct((ch, count, 2 * spectra), jnp.bfloat16),
+        scratch_shapes=[pltpu.VMEM((ch, 2 * STEPS * STEP, count), jnp.bfloat16)],
         compiler_params=pltpu.CompilerParams(vmem_limit_bytes=40 << 20),
+        cost_estimate=pl.CostEstimate(
+            flops=8 * spectra * ch * 2 * SPAN * ch * count,
+            bytes_accessed=4 * words.size + 4 * ch * spectra * count,
+            transcendentals=0,
+        ),
         name="own_spectra",
     )(words, words, gains, weights)
 
@@ -371,11 +385,8 @@
     def _():
         each = own_ref.shape[0]
         for index in range(each):
-            products = lax.dot_general(
-                own_ref[index],
-                left[(step - steps) * each + index],
-                (((0,), (0,)), ((), ())),
-                preferred_element_type=jnp.float32,
+            products = jnp.dot(
+                own_ref[index], left[(step - steps) * each + index], preferred_element_type=jnp.float32
             )
             count = products.shape[0]
             largest = jnp.maximum(jnp.max(jnp.abs(products), axis=0, keepdims=True), 2.0**-60)
@@ -387,7 +398,7 @@
 
 
 def row_products(words, parts, own, weights, index):
-    ch, width, count = own.shape
+    ch, count, width = own.shape
     rows = LANES
     main = STEPS * STEP * ch
     steps = width // (2 * STEPS * STEP)
@@ -400,19 +411,23 @@
             pl.BlockSpec((STEP * ch, rows), lambda i: ((jnp.minimum(i, steps - 1) + 1) * STEPS, index)),
             pl.BlockSpec((parts.shape[0], rows), lambda i: (0, index)),
             pl.BlockSpec(weights.shape, lambda i: (0, 0, 0)),
-            pl.BlockSpec((each, width, count), lambda i: (jnp.maximum(i - steps, 0), 0, 0)),
+            pl.BlockSpec((each, count, width), lambda i: (jnp.maximum(i - steps, 0), 0, 0)),
         ],
         out_specs=pl.BlockSpec((each, count + 16, 2 * rows), lambda i: (jnp.maximum(i - steps, 0), 0, 0)),
         out_shape=jax.ShapeDtypeStruct((ch, count + 16, 2 * rows), jnp.int16),
         scratch_shapes=[pltpu.VMEM((ch, width, 2 * rows), jnp.bfloat16)],
         compiler_params=pltpu.CompilerParams(vmem_limit_bytes=40 << 20),
+        cost_estimate=pl.CostEstimate(
+            flops=8 * width * ch * SPAN * ch * rows + 4 * ch * width * rows * count,
+            bytes_accessed=2 * words.size + 2 * own.size + 4 * ch * rows * count,
+            transcendentals=0,
+        ),
         name="row_products",
     )(words, words, parts, weights, own)
 
 
 def finish_kernel(scale, slot_ref, coded_ref, *refs):
-    out_ref, products, tile = refs[-3:]
-    step = pl.program_id(0)
+    out_ref, products, tile, mixed = refs[-4:]
     sources, lines, width = coded_ref.shape
     count = lines - 16
     pieces = width // LANES
@@ -426,18 +441,21 @@
                 :, piece * LANES : (piece + 1) * LANES
             ]
 
-    @pl.loop(0, feeds // LANES)
+    together = 8 // pieces
+
+    @pl.loop(0, feeds // LANES // together)
     def _(j):
-        @pl.loop(0, LANES, unroll=16)
-        def _(i):
-            slot = slot_ref[j * LANES + i]
-            tile[pl.ds(pl.multiple_of(i * pieces, pieces), pieces), :] = products[
-                pl.ds(pl.multiple_of(slot * pieces, pieces), pieces), :
-            ]
-
-        for piece in range(pieces):
-            turned = tile[pl.ds(piece, LANES, stride=pieces), :].T
-            out_ref[pl.ds(2 * j + piece, LANES, stride=columns), :] = turned
+        for part in range(together):
+            for i in range(LANES):
+                slot = slot_ref[(j * together + part) * LANES + i]
+                tile[i * pieces : (i + 1) * pieces, :] = products[
+                    pl.ds(pl.multiple_of(slot * pieces, pieces), pieces), :
+                ]
+            for piece in range(pieces):
+                turned = tile[pl.ds(piece, LANES, stride=pieces), :].T
+                mixed[pl.ds(part * pieces + piece, LANES, stride=8), :] = turned
+        for row in range(LANES):
+            out_ref[pl.ds(pl.multiple_of(row * columns + j * 8, 8), 8), :] = mixed[row * 8 : (row + 1) * 8, :]
 
 
 def finish(coded, feed_slot, index, pieces, scale, before):
@@ -459,6 +477,7 @@
         scratch_shapes=[
             pltpu.VMEM((feeds * width // LANES, LANES), jnp.float32),
             pltpu.VMEM((width, LANES), jnp.float32),
+            pltpu.VMEM((8 * LANES, LANES), jnp.float32),
         ],
         input_output_aliases={2: 0} if earlier else {},
         compiler_params=pltpu.CompilerParams(vmem_limit_bytes=40 << 20),

time: 259 us -> 254 us (0.981)
  Pallas kernels: 86.7 us -> 71.2 us
  waiting for transfers between devices: 127 us -> 135 us
  local copies, waits for them, and re-layouts: 18.2 us -> 20.9 us
    pallas_call x2, Pallas kernels: 30.5 us -> 19.3 us  [finish(): pl.pallas_call(functools.partial(finish_kernel, scale), grid=(1,), in_spe...]
    pallas_call x2, Pallas kernels: 41.3 us -> 32.9 us  [row_products(): pl.pallas_call(rows_kernel, grid=(2 * steps,), in_specs=[pl.BlockSpec((ma...]
    all_to_all x2, waiting for transfers between devices: 62.8 us -> 71.3 us  [through_rows(): lax.all_to_all(coded, 'feed', split_axis=0, concat_axis=0, tiled=True)]
    pallas_call x1, Pallas kernels: 12.2 us -> 16.4 us  [own_spectra(): pl.pallas_call(own_kernel, grid=(spectra // (STEPS * STEP),), in_specs=[p...]
    unnamed x18 -> x22, local copies, waits for them, and re-layouts: 12.2 us -> 14.9 us
  transfers between devices with their start and end apart: 14 -> 14, of which waited for: 10 -> 10; matrix products, arithmetic and copies ran while one was open for 1% -> 1% of each run, Pallas kernels for 19% -> 17%
where the time goes in v4:
time: 254 us; the launch traced here: 253 us
  waiting for transfers between devices  135 us (53%)
  Pallas kernels  71.2 us (28%)
  local copies, waits for them, and re-layouts  20.9 us (8%)
  starting transfers between devices  19.2 us (8%)
  other arithmetic  6.93 us (3%)
    all_to_all x2, waiting for transfers between devices, through_rows(): lax.all_to_all(coded, 'feed', split_axis=0, concat_axis=0, tiled=True)  71.3 us
    ppermute x12, waiting for transfers between devices, swap(): return lax.ppermute(value, 'feed', pairs)  63.7 us
    pallas_call x2, Pallas kernels, row_products(): pl.pallas_call(rows_kernel, grid=(2 * steps,), in_specs=[pl.BlockSpec((ma...  32.9 us
    pallas_call x2, Pallas kernels, finish(): pl.pallas_call(functools.partial(finish_kernel, scale), grid=(1,), in_spe...  19.3 us
    pallas_call x1, Pallas kernels, own_spectra(): pl.pallas_call(own_kernel, grid=(spectra // (STEPS * STEP),), in_specs=[p...  16.4 us
    unnamed x22, local copies, waits for them, and re-layouts  14.9 us
    all_to_all x2, starting transfers between devices, through_rows(): lax.all_to_all(coded, 'feed', split_axis=0, concat_axis=0, tiled=True)  11.7 us
    ppermute x12, starting transfers between devices, swap(): return lax.ppermute(value, 'feed', pairs)  7.49 us
  transfers between devices with their start and end apart: 14, of which 10 were waited for; matrix products, arithmetic and copies ran while one was open for 1% of the time, Pallas kernels for 17%

profile of v4, /device:TPU:13, one launch (start us, length us, event | category | flops | bytes accessed | tf_op | source)
XLA Modules:
  0.0 253.5 jit_solution(12149735922915380501)
XLA Ops:
  0.0 0.8 fusion.1
  0.9 0.7 slice_subtract_fusion
  1.6 3.4 %copy-done.3 = s32[256,16,519]{0,1,2:T(8,128)S(1)} copy-done((s32[256,16,519]{0,1,2:T(8,128)S(1)}, s32[256,16,519]{0,1,2:T(8,128)}, u32[]{:S(2)}) %copy-start.3) | copy-done | bytes 8503320
  5.0 2.6 %select_rows.1 = bf16[8448,256]{1,0:T(8,128)(2,1)S(1)} custom-call(s32[1,256]{1,0:T(1,128)S(1)} %bitcast.18, s32[8304,256]{1,0:T(8,128)S(1)} %bitcast.16, bf16[64,256]{1,0:T(8,128)(2,1)S(1)} %pad_maximum_fusion.1.parts_ref), custom_call_target="tpu_custom_call" | custom-call | tf_op jit(solution)/shard_map/select_rows/pallas_call | solution.py:315
  7.6 1.6 constant_dynamic-slice_fusion.4
  9.2 1.1 copy-done
  10.3 0.7 collective-permute-start
  11.0 4.1 %collective-permute-done = bf16[4224,256]{1,0:T(8,128)(2,1)S(1)} collective-permute-done((bf16[4224,256]{1,0:T(8,128)(2,1)}, bf16[4224,256]{1,0:T(8,128)(2,1)S(1)}, u32[]{:S(2)}, u32[]{:S(2)}) %collective-permute-start) | collective-permute-done | bytes 2162720 | tf_op jit(solution)/shard_map/ppermute | solution.py:332
  15.1 2.2 dynamic-slice_add_fusion
  17.2 1.1 fusion
  18.4 1.1 constant_dynamic-slice_fusion.1
  19.5 0.2 collective-permute-start.6
  19.7 0.1 collective-permute-start.1
  19.9 13.1 %collective-permute-done.6 = bf16[1056,256]{1,0:T(8,128)(2,1)S(1)} collective-permute-done((bf16[1056,256]{1,0:T(8,128)(2,1)S(1)}, bf16[1056,256]{1,0:T(8,128)(2,1)S(1)}, u32[]{:S(2)}, u32[]{:S(2)}) %collective-permute-start.6) | collective-permute-done | bytes 540704 | tf_op jit(solution)/shard_map/ppermute | solution.py:332
  33.0 1.2 dynamic-slice_add_fusion.1
  34.3 0.2 collective-permute-start.7
  34.5 0.1 dynamic-slice_add_fusion.2
  34.7 0.4 collective-permute-start.2
  35.1 6.0 %collective-permute-done.7 = bf16[528,256]{1,0:T(8,128)(2,1)S(1)} collective-permute-done((bf16[528,256]{1,0:T(8,128)(2,1)S(1)}, bf16[528,256]{1,0:T(8,128)(2,1)S(1)}, u32[]{:S(2)}, u32[]{:S(2)}) %collective-permute-start.7) | collective-permute-done | bytes 270368 | tf_op jit(solution)/shard_map/ppermute | solution.py:332
  41.2 2.4 collective-permute-start.8
  43.6 0.1 collective-permute-start.3
  43.8 17.4 %collective-permute-done.8 = bf16[528,256]{1,0:T(8,128)(2,1)S(1)} collective-permute-done((bf16[528,256]{1,0:T(8,128)(2,1)S(1)}, bf16[528,256]{1,0:T(8,128)(2,1)S(1)}, u32[]{:S(2)}, u32[]{:S(2)}) %collective-permute-start.8) | collective-permute-done | bytes 270368 | tf_op jit(solution)/shard_map/ppermute | solution.py:332
  61.2 0.4 collective-permute-start.9
  61.6 5.4 %collective-permute-done.3 = bf16[528,256]{1,0:T(8,128)(2,1)S(1)} collective-permute-done((bf16[528,256]{1,0:T(8,128)(2,1)S(1)}, bf16[528,256]{1,0:T(8,128)(2,1)S(1)}, u32[]{:S(2)}, u32[]{:S(2)}) %collective-permute-start.3) | collective-permute-done | bytes 270368 | tf_op jit(solution)/shard_map/ppermute | solution.py:332
  67.0 0.1 collective-permute-start.4
  67.2 1.6 collective-permute-done.9
  68.9 5.8 %collective-permute-done.4 = bf16[528,256]{1,0:T(8,128)(2,1)S(1)} collective-permute-done((bf16[528,256]{1,0:T(8,128)(2,1)S(1)}, bf16[528,256]{1,0:T(8,128)(2,1)S(1)}, u32[]{:S(2)}, u32[]{:S(2)}) %collective-permute-start.4) | collective-permute-done | bytes 270368 | tf_op jit(solution)/shard_map/ppermute | solution.py:332
  74.7 0.4 collective-permute-start.5
  75.0 0.8 constant_dynamic-update-slice_fusion.3
  75.9 10.3 %collective-permute-done.10 = bf16[1056,256]{1,0:T(8,128)(2,1)S(1)} collective-permute-done((bf16[1056,256]{1,0:T(8,128)(2,1)S(1)}, bf16[1056,256]{1,0:T(8,128)(2,1)S(1)}, u32[]{:S(2)}, u32[]{:S(2)}) %collective-permute-start.10) | collective-permute-done | bytes 540704 | tf_op jit(solution)/shard_map/ppermute | solution.py:332
  86.2 0.8 constant_dynamic-update-slice_fusion.2
  87.2 1.6 pad_maximum_fusion
  88.8 2.4 collective-permute-start.11
  91.2 16.4 %own_spectra.1.own_ref = bf16[16,256,1024]{2,1,0:T(8,128)(2,1)S(1)} custom-call(s32[8304,256]{1,0:T(8,128)} %bitcast.14, s32[8304,256]{1,0:T(8,128)} %bitcast.15, f32[32,256]{1,0:T(8,128)S(1)} %bitcast.17, bf16[4,256,256]{2,1,0:T(8,128)(2,1)S(1)} %copy-done.7), custom_call_target="tpu_custom_call" | custom-call | flops 8589934592 | bytes 16891904 | tf_op jit(solution)/shard_map/own_spectra/pallas_call | solution.py:270
  107.6 3.4 %copy-done.8 = bf16[16,256,1024]{2,1,0:T(8,128)(2,1)} copy-done((bf16[16,256,1024]{2,1,0:T(8,128)(2,1)}, bf16[16,256,1024]{2,1,0:T(8,128)(2,1)S(1)}, u32[]{:S(2)}) %copy-start.8) | copy-done | bytes 8388632
  111.0 0.3 constant_dynamic-update-slice_fusion.main_ref.next_ref
  111.3 16.5 %row_products.3 = s16[16,272,256]{2,1,0:T(8,128)(2,1)S(1)} custom-call(bf16[8448,256]{1,0:T(8,128)(2,1)S(1)} %constant_dynamic-update-slice_fusion.main_ref.next_ref, bf16[8448,256]{1,0:T(8,128)(2,1)S(1)} %constant_dynamic-update-slice_fusion.main_ref.next_ref, bf16[64,256]{1,0:T(8,128)(2,1)S(1)} %slice.18.parts_ref, bf16[4,256,256]{2,1,0:T(8,128)(2,1)S(1)} %copy-done.7, ...), custom_call_target="tpu_custom_call" | custom-call | flops 6442450944 | bytes 14811136 | tf_op jit(solution)/shard_map/row_products/pallas_call | solution.py:406
  127.8 2.0 copy-done.1
  129.8 1.4 copy-done.5
  131.2 6.8 %all-to-all-start.1 = ((s16[16,272,256]{2,1,0:T(8,128)(2,1)}), s16[16,272,256]{2,1,0:T(8,128)(2,1)S(1)}, u32[]{:S(2)}, u32[]{:S(2)}) async-start(s16[16,272,256]{2,1,0:T(8,128)(2,1)} %copy-done.5), calls=%async_computation.1 | async-start | bytes 4456448 | tf_op jit(solution)/shard_map/all_to_all | solution.py:506
  137.9 2.2 copy-done.2
  140.2 16.4 %row_products.2 = s16[16,272,256]{2,1,0:T(8,128)(2,1)S(1)} custom-call(bf16[8448,256]{1,0:T(8,128)(2,1)S(1)} %copy-done.2, bf16[8448,256]{1,0:T(8,128)(2,1)S(1)} %copy-done.2, bf16[64,256]{1,0:T(8,128)(2,1)S(1)} %slice.18.parts_ref, bf16[4,256,256]{2,1,0:T(8,128)(2,1)S(1)} %copy-done.7, bf16[16,256,1024]{2,1,0:T(8,128)(2,1)} %copy-done.8), custom_call_target="tpu_custom_call" | custom-call | flops 6442450944 | bytes 14811136 | tf_op jit(solution)/shard_map/row_products/pallas_call | solution.py:406
  156.6 1.4 copy-done.4
  158.0 30.2 %all-to-all-done.1.coded_ref = s16[16,272,256]{2,1,0:T(8,128)(2,1)S(1)} async-done(((s16[16,272,256]{2,1,0:T(8,128)(2,1)}), s16[16,272,256]{2,1,0:T(8,128)(2,1)S(1)}, u32[]{:S(2)}, u32[]{:S(2)}) %all-to-all-start.1) | async-done | bytes 2228256 | tf_op jit(solution)/shard_map/all_to_all | solution.py:506
  188.2 4.9 %all-to-all-start = ((s16[16,272,256]{2,1,0:T(8,128)(2,1)}), s16[16,272,256]{2,1,0:T(8,128)(2,1)}, u32[]{:S(2)}, u32[]{:S(2)}) async-start(s16[16,272,256]{2,1,0:T(8,128)(2,1)} %copy-done.4), calls=%async_computation | async-start | bytes 4456448 | tf_op jit(solution)/shard_map/all_to_all | solution.py:506
  193.1 9.2 %finish.2.refs_0_ = f32[16384,128]{1,0:T(8,128)} custom-call(s32[4096]{0:T(1024)S(1)} %copy-done.6, s16[16,272,256]{2,1,0:T(8,128)(2,1)S(1)} %all-to-all-done.1.coded_ref), custom_call_target="tpu_custom_call" | custom-call | tf_op jit(solution)/shard_map/finish/pallas_call | solution.py:467
  202.3 41.1 %all-to-all-done.coded_ref = s16[16,272,256]{2,1,0:T(8,128)(2,1)} async-done(((s16[16,272,256]{2,1,0:T(8,128)(2,1)}), s16[16,272,256]{2,1,0:T(8,128)(2,1)}, u32[]{:S(2)}, u32[]{:S(2)}) %all-to-all-start) | async-done | bytes 2228256 | tf_op jit(solution)/shard_map/all_to_all | solution.py:506
  243.4 10.1 %finish.3 = f32[16384,128]{1,0:T(8,128)} custom-call(s32[4096]{0:T(1024)S(1)} %copy-done.6, s16[16,272,256]{2,1,0:T(8,128)(2,1)} %all-to-all-done.coded_ref, f32[16384,128]{1,0:T(8,128)} %finish.2.refs_0_), custom_call_target="tpu_custom_call", output_to_operand_aliasing={{}: (2, {})} | custom-call | tf_op jit(solution)/shard_map/finish/pallas_call | solution.py:467
  (34 shorter events, 0.6 us)
Async XLA Ops:
  1.6 3.4 %copy-start.3 = (s32[256,16,519]{0,1,2:T(8,128)S(1)}, s32[256,16,519]{0,1,2:T(8,128)}, u32[]{:S(2)}) copy-start(s32[256,16,519]{0,1,2:T(8,128)} %param.4) | copy-start | bytes 25509892
  7.6 2.7 %copy-start = (bf16[8448,256]{1,0:T(8,128)(2,1)}, bf16[8448,256]{1,0:T(8,128)(2,1)S(1)}, u32[]{:S(2)}) copy-start(bf16[8448,256]{1,0:T(8,128)(2,1)S(1)} %select_rows.1) | copy-start | bytes 12976132
  10.3 4.8 %collective-permute-start = (bf16[4224,256]{1,0:T(8,128)(2,1)}, bf16[4224,256]{1,0:T(8,128)(2,1)S(1)}, u32[]{:S(2)}, u32[]{:S(2)}) collective-permute-start(bf16[4224,256]{1,0:T(8,128)(2,1)} %constant_dynamic-slice_fusion.4), channel_id=1, source_target_pairs={{0,1},{1,0},{2,3},{3,2},{4,5},{5,4},{6,7},{7,6},{8,9},{9,8},{10,11... | collective-permute-start | bytes 6488072 | tf_op jit(solution)/shard_map/ppermute | solution.py:332
  19.5 13.6 %collective-permute-start.6 = (bf16[1056,256]{1,0:T(8,128)(2,1)S(1)}, bf16[1056,256]{1,0:T(8,128)(2,1)S(1)}, u32[]{:S(2)}, u32[]{:S(2)}) collective-permute-start(bf16[1056,256]{1,0:T(8,128)(2,1)S(1)} %constant_dynamic-slice_fusion.1), channel_id=1, source_target_pairs={{0,4},{1,5},{2,6},{3,7},{4,0},{5,1},{6,2},{7,3},{8,12},{9,13},{10,... | collective-permute-start | bytes 1622024 | tf_op jit(solution)/shard_map/ppermute | solution.py:332
  19.7 14.8 %collective-permute-start.1 = (bf16[1056,256]{1,0:T(8,128)(2,1)S(1)}, bf16[1056,256]{1,0:T(8,128)(2,1)S(1)}, u32[]{:S(2)}, u32[]{:S(2)}) collective-permute-start(bf16[1056,256]{1,0:T(8,128)(2,1)S(1)} %constant_dynamic-slice_fusion.3), channel_id=1, source_target_pairs={{0,2},{1,3},{2,0},{3,1},{4,6},{5,7},{6,4},{7,5},{8,10},{9,11},{10,... | collective-permute-start | bytes 1622024 | tf_op jit(solution)/shard_map/ppermute | solution.py:332
  33.0 54.1 %slice-start = ((s8[4325376]{0:T(1024)(128)(4,1)}), s8[131072]{0:T(1024)(128)(4,1)S(1)}, s32[]{:S(2)}) async-start(s8[4325376]{0:T(1024)(128)(4,1)} %bitcast.12), calls=%async_computation.2 | async-start | bytes 262144
  34.3 6.8 %collective-permute-start.7 = (bf16[528,256]{1,0:T(8,128)(2,1)S(1)}, bf16[528,256]{1,0:T(8,128)(2,1)S(1)}, u32[]{:S(2)}, u32[]{:S(2)}) collective-permute-start(bf16[528,256]{1,0:T(8,128)(2,1)S(1)} %constant_dynamic-slice_fusion), channel_id=1, source_target_pairs={{0,2},{1,3},{2,0},{3,1},{4,6},{5,7},{6,4},{7,5},{8,10},{9,11},{10,... | collective-permute-start | bytes 811016 | tf_op jit(solution)/shard_map/ppermute | solution.py:332
  34.7 8.9 %collective-permute-start.2 = (bf16[528,256]{1,0:T(8,128)(2,1)S(1)}, bf16[528,256]{1,0:T(8,128)(2,1)S(1)}, u32[]{:S(2)}, u32[]{:S(2)}) collective-permute-start(bf16[528,256]{1,0:T(8,128)(2,1)S(1)} %constant_dynamic-slice_fusion.2), channel_id=1, source_target_pairs={{0,4},{1,5},{2,6},{3,7},{4,0},{5,1},{6,2},{7,3},{8,12},{9,13},{10,... | collective-permute-start | bytes 811016 | tf_op jit(solution)/shard_map/ppermute | solution.py:332
  41.2 20.0 %collective-permute-start.8 = (bf16[528,256]{1,0:T(8,128)(2,1)S(1)}, bf16[528,256]{1,0:T(8,128)(2,1)S(1)}, u32[]{:S(2)}, u32[]{:S(2)}) collective-permute-start(bf16[528,256]{1,0:T(8,128)(2,1)S(1)} %dynamic-slice_add_fusion.3), channel_id=1, source_target_pairs={{0,8},{1,9},{2,10},{3,11},{4,12},{5,13},{6,14},{7,15},{8,0},{9,1},... | collective-permute-start | bytes 811016 | tf_op jit(solution)/shard_map/ppermute | solution.py:332
  43.6 43.5 %slice-start.1 = ((s8[4325376]{0:T(1024)(128)(4,1)}), s8[4194304]{0:T(1024)(128)(4,1)S(1)}, s32[]{:S(2)}) async-start(s8[4325376]{0:T(1024)(128)(4,1)} %bitcast.12), calls=%async_computation.3 | async-start | bytes 8388608
  43.6 23.3 %collective-permute-start.3 = (bf16[528,256]{1,0:T(8,128)(2,1)S(1)}, bf16[528,256]{1,0:T(8,128)(2,1)S(1)}, u32[]{:S(2)}, u32[]{:S(2)}) collective-permute-start(bf16[528,256]{1,0:T(8,128)(2,1)S(1)} %dynamic-slice_add_fusion.4), channel_id=1, source_target_pairs={{0,8},{1,9},{2,10},{3,11},{4,12},{5,13},{6,14},{7,15},{8,0},{9,1},... | collective-permute-start | bytes 811016 | tf_op jit(solution)/shard_map/ppermute | solution.py:332
  61.2 7.5 %collective-permute-start.9 = (bf16[528,256]{1,0:T(8,128)(2,1)S(1)}, bf16[528,256]{1,0:T(8,128)(2,1)S(1)}, u32[]{:S(2)}, u32[]{:S(2)}) collective-permute-start(bf16[528,256]{1,0:T(8,128)(2,1)S(1)} %get-tuple-element.8), channel_id=1, source_target_pairs={{0,2},{1,3},{2,0},{3,1},{4,6},{5,7},{6,4},{7,5},{8,10},{9,11},{10,... | collective-permute-start | bytes 811016 | tf_op jit(solution)/shard_map/ppermute | solution.py:332
  67.0 7.6 %collective-permute-start.4 = (bf16[528,256]{1,0:T(8,128)(2,1)S(1)}, bf16[528,256]{1,0:T(8,128)(2,1)S(1)}, u32[]{:S(2)}, u32[]{:S(2)}) collective-permute-start(bf16[528,256]{1,0:T(8,128)(2,1)S(1)} %get-tuple-element.6), channel_id=1, source_target_pairs={{0,4},{1,5},{2,6},{3,7},{4,0},{5,1},{6,2},{7,3},{8,12},{9,13},{10,... | collective-permute-start | bytes 811016 | tf_op jit(solution)/shard_map/ppermute | solution.py:332
  68.8 17.5 %collective-permute-start.10 = (bf16[1056,256]{1,0:T(8,128)(2,1)S(1)}, bf16[1056,256]{1,0:T(8,128)(2,1)S(1)}, u32[]{:S(2)}, u32[]{:S(2)}) collective-permute-start(bf16[1056,256]{1,0:T(8,128)(2,1)S(1)} %constant_dynamic-update-slice_fusion.4), channel_id=1, source_target_pairs={{0,4},{1,5},{2,6},{3,7},{4,0},{5,1},{6,2},{7,3},{8,12},{9,13},{10,... | collective-permute-start | bytes 1622024 | tf_op jit(solution)/shard_map/ppermute | solution.py:332
  74.7 12.4 %collective-permute-start.5 = (bf16[1056,256]{1,0:T(8,128)(2,1)S(1)}, bf16[1056,256]{1,0:T(8,128)(2,1)S(1)}, u32[]{:S(2)}, u32[]{:S(2)}) collective-permute-start(bf16[1056,256]{1,0:T(8,128)(2,1)S(1)} %constant_dynamic-update-slice_fusion.8), channel_id=1, source_target_pairs={{0,2},{1,3},{2,0},{3,1},{4,6},{5,7},{6,4},{7,5},{8,10},{9,11},{10,... | collective-permute-start | bytes 1622024 | tf_op jit(solution)/shard_map/ppermute | solution.py:332
  87.2 4.0 %copy-start.7 = (bf16[4,256,256]{2,1,0:T(8,128)(2,1)S(1)}, bf16[4,256,256]{2,1,0:T(8,128)(2,1)}, u32[]{:S(2)}) copy-start(bf16[4,256,256]{2,1,0:T(8,128)(2,1)} %constant.142.clone.weights_ref) | copy-start | bytes 1572868
  88.8 22.2 %collective-permute-start.11 = (bf16[4224,256]{1,0:T(8,128)(2,1)S(1)}, bf16[4224,256]{1,0:T(8,128)(2,1)S(1)}, u32[]{:S(2)}, u32[]{:S(2)}) collective-permute-start(bf16[4224,256]{1,0:T(8,128)(2,1)S(1)} %get-tuple-element.9), channel_id=1, source_target_pairs={{0,1},{1,0},{2,3},{3,2},{4,5},{5,4},{6,7},{7,6},{8,9},{9,8},{10,11... | collective-permute-start | bytes 6488072 | tf_op jit(solution)/shard_map/ppermute | solution.py:332
  107.6 3.4 %copy-start.8 = (bf16[16,256,1024]{2,1,0:T(8,128)(2,1)}, bf16[16,256,1024]{2,1,0:T(8,128)(2,1)S(1)}, u32[]{:S(2)}) copy-start(bf16[16,256,1024]{2,1,0:T(8,128)(2,1)S(1)} %own_spectra.1.own_ref) | copy-start | bytes 25165828
  127.7 2.0 copy-start.1
  129.8 1.4 copy-start.5
  131.2 57.0 %all-to-all-start.1 = ((s16[16,272,256]{2,1,0:T(8,128)(2,1)}), s16[16,272,256]{2,1,0:T(8,128)(2,1)S(1)}, u32[]{:S(2)}, u32[]{:S(2)}) async-start(s16[16,272,256]{2,1,0:T(8,128)(2,1)} %copy-done.5), calls=%async_computation.1 | async-start | bytes 4456448 | tf_op jit(solution)/shard_map/all_to_all | solution.py:506
  137.9 2.2 copy-start.2
  156.6 1.4 copy-start.4
  158.0 35.1 %copy-start.6 = (s32[4096]{0:T(1024)S(1)}, s32[4096]{0:T(1024)}, u32[]{:S(2)}) copy-start(s32[4096]{0:T(1024)} %slot_ref.3) | copy-start | bytes 49156
  188.2 55.2 %all-to-all-start = ((s16[16,272,256]{2,1,0:T(8,128)(2,1)}), s16[16,272,256]{2,1,0:T(8,128)(2,1)}, u32[]{:S(2)}, u32[]{:S(2)}) async-start(s16[16,272,256]{2,1,0:T(8,128)(2,1)} %copy-done.4), calls=%async_computation | async-start | bytes 4456448 | tf_op jit(solution)/shard_map/all_to_all | solution.py:506

commit v5 on v4

--- a/solution.py
+++ b/solution.py
@@ -205,37 +205,44 @@
 
 def filter_weights(ch):
     taps = filter_taps(ch) * (0.125 / math.sqrt(ch) / 2048.0)
-    weights = np.zeros((ch, 2, STEP, 2, SPAN, ch))
-    angle = 2.0 * math.pi * (np.arange(ch)[:, None] * np.arange(ch)[None, :] % ch) / ch
+    half = ch // 2
+    weights = np.zeros((ch, STEP, SPAN, ch))
+    angle = 2.0 * math.pi * (np.arange(half + 1)[:, None] * np.arange(ch)[None, :] % ch) / ch
+    sums = np.concatenate([np.cos(angle), np.sin(angle[1:half])], axis=0)
     for spectrum in range(STEP):
         for t in range(TAPS):
-            cosine, sine = taps[t] * np.cos(angle), taps[t] * np.sin(angle)
-            weights[:, 0, spectrum, 0, spectrum + t] = cosine
-            weights[:, 0, spectrum, 1, spectrum + t] = sine
-            weights[:, 1, spectrum, 0, spectrum + t] = -sine
-            weights[:, 1, spectrum, 1, spectrum + t] = cosine
-    weights = weights.reshape(ch * 2 * STEP, 2, SPAN * ch)
+            weights[:, spectrum, spectrum + t] = taps[t] * sums
+    weights = weights.reshape(ch * STEP, SPAN * ch)
     high = weights.astype(jnp.bfloat16)
     low = (weights - high.astype(np.float64)).astype(jnp.bfloat16)
-    return np.stack([high[:, 0], high[:, 1], low[:, 0], low[:, 1]])
+    return np.concatenate([high, low])
 
 
 def spectra_of(weights_ref, levels, gains, ch, store):
     count = levels[0].shape[1]
+    half, size = ch // 2, ch * STEP
     beside = max(1, 256 // count)
     for first in range(0, STEPS, beside):
-        total = None
-        for part in range(2):
-            slabs = [levels[part][b * STEP * ch : (b * STEP + SPAN) * ch] for b in range(first, first + beside)]
+        totals = []
+        for level in levels:
+            slabs = [level[b * size : b * size + SPAN * ch] for b in range(first, first + beside)]
             slab = jnp.concatenate(slabs, axis=1) if beside > 1 else slabs[0]
-            for split in range(2):
-                term = jnp.dot(weights_ref[2 * split + part], slab, preferred_element_type=jnp.float32)
-                total = term if total is None else total + term
+            both = jnp.dot(weights_ref[...], slab, preferred_element_type=jnp.float32)
+            totals.append(both[:size] + both[size:])
         for index in range(beside):
-            mine = total[:, index * count : (index + 1) * count]
+            lanes = slice(index * count, (index + 1) * count)
+            parts = [
+                [total[d * STEP : (d + 1) * STEP, lanes] for d in range(ch)] for total in totals
+            ]
             for c in range(ch):
-                real = mine[c * 2 * STEP : c * 2 * STEP + STEP]
-                imag = mine[c * 2 * STEP + STEP : (c + 1) * 2 * STEP]
+                place = min(c, ch - c)
+                real, imag = parts[0][place], parts[1][place]
+                if c % half:
+                    sine_real, sine_imag = parts[0][half + place], parts[1][half + place]
+                    if c < half:
+                        real, imag = real + sine_imag, imag - sine_real
+                    else:
+                        real, imag = real - sine_imag, imag + sine_real
                 gain_real, gain_imag = gains[c : c + 1], gains[ch + c : ch + c + 1]
                 store(
                     first + index,
@@ -252,8 +259,9 @@
     ]
 
 
-def own_kernel(main_ref, next_ref, gains_ref, weights_ref, out_ref, held):
+def own_kernel(main_ref, next_ref, gains_ref, weights_ref, out_ref, zero_ref, held):
     ch = out_ref.shape[0]
+    zero_ref[...] = jnp.zeros_like(zero_ref)
     words = jnp.concatenate([main_ref[...], next_ref[...]], axis=0)
 
     def store(b, c, real, imag):
@@ -274,14 +282,20 @@
             pl.BlockSpec((main, count), lambda i: (i, 0)),
             pl.BlockSpec((STEP * ch, count), lambda i: ((i + 1) * STEPS, 0)),
             pl.BlockSpec(gains.shape, lambda i: (0, 0)),
-            pl.BlockSpec(weights.shape, lambda i: (0, 0, 0)),
-        ],
-        out_specs=pl.BlockSpec((ch, count, 2 * STEPS * STEP), lambda i: (0, 0, i)),
-        out_shape=jax.ShapeDtypeStruct((ch, count, 2 * spectra), jnp.bfloat16),
+            pl.BlockSpec(weights.shape, lambda i: (0, 0)),
+        ],
+        out_specs=[
+            pl.BlockSpec((ch, count, 2 * STEPS * STEP), lambda i: (0, 0, i)),
+            pl.BlockSpec((16, LANES), lambda i: (0, 0)),
+        ],
+        out_shape=[
+            jax.ShapeDtypeStruct((ch, count, 2 * spectra), jnp.bfloat16),
+            jax.ShapeDtypeStruct((16, LANES), jnp.bfloat16),
+        ],
         scratch_shapes=[pltpu.VMEM((ch, 2 * STEPS * STEP, count), jnp.bfloat16)],
-        compiler_params=pltpu.CompilerParams(vmem_limit_bytes=40 << 20),
+        compiler_params=pltpu.CompilerParams(vmem_limit_bytes=58 << 20),
         cost_estimate=pl.CostEstimate(
-            flops=8 * spectra * ch * 2 * SPAN * ch * count,
+            flops=4 * spectra * ch * 2 * SPAN * ch * count,
             bytes_accessed=4 * words.size + 4 * ch * spectra * count,
             transcendentals=0,
         ),
@@ -350,11 +364,11 @@
     return lax.dynamic_update_slice_in_dim(buffer, other, (1 - side(bit)) * size, 0)
 
 
-def sum_over_feed(value):
+def sum_over_feed(value, zero):
     half = reduce_half(value, 1)
     size = half.shape[0] // 2
     left, right = half[:size], half[size:]
-    left_1, right_1 = reduce_half(left, 2), reduce_half(right, 4)
+    left_1, right_1 = reduce_half(left, 2) + zero, reduce_half(right, 4)
     left_2, right_2 = reduce_half(left_1, 4), reduce_half(right_1, 2)
     left_3, right_3 = left_2 + swap(left_2, 8), right_2 + swap(right_2, 8)
     left_1, right_1 = gather_half(left_3, 4, left_1), gather_half(right_3, 2, right_1)
@@ -410,15 +424,15 @@
             pl.BlockSpec((main, rows), lambda i: (jnp.minimum(i, steps - 1), index)),
             pl.BlockSpec((STEP * ch, rows), lambda i: ((jnp.minimum(i, steps - 1) + 1) * STEPS, index)),
             pl.BlockSpec((parts.shape[0], rows), lambda i: (0, index)),
-            pl.BlockSpec(weights.shape, lambda i: (0, 0, 0)),
+            pl.BlockSpec(weights.shape, lambda i: (0, 0)),
             pl.BlockSpec((each, count, width), lambda i: (jnp.maximum(i - steps, 0), 0, 0)),
         ],
         out_specs=pl.BlockSpec((each, count + 16, 2 * rows), lambda i: (jnp.maximum(i - steps, 0), 0, 0)),
         out_shape=jax.ShapeDtypeStruct((ch, count + 16, 2 * rows), jnp.int16),
         scratch_shapes=[pltpu.VMEM((ch, width, 2 * rows), jnp.bfloat16)],
-        compiler_params=pltpu.CompilerParams(vmem_limit_bytes=40 << 20),
+        compiler_params=pltpu.CompilerParams(vmem_limit_bytes=58 << 20),
         cost_estimate=pl.CostEstimate(
-            flops=8 * width * ch * SPAN * ch * rows + 4 * ch * width * rows * count,
+            flops=4 * width * ch * SPAN * ch * rows + 4 * ch * width * rows * count,
             bytes_accessed=2 * words.size + 2 * own.size + 4 * ch * rows * count,
             transcendentals=0,
         ),
@@ -480,7 +494,7 @@
             pltpu.VMEM((8 * LANES, LANES), jnp.float32),
         ],
         input_output_aliases={2: 0} if earlier else {},
-        compiler_params=pltpu.CompilerParams(vmem_limit_bytes=40 << 20),
+        compiler_params=pltpu.CompilerParams(vmem_limit_bytes=58 << 20),
         name="finish",
     )(feed_slot, coded, *earlier)
 
@@ -497,8 +511,8 @@
     weights = jnp.asarray(filter_weights(ch))
     slots = (feed_slot[:ROWS] - lax.axis_index("feed") * count).reshape(1, ROWS)
     picked = select_rows(words, scales, slots, total)
-    own = own_spectra(words, scales.astype(jnp.float32), weights, ch, spectra)
-    rows = sum_over_feed(picked)
+    own, zero = own_spectra(words, scales.astype(jnp.float32), weights, ch, spectra)
+    rows = sum_over_feed(picked, zero[0, 0])
     parts = rows[lines : lines + 4 * ch]
     out = None
     for index in range(pieces):

time: 254 us -> 251 us (0.988)
  local copies, waits for them, and re-layouts: 20.9 us -> 15.8 us
  starting transfers between devices: 19.2 us -> 23.2 us
  Pallas kernels: 71.2 us -> 67.4 us
  other arithmetic: 6.93 us -> 10.7 us
  waiting for transfers between devices: 135 us -> 132 us
    unnamed x22 -> x16, local copies, waits for them, and re-layouts: 14.9 us -> 8.26 us
    ppermute x12, waiting for transfers between devices: 63.7 us -> 57.3 us  [swap(): return lax.ppermute(value, 'feed', pairs)]
    ppermute x12, starting transfers between devices: 7.49 us -> 12 us  [swap(): return lax.ppermute(value, 'feed', pairs)]
    all_to_all x2, waiting for transfers between devices: 71.3 us -> 74.8 us  [through_rows(): lax.all_to_all(coded, 'feed', split_axis=0, concat_axis=0, tiled=True)]
    pallas_call x1, Pallas kernels: 16.4 us -> 13.2 us  [own_spectra(): pl.pallas_call(own_kernel, grid=(spectra // (STEPS * STEP),), in_specs=[p...]
  transfers between devices with their start and end apart: 14 -> 14, of which waited for: 10 -> 10; matrix products, arithmetic and copies ran while one was open for 1% -> 4% of each run, Pallas kernels for 17% -> 16%
where the time goes in v5:
time: 251 us; the launch traced here: 249 us
  waiting for transfers between devices  132 us (53%)
  Pallas kernels  67.4 us (27%)
  starting transfers between devices  23.2 us (9%)
  local copies, waits for them, and re-layouts  15.8 us (6%)
  other arithmetic  10.7 us (4%)
    all_to_all x2, waiting for transfers between devices, through_rows(): lax.all_to_all(coded, 'feed', split_axis=0, concat_axis=0, tiled=True)  74.8 us
    ppermute x12, waiting for transfers between devices, swap(): return lax.ppermute(value, 'feed', pairs)  57.3 us
    pallas_call x2, Pallas kernels, row_products(): pl.pallas_call(rows_kernel, grid=(2 * steps,), in_specs=[pl.BlockSpec((ma...  31.5 us
    pallas_call x2, Pallas kernels, finish(): pl.pallas_call(functools.partial(finish_kernel, scale), grid=(1,), in_spe...  20.1 us
    pallas_call x1, Pallas kernels, own_spectra(): pl.pallas_call(own_kernel, grid=(spectra // (STEPS * STEP),), in_specs=[p...  13.2 us
    ppermute x12, starting transfers between devices, swap(): return lax.ppermute(value, 'feed', pairs)  12 us
    all_to_all x2, starting transfers between devices, through_rows(): lax.all_to_all(coded, 'feed', split_axis=0, concat_axis=0, tiled=True)  11.2 us
    unnamed x16, local copies, waits for them, and re-layouts  8.26 us
  transfers between devices with their start and end apart: 14, of which 10 were waited for; matrix products, arithmetic and copies ran while one was open for 4% of the time, Pallas kernels for 16%

profile of v5, /device:TPU:13, one launch (start us, length us, event | category | flops | bytes accessed | tf_op | source)
XLA Modules:
  0.0 249.3 jit_solution(17192409396451599379)
XLA Ops:
  0.0 1.4 fusion.1
  1.4 0.7 slice_subtract_fusion
  2.1 3.4 %copy-done.2 = s32[256,16,519]{0,1,2:T(8,128)S(1)} copy-done((s32[256,16,519]{0,1,2:T(8,128)S(1)}, s32[256,16,519]{0,1,2:T(8,128)}, u32[]{:S(2)}) %copy-start.2) | copy-done | bytes 8503320
  5.6 2.6 %select_rows.1 = bf16[8448,256]{1,0:T(8,128)(2,1)S(1)} custom-call(s32[1,256]{1,0:T(1,128)S(1)} %bitcast.18, s32[8304,256]{1,0:T(8,128)S(1)} %bitcast.17, bf16[64,256]{1,0:T(8,128)(2,1)S(1)} %pad_maximum_fusion.1.parts_ref), custom_call_target="tpu_custom_call" | custom-call | tf_op jit(solution)/shard_map/select_rows/pallas_call | solution.py:329
  8.2 2.0 copy-done
  10.2 1.5 constant_dynamic-slice_fusion.4
  11.7 0.7 collective-permute-start
  12.4 4.1 %collective-permute-done = bf16[4224,256]{1,0:T(8,128)(2,1)S(1)} collective-permute-done((bf16[4224,256]{1,0:T(8,128)(2,1)}, bf16[4224,256]{1,0:T(8,128)(2,1)S(1)}, u32[]{:S(2)}, u32[]{:S(2)}) %collective-permute-start) | collective-permute-done | bytes 2162720 | tf_op jit(solution)/shard_map/ppermute | solution.py:346
  16.5 2.2 dynamic-slice_add_fusion
  18.9 0.2 collective-permute-start.6
  19.1 13.2 %own_spectra.1 = (bf16[16,256,1024]{2,1,0:T(8,128)(2,1)}, bf16[16,128]{1,0:T(8,128)(2,1)}) custom-call(s32[8304,256]{1,0:T(8,128)} %bitcast.15, s32[8304,256]{1,0:T(8,128)} %bitcast.16, f32[32,256]{1,0:T(8,128)} %bitcast.19, bf16[256,256]{1,0:T(8,128)(2,1)} %constant.142.clone.weights_ref), custom_call_target="tpu_custom_call" | custom-call | flops 4294967296 | bytes 16891904 | tf_op jit(solution)/shard_map/own_spectra/pallas_call | solution.py:278
  32.2 1.2 slice.17
  33.5 0.3 collective-permute-start.1
  33.8 1.2 dynamic-slice_add_fusion.1
  35.0 1.3 collective-permute-start.7
  36.3 10.5 %collective-permute-done.1 = bf16[1056,256]{1,0:T(8,128)(2,1)S(1)} collective-permute-done((bf16[1056,256]{1,0:T(8,128)(2,1)S(1)}, bf16[1056,256]{1,0:T(8,128)(2,1)S(1)}, u32[]{:S(2)}, u32[]{:S(2)}) %collective-permute-start.1) | collective-permute-done | bytes 540704 | tf_op jit(solution)/shard_map/ppermute | solution.py:346
  46.8 0.7 add_add_fusion
  47.6 1.2 collective-permute-start.2
  48.8 3.9 %collective-permute-done.7 = bf16[528,256]{1,0:T(8,128)(2,1)} collective-permute-done((bf16[528,256]{1,0:T(8,128)(2,1)S(1)}, bf16[528,256]{1,0:T(8,128)(2,1)}, u32[]{:S(2)}, u32[]{:S(2)}) %collective-permute-start.7) | collective-permute-done | bytes 270368 | tf_op jit(solution)/shard_map/ppermute | solution.py:346
  52.7 1.0 dynamic-slice_add_fusion.2
  53.7 2.3 collective-permute-start.8
  56.3 16.6 %collective-permute-done.8 = bf16[528,256]{1,0:T(8,128)(2,1)} collective-permute-done((bf16[528,256]{1,0:T(8,128)(2,1)S(1)}, bf16[528,256]{1,0:T(8,128)(2,1)}, u32[]{:S(2)}, u32[]{:S(2)}) %collective-permute-start.8) | collective-permute-done | bytes 270368 | tf_op jit(solution)/shard_map/ppermute | solution.py:346
  72.9 1.0 constant_dynamic-update-slice_fusion.5
  74.0 4.7 %collective-permute-done.3 = bf16[528,256]{1,0:T(8,128)(2,1)S(1)} collective-permute-done((bf16[528,256]{1,0:T(8,128)(2,1)S(1)}, bf16[528,256]{1,0:T(8,128)(2,1)S(1)}, u32[]{:S(2)}, u32[]{:S(2)}) %collective-permute-start.3) | collective-permute-done | bytes 270368 | tf_op jit(solution)/shard_map/ppermute | solution.py:346
  78.7 0.8 constant_dynamic-update-slice_fusion.9
  79.5 2.0 collective-permute-start.4
  81.5 0.3 collective-permute-start.10
  81.7 5.0 %collective-permute-done.4 = bf16[528,256]{1,0:T(8,128)(2,1)S(1)} collective-permute-done((bf16[528,256]{1,0:T(8,128)(2,1)S(1)}, bf16[528,256]{1,0:T(8,128)(2,1)S(1)}, u32[]{:S(2)}, u32[]{:S(2)}) %collective-permute-start.4) | collective-permute-done | bytes 270368 | tf_op jit(solution)/shard_map/ppermute | solution.py:346
  86.7 0.7 constant_dynamic-update-slice_fusion.8
  87.7 0.9 constant_dynamic-update-slice_fusion.3
  88.5 1.1 constant_dynamic-update-slice_fusion.7
  89.6 8.7 %collective-permute-done.10 = bf16[1056,256]{1,0:T(8,128)(2,1)S(1)} collective-permute-done((bf16[1056,256]{1,0:T(8,128)(2,1)S(1)}, bf16[1056,256]{1,0:T(8,128)(2,1)S(1)}, u32[]{:S(2)}, u32[]{:S(2)}) %collective-permute-start.10) | collective-permute-done | bytes 540704 | tf_op jit(solution)/shard_map/ppermute | solution.py:346
  98.3 0.8 constant_dynamic-update-slice_fusion.2
  99.2 1.6 pad_maximum_fusion
  100.8 3.3 %collective-permute-start.11 = (bf16[4224,256]{1,0:T(8,128)(2,1)S(1)}, bf16[4224,256]{1,0:T(8,128)(2,1)S(1)}, u32[]{:S(2)}, u32[]{:S(2)}) collective-permute-start(bf16[4224,256]{1,0:T(8,128)(2,1)S(1)} %get-tuple-element.13), channel_id=1, source_target_pairs={{0,1},{1,0},{2,3},{3,2},{4,5},{5,4},{6,7},{7,6},{8,9},{9,8},{10,11... | collective-permute-start | bytes 6488072 | tf_op jit(solution)/shard_map/ppermute | solution.py:346
  104.1 3.9 %collective-permute-done.11 = bf16[4224,256]{1,0:T(8,128)(2,1)S(1)} collective-permute-done((bf16[4224,256]{1,0:T(8,128)(2,1)S(1)}, bf16[4224,256]{1,0:T(8,128)(2,1)S(1)}, u32[]{:S(2)}, u32[]{:S(2)}) %collective-permute-start.11) | collective-permute-done | bytes 2162720 | tf_op jit(solution)/shard_map/ppermute | solution.py:346
  108.0 0.4 constant_dynamic-update-slice_fusion.main_ref.next_ref
  108.3 0.7 slice.22.parts_ref
  109.0 1.4 copy-done.1
  110.4 15.7 %row_products.3 = s16[16,272,256]{2,1,0:T(8,128)(2,1)} custom-call(bf16[8448,256]{1,0:T(8,128)(2,1)} %copy-done.1, bf16[8448,256]{1,0:T(8,128)(2,1)} %copy-done.1, bf16[64,256]{1,0:T(8,128)(2,1)} %slice.22.parts_ref, bf16[256,256]{1,0:T(8,128)(2,1)} %constant.142.clone.weights_ref, bf16[16,256,1024]{2,1,0:T(8,128)(2,1)} %get-tuple-element.8.own_ref), custom_call_target="tpu_custom_call" | custom-call | flops 4294967296 | bytes 14811136 | tf_op jit(solution)/shard_map/row_products/pallas_call | solution.py:420
  126.1 6.3 %all-to-all-start.1 = ((s16[16,272,256]{2,1,0:T(8,128)(2,1)}), s16[16,272,256]{2,1,0:T(8,128)(2,1)S(1)}, u32[]{:S(2)}, u32[]{:S(2)}) async-start(s16[16,272,256]{2,1,0:T(8,128)(2,1)} %row_products.3), calls=%async_computation.1 | async-start | bytes 4456448 | tf_op jit(solution)/shard_map/all_to_all | solution.py:520
  132.4 15.8 %row_products.2 = s16[16,272,256]{2,1,0:T(8,128)(2,1)} custom-call(bf16[8448,256]{1,0:T(8,128)(2,1)} %copy-done.1, bf16[8448,256]{1,0:T(8,128)(2,1)} %copy-done.1, bf16[64,256]{1,0:T(8,128)(2,1)} %slice.22.parts_ref, bf16[256,256]{1,0:T(8,128)(2,1)} %constant.142.clone.weights_ref, bf16[16,256,1024]{2,1,0:T(8,128)(2,1)} %get-tuple-element.8.own_ref), custom_call_target="tpu_custom_call" | custom-call | flops 4294967296 | bytes 14811136 | tf_op jit(solution)/shard_map/row_products/pallas_call | solution.py:420
  148.2 34.5 %all-to-all-done.1.coded_ref = s16[16,272,256]{2,1,0:T(8,128)(2,1)S(1)} async-done(((s16[16,272,256]{2,1,0:T(8,128)(2,1)}), s16[16,272,256]{2,1,0:T(8,128)(2,1)S(1)}, u32[]{:S(2)}, u32[]{:S(2)}) %all-to-all-start.1) | async-done | bytes 2228256 | tf_op jit(solution)/shard_map/all_to_all | solution.py:520
  182.6 1.4 copy-done.4
  184.1 4.9 %all-to-all-start = ((s16[16,272,256]{2,1,0:T(8,128)(2,1)}), s16[16,272,256]{2,1,0:T(8,128)(2,1)}, u32[]{:S(2)}, u32[]{:S(2)}) async-start(s16[16,272,256]{2,1,0:T(8,128)(2,1)} %row_products.2), calls=%async_computation | async-start | bytes 4456448 | tf_op jit(solution)/shard_map/all_to_all | solution.py:520
  189.0 10.0 %finish.2.refs_0_ = f32[16384,128]{1,0:T(8,128)} custom-call(s32[4096]{0:T(1024)} %slot_ref.3, s16[16,272,256]{2,1,0:T(8,128)(2,1)} %copy-done.4), custom_call_target="tpu_custom_call" | custom-call | tf_op jit(solution)/shard_map/finish/pallas_call | solution.py:481
  199.0 40.3 %all-to-all-done.coded_ref = s16[16,272,256]{2,1,0:T(8,128)(2,1)} async-done(((s16[16,272,256]{2,1,0:T(8,128)(2,1)}), s16[16,272,256]{2,1,0:T(8,128)(2,1)}, u32[]{:S(2)}, u32[]{:S(2)}) %all-to-all-start) | async-done | bytes 2228256 | tf_op jit(solution)/shard_map/all_to_all | solution.py:520
  239.3 10.1 %finish.3 = f32[16384,128]{1,0:T(8,128)} custom-call(s32[4096]{0:T(1024)} %slot_ref.3, s16[16,272,256]{2,1,0:T(8,128)(2,1)} %all-to-all-done.coded_ref, f32[16384,128]{1,0:T(8,128)} %finish.2.refs_0_), custom_call_target="tpu_custom_call", output_to_operand_aliasing={{}: (2, {})} | custom-call | tf_op jit(solution)/shard_map/finish/pallas_call | solution.py:481
  (29 shorter events, 0.9 us)
Async XLA Ops:
  2.1 3.4 %copy-start.2 = (s32[256,16,519]{0,1,2:T(8,128)S(1)}, s32[256,16,519]{0,1,2:T(8,128)}, u32[]{:S(2)}) copy-start(s32[256,16,519]{0,1,2:T(8,128)} %param.4) | copy-start | bytes 25509892
  8.2 2.0 copy-start
  11.7 4.8 %collective-permute-start = (bf16[4224,256]{1,0:T(8,128)(2,1)}, bf16[4224,256]{1,0:T(8,128)(2,1)S(1)}, u32[]{:S(2)}, u32[]{:S(2)}) collective-permute-start(bf16[4224,256]{1,0:T(8,128)(2,1)} %constant_dynamic-slice_fusion.4), channel_id=1, source_target_pairs={{0,1},{1,0},{2,3},{3,2},{4,5},{5,4},{6,7},{7,6},{8,9},{9,8},{10,11... | collective-permute-start | bytes 6488072 | tf_op jit(solution)/shard_map/ppermute | solution.py:346
  18.8 15.0 %copy-start.3 = (bf16[2112,256]{1,0:T(8,128)(2,1)}, bf16[2112,256]{1,0:T(8,128)(2,1)S(1)}, u32[]{:S(2)}) copy-start(bf16[2112,256]{1,0:T(8,128)(2,1)S(1)} %get-tuple-element.16) | copy-start | bytes 3244036
  18.9 14.9 %collective-permute-start.6 = (bf16[1056,256]{1,0:T(8,128)(2,1)S(1)}, bf16[1056,256]{1,0:T(8,128)(2,1)}, u32[]{:S(2)}, u32[]{:S(2)}) collective-permute-start(bf16[1056,256]{1,0:T(8,128)(2,1)S(1)} %constant_dynamic-slice_fusion.1), channel_id=1, source_target_pairs={{0,4},{1,5},{2,6},{3,7},{4,0},{5,1},{6,2},{7,3},{8,12},{9,13},{10,... | collective-permute-start | bytes 1622024 | tf_op jit(solution)/shard_map/ppermute | solution.py:346
  33.5 13.3 %collective-permute-start.1 = (bf16[1056,256]{1,0:T(8,128)(2,1)S(1)}, bf16[1056,256]{1,0:T(8,128)(2,1)S(1)}, u32[]{:S(2)}, u32[]{:S(2)}) collective-permute-start(bf16[1056,256]{1,0:T(8,128)(2,1)S(1)} %constant_dynamic-slice_fusion.3), channel_id=1, source_target_pairs={{0,2},{1,3},{2,0},{3,1},{4,6},{5,7},{6,4},{7,5},{8,10},{9,11},{10,... | collective-permute-start | bytes 1622024 | tf_op jit(solution)/shard_map/ppermute | solution.py:346
  33.8 65.4 %slice-start = ((s8[4325376]{0:T(1024)(128)(4,1)}), s8[131072]{0:T(1024)(128)(4,1)S(1)}, s32[]{:S(2)}) async-start(s8[4325376]{0:T(1024)(128)(4,1)} %bitcast.13), calls=%async_computation.2 | async-start | bytes 262144
  35.0 17.7 %collective-permute-start.7 = (bf16[528,256]{1,0:T(8,128)(2,1)S(1)}, bf16[528,256]{1,0:T(8,128)(2,1)}, u32[]{:S(2)}, u32[]{:S(2)}) collective-permute-start(bf16[528,256]{1,0:T(8,128)(2,1)S(1)} %constant_dynamic-slice_fusion), channel_id=1, source_target_pairs={{0,2},{1,3},{2,0},{3,1},{4,6},{5,7},{6,4},{7,5},{8,10},{9,11},{10,... | collective-permute-start | bytes 811016 | tf_op jit(solution)/shard_map/ppermute | solution.py:346
  47.6 8.5 %copy-start.5 = (bf16[1056,256]{1,0:T(8,128)(2,1)}, bf16[1056,256]{1,0:T(8,128)(2,1)S(1)}, u32[]{:S(2)}) copy-start(bf16[1056,256]{1,0:T(8,128)(2,1)S(1)} %add_add_fusion) | copy-start | bytes 1622020
  47.6 8.5 %collective-permute-start.2 = (bf16[528,256]{1,0:T(8,128)(2,1)S(1)}, bf16[528,256]{1,0:T(8,128)(2,1)S(1)}, u32[]{:S(2)}, u32[]{:S(2)}) collective-permute-start(bf16[528,256]{1,0:T(8,128)(2,1)S(1)} %constant_dynamic-slice_fusion.2), channel_id=1, source_target_pairs={{0,4},{1,5},{2,6},{3,7},{4,0},{5,1},{6,2},{7,3},{8,12},{9,13},{10,... | collective-permute-start | bytes 811016 | tf_op jit(solution)/shard_map/ppermute | solution.py:346
  53.7 19.2 %collective-permute-start.8 = (bf16[528,256]{1,0:T(8,128)(2,1)S(1)}, bf16[528,256]{1,0:T(8,128)(2,1)}, u32[]{:S(2)}, u32[]{:S(2)}) collective-permute-start(bf16[528,256]{1,0:T(8,128)(2,1)S(1)} %dynamic-slice_add_fusion.2), channel_id=1, source_target_pairs={{0,8},{1,9},{2,10},{3,11},{4,12},{5,13},{6,14},{7,15},{8,0},{9,1},... | collective-permute-start | bytes 811016 | tf_op jit(solution)/shard_map/ppermute | solution.py:346
  56.2 43.1 %slice-start.1 = ((s8[4325376]{0:T(1024)(128)(4,1)}), s8[4194304]{0:T(1024)(128)(4,1)S(1)}, s32[]{:S(2)}) async-start(s8[4325376]{0:T(1024)(128)(4,1)} %bitcast.13), calls=%async_computation.3 | async-start | bytes 8388608
  56.2 22.5 %collective-permute-start.3 = (bf16[528,256]{1,0:T(8,128)(2,1)S(1)}, bf16[528,256]{1,0:T(8,128)(2,1)S(1)}, u32[]{:S(2)}, u32[]{:S(2)}) collective-permute-start(bf16[528,256]{1,0:T(8,128)(2,1)S(1)} %dynamic-slice_add_fusion.3), channel_id=1, source_target_pairs={{0,8},{1,9},{2,10},{3,11},{4,12},{5,13},{6,14},{7,15},{8,0},{9,1},... | collective-permute-start | bytes 811016 | tf_op jit(solution)/shard_map/ppermute | solution.py:346
  73.9 7.5 %collective-permute-start.9 = (bf16[528,256]{1,0:T(8,128)(2,1)S(1)}, bf16[528,256]{1,0:T(8,128)(2,1)S(1)}, u32[]{:S(2)}, u32[]{:S(2)}) collective-permute-start(bf16[528,256]{1,0:T(8,128)(2,1)S(1)} %get-tuple-element.12), channel_id=1, source_target_pairs={{0,2},{1,3},{2,0},{3,1},{4,6},{5,7},{6,4},{7,5},{8,10},{9,11},{10,... | collective-permute-start | bytes 811016 | tf_op jit(solution)/shard_map/ppermute | solution.py:346
  79.5 7.3 %collective-permute-start.4 = (bf16[528,256]{1,0:T(8,128)(2,1)S(1)}, bf16[528,256]{1,0:T(8,128)(2,1)S(1)}, u32[]{:S(2)}, u32[]{:S(2)}) collective-permute-start(bf16[528,256]{1,0:T(8,128)(2,1)S(1)} %get-tuple-element.10), channel_id=1, source_target_pairs={{0,4},{1,5},{2,6},{3,7},{4,0},{5,1},{6,2},{7,3},{8,12},{9,13},{10,... | collective-permute-start | bytes 811016 | tf_op jit(solution)/shard_map/ppermute | solution.py:346
  81.5 16.9 %collective-permute-start.10 = (bf16[1056,256]{1,0:T(8,128)(2,1)S(1)}, bf16[1056,256]{1,0:T(8,128)(2,1)S(1)}, u32[]{:S(2)}, u32[]{:S(2)}) collective-permute-start(bf16[1056,256]{1,0:T(8,128)(2,1)S(1)} %constant_dynamic-update-slice_fusion.4), channel_id=1, source_target_pairs={{0,4},{1,5},{2,6},{3,7},{4,0},{5,1},{6,2},{7,3},{8,12},{9,13},{10,... | collective-permute-start | bytes 1622024 | tf_op jit(solution)/shard_map/ppermute | solution.py:346
  87.5 11.7 %collective-permute-start.5 = (bf16[1056,256]{1,0:T(8,128)(2,1)}, bf16[1056,256]{1,0:T(8,128)(2,1)S(1)}, u32[]{:S(2)}, u32[]{:S(2)}) collective-permute-start(bf16[1056,256]{1,0:T(8,128)(2,1)} %constant_dynamic-update-slice_fusion.8), channel_id=1, source_target_pairs={{0,2},{1,3},{2,0},{3,1},{4,6},{5,7},{6,4},{7,5},{8,10},{9,11},{10,... | collective-permute-start | bytes 1622024 | tf_op jit(solution)/shard_map/ppermute | solution.py:346
  100.8 7.2 %collective-permute-start.11 = (bf16[4224,256]{1,0:T(8,128)(2,1)S(1)}, bf16[4224,256]{1,0:T(8,128)(2,1)S(1)}, u32[]{:S(2)}, u32[]{:S(2)}) collective-permute-start(bf16[4224,256]{1,0:T(8,128)(2,1)S(1)} %get-tuple-element.13), channel_id=1, source_target_pairs={{0,1},{1,0},{2,3},{3,2},{4,5},{5,4},{6,7},{7,6},{8,9},{9,8},{10,11... | collective-permute-start | bytes 6488072 | tf_op jit(solution)/shard_map/ppermute | solution.py:346
  108.3 2.0 copy-start.1
  126.1 56.5 %all-to-all-start.1 = ((s16[16,272,256]{2,1,0:T(8,128)(2,1)}), s16[16,272,256]{2,1,0:T(8,128)(2,1)S(1)}, u32[]{:S(2)}, u32[]{:S(2)}) async-start(s16[16,272,256]{2,1,0:T(8,128)(2,1)} %row_products.3), calls=%async_computation.1 | async-start | bytes 4456448 | tf_op jit(solution)/shard_map/all_to_all | solution.py:520
  182.6 1.4 copy-start.4
  184.1 55.2 %all-to-all-start = ((s16[16,272,256]{2,1,0:T(8,128)(2,1)}), s16[16,272,256]{2,1,0:T(8,128)(2,1)}, u32[]{:S(2)}, u32[]{:S(2)}) async-start(s16[16,272,256]{2,1,0:T(8,128)(2,1)} %row_products.2), calls=%async_computation | async-start | bytes 4456448 | tf_op jit(solution)/shard_map/all_to_all | solution.py:520

commit v6 on v5

--- a/solution.py
+++ b/solution.py
@@ -293,7 +293,7 @@
             jax.ShapeDtypeStruct((16, LANES), jnp.bfloat16),
         ],
         scratch_shapes=[pltpu.VMEM((ch, 2 * STEPS * STEP, count), jnp.bfloat16)],
-        compiler_params=pltpu.CompilerParams(vmem_limit_bytes=58 << 20),
+        compiler_params=pltpu.CompilerParams(vmem_limit_bytes=12 << 20),
         cost_estimate=pl.CostEstimate(
             flops=4 * spectra * ch * 2 * SPAN * ch * count,
             bytes_accessed=4 * words.size + 4 * ch * spectra * count,
@@ -336,7 +336,7 @@
         ],
         out_specs=pl.BlockSpec((block, rows), lambda i: (i, 0)),
         out_shape=jax.ShapeDtypeStruct((total, rows), jnp.bfloat16),
-        compiler_params=pltpu.CompilerParams(vmem_limit_bytes=24 << 20),
+        compiler_params=pltpu.CompilerParams(vmem_limit_bytes=8 << 20),
         name="select_rows",
     )(slots, words, parts)
 
@@ -430,7 +430,7 @@
         out_specs=pl.BlockSpec((each, count + 16, 2 * rows), lambda i: (jnp.maximum(i - steps, 0), 0, 0)),
         out_shape=jax.ShapeDtypeStruct((ch, count + 16, 2 * rows), jnp.int16),
         scratch_shapes=[pltpu.VMEM((ch, width, 2 * rows), jnp.bfloat16)],
-        compiler_params=pltpu.CompilerParams(vmem_limit_bytes=58 << 20),
+        compiler_params=pltpu.CompilerParams(vmem_limit_bytes=18 << 20),
         cost_estimate=pl.CostEstimate(
             flops=4 * width * ch * SPAN * ch * rows + 4 * ch * width * rows * count,
             bytes_accessed=2 * words.size + 2 * own.size + 4 * ch * rows * count,
@@ -494,7 +494,7 @@
             pltpu.VMEM((8 * LANES, LANES), jnp.float32),
         ],
         input_output_aliases={2: 0} if earlier else {},
-        compiler_params=pltpu.CompilerParams(vmem_limit_bytes=58 << 20),
+        compiler_params=pltpu.CompilerParams(vmem_limit_bytes=22 << 20),
         name="finish",
     )(feed_slot, coded, *earlier)
 

time: 251 us -> 248 us (0.988)
  Pallas kernels: 67.4 us -> 55.8 us
  local copies, waits for them, and re-layouts: 15.8 us -> 26.8 us
  waiting for transfers between devices: 132 us -> 128 us
    unnamed x16 -> x24, local copies, waits for them, and re-layouts: 8.26 us -> 20.4 us
    pallas_call x2, Pallas kernels: 31.5 us -> 22.5 us  [row_products(): pl.pallas_call(rows_kernel, grid=(2 * steps,), in_specs=[pl.BlockSpec((ma...]
    ppermute x12, waiting for transfers between devices: 57.3 us -> 53.5 us  [swap(): return lax.ppermute(value, 'feed', pairs)]
  transfers between devices with their start and end apart: 14 -> 14, of which waited for: 10 -> 11; matrix products, arithmetic and copies ran while one was open for 4% -> 4% of each run, Pallas kernels for 16% -> 13%
where the time goes in v6:
time: 248 us; the launch traced here: 247 us
  waiting for transfers between devices  128 us (52%)
  Pallas kernels  55.8 us (22%)
  local copies, waits for them, and re-layouts  26.8 us (11%)
  starting transfers between devices  25.6 us (10%)
  other arithmetic  10.9 us (4%)
    all_to_all x2, waiting for transfers between devices, through_rows(): lax.all_to_all(coded, 'feed', split_axis=0, concat_axis=0, tiled=True)  74.5 us
    ppermute x12, waiting for transfers between devices, swap(): return lax.ppermute(value, 'feed', pairs)  53.5 us
    pallas_call x2, Pallas kernels, row_products(): pl.pallas_call(rows_kernel, grid=(2 * steps,), in_specs=[pl.BlockSpec((ma...  22.5 us
    unnamed x24, local copies, waits for them, and re-layouts  20.4 us
    pallas_call x2, Pallas kernels, finish(): pl.pallas_call(functools.partial(finish_kernel, scale), grid=(1,), in_spe...  19.3 us
    ppermute x12, starting transfers between devices, swap(): return lax.ppermute(value, 'feed', pairs)  13.6 us
    all_to_all x2, starting transfers between devices, through_rows(): lax.all_to_all(coded, 'feed', split_axis=0, concat_axis=0, tiled=True)  12 us
    pallas_call x1, Pallas kernels, own_spectra(): pl.pallas_call(own_kernel, grid=(spectra // (STEPS * STEP),), in_specs=[p...  11.3 us
  transfers between devices with their start and end apart: 14, of which 11 were waited for; matrix products, arithmetic and copies ran while one was open for 4% of the time, Pallas kernels for 13%

profile of v6, /device:TPU:13, one launch (start us, length us, event | category | flops | bytes accessed | tf_op | source)
XLA Modules:
  0.0 247.2 jit_solution(12472763683631295405)
XLA Ops:
  0.0 0.8 fusion.1
  0.9 0.7 slice_subtract_fusion
  1.6 3.4 %copy-done.3 = s32[256,16,519]{0,1,2:T(8,128)S(1)} copy-done((s32[256,16,519]{0,1,2:T(8,128)S(1)}, s32[256,16,519]{0,1,2:T(8,128)}, u32[]{:S(2)}) %copy-start.3) | copy-done | bytes 8503320
  5.0 2.6 %select_rows.1 = bf16[8448,256]{1,0:T(8,128)(2,1)S(1)} custom-call(s32[1,256]{1,0:T(1,128)S(1)} %bitcast.19, s32[8304,256]{1,0:T(8,128)S(1)} %bitcast.15, bf16[64,256]{1,0:T(8,128)(2,1)S(1)} %pad_maximum_fusion.1.parts_ref), custom_call_target="tpu_custom_call" | custom-call | tf_op jit(solution)/shard_map/select_rows/pallas_call | solution.py:329
  7.6 1.6 constant_dynamic-slice_fusion.4
  9.2 1.1 copy-done
  10.3 0.7 collective-permute-start
  11.0 4.1 %collective-permute-done = bf16[4224,256]{1,0:T(8,128)(2,1)S(1)} collective-permute-done((bf16[4224,256]{1,0:T(8,128)(2,1)}, bf16[4224,256]{1,0:T(8,128)(2,1)S(1)}, u32[]{:S(2)}, u32[]{:S(2)}) %collective-permute-start) | collective-permute-done | bytes 2162720 | tf_op jit(solution)/shard_map/ppermute | solution.py:346
  15.0 2.3 dynamic-slice_add_fusion
  17.8 1.3 copy-done.4
  19.2 11.3 %own_spectra.1 = (bf16[16,256,1024]{2,1,0:T(8,128)(2,1)S(1)}, bf16[16,128]{1,0:T(8,128)(2,1)S(1)}) custom-call(s32[8304,256]{1,0:T(8,128)S(1)} %bitcast.16, s32[8304,256]{1,0:T(8,128)S(1)} %bitcast.17, f32[32,256]{1,0:T(8,128)S(1)} %bitcast.18, bf16[256,256]{1,0:T(8,128)(2,1)S(1)} %copy-done.8), custom_call_target="tpu_custom_call" | custom-call | flops 4294967296 | bytes 16891904 | tf_op jit(solution)/shard_map/own_spectra/pallas_call | solution.py:278
  30.6 3.4 %copy-done.5 = bf16[16,256,1024]{2,1,0:T(8,128)(2,1)} copy-done((bf16[16,256,1024]{2,1,0:T(8,128)(2,1)}, bf16[16,256,1024]{2,1,0:T(8,128)(2,1)S(1)}, u32[]{:S(2)}) %copy-start.5) | copy-done | bytes 8388632
  34.0 0.5 slice.17
  34.8 1.2 dynamic-slice_add_fusion.1
  36.0 1.4 collective-permute-start.7
  37.4 10.7 %collective-permute-done.1 = bf16[1056,256]{1,0:T(8,128)(2,1)S(1)} collective-permute-done((bf16[1056,256]{1,0:T(8,128)(2,1)S(1)}, bf16[1056,256]{1,0:T(8,128)(2,1)S(1)}, u32[]{:S(2)}, u32[]{:S(2)}) %collective-permute-start.1) | collective-permute-done | bytes 540704 | tf_op jit(solution)/shard_map/ppermute | solution.py:346
  48.1 1.6 add_add_fusion
  49.7 1.7 constant_dynamic-slice_fusion.2
  51.5 2.5 collective-permute-done.7
  54.0 1.0 dynamic-slice_add_fusion.2
  55.0 2.4 collective-permute-start.8
  57.6 1.1 dynamic-slice_add_fusion.3
  58.7 2.4 collective-permute-start.3
  61.1 13.2 %collective-permute-done.8 = bf16[528,256]{1,0:T(8,128)(2,1)} collective-permute-done((bf16[528,256]{1,0:T(8,128)(2,1)S(1)}, bf16[528,256]{1,0:T(8,128)(2,1)}, u32[]{:S(2)}, u32[]{:S(2)}) %collective-permute-start.8) | collective-permute-done | bytes 270368 | tf_op jit(solution)/shard_map/ppermute | solution.py:346
  74.3 1.0 constant_dynamic-update-slice_fusion.5
  75.7 4.4 %collective-permute-done.3 = bf16[528,256]{1,0:T(8,128)(2,1)S(1)} collective-permute-done((bf16[528,256]{1,0:T(8,128)(2,1)S(1)}, bf16[528,256]{1,0:T(8,128)(2,1)S(1)}, u32[]{:S(2)}, u32[]{:S(2)}) %collective-permute-start.3) | collective-permute-done | bytes 270368 | tf_op jit(solution)/shard_map/ppermute | solution.py:346
  80.1 0.8 constant_dynamic-update-slice_fusion.9
  80.8 0.7 collective-permute-start.4
  81.5 0.9 collective-permute-start.10
  82.4 5.1 %collective-permute-done.4 = bf16[528,256]{1,0:T(8,128)(2,1)S(1)} collective-permute-done((bf16[528,256]{1,0:T(8,128)(2,1)S(1)}, bf16[528,256]{1,0:T(8,128)(2,1)S(1)}, u32[]{:S(2)}, u32[]{:S(2)}) %collective-permute-start.4) | collective-permute-done | bytes 270368 | tf_op jit(solution)/shard_map/ppermute | solution.py:346
  87.5 0.7 constant_dynamic-update-slice_fusion.8
  88.6 1.1 constant_dynamic-update-slice_fusion.7
  89.7 9.4 %collective-permute-done.10 = bf16[1056,256]{1,0:T(8,128)(2,1)S(1)} collective-permute-done((bf16[1056,256]{1,0:T(8,128)(2,1)S(1)}, bf16[1056,256]{1,0:T(8,128)(2,1)S(1)}, u32[]{:S(2)}, u32[]{:S(2)}) %collective-permute-start.10) | collective-permute-done | bytes 540704 | tf_op jit(solution)/shard_map/ppermute | solution.py:346
  99.6 4.1 %collective-permute-start.11 = (bf16[4224,256]{1,0:T(8,128)(2,1)S(1)}, bf16[4224,256]{1,0:T(8,128)(2,1)S(1)}, u32[]{:S(2)}, u32[]{:S(2)}) collective-permute-start(bf16[4224,256]{1,0:T(8,128)(2,1)S(1)} %get-tuple-element.13), channel_id=1, source_target_pairs={{0,1},{1,0},{2,3},{3,2},{4,5},{5,4},{6,7},{7,6},{8,9},{9,8},{10,11... | collective-permute-start | bytes 6488072 | tf_op jit(solution)/shard_map/ppermute | solution.py:346
  103.6 3.9 %collective-permute-done.11 = bf16[4224,256]{1,0:T(8,128)(2,1)S(1)} collective-permute-done((bf16[4224,256]{1,0:T(8,128)(2,1)S(1)}, bf16[4224,256]{1,0:T(8,128)(2,1)S(1)}, u32[]{:S(2)}, u32[]{:S(2)}) %collective-permute-start.11) | collective-permute-done | bytes 2162720 | tf_op jit(solution)/shard_map/ppermute | solution.py:346
  107.5 0.4 constant_dynamic-update-slice_fusion.main_ref.next_ref
  107.9 3.4 %copy-done.6 = bf16[16,256,1024]{2,1,0:T(8,128)(2,1)S(1)} copy-done((bf16[16,256,1024]{2,1,0:T(8,128)(2,1)S(1)}, bf16[16,256,1024]{2,1,0:T(8,128)(2,1)}, u32[]{:S(2)}) %copy-start.6) | copy-done | bytes 8388632
  111.3 11.3 %row_products.3 = s16[16,272,256]{2,1,0:T(8,128)(2,1)} custom-call(bf16[8448,256]{1,0:T(8,128)(2,1)S(1)} %constant_dynamic-update-slice_fusion.main_ref.next_ref, bf16[8448,256]{1,0:T(8,128)(2,1)S(1)} %constant_dynamic-update-slice_fusion.main_ref.next_ref, bf16[64,256]{1,0:T(8,128)(2,1)S(1)} %slice.22.parts_ref, bf16[256,256]{1,0:T(8,128)(2,1)S(1)} %copy-done.8, ...), custom_call_target="tpu_custom_call" | custom-call | flops 4294967296 | bytes 14811136 | tf_op jit(solution)/shard_map/row_products/pallas_call | solution.py:420
  122.6 2.0 copy-done.1
  124.6 7.0 %all-to-all-start.1 = ((s16[16,272,256]{2,1,0:T(8,128)(2,1)}), s16[16,272,256]{2,1,0:T(8,128)(2,1)S(1)}, u32[]{:S(2)}, u32[]{:S(2)}) async-start(s16[16,272,256]{2,1,0:T(8,128)(2,1)} %row_products.3), calls=%async_computation.1 | async-start | bytes 4456448 | tf_op jit(solution)/shard_map/all_to_all | solution.py:520
  131.7 2.2 copy-done.2
  133.9 3.4 %copy-done.7 = bf16[16,256,1024]{2,1,0:T(8,128)(2,1)S(1)} copy-done((bf16[16,256,1024]{2,1,0:T(8,128)(2,1)S(1)}, bf16[16,256,1024]{2,1,0:T(8,128)(2,1)}, u32[]{:S(2)}) %copy-start.7) | copy-done | bytes 8388632
  137.3 11.3 %row_products.2 = s16[16,272,256]{2,1,0:T(8,128)(2,1)} custom-call(bf16[8448,256]{1,0:T(8,128)(2,1)S(1)} %copy-done.2, bf16[8448,256]{1,0:T(8,128)(2,1)S(1)} %copy-done.2, bf16[64,256]{1,0:T(8,128)(2,1)S(1)} %slice.22.parts_ref, bf16[256,256]{1,0:T(8,128)(2,1)S(1)} %copy-done.8, bf16[16,256,1024]{2,1,0:T(8,128)(2,1)S(1)} %copy-done.7), custom_call_target="tpu_custom_call" | custom-call | flops 4294967296 | bytes 14811136 | tf_op jit(solution)/shard_map/row_products/pallas_call | solution.py:420
  148.5 33.4 %all-to-all-done.1.coded_ref = s16[16,272,256]{2,1,0:T(8,128)(2,1)S(1)} async-done(((s16[16,272,256]{2,1,0:T(8,128)(2,1)}), s16[16,272,256]{2,1,0:T(8,128)(2,1)S(1)}, u32[]{:S(2)}, u32[]{:S(2)}) %all-to-all-start.1) | async-done | bytes 2228256 | tf_op jit(solution)/shard_map/all_to_all | solution.py:520
  181.9 4.9 %all-to-all-start = ((s16[16,272,256]{2,1,0:T(8,128)(2,1)}), s16[16,272,256]{2,1,0:T(8,128)(2,1)}, u32[]{:S(2)}, u32[]{:S(2)}) async-start(s16[16,272,256]{2,1,0:T(8,128)(2,1)} %row_products.2), calls=%async_computation | async-start | bytes 4456448 | tf_op jit(solution)/shard_map/all_to_all | solution.py:520
  186.8 9.2 %finish.2.refs_0_ = f32[16384,128]{1,0:T(8,128)} custom-call(s32[4096]{0:T(1024)S(1)} %copy-done.9, s16[16,272,256]{2,1,0:T(8,128)(2,1)S(1)} %all-to-all-done.1.coded_ref), custom_call_target="tpu_custom_call" | custom-call | tf_op jit(solution)/shard_map/finish/pallas_call | solution.py:481
  196.0 41.1 %all-to-all-done.coded_ref = s16[16,272,256]{2,1,0:T(8,128)(2,1)} async-done(((s16[16,272,256]{2,1,0:T(8,128)(2,1)}), s16[16,272,256]{2,1,0:T(8,128)(2,1)}, u32[]{:S(2)}, u32[]{:S(2)}) %all-to-all-start) | async-done | bytes 2228256 | tf_op jit(solution)/shard_map/all_to_all | solution.py:520
  237.1 10.1 %finish.3 = f32[16384,128]{1,0:T(8,128)} custom-call(s32[4096]{0:T(1024)S(1)} %copy-done.9, s16[16,272,256]{2,1,0:T(8,128)(2,1)} %all-to-all-done.coded_ref, f32[16384,128]{1,0:T(8,128)} %finish.2.refs_0_), custom_call_target="tpu_custom_call", output_to_operand_aliasing={{}: (2, {})} | custom-call | tf_op jit(solution)/shard_map/finish/pallas_call | solution.py:481
  (37 shorter events, 2.4 us)
Async XLA Ops:
  1.6 3.4 %copy-start.3 = (s32[256,16,519]{0,1,2:T(8,128)S(1)}, s32[256,16,519]{0,1,2:T(8,128)}, u32[]{:S(2)}) copy-start(s32[256,16,519]{0,1,2:T(8,128)} %param.4) | copy-start | bytes 25509892
  7.6 2.7 %copy-start = (bf16[8448,256]{1,0:T(8,128)(2,1)}, bf16[8448,256]{1,0:T(8,128)(2,1)S(1)}, u32[]{:S(2)}) copy-start(bf16[8448,256]{1,0:T(8,128)(2,1)S(1)} %select_rows.1) | copy-start | bytes 12976132
  10.3 4.8 %collective-permute-start = (bf16[4224,256]{1,0:T(8,128)(2,1)}, bf16[4224,256]{1,0:T(8,128)(2,1)S(1)}, u32[]{:S(2)}, u32[]{:S(2)}) collective-permute-start(bf16[4224,256]{1,0:T(8,128)(2,1)} %constant_dynamic-slice_fusion.4), channel_id=1, source_target_pairs={{0,1},{1,0},{2,3},{3,2},{4,5},{5,4},{6,7},{7,6},{8,9},{9,8},{10,11... | collective-permute-start | bytes 6488072 | tf_op jit(solution)/shard_map/ppermute | solution.py:346
  15.0 4.1 %copy-start.4 = (s32[256,16,519]{0,1,2:T(8,128)S(1)}, s32[256,16,519]{0,1,2:T(8,128)}, u32[]{:S(2)}) copy-start(s32[256,16,519]{0,1,2:T(8,128)} %param.4) | copy-start | bytes 25509892
  17.4 1.9 copy-start.8
  17.6 17.2 %collective-permute-start.6 = (bf16[1056,256]{1,0:T(8,128)(2,1)S(1)}, bf16[1056,256]{1,0:T(8,128)(2,1)}, u32[]{:S(2)}, u32[]{:S(2)}) collective-permute-start(bf16[1056,256]{1,0:T(8,128)(2,1)S(1)} %constant_dynamic-slice_fusion.1), channel_id=1, source_target_pairs={{0,4},{1,5},{2,6},{3,7},{4,0},{5,1},{6,2},{7,3},{8,12},{9,13},{10,... | collective-permute-start | bytes 1622024 | tf_op jit(solution)/shard_map/ppermute | solution.py:346
  30.6 3.4 %copy-start.5 = (bf16[16,256,1024]{2,1,0:T(8,128)(2,1)}, bf16[16,256,1024]{2,1,0:T(8,128)(2,1)S(1)}, u32[]{:S(2)}) copy-start(bf16[16,256,1024]{2,1,0:T(8,128)(2,1)S(1)} %get-tuple-element.8.own_ref) | copy-start | bytes 25165828
  34.5 13.6 %collective-permute-start.1 = (bf16[1056,256]{1,0:T(8,128)(2,1)S(1)}, bf16[1056,256]{1,0:T(8,128)(2,1)S(1)}, u32[]{:S(2)}, u32[]{:S(2)}) collective-permute-start(bf16[1056,256]{1,0:T(8,128)(2,1)S(1)} %constant_dynamic-slice_fusion.3), channel_id=1, source_target_pairs={{0,2},{1,3},{2,0},{3,1},{4,6},{5,7},{6,4},{7,5},{8,10},{9,11},{10,... | collective-permute-start | bytes 1622024 | tf_op jit(solution)/shard_map/ppermute | solution.py:346
  34.8 64.5 %slice-start = ((s8[4325376]{0:T(1024)(128)(4,1)}), s8[131072]{0:T(1024)(128)(4,1)S(1)}, s32[]{:S(2)}) async-start(s8[4325376]{0:T(1024)(128)(4,1)} %bitcast.13), calls=%async_computation.2 | async-start | bytes 262144
  36.0 18.0 %collective-permute-start.7 = (bf16[528,256]{1,0:T(8,128)(2,1)S(1)}, bf16[528,256]{1,0:T(8,128)(2,1)}, u32[]{:S(2)}, u32[]{:S(2)}) collective-permute-start(bf16[528,256]{1,0:T(8,128)(2,1)S(1)} %constant_dynamic-slice_fusion), channel_id=1, source_target_pairs={{0,2},{1,3},{2,0},{3,1},{4,6},{5,7},{6,4},{7,5},{8,10},{9,11},{10,... | collective-permute-start | bytes 811016 | tf_op jit(solution)/shard_map/ppermute | solution.py:346
  51.3 6.3 %collective-permute-start.2 = (bf16[528,256]{1,0:T(8,128)(2,1)}, bf16[528,256]{1,0:T(8,128)(2,1)}, u32[]{:S(2)}, u32[]{:S(2)}) collective-permute-start(bf16[528,256]{1,0:T(8,128)(2,1)} %constant_dynamic-slice_fusion.2), channel_id=1, source_target_pairs={{0,4},{1,5},{2,6},{3,7},{4,0},{5,1},{6,2},{7,3},{8,12},{9,13},{10,... | collective-permute-start | bytes 811016 | tf_op jit(solution)/shard_map/ppermute | solution.py:346
  55.0 19.3 %collective-permute-start.8 = (bf16[528,256]{1,0:T(8,128)(2,1)S(1)}, bf16[528,256]{1,0:T(8,128)(2,1)}, u32[]{:S(2)}, u32[]{:S(2)}) collective-permute-start(bf16[528,256]{1,0:T(8,128)(2,1)S(1)} %dynamic-slice_add_fusion.2), channel_id=1, source_target_pairs={{0,8},{1,9},{2,10},{3,11},{4,12},{5,13},{6,14},{7,15},{8,0},{9,1},... | collective-permute-start | bytes 811016 | tf_op jit(solution)/shard_map/ppermute | solution.py:346
  58.7 40.5 %slice-start.1 = ((s8[4325376]{0:T(1024)(128)(4,1)}), s8[4194304]{0:T(1024)(128)(4,1)S(1)}, s32[]{:S(2)}) async-start(s8[4325376]{0:T(1024)(128)(4,1)} %bitcast.13), calls=%async_computation.3 | async-start | bytes 8388608
  58.7 21.3 %collective-permute-start.3 = (bf16[528,256]{1,0:T(8,128)(2,1)S(1)}, bf16[528,256]{1,0:T(8,128)(2,1)S(1)}, u32[]{:S(2)}, u32[]{:S(2)}) collective-permute-start(bf16[528,256]{1,0:T(8,128)(2,1)S(1)} %dynamic-slice_add_fusion.3), channel_id=1, source_target_pairs={{0,8},{1,9},{2,10},{3,11},{4,12},{5,13},{6,14},{7,15},{8,0},{9,1},... | collective-permute-start | bytes 811016 | tf_op jit(solution)/shard_map/ppermute | solution.py:346
  75.3 6.2 %collective-permute-start.9 = (bf16[528,256]{1,0:T(8,128)(2,1)S(1)}, bf16[528,256]{1,0:T(8,128)(2,1)S(1)}, u32[]{:S(2)}, u32[]{:S(2)}) collective-permute-start(bf16[528,256]{1,0:T(8,128)(2,1)S(1)} %get-tuple-element.12), channel_id=1, source_target_pairs={{0,2},{1,3},{2,0},{3,1},{4,6},{5,7},{6,4},{7,5},{8,10},{9,11},{10,... | collective-permute-start | bytes 811016 | tf_op jit(solution)/shard_map/ppermute | solution.py:346
  80.8 6.7 %collective-permute-start.4 = (bf16[528,256]{1,0:T(8,128)(2,1)S(1)}, bf16[528,256]{1,0:T(8,128)(2,1)S(1)}, u32[]{:S(2)}, u32[]{:S(2)}) collective-permute-start(bf16[528,256]{1,0:T(8,128)(2,1)S(1)} %get-tuple-element.10), channel_id=1, source_target_pairs={{0,4},{1,5},{2,6},{3,7},{4,0},{5,1},{6,2},{7,3},{8,12},{9,13},{10,... | collective-permute-start | bytes 811016 | tf_op jit(solution)/shard_map/ppermute | solution.py:346
  81.5 17.6 %collective-permute-start.10 = (bf16[1056,256]{1,0:T(8,128)(2,1)S(1)}, bf16[1056,256]{1,0:T(8,128)(2,1)S(1)}, u32[]{:S(2)}, u32[]{:S(2)}) collective-permute-start(bf16[1056,256]{1,0:T(8,128)(2,1)S(1)} %constant_dynamic-update-slice_fusion.4), channel_id=1, source_target_pairs={{0,4},{1,5},{2,6},{3,7},{4,0},{5,1},{6,2},{7,3},{8,12},{9,13},{10,... | collective-permute-start | bytes 1622024 | tf_op jit(solution)/shard_map/ppermute | solution.py:346
  88.3 10.9 %collective-permute-start.5 = (bf16[1056,256]{1,0:T(8,128)(2,1)}, bf16[1056,256]{1,0:T(8,128)(2,1)S(1)}, u32[]{:S(2)}, u32[]{:S(2)}) collective-permute-start(bf16[1056,256]{1,0:T(8,128)(2,1)} %constant_dynamic-update-slice_fusion.8), channel_id=1, source_target_pairs={{0,2},{1,3},{2,0},{3,1},{4,6},{5,7},{6,4},{7,5},{8,10},{9,11},{10,... | collective-permute-start | bytes 1622024 | tf_op jit(solution)/shard_map/ppermute | solution.py:346
  99.6 7.9 %collective-permute-start.11 = (bf16[4224,256]{1,0:T(8,128)(2,1)S(1)}, bf16[4224,256]{1,0:T(8,128)(2,1)S(1)}, u32[]{:S(2)}, u32[]{:S(2)}) collective-permute-start(bf16[4224,256]{1,0:T(8,128)(2,1)S(1)} %get-tuple-element.13), channel_id=1, source_target_pairs={{0,1},{1,0},{2,3},{3,2},{4,5},{5,4},{6,7},{7,6},{8,9},{9,8},{10,11... | collective-permute-start | bytes 6488072 | tf_op jit(solution)/shard_map/ppermute | solution.py:346
  107.9 3.4 %copy-start.6 = (bf16[16,256,1024]{2,1,0:T(8,128)(2,1)S(1)}, bf16[16,256,1024]{2,1,0:T(8,128)(2,1)}, u32[]{:S(2)}) copy-start(bf16[16,256,1024]{2,1,0:T(8,128)(2,1)} %copy-done.5) | copy-start | bytes 25165828
  122.6 2.0 copy-start.1
  124.6 57.3 %all-to-all-start.1 = ((s16[16,272,256]{2,1,0:T(8,128)(2,1)}), s16[16,272,256]{2,1,0:T(8,128)(2,1)S(1)}, u32[]{:S(2)}, u32[]{:S(2)}) async-start(s16[16,272,256]{2,1,0:T(8,128)(2,1)} %row_products.3), calls=%async_computation.1 | async-start | bytes 4456448 | tf_op jit(solution)/shard_map/all_to_all | solution.py:520
  131.6 2.2 copy-start.2
  133.9 3.4 %copy-start.7 = (bf16[16,256,1024]{2,1,0:T(8,128)(2,1)S(1)}, bf16[16,256,1024]{2,1,0:T(8,128)(2,1)}, u32[]{:S(2)}) copy-start(bf16[16,256,1024]{2,1,0:T(8,128)(2,1)} %copy-done.5) | copy-start | bytes 25165828
  148.5 38.3 %copy-start.9 = (s32[4096]{0:T(1024)S(1)}, s32[4096]{0:T(1024)}, u32[]{:S(2)}) copy-start(s32[4096]{0:T(1024)} %slot_ref.3) | copy-start | bytes 49156
  181.9 55.2 %all-to-all-start = ((s16[16,272,256]{2,1,0:T(8,128)(2,1)}), s16[16,272,256]{2,1,0:T(8,128)(2,1)}, u32[]{:S(2)}, u32[]{:S(2)}) async-start(s16[16,272,256]{2,1,0:T(8,128)(2,1)} %row_products.2), calls=%async_computation | async-start | bytes 4456448 | tf_op jit(solution)/shard_map/all_to_all | solution.py:520

commit v7 on v6

--- a/solution.py
+++ b/solution.py
@@ -259,40 +259,62 @@
     ]
 
 
-def own_kernel(main_ref, next_ref, gains_ref, weights_ref, out_ref, zero_ref, held):
+def own_kernel(main_ref, next_ref, gains_ref, weights_ref, after_ref, out_ref, zero_ref, held, turned, sems):
+    step = pl.program_id(0)
+    slot = step % 2
     ch = out_ref.shape[0]
     zero_ref[...] = jnp.zeros_like(zero_ref)
     words = jnp.concatenate([main_ref[...], next_ref[...]], axis=0)
 
+    def copy(index):
+        return pltpu.make_async_copy(turned.at[index % 2], out_ref.at[:, index], sems.at[index % 2])
+
     def store(b, c, real, imag):
         held[c, b * 2 * STEP : (b + 1) * 2 * STEP, :] = jnp.concatenate([real, imag], axis=0).astype(held.dtype)
 
     spectra_of(weights_ref, levels_of(words), gains_ref[...], ch, store)
+
+    @pl.when(step >= 2)
+    def _():
+        copy(step - 2).wait()
+
     for c in range(ch):
-        out_ref[c] = held[c].T
-
-
-def own_spectra(words, gains, weights, ch, spectra):
+        turned[slot, c] = held[c].T
+    copy(step).start()
+
+    @pl.when(step == pl.num_programs(0) - 1)
+    def _():
+        copy(step - 1).wait()
+        copy(step).wait()
+
+
+def own_spectra(words, gains, weights, ch, spectra, after):
     count = words.shape[1]
     main = STEPS * STEP * ch
+    steps = spectra // (STEPS * STEP)
     return pl.pallas_call(
         own_kernel,
-        grid=(spectra // (STEPS * STEP),),
+        grid=(steps,),
         in_specs=[
             pl.BlockSpec((main, count), lambda i: (i, 0)),
             pl.BlockSpec((STEP * ch, count), lambda i: ((i + 1) * STEPS, 0)),
             pl.BlockSpec(gains.shape, lambda i: (0, 0)),
             pl.BlockSpec(weights.shape, lambda i: (0, 0)),
+            pl.BlockSpec(memory_space=pl.ANY),
         ],
         out_specs=[
-            pl.BlockSpec((ch, count, 2 * STEPS * STEP), lambda i: (0, 0, i)),
+            pl.BlockSpec(memory_space=pltpu.HBM),
             pl.BlockSpec((16, LANES), lambda i: (0, 0)),
         ],
         out_shape=[
-            jax.ShapeDtypeStruct((ch, count, 2 * spectra), jnp.bfloat16),
+            jax.ShapeDtypeStruct((ch, steps, count, 2 * STEPS * STEP), jnp.bfloat16),
             jax.ShapeDtypeStruct((16, LANES), jnp.bfloat16),
         ],
-        scratch_shapes=[pltpu.VMEM((ch, 2 * STEPS * STEP, count), jnp.bfloat16)],
+        scratch_shapes=[
+            pltpu.VMEM((ch, 2 * STEPS * STEP, count), jnp.bfloat16),
+            pltpu.VMEM((2, ch, count, 2 * STEPS * STEP), jnp.bfloat16),
+            pltpu.SemaphoreType.DMA((2,)),
+        ],
         compiler_params=pltpu.CompilerParams(vmem_limit_bytes=12 << 20),
         cost_estimate=pl.CostEstimate(
             flops=4 * spectra * ch * 2 * SPAN * ch * count,
@@ -300,25 +322,27 @@
             transcendentals=0,
         ),
         name="own_spectra",
-    )(words, words, gains, weights)
-
-
-def select_kernel(last_rows, slots_ref, words_ref, parts_ref, out_ref):
+    )(words, words, gains, weights, after)
+
+
+def select_kernel(last_rows, slots_ref, words_ref, parts_ref, *outs):
     step = pl.program_id(0)
-    count, rows = words_ref.shape[1], out_ref.shape[1]
+    count, rows = words_ref.shape[1], slots_ref.shape[1]
     words = words_ref[...].astype(jnp.float32).astype(jnp.bfloat16)
     place = lax.broadcasted_iota(jnp.int32, (count, rows), 0)
     choice = jnp.where(slots_ref[...] == place, 1.0, 0.0).astype(jnp.bfloat16)
-    out_ref[...] = jnp.dot(words, choice, preferred_element_type=jnp.float32).astype(out_ref.dtype)
+    taken = jnp.dot(words, choice, preferred_element_type=jnp.float32).astype(outs[0].dtype)
+    for index, out_ref in enumerate(outs):
+        out_ref[...] = taken[:, index * LANES : (index + 1) * LANES]
 
     @pl.when(step == pl.num_programs(0) - 1)
     def _():
         extra = parts_ref.shape[0]
-        out_ref[last_rows : last_rows + extra, :] = jnp.dot(
-            parts_ref[...], choice, preferred_element_type=jnp.float32
-        ).astype(out_ref.dtype)
-        left = out_ref.shape[0] - last_rows - extra
-        out_ref[last_rows + extra :, :] = jnp.zeros((left, rows), out_ref.dtype)
+        gains = jnp.dot(parts_ref[...], choice, preferred_element_type=jnp.float32).astype(outs[0].dtype)
+        for index, out_ref in enumerate(outs):
+            out_ref[last_rows : last_rows + extra, :] = gains[:, index * LANES : (index + 1) * LANES]
+            left = out_ref.shape[0] - last_rows - extra
+            out_ref[last_rows + extra :, :] = jnp.zeros((left, LANES), out_ref.dtype)
 
 
 def select_rows(words, gains, slots, total):
@@ -334,8 +358,8 @@
             pl.BlockSpec((block, count), lambda i: (i, 0)),
             pl.BlockSpec(parts.shape, lambda i: (0, 0)),
         ],
-        out_specs=pl.BlockSpec((block, rows), lambda i: (i, 0)),
-        out_shape=jax.ShapeDtypeStruct((total, rows), jnp.bfloat16),
+        out_specs=[pl.BlockSpec((block, LANES), lambda i: (i, 0))] * (rows // LANES),
+        out_shape=[jax.ShapeDtypeStruct((total, LANES), jnp.bfloat16)] * (rows // LANES),
         compiler_params=pltpu.CompilerParams(vmem_limit_bytes=8 << 20),
         name="select_rows",
     )(slots, words, parts)
@@ -364,23 +388,34 @@
     return lax.dynamic_update_slice_in_dim(buffer, other, (1 - side(bit)) * size, 0)
 
 
-def sum_over_feed(value, zero):
+def sum_over_feed(value, work=None):
     half = reduce_half(value, 1)
     size = half.shape[0] // 2
     left, right = half[:size], half[size:]
-    left_1, right_1 = reduce_half(left, 2) + zero, reduce_half(right, 4)
+    left_1, right_1 = reduce_half(left, 2), reduce_half(right, 4)
     left_2, right_2 = reduce_half(left_1, 4), reduce_half(right_1, 2)
     left_3, right_3 = left_2 + swap(left_2, 8), right_2 + swap(right_2, 8)
+    if work is not None:
+        left_3 = left_3 + work(left_2)
     left_1, right_1 = gather_half(left_3, 4, left_1), gather_half(right_3, 2, right_1)
     left, right = gather_half(left_1, 2, left), gather_half(right_1, 4, right)
-    return gather_half(jnp.concatenate([left, right], axis=0), 1, value)
-
-
-def rows_kernel(main_ref, next_ref, parts_ref, weights_ref, own_ref, out_ref, left):
+    half = jnp.concatenate([left, right], axis=0)
+    return half, lambda: gather_half(half, 1, value)
+
+
+def rows_kernel(main_ref, next_ref, parts_ref, weights_ref, own_ref, after_ref, out_ref, left, own, sems):
     step = pl.program_id(0)
     steps = pl.num_programs(0) // 2
     ch = left.shape[0]
     rows = main_ref.shape[1]
+
+    def copy(c):
+        return pltpu.make_async_copy(own_ref.at[c], own.at[c], sems.at[c])
+
+    @pl.when(step == 0)
+    def _():
+        for c in range(ch):
+            copy(c).start()
 
     @pl.when(step < steps)
     def _():
@@ -397,11 +432,12 @@
 
     @pl.when(step >= steps)
     def _():
-        each = own_ref.shape[0]
+        each = out_ref.shape[0]
         for index in range(each):
-            products = jnp.dot(
-                own_ref[index], left[(step - steps) * each + index], preferred_element_type=jnp.float32
-            )
+            c = (step - steps) * each + index
+            copy(c).wait()
+            spectra = jnp.concatenate([own[c, part] for part in range(own.shape[1])], axis=1)
+            products = jnp.dot(spectra, left[c], preferred_element_type=jnp.float32)
             count = products.shape[0]
             largest = jnp.maximum(jnp.max(jnp.abs(products), axis=0, keepdims=True), 2.0**-60)
             power = jnp.floor(jnp.log2(largest))
@@ -411,33 +447,37 @@
             out_ref[index, count:, :] = line.astype(jnp.int32).astype(jnp.int16)
 
 
-def row_products(words, parts, own, weights, index):
-    ch, count, width = own.shape
-    rows = LANES
+def row_products(words, parts, own, weights, after):
+    ch, steps, count, width = own.shape
+    rows = words.shape[1]
     main = STEPS * STEP * ch
-    steps = width // (2 * STEPS * STEP)
     each = ch // steps
     return pl.pallas_call(
         rows_kernel,
         grid=(2 * steps,),
         in_specs=[
-            pl.BlockSpec((main, rows), lambda i: (jnp.minimum(i, steps - 1), index)),
-            pl.BlockSpec((STEP * ch, rows), lambda i: ((jnp.minimum(i, steps - 1) + 1) * STEPS, index)),
-            pl.BlockSpec((parts.shape[0], rows), lambda i: (0, index)),
+            pl.BlockSpec((main, rows), lambda i: (jnp.minimum(i, steps - 1), 0)),
+            pl.BlockSpec((STEP * ch, rows), lambda i: ((jnp.minimum(i, steps - 1) + 1) * STEPS, 0)),
+            pl.BlockSpec(parts.shape, lambda i: (0, 0)),
             pl.BlockSpec(weights.shape, lambda i: (0, 0)),
-            pl.BlockSpec((each, count, width), lambda i: (jnp.maximum(i - steps, 0), 0, 0)),
+            pl.BlockSpec(memory_space=pltpu.HBM),
+            pl.BlockSpec(memory_space=pl.ANY),
         ],
         out_specs=pl.BlockSpec((each, count + 16, 2 * rows), lambda i: (jnp.maximum(i - steps, 0), 0, 0)),
         out_shape=jax.ShapeDtypeStruct((ch, count + 16, 2 * rows), jnp.int16),
-        scratch_shapes=[pltpu.VMEM((ch, width, 2 * rows), jnp.bfloat16)],
-        compiler_params=pltpu.CompilerParams(vmem_limit_bytes=18 << 20),
+        scratch_shapes=[
+            pltpu.VMEM((ch, steps * width, 2 * rows), jnp.bfloat16),
+            pltpu.VMEM(own.shape, jnp.bfloat16),
+            pltpu.SemaphoreType.DMA((ch,)),
+        ],
+        compiler_params=pltpu.CompilerParams(vmem_limit_bytes=24 << 20),
         cost_estimate=pl.CostEstimate(
-            flops=4 * width * ch * SPAN * ch * rows + 4 * ch * width * rows * count,
+            flops=4 * steps * width * ch * SPAN * ch * rows + 4 * ch * steps * width * rows * count,
             bytes_accessed=2 * words.size + 2 * own.size + 4 * ch * rows * count,
             transcendentals=0,
         ),
         name="row_products",
-    )(words, words, parts, weights, own)
+    )(words, words, parts, weights, own, after)
 
 
 def finish_kernel(scale, slot_ref, coded_ref, *refs):
@@ -511,12 +551,20 @@
     weights = jnp.asarray(filter_weights(ch))
     slots = (feed_slot[:ROWS] - lax.axis_index("feed") * count).reshape(1, ROWS)
     picked = select_rows(words, scales, slots, total)
-    own, zero = own_spectra(words, scales.astype(jnp.float32), weights, ch, spectra)
-    rows = sum_over_feed(picked, zero[0, 0])
-    parts = rows[lines : lines + 4 * ch]
+    held = []
+
+    def work(after):
+        own, zero = own_spectra(words, scales.astype(jnp.float32), weights, ch, spectra, after)
+        held.append(own)
+        return zero[0, 0]
+
+    sums = [sum_over_feed(value, None if index else work) for index, value in enumerate(picked)]
+    own = held[0]
     out = None
     for index in range(pieces):
-        coded = row_products(rows, parts, own, weights, index)
+        rows = sums[index][1]()
+        parts = rows[lines : lines + 4 * ch]
+        coded = row_products(rows, parts, own, weights, sums[-1][0])
         moved = lax.all_to_all(coded, "feed", split_axis=0, concat_axis=0, tiled=True)
         out = finish(moved, feed_slot, index, pieces, 1.0 / spectra, out)
     feeds = feed_slot.shape[0]

time: 248 us -> 213 us (0.86)
  waiting for transfers between devices: 128 us -> 97.5 us
  local copies, waits for them, and re-layouts: 26.8 us -> 12.8 us
  starting transfers between devices: 25.6 us -> 36.7 us
  other arithmetic: 10.9 us -> 6.94 us
    ppermute x12 -> x24, waiting for transfers between devices: 53.5 us -> 28 us  [swap(): return lax.ppermute(value, 'feed', pairs)]
    ppermute x12 -> x24, starting transfers between devices: 13.6 us -> 24.8 us  [swap(): return lax.ppermute(value, 'feed', pairs)]
    unnamed x24, local copies, waits for them, and re-layouts: 20.4 us -> 10.1 us
    all_to_all x2, waiting for transfers between devices: 74.5 us -> 69.5 us  [through_rows(): lax.all_to_all(coded, 'feed', split_axis=0, concat_axis=0, tiled=True)]
    pallas_call x2, Pallas kernels: 22.5 us -> 26.7 us  [row_products(): pl.pallas_call(rows_kernel, grid=(2 * steps,), in_specs=[pl.BlockSpec((ma...]
    add x4 -> x10, other arithmetic: 5.66 us -> 4.12 us  [reduce_half(): return keep + swap(send, bit)]
  transfers between devices with their start and end apart: 14 -> 26, of which waited for: 11 -> 15; matrix products, arithmetic and copies ran while one was open for 4% -> 4% of each run, Pallas kernels for 13% -> 16%
where the time goes in v7:
time: 213 us
  waiting for transfers between devices  97.5 us (46%)
  Pallas kernels  58.2 us (27%)
  starting transfers between devices  36.7 us (17%)
  local copies, waits for them, and re-layouts  12.8 us (6%)
  other arithmetic  6.94 us (3%)
    all_to_all x2, waiting for transfers between devices, through_rows(): lax.all_to_all(coded, 'feed', split_axis=0, concat_axis=0, tiled=True)  69.5 us
    ppermute x24, waiting for transfers between devices, swap(): return lax.ppermute(value, 'feed', pairs)  28 us
    pallas_call x2, Pallas kernels, row_products(): pl.pallas_call(rows_kernel, grid=(2 * steps,), in_specs=[pl.BlockSpec((ma...  26.7 us
    ppermute x24, starting transfers between devices, swap(): return lax.ppermute(value, 'feed', pairs)  24.8 us
    pallas_call x2, Pallas kernels, finish(): pl.pallas_call(functools.partial(finish_kernel, scale), grid=(1,), in_spe...  19.3 us
    all_to_all x2, starting transfers between devices, through_rows(): lax.all_to_all(coded, 'feed', split_axis=0, concat_axis=0, tiled=True)  12 us
    unnamed x24, local copies, waits for them, and re-layouts  10.1 us
    pallas_call x1, Pallas kernels, own_spectra(): pl.pallas_call(own_kernel, grid=(steps,), in_specs=[pl.BlockSpec((main, c...  9.61 us
  transfers between devices with their start and end apart: 26, of which 15 were waited for; matrix products, arithmetic and copies ran while one was open for 4% of the time, Pallas kernels for 16%

profile of v7, /device:TPU:13, one launch (start us, length us, event | category | flops | bytes accessed | tf_op | source)
XLA Modules:
  0.0 212.6 jit_solution(14467176074647722261)
XLA Ops:
  0.0 0.8 fusion.2
  0.9 0.7 slice_subtract_fusion
  1.6 3.4 %copy-done = s32[256,16,519]{0,1,2:T(8,128)S(1)} copy-done((s32[256,16,519]{0,1,2:T(8,128)S(1)}, s32[256,16,519]{0,1,2:T(8,128)}, u32[]{:S(2)}) %copy-start) | copy-done | bytes 8503320
  5.0 2.6 %select_rows.1 = (bf16[8448,128]{1,0:T(8,128)(2,1)S(1)}, bf16[8448,128]{1,0:T(8,128)(2,1)S(1)}) custom-call(s32[1,256]{1,0:T(1,128)S(1)} %bitcast.19, s32[8304,256]{1,0:T(8,128)S(1)} %bitcast.13, bf16[64,256]{1,0:T(8,128)(2,1)S(1)} %pad_maximum_fusion.2.parts_ref), custom_call_target="tpu_custom_call" | custom-call | tf_op jit(solution)/shard_map/select_rows/pallas_call | solution.py:353
  7.7 0.7 collective-permute-start.12
  8.4 0.5 copy-done.3
  9.0 1.1 constant_dynamic-slice_fusion.9
  10.0 0.7 collective-permute-start
  10.9 1.8 dynamic-slice_add_fusion
  13.4 1.8 dynamic-slice_add_fusion.1
  15.3 1.1 collective-permute-start.6
  16.4 1.3 collective-permute-start.1
  17.8 2.9 %collective-permute-done.13 = bf16[1056,128]{1,0:T(8,128)(2,1)S(1)} collective-permute-done((bf16[1056,128]{1,0:T(8,128)(2,1)S(1)}, bf16[1056,128]{1,0:T(8,128)(2,1)S(1)}, u32[]{:S(2)}, u32[]{:S(2)}) %collective-permute-start.13) | collective-permute-done | bytes 270368 | tf_op jit(solution)/shard_map/ppermute | solution.py:370
  21.1 0.9 collective-permute-start.19
  22.0 4.4 %collective-permute-done.6 = bf16[1056,128]{1,0:T(8,128)(2,1)S(1)} collective-permute-done((bf16[1056,128]{1,0:T(8,128)(2,1)S(1)}, bf16[1056,128]{1,0:T(8,128)(2,1)S(1)}, u32[]{:S(2)}, u32[]{:S(2)}) %collective-permute-start.6) | collective-permute-done | bytes 270368 | tf_op jit(solution)/shard_map/ppermute | solution.py:370
  26.5 1.3 collective-permute-start.7
  28.2 1.1 collective-permute-done.14
  29.3 2.4 %collective-permute-start.15 = (bf16[528,128]{1,0:T(8,128)(2,1)S(1)}, bf16[528,128]{1,0:T(8,128)(2,1)S(1)}, u32[]{:S(2)}, u32[]{:S(2)}) collective-permute-start(bf16[528,128]{1,0:T(8,128)(2,1)S(1)} %dynamic-slice_add_fusion.7.after_ref), channel_id=1, source_target_pairs={{0,8},{1,9},{2,10},{3,11},{4,12},{5,13},{6,14},{7,15},{8,0},{9,1},... | collective-permute-start | bytes 405512 | tf_op jit(solution)/shard_map/ppermute | solution.py:370
  31.9 2.4 %collective-permute-start.8 = (bf16[528,128]{1,0:T(8,128)(2,1)S(1)}, bf16[528,128]{1,0:T(8,128)(2,1)S(1)}, u32[]{:S(2)}, u32[]{:S(2)}) collective-permute-start(bf16[528,128]{1,0:T(8,128)(2,1)S(1)} %dynamic-slice_add_fusion.8), channel_id=1, source_target_pairs={{0,8},{1,9},{2,10},{3,11},{4,12},{5,13},{6,14},{7,15},{8,0},{9,1},... | collective-permute-start | bytes 405512 | tf_op jit(solution)/shard_map/ppermute | solution.py:370
  34.5 9.6 %own_spectra.1 = (bf16[16,8,256,128]{3,2,1,0:T(8,128)(2,1)S(1)}, bf16[16,128]{1,0:T(8,128)(2,1)S(1)}) custom-call(s32[8304,256]{1,0:T(8,128)S(1)} %bitcast.16, s32[8304,256]{1,0:T(8,128)S(1)} %bitcast.17, f32[32,256]{1,0:T(8,128)S(1)} %bitcast.18, bf16[256,256]{1,0:T(8,128)(2,1)S(1)} %copy-done.7, bf16[528,128]{1,0:T(8,128)(2,1)S(1)} %dynamic-slice_add_fusion.7.after_ref), custom_call_target="tpu_custom_call" | custom-call | flops 4294967296 | bytes 16891904 | tf_op jit(solution)/shard_map/own_spectra/pallas_call | solution.py:295
  44.1 0.6 slice.29
  44.7 3.9 %collective-permute-done.20 = bf16[528,128]{1,0:T(8,128)(2,1)S(1)} collective-permute-done((bf16[528,128]{1,0:T(8,128)(2,1)S(1)}, bf16[528,128]{1,0:T(8,128)(2,1)S(1)}, u32[]{:S(2)}, u32[]{:S(2)}) %collective-permute-start.20) | collective-permute-done | bytes 135200 | tf_op jit(solution)/shard_map/ppermute | solution.py:370
  48.7 0.9 collective-permute-start.21
  49.5 1.9 collective-permute-done.8
  51.5 0.9 collective-permute-start.9
  52.4 1.9 collective-permute-done.3
  54.6 0.6 constant_dynamic-update-slice_fusion.9
  55.3 1.4 collective-permute-start.16
  57.0 1.4 collective-permute-start.10
  58.5 1.1 collective-permute-start.5
  59.6 1.4 collective-permute-done.16
  61.0 1.5 collective-permute-start.17
  62.5 4.3 %collective-permute-done.22 = bf16[1056,128]{1,0:T(8,128)(2,1)S(1)} collective-permute-done((bf16[1056,128]{1,0:T(8,128)(2,1)S(1)}, bf16[1056,128]{1,0:T(8,128)(2,1)S(1)}, u32[]{:S(2)}, u32[]{:S(2)}) %collective-permute-start.22) | collective-permute-done | bytes 270368 | tf_op jit(solution)/shard_map/ppermute | solution.py:370
  66.8 1.5 collective-permute-done.17
  68.5 5.1 %collective-permute-start.23 = (bf16[4224,128]{1,0:T(8,128)(2,1)S(1)}, bf16[4224,128]{1,0:T(8,128)(2,1)S(1)}, u32[]{:S(2)}, u32[]{:S(2)}) collective-permute-start(bf16[4224,128]{1,0:T(8,128)(2,1)S(1)} %get-tuple-element.21), channel_id=1, source_target_pairs={{0,1},{1,0},{2,3},{3,2},{4,5},{5,4},{6,7},{7,6},{8,9},{9,8},{10,11... | collective-permute-start | bytes 3244040 | tf_op jit(solution)/shard_map/ppermute | solution.py:370
  73.9 2.0 collective-permute-done.23
  76.1 13.4 %row_products.3 = s16[16,272,256]{2,1,0:T(8,128)(2,1)S(1)} custom-call(bf16[8448,128]{1,0:T(8,128)(2,1)S(1)} %constant_dynamic-update-slice_fusion.main_ref.next_ref, bf16[8448,128]{1,0:T(8,128)(2,1)S(1)} %constant_dynamic-update-slice_fusion.main_ref.next_ref, bf16[64,128]{1,0:T(8,128)(2,1)S(1)} %slice.37.parts_ref, bf16[256,256]{1,0:T(8,128)(2,1)S(1)} %copy-done.7, ...), custom_call_target="tpu_custom_call" | custom-call | flops 4294967296 | bytes 12648448 | tf_op jit(solution)/shard_map/row_products/pallas_call | solution.py:455
  89.5 1.4 copy-done.5
  90.9 7.0 %all-to-all-start.1 = ((s16[16,272,256]{2,1,0:T(8,128)(2,1)}), s16[16,272,256]{2,1,0:T(8,128)(2,1)}, u32[]{:S(2)}, u32[]{:S(2)}) async-start(s16[16,272,256]{2,1,0:T(8,128)(2,1)} %copy-done.5), calls=%async_computation.1 | async-start | bytes 4456448 | tf_op jit(solution)/shard_map/all_to_all | solution.py:568
  98.3 2.4 %collective-permute-done.11 = bf16[4224,128]{1,0:T(8,128)(2,1)S(1)} collective-permute-done((bf16[4224,128]{1,0:T(8,128)(2,1)S(1)}, bf16[4224,128]{1,0:T(8,128)(2,1)S(1)}, u32[]{:S(2)}, u32[]{:S(2)}) %collective-permute-start.11) | collective-permute-done | bytes 1081376 | tf_op jit(solution)/shard_map/ppermute | solution.py:370
  100.8 3.4 %copy-done.2 = bf16[16,8,256,128]{3,2,1,0:T(8,128)(2,1)S(1)} copy-done((bf16[16,8,256,128]{3,2,1,0:T(8,128)(2,1)S(1)}, bf16[16,8,256,128]{3,2,1,0:T(8,128)(2,1)}, u32[]{:S(2)}) %copy-start.2) | copy-done | bytes 8388632
  104.2 13.3 %row_products.2 = s16[16,272,256]{2,1,0:T(8,128)(2,1)S(1)} custom-call(bf16[8448,128]{1,0:T(8,128)(2,1)S(1)} %constant_dynamic-update-slice_fusion.10.main_ref.next_ref, bf16[8448,128]{1,0:T(8,128)(2,1)S(1)} %constant_dynamic-update-slice_fusion.10.main_ref.next_ref, bf16[64,128]{1,0:T(8,128)(2,1)S(1)} %slice.34.parts_ref, bf16[256,256]{1,0:T(8,128)(2,1)S(1)} %copy-done.7, ...), custom_call_target="tpu_custom_call" | custom-call | flops 4294967296 | bytes 12648448 | tf_op jit(solution)/shard_map/row_products/pallas_call | solution.py:455
  117.6 1.4 copy-done.6
  119.0 29.3 %all-to-all-done.1.coded_ref = s16[16,272,256]{2,1,0:T(8,128)(2,1)} async-done(((s16[16,272,256]{2,1,0:T(8,128)(2,1)}), s16[16,272,256]{2,1,0:T(8,128)(2,1)}, u32[]{:S(2)}, u32[]{:S(2)}) %all-to-all-start.1) | async-done | bytes 2228256 | tf_op jit(solution)/shard_map/all_to_all | solution.py:568
  148.3 4.9 %all-to-all-start = ((s16[16,272,256]{2,1,0:T(8,128)(2,1)}), s16[16,272,256]{2,1,0:T(8,128)(2,1)S(1)}, u32[]{:S(2)}, u32[]{:S(2)}) async-start(s16[16,272,256]{2,1,0:T(8,128)(2,1)} %copy-done.6), calls=%async_computation | async-start | bytes 4456448 | tf_op jit(solution)/shard_map/all_to_all | solution.py:568
  153.2 10.1 %finish.2.refs_0_ = f32[16384,128]{1,0:T(8,128)} custom-call(s32[4096]{0:T(1024)S(1)} %copy-done.8, s16[16,272,256]{2,1,0:T(8,128)(2,1)} %all-to-all-done.1.coded_ref), custom_call_target="tpu_custom_call" | custom-call | tf_op jit(solution)/shard_map/finish/pallas_call | solution.py:521
  163.2 40.2 %all-to-all-done.coded_ref = s16[16,272,256]{2,1,0:T(8,128)(2,1)S(1)} async-done(((s16[16,272,256]{2,1,0:T(8,128)(2,1)}), s16[16,272,256]{2,1,0:T(8,128)(2,1)S(1)}, u32[]{:S(2)}, u32[]{:S(2)}) %all-to-all-start) | async-done | bytes 2228256 | tf_op jit(solution)/shard_map/all_to_all | solution.py:568
  203.4 9.2 %finish.3 = f32[16384,128]{1,0:T(8,128)} custom-call(s32[4096]{0:T(1024)S(1)} %copy-done.8, s16[16,272,256]{2,1,0:T(8,128)(2,1)S(1)} %all-to-all-done.coded_ref, f32[16384,128]{1,0:T(8,128)} %finish.2.refs_0_), custom_call_target="tpu_custom_call", output_to_operand_aliasing={{}: (2, {})} | custom-call | tf_op jit(solution)/shard_map/finish/pallas_call | solution.py:521
  (83 shorter events, 4.4 us)
Async XLA Ops:
  1.6 3.4 %copy-start = (s32[256,16,519]{0,1,2:T(8,128)S(1)}, s32[256,16,519]{0,1,2:T(8,128)}, u32[]{:S(2)}) copy-start(s32[256,16,519]{0,1,2:T(8,128)} %param.4) | copy-start | bytes 25509892
  7.6 1.4 copy-start.3
  7.7 3.2 %collective-permute-start.12 = (bf16[4224,128]{1,0:T(8,128)(2,1)S(1)}, bf16[4224,128]{1,0:T(8,128)(2,1)}, u32[]{:S(2)}, u32[]{:S(2)}) collective-permute-start(bf16[4224,128]{1,0:T(8,128)(2,1)S(1)} %constant_dynamic-slice_fusion.4), channel_id=1, source_target_pairs={{0,1},{1,0},{2,3},{3,2},{4,5},{5,4},{6,7},{7,6},{8,9},{9,8},{10,11... | collective-permute-start | bytes 3244040 | tf_op jit(solution)/shard_map/ppermute | solution.py:370
  9.0 25.5 %slice-start = ((s8[8503296]{0:T(1024)(128)(4,1)}), s8[114688]{0:T(1024)(128)(4,1)S(1)}, s32[]{:S(2)}) async-start(s8[8503296]{0:T(1024)(128)(4,1)} %bitcast.14), calls=%async_computation.2 | async-start | bytes 229376
  10.0 3.3 %collective-permute-start = (bf16[4224,128]{1,0:T(8,128)(2,1)}, bf16[4224,128]{1,0:T(8,128)(2,1)}, u32[]{:S(2)}, u32[]{:S(2)}) collective-permute-start(bf16[4224,128]{1,0:T(8,128)(2,1)} %constant_dynamic-slice_fusion.9), channel_id=1, source_target_pairs={{0,1},{1,0},{2,3},{3,2},{4,5},{5,4},{6,7},{7,6},{8,9},{9,8},{10,11... | collective-permute-start | bytes 3244040 | tf_op jit(solution)/shard_map/ppermute | solution.py:370
  12.7 21.7 %slice-start.1 = ((s8[8503296]{0:T(1024)(128)(4,1)}), s8[4194304]{0:T(1024)(128)(4,1)S(1)}, s32[]{:S(2)}) async-start(s8[8503296]{0:T(1024)(128)(4,1)} %bitcast.14), calls=%async_computation.3 | async-start | bytes 8388608
  12.9 7.8 %collective-permute-start.13 = (bf16[1056,128]{1,0:T(8,128)(2,1)S(1)}, bf16[1056,128]{1,0:T(8,128)(2,1)S(1)}, u32[]{:S(2)}, u32[]{:S(2)}) collective-permute-start(bf16[1056,128]{1,0:T(8,128)(2,1)S(1)} %constant_dynamic-slice_fusion.3), channel_id=1, source_target_pairs={{0,2},{1,3},{2,0},{3,1},{4,6},{5,7},{6,4},{7,5},{8,10},{9,11},{10,... | collective-permute-start | bytes 811016 | tf_op jit(solution)/shard_map/ppermute | solution.py:370
  13.2 7.8 %collective-permute-start.18 = (bf16[1056,128]{1,0:T(8,128)(2,1)S(1)}, bf16[1056,128]{1,0:T(8,128)(2,1)S(1)}, u32[]{:S(2)}, u32[]{:S(2)}) collective-permute-start(bf16[1056,128]{1,0:T(8,128)(2,1)S(1)} %constant_dynamic-slice_fusion.1), channel_id=1, source_target_pairs={{0,4},{1,5},{2,6},{3,7},{4,0},{5,1},{6,2},{7,3},{8,12},{9,13},{10,... | collective-permute-start | bytes 811016 | tf_op jit(solution)/shard_map/ppermute | solution.py:370
  15.2 19.3 %slice-start.2 = ((s8[8503296]{0:T(1024)(128)(4,1)}), s8[4194304]{0:T(1024)(128)(4,1)S(1)}, s32[]{:S(2)}) async-start(s8[8503296]{0:T(1024)(128)(4,1)} %bitcast.14), calls=%async_computation.4 | async-start | bytes 8388608
  15.3 11.1 %collective-permute-start.6 = (bf16[1056,128]{1,0:T(8,128)(2,1)S(1)}, bf16[1056,128]{1,0:T(8,128)(2,1)S(1)}, u32[]{:S(2)}, u32[]{:S(2)}) collective-permute-start(bf16[1056,128]{1,0:T(8,128)(2,1)S(1)} %constant_dynamic-slice_fusion.6), channel_id=1, source_target_pairs={{0,4},{1,5},{2,6},{3,7},{4,0},{5,1},{6,2},{7,3},{8,12},{9,13},{10,... | collective-permute-start | bytes 811016 | tf_op jit(solution)/shard_map/ppermute | solution.py:370
  16.4 11.4 %collective-permute-start.1 = (bf16[1056,128]{1,0:T(8,128)(2,1)S(1)}, bf16[1056,128]{1,0:T(8,128)(2,1)S(1)}, u32[]{:S(2)}, u32[]{:S(2)}) collective-permute-start(bf16[1056,128]{1,0:T(8,128)(2,1)S(1)} %constant_dynamic-slice_fusion.8), channel_id=1, source_target_pairs={{0,2},{1,3},{2,0},{3,1},{4,6},{5,7},{6,4},{7,5},{8,10},{9,11},{10,... | collective-permute-start | bytes 811016 | tf_op jit(solution)/shard_map/ppermute | solution.py:370
  20.7 8.6 %collective-permute-start.14 = (bf16[528,128]{1,0:T(8,128)(2,1)S(1)}, bf16[528,128]{1,0:T(8,128)(2,1)S(1)}, u32[]{:S(2)}, u32[]{:S(2)}) collective-permute-start(bf16[528,128]{1,0:T(8,128)(2,1)S(1)} %constant_dynamic-slice_fusion.2), channel_id=1, source_target_pairs={{0,4},{1,5},{2,6},{3,7},{4,0},{5,1},{6,2},{7,3},{8,12},{9,13},{10,... | collective-permute-start | bytes 405512 | tf_op jit(solution)/shard_map/ppermute | solution.py:370
  21.0 13.4 %copy-start.7 = (bf16[256,256]{1,0:T(8,128)(2,1)S(1)}, bf16[256,256]{1,0:T(8,128)(2,1)}, u32[]{:S(2)}) copy-start(bf16[256,256]{1,0:T(8,128)(2,1)} %constant.222.clone.weights_ref) | copy-start | bytes 393220
  21.1 10.6 %collective-permute-start.19 = (bf16[528,128]{1,0:T(8,128)(2,1)S(1)}, bf16[528,128]{1,0:T(8,128)(2,1)S(1)}, u32[]{:S(2)}, u32[]{:S(2)}) collective-permute-start(bf16[528,128]{1,0:T(8,128)(2,1)S(1)} %constant_dynamic-slice_fusion), channel_id=1, source_target_pairs={{0,2},{1,3},{2,0},{3,1},{4,6},{5,7},{6,4},{7,5},{8,10},{9,11},{10,... | collective-permute-start | bytes 405512 | tf_op jit(solution)/shard_map/ppermute | solution.py:370
  26.5 5.4 %collective-permute-start.7 = (bf16[528,128]{1,0:T(8,128)(2,1)S(1)}, bf16[528,128]{1,0:T(8,128)(2,1)S(1)}, u32[]{:S(2)}, u32[]{:S(2)}) collective-permute-start(bf16[528,128]{1,0:T(8,128)(2,1)S(1)} %constant_dynamic-slice_fusion.5), channel_id=1, source_target_pairs={{0,2},{1,3},{2,0},{3,1},{4,6},{5,7},{6,4},{7,5},{8,10},{9,11},{10,... | collective-permute-start | bytes 405512 | tf_op jit(solution)/shard_map/ppermute | solution.py:370
  27.9 6.4 %collective-permute-start.2 = (bf16[528,128]{1,0:T(8,128)(2,1)S(1)}, bf16[528,128]{1,0:T(8,128)(2,1)S(1)}, u32[]{:S(2)}, u32[]{:S(2)}) collective-permute-start(bf16[528,128]{1,0:T(8,128)(2,1)S(1)} %constant_dynamic-slice_fusion.7), channel_id=1, source_target_pairs={{0,4},{1,5},{2,6},{3,7},{4,0},{5,1},{6,2},{7,3},{8,12},{9,13},{10,... | collective-permute-start | bytes 405512 | tf_op jit(solution)/shard_map/ppermute | solution.py:370
  29.3 25.3 %collective-permute-start.15 = (bf16[528,128]{1,0:T(8,128)(2,1)S(1)}, bf16[528,128]{1,0:T(8,128)(2,1)S(1)}, u32[]{:S(2)}, u32[]{:S(2)}) collective-permute-start(bf16[528,128]{1,0:T(8,128)(2,1)S(1)} %dynamic-slice_add_fusion.7.after_ref), channel_id=1, source_target_pairs={{0,8},{1,9},{2,10},{3,11},{4,12},{5,13},{6,14},{7,15},{8,0},{9,1},... | collective-permute-start | bytes 405512 | tf_op jit(solution)/shard_map/ppermute | solution.py:370
  31.8 16.8 %collective-permute-start.20 = (bf16[528,128]{1,0:T(8,128)(2,1)S(1)}, bf16[528,128]{1,0:T(8,128)(2,1)S(1)}, u32[]{:S(2)}, u32[]{:S(2)}) collective-permute-start(bf16[528,128]{1,0:T(8,128)(2,1)S(1)} %dynamic-slice_add_fusion.6), channel_id=1, source_target_pairs={{0,8},{1,9},{2,10},{3,11},{4,12},{5,13},{6,14},{7,15},{8,0},{9,1},... | collective-permute-start | bytes 405512 | tf_op jit(solution)/shard_map/ppermute | solution.py:370
  31.9 19.6 %collective-permute-start.8 = (bf16[528,128]{1,0:T(8,128)(2,1)S(1)}, bf16[528,128]{1,0:T(8,128)(2,1)S(1)}, u32[]{:S(2)}, u32[]{:S(2)}) collective-permute-start(bf16[528,128]{1,0:T(8,128)(2,1)S(1)} %dynamic-slice_add_fusion.8), channel_id=1, source_target_pairs={{0,8},{1,9},{2,10},{3,11},{4,12},{5,13},{6,14},{7,15},{8,0},{9,1},... | collective-permute-start | bytes 405512 | tf_op jit(solution)/shard_map/ppermute | solution.py:370
  34.4 20.0 %collective-permute-start.3 = (bf16[528,128]{1,0:T(8,128)(2,1)S(1)}, bf16[528,128]{1,0:T(8,128)(2,1)S(1)}, u32[]{:S(2)}, u32[]{:S(2)}) collective-permute-start(bf16[528,128]{1,0:T(8,128)(2,1)S(1)} %dynamic-slice_add_fusion.9), channel_id=1, source_target_pairs={{0,8},{1,9},{2,10},{3,11},{4,12},{5,13},{6,14},{7,15},{8,0},{9,1},... | collective-permute-start | bytes 405512 | tf_op jit(solution)/shard_map/ppermute | solution.py:370
  44.1 32.0 %copy-start.1 = (bf16[16,8,256,128]{3,2,1,0:T(8,128)(2,1)}, bf16[16,8,256,128]{3,2,1,0:T(8,128)(2,1)S(1)}, u32[]{:S(2)}) copy-start(bf16[16,8,256,128]{3,2,1,0:T(8,128)(2,1)S(1)} %get-tuple-element.11.own_ref) | copy-start | bytes 25165828
  48.7 8.0 %collective-permute-start.21 = (bf16[528,128]{1,0:T(8,128)(2,1)S(1)}, bf16[528,128]{1,0:T(8,128)(2,1)S(1)}, u32[]{:S(2)}, u32[]{:S(2)}) collective-permute-start(bf16[528,128]{1,0:T(8,128)(2,1)S(1)} %get-tuple-element.16), channel_id=1, source_target_pairs={{0,2},{1,3},{2,0},{3,1},{4,6},{5,7},{6,4},{7,5},{8,10},{9,11},{10,... | collective-permute-start | bytes 405512 | tf_op jit(solution)/shard_map/ppermute | solution.py:370
  51.5 5.4 %collective-permute-start.9 = (bf16[528,128]{1,0:T(8,128)(2,1)S(1)}, bf16[528,128]{1,0:T(8,128)(2,1)S(1)}, u32[]{:S(2)}, u32[]{:S(2)}) collective-permute-start(bf16[528,128]{1,0:T(8,128)(2,1)S(1)} %get-tuple-element.20), channel_id=1, source_target_pairs={{0,2},{1,3},{2,0},{3,1},{4,6},{5,7},{6,4},{7,5},{8,10},{9,11},{10,... | collective-permute-start | bytes 405512 | tf_op jit(solution)/shard_map/ppermute | solution.py:370
  54.4 4.0 %collective-permute-start.4 = (bf16[528,128]{1,0:T(8,128)(2,1)S(1)}, bf16[528,128]{1,0:T(8,128)(2,1)S(1)}, u32[]{:S(2)}, u32[]{:S(2)}) collective-permute-start(bf16[528,128]{1,0:T(8,128)(2,1)S(1)} %get-tuple-element.18), channel_id=1, source_target_pairs={{0,4},{1,5},{2,6},{3,7},{4,0},{5,1},{6,2},{7,3},{8,12},{9,13},{10,... | collective-permute-start | bytes 405512 | tf_op jit(solution)/shard_map/ppermute | solution.py:370
  55.3 5.7 %collective-permute-start.16 = (bf16[528,128]{1,0:T(8,128)(2,1)S(1)}, bf16[528,128]{1,0:T(8,128)(2,1)S(1)}, u32[]{:S(2)}, u32[]{:S(2)}) collective-permute-start(bf16[528,128]{1,0:T(8,128)(2,1)S(1)} %get-tuple-element.14), channel_id=1, source_target_pairs={{0,4},{1,5},{2,6},{3,7},{4,0},{5,1},{6,2},{7,3},{8,12},{9,13},{10,... | collective-permute-start | bytes 405512 | tf_op jit(solution)/shard_map/ppermute | solution.py:370
  56.7 11.6 %copy-start.4 = (bf16[8448,128]{1,0:T(8,128)(2,1)S(1)}, bf16[8448,128]{1,0:T(8,128)(2,1)}, u32[]{:S(2)}) copy-start(bf16[8448,128]{1,0:T(8,128)(2,1)} %copy-done.3) | copy-start | bytes 6488068
  56.7 10.1 %collective-permute-start.22 = (bf16[1056,128]{1,0:T(8,128)(2,1)S(1)}, bf16[1056,128]{1,0:T(8,128)(2,1)S(1)}, u32[]{:S(2)}, u32[]{:S(2)}) collective-permute-start(bf16[1056,128]{1,0:T(8,128)(2,1)S(1)} %constant_dynamic-update-slice_fusion.4), channel_id=1, source_target_pairs={{0,4},{1,5},{2,6},{3,7},{4,0},{5,1},{6,2},{7,3},{8,12},{9,13},{10,... | collective-permute-start | bytes 811016 | tf_op jit(solution)/shard_map/ppermute | solution.py:370
  57.0 16.6 %collective-permute-start.10 = (bf16[1056,128]{1,0:T(8,128)(2,1)S(1)}, bf16[1056,128]{1,0:T(8,128)(2,1)S(1)}, u32[]{:S(2)}, u32[]{:S(2)}) collective-permute-start(bf16[1056,128]{1,0:T(8,128)(2,1)S(1)} %constant_dynamic-update-slice_fusion.14), channel_id=1, source_target_pairs={{0,4},{1,5},{2,6},{3,7},{4,0},{5,1},{6,2},{7,3},{8,12},{9,13},{10,... | collective-permute-start | bytes 811016 | tf_op jit(solution)/shard_map/ppermute | solution.py:370
  58.5 15.1 %collective-permute-start.5 = (bf16[1056,128]{1,0:T(8,128)(2,1)S(1)}, bf16[1056,128]{1,0:T(8,128)(2,1)S(1)}, u32[]{:S(2)}, u32[]{:S(2)}) collective-permute-start(bf16[1056,128]{1,0:T(8,128)(2,1)S(1)} %constant_dynamic-update-slice_fusion.18), channel_id=1, source_target_pairs={{0,2},{1,3},{2,0},{3,1},{4,6},{5,7},{6,4},{7,5},{8,10},{9,11},{10,... | collective-permute-start | bytes 811016 | tf_op jit(solution)/shard_map/ppermute | solution.py:370
  61.0 7.3 %collective-permute-start.17 = (bf16[1056,128]{1,0:T(8,128)(2,1)S(1)}, bf16[1056,128]{1,0:T(8,128)(2,1)S(1)}, u32[]{:S(2)}, u32[]{:S(2)}) collective-permute-start(bf16[1056,128]{1,0:T(8,128)(2,1)S(1)} %constant_dynamic-update-slice_fusion.8), channel_id=1, source_target_pairs={{0,2},{1,3},{2,0},{3,1},{4,6},{5,7},{6,4},{7,5},{8,10},{9,11},{10,... | collective-permute-start | bytes 811016 | tf_op jit(solution)/shard_map/ppermute | solution.py:370
  68.5 7.4 %collective-permute-start.23 = (bf16[4224,128]{1,0:T(8,128)(2,1)S(1)}, bf16[4224,128]{1,0:T(8,128)(2,1)S(1)}, u32[]{:S(2)}, u32[]{:S(2)}) collective-permute-start(bf16[4224,128]{1,0:T(8,128)(2,1)S(1)} %get-tuple-element.21), channel_id=1, source_target_pairs={{0,1},{1,0},{2,3},{3,2},{4,5},{5,4},{6,7},{7,6},{8,9},{9,8},{10,11... | collective-permute-start | bytes 3244040 | tf_op jit(solution)/shard_map/ppermute | solution.py:370
  89.5 1.4 copy-start.5
  90.9 57.4 %all-to-all-start.1 = ((s16[16,272,256]{2,1,0:T(8,128)(2,1)}), s16[16,272,256]{2,1,0:T(8,128)(2,1)}, u32[]{:S(2)}, u32[]{:S(2)}) async-start(s16[16,272,256]{2,1,0:T(8,128)(2,1)} %copy-done.5), calls=%async_computation.1 | async-start | bytes 4456448 | tf_op jit(solution)/shard_map/all_to_all | solution.py:568
  97.9 2.8 %collective-permute-start.11 = (bf16[4224,128]{1,0:T(8,128)(2,1)S(1)}, bf16[4224,128]{1,0:T(8,128)(2,1)S(1)}, u32[]{:S(2)}, u32[]{:S(2)}) collective-permute-start(bf16[4224,128]{1,0:T(8,128)(2,1)S(1)} %get-tuple-element.25.after_ref), channel_id=1, source_target_pairs={{0,1},{1,0},{2,3},{3,2},{4,5},{5,4},{6,7},{7,6},{8,9},{9,8},{10,11... | collective-permute-start | bytes 3244040 | tf_op jit(solution)/shard_map/ppermute | solution.py:370
  100.8 3.4 %copy-start.2 = (bf16[16,8,256,128]{3,2,1,0:T(8,128)(2,1)S(1)}, bf16[16,8,256,128]{3,2,1,0:T(8,128)(2,1)}, u32[]{:S(2)}) copy-start(bf16[16,8,256,128]{3,2,1,0:T(8,128)(2,1)} %copy-done.1) | copy-start | bytes 25165828
  117.6 1.4 copy-start.6
  119.0 34.2 %copy-start.8 = (s32[4096]{0:T(1024)S(1)}, s32[4096]{0:T(1024)}, u32[]{:S(2)}) copy-start(s32[4096]{0:T(1024)} %slot_ref.3) | copy-start | bytes 49156
  148.3 55.1 %all-to-all-start = ((s16[16,272,256]{2,1,0:T(8,128)(2,1)}), s16[16,272,256]{2,1,0:T(8,128)(2,1)S(1)}, u32[]{:S(2)}, u32[]{:S(2)}) async-start(s16[16,272,256]{2,1,0:T(8,128)(2,1)} %copy-done.6), calls=%async_computation | async-start | bytes 4456448 | tf_op jit(solution)/shard_map/all_to_all | solution.py:568

commit v8 on v7

--- a/solution.py
+++ b/solution.py
@@ -259,7 +259,7 @@
     ]
 
 
-def own_kernel(main_ref, next_ref, gains_ref, weights_ref, after_ref, out_ref, zero_ref, held, turned, sems):
+def own_kernel(place_ref, main_ref, next_ref, gains_ref, weights_ref, after_ref, out_ref, zero_ref, held, turned, sems):
     step = pl.program_id(0)
     slot = step % 2
     ch = out_ref.shape[0]
@@ -279,7 +279,7 @@
         copy(step - 2).wait()
 
     for c in range(ch):
-        turned[slot, c] = held[c].T
+        turned[slot, c ^ place_ref[0]] = held[c].T
     copy(step).start()
 
     @pl.when(step == pl.num_programs(0) - 1)
@@ -288,7 +288,7 @@
         copy(step).wait()
 
 
-def own_spectra(words, gains, weights, ch, spectra, after):
+def own_spectra(place, words, gains, weights, ch, spectra, after):
     count = words.shape[1]
     main = STEPS * STEP * ch
     steps = spectra // (STEPS * STEP)
@@ -296,6 +296,7 @@
         own_kernel,
         grid=(steps,),
         in_specs=[
+            pl.BlockSpec(memory_space=pltpu.SMEM),
             pl.BlockSpec((main, count), lambda i: (i, 0)),
             pl.BlockSpec((STEP * ch, count), lambda i: ((i + 1) * STEPS, 0)),
             pl.BlockSpec(gains.shape, lambda i: (0, 0)),
@@ -322,7 +323,7 @@
             transcendentals=0,
         ),
         name="own_spectra",
-    )(words, words, gains, weights, after)
+    )(place, words, words, gains, weights, after)
 
 
 def select_kernel(last_rows, slots_ref, words_ref, parts_ref, *outs):
@@ -403,19 +404,32 @@
     return half, lambda: gather_half(half, 1, value)
 
 
-def rows_kernel(main_ref, next_ref, parts_ref, weights_ref, own_ref, after_ref, out_ref, left, own, sems):
+def code(products, out_ref, index):
+    largest = jnp.maximum(jnp.max(jnp.abs(products), axis=0, keepdims=True), 2.0**-60)
+    power = jnp.floor(jnp.log2(largest))
+    coded = jnp.clip(jnp.round(products * jnp.exp2(RANGE - power)), -32767.0, 32767.0)
+    count = products.shape[0]
+    out_ref[index, :count, :] = coded.astype(jnp.int32).astype(jnp.int16)
+    line = jnp.broadcast_to(power, (out_ref.shape[1] - count, power.shape[1]))
+    out_ref[index, count:, :] = line.astype(jnp.int32).astype(jnp.int16)
+
+
+def rows_kernel(
+    place_ref, main_ref, next_ref, parts_ref, weights_ref, own_ref, *refs
+):
+    out_ref, mine_ref, left, own, sems = refs[-5:]
     step = pl.program_id(0)
     steps = pl.num_programs(0) // 2
     ch = left.shape[0]
     rows = main_ref.shape[1]
 
-    def copy(c):
-        return pltpu.make_async_copy(own_ref.at[c], own.at[c], sems.at[c])
+    def copy(k):
+        return pltpu.make_async_copy(own_ref.at[k], own.at[k], sems.at[k])
 
     @pl.when(step == 0)
     def _():
-        for c in range(ch):
-            copy(c).start()
+        for k in range(ch):
+            copy(k).start()
 
     @pl.when(step < steps)
     def _():
@@ -434,20 +448,17 @@
     def _():
         each = out_ref.shape[0]
         for index in range(each):
-            c = (step - steps) * each + index
-            copy(c).wait()
-            spectra = jnp.concatenate([own[c, part] for part in range(own.shape[1])], axis=1)
-            products = jnp.dot(spectra, left[c], preferred_element_type=jnp.float32)
-            count = products.shape[0]
-            largest = jnp.maximum(jnp.max(jnp.abs(products), axis=0, keepdims=True), 2.0**-60)
-            power = jnp.floor(jnp.log2(largest))
-            coded = jnp.clip(jnp.round(products * jnp.exp2(RANGE - power)), -32767.0, 32767.0)
-            out_ref[index, :count, :] = coded.astype(jnp.int32).astype(jnp.int16)
-            line = jnp.broadcast_to(power, (out_ref.shape[1] - count, power.shape[1]))
-            out_ref[index, count:, :] = line.astype(jnp.int32).astype(jnp.int16)
-
-
-def row_products(words, parts, own, weights, after):
+            k = (step - steps) * each + index
+            copy(k).wait()
+            spectra = jnp.concatenate([own[k, part] for part in range(own.shape[1])], axis=1)
+            code(jnp.dot(spectra, left[k ^ place_ref[0]], preferred_element_type=jnp.float32), out_ref, index)
+
+    @pl.when(step == 2 * steps - 1)
+    def _():
+        mine_ref[...] = left[place_ref[0]]
+
+
+def row_products(place, words, parts, own, weights, after):
     ch, steps, count, width = own.shape
     rows = words.shape[1]
     main = STEPS * STEP * ch
@@ -456,15 +467,22 @@
         rows_kernel,
         grid=(2 * steps,),
         in_specs=[
+            pl.BlockSpec(memory_space=pltpu.SMEM),
             pl.BlockSpec((main, rows), lambda i: (jnp.minimum(i, steps - 1), 0)),
             pl.BlockSpec((STEP * ch, rows), lambda i: ((jnp.minimum(i, steps - 1) + 1) * STEPS, 0)),
             pl.BlockSpec(parts.shape, lambda i: (0, 0)),
             pl.BlockSpec(weights.shape, lambda i: (0, 0)),
             pl.BlockSpec(memory_space=pltpu.HBM),
-            pl.BlockSpec(memory_space=pl.ANY),
-        ],
-        out_specs=pl.BlockSpec((each, count + 16, 2 * rows), lambda i: (jnp.maximum(i - steps, 0), 0, 0)),
-        out_shape=jax.ShapeDtypeStruct((ch, count + 16, 2 * rows), jnp.int16),
+        ]
+        + [pl.BlockSpec(memory_space=pl.ANY)] * len(after),
+        out_specs=[
+            pl.BlockSpec((each, count + 16, 2 * rows), lambda i: (jnp.maximum(i - steps, 0), 0, 0)),
+            pl.BlockSpec((steps * width, 2 * rows), lambda i: (0, 0)),
+        ],
+        out_shape=[
+            jax.ShapeDtypeStruct((ch, count + 16, 2 * rows), jnp.int16),
+            jax.ShapeDtypeStruct((steps * width, 2 * rows), jnp.bfloat16),
+        ],
         scratch_shapes=[
             pltpu.VMEM((ch, steps * width, 2 * rows), jnp.bfloat16),
             pltpu.VMEM(own.shape, jnp.bfloat16),
@@ -477,19 +495,40 @@
             transcendentals=0,
         ),
         name="row_products",
-    )(words, words, parts, weights, own, after)
-
-
-def finish_kernel(scale, slot_ref, coded_ref, *refs):
-    out_ref, products, tile, mixed = refs[-4:]
-    sources, lines, width = coded_ref.shape
+    )(place, words, words, parts, weights, own, *after)
+
+
+def near_kernel(mine_ref, *refs):
+    *spectra_refs, out_ref = refs
+    for index, ref in enumerate(spectra_refs):
+        spectra = jnp.concatenate([ref[part] for part in range(ref.shape[0])], axis=1)
+        code(jnp.dot(spectra, mine_ref[...], preferred_element_type=jnp.float32), out_ref, index)
+
+
+def near_products(spectra, mine):
+    count = spectra[0].shape[1]
+    return pl.pallas_call(
+        near_kernel,
+        out_shape=jax.ShapeDtypeStruct((len(spectra), count + 16, mine.shape[1]), jnp.int16),
+        compiler_params=pltpu.CompilerParams(vmem_limit_bytes=12 << 20),
+        cost_estimate=pl.CostEstimate(
+            flops=2 * len(spectra) * count * mine.size, bytes_accessed=4 * spectra[0].size * len(spectra), transcendentals=0
+        ),
+        name="near_products",
+    )(mine, *spectra)
+
+
+def finish_kernel(scale, sources, slot_ref, *refs):
+    coded_refs, (out_ref, products, tile, mixed) = refs[:sources], refs[-4:]
+    lines, width = coded_refs[0].shape
     count = lines - 16
     pieces = width // LANES
     feeds = sources * count
     columns = 2 * (feeds // LANES)
     for source in range(sources):
-        power = coded_ref[source, count : count + 16, :][:1].astype(jnp.float32)
-        values = coded_ref[source, :count, :].astype(jnp.float32) * (jnp.exp2(power - RANGE) * scale)
+        coded_ref = coded_refs[source]
+        power = coded_ref[count : count + 16, :][:1].astype(jnp.float32)
+        values = coded_ref[:count, :].astype(jnp.float32) * (jnp.exp2(power - RANGE) * scale)
         for piece in range(pieces):
             products[pl.ds(source * count * pieces + piece, count, stride=pieces), :] = values[
                 :, piece * LANES : (piece + 1) * LANES
@@ -512,19 +551,18 @@
             out_ref[pl.ds(pl.multiple_of(row * columns + j * 8, 8), 8), :] = mixed[row * 8 : (row + 1) * 8, :]
 
 
-def finish(coded, feed_slot, index, pieces, scale, before):
-    sources, lines, width = coded.shape
+def finish(coded, slots, index, pieces, scale, before):
+    sources = len(coded)
+    lines, width = coded[0].shape
     rows = width // 2
     feeds = sources * (lines - 16)
     columns = 2 * (feeds // LANES)
     earlier = [] if before is None else [before]
     return pl.pallas_call(
-        functools.partial(finish_kernel, scale),
+        functools.partial(finish_kernel, scale, sources),
         grid=(1,),
-        in_specs=[
-            pl.BlockSpec(memory_space=pltpu.SMEM),
-            pl.BlockSpec(coded.shape, lambda i: (0, 0, 0)),
-        ]
+        in_specs=[pl.BlockSpec(memory_space=pltpu.SMEM)]
+        + [pl.BlockSpec((lines, width), lambda i: (0, 0))] * sources
         + [pl.BlockSpec(memory_space=pl.ANY)] * len(earlier),
         out_specs=pl.BlockSpec((rows * columns, LANES), lambda i: (index, 0)),
         out_shape=jax.ShapeDtypeStruct((pieces * rows * columns, LANES), jnp.float32),
@@ -533,10 +571,15 @@
             pltpu.VMEM((width, LANES), jnp.float32),
             pltpu.VMEM((8 * LANES, LANES), jnp.float32),
         ],
-        input_output_aliases={2: 0} if earlier else {},
+        input_output_aliases={1 + sources: 0} if earlier else {},
         compiler_params=pltpu.CompilerParams(vmem_limit_bytes=22 << 20),
         name="finish",
-    )(feed_slot, coded, *earlier)
+    )(slots, *coded, *earlier)
+
+
+def across(value, k, where):
+    pairs = [(index, index ^ k) for index in range(lax.axis_size("feed")) if index // 4 in where]
+    return lax.ppermute(value, "feed", pairs)
 
 
 def through_rows(samples, gains, feed_slot):
@@ -549,24 +592,39 @@
     words = jnp.transpose(samples, (2, 1, 0)).reshape(lines, count)
     scales = gains.reshape(2 * ch, count)
     weights = jnp.asarray(filter_weights(ch))
-    slots = (feed_slot[:ROWS] - lax.axis_index("feed") * count).reshape(1, ROWS)
+    me = lax.axis_index("feed")
+    place = me.reshape(1)
+    slots = (feed_slot[:ROWS] - me * count).reshape(1, ROWS)
     picked = select_rows(words, scales, slots, total)
     held = []
 
     def work(after):
-        own, zero = own_spectra(words, scales.astype(jnp.float32), weights, ch, spectra, after)
+        own, zero = own_spectra(place, words, scales.astype(jnp.float32), weights, ch, spectra, after)
         held.append(own)
         return zero[0, 0]
 
     sums = [sum_over_feed(value, None if index else work) for index, value in enumerate(picked)]
     own = held[0]
+    middle, devices = (1, 2), lax.axis_size("feed")
+    met = range(12, devices)
+    in_middle = (me // 4 == middle[0]) | (me // 4 == middle[1])
+    spectra_met = [across(own[k], k, middle) for k in met]
+    places = (feed_slot // count ^ me) * count + feed_slot % count
     out = None
     for index in range(pieces):
         rows = sums[index][1]()
         parts = rows[lines : lines + 4 * ch]
-        coded = row_products(rows, parts, own, weights, sums[-1][0])
-        moved = lax.all_to_all(coded, "feed", split_axis=0, concat_axis=0, tiled=True)
-        out = finish(moved, feed_slot, index, pieces, 1.0 / spectra, out)
+        after = [sums[-1][0]] + spectra_met[:2]
+        coded, mine = row_products(place, rows, parts, own, weights, after)
+        near = near_products(spectra_met, mine)
+        moved = [coded[0]]
+        for k in range(1, devices):
+            if k in met:
+                other = across(coded[k], k, (0, 3))
+                moved.append(jnp.where(in_middle, near[k - met[0]], other))
+            else:
+                moved.append(across(coded[k], k, range(devices // 4)))
+        out = finish(moved, places, index, pieces, 1.0 / spectra, out)
     feeds = feed_slot.shape[0]
     out = out.reshape(ROWS, feeds // LANES, 2, LANES)
     return jnp.transpose(out, (0, 2, 1, 3)).reshape(ROWS, 2, feeds)

time: 213 us -> 270 us (1.27); the launches traced: 213 us -> 265 us
  starting transfers between devices: 36.7 us -> 81.5 us
  waiting for transfers between devices: 97.5 us -> 101 us
    ppermute x0 -> x34, waiting for transfers between devices: none -> 70.8 us  [across(): return lax.ppermute(value, 'feed', pairs)]
    all_to_all x2 -> x0, waiting for transfers between devices: 69.5 us -> none  [through_rows(): lax.all_to_all(coded, 'feed', split_axis=0, concat_axis=0, tiled=True)]
    ppermute x0 -> x34, starting transfers between devices: none -> 59.9 us  [across(): return lax.ppermute(value, 'feed', pairs)]
    all_to_all x2 -> x0, starting transfers between devices: 12 us -> none  [through_rows(): lax.all_to_all(coded, 'feed', split_axis=0, concat_axis=0, tiled=True)]
    ppermute x24, starting transfers between devices: 24.8 us -> 21.6 us  [swap(): return lax.ppermute(value, 'feed', pairs)]
    pallas_call x5 -> x7, Pallas kernels: 55.6 us -> 57.4 us  [the longest x2 27.1 us: row_products(): pl.pallas_call(rows_kernel, grid=(2 * steps,), in_specs=[pl.BlockSpec(mem...]
    unnamed x24 -> x112, local copies, waits for them, and re-layouts: 10.1 us -> 9.75 us
  transfers between devices with their start and end apart: 26 -> 58, of which waited for: 15 -> 17; matrix products, arithmetic and copies ran while one was open for 4% -> 4% of each run, Pallas kernels for 16% -> 18%
where the time goes in v8:
time: 270 us; the launch traced here: 265 us
  waiting for transfers between devices  101 us (37%)
  starting transfers between devices  81.5 us (30%)
  Pallas kernels  60 us (22%)
  local copies, waits for them, and re-layouts  14.8 us (5%)
  other arithmetic  7.04 us (3%)
    ppermute x34, waiting for transfers between devices, across(): return lax.ppermute(value, 'feed', pairs)  70.8 us
    ppermute x34, starting transfers between devices, across(): return lax.ppermute(value, 'feed', pairs)  59.9 us
    ppermute x24, waiting for transfers between devices, swap(): return lax.ppermute(value, 'feed', pairs)  30 us
    pallas_call x2, Pallas kernels, row_products(): pl.pallas_call(rows_kernel, grid=(2 * steps,), in_specs=[pl.BlockSpec(mem...  27.1 us
    ppermute x24, starting transfers between devices, swap(): return lax.ppermute(value, 'feed', pairs)  21.6 us
    pallas_call x2, Pallas kernels, finish(): pl.pallas_call(functools.partial(finish_kernel, scale, sources), grid=(1,...  19 us
    unnamed x112, local copies, waits for them, and re-layouts  9.75 us
    pallas_call x1, Pallas kernels, own_spectra(): pl.pallas_call(own_kernel, grid=(steps,), in_specs=[pl.BlockSpec(memory_s...  9.69 us
  transfers between devices with their start and end apart: 58, of which 17 were waited for; matrix products, arithmetic and copies ran while one was open for 4% of the time, Pallas kernels for 18%

profile of v8, /device:TPU:13, one launch (start us, length us, event | category | flops | bytes accessed | tf_op | source)
XLA Modules:
  0.0 265.3 jit_solution(12857078231643895922)
XLA Ops:
  1.6 3.4 %copy-done = s32[256,16,519]{0,1,2:T(8,128)S(1)} copy-done((s32[256,16,519]{0,1,2:T(8,128)S(1)}, s32[256,16,519]{0,1,2:T(8,128)}, u32[]{:S(2)}) %copy-start) | copy-done | bytes 8503320
  5.0 2.6 select_rows.1
  10.2 2.1 collective-permute-done.12
  12.3 1.7 dynamic-slice_add_fusion
  14.3 1.7 dynamic-slice_add_fusion.1
  16.1 1.3 collective-permute-start.6
  17.5 1.5 collective-permute-start.1
  19.0 2.9 %collective-permute-done.13 = bf16[1056,128]{1,0:T(8,128)(2,1)S(1)} collective-permute-done((bf16[1056,128]{1,0:T(8,128)(2,1)S(1)}, bf16[1056,128]{1,0:T(8,128)(2,1)S(1)}, u32[]{:S(2)}, u32[]{:S(2)}) %collective-permute-start.13) | collective-permute-done | bytes 270368 | tf_op jit(solution)/shard_map/ppermute | solution.py:371
  23.3 4.2 %collective-permute-done.6 = bf16[1056,128]{1,0:T(8,128)(2,1)S(1)} collective-permute-done((bf16[1056,128]{1,0:T(8,128)(2,1)S(1)}, bf16[1056,128]{1,0:T(8,128)(2,1)S(1)}, u32[]{:S(2)}, u32[]{:S(2)}) %collective-permute-start.6) | collective-permute-done | bytes 270368 | tf_op jit(solution)/shard_map/ppermute | solution.py:371
  27.6 1.5 collective-permute-start.7
  30.4 2.4 collective-permute-start.34
  33.0 2.4 collective-permute-start.8
  35.5 9.7 %own_spectra.1 = (bf16[16,8,256,128]{3,2,1,0:T(8,128)(2,1)S(1)}, bf16[16,128]{1,0:T(8,128)(2,1)S(1)}) custom-call(s32[1]{0:T(128)} %bitcast.place_ref, s32[8304,256]{1,0:T(8,128)S(1)} %bitcast.121, s32[8304,256]{1,0:T(8,128)S(1)} %bitcast.122, f32[32,256]{1,0:T(8,128)S(1)} %bitcast.123, bf16[256,256]{1,0:T(8,128)(2,1)S(1)} %copy-done.25, ...), custom_call_target="tpu_custom_call" | custom-call | flops 4294967296 | bytes 16891904 | tf_op jit(solution)/shard_map/own_spectra/pallas_call | solution.py:295
  45.8 4.0 %collective-permute-done.39 = bf16[528,128]{1,0:T(8,128)(2,1)S(1)} collective-permute-done((bf16[528,128]{1,0:T(8,128)(2,1)S(1)}, bf16[528,128]{1,0:T(8,128)(2,1)S(1)}, u32[]{:S(2)}, u32[]{:S(2)}) %collective-permute-start.39) | collective-permute-done | bytes 135200 | tf_op jit(solution)/shard_map/ppermute | solution.py:371
  50.6 2.1 collective-permute-done.8
  53.5 2.1 collective-permute-done.3
  56.4 1.5 collective-permute-start.35
  58.1 1.5 collective-permute-start.10
  60.6 1.6 collective-permute-done.35
  62.3 1.5 collective-permute-start.36
  63.7 10.1 %collective-permute-done.10 = bf16[1056,128]{1,0:T(8,128)(2,1)S(1)} collective-permute-done((bf16[1056,128]{1,0:T(8,128)(2,1)S(1)}, bf16[1056,128]{1,0:T(8,128)(2,1)S(1)}, u32[]{:S(2)}, u32[]{:S(2)}) %collective-permute-start.10) | collective-permute-done | bytes 270368 | tf_op jit(solution)/shard_map/ppermute | solution.py:371
  74.1 2.4 collective-permute-start.11
  77.1 5.1 %collective-permute-start.29 = (bf16[8,256,128]{2,1,0:T(8,128)(2,1)S(1)}, bf16[8,256,128]{2,1,0:T(8,128)(2,1)S(1)}, u32[]{:S(2)}, u32[]{:S(2)}) collective-permute-start(bf16[8,256,128]{2,1,0:T(8,128)(2,1)S(1)} %get-tuple-element.29), channel_id=1, source_target_pairs={{4,11},{5,10},{6,9},{7,8},{8,7},{9,6},{10,5},{11,4},{20,27},{21,26... | collective-permute-start | bytes 1572872 | tf_op jit(solution)/shard_map/ppermute | solution.py:582
  82.3 1.9 collective-permute-start.28
  84.2 3.7 %collective-permute-start.16 = (bf16[8,256,128]{2,1,0:T(8,128)(2,1)S(1)}, bf16[8,256,128]{2,1,0:T(8,128)(2,1)S(1)}, u32[]{:S(2)}, u32[]{:S(2)}) collective-permute-start(bf16[8,256,128]{2,1,0:T(8,128)(2,1)S(1)} %get-tuple-element.31), channel_id=1, source_target_pairs={{4,9},{5,8},{6,11},{7,10},{8,5},{9,4},{10,7},{11,6},{20,25},{21,24... | collective-permute-start | bytes 1572872 | tf_op jit(solution)/shard_map/ppermute | solution.py:582
  87.9 1.9 collective-permute-start.15
  90.1 35.4 %collective-permute-done.16.refs_2_.refs_1_ = bf16[8,256,128]{2,1,0:T(8,128)(2,1)S(1)} collective-permute-done((bf16[8,256,128]{2,1,0:T(8,128)(2,1)S(1)}, bf16[8,256,128]{2,1,0:T(8,128)(2,1)S(1)}, u32[]{:S(2)}, u32[]{:S(2)}) %collective-permute-start.16) | collective-permute-done | bytes 524320 | tf_op jit(solution)/shard_map/ppermute | solution.py:582
  125.5 14.1 %collective-permute-done.15.refs_1_.refs_0_ = bf16[8,256,128]{2,1,0:T(8,128)(2,1)S(1)} collective-permute-done((bf16[8,256,128]{2,1,0:T(8,128)(2,1)S(1)}, bf16[8,256,128]{2,1,0:T(8,128)(2,1)S(1)}, u32[]{:S(2)}, u32[]{:S(2)}) %collective-permute-start.15) | collective-permute-done | bytes 524320 | tf_op jit(solution)/shard_map/ppermute | solution.py:582
  139.6 13.5 %row_products.2 = (s16[16,272,256]{2,1,0:T(8,128)(2,1)S(1)}, bf16[1024,256]{1,0:T(8,128)(2,1)S(1)}) custom-call(s32[1]{0:T(128)} %bitcast.place_ref, bf16[8448,128]{1,0:T(8,128)(2,1)S(1)} %constant_dynamic-update-slice_fusion.10.main_ref.next_ref, bf16[8448,128]{1,0:T(8,128)(2,1)S(1)} %constant_dynamic-update-slice_fusion.10.main_ref.next_ref, ...), custom_call_target="tpu_custom_call" | custom-call | flops 4294967296 | bytes 12648448 | tf_op jit(solution)/shard_map/row_products/pallas_call | solution.py:466
  156.5 13.6 %row_products.3 = (s16[16,272,256]{2,1,0:T(8,128)(2,1)S(1)}, bf16[1024,256]{1,0:T(8,128)(2,1)S(1)}) custom-call(s32[1]{0:T(128)} %bitcast.place_ref, bf16[8448,128]{1,0:T(8,128)(2,1)S(1)} %constant_dynamic-update-slice_fusion.main_ref.next_ref, bf16[8448,128]{1,0:T(8,128)(2,1)S(1)} %constant_dynamic-update-slice_fusion.main_ref.next_ref, ...), custom_call_target="tpu_custom_call" | custom-call | flops 4294967296 | bytes 12648448 | tf_op jit(solution)/shard_map/row_products/pallas_call | solution.py:466
  174.9 3.9 %collective-permute-done.27.refs_11_ = s16[272,256]{1,0:T(8,128)(2,1)S(1)} collective-permute-done((s16[272,256]{1,0:T(8,128)(2,1)S(1)}, s16[272,256]{1,0:T(8,128)(2,1)S(1)}, u32[]{:S(2)}, u32[]{:S(2)}) %collective-permute-start.27) | collective-permute-done | bytes 139296 | tf_op jit(solution)/shard_map/ppermute | solution.py:582
  179.5 12.7 %collective-permute-start.53 = (s16[272,256]{1,0:T(8,128)(2,1)S(1)}, s16[272,256]{1,0:T(8,128)(2,1)S(1)}, u32[]{:S(2)}, u32[]{:S(2)}) collective-permute-start(s16[272,256]{1,0:T(8,128)(2,1)S(1)} %get-tuple-element.37), channel_id=1, source_target_pairs={{0,11},{1,10},{2,9},{3,8},{4,15},{5,14},{6,13},{7,12},{8,3},{9,2},... | collective-permute-start | bytes 417800 | tf_op jit(solution)/shard_map/ppermute | solution.py:582
  192.8 2.6 collective-permute-start.51
  195.7 3.6 %collective-permute-start.49 = (s16[272,256]{1,0:T(8,128)(2,1)S(1)}, s16[272,256]{1,0:T(8,128)(2,1)S(1)}, u32[]{:S(2)}, u32[]{:S(2)}) collective-permute-start(s16[272,256]{1,0:T(8,128)(2,1)S(1)} %get-tuple-element.41), channel_id=1, source_target_pairs={{0,7},{1,6},{2,5},{3,4},{4,3},{5,2},{6,1},{7,0},{8,15},{9,14},{10,... | collective-permute-start | bytes 417800 | tf_op jit(solution)/shard_map/ppermute | solution.py:582
  199.3 10.2 %collective-permute-done.53.refs_11_ = s16[272,256]{1,0:T(8,128)(2,1)S(1)} collective-permute-done((s16[272,256]{1,0:T(8,128)(2,1)S(1)}, s16[272,256]{1,0:T(8,128)(2,1)S(1)}, u32[]{:S(2)}, u32[]{:S(2)}) %collective-permute-start.53) | collective-permute-done | bytes 139296 | tf_op jit(solution)/shard_map/ppermute | solution.py:582
  210.2 2.8 %collective-permute-start.48 = (s16[272,256]{1,0:T(8,128)(2,1)S(1)}, s16[272,256]{1,0:T(8,128)(2,1)S(1)}, u32[]{:S(2)}, u32[]{:S(2)}) collective-permute-start(s16[272,256]{1,0:T(8,128)(2,1)S(1)} %get-tuple-element.42), channel_id=1, source_target_pairs={{0,6},{1,7},{2,4},{3,5},{4,2},{5,3},{6,0},{7,1},{8,14},{9,15},{10,... | collective-permute-start | bytes 417800 | tf_op jit(solution)/shard_map/ppermute | solution.py:582
  213.6 2.6 collective-permute-start.47
  219.1 1.4 collective-permute-start.45
  225.5 4.1 %collective-permute-start.26 = (s16[272,256]{1,0:T(8,128)(2,1)S(1)}, s16[272,256]{1,0:T(8,128)(2,1)S(1)}, u32[]{:S(2)}, u32[]{:S(2)}) collective-permute-start(s16[272,256]{1,0:T(8,128)(2,1)S(1)} %copy-done.43), channel_id=1, source_target_pairs={{0,10},{1,11},{2,8},{3,9},{4,14},{5,15},{6,12},{7,13},{8,2},{9,3},... | collective-permute-start | bytes 417800 | tf_op jit(solution)/shard_map/ppermute | solution.py:582
  229.6 1.3 collective-permute-start.25
  231.0 1.3 collective-permute-start.24
  233.1 1.9 collective-permute-start.22
  235.3 9.8 %finish.2.refs_16_ = f32[16384,128]{1,0:T(8,128)} custom-call(s32[4096]{0:T(1024)S(1)} %fusion.10.slot_ref, s16[272,256]{1,0:T(8,128)(2,1)S(1)} %get-tuple-element.48.refs_0_, s16[272,256]{1,0:T(8,128)(2,1)} %collective-permute-done.43.refs_1_, s16[272,256]{1,0:T(8,128)(2,1)} %collective-permute-done.44.refs_2_, ...), custom_call_target="tpu_custom_call" | custom-call | tf_op jit(solution)/shard_map/finish/pallas_call | solution.py:561
  245.3 1.6 collective-permute-start.20
  249.3 2.1 collective-permute-done.21.refs_5_
  251.4 2.7 %collective-permute-done.20.refs_4_ = s16[272,256]{1,0:T(8,128)(2,1)S(1)} collective-permute-done((s16[272,256]{1,0:T(8,128)(2,1)S(1)}, s16[272,256]{1,0:T(8,128)(2,1)S(1)}, u32[]{:S(2)}, u32[]{:S(2)}) %collective-permute-start.20) | collective-permute-done | bytes 139296 | tf_op jit(solution)/shard_map/ppermute | solution.py:582
  254.1 2.0 collective-permute-done.18.refs_2_
  256.1 9.2 %finish.3 = f32[16384,128]{1,0:T(8,128)} custom-call(s32[4096]{0:T(1024)S(1)} %fusion.10.slot_ref, s16[272,256]{1,0:T(8,128)(2,1)S(1)} %get-tuple-element.64.refs_0_, s16[272,256]{1,0:T(8,128)(2,1)S(1)} %collective-permute-done.17.refs_1_, s16[272,256]{1,0:T(8,128)(2,1)S(1)} %collective-permute-done.18.refs_2_, ...), custom_call_target="tpu_custom_call", output_to_operand_aliasing={{}: (17, {})} | custom-call | tf_op jit(solution)/shard_map/finish/pallas_call | solution.py:561
  (243 shorter events, 35.2 us)
Async XLA Ops:
  14.1 7.8 %collective-permute-start.13 = (bf16[1056,128]{1,0:T(8,128)(2,1)S(1)}, bf16[1056,128]{1,0:T(8,128)(2,1)S(1)}, u32[]{:S(2)}, u32[]{:S(2)}) collective-permute-start(bf16[1056,128]{1,0:T(8,128)(2,1)S(1)} %constant_dynamic-slice_fusion.3), channel_id=1, source_target_pairs={{0,2},{1,3},{2,0},{3,1},{4,6},{5,7},{6,4},{7,5},{8,10},{9,11},{10,... | collective-permute-start | bytes 811016 | tf_op jit(solution)/shard_map/ppermute | solution.py:371
  14.2 7.8 %collective-permute-start.37 = (bf16[1056,128]{1,0:T(8,128)(2,1)S(1)}, bf16[1056,128]{1,0:T(8,128)(2,1)S(1)}, u32[]{:S(2)}, u32[]{:S(2)}) collective-permute-start(bf16[1056,128]{1,0:T(8,128)(2,1)S(1)} %constant_dynamic-slice_fusion.1), channel_id=1, source_target_pairs={{0,4},{1,5},{2,6},{3,7},{4,0},{5,1},{6,2},{7,3},{8,12},{9,13},{10,... | collective-permute-start | bytes 811016 | tf_op jit(solution)/shard_map/ppermute | solution.py:371
  16.1 11.3 %collective-permute-start.6 = (bf16[1056,128]{1,0:T(8,128)(2,1)S(1)}, bf16[1056,128]{1,0:T(8,128)(2,1)S(1)}, u32[]{:S(2)}, u32[]{:S(2)}) collective-permute-start(bf16[1056,128]{1,0:T(8,128)(2,1)S(1)} %constant_dynamic-slice_fusion.6), channel_id=1, source_target_pairs={{0,4},{1,5},{2,6},{3,7},{4,0},{5,1},{6,2},{7,3},{8,12},{9,13},{10,... | collective-permute-start | bytes 811016 | tf_op jit(solution)/shard_map/ppermute | solution.py:371
  17.5 11.6 %collective-permute-start.1 = (bf16[1056,128]{1,0:T(8,128)(2,1)S(1)}, bf16[1056,128]{1,0:T(8,128)(2,1)S(1)}, u32[]{:S(2)}, u32[]{:S(2)}) collective-permute-start(bf16[1056,128]{1,0:T(8,128)(2,1)S(1)} %constant_dynamic-slice_fusion.8), channel_id=1, source_target_pairs={{0,2},{1,3},{2,0},{3,1},{4,6},{5,7},{6,4},{7,5},{8,10},{9,11},{10,... | collective-permute-start | bytes 811016 | tf_op jit(solution)/shard_map/ppermute | solution.py:371
  22.0 8.4 %collective-permute-start.14 = (bf16[528,128]{1,0:T(8,128)(2,1)S(1)}, bf16[528,128]{1,0:T(8,128)(2,1)S(1)}, u32[]{:S(2)}, u32[]{:S(2)}) collective-permute-start(bf16[528,128]{1,0:T(8,128)(2,1)S(1)} %constant_dynamic-slice_fusion.2), channel_id=1, source_target_pairs={{0,4},{1,5},{2,6},{3,7},{4,0},{5,1},{6,2},{7,3},{8,12},{9,13},{10,... | collective-permute-start | bytes 405512 | tf_op jit(solution)/shard_map/ppermute | solution.py:371
  22.2 10.6 %collective-permute-start.38 = (bf16[528,128]{1,0:T(8,128)(2,1)S(1)}, bf16[528,128]{1,0:T(8,128)(2,1)S(1)}, u32[]{:S(2)}, u32[]{:S(2)}) collective-permute-start(bf16[528,128]{1,0:T(8,128)(2,1)S(1)} %constant_dynamic-slice_fusion), channel_id=1, source_target_pairs={{0,2},{1,3},{2,0},{3,1},{4,6},{5,7},{6,4},{7,5},{8,10},{9,11},{10,... | collective-permute-start | bytes 405512 | tf_op jit(solution)/shard_map/ppermute | solution.py:371
  30.4 25.3 %collective-permute-start.34 = (bf16[528,128]{1,0:T(8,128)(2,1)S(1)}, bf16[528,128]{1,0:T(8,128)(2,1)S(1)}, u32[]{:S(2)}, u32[]{:S(2)}) collective-permute-start(bf16[528,128]{1,0:T(8,128)(2,1)S(1)} %dynamic-slice_add_fusion.7.after_ref), channel_id=1, source_target_pairs={{0,8},{1,9},{2,10},{3,11},{4,12},{5,13},{6,14},{7,15},{8,0},{9,1},... | collective-permute-start | bytes 405512 | tf_op jit(solution)/shard_map/ppermute | solution.py:371
  32.8 16.9 %collective-permute-start.39 = (bf16[528,128]{1,0:T(8,128)(2,1)S(1)}, bf16[528,128]{1,0:T(8,128)(2,1)S(1)}, u32[]{:S(2)}, u32[]{:S(2)}) collective-permute-start(bf16[528,128]{1,0:T(8,128)(2,1)S(1)} %dynamic-slice_add_fusion.6), channel_id=1, source_target_pairs={{0,8},{1,9},{2,10},{3,11},{4,12},{5,13},{6,14},{7,15},{8,0},{9,1},... | collective-permute-start | bytes 405512 | tf_op jit(solution)/shard_map/ppermute | solution.py:371
  33.0 19.6 %collective-permute-start.8 = (bf16[528,128]{1,0:T(8,128)(2,1)S(1)}, bf16[528,128]{1,0:T(8,128)(2,1)S(1)}, u32[]{:S(2)}, u32[]{:S(2)}) collective-permute-start(bf16[528,128]{1,0:T(8,128)(2,1)S(1)} %dynamic-slice_add_fusion.8), channel_id=1, source_target_pairs={{0,8},{1,9},{2,10},{3,11},{4,12},{5,13},{6,14},{7,15},{8,0},{9,1},... | collective-permute-start | bytes 405512 | tf_op jit(solution)/shard_map/ppermute | solution.py:371
  35.4 20.1 %collective-permute-start.3 = (bf16[528,128]{1,0:T(8,128)(2,1)S(1)}, bf16[528,128]{1,0:T(8,128)(2,1)S(1)}, u32[]{:S(2)}, u32[]{:S(2)}) collective-permute-start(bf16[528,128]{1,0:T(8,128)(2,1)S(1)} %dynamic-slice_add_fusion.9), channel_id=1, source_target_pairs={{0,8},{1,9},{2,10},{3,11},{4,12},{5,13},{6,14},{7,15},{8,0},{9,1},... | collective-permute-start | bytes 405512 | tf_op jit(solution)/shard_map/ppermute | solution.py:371
  49.8 8.1 %collective-permute-start.40 = (bf16[528,128]{1,0:T(8,128)(2,1)S(1)}, bf16[528,128]{1,0:T(8,128)(2,1)S(1)}, u32[]{:S(2)}, u32[]{:S(2)}) collective-permute-start(bf16[528,128]{1,0:T(8,128)(2,1)S(1)} %get-tuple-element.24), channel_id=1, source_target_pairs={{0,2},{1,3},{2,0},{3,1},{4,6},{5,7},{6,4},{7,5},{8,10},{9,11},{10,... | collective-permute-start | bytes 405512 | tf_op jit(solution)/shard_map/ppermute | solution.py:371
  57.9 18.6 %collective-permute-start.41 = (bf16[1056,128]{1,0:T(8,128)(2,1)S(1)}, bf16[1056,128]{1,0:T(8,128)(2,1)S(1)}, u32[]{:S(2)}, u32[]{:S(2)}) collective-permute-start(bf16[1056,128]{1,0:T(8,128)(2,1)S(1)} %constant_dynamic-update-slice_fusion.4), channel_id=1, source_target_pairs={{0,4},{1,5},{2,6},{3,7},{4,0},{5,1},{6,2},{7,3},{8,12},{9,13},{10,... | collective-permute-start | bytes 811016 | tf_op jit(solution)/shard_map/ppermute | solution.py:371
  58.1 15.7 %collective-permute-start.10 = (bf16[1056,128]{1,0:T(8,128)(2,1)S(1)}, bf16[1056,128]{1,0:T(8,128)(2,1)S(1)}, u32[]{:S(2)}, u32[]{:S(2)}) collective-permute-start(bf16[1056,128]{1,0:T(8,128)(2,1)S(1)} %constant_dynamic-update-slice_fusion.14), channel_id=1, source_target_pairs={{0,4},{1,5},{2,6},{3,7},{4,0},{5,1},{6,2},{7,3},{8,12},{9,13},{10,... | collective-permute-start | bytes 811016 | tf_op jit(solution)/shard_map/ppermute | solution.py:371
  59.7 14.1 %collective-permute-start.5 = (bf16[1056,128]{1,0:T(8,128)(2,1)S(1)}, bf16[1056,128]{1,0:T(8,128)(2,1)S(1)}, u32[]{:S(2)}, u32[]{:S(2)}) collective-permute-start(bf16[1056,128]{1,0:T(8,128)(2,1)S(1)} %constant_dynamic-update-slice_fusion.18), channel_id=1, source_target_pairs={{0,2},{1,3},{2,0},{3,1},{4,6},{5,7},{6,4},{7,5},{8,10},{9,11},{10,... | collective-permute-start | bytes 811016 | tf_op jit(solution)/shard_map/ppermute | solution.py:371
  62.3 14.3 %collective-permute-start.36 = (bf16[1056,128]{1,0:T(8,128)(2,1)S(1)}, bf16[1056,128]{1,0:T(8,128)(2,1)S(1)}, u32[]{:S(2)}, u32[]{:S(2)}) collective-permute-start(bf16[1056,128]{1,0:T(8,128)(2,1)S(1)} %constant_dynamic-update-slice_fusion.8), channel_id=1, source_target_pairs={{0,2},{1,3},{2,0},{3,1},{4,6},{5,7},{6,4},{7,5},{8,10},{9,11},{10,... | collective-permute-start | bytes 811016 | tf_op jit(solution)/shard_map/ppermute | solution.py:371
  74.1 13.7 %collective-permute-start.11 = (bf16[4224,128]{1,0:T(8,128)(2,1)S(1)}, bf16[4224,128]{1,0:T(8,128)(2,1)S(1)}, u32[]{:S(2)}, u32[]{:S(2)}) collective-permute-start(bf16[4224,128]{1,0:T(8,128)(2,1)S(1)} %get-tuple-element.69.refs_0_), channel_id=1, source_target_pairs={{0,1},{1,0},{2,3},{3,2},{4,5},{5,4},{6,7},{7,6},{8,9},{9,8},{10,11... | collective-permute-start | bytes 3244040 | tf_op jit(solution)/shard_map/ppermute | solution.py:371
  76.9 13.1 %collective-permute-start.42 = (bf16[4224,128]{1,0:T(8,128)(2,1)S(1)}, bf16[4224,128]{1,0:T(8,128)(2,1)S(1)}, u32[]{:S(2)}, u32[]{:S(2)}) collective-permute-start(bf16[4224,128]{1,0:T(8,128)(2,1)S(1)} %get-tuple-element.65), channel_id=1, source_target_pairs={{0,1},{1,0},{2,3},{3,2},{4,5},{5,4},{6,7},{7,6},{8,9},{9,8},{10,11... | collective-permute-start | bytes 3244040 | tf_op jit(solution)/shard_map/ppermute | solution.py:371
  77.1 93.0 %collective-permute-start.29 = (bf16[8,256,128]{2,1,0:T(8,128)(2,1)S(1)}, bf16[8,256,128]{2,1,0:T(8,128)(2,1)S(1)}, u32[]{:S(2)}, u32[]{:S(2)}) collective-permute-start(bf16[8,256,128]{2,1,0:T(8,128)(2,1)S(1)} %get-tuple-element.29), channel_id=1, source_target_pairs={{4,11},{5,10},{6,9},{7,8},{8,7},{9,6},{10,5},{11,4},{20,27},{21,26... | collective-permute-start | bytes 1572872 | tf_op jit(solution)/shard_map/ppermute | solution.py:582
  82.3 88.5 %collective-permute-start.28 = (bf16[8,256,128]{2,1,0:T(8,128)(2,1)S(1)}, bf16[8,256,128]{2,1,0:T(8,128)(2,1)S(1)}, u32[]{:S(2)}, u32[]{:S(2)}) collective-permute-start(bf16[8,256,128]{2,1,0:T(8,128)(2,1)S(1)} %get-tuple-element.30), channel_id=1, source_target_pairs={{4,10},{5,11},{6,8},{7,9},{8,6},{9,7},{10,4},{11,5},{20,26},{21,27... | collective-permute-start | bytes 1572872 | tf_op jit(solution)/shard_map/ppermute | solution.py:582
  84.2 41.3 %collective-permute-start.16 = (bf16[8,256,128]{2,1,0:T(8,128)(2,1)S(1)}, bf16[8,256,128]{2,1,0:T(8,128)(2,1)S(1)}, u32[]{:S(2)}, u32[]{:S(2)}) collective-permute-start(bf16[8,256,128]{2,1,0:T(8,128)(2,1)S(1)} %get-tuple-element.31), channel_id=1, source_target_pairs={{4,9},{5,8},{6,11},{7,10},{8,5},{9,4},{10,7},{11,6},{20,25},{21,24... | collective-permute-start | bytes 1572872 | tf_op jit(solution)/shard_map/ppermute | solution.py:582
  87.9 51.7 %collective-permute-start.15 = (bf16[8,256,128]{2,1,0:T(8,128)(2,1)S(1)}, bf16[8,256,128]{2,1,0:T(8,128)(2,1)S(1)}, u32[]{:S(2)}, u32[]{:S(2)}) collective-permute-start(bf16[8,256,128]{2,1,0:T(8,128)(2,1)S(1)} %get-tuple-element.32), channel_id=1, source_target_pairs={{4,8},{5,9},{6,10},{7,11},{8,4},{9,5},{10,6},{11,7},{20,24},{21,25... | collective-permute-start | bytes 1572872 | tf_op jit(solution)/shard_map/ppermute | solution.py:582
  154.4 17.4 %collective-permute-start.33 = (s16[272,256]{1,0:T(8,128)(2,1)S(1)}, s16[272,256]{1,0:T(8,128)(2,1)S(1)}, u32[]{:S(2)}, u32[]{:S(2)}) collective-permute-start(s16[272,256]{1,0:T(8,128)(2,1)S(1)} %get-tuple-element.49), channel_id=1, source_target_pairs={{0,15},{1,14},{2,13},{3,12},{12,3},{13,2},{14,1},{15,0},{16,31},{1... | collective-permute-start | bytes 417800 | tf_op jit(solution)/shard_map/ppermute | solution.py:582
  155.1 17.6 %collective-permute-start.32 = (s16[272,256]{1,0:T(8,128)(2,1)S(1)}, s16[272,256]{1,0:T(8,128)(2,1)S(1)}, u32[]{:S(2)}, u32[]{:S(2)}) collective-permute-start(s16[272,256]{1,0:T(8,128)(2,1)S(1)} %get-tuple-element.50), channel_id=1, source_target_pairs={{0,14},{1,15},{2,12},{3,13},{12,2},{13,3},{14,0},{15,1},{16,30},{1... | collective-permute-start | bytes 417800 | tf_op jit(solution)/shard_map/ppermute | solution.py:582
  155.8 17.6 %collective-permute-start.31 = (s16[272,256]{1,0:T(8,128)(2,1)S(1)}, s16[272,256]{1,0:T(8,128)(2,1)S(1)}, u32[]{:S(2)}, u32[]{:S(2)}) collective-permute-start(s16[272,256]{1,0:T(8,128)(2,1)S(1)} %get-tuple-element.51), channel_id=1, source_target_pairs={{0,13},{1,12},{2,15},{3,14},{12,1},{13,0},{14,3},{15,2},{16,29},{1... | collective-permute-start | bytes 417800 | tf_op jit(solution)/shard_map/ppermute | solution.py:582
  170.8 8.0 %collective-permute-start.27 = (s16[272,256]{1,0:T(8,128)(2,1)S(1)}, s16[272,256]{1,0:T(8,128)(2,1)S(1)}, u32[]{:S(2)}, u32[]{:S(2)}) collective-permute-start(s16[272,256]{1,0:T(8,128)(2,1)S(1)} %get-tuple-element.53), channel_id=1, source_target_pairs={{0,11},{1,10},{2,9},{3,8},{4,15},{5,14},{6,13},{7,12},{8,3},{9,2},... | collective-permute-start | bytes 417800 | tf_op jit(solution)/shard_map/ppermute | solution.py:582
  171.9 20.3 %collective-permute-start.57 = (s16[272,256]{1,0:T(8,128)(2,1)S(1)}, s16[272,256]{1,0:T(8,128)(2,1)S(1)}, u32[]{:S(2)}, u32[]{:S(2)}) collective-permute-start(s16[272,256]{1,0:T(8,128)(2,1)S(1)} %get-tuple-element.33), channel_id=1, source_target_pairs={{0,15},{1,14},{2,13},{3,12},{12,3},{13,2},{14,1},{15,0},{16,31},{1... | collective-permute-start | bytes 417800 | tf_op jit(solution)/shard_map/ppermute | solution.py:582
  172.7 19.7 %collective-permute-start.56 = (s16[272,256]{1,0:T(8,128)(2,1)S(1)}, s16[272,256]{1,0:T(8,128)(2,1)S(1)}, u32[]{:S(2)}, u32[]{:S(2)}) collective-permute-start(s16[272,256]{1,0:T(8,128)(2,1)S(1)} %get-tuple-element.34), channel_id=1, source_target_pairs={{0,14},{1,15},{2,12},{3,13},{12,2},{13,3},{14,0},{15,1},{16,30},{1... | collective-permute-start | bytes 417800 | tf_op jit(solution)/shard_map/ppermute | solution.py:582
  173.4 22.1 %collective-permute-start.55 = (s16[272,256]{1,0:T(8,128)(2,1)S(1)}, s16[272,256]{1,0:T(8,128)(2,1)S(1)}, u32[]{:S(2)}, u32[]{:S(2)}) collective-permute-start(s16[272,256]{1,0:T(8,128)(2,1)S(1)} %get-tuple-element.35), channel_id=1, source_target_pairs={{0,13},{1,12},{2,15},{3,14},{12,1},{13,0},{14,3},{15,2},{16,29},{1... | collective-permute-start | bytes 417800 | tf_op jit(solution)/shard_map/ppermute | solution.py:582
  174.1 21.6 %collective-permute-start.54 = (s16[272,256]{1,0:T(8,128)(2,1)S(1)}, s16[272,256]{1,0:T(8,128)(2,1)S(1)}, u32[]{:S(2)}, u32[]{:S(2)}) collective-permute-start(s16[272,256]{1,0:T(8,128)(2,1)S(1)} %get-tuple-element.36), channel_id=1, source_target_pairs={{0,12},{1,13},{2,14},{3,15},{12,0},{13,1},{14,2},{15,3},{16,28},{1... | collective-permute-start | bytes 417800 | tf_op jit(solution)/shard_map/ppermute | solution.py:582
  179.5 30.0 %collective-permute-start.53 = (s16[272,256]{1,0:T(8,128)(2,1)S(1)}, s16[272,256]{1,0:T(8,128)(2,1)S(1)}, u32[]{:S(2)}, u32[]{:S(2)}) collective-permute-start(s16[272,256]{1,0:T(8,128)(2,1)S(1)} %get-tuple-element.37), channel_id=1, source_target_pairs={{0,11},{1,10},{2,9},{3,8},{4,15},{5,14},{6,13},{7,12},{8,3},{9,2},... | collective-permute-start | bytes 417800 | tf_op jit(solution)/shard_map/ppermute | solution.py:582
  192.2 20.7 %collective-permute-start.52 = (s16[272,256]{1,0:T(8,128)(2,1)S(1)}, s16[272,256]{1,0:T(8,128)(2,1)S(1)}, u32[]{:S(2)}, u32[]{:S(2)}) collective-permute-start(s16[272,256]{1,0:T(8,128)(2,1)S(1)} %get-tuple-element.38), channel_id=1, source_target_pairs={{0,10},{1,11},{2,8},{3,9},{4,14},{5,15},{6,12},{7,13},{8,2},{9,3},... | collective-permute-start | bytes 417800 | tf_op jit(solution)/shard_map/ppermute | solution.py:582
  192.8 23.4 %collective-permute-start.51 = (s16[272,256]{1,0:T(8,128)(2,1)S(1)}, s16[272,256]{1,0:T(8,128)(2,1)S(1)}, u32[]{:S(2)}, u32[]{:S(2)}) collective-permute-start(s16[272,256]{1,0:T(8,128)(2,1)S(1)} %get-tuple-element.39), channel_id=1, source_target_pairs={{0,9},{1,8},{2,11},{3,10},{4,13},{5,12},{6,15},{7,14},{8,1},{9,0},... | collective-permute-start | bytes 417800 | tf_op jit(solution)/shard_map/ppermute | solution.py:582
  195.5 23.0 %collective-permute-start.50 = (s16[272,256]{1,0:T(8,128)(2,1)S(1)}, s16[272,256]{1,0:T(8,128)(2,1)S(1)}, u32[]{:S(2)}, u32[]{:S(2)}) collective-permute-start(s16[272,256]{1,0:T(8,128)(2,1)S(1)} %get-tuple-element.40), channel_id=1, source_target_pairs={{0,8},{1,9},{2,10},{3,11},{4,12},{5,13},{6,14},{7,15},{8,0},{9,1},... | collective-permute-start | bytes 417800 | tf_op jit(solution)/shard_map/ppermute | solution.py:582
  195.7 24.9 %collective-permute-start.49 = (s16[272,256]{1,0:T(8,128)(2,1)S(1)}, s16[272,256]{1,0:T(8,128)(2,1)S(1)}, u32[]{:S(2)}, u32[]{:S(2)}) collective-permute-start(s16[272,256]{1,0:T(8,128)(2,1)S(1)} %get-tuple-element.41), channel_id=1, source_target_pairs={{0,7},{1,6},{2,5},{3,4},{4,3},{5,2},{6,1},{7,0},{8,15},{9,14},{10,... | collective-permute-start | bytes 417800 | tf_op jit(solution)/shard_map/ppermute | solution.py:582
  210.2 11.5 %collective-permute-start.48 = (s16[272,256]{1,0:T(8,128)(2,1)S(1)}, s16[272,256]{1,0:T(8,128)(2,1)S(1)}, u32[]{:S(2)}, u32[]{:S(2)}) collective-permute-start(s16[272,256]{1,0:T(8,128)(2,1)S(1)} %get-tuple-element.42), channel_id=1, source_target_pairs={{0,6},{1,7},{2,4},{3,5},{4,2},{5,3},{6,0},{7,1},{8,14},{9,15},{10,... | collective-permute-start | bytes 417800 | tf_op jit(solution)/shard_map/ppermute | solution.py:582
  213.6 11.9 %collective-permute-start.47 = (s16[272,256]{1,0:T(8,128)(2,1)}, s16[272,256]{1,0:T(8,128)(2,1)}, u32[]{:S(2)}, u32[]{:S(2)}) collective-permute-start(s16[272,256]{1,0:T(8,128)(2,1)} %get-tuple-element.43), channel_id=1, source_target_pairs={{0,5},{1,4},{2,7},{3,6},{4,1},{5,0},{6,3},{7,2},{8,13},{9,12},{10,... | collective-permute-start | bytes 417800 | tf_op jit(solution)/shard_map/ppermute | solution.py:582
  216.9 12.8 %collective-permute-start.46 = (s16[272,256]{1,0:T(8,128)(2,1)}, s16[272,256]{1,0:T(8,128)(2,1)}, u32[]{:S(2)}, u32[]{:S(2)}) collective-permute-start(s16[272,256]{1,0:T(8,128)(2,1)} %get-tuple-element.44), channel_id=1, source_target_pairs={{0,4},{1,5},{2,6},{3,7},{4,0},{5,1},{6,2},{7,3},{8,12},{9,13},{10,... | collective-permute-start | bytes 417800 | tf_op jit(solution)/shard_map/ppermute | solution.py:582
  219.1 11.8 %collective-permute-start.45 = (s16[272,256]{1,0:T(8,128)(2,1)}, s16[272,256]{1,0:T(8,128)(2,1)}, u32[]{:S(2)}, u32[]{:S(2)}) collective-permute-start(s16[272,256]{1,0:T(8,128)(2,1)} %get-tuple-element.45), channel_id=1, source_target_pairs={{0,3},{1,2},{2,1},{3,0},{4,7},{5,6},{6,5},{7,4},{8,11},{9,10},{10,... | collective-permute-start | bytes 417800 | tf_op jit(solution)/shard_map/ppermute | solution.py:582
  221.2 11.1 %collective-permute-start.44 = (s16[272,256]{1,0:T(8,128)(2,1)}, s16[272,256]{1,0:T(8,128)(2,1)}, u32[]{:S(2)}, u32[]{:S(2)}) collective-permute-start(s16[272,256]{1,0:T(8,128)(2,1)} %get-tuple-element.46), channel_id=1, source_target_pairs={{0,2},{1,3},{2,0},{3,1},{4,6},{5,7},{6,4},{7,5},{8,10},{9,11},{10,... | collective-permute-start | bytes 417800 | tf_op jit(solution)/shard_map/ppermute | solution.py:582
  222.3 10.8 %collective-permute-start.43 = (s16[272,256]{1,0:T(8,128)(2,1)}, s16[272,256]{1,0:T(8,128)(2,1)}, u32[]{:S(2)}, u32[]{:S(2)}) collective-permute-start(s16[272,256]{1,0:T(8,128)(2,1)} %get-tuple-element.47), channel_id=1, source_target_pairs={{0,1},{1,0},{2,3},{3,2},{4,5},{5,4},{6,7},{7,6},{8,9},{9,8},{10,11... | collective-permute-start | bytes 417800 | tf_op jit(solution)/shard_map/ppermute | solution.py:582
  225.5 19.5 %collective-permute-start.26 = (s16[272,256]{1,0:T(8,128)(2,1)S(1)}, s16[272,256]{1,0:T(8,128)(2,1)S(1)}, u32[]{:S(2)}, u32[]{:S(2)}) collective-permute-start(s16[272,256]{1,0:T(8,128)(2,1)S(1)} %copy-done.43), channel_id=1, source_target_pairs={{0,10},{1,11},{2,8},{3,9},{4,14},{5,15},{6,12},{7,13},{8,2},{9,3},... | collective-permute-start | bytes 417800 | tf_op jit(solution)/shard_map/ppermute | solution.py:582
  229.6 15.7 %collective-permute-start.25 = (s16[272,256]{1,0:T(8,128)(2,1)S(1)}, s16[272,256]{1,0:T(8,128)(2,1)S(1)}, u32[]{:S(2)}, u32[]{:S(2)}) collective-permute-start(s16[272,256]{1,0:T(8,128)(2,1)S(1)} %copy-done.40), channel_id=1, source_target_pairs={{0,9},{1,8},{2,11},{3,10},{4,13},{5,12},{6,15},{7,14},{8,1},{9,0},... | collective-permute-start | bytes 417800 | tf_op jit(solution)/shard_map/ppermute | solution.py:582
  231.0 16.0 %collective-permute-start.24 = (s16[272,256]{1,0:T(8,128)(2,1)S(1)}, s16[272,256]{1,0:T(8,128)(2,1)S(1)}, u32[]{:S(2)}, u32[]{:S(2)}) collective-permute-start(s16[272,256]{1,0:T(8,128)(2,1)S(1)} %copy-done.39), channel_id=1, source_target_pairs={{0,8},{1,9},{2,10},{3,11},{4,12},{5,13},{6,14},{7,15},{8,0},{9,1},... | collective-permute-start | bytes 417800 | tf_op jit(solution)/shard_map/ppermute | solution.py:582
  232.3 15.9 %collective-permute-start.23 = (s16[272,256]{1,0:T(8,128)(2,1)S(1)}, s16[272,256]{1,0:T(8,128)(2,1)S(1)}, u32[]{:S(2)}, u32[]{:S(2)}) collective-permute-start(s16[272,256]{1,0:T(8,128)(2,1)S(1)} %copy-done.38), channel_id=1, source_target_pairs={{0,7},{1,6},{2,5},{3,4},{4,3},{5,2},{6,1},{7,0},{8,15},{9,14},{10,... | collective-permute-start | bytes 417800 | tf_op jit(solution)/shard_map/ppermute | solution.py:582
  233.1 15.9 %collective-permute-start.22 = (s16[272,256]{1,0:T(8,128)(2,1)S(1)}, s16[272,256]{1,0:T(8,128)(2,1)S(1)}, u32[]{:S(2)}, u32[]{:S(2)}) collective-permute-start(s16[272,256]{1,0:T(8,128)(2,1)S(1)} %copy-done.31), channel_id=1, source_target_pairs={{0,6},{1,7},{2,4},{3,5},{4,2},{5,3},{6,0},{7,1},{8,14},{9,15},{10,... | collective-permute-start | bytes 417800 | tf_op jit(solution)/shard_map/ppermute | solution.py:582
  245.3 8.7 %collective-permute-start.20 = (s16[272,256]{1,0:T(8,128)(2,1)S(1)}, s16[272,256]{1,0:T(8,128)(2,1)S(1)}, u32[]{:S(2)}, u32[]{:S(2)}) collective-permute-start(s16[272,256]{1,0:T(8,128)(2,1)S(1)} %copy-done.29), channel_id=1, source_target_pairs={{0,4},{1,5},{2,6},{3,7},{4,0},{5,1},{6,2},{7,3},{8,12},{9,13},{10,... | collective-permute-start | bytes 417800 | tf_op jit(solution)/shard_map/ppermute | solution.py:582
  248.2 7.9 %collective-permute-start.18 = (s16[272,256]{1,0:T(8,128)(2,1)S(1)}, s16[272,256]{1,0:T(8,128)(2,1)S(1)}, u32[]{:S(2)}, u32[]{:S(2)}) collective-permute-start(s16[272,256]{1,0:T(8,128)(2,1)S(1)} %copy-done.27), channel_id=1, source_target_pairs={{0,2},{1,3},{2,0},{3,1},{4,6},{5,7},{6,4},{7,5},{8,10},{9,11},{10,... | collective-permute-start | bytes 417800 | tf_op jit(solution)/shard_map/ppermute | solution.py:582
  249.0 7.1 %collective-permute-start.17 = (s16[272,256]{1,0:T(8,128)(2,1)S(1)}, s16[272,256]{1,0:T(8,128)(2,1)S(1)}, u32[]{:S(2)}, u32[]{:S(2)}) collective-permute-start(s16[272,256]{1,0:T(8,128)(2,1)S(1)} %copy-done.26), channel_id=1, source_target_pairs={{0,1},{1,0},{2,3},{3,2},{4,5},{5,4},{6,7},{7,6},{8,9},{9,8},{10,11... | collective-permute-start | bytes 417800 | tf_op jit(solution)/shard_map/ppermute | solution.py:582
  (66 other events, 897.8 us)

commit v9 on v8

--- a/solution.py
+++ b/solution.py
@@ -606,7 +606,7 @@
     sums = [sum_over_feed(value, None if index else work) for index, value in enumerate(picked)]
     own = held[0]
     middle, devices = (1, 2), lax.axis_size("feed")
-    met = range(12, devices)
+    met = range(devices, devices)
     in_middle = (me // 4 == middle[0]) | (me // 4 == middle[1])
     spectra_met = [across(own[k], k, middle) for k in met]
     places = (feed_slot // count ^ me) * count + feed_slot % count
@@ -616,7 +616,7 @@
         parts = rows[lines : lines + 4 * ch]
         after = [sums[-1][0]] + spectra_met[:2]
         coded, mine = row_products(place, rows, parts, own, weights, after)
-        near = near_products(spectra_met, mine)
+        near = near_products(spectra_met, mine) if spectra_met else None
         moved = [coded[0]]
         for k in range(1, devices):
             if k in met:

time: 270 us -> 228 us (0.84); the launches traced: 265 us -> 227 us
  waiting for transfers between devices: 101 us -> 76.7 us
  local copies, waits for them, and re-layouts: 14.8 us -> 6.44 us
  starting transfers between devices: 81.5 us -> 76.7 us
    ppermute x34 -> x30, waiting for transfers between devices: 70.8 us -> 44.8 us  [across(): return lax.ppermute(value, 'feed', pairs)]
    unnamed x112 -> x16, local copies, waits for them, and re-layouts: 9.75 us -> 3.45 us
    ppermute x34 -> x30, starting transfers between devices: 59.9 us -> 55 us  [across(): return lax.ppermute(value, 'feed', pairs)]
  transfers between devices with their start and end apart: 58 -> 54, of which waited for: 17 -> 26; matrix products, arithmetic and copies ran while one was open for 4% -> 3% of each run, Pallas kernels for 18% -> 21%
where the time goes in v9:
time: 228 us; the launch traced here: 227 us
  starting transfers between devices  76.7 us (34%)
  waiting for transfers between devices  76.7 us (34%)
  Pallas kernels  59.7 us (26%)
  other arithmetic  6.76 us (3%)
  local copies, waits for them, and re-layouts  6.44 us (3%)
    ppermute x30, starting transfers between devices, across(): return lax.ppermute(value, 'feed', pairs)  55 us
    ppermute x30, waiting for transfers between devices, across(): return lax.ppermute(value, 'feed', pairs)  44.8 us
    ppermute x24, waiting for transfers between devices, swap(): return lax.ppermute(value, 'feed', pairs)  31.9 us
    pallas_call x2, Pallas kernels, row_products(): pl.pallas_call(rows_kernel, grid=(2 * steps,), in_specs=[pl.BlockSpec(mem...  28.9 us
    ppermute x24, starting transfers between devices, swap(): return lax.ppermute(value, 'feed', pairs)  21.6 us
    pallas_call x2, Pallas kernels, finish(): pl.pallas_call(functools.partial(finish_kernel, scale, sources), grid=(1,...  18.5 us
    pallas_call x1, Pallas kernels, own_spectra(): pl.pallas_call(own_kernel, grid=(steps,), in_specs=[pl.BlockSpec(memory_s...  9.74 us
  transfers between devices with their start and end apart: 54, of which 26 were waited for; matrix products, arithmetic and copies ran while one was open for 3% of the time, Pallas kernels for 21%

profile of v9, /device:TPU:13, one launch (start us, length us, event | category | flops | bytes accessed | tf_op | source)
XLA Modules:
  0.0 226.8 jit_solution(4640976550221276443)
XLA Ops:
  1.6 3.4 %copy-done = s32[256,16,519]{0,1,2:T(8,128)S(1)} copy-done((s32[256,16,519]{0,1,2:T(8,128)S(1)}, s32[256,16,519]{0,1,2:T(8,128)}, u32[]{:S(2)}) %copy-start) | copy-done | bytes 8503320
  5.0 2.6 %select_rows.1 = (bf16[8448,128]{1,0:T(8,128)(2,1)S(1)}, bf16[8448,128]{1,0:T(8,128)(2,1)S(1)}) custom-call(s32[1,256]{1,0:T(1,128)S(1)} %bitcast.84, s32[8304,256]{1,0:T(8,128)S(1)} %bitcast.78, bf16[64,256]{1,0:T(8,128)(2,1)S(1)} %pad_maximum_fusion.2.parts_ref), custom_call_target="tpu_custom_call" | custom-call | tf_op jit(solution)/shard_map/select_rows/pallas_call | solution.py:354
  10.2 2.1 collective-permute-done.12
  12.3 1.7 dynamic-slice_add_fusion
  14.3 1.7 dynamic-slice_add_fusion.1
  17.5 1.5 collective-permute-start.1
  19.0 2.9 %collective-permute-done.13 = bf16[1056,128]{1,0:T(8,128)(2,1)S(1)} collective-permute-done((bf16[1056,128]{1,0:T(8,128)(2,1)S(1)}, bf16[1056,128]{1,0:T(8,128)(2,1)S(1)}, u32[]{:S(2)}, u32[]{:S(2)}) %collective-permute-start.13) | collective-permute-done | bytes 270368 | tf_op jit(solution)/shard_map/ppermute | solution.py:371
  23.2 4.2 %collective-permute-done.6 = bf16[1056,128]{1,0:T(8,128)(2,1)S(1)} collective-permute-done((bf16[1056,128]{1,0:T(8,128)(2,1)S(1)}, bf16[1056,128]{1,0:T(8,128)(2,1)S(1)}, u32[]{:S(2)}, u32[]{:S(2)}) %collective-permute-start.6) | collective-permute-done | bytes 270368 | tf_op jit(solution)/shard_map/ppermute | solution.py:371
  30.4 2.4 %collective-permute-start.30 = (bf16[528,128]{1,0:T(8,128)(2,1)S(1)}, bf16[528,128]{1,0:T(8,128)(2,1)S(1)}, u32[]{:S(2)}, u32[]{:S(2)}) collective-permute-start(bf16[528,128]{1,0:T(8,128)(2,1)S(1)} %dynamic-slice_add_fusion.7.after_ref), channel_id=1, source_target_pairs={{0,8},{1,9},{2,10},{3,11},{4,12},{5,13},{6,14},{7,15},{8,0},{9,1},... | collective-permute-start | bytes 405512 | tf_op jit(solution)/shard_map/ppermute | solution.py:371
  33.0 2.4 %collective-permute-start.8 = (bf16[528,128]{1,0:T(8,128)(2,1)S(1)}, bf16[528,128]{1,0:T(8,128)(2,1)S(1)}, u32[]{:S(2)}, u32[]{:S(2)}) collective-permute-start(bf16[528,128]{1,0:T(8,128)(2,1)S(1)} %dynamic-slice_add_fusion.8), channel_id=1, source_target_pairs={{0,8},{1,9},{2,10},{3,11},{4,12},{5,13},{6,14},{7,15},{8,0},{9,1},... | collective-permute-start | bytes 405512 | tf_op jit(solution)/shard_map/ppermute | solution.py:371
  35.5 9.7 %own_spectra.1 = (bf16[16,8,256,128]{3,2,1,0:T(8,128)(2,1)S(1)}, bf16[16,128]{1,0:T(8,128)(2,1)S(1)}) custom-call(s32[1]{0:T(128)} %bitcast.place_ref, s32[8304,256]{1,0:T(8,128)S(1)} %bitcast.81, s32[8304,256]{1,0:T(8,128)S(1)} %bitcast.82, f32[32,256]{1,0:T(8,128)S(1)} %bitcast.83, bf16[256,256]{1,0:T(8,128)(2,1)S(1)} %copy-done.3, ...), custom_call_target="tpu_custom_call" | custom-call | flops 4294967296 | bytes 16891904 | tf_op jit(solution)/shard_map/own_spectra/pallas_call | solution.py:295
  45.8 3.9 %collective-permute-done.35 = bf16[528,128]{1,0:T(8,128)(2,1)S(1)} collective-permute-done((bf16[528,128]{1,0:T(8,128)(2,1)S(1)}, bf16[528,128]{1,0:T(8,128)(2,1)S(1)}, u32[]{:S(2)}, u32[]{:S(2)}) %collective-permute-start.35) | collective-permute-done | bytes 135200 | tf_op jit(solution)/shard_map/ppermute | solution.py:371
  50.5 2.1 collective-permute-done.8
  53.4 2.1 collective-permute-done.3
  56.4 1.5 collective-permute-start.31
  58.1 1.5 collective-permute-start.10
  60.6 1.6 collective-permute-done.31
  63.7 10.1 %collective-permute-done.10 = bf16[1056,128]{1,0:T(8,128)(2,1)S(1)} collective-permute-done((bf16[1056,128]{1,0:T(8,128)(2,1)S(1)}, bf16[1056,128]{1,0:T(8,128)(2,1)S(1)}, u32[]{:S(2)}, u32[]{:S(2)}) %collective-permute-start.10) | collective-permute-done | bytes 270368 | tf_op jit(solution)/shard_map/ppermute | solution.py:371
  74.1 2.4 %collective-permute-start.11 = (bf16[4224,128]{1,0:T(8,128)(2,1)S(1)}, bf16[4224,128]{1,0:T(8,128)(2,1)S(1)}, u32[]{:S(2)}, u32[]{:S(2)}) collective-permute-start(bf16[4224,128]{1,0:T(8,128)(2,1)S(1)} %get-tuple-element.61.refs_0_), channel_id=1, source_target_pairs={{0,1},{1,0},{2,3},{3,2},{4,5},{5,4},{6,7},{7,6},{8,9},{9,8},{10,11... | collective-permute-start | bytes 3244040 | tf_op jit(solution)/shard_map/ppermute | solution.py:371
  76.9 1.9 collective-permute-done.11
  79.0 14.4 %row_products.2 = (s16[16,272,256]{2,1,0:T(8,128)(2,1)S(1)}, bf16[1024,256]{1,0:T(8,128)(2,1)}) custom-call(s32[1]{0:T(128)} %bitcast.place_ref, bf16[8448,128]{1,0:T(8,128)(2,1)S(1)} %constant_dynamic-update-slice_fusion.10.main_ref.next_ref, bf16[8448,128]{1,0:T(8,128)(2,1)S(1)} %constant_dynamic-update-slice_fusion.10.main_ref.next_ref, ...), custom_call_target="tpu_custom_call" | custom-call | flops 4294967296 | bytes 12648448 | tf_op jit(solution)/shard_map/row_products/pallas_call | solution.py:466
  93.6 3.1 %collective-permute-start.29 = (s16[272,256]{1,0:T(8,128)(2,1)S(1)}, s16[272,256]{1,0:T(8,128)(2,1)S(1)}, u32[]{:S(2)}, u32[]{:S(2)}) collective-permute-start(s16[272,256]{1,0:T(8,128)(2,1)S(1)} %get-tuple-element.41), channel_id=1, source_target_pairs={{0,15},{1,14},{2,13},{3,12},{4,11},{5,10},{6,9},{7,8},{8,7},{9,6},... | collective-permute-start | bytes 417800 | tf_op jit(solution)/shard_map/ppermute | solution.py:582
  96.7 1.9 collective-permute-start.27
  98.6 6.7 %collective-permute-start.25 = (s16[272,256]{1,0:T(8,128)(2,1)S(1)}, s16[272,256]{1,0:T(8,128)(2,1)S(1)}, u32[]{:S(2)}, u32[]{:S(2)}) collective-permute-start(s16[272,256]{1,0:T(8,128)(2,1)S(1)} %get-tuple-element.45), channel_id=1, source_target_pairs={{0,11},{1,10},{2,9},{3,8},{4,15},{5,14},{6,13},{7,12},{8,3},{9,2},... | collective-permute-start | bytes 417800 | tf_op jit(solution)/shard_map/ppermute | solution.py:582
  105.5 14.5 %row_products.3 = (s16[16,272,256]{2,1,0:T(8,128)(2,1)S(1)}, bf16[1024,256]{1,0:T(8,128)(2,1)}) custom-call(s32[1]{0:T(128)} %bitcast.place_ref, bf16[8448,128]{1,0:T(8,128)(2,1)S(1)} %constant_dynamic-update-slice_fusion.main_ref.next_ref, bf16[8448,128]{1,0:T(8,128)(2,1)S(1)} %constant_dynamic-update-slice_fusion.main_ref.next_ref, ...), custom_call_target="tpu_custom_call" | custom-call | flops 4294967296 | bytes 12648448 | tf_op jit(solution)/shard_map/row_products/pallas_call | solution.py:466
  120.1 3.2 %collective-permute-start.23 = (s16[272,256]{1,0:T(8,128)(2,1)S(1)}, s16[272,256]{1,0:T(8,128)(2,1)S(1)}, u32[]{:S(2)}, u32[]{:S(2)}) collective-permute-start(s16[272,256]{1,0:T(8,128)(2,1)S(1)} %get-tuple-element.47), channel_id=1, source_target_pairs={{0,9},{1,8},{2,11},{3,10},{4,13},{5,12},{6,15},{7,14},{8,1},{9,0},... | collective-permute-start | bytes 417800 | tf_op jit(solution)/shard_map/ppermute | solution.py:582
  123.3 8.0 %collective-permute-done.26.refs_12_ = s16[272,256]{1,0:T(8,128)(2,1)S(1)} collective-permute-done((s16[272,256]{1,0:T(8,128)(2,1)S(1)}, s16[272,256]{1,0:T(8,128)(2,1)S(1)}, u32[]{:S(2)}, u32[]{:S(2)}) %collective-permute-start.26) | collective-permute-done | bytes 139296 | tf_op jit(solution)/shard_map/ppermute | solution.py:582
  131.3 4.5 %collective-permute-done.25.refs_11_ = s16[272,256]{1,0:T(8,128)(2,1)S(1)} collective-permute-done((s16[272,256]{1,0:T(8,128)(2,1)S(1)}, s16[272,256]{1,0:T(8,128)(2,1)S(1)}, u32[]{:S(2)}, u32[]{:S(2)}) %collective-permute-start.25) | collective-permute-done | bytes 139296 | tf_op jit(solution)/shard_map/ppermute | solution.py:582
  135.8 2.7 %collective-permute-start.20 = (s16[272,256]{1,0:T(8,128)(2,1)S(1)}, s16[272,256]{1,0:T(8,128)(2,1)S(1)}, u32[]{:S(2)}, u32[]{:S(2)}) collective-permute-start(s16[272,256]{1,0:T(8,128)(2,1)S(1)} %get-tuple-element.50), channel_id=1, source_target_pairs={{0,6},{1,7},{2,4},{3,5},{4,2},{5,3},{6,0},{7,1},{8,14},{9,15},{10,... | collective-permute-start | bytes 417800 | tf_op jit(solution)/shard_map/ppermute | solution.py:582
  138.8 2.2 collective-permute-start.53
  142.0 2.8 %collective-permute-done.22.refs_8_ = s16[272,256]{1,0:T(8,128)(2,1)S(1)} collective-permute-done((s16[272,256]{1,0:T(8,128)(2,1)S(1)}, s16[272,256]{1,0:T(8,128)(2,1)S(1)}, u32[]{:S(2)}, u32[]{:S(2)}) %collective-permute-start.22) | collective-permute-done | bytes 139296 | tf_op jit(solution)/shard_map/ppermute | solution.py:582
  144.8 3.2 %collective-permute-start.51 = (s16[272,256]{1,0:T(8,128)(2,1)S(1)}, s16[272,256]{1,0:T(8,128)(2,1)S(1)}, u32[]{:S(2)}, u32[]{:S(2)}) collective-permute-start(s16[272,256]{1,0:T(8,128)(2,1)S(1)} %get-tuple-element.27), channel_id=1, source_target_pairs={{0,13},{1,12},{2,15},{3,14},{4,9},{5,8},{6,11},{7,10},{8,5},{9,4},... | collective-permute-start | bytes 417800 | tf_op jit(solution)/shard_map/ppermute | solution.py:582
  148.0 3.8 %collective-permute-done.21.refs_7_ = s16[272,256]{1,0:T(8,128)(2,1)S(1)} collective-permute-done((s16[272,256]{1,0:T(8,128)(2,1)S(1)}, s16[272,256]{1,0:T(8,128)(2,1)S(1)}, u32[]{:S(2)}, u32[]{:S(2)}) %collective-permute-start.21) | collective-permute-done | bytes 139296 | tf_op jit(solution)/shard_map/ppermute | solution.py:582
  152.9 1.9 collective-permute-done.20.refs_6_
  154.8 8.4 %collective-permute-start.49 = (s16[272,256]{1,0:T(8,128)(2,1)S(1)}, s16[272,256]{1,0:T(8,128)(2,1)S(1)}, u32[]{:S(2)}, u32[]{:S(2)}) collective-permute-start(s16[272,256]{1,0:T(8,128)(2,1)S(1)} %get-tuple-element.29), channel_id=1, source_target_pairs={{0,11},{1,10},{2,9},{3,8},{4,15},{5,14},{6,13},{7,12},{8,3},{9,2},... | collective-permute-start | bytes 417800 | tf_op jit(solution)/shard_map/ppermute | solution.py:582
  163.2 6.7 %collective-permute-start.47 = (s16[272,256]{1,0:T(8,128)(2,1)S(1)}, s16[272,256]{1,0:T(8,128)(2,1)S(1)}, u32[]{:S(2)}, u32[]{:S(2)}) collective-permute-start(s16[272,256]{1,0:T(8,128)(2,1)S(1)} %get-tuple-element.31), channel_id=1, source_target_pairs={{0,9},{1,8},{2,11},{3,10},{4,13},{5,12},{6,15},{7,14},{8,1},{9,0},... | collective-permute-start | bytes 417800 | tf_op jit(solution)/shard_map/ppermute | solution.py:582
  169.9 10.9 %collective-permute-done.50.refs_12_ = s16[272,256]{1,0:T(8,128)(2,1)S(1)} collective-permute-done((s16[272,256]{1,0:T(8,128)(2,1)S(1)}, s16[272,256]{1,0:T(8,128)(2,1)S(1)}, u32[]{:S(2)}, u32[]{:S(2)}) %collective-permute-start.50) | collective-permute-done | bytes 139296 | tf_op jit(solution)/shard_map/ppermute | solution.py:582
  180.7 2.9 %collective-permute-done.49.refs_11_ = s16[272,256]{1,0:T(8,128)(2,1)S(1)} collective-permute-done((s16[272,256]{1,0:T(8,128)(2,1)S(1)}, s16[272,256]{1,0:T(8,128)(2,1)S(1)}, u32[]{:S(2)}, u32[]{:S(2)}) %collective-permute-start.49) | collective-permute-done | bytes 139296 | tf_op jit(solution)/shard_map/ppermute | solution.py:582
  183.6 2.7 %collective-permute-start.44 = (s16[272,256]{1,0:T(8,128)(2,1)S(1)}, s16[272,256]{1,0:T(8,128)(2,1)S(1)}, u32[]{:S(2)}, u32[]{:S(2)}) collective-permute-start(s16[272,256]{1,0:T(8,128)(2,1)S(1)} %get-tuple-element.34), channel_id=1, source_target_pairs={{0,6},{1,7},{2,4},{3,5},{4,2},{5,3},{6,0},{7,1},{8,14},{9,15},{10,... | collective-permute-start | bytes 417800 | tf_op jit(solution)/shard_map/ppermute | solution.py:582
  186.6 2.7 %collective-permute-start.43 = (s16[272,256]{1,0:T(8,128)(2,1)S(1)}, s16[272,256]{1,0:T(8,128)(2,1)S(1)}, u32[]{:S(2)}, u32[]{:S(2)}) collective-permute-start(s16[272,256]{1,0:T(8,128)(2,1)S(1)} %get-tuple-element.35), channel_id=1, source_target_pairs={{0,5},{1,4},{2,7},{3,6},{4,1},{5,0},{6,3},{7,2},{8,13},{9,12},{10,... | collective-permute-start | bytes 417800 | tf_op jit(solution)/shard_map/ppermute | solution.py:582
  189.6 1.8 collective-permute-start.42
  194.9 3.0 %collective-permute-done.44.refs_6_ = s16[272,256]{1,0:T(8,128)(2,1)S(1)} collective-permute-done((s16[272,256]{1,0:T(8,128)(2,1)S(1)}, s16[272,256]{1,0:T(8,128)(2,1)S(1)}, u32[]{:S(2)}, u32[]{:S(2)}) %collective-permute-start.44) | collective-permute-done | bytes 139296 | tf_op jit(solution)/shard_map/ppermute | solution.py:582
  198.5 2.4 %collective-permute-done.43.refs_5_ = s16[272,256]{1,0:T(8,128)(2,1)S(1)} collective-permute-done((s16[272,256]{1,0:T(8,128)(2,1)S(1)}, s16[272,256]{1,0:T(8,128)(2,1)S(1)}, u32[]{:S(2)}, u32[]{:S(2)}) %collective-permute-start.43) | collective-permute-done | bytes 139296 | tf_op jit(solution)/shard_map/ppermute | solution.py:582
  200.9 2.5 %collective-permute-start.19 = (s16[272,256]{1,0:T(8,128)(2,1)S(1)}, s16[272,256]{1,0:T(8,128)(2,1)S(1)}, u32[]{:S(2)}, u32[]{:S(2)}) collective-permute-start(s16[272,256]{1,0:T(8,128)(2,1)S(1)} %get-tuple-element.51), channel_id=1, source_target_pairs={{0,5},{1,4},{2,7},{3,6},{4,1},{5,0},{6,3},{7,2},{8,13},{9,12},{10,... | collective-permute-start | bytes 417800 | tf_op jit(solution)/shard_map/ppermute | solution.py:582
  203.9 2.2 collective-permute-start.18
  206.1 2.1 collective-permute-start.16
  208.3 9.2 %finish.2.refs_16_ = f32[16384,128]{1,0:T(8,128)} custom-call(s32[4096]{0:T(1024)S(1)} %fusion.2.slot_ref, s16[272,256]{1,0:T(8,128)(2,1)S(1)} %get-tuple-element.40.refs_0_, s16[272,256]{1,0:T(8,128)(2,1)S(1)} %collective-permute-done.39.refs_1_, s16[272,256]{1,0:T(8,128)(2,1)S(1)} %collective-permute-done.40.refs_2_, ...), custom_call_target="tpu_custom_call" | custom-call | tf_op jit(solution)/shard_map/finish/pallas_call | solution.py:561
  217.5 9.2 %finish.3 = f32[16384,128]{1,0:T(8,128)} custom-call(s32[4096]{0:T(1024)S(1)} %fusion.2.slot_ref, s16[272,256]{1,0:T(8,128)(2,1)S(1)} %get-tuple-element.56.refs_0_, s16[272,256]{1,0:T(8,128)(2,1)S(1)} %collective-permute-done.15.refs_1_, s16[272,256]{1,0:T(8,128)(2,1)S(1)} %collective-permute-done.16.refs_2_, ...), custom_call_target="tpu_custom_call", output_to_operand_aliasing={{}: (17, {})} | custom-call | tf_op jit(solution)/shard_map/finish/pallas_call | solution.py:561
  (134 shorter events, 25.1 us)
Async XLA Ops:
  14.1 7.8 %collective-permute-start.13 = (bf16[1056,128]{1,0:T(8,128)(2,1)S(1)}, bf16[1056,128]{1,0:T(8,128)(2,1)S(1)}, u32[]{:S(2)}, u32[]{:S(2)}) collective-permute-start(bf16[1056,128]{1,0:T(8,128)(2,1)S(1)} %constant_dynamic-slice_fusion.3), channel_id=1, source_target_pairs={{0,2},{1,3},{2,0},{3,1},{4,6},{5,7},{6,4},{7,5},{8,10},{9,11},{10,... | collective-permute-start | bytes 811016 | tf_op jit(solution)/shard_map/ppermute | solution.py:371
  14.2 7.8 %collective-permute-start.33 = (bf16[1056,128]{1,0:T(8,128)(2,1)S(1)}, bf16[1056,128]{1,0:T(8,128)(2,1)S(1)}, u32[]{:S(2)}, u32[]{:S(2)}) collective-permute-start(bf16[1056,128]{1,0:T(8,128)(2,1)S(1)} %constant_dynamic-slice_fusion.1), channel_id=1, source_target_pairs={{0,4},{1,5},{2,6},{3,7},{4,0},{5,1},{6,2},{7,3},{8,12},{9,13},{10,... | collective-permute-start | bytes 811016 | tf_op jit(solution)/shard_map/ppermute | solution.py:371
  16.1 11.3 %collective-permute-start.6 = (bf16[1056,128]{1,0:T(8,128)(2,1)S(1)}, bf16[1056,128]{1,0:T(8,128)(2,1)S(1)}, u32[]{:S(2)}, u32[]{:S(2)}) collective-permute-start(bf16[1056,128]{1,0:T(8,128)(2,1)S(1)} %constant_dynamic-slice_fusion.6), channel_id=1, source_target_pairs={{0,4},{1,5},{2,6},{3,7},{4,0},{5,1},{6,2},{7,3},{8,12},{9,13},{10,... | collective-permute-start | bytes 811016 | tf_op jit(solution)/shard_map/ppermute | solution.py:371
  17.5 11.6 %collective-permute-start.1 = (bf16[1056,128]{1,0:T(8,128)(2,1)S(1)}, bf16[1056,128]{1,0:T(8,128)(2,1)S(1)}, u32[]{:S(2)}, u32[]{:S(2)}) collective-permute-start(bf16[1056,128]{1,0:T(8,128)(2,1)S(1)} %constant_dynamic-slice_fusion.8), channel_id=1, source_target_pairs={{0,2},{1,3},{2,0},{3,1},{4,6},{5,7},{6,4},{7,5},{8,10},{9,11},{10,... | collective-permute-start | bytes 811016 | tf_op jit(solution)/shard_map/ppermute | solution.py:371
  21.9 8.4 %collective-permute-start.14 = (bf16[528,128]{1,0:T(8,128)(2,1)S(1)}, bf16[528,128]{1,0:T(8,128)(2,1)S(1)}, u32[]{:S(2)}, u32[]{:S(2)}) collective-permute-start(bf16[528,128]{1,0:T(8,128)(2,1)S(1)} %constant_dynamic-slice_fusion.2), channel_id=1, source_target_pairs={{0,4},{1,5},{2,6},{3,7},{4,0},{5,1},{6,2},{7,3},{8,12},{9,13},{10,... | collective-permute-start | bytes 405512 | tf_op jit(solution)/shard_map/ppermute | solution.py:371
  22.2 10.6 %collective-permute-start.34 = (bf16[528,128]{1,0:T(8,128)(2,1)S(1)}, bf16[528,128]{1,0:T(8,128)(2,1)S(1)}, u32[]{:S(2)}, u32[]{:S(2)}) collective-permute-start(bf16[528,128]{1,0:T(8,128)(2,1)S(1)} %constant_dynamic-slice_fusion), channel_id=1, source_target_pairs={{0,2},{1,3},{2,0},{3,1},{4,6},{5,7},{6,4},{7,5},{8,10},{9,11},{10,... | collective-permute-start | bytes 405512 | tf_op jit(solution)/shard_map/ppermute | solution.py:371
  29.1 6.2 %collective-permute-start.2 = (bf16[528,128]{1,0:T(8,128)(2,1)S(1)}, bf16[528,128]{1,0:T(8,128)(2,1)S(1)}, u32[]{:S(2)}, u32[]{:S(2)}) collective-permute-start(bf16[528,128]{1,0:T(8,128)(2,1)S(1)} %constant_dynamic-slice_fusion.7), channel_id=1, source_target_pairs={{0,4},{1,5},{2,6},{3,7},{4,0},{5,1},{6,2},{7,3},{8,12},{9,13},{10,... | collective-permute-start | bytes 405512 | tf_op jit(solution)/shard_map/ppermute | solution.py:371
  30.4 25.3 %collective-permute-start.30 = (bf16[528,128]{1,0:T(8,128)(2,1)S(1)}, bf16[528,128]{1,0:T(8,128)(2,1)S(1)}, u32[]{:S(2)}, u32[]{:S(2)}) collective-permute-start(bf16[528,128]{1,0:T(8,128)(2,1)S(1)} %dynamic-slice_add_fusion.7.after_ref), channel_id=1, source_target_pairs={{0,8},{1,9},{2,10},{3,11},{4,12},{5,13},{6,14},{7,15},{8,0},{9,1},... | collective-permute-start | bytes 405512 | tf_op jit(solution)/shard_map/ppermute | solution.py:371
  32.8 16.9 %collective-permute-start.35 = (bf16[528,128]{1,0:T(8,128)(2,1)S(1)}, bf16[528,128]{1,0:T(8,128)(2,1)S(1)}, u32[]{:S(2)}, u32[]{:S(2)}) collective-permute-start(bf16[528,128]{1,0:T(8,128)(2,1)S(1)} %dynamic-slice_add_fusion.6), channel_id=1, source_target_pairs={{0,8},{1,9},{2,10},{3,11},{4,12},{5,13},{6,14},{7,15},{8,0},{9,1},... | collective-permute-start | bytes 405512 | tf_op jit(solution)/shard_map/ppermute | solution.py:371
  33.0 19.6 %collective-permute-start.8 = (bf16[528,128]{1,0:T(8,128)(2,1)S(1)}, bf16[528,128]{1,0:T(8,128)(2,1)S(1)}, u32[]{:S(2)}, u32[]{:S(2)}) collective-permute-start(bf16[528,128]{1,0:T(8,128)(2,1)S(1)} %dynamic-slice_add_fusion.8), channel_id=1, source_target_pairs={{0,8},{1,9},{2,10},{3,11},{4,12},{5,13},{6,14},{7,15},{8,0},{9,1},... | collective-permute-start | bytes 405512 | tf_op jit(solution)/shard_map/ppermute | solution.py:371
  35.4 20.1 %collective-permute-start.3 = (bf16[528,128]{1,0:T(8,128)(2,1)S(1)}, bf16[528,128]{1,0:T(8,128)(2,1)S(1)}, u32[]{:S(2)}, u32[]{:S(2)}) collective-permute-start(bf16[528,128]{1,0:T(8,128)(2,1)S(1)} %dynamic-slice_add_fusion.9), channel_id=1, source_target_pairs={{0,8},{1,9},{2,10},{3,11},{4,12},{5,13},{6,14},{7,15},{8,0},{9,1},... | collective-permute-start | bytes 405512 | tf_op jit(solution)/shard_map/ppermute | solution.py:371
  49.8 8.1 %collective-permute-start.36 = (bf16[528,128]{1,0:T(8,128)(2,1)S(1)}, bf16[528,128]{1,0:T(8,128)(2,1)S(1)}, u32[]{:S(2)}, u32[]{:S(2)}) collective-permute-start(bf16[528,128]{1,0:T(8,128)(2,1)S(1)} %get-tuple-element.20), channel_id=1, source_target_pairs={{0,2},{1,3},{2,0},{3,1},{4,6},{5,7},{6,4},{7,5},{8,10},{9,11},{10,... | collective-permute-start | bytes 405512 | tf_op jit(solution)/shard_map/ppermute | solution.py:371
  56.4 5.8 %collective-permute-start.31 = (bf16[528,128]{1,0:T(8,128)(2,1)S(1)}, bf16[528,128]{1,0:T(8,128)(2,1)S(1)}, u32[]{:S(2)}, u32[]{:S(2)}) collective-permute-start(bf16[528,128]{1,0:T(8,128)(2,1)S(1)} %get-tuple-element.18), channel_id=1, source_target_pairs={{0,4},{1,5},{2,6},{3,7},{4,0},{5,1},{6,2},{7,3},{8,12},{9,13},{10,... | collective-permute-start | bytes 405512 | tf_op jit(solution)/shard_map/ppermute | solution.py:371
  57.9 18.6 %collective-permute-start.37 = (bf16[1056,128]{1,0:T(8,128)(2,1)S(1)}, bf16[1056,128]{1,0:T(8,128)(2,1)S(1)}, u32[]{:S(2)}, u32[]{:S(2)}) collective-permute-start(bf16[1056,128]{1,0:T(8,128)(2,1)S(1)} %constant_dynamic-update-slice_fusion.4), channel_id=1, source_target_pairs={{0,4},{1,5},{2,6},{3,7},{4,0},{5,1},{6,2},{7,3},{8,12},{9,13},{10,... | collective-permute-start | bytes 811016 | tf_op jit(solution)/shard_map/ppermute | solution.py:371
  58.1 15.7 %collective-permute-start.10 = (bf16[1056,128]{1,0:T(8,128)(2,1)S(1)}, bf16[1056,128]{1,0:T(8,128)(2,1)S(1)}, u32[]{:S(2)}, u32[]{:S(2)}) collective-permute-start(bf16[1056,128]{1,0:T(8,128)(2,1)S(1)} %constant_dynamic-update-slice_fusion.14), channel_id=1, source_target_pairs={{0,4},{1,5},{2,6},{3,7},{4,0},{5,1},{6,2},{7,3},{8,12},{9,13},{10,... | collective-permute-start | bytes 811016 | tf_op jit(solution)/shard_map/ppermute | solution.py:371
  59.7 14.2 %collective-permute-start.5 = (bf16[1056,128]{1,0:T(8,128)(2,1)S(1)}, bf16[1056,128]{1,0:T(8,128)(2,1)S(1)}, u32[]{:S(2)}, u32[]{:S(2)}) collective-permute-start(bf16[1056,128]{1,0:T(8,128)(2,1)S(1)} %constant_dynamic-update-slice_fusion.18), channel_id=1, source_target_pairs={{0,2},{1,3},{2,0},{3,1},{4,6},{5,7},{6,4},{7,5},{8,10},{9,11},{10,... | collective-permute-start | bytes 811016 | tf_op jit(solution)/shard_map/ppermute | solution.py:371
  62.3 14.3 %collective-permute-start.32 = (bf16[1056,128]{1,0:T(8,128)(2,1)S(1)}, bf16[1056,128]{1,0:T(8,128)(2,1)S(1)}, u32[]{:S(2)}, u32[]{:S(2)}) collective-permute-start(bf16[1056,128]{1,0:T(8,128)(2,1)S(1)} %constant_dynamic-update-slice_fusion.8), channel_id=1, source_target_pairs={{0,2},{1,3},{2,0},{3,1},{4,6},{5,7},{6,4},{7,5},{8,10},{9,11},{10,... | collective-permute-start | bytes 811016 | tf_op jit(solution)/shard_map/ppermute | solution.py:371
  76.8 21.8 %collective-permute-start.38 = (bf16[4224,128]{1,0:T(8,128)(2,1)S(1)}, bf16[4224,128]{1,0:T(8,128)(2,1)S(1)}, u32[]{:S(2)}, u32[]{:S(2)}) collective-permute-start(bf16[4224,128]{1,0:T(8,128)(2,1)S(1)} %get-tuple-element.57), channel_id=1, source_target_pairs={{0,1},{1,0},{2,3},{3,2},{4,5},{5,4},{6,7},{7,6},{8,9},{9,8},{10,11... | collective-permute-start | bytes 3244040 | tf_op jit(solution)/shard_map/ppermute | solution.py:371
  93.6 26.4 %collective-permute-start.29 = (s16[272,256]{1,0:T(8,128)(2,1)S(1)}, s16[272,256]{1,0:T(8,128)(2,1)S(1)}, u32[]{:S(2)}, u32[]{:S(2)}) collective-permute-start(s16[272,256]{1,0:T(8,128)(2,1)S(1)} %get-tuple-element.41), channel_id=1, source_target_pairs={{0,15},{1,14},{2,13},{3,12},{4,11},{5,10},{6,9},{7,8},{8,7},{9,6},... | collective-permute-start | bytes 417800 | tf_op jit(solution)/shard_map/ppermute | solution.py:582
  96.7 23.4 %collective-permute-start.28 = (s16[272,256]{1,0:T(8,128)(2,1)S(1)}, s16[272,256]{1,0:T(8,128)(2,1)S(1)}, u32[]{:S(2)}, u32[]{:S(2)}) collective-permute-start(s16[272,256]{1,0:T(8,128)(2,1)S(1)} %get-tuple-element.42), channel_id=1, source_target_pairs={{0,14},{1,15},{2,12},{3,13},{4,10},{5,11},{6,8},{7,9},{8,6},{9,7},... | collective-permute-start | bytes 417800 | tf_op jit(solution)/shard_map/ppermute | solution.py:582
  96.7 26.5 %collective-permute-start.27 = (s16[272,256]{1,0:T(8,128)(2,1)S(1)}, s16[272,256]{1,0:T(8,128)(2,1)S(1)}, u32[]{:S(2)}, u32[]{:S(2)}) collective-permute-start(s16[272,256]{1,0:T(8,128)(2,1)S(1)} %get-tuple-element.43), channel_id=1, source_target_pairs={{0,13},{1,12},{2,15},{3,14},{4,9},{5,8},{6,11},{7,10},{8,5},{9,4},... | collective-permute-start | bytes 417800 | tf_op jit(solution)/shard_map/ppermute | solution.py:582
  98.6 32.7 %collective-permute-start.26 = (s16[272,256]{1,0:T(8,128)(2,1)S(1)}, s16[272,256]{1,0:T(8,128)(2,1)S(1)}, u32[]{:S(2)}, u32[]{:S(2)}) collective-permute-start(s16[272,256]{1,0:T(8,128)(2,1)S(1)} %get-tuple-element.44), channel_id=1, source_target_pairs={{0,12},{1,13},{2,14},{3,15},{4,8},{5,9},{6,10},{7,11},{8,4},{9,5},... | collective-permute-start | bytes 417800 | tf_op jit(solution)/shard_map/ppermute | solution.py:582
  98.6 37.2 %collective-permute-start.25 = (s16[272,256]{1,0:T(8,128)(2,1)S(1)}, s16[272,256]{1,0:T(8,128)(2,1)S(1)}, u32[]{:S(2)}, u32[]{:S(2)}) collective-permute-start(s16[272,256]{1,0:T(8,128)(2,1)S(1)} %get-tuple-element.45), channel_id=1, source_target_pairs={{0,11},{1,10},{2,9},{3,8},{4,15},{5,14},{6,13},{7,12},{8,3},{9,2},... | collective-permute-start | bytes 417800 | tf_op jit(solution)/shard_map/ppermute | solution.py:582
  120.0 18.8 %collective-permute-start.24 = (s16[272,256]{1,0:T(8,128)(2,1)S(1)}, s16[272,256]{1,0:T(8,128)(2,1)S(1)}, u32[]{:S(2)}, u32[]{:S(2)}) collective-permute-start(s16[272,256]{1,0:T(8,128)(2,1)S(1)} %get-tuple-element.46), channel_id=1, source_target_pairs={{0,10},{1,11},{2,8},{3,9},{4,14},{5,15},{6,12},{7,13},{8,2},{9,3},... | collective-permute-start | bytes 417800 | tf_op jit(solution)/shard_map/ppermute | solution.py:582
  120.1 21.7 %collective-permute-start.23 = (s16[272,256]{1,0:T(8,128)(2,1)S(1)}, s16[272,256]{1,0:T(8,128)(2,1)S(1)}, u32[]{:S(2)}, u32[]{:S(2)}) collective-permute-start(s16[272,256]{1,0:T(8,128)(2,1)S(1)} %get-tuple-element.47), channel_id=1, source_target_pairs={{0,9},{1,8},{2,11},{3,10},{4,13},{5,12},{6,15},{7,14},{8,1},{9,0},... | collective-permute-start | bytes 417800 | tf_op jit(solution)/shard_map/ppermute | solution.py:582
  123.3 21.5 %collective-permute-start.22 = (s16[272,256]{1,0:T(8,128)(2,1)S(1)}, s16[272,256]{1,0:T(8,128)(2,1)S(1)}, u32[]{:S(2)}, u32[]{:S(2)}) collective-permute-start(s16[272,256]{1,0:T(8,128)(2,1)S(1)} %get-tuple-element.48), channel_id=1, source_target_pairs={{0,8},{1,9},{2,10},{3,11},{4,12},{5,13},{6,14},{7,15},{8,0},{9,1},... | collective-permute-start | bytes 417800 | tf_op jit(solution)/shard_map/ppermute | solution.py:582
  131.3 20.5 %collective-permute-start.21 = (s16[272,256]{1,0:T(8,128)(2,1)S(1)}, s16[272,256]{1,0:T(8,128)(2,1)S(1)}, u32[]{:S(2)}, u32[]{:S(2)}) collective-permute-start(s16[272,256]{1,0:T(8,128)(2,1)S(1)} %get-tuple-element.49), channel_id=1, source_target_pairs={{0,7},{1,6},{2,5},{3,4},{4,3},{5,2},{6,1},{7,0},{8,15},{9,14},{10,... | collective-permute-start | bytes 417800 | tf_op jit(solution)/shard_map/ppermute | solution.py:582
  135.8 18.9 %collective-permute-start.20 = (s16[272,256]{1,0:T(8,128)(2,1)S(1)}, s16[272,256]{1,0:T(8,128)(2,1)S(1)}, u32[]{:S(2)}, u32[]{:S(2)}) collective-permute-start(s16[272,256]{1,0:T(8,128)(2,1)S(1)} %get-tuple-element.50), channel_id=1, source_target_pairs={{0,6},{1,7},{2,4},{3,5},{4,2},{5,3},{6,0},{7,1},{8,14},{9,15},{10,... | collective-permute-start | bytes 417800 | tf_op jit(solution)/shard_map/ppermute | solution.py:582
  138.8 24.4 %collective-permute-start.53 = (s16[272,256]{1,0:T(8,128)(2,1)S(1)}, s16[272,256]{1,0:T(8,128)(2,1)S(1)}, u32[]{:S(2)}, u32[]{:S(2)}) collective-permute-start(s16[272,256]{1,0:T(8,128)(2,1)S(1)} %get-tuple-element.25), channel_id=1, source_target_pairs={{0,15},{1,14},{2,13},{3,12},{4,11},{5,10},{6,9},{7,8},{8,7},{9,6},... | collective-permute-start | bytes 417800 | tf_op jit(solution)/shard_map/ppermute | solution.py:582
  141.8 21.4 %collective-permute-start.52 = (s16[272,256]{1,0:T(8,128)(2,1)S(1)}, s16[272,256]{1,0:T(8,128)(2,1)S(1)}, u32[]{:S(2)}, u32[]{:S(2)}) collective-permute-start(s16[272,256]{1,0:T(8,128)(2,1)S(1)} %get-tuple-element.26), channel_id=1, source_target_pairs={{0,14},{1,15},{2,12},{3,13},{4,10},{5,11},{6,8},{7,9},{8,6},{9,7},... | collective-permute-start | bytes 417800 | tf_op jit(solution)/shard_map/ppermute | solution.py:582
  144.8 25.1 %collective-permute-start.51 = (s16[272,256]{1,0:T(8,128)(2,1)S(1)}, s16[272,256]{1,0:T(8,128)(2,1)S(1)}, u32[]{:S(2)}, u32[]{:S(2)}) collective-permute-start(s16[272,256]{1,0:T(8,128)(2,1)S(1)} %get-tuple-element.27), channel_id=1, source_target_pairs={{0,13},{1,12},{2,15},{3,14},{4,9},{5,8},{6,11},{7,10},{8,5},{9,4},... | collective-permute-start | bytes 417800 | tf_op jit(solution)/shard_map/ppermute | solution.py:582
  151.8 28.9 %collective-permute-start.50 = (s16[272,256]{1,0:T(8,128)(2,1)S(1)}, s16[272,256]{1,0:T(8,128)(2,1)S(1)}, u32[]{:S(2)}, u32[]{:S(2)}) collective-permute-start(s16[272,256]{1,0:T(8,128)(2,1)S(1)} %get-tuple-element.28), channel_id=1, source_target_pairs={{0,12},{1,13},{2,14},{3,15},{4,8},{5,9},{6,10},{7,11},{8,4},{9,5},... | collective-permute-start | bytes 417800 | tf_op jit(solution)/shard_map/ppermute | solution.py:582
  154.8 28.8 %collective-permute-start.49 = (s16[272,256]{1,0:T(8,128)(2,1)S(1)}, s16[272,256]{1,0:T(8,128)(2,1)S(1)}, u32[]{:S(2)}, u32[]{:S(2)}) collective-permute-start(s16[272,256]{1,0:T(8,128)(2,1)S(1)} %get-tuple-element.29), channel_id=1, source_target_pairs={{0,11},{1,10},{2,9},{3,8},{4,15},{5,14},{6,13},{7,12},{8,3},{9,2},... | collective-permute-start | bytes 417800 | tf_op jit(solution)/shard_map/ppermute | solution.py:582
  163.2 23.4 %collective-permute-start.48 = (s16[272,256]{1,0:T(8,128)(2,1)S(1)}, s16[272,256]{1,0:T(8,128)(2,1)S(1)}, u32[]{:S(2)}, u32[]{:S(2)}) collective-permute-start(s16[272,256]{1,0:T(8,128)(2,1)S(1)} %get-tuple-element.30), channel_id=1, source_target_pairs={{0,10},{1,11},{2,8},{3,9},{4,14},{5,15},{6,12},{7,13},{8,2},{9,3},... | collective-permute-start | bytes 417800 | tf_op jit(solution)/shard_map/ppermute | solution.py:582
  163.2 26.4 %collective-permute-start.47 = (s16[272,256]{1,0:T(8,128)(2,1)S(1)}, s16[272,256]{1,0:T(8,128)(2,1)S(1)}, u32[]{:S(2)}, u32[]{:S(2)}) collective-permute-start(s16[272,256]{1,0:T(8,128)(2,1)S(1)} %get-tuple-element.31), channel_id=1, source_target_pairs={{0,9},{1,8},{2,11},{3,10},{4,13},{5,12},{6,15},{7,14},{8,1},{9,0},... | collective-permute-start | bytes 417800 | tf_op jit(solution)/shard_map/ppermute | solution.py:582
  169.9 22.7 %collective-permute-start.46 = (s16[272,256]{1,0:T(8,128)(2,1)S(1)}, s16[272,256]{1,0:T(8,128)(2,1)S(1)}, u32[]{:S(2)}, u32[]{:S(2)}) collective-permute-start(s16[272,256]{1,0:T(8,128)(2,1)S(1)} %get-tuple-element.32), channel_id=1, source_target_pairs={{0,8},{1,9},{2,10},{3,11},{4,12},{5,13},{6,14},{7,15},{8,0},{9,1},... | collective-permute-start | bytes 417800 | tf_op jit(solution)/shard_map/ppermute | solution.py:582
  180.7 14.2 %collective-permute-start.45 = (s16[272,256]{1,0:T(8,128)(2,1)S(1)}, s16[272,256]{1,0:T(8,128)(2,1)S(1)}, u32[]{:S(2)}, u32[]{:S(2)}) collective-permute-start(s16[272,256]{1,0:T(8,128)(2,1)S(1)} %get-tuple-element.33), channel_id=1, source_target_pairs={{0,7},{1,6},{2,5},{3,4},{4,3},{5,2},{6,1},{7,0},{8,15},{9,14},{10,... | collective-permute-start | bytes 417800 | tf_op jit(solution)/shard_map/ppermute | solution.py:582
  183.6 14.3 %collective-permute-start.44 = (s16[272,256]{1,0:T(8,128)(2,1)S(1)}, s16[272,256]{1,0:T(8,128)(2,1)S(1)}, u32[]{:S(2)}, u32[]{:S(2)}) collective-permute-start(s16[272,256]{1,0:T(8,128)(2,1)S(1)} %get-tuple-element.34), channel_id=1, source_target_pairs={{0,6},{1,7},{2,4},{3,5},{4,2},{5,3},{6,0},{7,1},{8,14},{9,15},{10,... | collective-permute-start | bytes 417800 | tf_op jit(solution)/shard_map/ppermute | solution.py:582
  186.6 14.3 %collective-permute-start.43 = (s16[272,256]{1,0:T(8,128)(2,1)S(1)}, s16[272,256]{1,0:T(8,128)(2,1)S(1)}, u32[]{:S(2)}, u32[]{:S(2)}) collective-permute-start(s16[272,256]{1,0:T(8,128)(2,1)S(1)} %get-tuple-element.35), channel_id=1, source_target_pairs={{0,5},{1,4},{2,7},{3,6},{4,1},{5,0},{6,3},{7,2},{8,13},{9,12},{10,... | collective-permute-start | bytes 417800 | tf_op jit(solution)/shard_map/ppermute | solution.py:582
  189.6 14.3 %collective-permute-start.42 = (s16[272,256]{1,0:T(8,128)(2,1)S(1)}, s16[272,256]{1,0:T(8,128)(2,1)S(1)}, u32[]{:S(2)}, u32[]{:S(2)}) collective-permute-start(s16[272,256]{1,0:T(8,128)(2,1)S(1)} %get-tuple-element.36), channel_id=1, source_target_pairs={{0,4},{1,5},{2,6},{3,7},{4,0},{5,1},{6,2},{7,3},{8,12},{9,13},{10,... | collective-permute-start | bytes 417800 | tf_op jit(solution)/shard_map/ppermute | solution.py:582
  192.6 13.5 %collective-permute-start.41 = (s16[272,256]{1,0:T(8,128)(2,1)S(1)}, s16[272,256]{1,0:T(8,128)(2,1)S(1)}, u32[]{:S(2)}, u32[]{:S(2)}) collective-permute-start(s16[272,256]{1,0:T(8,128)(2,1)S(1)} %get-tuple-element.37), channel_id=1, source_target_pairs={{0,3},{1,2},{2,1},{3,0},{4,7},{5,6},{6,5},{7,4},{8,11},{9,10},{10,... | collective-permute-start | bytes 417800 | tf_op jit(solution)/shard_map/ppermute | solution.py:582
  194.9 11.2 %collective-permute-start.40 = (s16[272,256]{1,0:T(8,128)(2,1)S(1)}, s16[272,256]{1,0:T(8,128)(2,1)S(1)}, u32[]{:S(2)}, u32[]{:S(2)}) collective-permute-start(s16[272,256]{1,0:T(8,128)(2,1)S(1)} %get-tuple-element.38), channel_id=1, source_target_pairs={{0,2},{1,3},{2,0},{3,1},{4,6},{5,7},{6,4},{7,5},{8,10},{9,11},{10,... | collective-permute-start | bytes 417800 | tf_op jit(solution)/shard_map/ppermute | solution.py:582
  197.9 10.3 %collective-permute-start.39 = (s16[272,256]{1,0:T(8,128)(2,1)S(1)}, s16[272,256]{1,0:T(8,128)(2,1)S(1)}, u32[]{:S(2)}, u32[]{:S(2)}) collective-permute-start(s16[272,256]{1,0:T(8,128)(2,1)S(1)} %get-tuple-element.39), channel_id=1, source_target_pairs={{0,1},{1,0},{2,3},{3,2},{4,5},{5,4},{6,7},{7,6},{8,9},{9,8},{10,11... | collective-permute-start | bytes 417800 | tf_op jit(solution)/shard_map/ppermute | solution.py:582
  200.9 16.6 %collective-permute-start.19 = (s16[272,256]{1,0:T(8,128)(2,1)S(1)}, s16[272,256]{1,0:T(8,128)(2,1)S(1)}, u32[]{:S(2)}, u32[]{:S(2)}) collective-permute-start(s16[272,256]{1,0:T(8,128)(2,1)S(1)} %get-tuple-element.51), channel_id=1, source_target_pairs={{0,5},{1,4},{2,7},{3,6},{4,1},{5,0},{6,3},{7,2},{8,13},{9,12},{10,... | collective-permute-start | bytes 417800 | tf_op jit(solution)/shard_map/ppermute | solution.py:582
  203.9 13.6 %collective-permute-start.18 = (s16[272,256]{1,0:T(8,128)(2,1)S(1)}, s16[272,256]{1,0:T(8,128)(2,1)S(1)}, u32[]{:S(2)}, u32[]{:S(2)}) collective-permute-start(s16[272,256]{1,0:T(8,128)(2,1)S(1)} %get-tuple-element.52), channel_id=1, source_target_pairs={{0,4},{1,5},{2,6},{3,7},{4,0},{5,1},{6,2},{7,3},{8,12},{9,13},{10,... | collective-permute-start | bytes 417800 | tf_op jit(solution)/shard_map/ppermute | solution.py:582
  206.1 11.4 %collective-permute-start.17 = (s16[272,256]{1,0:T(8,128)(2,1)S(1)}, s16[272,256]{1,0:T(8,128)(2,1)S(1)}, u32[]{:S(2)}, u32[]{:S(2)}) collective-permute-start(s16[272,256]{1,0:T(8,128)(2,1)S(1)} %get-tuple-element.53), channel_id=1, source_target_pairs={{0,3},{1,2},{2,1},{3,0},{4,7},{5,6},{6,5},{7,4},{8,11},{9,10},{10,... | collective-permute-start | bytes 417800 | tf_op jit(solution)/shard_map/ppermute | solution.py:582
  206.1 11.4 %collective-permute-start.16 = (s16[272,256]{1,0:T(8,128)(2,1)S(1)}, s16[272,256]{1,0:T(8,128)(2,1)S(1)}, u32[]{:S(2)}, u32[]{:S(2)}) collective-permute-start(s16[272,256]{1,0:T(8,128)(2,1)S(1)} %get-tuple-element.54), channel_id=1, source_target_pairs={{0,2},{1,3},{2,0},{3,1},{4,6},{5,7},{6,4},{7,5},{8,10},{9,11},{10,... | collective-permute-start | bytes 417800 | tf_op jit(solution)/shard_map/ppermute | solution.py:582
  208.2 9.3 %collective-permute-start.15 = (s16[272,256]{1,0:T(8,128)(2,1)S(1)}, s16[272,256]{1,0:T(8,128)(2,1)S(1)}, u32[]{:S(2)}, u32[]{:S(2)}) collective-permute-start(s16[272,256]{1,0:T(8,128)(2,1)S(1)} %get-tuple-element.55), channel_id=1, source_target_pairs={{0,1},{1,0},{2,3},{3,2},{4,5},{5,4},{6,7},{7,6},{8,9},{9,8},{10,11... | collective-permute-start | bytes 417800 | tf_op jit(solution)/shard_map/ppermute | solution.py:582
  (14 other events, 185.3 us)

commit v10 on v7

--- a/solution.py
+++ b/solution.py
@@ -307,7 +307,7 @@
             pl.BlockSpec((16, LANES), lambda i: (0, 0)),
         ],
         out_shape=[
-            jax.ShapeDtypeStruct((ch, steps, count, 2 * STEPS * STEP), jnp.bfloat16),
+            pltpu.HBM((ch, steps, count, 2 * STEPS * STEP), jnp.bfloat16),
             jax.ShapeDtypeStruct((16, LANES), jnp.bfloat16),
         ],
         scratch_shapes=[
@@ -400,25 +400,22 @@
     left_1, right_1 = gather_half(left_3, 4, left_1), gather_half(right_3, 2, right_1)
     left, right = gather_half(left_1, 2, left), gather_half(right_1, 4, right)
     half = jnp.concatenate([left, right], axis=0)
-    return half, lambda: gather_half(half, 1, value)
-
-
-def rows_kernel(main_ref, next_ref, parts_ref, weights_ref, own_ref, after_ref, out_ref, left, own, sems):
+    return (left_1, right_1), lambda: gather_half(half, 1, value)
+
+
+def rows_kernel(main_ref, next_ref, parts_ref, weights_ref, own_ref, *refs):
+    out_ref, left, own, sems = refs[-4:]
     step = pl.program_id(0)
-    steps = pl.num_programs(0) // 2
-    ch = left.shape[0]
+    ch, steps = own.shape[:2]
     rows = main_ref.shape[1]
 
     def copy(c):
         return pltpu.make_async_copy(own_ref.at[c], own.at[c], sems.at[c])
 
-    @pl.when(step == 0)
-    def _():
-        for c in range(ch):
-            copy(c).start()
-
     @pl.when(step < steps)
     def _():
+        for index in range(ch // steps):
+            copy(step * (ch // steps) + index).start()
         words = jnp.concatenate([main_ref[...], next_ref[...]], axis=0).astype(jnp.float32).astype(jnp.int32)
         parts = parts_ref[...].astype(jnp.float32)
         gains = parts[: 2 * ch] * 16.0 + parts[2 * ch :]
@@ -451,20 +448,20 @@
     ch, steps, count, width = own.shape
     rows = words.shape[1]
     main = STEPS * STEP * ch
-    each = ch // steps
+    each = 4
     return pl.pallas_call(
         rows_kernel,
-        grid=(2 * steps,),
+        grid=(steps + ch // each,),
         in_specs=[
             pl.BlockSpec((main, rows), lambda i: (jnp.minimum(i, steps - 1), 0)),
             pl.BlockSpec((STEP * ch, rows), lambda i: ((jnp.minimum(i, steps - 1) + 1) * STEPS, 0)),
             pl.BlockSpec(parts.shape, lambda i: (0, 0)),
             pl.BlockSpec(weights.shape, lambda i: (0, 0)),
             pl.BlockSpec(memory_space=pltpu.HBM),
-            pl.BlockSpec(memory_space=pl.ANY),
-        ],
+        ]
+        + [pl.BlockSpec(memory_space=pl.ANY)] * len(after),
         out_specs=pl.BlockSpec((each, count + 16, 2 * rows), lambda i: (jnp.maximum(i - steps, 0), 0, 0)),
-        out_shape=jax.ShapeDtypeStruct((ch, count + 16, 2 * rows), jnp.int16),
+        out_shape=pltpu.HBM((ch, count + 16, 2 * rows), jnp.int16),
         scratch_shapes=[
             pltpu.VMEM((ch, steps * width, 2 * rows), jnp.bfloat16),
             pltpu.VMEM(own.shape, jnp.bfloat16),
@@ -477,7 +474,7 @@
             transcendentals=0,
         ),
         name="row_products",
-    )(words, words, parts, weights, own, after)
+    )(words, words, parts, weights, own, *after)
 
 
 def finish_kernel(scale, slot_ref, coded_ref, *refs):
@@ -560,11 +557,12 @@
 
     sums = [sum_over_feed(value, None if index else work) for index, value in enumerate(picked)]
     own = held[0]
-    out = None
+    out, after = None, sums[-1][0]
     for index in range(pieces):
         rows = sums[index][1]()
         parts = rows[lines : lines + 4 * ch]
-        coded = row_products(rows, parts, own, weights, sums[-1][0])
+        coded = row_products(rows, parts, own, weights, after)
+        after = [coded]
         moved = lax.all_to_all(coded, "feed", split_axis=0, concat_axis=0, tiled=True)
         out = finish(moved, feed_slot, index, pieces, 1.0 / spectra, out)
     feeds = feed_slot.shape[0]

time: 213 us -> 237 us (1.11)
  waiting for transfers between devices: 97.5 us -> 119 us
  Pallas kernels: 58.2 us -> 60.9 us
    ppermute x24, waiting for transfers between devices: 28 us -> 78.9 us  [swap(): return lax.ppermute(value, 'feed', pairs)]
    all_to_all x2, waiting for transfers between devices: 69.5 us -> 40.3 us  [through_rows(): lax.all_to_all(coded, 'feed', split_axis=0, concat_axis=0, tiled=True)]
    unnamed x24, local copies, waits for them, and re-layouts: 10.1 us -> 6.85 us
  transfers between devices with their start and end apart: 26 -> 26, of which waited for: 15 -> 15; matrix products, arithmetic and copies ran while one was open for 4% -> 4% of each run, Pallas kernels for 16% -> 14%
where the time goes in v10:
time: 237 us; the launch traced here: 236 us
  waiting for transfers between devices  119 us (50%)
  Pallas kernels  60.9 us (26%)
  starting transfers between devices  37 us (16%)
  local copies, waits for them, and re-layouts  10.8 us (5%)
  other arithmetic  7.9 us (3%)
    ppermute x24, waiting for transfers between devices, swap(): return lax.ppermute(value, 'feed', pairs)  78.9 us
    all_to_all x2, waiting for transfers between devices, through_rows(): lax.all_to_all(coded, 'feed', split_axis=0, concat_axis=0, tiled=True)  40.3 us
    pallas_call x2, Pallas kernels, row_products(): pl.pallas_call(rows_kernel, grid=(steps + ch // each,), in_specs=[pl.Bloc...  28.3 us
    ppermute x24, starting transfers between devices, swap(): return lax.ppermute(value, 'feed', pairs)  23.3 us
    pallas_call x2, Pallas kernels, finish(): pl.pallas_call(functools.partial(finish_kernel, scale), grid=(1,), in_spe...  20.1 us
    all_to_all x2, starting transfers between devices, through_rows(): lax.all_to_all(coded, 'feed', split_axis=0, concat_axis=0, tiled=True)  13.7 us
    pallas_call x1, Pallas kernels, own_spectra(): pl.pallas_call(own_kernel, grid=(steps,), in_specs=[pl.BlockSpec((main, c...  9.86 us
    unnamed x24, local copies, waits for them, and re-layouts  6.85 us
  transfers between devices with their start and end apart: 26, of which 15 were waited for; matrix products, arithmetic and copies ran while one was open for 4% of the time, Pallas kernels for 14%

profile of v10, /device:TPU:13, one launch (start us, length us, event | category | flops | bytes accessed | tf_op | source)
XLA Modules:
  0.0 236.2 jit_solution(13429325922938211956)
XLA Ops:
  0.0 0.8 fusion.2
  0.9 0.7 slice_subtract_fusion
  1.6 3.4 %copy-done = s32[256,16,519]{0,1,2:T(8,128)S(1)} copy-done((s32[256,16,519]{0,1,2:T(8,128)S(1)}, s32[256,16,519]{0,1,2:T(8,128)}, u32[]{:S(2)}) %copy-start) | copy-done | bytes 8503320
  5.0 2.6 %select_rows.1 = (bf16[8448,128]{1,0:T(8,128)(2,1)S(1)}, bf16[8448,128]{1,0:T(8,128)(2,1)S(1)}) custom-call(s32[1,256]{1,0:T(1,128)S(1)} %bitcast.19, s32[8304,256]{1,0:T(8,128)S(1)} %bitcast.13, bf16[64,256]{1,0:T(8,128)(2,1)S(1)} %pad_maximum_fusion.2.parts_ref), custom_call_target="tpu_custom_call" | custom-call | tf_op jit(solution)/shard_map/select_rows/pallas_call | solution.py:353
  7.6 1.1 constant_dynamic-slice_fusion.4
  8.7 0.7 collective-permute-start.12
  9.4 0.6 collective-permute-start
  10.0 2.0 collective-permute-done.12
  12.0 1.8 dynamic-slice_add_fusion
  14.4 1.5 dynamic-slice_add_fusion.1
  16.0 1.5 collective-permute-start.6
  17.6 1.3 collective-permute-start.1
  18.9 2.9 %collective-permute-done.13 = bf16[1056,128]{1,0:T(8,128)(2,1)S(1)} collective-permute-done((bf16[1056,128]{1,0:T(8,128)(2,1)S(1)}, bf16[1056,128]{1,0:T(8,128)(2,1)S(1)}, u32[]{:S(2)}, u32[]{:S(2)}) %collective-permute-start.13) | collective-permute-done | bytes 270368 | tf_op jit(solution)/shard_map/ppermute | solution.py:370
  22.2 0.9 collective-permute-start.19
  23.1 4.4 %collective-permute-done.6 = bf16[1056,128]{1,0:T(8,128)(2,1)S(1)} collective-permute-done((bf16[1056,128]{1,0:T(8,128)(2,1)S(1)}, bf16[1056,128]{1,0:T(8,128)(2,1)S(1)}, u32[]{:S(2)}, u32[]{:S(2)}) %collective-permute-start.6) | collective-permute-done | bytes 270368 | tf_op jit(solution)/shard_map/ppermute | solution.py:370
  27.6 1.3 collective-permute-start.7
  29.3 1.1 collective-permute-done.14
  30.5 2.4 %collective-permute-start.15 = (bf16[528,128]{1,0:T(8,128)(2,1)S(1)}, bf16[528,128]{1,0:T(8,128)(2,1)S(1)}, u32[]{:S(2)}, u32[]{:S(2)}) collective-permute-start(bf16[528,128]{1,0:T(8,128)(2,1)S(1)} %dynamic-slice_add_fusion.7.after_ref), channel_id=1, source_target_pairs={{0,8},{1,9},{2,10},{3,11},{4,12},{5,13},{6,14},{7,15},{8,0},{9,1},... | collective-permute-start | bytes 405512 | tf_op jit(solution)/shard_map/ppermute | solution.py:370
  33.0 9.9 %own_spectra.1 = (bf16[16,8,256,128]{3,2,1,0:T(8,128)(2,1)}, bf16[16,128]{1,0:T(8,128)(2,1)S(1)}) custom-call(s32[8304,256]{1,0:T(8,128)S(1)} %bitcast.16, s32[8304,256]{1,0:T(8,128)S(1)} %bitcast.17, f32[32,256]{1,0:T(8,128)S(1)} %bitcast.18, bf16[256,256]{1,0:T(8,128)(2,1)S(1)} %copy-done.6, bf16[528,128]{1,0:T(8,128)(2,1)S(1)} %dynamic-slice_add_fusion.7.after_ref), custom_call_target="tpu_custom_call" | custom-call | flops 4294967296 | bytes 16891904 | tf_op jit(solution)/shard_map/own_spectra/pallas_call | solution.py:295
  43.4 0.5 collective-permute-done.20
  44.0 0.9 collective-permute-start.21
  44.9 0.6 constant_dynamic-update-slice_fusion.9
  45.5 1.2 collective-permute-start.16
  46.7 1.2 collective-permute-done.21
  47.9 0.5 collective-permute-start.22
  48.5 1.2 collective-permute-done.16
  50.2 5.3 %collective-permute-done.22 = bf16[1056,128]{1,0:T(8,128)(2,1)S(1)} collective-permute-done((bf16[1056,128]{1,0:T(8,128)(2,1)S(1)}, bf16[1056,128]{1,0:T(8,128)(2,1)S(1)}, u32[]{:S(2)}, u32[]{:S(2)}) %collective-permute-start.22) | collective-permute-done | bytes 270368 | tf_op jit(solution)/shard_map/ppermute | solution.py:370
  55.9 6.0 %collective-permute-start.23 = (bf16[4224,128]{1,0:T(8,128)(2,1)S(1)}, bf16[4224,128]{1,0:T(8,128)(2,1)S(1)}, u32[]{:S(2)}, u32[]{:S(2)}) collective-permute-start(bf16[4224,128]{1,0:T(8,128)(2,1)S(1)} %get-tuple-element.21), channel_id=1, source_target_pairs={{0,1},{1,0},{2,3},{3,2},{4,5},{5,4},{6,7},{7,6},{8,9},{9,8},{10,11... | collective-permute-start | bytes 3244040 | tf_op jit(solution)/shard_map/ppermute | solution.py:370
  61.9 2.4 %collective-permute-start.8 = (bf16[528,128]{1,0:T(8,128)(2,1)S(1)}, bf16[528,128]{1,0:T(8,128)(2,1)S(1)}, u32[]{:S(2)}, u32[]{:S(2)}) collective-permute-start(bf16[528,128]{1,0:T(8,128)(2,1)S(1)} %dynamic-slice_add_fusion.8), channel_id=1, source_target_pairs={{0,8},{1,9},{2,10},{3,11},{4,12},{5,13},{6,14},{7,15},{8,0},{9,1},... | collective-permute-start | bytes 405512 | tf_op jit(solution)/shard_map/ppermute | solution.py:370
  64.5 8.8 %collective-permute-done.8 = bf16[528,128]{1,0:T(8,128)(2,1)S(1)} collective-permute-done((bf16[528,128]{1,0:T(8,128)(2,1)S(1)}, bf16[528,128]{1,0:T(8,128)(2,1)S(1)}, u32[]{:S(2)}, u32[]{:S(2)}) %collective-permute-start.8) | collective-permute-done | bytes 135200 | tf_op jit(solution)/shard_map/ppermute | solution.py:370
  73.4 2.7 %collective-permute-done.3 = bf16[528,128]{1,0:T(8,128)(2,1)S(1)} collective-permute-done((bf16[528,128]{1,0:T(8,128)(2,1)S(1)}, bf16[528,128]{1,0:T(8,128)(2,1)S(1)}, u32[]{:S(2)}, u32[]{:S(2)}) %collective-permute-start.3) | collective-permute-done | bytes 135200 | tf_op jit(solution)/shard_map/ppermute | solution.py:370
  76.2 0.8 collective-permute-start.4
  77.0 1.1 collective-permute-done.9
  78.1 2.9 %collective-permute-done.4 = bf16[528,128]{1,0:T(8,128)(2,1)S(1)} collective-permute-done((bf16[528,128]{1,0:T(8,128)(2,1)S(1)}, bf16[528,128]{1,0:T(8,128)(2,1)S(1)}, u32[]{:S(2)}, u32[]{:S(2)}) %collective-permute-start.4) | collective-permute-done | bytes 135200 | tf_op jit(solution)/shard_map/ppermute | solution.py:370
  81.2 14.2 %row_products.2.refs_0_ = s16[16,272,256]{2,1,0:T(8,128)(2,1)} custom-call(bf16[8448,128]{1,0:T(8,128)(2,1)S(1)} %constant_dynamic-update-slice_fusion.main_ref.next_ref, bf16[8448,128]{1,0:T(8,128)(2,1)S(1)} %constant_dynamic-update-slice_fusion.main_ref.next_ref, bf16[64,128]{1,0:T(8,128)(2,1)S(1)} %slice.37.parts_ref, bf16[256,256]{1,0:T(8,128)(2,1)S(1)} %copy-done.6, ...), custom_call_target="tpu_custom_call" | custom-call | flops 4294967296 | bytes 12648448 | tf_op jit(solution)/shard_map/row_products/pallas_call | solution.py:452
  95.4 8.0 %all-to-all-start.1 = ((s16[16,272,256]{2,1,0:T(8,128)(2,1)}), s16[16,272,256]{2,1,0:T(8,128)(2,1)}, u32[]{:S(2)}, u32[]{:S(2)}) async-start(s16[16,272,256]{2,1,0:T(8,128)(2,1)} %row_products.2.refs_0_), calls=%async_computation.1 | async-start | bytes 4456448 | tf_op jit(solution)/shard_map/all_to_all | solution.py:566
  103.6 0.7 constant_dynamic-update-slice_fusion.13
  104.5 42.4 %collective-permute-done.10 = bf16[1056,128]{1,0:T(8,128)(2,1)S(1)} collective-permute-done((bf16[1056,128]{1,0:T(8,128)(2,1)S(1)}, bf16[1056,128]{1,0:T(8,128)(2,1)S(1)}, u32[]{:S(2)}, u32[]{:S(2)}) %collective-permute-start.10) | collective-permute-done | bytes 270368 | tf_op jit(solution)/shard_map/ppermute | solution.py:370
  146.9 0.7 constant_dynamic-update-slice_fusion.12
  147.7 1.5 pad_maximum_fusion
  149.1 0.9 collective-permute-start.11
  150.1 2.3 collective-permute-done.11
  152.6 3.4 %copy-done.3 = bf16[16,8,256,128]{3,2,1,0:T(8,128)(2,1)S(1)} copy-done((bf16[16,8,256,128]{3,2,1,0:T(8,128)(2,1)S(1)}, bf16[16,8,256,128]{3,2,1,0:T(8,128)(2,1)}, u32[]{:S(2)}) %copy-start.3) | copy-done | bytes 8388632
  156.0 14.1 %row_products.3 = s16[16,272,256]{2,1,0:T(8,128)(2,1)} custom-call(bf16[8448,128]{1,0:T(8,128)(2,1)S(1)} %constant_dynamic-update-slice_fusion.10.main_ref.next_ref, bf16[8448,128]{1,0:T(8,128)(2,1)S(1)} %constant_dynamic-update-slice_fusion.10.main_ref.next_ref, bf16[64,128]{1,0:T(8,128)(2,1)S(1)} %slice.34.parts_ref, bf16[256,256]{1,0:T(8,128)(2,1)S(1)} %copy-done.6, ...), custom_call_target="tpu_custom_call" | custom-call | flops 4294967296 | bytes 12648448 | tf_op jit(solution)/shard_map/row_products/pallas_call | solution.py:452
  170.1 5.7 %all-to-all-start = ((s16[16,272,256]{2,1,0:T(8,128)(2,1)}), s16[16,272,256]{2,1,0:T(8,128)(2,1)}, u32[]{:S(2)}, u32[]{:S(2)}) async-start(s16[16,272,256]{2,1,0:T(8,128)(2,1)} %row_products.3), calls=%async_computation | async-start | bytes 4456448 | tf_op jit(solution)/shard_map/all_to_all | solution.py:566
  175.9 10.1 %finish.2.refs_0_ = f32[16384,128]{1,0:T(8,128)} custom-call(s32[4096]{0:T(1024)S(1)} %copy-done.7, s16[16,272,256]{2,1,0:T(8,128)(2,1)} %all-to-all-done.1.coded_ref), custom_call_target="tpu_custom_call" | custom-call | tf_op jit(solution)/shard_map/finish/pallas_call | solution.py:518
  185.9 40.3 %all-to-all-done.coded_ref = s16[16,272,256]{2,1,0:T(8,128)(2,1)} async-done(((s16[16,272,256]{2,1,0:T(8,128)(2,1)}), s16[16,272,256]{2,1,0:T(8,128)(2,1)}, u32[]{:S(2)}, u32[]{:S(2)}) %all-to-all-start) | async-done | bytes 2228256 | tf_op jit(solution)/shard_map/all_to_all | solution.py:566
  226.2 10.1 %finish.3 = f32[16384,128]{1,0:T(8,128)} custom-call(s32[4096]{0:T(1024)S(1)} %copy-done.7, s16[16,272,256]{2,1,0:T(8,128)(2,1)} %all-to-all-done.coded_ref, f32[16384,128]{1,0:T(8,128)} %finish.2.refs_0_), custom_call_target="tpu_custom_call", output_to_operand_aliasing={{}: (2, {})} | custom-call | tf_op jit(solution)/shard_map/finish/pallas_call | solution.py:518
  (83 shorter events, 4.4 us)
Async XLA Ops:
  1.6 3.4 %copy-start = (s32[256,16,519]{0,1,2:T(8,128)S(1)}, s32[256,16,519]{0,1,2:T(8,128)}, u32[]{:S(2)}) copy-start(s32[256,16,519]{0,1,2:T(8,128)} %param.4) | copy-start | bytes 25509892
  7.6 1.8 copy-start.4
  7.6 25.4 %slice-start = ((s8[8503296]{0:T(1024)(128)(4,1)}), s8[114688]{0:T(1024)(128)(4,1)S(1)}, s32[]{:S(2)}) async-start(s8[8503296]{0:T(1024)(128)(4,1)} %bitcast.14), calls=%async_computation.2 | async-start | bytes 229376
  8.7 3.3 %collective-permute-start.12 = (bf16[4224,128]{1,0:T(8,128)(2,1)}, bf16[4224,128]{1,0:T(8,128)(2,1)}, u32[]{:S(2)}, u32[]{:S(2)}) collective-permute-start(bf16[4224,128]{1,0:T(8,128)(2,1)} %constant_dynamic-slice_fusion.4), channel_id=1, source_target_pairs={{0,1},{1,0},{2,3},{3,2},{4,5},{5,4},{6,7},{7,6},{8,9},{9,8},{10,11... | collective-permute-start | bytes 3244040 | tf_op jit(solution)/shard_map/ppermute | solution.py:370
  9.4 4.9 %collective-permute-start = (bf16[4224,128]{1,0:T(8,128)(2,1)S(1)}, bf16[4224,128]{1,0:T(8,128)(2,1)}, u32[]{:S(2)}, u32[]{:S(2)}) collective-permute-start(bf16[4224,128]{1,0:T(8,128)(2,1)S(1)} %constant_dynamic-slice_fusion.9), channel_id=1, source_target_pairs={{0,1},{1,0},{2,3},{3,2},{4,5},{5,4},{6,7},{7,6},{8,9},{9,8},{10,11... | collective-permute-start | bytes 3244040 | tf_op jit(solution)/shard_map/ppermute | solution.py:370
  10.0 23.0 %slice-start.1 = ((s8[8503296]{0:T(1024)(128)(4,1)}), s8[4194304]{0:T(1024)(128)(4,1)S(1)}, s32[]{:S(2)}) async-start(s8[8503296]{0:T(1024)(128)(4,1)} %bitcast.14), calls=%async_computation.3 | async-start | bytes 8388608
  14.0 7.8 %collective-permute-start.13 = (bf16[1056,128]{1,0:T(8,128)(2,1)S(1)}, bf16[1056,128]{1,0:T(8,128)(2,1)S(1)}, u32[]{:S(2)}, u32[]{:S(2)}) collective-permute-start(bf16[1056,128]{1,0:T(8,128)(2,1)S(1)} %constant_dynamic-slice_fusion.3), channel_id=1, source_target_pairs={{0,2},{1,3},{2,0},{3,1},{4,6},{5,7},{6,4},{7,5},{8,10},{9,11},{10,... | collective-permute-start | bytes 811016 | tf_op jit(solution)/shard_map/ppermute | solution.py:370
  14.3 7.8 %collective-permute-start.18 = (bf16[1056,128]{1,0:T(8,128)(2,1)S(1)}, bf16[1056,128]{1,0:T(8,128)(2,1)S(1)}, u32[]{:S(2)}, u32[]{:S(2)}) collective-permute-start(bf16[1056,128]{1,0:T(8,128)(2,1)S(1)} %constant_dynamic-slice_fusion.1), channel_id=1, source_target_pairs={{0,4},{1,5},{2,6},{3,7},{4,0},{5,1},{6,2},{7,3},{8,12},{9,13},{10,... | collective-permute-start | bytes 811016 | tf_op jit(solution)/shard_map/ppermute | solution.py:370
  15.9 17.1 %slice-start.2 = ((s8[8503296]{0:T(1024)(128)(4,1)}), s8[4194304]{0:T(1024)(128)(4,1)S(1)}, s32[]{:S(2)}) async-start(s8[8503296]{0:T(1024)(128)(4,1)} %bitcast.14), calls=%async_computation.4 | async-start | bytes 8388608
  16.0 11.6 %copy-start.8 = (bf16[2112,128]{1,0:T(8,128)(2,1)}, bf16[2112,128]{1,0:T(8,128)(2,1)S(1)}, u32[]{:S(2)}) copy-start(bf16[2112,128]{1,0:T(8,128)(2,1)S(1)} %get-tuple-element.28) | copy-start | bytes 1622020
  16.0 11.5 %collective-permute-start.6 = (bf16[1056,128]{1,0:T(8,128)(2,1)S(1)}, bf16[1056,128]{1,0:T(8,128)(2,1)S(1)}, u32[]{:S(2)}, u32[]{:S(2)}) collective-permute-start(bf16[1056,128]{1,0:T(8,128)(2,1)S(1)} %constant_dynamic-slice_fusion.6), channel_id=1, source_target_pairs={{0,4},{1,5},{2,6},{3,7},{4,0},{5,1},{6,2},{7,3},{8,12},{9,13},{10,... | collective-permute-start | bytes 811016 | tf_op jit(solution)/shard_map/ppermute | solution.py:370
  17.6 11.4 %collective-permute-start.1 = (bf16[1056,128]{1,0:T(8,128)(2,1)S(1)}, bf16[1056,128]{1,0:T(8,128)(2,1)S(1)}, u32[]{:S(2)}, u32[]{:S(2)}) collective-permute-start(bf16[1056,128]{1,0:T(8,128)(2,1)S(1)} %constant_dynamic-slice_fusion.8), channel_id=1, source_target_pairs={{0,2},{1,3},{2,0},{3,1},{4,6},{5,7},{6,4},{7,5},{8,10},{9,11},{10,... | collective-permute-start | bytes 811016 | tf_op jit(solution)/shard_map/ppermute | solution.py:370
  21.8 11.2 %copy-start.6 = (bf16[256,256]{1,0:T(8,128)(2,1)S(1)}, bf16[256,256]{1,0:T(8,128)(2,1)}, u32[]{:S(2)}) copy-start(bf16[256,256]{1,0:T(8,128)(2,1)} %constant.222.clone.weights_ref) | copy-start | bytes 393220
  21.9 8.6 %collective-permute-start.14 = (bf16[528,128]{1,0:T(8,128)(2,1)S(1)}, bf16[528,128]{1,0:T(8,128)(2,1)S(1)}, u32[]{:S(2)}, u32[]{:S(2)}) collective-permute-start(bf16[528,128]{1,0:T(8,128)(2,1)S(1)} %constant_dynamic-slice_fusion.2), channel_id=1, source_target_pairs={{0,4},{1,5},{2,6},{3,7},{4,0},{5,1},{6,2},{7,3},{8,12},{9,13},{10,... | collective-permute-start | bytes 405512 | tf_op jit(solution)/shard_map/ppermute | solution.py:370
  22.2 10.6 %collective-permute-start.19 = (bf16[528,128]{1,0:T(8,128)(2,1)S(1)}, bf16[528,128]{1,0:T(8,128)(2,1)S(1)}, u32[]{:S(2)}, u32[]{:S(2)}) collective-permute-start(bf16[528,128]{1,0:T(8,128)(2,1)S(1)} %constant_dynamic-slice_fusion), channel_id=1, source_target_pairs={{0,2},{1,3},{2,0},{3,1},{4,6},{5,7},{6,4},{7,5},{8,10},{9,11},{10,... | collective-permute-start | bytes 405512 | tf_op jit(solution)/shard_map/ppermute | solution.py:370
  27.6 34.2 %collective-permute-start.7 = (bf16[528,128]{1,0:T(8,128)(2,1)S(1)}, bf16[528,128]{1,0:T(8,128)(2,1)S(1)}, u32[]{:S(2)}, u32[]{:S(2)}) collective-permute-start(bf16[528,128]{1,0:T(8,128)(2,1)S(1)} %constant_dynamic-slice_fusion.5), channel_id=1, source_target_pairs={{0,2},{1,3},{2,0},{3,1},{4,6},{5,7},{6,4},{7,5},{8,10},{9,11},{10,... | collective-permute-start | bytes 405512 | tf_op jit(solution)/shard_map/ppermute | solution.py:370
  29.1 35.2 %collective-permute-start.2 = (bf16[528,128]{1,0:T(8,128)(2,1)S(1)}, bf16[528,128]{1,0:T(8,128)(2,1)S(1)}, u32[]{:S(2)}, u32[]{:S(2)}) collective-permute-start(bf16[528,128]{1,0:T(8,128)(2,1)S(1)} %constant_dynamic-slice_fusion.7), channel_id=1, source_target_pairs={{0,4},{1,5},{2,6},{3,7},{4,0},{5,1},{6,2},{7,3},{8,12},{9,13},{10,... | collective-permute-start | bytes 405512 | tf_op jit(solution)/shard_map/ppermute | solution.py:370
  30.5 14.4 %collective-permute-start.15 = (bf16[528,128]{1,0:T(8,128)(2,1)S(1)}, bf16[528,128]{1,0:T(8,128)(2,1)S(1)}, u32[]{:S(2)}, u32[]{:S(2)}) collective-permute-start(bf16[528,128]{1,0:T(8,128)(2,1)S(1)} %dynamic-slice_add_fusion.7.after_ref), channel_id=1, source_target_pairs={{0,8},{1,9},{2,10},{3,11},{4,12},{5,13},{6,14},{7,15},{8,0},{9,1},... | collective-permute-start | bytes 405512 | tf_op jit(solution)/shard_map/ppermute | solution.py:370
  32.9 11.0 %collective-permute-start.20 = (bf16[528,128]{1,0:T(8,128)(2,1)S(1)}, bf16[528,128]{1,0:T(8,128)(2,1)S(1)}, u32[]{:S(2)}, u32[]{:S(2)}) collective-permute-start(bf16[528,128]{1,0:T(8,128)(2,1)S(1)} %dynamic-slice_add_fusion.6), channel_id=1, source_target_pairs={{0,8},{1,9},{2,10},{3,11},{4,12},{5,13},{6,14},{7,15},{8,0},{9,1},... | collective-permute-start | bytes 405512 | tf_op jit(solution)/shard_map/ppermute | solution.py:370
  42.9 12.7 %copy-start.5 = (bf16[8448,128]{1,0:T(8,128)(2,1)S(1)}, bf16[8448,128]{1,0:T(8,128)(2,1)}, u32[]{:S(2)}) copy-start(bf16[8448,128]{1,0:T(8,128)(2,1)} %copy-done.4) | copy-start | bytes 6488068
  44.0 3.9 %collective-permute-start.21 = (bf16[528,128]{1,0:T(8,128)(2,1)S(1)}, bf16[528,128]{1,0:T(8,128)(2,1)S(1)}, u32[]{:S(2)}, u32[]{:S(2)}) collective-permute-start(bf16[528,128]{1,0:T(8,128)(2,1)S(1)} %get-tuple-element.16), channel_id=1, source_target_pairs={{0,2},{1,3},{2,0},{3,1},{4,6},{5,7},{6,4},{7,5},{8,10},{9,11},{10,... | collective-permute-start | bytes 405512 | tf_op jit(solution)/shard_map/ppermute | solution.py:370
  45.5 4.2 %collective-permute-start.16 = (bf16[528,128]{1,0:T(8,128)(2,1)S(1)}, bf16[528,128]{1,0:T(8,128)(2,1)S(1)}, u32[]{:S(2)}, u32[]{:S(2)}) collective-permute-start(bf16[528,128]{1,0:T(8,128)(2,1)S(1)} %get-tuple-element.14), channel_id=1, source_target_pairs={{0,4},{1,5},{2,6},{3,7},{4,0},{5,1},{6,2},{7,3},{8,12},{9,13},{10,... | collective-permute-start | bytes 405512 | tf_op jit(solution)/shard_map/ppermute | solution.py:370
  47.9 7.6 %collective-permute-start.22 = (bf16[1056,128]{1,0:T(8,128)(2,1)S(1)}, bf16[1056,128]{1,0:T(8,128)(2,1)S(1)}, u32[]{:S(2)}, u32[]{:S(2)}) collective-permute-start(bf16[1056,128]{1,0:T(8,128)(2,1)S(1)} %constant_dynamic-update-slice_fusion.4), channel_id=1, source_target_pairs={{0,4},{1,5},{2,6},{3,7},{4,0},{5,1},{6,2},{7,3},{8,12},{9,13},{10,... | collective-permute-start | bytes 811016 | tf_op jit(solution)/shard_map/ppermute | solution.py:370
  49.7 5.8 %collective-permute-start.17 = (bf16[1056,128]{1,0:T(8,128)(2,1)S(1)}, bf16[1056,128]{1,0:T(8,128)(2,1)S(1)}, u32[]{:S(2)}, u32[]{:S(2)}) collective-permute-start(bf16[1056,128]{1,0:T(8,128)(2,1)S(1)} %constant_dynamic-update-slice_fusion.8), channel_id=1, source_target_pairs={{0,2},{1,3},{2,0},{3,1},{4,6},{5,7},{6,4},{7,5},{8,10},{9,11},{10,... | collective-permute-start | bytes 811016 | tf_op jit(solution)/shard_map/ppermute | solution.py:370
  55.6 25.6 %copy-start.2 = (bf16[16,8,256,128]{3,2,1,0:T(8,128)(2,1)S(1)}, bf16[16,8,256,128]{3,2,1,0:T(8,128)(2,1)}, u32[]{:S(2)}) copy-start(bf16[16,8,256,128]{3,2,1,0:T(8,128)(2,1)} %get-tuple-element.11.own_ref) | copy-start | bytes 25165828
  55.9 25.1 %collective-permute-start.23 = (bf16[4224,128]{1,0:T(8,128)(2,1)S(1)}, bf16[4224,128]{1,0:T(8,128)(2,1)S(1)}, u32[]{:S(2)}, u32[]{:S(2)}) collective-permute-start(bf16[4224,128]{1,0:T(8,128)(2,1)S(1)} %get-tuple-element.21), channel_id=1, source_target_pairs={{0,1},{1,0},{2,3},{3,2},{4,5},{5,4},{6,7},{7,6},{8,9},{9,8},{10,11... | collective-permute-start | bytes 3244040 | tf_op jit(solution)/shard_map/ppermute | solution.py:370
  61.9 11.3 %collective-permute-start.8 = (bf16[528,128]{1,0:T(8,128)(2,1)S(1)}, bf16[528,128]{1,0:T(8,128)(2,1)S(1)}, u32[]{:S(2)}, u32[]{:S(2)}) collective-permute-start(bf16[528,128]{1,0:T(8,128)(2,1)S(1)} %dynamic-slice_add_fusion.8), channel_id=1, source_target_pairs={{0,8},{1,9},{2,10},{3,11},{4,12},{5,13},{6,14},{7,15},{8,0},{9,1},... | collective-permute-start | bytes 405512 | tf_op jit(solution)/shard_map/ppermute | solution.py:370
  64.3 11.8 %collective-permute-start.3 = (bf16[528,128]{1,0:T(8,128)(2,1)S(1)}, bf16[528,128]{1,0:T(8,128)(2,1)S(1)}, u32[]{:S(2)}, u32[]{:S(2)}) collective-permute-start(bf16[528,128]{1,0:T(8,128)(2,1)S(1)} %dynamic-slice_add_fusion.9), channel_id=1, source_target_pairs={{0,8},{1,9},{2,10},{3,11},{4,12},{5,13},{6,14},{7,15},{8,0},{9,1},... | collective-permute-start | bytes 405512 | tf_op jit(solution)/shard_map/ppermute | solution.py:370
  73.3 4.7 %collective-permute-start.9 = (bf16[528,128]{1,0:T(8,128)(2,1)S(1)}, bf16[528,128]{1,0:T(8,128)(2,1)S(1)}, u32[]{:S(2)}, u32[]{:S(2)}) collective-permute-start(bf16[528,128]{1,0:T(8,128)(2,1)S(1)} %get-tuple-element.20), channel_id=1, source_target_pairs={{0,2},{1,3},{2,0},{3,1},{4,6},{5,7},{6,4},{7,5},{8,10},{9,11},{10,... | collective-permute-start | bytes 405512 | tf_op jit(solution)/shard_map/ppermute | solution.py:370
  76.2 4.8 %collective-permute-start.4 = (bf16[528,128]{1,0:T(8,128)(2,1)S(1)}, bf16[528,128]{1,0:T(8,128)(2,1)S(1)}, u32[]{:S(2)}, u32[]{:S(2)}) collective-permute-start(bf16[528,128]{1,0:T(8,128)(2,1)S(1)} %get-tuple-element.18), channel_id=1, source_target_pairs={{0,4},{1,5},{2,6},{3,7},{4,0},{5,1},{6,2},{7,3},{8,12},{9,13},{10,... | collective-permute-start | bytes 405512 | tf_op jit(solution)/shard_map/ppermute | solution.py:370
  95.4 74.8 %all-to-all-start.1 = ((s16[16,272,256]{2,1,0:T(8,128)(2,1)}), s16[16,272,256]{2,1,0:T(8,128)(2,1)}, u32[]{:S(2)}, u32[]{:S(2)}) async-start(s16[16,272,256]{2,1,0:T(8,128)(2,1)} %row_products.2.refs_0_), calls=%async_computation.1 | async-start | bytes 4456448 | tf_op jit(solution)/shard_map/all_to_all | solution.py:566
  103.4 43.5 %collective-permute-start.10 = (bf16[1056,128]{1,0:T(8,128)(2,1)S(1)}, bf16[1056,128]{1,0:T(8,128)(2,1)S(1)}, u32[]{:S(2)}, u32[]{:S(2)}) collective-permute-start(bf16[1056,128]{1,0:T(8,128)(2,1)S(1)} %constant_dynamic-update-slice_fusion.14.refs_1_), channel_id=1, source_target_pairs={{0,4},{1,5},{2,6},{3,7},{4,0},{5,1},{6,2},{7,3},{8,12},{9,13},{10,... | collective-permute-start | bytes 811016 | tf_op jit(solution)/shard_map/ppermute | solution.py:370
  104.4 43.2 %collective-permute-start.5 = (bf16[1056,128]{1,0:T(8,128)(2,1)S(1)}, bf16[1056,128]{1,0:T(8,128)(2,1)S(1)}, u32[]{:S(2)}, u32[]{:S(2)}) collective-permute-start(bf16[1056,128]{1,0:T(8,128)(2,1)S(1)} %constant_dynamic-update-slice_fusion.18.refs_0_), channel_id=1, source_target_pairs={{0,2},{1,3},{2,0},{3,1},{4,6},{5,7},{6,4},{7,5},{8,10},{9,11},{10,... | collective-permute-start | bytes 811016 | tf_op jit(solution)/shard_map/ppermute | solution.py:370
  147.6 4.9 %copy-start.1 = (s16[16,272,256]{2,1,0:T(8,128)(2,1)S(1)}, s16[16,272,256]{2,1,0:T(8,128)(2,1)}, u32[]{:S(2)}) copy-start(s16[16,272,256]{2,1,0:T(8,128)(2,1)} %row_products.2.refs_0_) | copy-start | bytes 6684676
  149.1 3.3 %collective-permute-start.11 = (bf16[4224,128]{1,0:T(8,128)(2,1)S(1)}, bf16[4224,128]{1,0:T(8,128)(2,1)S(1)}, u32[]{:S(2)}, u32[]{:S(2)}) collective-permute-start(bf16[4224,128]{1,0:T(8,128)(2,1)S(1)} %get-tuple-element.25), channel_id=1, source_target_pairs={{0,1},{1,0},{2,3},{3,2},{4,5},{5,4},{6,7},{7,6},{8,9},{9,8},{10,11... | collective-permute-start | bytes 3244040 | tf_op jit(solution)/shard_map/ppermute | solution.py:370
  152.6 3.4 %copy-start.3 = (bf16[16,8,256,128]{3,2,1,0:T(8,128)(2,1)S(1)}, bf16[16,8,256,128]{3,2,1,0:T(8,128)(2,1)}, u32[]{:S(2)}) copy-start(bf16[16,8,256,128]{3,2,1,0:T(8,128)(2,1)} %get-tuple-element.11.own_ref) | copy-start | bytes 25165828
  170.1 5.8 %copy-start.7 = (s32[4096]{0:T(1024)S(1)}, s32[4096]{0:T(1024)}, u32[]{:S(2)}) copy-start(s32[4096]{0:T(1024)} %slot_ref.3) | copy-start | bytes 49156
  170.1 56.1 %all-to-all-start = ((s16[16,272,256]{2,1,0:T(8,128)(2,1)}), s16[16,272,256]{2,1,0:T(8,128)(2,1)}, u32[]{:S(2)}, u32[]{:S(2)}) async-start(s16[16,272,256]{2,1,0:T(8,128)(2,1)} %row_products.3), calls=%async_computation | async-start | bytes 4456448 | tf_op jit(solution)/shard_map/all_to_all | solution.py:566

commit v11 on v10

--- a/solution.py
+++ b/solution.py
@@ -259,33 +259,18 @@
     ]
 
 
-def own_kernel(main_ref, next_ref, gains_ref, weights_ref, after_ref, out_ref, zero_ref, held, turned, sems):
+def own_kernel(main_ref, next_ref, gains_ref, weights_ref, after_ref, out_ref, zero_ref, held):
     step = pl.program_id(0)
-    slot = step % 2
     ch = out_ref.shape[0]
     zero_ref[...] = jnp.zeros_like(zero_ref)
     words = jnp.concatenate([main_ref[...], next_ref[...]], axis=0)
 
-    def copy(index):
-        return pltpu.make_async_copy(turned.at[index % 2], out_ref.at[:, index], sems.at[index % 2])
-
     def store(b, c, real, imag):
         held[c, b * 2 * STEP : (b + 1) * 2 * STEP, :] = jnp.concatenate([real, imag], axis=0).astype(held.dtype)
 
     spectra_of(weights_ref, levels_of(words), gains_ref[...], ch, store)
-
-    @pl.when(step >= 2)
-    def _():
-        copy(step - 2).wait()
-
     for c in range(ch):
-        turned[slot, c] = held[c].T
-    copy(step).start()
-
-    @pl.when(step == pl.num_programs(0) - 1)
-    def _():
-        copy(step - 1).wait()
-        copy(step).wait()
+        out_ref[c, step] = held[c].T
 
 
 def own_spectra(words, gains, weights, ch, spectra, after):
@@ -303,17 +288,15 @@
             pl.BlockSpec(memory_space=pl.ANY),
         ],
         out_specs=[
-            pl.BlockSpec(memory_space=pltpu.HBM),
+            pl.BlockSpec(memory_space=pltpu.VMEM),
             pl.BlockSpec((16, LANES), lambda i: (0, 0)),
         ],
         out_shape=[
-            pltpu.HBM((ch, steps, count, 2 * STEPS * STEP), jnp.bfloat16),
+            jax.ShapeDtypeStruct((ch, steps, count, 2 * STEPS * STEP), jnp.bfloat16),
             jax.ShapeDtypeStruct((16, LANES), jnp.bfloat16),
         ],
         scratch_shapes=[
             pltpu.VMEM((ch, 2 * STEPS * STEP, count), jnp.bfloat16),
-            pltpu.VMEM((2, ch, count, 2 * STEPS * STEP), jnp.bfloat16),
-            pltpu.SemaphoreType.DMA((2,)),
         ],
         compiler_params=pltpu.CompilerParams(vmem_limit_bytes=12 << 20),
         cost_estimate=pl.CostEstimate(
@@ -400,22 +383,18 @@
     left_1, right_1 = gather_half(left_3, 4, left_1), gather_half(right_3, 2, right_1)
     left, right = gather_half(left_1, 2, left), gather_half(right_1, 4, right)
     half = jnp.concatenate([left, right], axis=0)
-    return (left_1, right_1), lambda: gather_half(half, 1, value)
+    return half, lambda: gather_half(half, 1, value)
 
 
 def rows_kernel(main_ref, next_ref, parts_ref, weights_ref, own_ref, *refs):
-    out_ref, left, own, sems = refs[-4:]
+    out_ref, done_ref, left = refs[-3:]
     step = pl.program_id(0)
-    ch, steps = own.shape[:2]
+    done_ref[...] = jnp.zeros_like(done_ref)
+    ch, steps = own_ref.shape[:2]
     rows = main_ref.shape[1]
-
-    def copy(c):
-        return pltpu.make_async_copy(own_ref.at[c], own.at[c], sems.at[c])
 
     @pl.when(step < steps)
     def _():
-        for index in range(ch // steps):
-            copy(step * (ch // steps) + index).start()
         words = jnp.concatenate([main_ref[...], next_ref[...]], axis=0).astype(jnp.float32).astype(jnp.int32)
         parts = parts_ref[...].astype(jnp.float32)
         gains = parts[: 2 * ch] * 16.0 + parts[2 * ch :]
@@ -432,8 +411,7 @@
         each = out_ref.shape[0]
         for index in range(each):
             c = (step - steps) * each + index
-            copy(c).wait()
-            spectra = jnp.concatenate([own[c, part] for part in range(own.shape[1])], axis=1)
+            spectra = jnp.concatenate([own_ref[c, part] for part in range(steps)], axis=1)
             products = jnp.dot(spectra, left[c], preferred_element_type=jnp.float32)
             count = products.shape[0]
             largest = jnp.maximum(jnp.max(jnp.abs(products), axis=0, keepdims=True), 2.0**-60)
@@ -457,17 +435,21 @@
             pl.BlockSpec((STEP * ch, rows), lambda i: ((jnp.minimum(i, steps - 1) + 1) * STEPS, 0)),
             pl.BlockSpec(parts.shape, lambda i: (0, 0)),
             pl.BlockSpec(weights.shape, lambda i: (0, 0)),
-            pl.BlockSpec(memory_space=pltpu.HBM),
+            pl.BlockSpec(memory_space=pltpu.VMEM),
         ]
         + [pl.BlockSpec(memory_space=pl.ANY)] * len(after),
-        out_specs=pl.BlockSpec((each, count + 16, 2 * rows), lambda i: (jnp.maximum(i - steps, 0), 0, 0)),
-        out_shape=pltpu.HBM((ch, count + 16, 2 * rows), jnp.int16),
+        out_specs=[
+            pl.BlockSpec((each, count + 16, 2 * rows), lambda i: (jnp.maximum(i - steps, 0), 0, 0)),
+            pl.BlockSpec((16, LANES), lambda i: (0, 0)),
+        ],
+        out_shape=[
+            pltpu.HBM((ch, count + 16, 2 * rows), jnp.int16),
+            jax.ShapeDtypeStruct((16, LANES), jnp.bfloat16),
+        ],
         scratch_shapes=[
             pltpu.VMEM((ch, steps * width, 2 * rows), jnp.bfloat16),
-            pltpu.VMEM(own.shape, jnp.bfloat16),
-            pltpu.SemaphoreType.DMA((ch,)),
-        ],
-        compiler_params=pltpu.CompilerParams(vmem_limit_bytes=24 << 20),
+        ],
+        compiler_params=pltpu.CompilerParams(vmem_limit_bytes=18 << 20),
         cost_estimate=pl.CostEstimate(
             flops=4 * steps * width * ch * SPAN * ch * rows + 4 * ch * steps * width * rows * count,
             bytes_accessed=2 * words.size + 2 * own.size + 4 * ch * rows * count,
@@ -557,12 +539,12 @@
 
     sums = [sum_over_feed(value, None if index else work) for index, value in enumerate(picked)]
     own = held[0]
-    out, after = None, sums[-1][0]
+    out, after = None, [sums[-1][0]]
     for index in range(pieces):
         rows = sums[index][1]()
         parts = rows[lines : lines + 4 * ch]
-        coded = row_products(rows, parts, own, weights, after)
-        after = [coded]
+        coded, done = row_products(rows, parts, own, weights, after)
+        after = [done]
         moved = lax.all_to_all(coded, "feed", split_axis=0, concat_axis=0, tiled=True)
         out = finish(moved, feed_slot, index, pieces, 1.0 / spectra, out)
     feeds = feed_slot.shape[0]

time: 237 us -> 209 us (0.88)
  waiting for transfers between devices: 119 us -> 101 us
  Pallas kernels: 60.9 us -> 49.2 us
  local copies, waits for them, and re-layouts: 10.8 us -> 13.3 us
    ppermute x24, waiting for transfers between devices: 78.9 us -> 28.6 us  [swap(): return lax.ppermute(value, 'feed', pairs)]
    all_to_all x2, waiting for transfers between devices: 40.3 us -> 72.8 us  [through_rows(): lax.all_to_all(coded, 'feed', split_axis=0, concat_axis=0, tiled=True)]
    pallas_call x2, Pallas kernels: 28.3 us -> 18.2 us  [row_products(): pl.pallas_call(rows_kernel, grid=(steps + ch // each,), in_specs=[pl.Bloc...]
  transfers between devices with their start and end apart: 26 -> 26, of which waited for: 15 -> 15; matrix products, arithmetic and copies ran while one was open for 4% -> 5% of each run, Pallas kernels for 14% -> 13%
where the time goes in v11:
time: 209 us; the launch traced here: 208 us
  waiting for transfers between devices  101 us (48%)
  Pallas kernels  49.2 us (24%)
  starting transfers between devices  36.9 us (18%)
  local copies, waits for them, and re-layouts  13.3 us (6%)
  other arithmetic  6.96 us (3%)
    all_to_all x2, waiting for transfers between devices, through_rows(): lax.all_to_all(coded, 'feed', split_axis=0, concat_axis=0, tiled=True)  72.8 us
    ppermute x24, waiting for transfers between devices, swap(): return lax.ppermute(value, 'feed', pairs)  28.6 us
    ppermute x24, starting transfers between devices, swap(): return lax.ppermute(value, 'feed', pairs)  24.8 us
    pallas_call x2, Pallas kernels, finish(): pl.pallas_call(functools.partial(finish_kernel, scale), grid=(1,), in_spe...  19.3 us
    pallas_call x2, Pallas kernels, row_products(): pl.pallas_call(rows_kernel, grid=(steps + ch // each,), in_specs=[pl.Bloc...  18.2 us
    all_to_all x2, starting transfers between devices, through_rows(): lax.all_to_all(coded, 'feed', split_axis=0, concat_axis=0, tiled=True)  12.1 us
    pallas_call x1, Pallas kernels, own_spectra(): pl.pallas_call(own_kernel, grid=(steps,), in_specs=[pl.BlockSpec((main, c...  9.05 us
    unnamed x24, local copies, waits for them, and re-layouts  9 us
  transfers between devices with their start and end apart: 26, of which 15 were waited for; matrix products, arithmetic and copies ran while one was open for 5% of the time, Pallas kernels for 13%

profile of v11, /device:TPU:13, one launch (start us, length us, event | category | flops | bytes accessed | tf_op | source)
XLA Modules:
  0.0 208.0 jit_solution(4598891505724659889)
XLA Ops:
  0.0 0.8 fusion.2
  0.9 0.7 slice_subtract_fusion
  1.6 3.4 %copy-done = s32[256,16,519]{0,1,2:T(8,128)S(1)} copy-done((s32[256,16,519]{0,1,2:T(8,128)S(1)}, s32[256,16,519]{0,1,2:T(8,128)}, u32[]{:S(2)}) %copy-start) | copy-done | bytes 8503320
  5.0 2.6 %select_rows.1 = (bf16[8448,128]{1,0:T(8,128)(2,1)S(1)}, bf16[8448,128]{1,0:T(8,128)(2,1)S(1)}) custom-call(s32[1,256]{1,0:T(1,128)S(1)} %bitcast.19, s32[8304,256]{1,0:T(8,128)S(1)} %bitcast.13, bf16[64,256]{1,0:T(8,128)(2,1)S(1)} %pad_maximum_fusion.2.parts_ref), custom_call_target="tpu_custom_call" | custom-call | tf_op jit(solution)/shard_map/select_rows/pallas_call | solution.py:336
  7.7 0.7 collective-permute-start.12
  9.0 1.1 constant_dynamic-slice_fusion.9
  10.0 0.7 collective-permute-start
  10.9 1.8 dynamic-slice_add_fusion
  13.4 1.8 dynamic-slice_add_fusion.1
  15.3 1.1 collective-permute-start.6
  16.4 1.3 collective-permute-start.1
  17.8 2.9 %collective-permute-done.13 = bf16[1056,128]{1,0:T(8,128)(2,1)S(1)} collective-permute-done((bf16[1056,128]{1,0:T(8,128)(2,1)S(1)}, bf16[1056,128]{1,0:T(8,128)(2,1)S(1)}, u32[]{:S(2)}, u32[]{:S(2)}) %collective-permute-start.13) | collective-permute-done | bytes 270368 | tf_op jit(solution)/shard_map/ppermute | solution.py:353
  21.1 0.9 collective-permute-start.19
  22.0 4.4 %collective-permute-done.6 = bf16[1056,128]{1,0:T(8,128)(2,1)S(1)} collective-permute-done((bf16[1056,128]{1,0:T(8,128)(2,1)S(1)}, bf16[1056,128]{1,0:T(8,128)(2,1)S(1)}, u32[]{:S(2)}, u32[]{:S(2)}) %collective-permute-start.6) | collective-permute-done | bytes 270368 | tf_op jit(solution)/shard_map/ppermute | solution.py:353
  26.5 1.3 collective-permute-start.7
  28.2 1.1 collective-permute-done.14
  29.3 2.4 %collective-permute-start.15 = (bf16[528,128]{1,0:T(8,128)(2,1)S(1)}, bf16[528,128]{1,0:T(8,128)(2,1)S(1)}, u32[]{:S(2)}, u32[]{:S(2)}) collective-permute-start(bf16[528,128]{1,0:T(8,128)(2,1)S(1)} %dynamic-slice_add_fusion.7.after_ref), channel_id=1, source_target_pairs={{0,8},{1,9},{2,10},{3,11},{4,12},{5,13},{6,14},{7,15},{8,0},{9,1},... | collective-permute-start | bytes 405512 | tf_op jit(solution)/shard_map/ppermute | solution.py:353
  31.9 2.4 %collective-permute-start.8 = (bf16[528,128]{1,0:T(8,128)(2,1)S(1)}, bf16[528,128]{1,0:T(8,128)(2,1)S(1)}, u32[]{:S(2)}, u32[]{:S(2)}) collective-permute-start(bf16[528,128]{1,0:T(8,128)(2,1)S(1)} %dynamic-slice_add_fusion.8), channel_id=1, source_target_pairs={{0,8},{1,9},{2,10},{3,11},{4,12},{5,13},{6,14},{7,15},{8,0},{9,1},... | collective-permute-start | bytes 405512 | tf_op jit(solution)/shard_map/ppermute | solution.py:353
  34.5 9.1 %own_spectra.1 = (bf16[16,8,256,128]{3,2,1,0:T(8,128)(2,1)S(1)}, bf16[16,128]{1,0:T(8,128)(2,1)S(1)}) custom-call(s32[8304,256]{1,0:T(8,128)S(1)} %bitcast.16, s32[8304,256]{1,0:T(8,128)S(1)} %bitcast.17, f32[32,256]{1,0:T(8,128)S(1)} %bitcast.18, bf16[256,256]{1,0:T(8,128)(2,1)S(1)} %copy-done.5, bf16[528,128]{1,0:T(8,128)(2,1)S(1)} %dynamic-slice_add_fusion.7.after_ref), custom_call_target="tpu_custom_call" | custom-call | flops 4294967296 | bytes 16891904 | tf_op jit(solution)/shard_map/own_spectra/pallas_call | solution.py:280
  43.6 0.6 slice.29
  44.1 4.4 %collective-permute-done.20 = bf16[528,128]{1,0:T(8,128)(2,1)S(1)} collective-permute-done((bf16[528,128]{1,0:T(8,128)(2,1)S(1)}, bf16[528,128]{1,0:T(8,128)(2,1)S(1)}, u32[]{:S(2)}, u32[]{:S(2)}) %collective-permute-start.20) | collective-permute-done | bytes 135200 | tf_op jit(solution)/shard_map/ppermute | solution.py:353
  48.7 0.9 collective-permute-start.21
  49.5 2.0 collective-permute-done.8
  51.6 0.9 collective-permute-start.9
  52.4 2.0 collective-permute-done.3
  54.6 0.6 constant_dynamic-update-slice_fusion.9
  55.3 1.4 collective-permute-start.16
  57.0 1.4 collective-permute-start.10
  58.5 1.1 collective-permute-start.5
  59.6 1.4 collective-permute-done.16
  61.0 1.5 collective-permute-start.17
  62.5 4.3 %collective-permute-done.22 = bf16[1056,128]{1,0:T(8,128)(2,1)S(1)} collective-permute-done((bf16[1056,128]{1,0:T(8,128)(2,1)S(1)}, bf16[1056,128]{1,0:T(8,128)(2,1)S(1)}, u32[]{:S(2)}, u32[]{:S(2)}) %collective-permute-start.22) | collective-permute-done | bytes 270368 | tf_op jit(solution)/shard_map/ppermute | solution.py:353
  66.8 1.5 collective-permute-done.17
  68.5 5.1 %collective-permute-start.23 = (bf16[4224,128]{1,0:T(8,128)(2,1)S(1)}, bf16[4224,128]{1,0:T(8,128)(2,1)S(1)}, u32[]{:S(2)}, u32[]{:S(2)}) collective-permute-start(bf16[4224,128]{1,0:T(8,128)(2,1)S(1)} %get-tuple-element.27), channel_id=1, source_target_pairs={{0,1},{1,0},{2,3},{3,2},{4,5},{5,4},{6,7},{7,6},{8,9},{9,8},{10,11... | collective-permute-start | bytes 3244040 | tf_op jit(solution)/shard_map/ppermute | solution.py:353
  73.9 2.0 collective-permute-done.23
  76.1 9.2 %row_products.2 = (s16[16,272,256]{2,1,0:T(8,128)(2,1)}, bf16[16,128]{1,0:T(8,128)(2,1)S(1)}) custom-call(bf16[8448,128]{1,0:T(8,128)(2,1)S(1)} %constant_dynamic-update-slice_fusion.main_ref.next_ref, bf16[8448,128]{1,0:T(8,128)(2,1)S(1)} %constant_dynamic-update-slice_fusion.main_ref.next_ref, bf16[64,128]{1,0:T(8,128)(2,1)S(1)} %slice.37.parts_ref, ...), custom_call_target="tpu_custom_call" | custom-call | flops 4294967296 | bytes 12648448 | tf_op jit(solution)/shard_map/row_products/pallas_call | solution.py:430
  85.3 7.1 %all-to-all-start.1 = ((s16[16,272,256]{2,1,0:T(8,128)(2,1)}), s16[16,272,256]{2,1,0:T(8,128)(2,1)S(1)}, u32[]{:S(2)}, u32[]{:S(2)}) async-start(s16[16,272,256]{2,1,0:T(8,128)(2,1)} %get-tuple-element.18), calls=%async_computation.1 | async-start | bytes 4456448 | tf_op jit(solution)/shard_map/all_to_all | solution.py:548
  92.7 2.4 %collective-permute-done.11 = bf16[4224,128]{1,0:T(8,128)(2,1)S(1)} collective-permute-done((bf16[4224,128]{1,0:T(8,128)(2,1)S(1)}, bf16[4224,128]{1,0:T(8,128)(2,1)S(1)}, u32[]{:S(2)}, u32[]{:S(2)}) %collective-permute-start.11) | collective-permute-done | bytes 1081376 | tf_op jit(solution)/shard_map/ppermute | solution.py:353
  95.1 1.1 constant_dynamic-update-slice_fusion.10.main_ref.next_ref
  96.1 0.7 slice.34.parts_ref
  96.9 1.6 copy-done.2
  98.5 3.4 %copy-done.8 = bf16[16,8,256,128]{3,2,1,0:T(8,128)(2,1)S(1)} copy-done((bf16[16,8,256,128]{3,2,1,0:T(8,128)(2,1)S(1)}, bf16[16,8,256,128]{3,2,1,0:T(8,128)(2,1)}, u32[]{:S(2)}) %copy-start.8) | copy-done | bytes 8388632
  101.9 9.0 %row_products.3 = (s16[16,272,256]{2,1,0:T(8,128)(2,1)}, bf16[16,128]{1,0:T(8,128)(2,1)}) custom-call(bf16[8448,128]{1,0:T(8,128)(2,1)S(1)} %copy-done.2, bf16[8448,128]{1,0:T(8,128)(2,1)S(1)} %copy-done.2, bf16[64,128]{1,0:T(8,128)(2,1)S(1)} %slice.34.parts_ref, bf16[256,256]{1,0:T(8,128)(2,1)S(1)} %copy-done.5, bf16[16,8,256,128]{3,2,1,0:T(8,128)(2,1)S(1)} %copy-done.8, ...), custom_call_target="tpu_custom_call" | custom-call | flops 4294967296 | bytes 12648448 | tf_op jit(solution)/shard_map/row_products/pallas_call | solution.py:430
  110.9 31.7 %all-to-all-done.1.coded_ref = s16[16,272,256]{2,1,0:T(8,128)(2,1)S(1)} async-done(((s16[16,272,256]{2,1,0:T(8,128)(2,1)}), s16[16,272,256]{2,1,0:T(8,128)(2,1)S(1)}, u32[]{:S(2)}, u32[]{:S(2)}) %all-to-all-start.1) | async-done | bytes 2228256 | tf_op jit(solution)/shard_map/all_to_all | solution.py:548
  142.6 5.0 %all-to-all-start = ((s16[16,272,256]{2,1,0:T(8,128)(2,1)}), s16[16,272,256]{2,1,0:T(8,128)(2,1)}, u32[]{:S(2)}, u32[]{:S(2)}) async-start(s16[16,272,256]{2,1,0:T(8,128)(2,1)} %get-tuple-element.17), calls=%async_computation | async-start | bytes 4456448 | tf_op jit(solution)/shard_map/all_to_all | solution.py:548
  147.6 9.2 %finish.2.refs_0_ = f32[16384,128]{1,0:T(8,128)} custom-call(s32[4096]{0:T(1024)S(1)} %copy-done.6, s16[16,272,256]{2,1,0:T(8,128)(2,1)S(1)} %all-to-all-done.1.coded_ref), custom_call_target="tpu_custom_call" | custom-call | tf_op jit(solution)/shard_map/finish/pallas_call | solution.py:500
  156.8 41.1 %all-to-all-done.coded_ref = s16[16,272,256]{2,1,0:T(8,128)(2,1)} async-done(((s16[16,272,256]{2,1,0:T(8,128)(2,1)}), s16[16,272,256]{2,1,0:T(8,128)(2,1)}, u32[]{:S(2)}, u32[]{:S(2)}) %all-to-all-start) | async-done | bytes 2228256 | tf_op jit(solution)/shard_map/all_to_all | solution.py:548
  197.9 10.1 %finish.3 = f32[16384,128]{1,0:T(8,128)} custom-call(s32[4096]{0:T(1024)S(1)} %copy-done.6, s16[16,272,256]{2,1,0:T(8,128)(2,1)} %all-to-all-done.coded_ref, f32[16384,128]{1,0:T(8,128)} %finish.2.refs_0_), custom_call_target="tpu_custom_call", output_to_operand_aliasing={{}: (2, {})} | custom-call | tf_op jit(solution)/shard_map/finish/pallas_call | solution.py:500
  (83 shorter events, 4.8 us)
Async XLA Ops:
  1.6 3.4 %copy-start = (s32[256,16,519]{0,1,2:T(8,128)S(1)}, s32[256,16,519]{0,1,2:T(8,128)}, u32[]{:S(2)}) copy-start(s32[256,16,519]{0,1,2:T(8,128)} %param.4) | copy-start | bytes 25509892
  7.6 1.4 copy-start.3
  7.7 3.2 %collective-permute-start.12 = (bf16[4224,128]{1,0:T(8,128)(2,1)S(1)}, bf16[4224,128]{1,0:T(8,128)(2,1)}, u32[]{:S(2)}, u32[]{:S(2)}) collective-permute-start(bf16[4224,128]{1,0:T(8,128)(2,1)S(1)} %constant_dynamic-slice_fusion.4), channel_id=1, source_target_pairs={{0,1},{1,0},{2,3},{3,2},{4,5},{5,4},{6,7},{7,6},{8,9},{9,8},{10,11... | collective-permute-start | bytes 3244040 | tf_op jit(solution)/shard_map/ppermute | solution.py:353
  9.0 25.5 %slice-start = ((s8[8503296]{0:T(1024)(128)(4,1)}), s8[114688]{0:T(1024)(128)(4,1)S(1)}, s32[]{:S(2)}) async-start(s8[8503296]{0:T(1024)(128)(4,1)} %bitcast.14), calls=%async_computation.2 | async-start | bytes 229376
  10.0 3.3 %collective-permute-start = (bf16[4224,128]{1,0:T(8,128)(2,1)}, bf16[4224,128]{1,0:T(8,128)(2,1)}, u32[]{:S(2)}, u32[]{:S(2)}) collective-permute-start(bf16[4224,128]{1,0:T(8,128)(2,1)} %constant_dynamic-slice_fusion.9), channel_id=1, source_target_pairs={{0,1},{1,0},{2,3},{3,2},{4,5},{5,4},{6,7},{7,6},{8,9},{9,8},{10,11... | collective-permute-start | bytes 3244040 | tf_op jit(solution)/shard_map/ppermute | solution.py:353
  12.7 21.7 %slice-start.1 = ((s8[8503296]{0:T(1024)(128)(4,1)}), s8[4194304]{0:T(1024)(128)(4,1)S(1)}, s32[]{:S(2)}) async-start(s8[8503296]{0:T(1024)(128)(4,1)} %bitcast.14), calls=%async_computation.3 | async-start | bytes 8388608
  12.9 7.8 %collective-permute-start.13 = (bf16[1056,128]{1,0:T(8,128)(2,1)S(1)}, bf16[1056,128]{1,0:T(8,128)(2,1)S(1)}, u32[]{:S(2)}, u32[]{:S(2)}) collective-permute-start(bf16[1056,128]{1,0:T(8,128)(2,1)S(1)} %constant_dynamic-slice_fusion.3), channel_id=1, source_target_pairs={{0,2},{1,3},{2,0},{3,1},{4,6},{5,7},{6,4},{7,5},{8,10},{9,11},{10,... | collective-permute-start | bytes 811016 | tf_op jit(solution)/shard_map/ppermute | solution.py:353
  13.2 7.8 %collective-permute-start.18 = (bf16[1056,128]{1,0:T(8,128)(2,1)S(1)}, bf16[1056,128]{1,0:T(8,128)(2,1)S(1)}, u32[]{:S(2)}, u32[]{:S(2)}) collective-permute-start(bf16[1056,128]{1,0:T(8,128)(2,1)S(1)} %constant_dynamic-slice_fusion.1), channel_id=1, source_target_pairs={{0,4},{1,5},{2,6},{3,7},{4,0},{5,1},{6,2},{7,3},{8,12},{9,13},{10,... | collective-permute-start | bytes 811016 | tf_op jit(solution)/shard_map/ppermute | solution.py:353
  15.2 19.3 %slice-start.2 = ((s8[8503296]{0:T(1024)(128)(4,1)}), s8[4194304]{0:T(1024)(128)(4,1)S(1)}, s32[]{:S(2)}) async-start(s8[8503296]{0:T(1024)(128)(4,1)} %bitcast.14), calls=%async_computation.4 | async-start | bytes 8388608
  15.3 11.1 %collective-permute-start.6 = (bf16[1056,128]{1,0:T(8,128)(2,1)S(1)}, bf16[1056,128]{1,0:T(8,128)(2,1)S(1)}, u32[]{:S(2)}, u32[]{:S(2)}) collective-permute-start(bf16[1056,128]{1,0:T(8,128)(2,1)S(1)} %constant_dynamic-slice_fusion.6), channel_id=1, source_target_pairs={{0,4},{1,5},{2,6},{3,7},{4,0},{5,1},{6,2},{7,3},{8,12},{9,13},{10,... | collective-permute-start | bytes 811016 | tf_op jit(solution)/shard_map/ppermute | solution.py:353
  16.4 11.4 %collective-permute-start.1 = (bf16[1056,128]{1,0:T(8,128)(2,1)S(1)}, bf16[1056,128]{1,0:T(8,128)(2,1)S(1)}, u32[]{:S(2)}, u32[]{:S(2)}) collective-permute-start(bf16[1056,128]{1,0:T(8,128)(2,1)S(1)} %constant_dynamic-slice_fusion.8), channel_id=1, source_target_pairs={{0,2},{1,3},{2,0},{3,1},{4,6},{5,7},{6,4},{7,5},{8,10},{9,11},{10,... | collective-permute-start | bytes 811016 | tf_op jit(solution)/shard_map/ppermute | solution.py:353
  20.7 8.6 %collective-permute-start.14 = (bf16[528,128]{1,0:T(8,128)(2,1)S(1)}, bf16[528,128]{1,0:T(8,128)(2,1)S(1)}, u32[]{:S(2)}, u32[]{:S(2)}) collective-permute-start(bf16[528,128]{1,0:T(8,128)(2,1)S(1)} %constant_dynamic-slice_fusion.2), channel_id=1, source_target_pairs={{0,4},{1,5},{2,6},{3,7},{4,0},{5,1},{6,2},{7,3},{8,12},{9,13},{10,... | collective-permute-start | bytes 405512 | tf_op jit(solution)/shard_map/ppermute | solution.py:353
  21.0 13.4 %copy-start.5 = (bf16[256,256]{1,0:T(8,128)(2,1)S(1)}, bf16[256,256]{1,0:T(8,128)(2,1)}, u32[]{:S(2)}) copy-start(bf16[256,256]{1,0:T(8,128)(2,1)} %constant.222.clone.weights_ref) | copy-start | bytes 393220
  21.1 10.6 %collective-permute-start.19 = (bf16[528,128]{1,0:T(8,128)(2,1)S(1)}, bf16[528,128]{1,0:T(8,128)(2,1)S(1)}, u32[]{:S(2)}, u32[]{:S(2)}) collective-permute-start(bf16[528,128]{1,0:T(8,128)(2,1)S(1)} %constant_dynamic-slice_fusion), channel_id=1, source_target_pairs={{0,2},{1,3},{2,0},{3,1},{4,6},{5,7},{6,4},{7,5},{8,10},{9,11},{10,... | collective-permute-start | bytes 405512 | tf_op jit(solution)/shard_map/ppermute | solution.py:353
  26.5 5.4 %collective-permute-start.7 = (bf16[528,128]{1,0:T(8,128)(2,1)S(1)}, bf16[528,128]{1,0:T(8,128)(2,1)S(1)}, u32[]{:S(2)}, u32[]{:S(2)}) collective-permute-start(bf16[528,128]{1,0:T(8,128)(2,1)S(1)} %constant_dynamic-slice_fusion.5), channel_id=1, source_target_pairs={{0,2},{1,3},{2,0},{3,1},{4,6},{5,7},{6,4},{7,5},{8,10},{9,11},{10,... | collective-permute-start | bytes 405512 | tf_op jit(solution)/shard_map/ppermute | solution.py:353
  27.9 6.4 %collective-permute-start.2 = (bf16[528,128]{1,0:T(8,128)(2,1)S(1)}, bf16[528,128]{1,0:T(8,128)(2,1)S(1)}, u32[]{:S(2)}, u32[]{:S(2)}) collective-permute-start(bf16[528,128]{1,0:T(8,128)(2,1)S(1)} %constant_dynamic-slice_fusion.7), channel_id=1, source_target_pairs={{0,4},{1,5},{2,6},{3,7},{4,0},{5,1},{6,2},{7,3},{8,12},{9,13},{10,... | collective-permute-start | bytes 405512 | tf_op jit(solution)/shard_map/ppermute | solution.py:353
  29.3 25.3 %collective-permute-start.15 = (bf16[528,128]{1,0:T(8,128)(2,1)S(1)}, bf16[528,128]{1,0:T(8,128)(2,1)S(1)}, u32[]{:S(2)}, u32[]{:S(2)}) collective-permute-start(bf16[528,128]{1,0:T(8,128)(2,1)S(1)} %dynamic-slice_add_fusion.7.after_ref), channel_id=1, source_target_pairs={{0,8},{1,9},{2,10},{3,11},{4,12},{5,13},{6,14},{7,15},{8,0},{9,1},... | collective-permute-start | bytes 405512 | tf_op jit(solution)/shard_map/ppermute | solution.py:353
  31.8 16.8 %collective-permute-start.20 = (bf16[528,128]{1,0:T(8,128)(2,1)S(1)}, bf16[528,128]{1,0:T(8,128)(2,1)S(1)}, u32[]{:S(2)}, u32[]{:S(2)}) collective-permute-start(bf16[528,128]{1,0:T(8,128)(2,1)S(1)} %dynamic-slice_add_fusion.6), channel_id=1, source_target_pairs={{0,8},{1,9},{2,10},{3,11},{4,12},{5,13},{6,14},{7,15},{8,0},{9,1},... | collective-permute-start | bytes 405512 | tf_op jit(solution)/shard_map/ppermute | solution.py:353
  31.9 19.6 %collective-permute-start.8 = (bf16[528,128]{1,0:T(8,128)(2,1)S(1)}, bf16[528,128]{1,0:T(8,128)(2,1)S(1)}, u32[]{:S(2)}, u32[]{:S(2)}) collective-permute-start(bf16[528,128]{1,0:T(8,128)(2,1)S(1)} %dynamic-slice_add_fusion.8), channel_id=1, source_target_pairs={{0,8},{1,9},{2,10},{3,11},{4,12},{5,13},{6,14},{7,15},{8,0},{9,1},... | collective-permute-start | bytes 405512 | tf_op jit(solution)/shard_map/ppermute | solution.py:353
  34.4 20.0 %collective-permute-start.3 = (bf16[528,128]{1,0:T(8,128)(2,1)S(1)}, bf16[528,128]{1,0:T(8,128)(2,1)S(1)}, u32[]{:S(2)}, u32[]{:S(2)}) collective-permute-start(bf16[528,128]{1,0:T(8,128)(2,1)S(1)} %dynamic-slice_add_fusion.9), channel_id=1, source_target_pairs={{0,8},{1,9},{2,10},{3,11},{4,12},{5,13},{6,14},{7,15},{8,0},{9,1},... | collective-permute-start | bytes 405512 | tf_op jit(solution)/shard_map/ppermute | solution.py:353
  43.5 32.5 %copy-start.7 = (bf16[16,8,256,128]{3,2,1,0:T(8,128)(2,1)}, bf16[16,8,256,128]{3,2,1,0:T(8,128)(2,1)S(1)}, u32[]{:S(2)}) copy-start(bf16[16,8,256,128]{3,2,1,0:T(8,128)(2,1)S(1)} %get-tuple-element.14.own_ref) | copy-start | bytes 25165828
  48.7 8.0 %collective-permute-start.21 = (bf16[528,128]{1,0:T(8,128)(2,1)S(1)}, bf16[528,128]{1,0:T(8,128)(2,1)S(1)}, u32[]{:S(2)}, u32[]{:S(2)}) collective-permute-start(bf16[528,128]{1,0:T(8,128)(2,1)S(1)} %get-tuple-element.22), channel_id=1, source_target_pairs={{0,2},{1,3},{2,0},{3,1},{4,6},{5,7},{6,4},{7,5},{8,10},{9,11},{10,... | collective-permute-start | bytes 405512 | tf_op jit(solution)/shard_map/ppermute | solution.py:353
  51.6 5.4 %collective-permute-start.9 = (bf16[528,128]{1,0:T(8,128)(2,1)S(1)}, bf16[528,128]{1,0:T(8,128)(2,1)S(1)}, u32[]{:S(2)}, u32[]{:S(2)}) collective-permute-start(bf16[528,128]{1,0:T(8,128)(2,1)S(1)} %get-tuple-element.26), channel_id=1, source_target_pairs={{0,2},{1,3},{2,0},{3,1},{4,6},{5,7},{6,4},{7,5},{8,10},{9,11},{10,... | collective-permute-start | bytes 405512 | tf_op jit(solution)/shard_map/ppermute | solution.py:353
  54.5 4.0 %collective-permute-start.4 = (bf16[528,128]{1,0:T(8,128)(2,1)S(1)}, bf16[528,128]{1,0:T(8,128)(2,1)S(1)}, u32[]{:S(2)}, u32[]{:S(2)}) collective-permute-start(bf16[528,128]{1,0:T(8,128)(2,1)S(1)} %get-tuple-element.24), channel_id=1, source_target_pairs={{0,4},{1,5},{2,6},{3,7},{4,0},{5,1},{6,2},{7,3},{8,12},{9,13},{10,... | collective-permute-start | bytes 405512 | tf_op jit(solution)/shard_map/ppermute | solution.py:353
  55.3 5.7 %collective-permute-start.16 = (bf16[528,128]{1,0:T(8,128)(2,1)S(1)}, bf16[528,128]{1,0:T(8,128)(2,1)S(1)}, u32[]{:S(2)}, u32[]{:S(2)}) collective-permute-start(bf16[528,128]{1,0:T(8,128)(2,1)S(1)} %get-tuple-element.20), channel_id=1, source_target_pairs={{0,4},{1,5},{2,6},{3,7},{4,0},{5,1},{6,2},{7,3},{8,12},{9,13},{10,... | collective-permute-start | bytes 405512 | tf_op jit(solution)/shard_map/ppermute | solution.py:353
  56.7 11.6 %copy-start.4 = (bf16[8448,128]{1,0:T(8,128)(2,1)S(1)}, bf16[8448,128]{1,0:T(8,128)(2,1)}, u32[]{:S(2)}) copy-start(bf16[8448,128]{1,0:T(8,128)(2,1)} %copy-done.3) | copy-start | bytes 6488068
  56.7 10.1 %collective-permute-start.22 = (bf16[1056,128]{1,0:T(8,128)(2,1)S(1)}, bf16[1056,128]{1,0:T(8,128)(2,1)S(1)}, u32[]{:S(2)}, u32[]{:S(2)}) collective-permute-start(bf16[1056,128]{1,0:T(8,128)(2,1)S(1)} %constant_dynamic-update-slice_fusion.4), channel_id=1, source_target_pairs={{0,4},{1,5},{2,6},{3,7},{4,0},{5,1},{6,2},{7,3},{8,12},{9,13},{10,... | collective-permute-start | bytes 811016 | tf_op jit(solution)/shard_map/ppermute | solution.py:353
  57.0 16.6 %collective-permute-start.10 = (bf16[1056,128]{1,0:T(8,128)(2,1)S(1)}, bf16[1056,128]{1,0:T(8,128)(2,1)S(1)}, u32[]{:S(2)}, u32[]{:S(2)}) collective-permute-start(bf16[1056,128]{1,0:T(8,128)(2,1)S(1)} %constant_dynamic-update-slice_fusion.14), channel_id=1, source_target_pairs={{0,4},{1,5},{2,6},{3,7},{4,0},{5,1},{6,2},{7,3},{8,12},{9,13},{10,... | collective-permute-start | bytes 811016 | tf_op jit(solution)/shard_map/ppermute | solution.py:353
  58.5 15.1 %collective-permute-start.5 = (bf16[1056,128]{1,0:T(8,128)(2,1)S(1)}, bf16[1056,128]{1,0:T(8,128)(2,1)S(1)}, u32[]{:S(2)}, u32[]{:S(2)}) collective-permute-start(bf16[1056,128]{1,0:T(8,128)(2,1)S(1)} %constant_dynamic-update-slice_fusion.18), channel_id=1, source_target_pairs={{0,2},{1,3},{2,0},{3,1},{4,6},{5,7},{6,4},{7,5},{8,10},{9,11},{10,... | collective-permute-start | bytes 811016 | tf_op jit(solution)/shard_map/ppermute | solution.py:353
  61.0 7.3 %collective-permute-start.17 = (bf16[1056,128]{1,0:T(8,128)(2,1)S(1)}, bf16[1056,128]{1,0:T(8,128)(2,1)S(1)}, u32[]{:S(2)}, u32[]{:S(2)}) collective-permute-start(bf16[1056,128]{1,0:T(8,128)(2,1)S(1)} %constant_dynamic-update-slice_fusion.8), channel_id=1, source_target_pairs={{0,2},{1,3},{2,0},{3,1},{4,6},{5,7},{6,4},{7,5},{8,10},{9,11},{10,... | collective-permute-start | bytes 811016 | tf_op jit(solution)/shard_map/ppermute | solution.py:353
  68.5 7.4 %collective-permute-start.23 = (bf16[4224,128]{1,0:T(8,128)(2,1)S(1)}, bf16[4224,128]{1,0:T(8,128)(2,1)S(1)}, u32[]{:S(2)}, u32[]{:S(2)}) collective-permute-start(bf16[4224,128]{1,0:T(8,128)(2,1)S(1)} %get-tuple-element.27), channel_id=1, source_target_pairs={{0,1},{1,0},{2,3},{3,2},{4,5},{5,4},{6,7},{7,6},{8,9},{9,8},{10,11... | collective-permute-start | bytes 3244040 | tf_op jit(solution)/shard_map/ppermute | solution.py:353
  73.9 11.4 %copy-start.1 = (bf16[8448,128]{1,0:T(8,128)(2,1)}, bf16[8448,128]{1,0:T(8,128)(2,1)S(1)}, u32[]{:S(2)}) copy-start(bf16[8448,128]{1,0:T(8,128)(2,1)S(1)} %get-tuple-element.32) | copy-start | bytes 6488068
  85.3 57.3 %all-to-all-start.1 = ((s16[16,272,256]{2,1,0:T(8,128)(2,1)}), s16[16,272,256]{2,1,0:T(8,128)(2,1)S(1)}, u32[]{:S(2)}, u32[]{:S(2)}) async-start(s16[16,272,256]{2,1,0:T(8,128)(2,1)} %get-tuple-element.18), calls=%async_computation.1 | async-start | bytes 4456448 | tf_op jit(solution)/shard_map/all_to_all | solution.py:548
  92.3 2.8 %collective-permute-start.11 = (bf16[4224,128]{1,0:T(8,128)(2,1)S(1)}, bf16[4224,128]{1,0:T(8,128)(2,1)S(1)}, u32[]{:S(2)}, u32[]{:S(2)}) collective-permute-start(bf16[4224,128]{1,0:T(8,128)(2,1)S(1)} %get-tuple-element.31.refs_0_), channel_id=1, source_target_pairs={{0,1},{1,0},{2,3},{3,2},{4,5},{5,4},{6,7},{7,6},{8,9},{9,8},{10,11... | collective-permute-start | bytes 3244040 | tf_op jit(solution)/shard_map/ppermute | solution.py:353
  96.9 1.6 copy-start.2
  98.5 3.4 %copy-start.8 = (bf16[16,8,256,128]{3,2,1,0:T(8,128)(2,1)S(1)}, bf16[16,8,256,128]{3,2,1,0:T(8,128)(2,1)}, u32[]{:S(2)}) copy-start(bf16[16,8,256,128]{3,2,1,0:T(8,128)(2,1)} %copy-done.7) | copy-start | bytes 25165828
  142.6 5.0 %copy-start.6 = (s32[4096]{0:T(1024)S(1)}, s32[4096]{0:T(1024)}, u32[]{:S(2)}) copy-start(s32[4096]{0:T(1024)} %slot_ref.3) | copy-start | bytes 49156
  142.6 55.4 %all-to-all-start = ((s16[16,272,256]{2,1,0:T(8,128)(2,1)}), s16[16,272,256]{2,1,0:T(8,128)(2,1)}, u32[]{:S(2)}, u32[]{:S(2)}) async-start(s16[16,272,256]{2,1,0:T(8,128)(2,1)} %get-tuple-element.17), calls=%async_computation | async-start | bytes 4456448 | tf_op jit(solution)/shard_map/all_to_all | solution.py:548

commit v12 on v11

--- a/solution.py
+++ b/solution.py
@@ -371,124 +371,132 @@
     return lax.dynamic_update_slice_in_dim(buffer, other, (1 - side(bit)) * size, 0)
 
 
-def sum_over_feed(value, work=None):
+def sum_over_feed(value, behind=None, work=None):
     half = reduce_half(value, 1)
     size = half.shape[0] // 2
     left, right = half[:size], half[size:]
     left_1, right_1 = reduce_half(left, 2), reduce_half(right, 4)
     left_2, right_2 = reduce_half(left_1, 4), reduce_half(right_1, 2)
+    if behind is not None:
+        left_2, right_2 = left_2 + behind, right_2 + behind
     left_3, right_3 = left_2 + swap(left_2, 8), right_2 + swap(right_2, 8)
     if work is not None:
         left_3 = left_3 + work(left_2)
+    crossed = (left_3[0, 0] + right_3[0, 0]) * 0
     left_1, right_1 = gather_half(left_3, 4, left_1), gather_half(right_3, 2, right_1)
     left, right = gather_half(left_1, 2, left), gather_half(right_1, 4, right)
     half = jnp.concatenate([left, right], axis=0)
-    return half, lambda: gather_half(half, 1, value)
-
-
-def rows_kernel(main_ref, next_ref, parts_ref, weights_ref, own_ref, *refs):
-    out_ref, done_ref, left = refs[-3:]
+    return half, lambda: gather_half(half, 1, value), crossed
+
+
+def rows_kernel(main_ref, next_ref, parts_ref, weights_ref, out_ref):
     step = pl.program_id(0)
-    done_ref[...] = jnp.zeros_like(done_ref)
-    ch, steps = own_ref.shape[:2]
-    rows = main_ref.shape[1]
-
-    @pl.when(step < steps)
-    def _():
-        words = jnp.concatenate([main_ref[...], next_ref[...]], axis=0).astype(jnp.float32).astype(jnp.int32)
-        parts = parts_ref[...].astype(jnp.float32)
-        gains = parts[: 2 * ch] * 16.0 + parts[2 * ch :]
-
-        def store(b, c, real, imag):
-            spot = pl.ds(pl.multiple_of(step * (2 * STEPS * STEP), 2 * STEPS * STEP) + b * 2 * STEP, 2 * STEP)
-            left[c, spot, :rows] = jnp.concatenate([real, imag], axis=0).astype(left.dtype)
-            left[c, spot, rows:] = jnp.concatenate([imag, -real], axis=0).astype(left.dtype)
-
-        spectra_of(weights_ref, levels_of(words), gains, ch, store)
-
-    @pl.when(step >= steps)
-    def _():
-        each = out_ref.shape[0]
-        for index in range(each):
-            c = (step - steps) * each + index
-            spectra = jnp.concatenate([own_ref[c, part] for part in range(steps)], axis=1)
-            products = jnp.dot(spectra, left[c], preferred_element_type=jnp.float32)
-            count = products.shape[0]
-            largest = jnp.maximum(jnp.max(jnp.abs(products), axis=0, keepdims=True), 2.0**-60)
-            power = jnp.floor(jnp.log2(largest))
-            coded = jnp.clip(jnp.round(products * jnp.exp2(RANGE - power)), -32767.0, 32767.0)
-            out_ref[index, :count, :] = coded.astype(jnp.int32).astype(jnp.int16)
-            line = jnp.broadcast_to(power, (out_ref.shape[1] - count, power.shape[1]))
-            out_ref[index, count:, :] = line.astype(jnp.int32).astype(jnp.int16)
-
-
-def row_products(words, parts, own, weights, after):
-    ch, steps, count, width = own.shape
+    ch, rows = out_ref.shape[0], main_ref.shape[1]
+    words = jnp.concatenate([main_ref[...], next_ref[...]], axis=0).astype(jnp.float32).astype(jnp.int32)
+    parts = parts_ref[...].astype(jnp.float32)
+    gains = parts[: 2 * ch] * 16.0 + parts[2 * ch :]
+
+    def store(b, c, real, imag):
+        spot = pl.ds(pl.multiple_of(step * (2 * STEPS * STEP), 2 * STEPS * STEP) + b * 2 * STEP, 2 * STEP)
+        out_ref[c, spot, :rows] = jnp.concatenate([real, imag], axis=0).astype(out_ref.dtype)
+        out_ref[c, spot, rows:] = jnp.concatenate([imag, -real], axis=0).astype(out_ref.dtype)
+
+    spectra_of(weights_ref, levels_of(words), gains, ch, store)
+
+
+def row_spectra(words, parts, weights, ch, spectra):
     rows = words.shape[1]
     main = STEPS * STEP * ch
+    return pl.pallas_call(
+        rows_kernel,
+        grid=(spectra // (STEPS * STEP),),
+        in_specs=[
+            pl.BlockSpec((main, rows), lambda i: (i, 0)),
+            pl.BlockSpec((STEP * ch, rows), lambda i: ((i + 1) * STEPS, 0)),
+            pl.BlockSpec(parts.shape, lambda i: (0, 0)),
+            pl.BlockSpec(weights.shape, lambda i: (0, 0)),
+        ],
+        out_specs=pl.BlockSpec(memory_space=pltpu.VMEM),
+        out_shape=jax.ShapeDtypeStruct((ch, 2 * spectra, 2 * rows), jnp.bfloat16),
+        compiler_params=pltpu.CompilerParams(vmem_limit_bytes=8 << 20),
+        cost_estimate=pl.CostEstimate(
+            flops=8 * spectra * ch * SPAN * ch * rows,
+            bytes_accessed=2 * words.size + 8 * ch * spectra * rows,
+            transcendentals=0,
+        ),
+        name="row_spectra",
+    )(words, words, parts, weights)
+
+
+def products_kernel(own_ref, left_ref, *refs):
+    out_ref, done_ref = refs[-2:]
+    done_ref[...] = jnp.zeros_like(done_ref)
+    each, steps = out_ref.shape[0], own_ref.shape[1]
+    for index in range(each):
+        c = pl.program_id(0) * each + index
+        spectra = jnp.concatenate([own_ref[c, part] for part in range(steps)], axis=1)
+        products = jnp.dot(spectra, left_ref[c], preferred_element_type=jnp.float32)
+        count = products.shape[0]
+        largest = jnp.maximum(jnp.max(jnp.abs(products), axis=0, keepdims=True), 2.0**-60)
+        power = jnp.floor(jnp.log2(largest))
+        coded = jnp.clip(jnp.round(products * jnp.exp2(RANGE - power)), -32767.0, 32767.0)
+        out_ref[index, :count, :] = coded.astype(jnp.int32).astype(jnp.int16)
+        line = jnp.broadcast_to(power, (out_ref.shape[1] - count, power.shape[1]))
+        out_ref[index, count:, :] = line.astype(jnp.int32).astype(jnp.int16)
+
+
+def row_products(own, left, after):
+    ch, steps, count, width = own.shape
+    columns = left.shape[2]
     each = 4
     return pl.pallas_call(
-        rows_kernel,
-        grid=(steps + ch // each,),
-        in_specs=[
-            pl.BlockSpec((main, rows), lambda i: (jnp.minimum(i, steps - 1), 0)),
-            pl.BlockSpec((STEP * ch, rows), lambda i: ((jnp.minimum(i, steps - 1) + 1) * STEPS, 0)),
-            pl.BlockSpec(parts.shape, lambda i: (0, 0)),
-            pl.BlockSpec(weights.shape, lambda i: (0, 0)),
-            pl.BlockSpec(memory_space=pltpu.VMEM),
-        ]
-        + [pl.BlockSpec(memory_space=pl.ANY)] * len(after),
+        products_kernel,
+        grid=(ch // each,),
+        in_specs=[pl.BlockSpec(memory_space=pltpu.VMEM)] * 2 + [pl.BlockSpec(memory_space=pl.ANY)] * len(after),
         out_specs=[
-            pl.BlockSpec((each, count + 16, 2 * rows), lambda i: (jnp.maximum(i - steps, 0), 0, 0)),
+            pl.BlockSpec((each, count + 16, columns), lambda i: (i, 0, 0)),
             pl.BlockSpec((16, LANES), lambda i: (0, 0)),
         ],
         out_shape=[
-            pltpu.HBM((ch, count + 16, 2 * rows), jnp.int16),
+            pltpu.HBM((ch, count + 16, columns), jnp.int16),
             jax.ShapeDtypeStruct((16, LANES), jnp.bfloat16),
         ],
-        scratch_shapes=[
-            pltpu.VMEM((ch, steps * width, 2 * rows), jnp.bfloat16),
-        ],
-        compiler_params=pltpu.CompilerParams(vmem_limit_bytes=18 << 20),
+        compiler_params=pltpu.CompilerParams(vmem_limit_bytes=10 << 20),
         cost_estimate=pl.CostEstimate(
-            flops=4 * steps * width * ch * SPAN * ch * rows + 4 * ch * steps * width * rows * count,
-            bytes_accessed=2 * words.size + 2 * own.size + 4 * ch * rows * count,
-            transcendentals=0,
+            flops=2 * left.size * count, bytes_accessed=2 * left.size + 2 * own.size, transcendentals=0
         ),
         name="row_products",
-    )(words, words, parts, weights, own, *after)
+    )(own, left, *after)
 
 
 def finish_kernel(scale, slot_ref, coded_ref, *refs):
     out_ref, products, tile, mixed = refs[-4:]
+    step = pl.program_id(0)
     sources, lines, width = coded_ref.shape
     count = lines - 16
     pieces = width // LANES
-    feeds = sources * count
-    columns = 2 * (feeds // LANES)
-    for source in range(sources):
-        power = coded_ref[source, count : count + 16, :][:1].astype(jnp.float32)
-        values = coded_ref[source, :count, :].astype(jnp.float32) * (jnp.exp2(power - RANGE) * scale)
+    together = 8 // pieces
+
+    @pl.when(step == 0)
+    def _():
+        for source in range(sources):
+            power = coded_ref[source, count : count + 16, :][:1].astype(jnp.float32)
+            values = coded_ref[source, :count, :].astype(jnp.float32) * (jnp.exp2(power - RANGE) * scale)
+            for piece in range(pieces):
+                products[pl.ds(source * count * pieces + piece, count, stride=pieces), :] = values[
+                    :, piece * LANES : (piece + 1) * LANES
+                ]
+
+    for part in range(together):
+        for i in range(LANES):
+            slot = slot_ref[(step * together + part) * LANES + i]
+            tile[i * pieces : (i + 1) * pieces, :] = products[
+                pl.ds(pl.multiple_of(slot * pieces, pieces), pieces), :
+            ]
         for piece in range(pieces):
-            products[pl.ds(source * count * pieces + piece, count, stride=pieces), :] = values[
-                :, piece * LANES : (piece + 1) * LANES
-            ]
-
-    together = 8 // pieces
-
-    @pl.loop(0, feeds // LANES // together)
-    def _(j):
-        for part in range(together):
-            for i in range(LANES):
-                slot = slot_ref[(j * together + part) * LANES + i]
-                tile[i * pieces : (i + 1) * pieces, :] = products[
-                    pl.ds(pl.multiple_of(slot * pieces, pieces), pieces), :
-                ]
-            for piece in range(pieces):
-                turned = tile[pl.ds(piece, LANES, stride=pieces), :].T
-                mixed[pl.ds(part * pieces + piece, LANES, stride=8), :] = turned
-        for row in range(LANES):
-            out_ref[pl.ds(pl.multiple_of(row * columns + j * 8, 8), 8), :] = mixed[row * 8 : (row + 1) * 8, :]
+            turned = tile[pl.ds(piece, LANES, stride=pieces), :].T
+            mixed[pl.ds(part * pieces + piece, LANES, stride=8), :] = turned
+    out_ref[...] = mixed[...].reshape(out_ref.shape)
 
 
 def finish(coded, feed_slot, index, pieces, scale, before):
@@ -499,21 +507,21 @@
     earlier = [] if before is None else [before]
     return pl.pallas_call(
         functools.partial(finish_kernel, scale),
-        grid=(1,),
+        grid=(columns // 8,),
         in_specs=[
             pl.BlockSpec(memory_space=pltpu.SMEM),
-            pl.BlockSpec(coded.shape, lambda i: (0, 0, 0)),
+            pl.BlockSpec(memory_space=pltpu.VMEM),
         ]
         + [pl.BlockSpec(memory_space=pl.ANY)] * len(earlier),
-        out_specs=pl.BlockSpec((rows * columns, LANES), lambda i: (index, 0)),
-        out_shape=jax.ShapeDtypeStruct((pieces * rows * columns, LANES), jnp.float32),
+        out_specs=pl.BlockSpec((rows, 8, LANES), lambda i: (index, i, 0)),
+        out_shape=jax.ShapeDtypeStruct((pieces * rows, columns, LANES), jnp.float32),
         scratch_shapes=[
             pltpu.VMEM((feeds * width // LANES, LANES), jnp.float32),
             pltpu.VMEM((width, LANES), jnp.float32),
             pltpu.VMEM((8 * LANES, LANES), jnp.float32),
         ],
         input_output_aliases={2: 0} if earlier else {},
-        compiler_params=pltpu.CompilerParams(vmem_limit_bytes=22 << 20),
+        compiler_params=pltpu.CompilerParams(vmem_limit_bytes=14 << 20),
         name="finish",
     )(feed_slot, coded, *earlier)
 
@@ -529,7 +537,7 @@
     scales = gains.reshape(2 * ch, count)
     weights = jnp.asarray(filter_weights(ch))
     slots = (feed_slot[:ROWS] - lax.axis_index("feed") * count).reshape(1, ROWS)
-    picked = select_rows(words, scales, slots, total)
+    picked = select_rows(pltpu.with_memory_space_constraint(words, pltpu.HBM), scales, slots, total)
     held = []
 
     def work(after):
@@ -537,13 +545,17 @@
         held.append(own)
         return zero[0, 0]
 
-    sums = [sum_over_feed(value, None if index else work) for index, value in enumerate(picked)]
+    sums, behind = [], None
+    for index, value in enumerate(picked):
+        sums.append(sum_over_feed(value, behind, None if index else work))
+        behind = sums[-1][2]
     own = held[0]
     out, after = None, [sums[-1][0]]
     for index in range(pieces):
         rows = sums[index][1]()
         parts = rows[lines : lines + 4 * ch]
-        coded, done = row_products(rows, parts, own, weights, after)
+        left = row_spectra(rows, parts, weights, ch, spectra)
+        coded, done = row_products(own, left, after)
         after = [done]
         moved = lax.all_to_all(coded, "feed", split_axis=0, concat_axis=0, tiled=True)
         out = finish(moved, feed_slot, index, pieces, 1.0 / spectra, out)

time: 209 us -> 212 us (1.014)
  local copies, waits for them, and re-layouts: 13.3 us -> 5.33 us
  starting transfers between devices: 36.9 us -> 44.5 us
    unnamed x24 -> x18, local copies, waits for them, and re-layouts: 9 us -> 1.13 us
    all_to_all x2, waiting for transfers between devices: 72.8 us -> 79.6 us  [through_rows(): lax.all_to_all(coded, 'feed', split_axis=0, concat_axis=0, tiled=True)]
    ppermute x24, waiting for transfers between devices: 28.6 us -> 22.7 us  [swap(): return lax.ppermute(value, 'feed', pairs)]
    ppermute x24, starting transfers between devices: 24.8 us -> 30.5 us  [swap(): return lax.ppermute(value, 'feed', pairs)]
    pallas_call x1, Pallas kernels: 2.61 us -> 6.85 us  [select_rows(): pl.pallas_call(functools.partial(select_kernel, lines - (STEPS - 1) * blo...]
    pallas_call x4 -> x6, Pallas kernels: 37.5 us -> 35.3 us  [the longest x2 17.1 us: finish(): pl.pallas_call(functools.partial(finish_kernel, scale), grid=(columns //...]
  transfers between devices with their start and end apart: 26 -> 26, of which waited for: 15 -> 14; matrix products, arithmetic and copies ran while one was open for 5% -> 4% of each run, Pallas kernels for 13% -> 13%
where the time goes in v12:
time: 212 us; the launch traced here: 211 us
  waiting for transfers between devices  102 us (48%)
  Pallas kernels  51.2 us (24%)
  starting transfers between devices  44.5 us (21%)
  other arithmetic  6.33 us (3%)
  local copies, waits for them, and re-layouts  5.33 us (3%)
    all_to_all x2, waiting for transfers between devices, through_rows(): lax.all_to_all(coded, 'feed', split_axis=0, concat_axis=0, tiled=True)  79.6 us
    ppermute x24, starting transfers between devices, swap(): return lax.ppermute(value, 'feed', pairs)  30.5 us
    ppermute x24, waiting for transfers between devices, swap(): return lax.ppermute(value, 'feed', pairs)  22.7 us
    pallas_call x2, Pallas kernels, finish(): pl.pallas_call(functools.partial(finish_kernel, scale), grid=(columns //...  17.1 us
    all_to_all x2, starting transfers between devices, through_rows(): lax.all_to_all(coded, 'feed', split_axis=0, concat_axis=0, tiled=True)  14 us
    pallas_call x2, Pallas kernels, row_spectra(): pl.pallas_call(rows_kernel, grid=(spectra // (STEPS * STEP),), in_specs=[...  9.59 us
    pallas_call x1, Pallas kernels, own_spectra(): pl.pallas_call(own_kernel, grid=(steps,), in_specs=[pl.BlockSpec((main, c...  8.99 us
    pallas_call x2, Pallas kernels, row_products(): pl.pallas_call(products_kernel, grid=(ch // each,), in_specs=[pl.BlockSpe...  8.64 us
  transfers between devices with their start and end apart: 26, of which 14 were waited for; matrix products, arithmetic and copies ran while one was open for 4% of the time, Pallas kernels for 13%

profile of v12, /device:TPU:13, one launch (start us, length us, event | category | flops | bytes accessed | tf_op | source)
XLA Modules:
  0.0 211.2 jit_solution(8310237601914047121)
XLA Ops:
  0.0 0.8 shift-right-arithmetic_convert_fusion
  0.9 0.7 slice_subtract_fusion
  1.5 6.8 %select_rows.1 = (bf16[8448,128]{1,0:T(8,128)(2,1)S(1)}, bf16[8448,128]{1,0:T(8,128)(2,1)S(1)}) custom-call(s32[1,256]{1,0:T(1,128)S(1)} %bitcast.20, s32[8304,256]{1,0:T(8,128)} %bitcast.14, bf16[64,256]{1,0:T(8,128)(2,1)S(1)} %pad_maximum_fusion.2.parts_ref), custom_call_target="tpu_custom_call" | custom-call | tf_op jit(solution)/shard_map/select_rows/pallas_call | solution.py:336
  8.4 1.1 constant_dynamic-slice_fusion.6
  9.5 0.7 collective-permute-start.3
  10.3 0.5 collective-permute-start
  10.8 2.1 collective-permute-done.3
  12.9 1.5 dynamic-slice_add_fusion
  14.9 1.1 copy-done.3
  16.0 1.5 dynamic-slice_add_fusion.1
  18.1 1.3 collective-permute-start.7
  19.4 2.9 %collective-permute-done.13 = bf16[1056,128]{1,0:T(8,128)(2,1)S(1)} collective-permute-done((bf16[1056,128]{1,0:T(8,128)(2,1)S(1)}, bf16[1056,128]{1,0:T(8,128)(2,1)S(1)}, u32[]{:S(2)}, u32[]{:S(2)}) %collective-permute-start.13) | collective-permute-done | bytes 270368 | tf_op jit(solution)/shard_map/ppermute | solution.py:353
  22.8 0.9 collective-permute-start.5
  23.7 4.4 %collective-permute-done.1 = bf16[1056,128]{1,0:T(8,128)(2,1)S(1)} collective-permute-done((bf16[1056,128]{1,0:T(8,128)(2,1)S(1)}, bf16[1056,128]{1,0:T(8,128)(2,1)S(1)}, u32[]{:S(2)}, u32[]{:S(2)}) %collective-permute-start.1) | collective-permute-done | bytes 270368 | tf_op jit(solution)/shard_map/ppermute | solution.py:353
  28.1 1.3 collective-permute-start.2
  29.9 3.0 %collective-permute-done.2 = bf16[528,128]{1,0:T(8,128)(2,1)S(1)} collective-permute-done((bf16[528,128]{1,0:T(8,128)(2,1)S(1)}, bf16[528,128]{1,0:T(8,128)(2,1)S(1)}, u32[]{:S(2)}, u32[]{:S(2)}) %collective-permute-start.2) | collective-permute-done | bytes 135200 | tf_op jit(solution)/shard_map/ppermute | solution.py:353
  33.0 2.4 %collective-permute-start.6 = (bf16[528,128]{1,0:T(8,128)(2,1)S(1)}, bf16[528,128]{1,0:T(8,128)(2,1)S(1)}, u32[]{:S(2)}, u32[]{:S(2)}) collective-permute-start(bf16[528,128]{1,0:T(8,128)(2,1)S(1)} %dynamic-slice_add_fusion.7.after_ref), channel_id=1, source_target_pairs={{0,8},{1,9},{2,10},{3,11},{4,12},{5,13},{6,14},{7,15},{8,0},{9,1},... | collective-permute-start | bytes 405512 | tf_op jit(solution)/shard_map/ppermute | solution.py:353
  35.4 0.5 collective-permute-start.9
  35.9 9.0 %own_spectra.1 = (bf16[16,8,256,128]{3,2,1,0:T(8,128)(2,1)S(1)}, bf16[16,128]{1,0:T(8,128)(2,1)S(1)}) custom-call(s32[8304,256]{1,0:T(8,128)S(1)} %bitcast.17, s32[8304,256]{1,0:T(8,128)S(1)} %bitcast.18, f32[32,256]{1,0:T(8,128)S(1)} %bitcast.19, bf16[256,256]{1,0:T(8,128)(2,1)S(1)} %copy-done.4, bf16[528,128]{1,0:T(8,128)(2,1)S(1)} %dynamic-slice_add_fusion.7.after_ref), custom_call_target="tpu_custom_call" | custom-call | flops 4294967296 | bytes 16891904 | tf_op jit(solution)/shard_map/own_spectra/pallas_call | solution.py:280
  44.9 0.5 slice.33
  45.5 1.3 collective-permute-done.9
  46.9 1.0 slice.44
  48.1 0.6 constant_dynamic-update-slice_fusion.9
  48.8 0.5 slice.42
  49.3 0.6 collective-permute-start.19
  51.2 2.1 collective-permute-start.10
  53.7 1.2 collective-permute-start.22
  54.9 1.2 collective-permute-done.10
  56.2 4.4 %collective-permute-start.11 = (bf16[528,128]{1,0:T(8,128)(2,1)S(1)}, bf16[528,128]{1,0:T(8,128)(2,1)S(1)}, u32[]{:S(2)}, u32[]{:S(2)}) collective-permute-start(bf16[528,128]{1,0:T(8,128)(2,1)S(1)} %get-tuple-element.24), channel_id=1, source_target_pairs={{0,4},{1,5},{2,6},{3,7},{4,0},{5,1},{6,2},{7,3},{8,12},{9,13},{10,... | collective-permute-start | bytes 405512 | tf_op jit(solution)/shard_map/ppermute | solution.py:353
  61.0 1.5 collective-permute-start.16
  62.8 2.5 %collective-permute-done.16 = bf16[528,128]{1,0:T(8,128)(2,1)S(1)} collective-permute-done((bf16[528,128]{1,0:T(8,128)(2,1)S(1)}, bf16[528,128]{1,0:T(8,128)(2,1)S(1)}, u32[]{:S(2)}, u32[]{:S(2)}) %collective-permute-start.16) | collective-permute-done | bytes 135200 | tf_op jit(solution)/shard_map/ppermute | solution.py:353
  65.3 4.1 %collective-permute-start.17 = (bf16[1056,128]{1,0:T(8,128)(2,1)S(1)}, bf16[1056,128]{1,0:T(8,128)(2,1)S(1)}, u32[]{:S(2)}, u32[]{:S(2)}) collective-permute-start(bf16[1056,128]{1,0:T(8,128)(2,1)S(1)} %constant_dynamic-update-slice_fusion.14), channel_id=1, source_target_pairs={{0,4},{1,5},{2,6},{3,7},{4,0},{5,1},{6,2},{7,3},{8,12},{9,13},{10,... | collective-permute-start | bytes 811016 | tf_op jit(solution)/shard_map/ppermute | solution.py:353
  69.4 0.5 collective-permute-done.11
  70.0 1.2 collective-permute-start.12
  71.6 5.2 %collective-permute-start.23 = (bf16[4224,128]{1,0:T(8,128)(2,1)S(1)}, bf16[4224,128]{1,0:T(8,128)(2,1)S(1)}, u32[]{:S(2)}, u32[]{:S(2)}) collective-permute-start(bf16[4224,128]{1,0:T(8,128)(2,1)S(1)} %get-tuple-element.27), channel_id=1, source_target_pairs={{0,1},{1,0},{2,3},{3,2},{4,5},{5,4},{6,7},{7,6},{8,9},{9,8},{10,11... | collective-permute-start | bytes 3244040 | tf_op jit(solution)/shard_map/ppermute | solution.py:353
  76.9 0.5 collective-permute-done.12
  77.6 1.5 collective-permute-done.23
  79.3 4.8 %row_spectra.3.left_ref = bf16[16,1024,256]{2,1,0:T(8,128)(2,1)S(1)} custom-call(bf16[8448,128]{1,0:T(8,128)(2,1)S(1)} %constant_dynamic-update-slice_fusion.main_ref.next_ref, bf16[8448,128]{1,0:T(8,128)(2,1)S(1)} %constant_dynamic-update-slice_fusion.main_ref.next_ref, bf16[64,128]{1,0:T(8,128)(2,1)S(1)} %slice.47.parts_ref, bf16[256,256]{1,0:T(8,128)(2,1)S(1)} %copy-done.4), custom_call_target="tpu_custom_call" | custom-call | flops 2147483648 | bytes 10551296 | tf_op jit(solution)/shard_map/row_spectra/pallas_call | solution.py:410
  84.1 4.3 %row_products.2 = (s16[16,272,256]{2,1,0:T(8,128)(2,1)}, bf16[16,128]{1,0:T(8,128)(2,1)S(1)}) custom-call(bf16[16,8,256,128]{3,2,1,0:T(8,128)(2,1)S(1)} %get-tuple-element.13.own_ref, bf16[16,1024,256]{2,1,0:T(8,128)(2,1)S(1)} %row_spectra.3.left_ref, bf16[4224,128]{1,0:T(8,128)(2,1)S(1)} %get-tuple-element.29.refs_0_), custom_call_target="tpu_custom_call" | custom-call | flops 2147483648 | bytes 16777216 | tf_op jit(solution)/shard_map/row_products/pallas_call | solution.py:452
  88.5 9.0 %all-to-all-start.1 = ((s16[16,272,256]{2,1,0:T(8,128)(2,1)}), s16[16,272,256]{2,1,0:T(8,128)(2,1)}, u32[]{:S(2)}, u32[]{:S(2)}) async-start(s16[16,272,256]{2,1,0:T(8,128)(2,1)} %get-tuple-element.18), calls=%async_computation.1 | async-start | bytes 4456448 | tf_op jit(solution)/shard_map/all_to_all | solution.py:560
  97.8 2.4 %collective-permute-done.18 = bf16[4224,128]{1,0:T(8,128)(2,1)S(1)} collective-permute-done((bf16[4224,128]{1,0:T(8,128)(2,1)S(1)}, bf16[4224,128]{1,0:T(8,128)(2,1)S(1)}, u32[]{:S(2)}, u32[]{:S(2)}) %collective-permute-start.18) | collective-permute-done | bytes 1081376 | tf_op jit(solution)/shard_map/ppermute | solution.py:353
  100.4 4.8 %row_spectra.2.left_ref = bf16[16,1024,256]{2,1,0:T(8,128)(2,1)S(1)} custom-call(bf16[8448,128]{1,0:T(8,128)(2,1)S(1)} %constant_dynamic-update-slice_fusion.10.main_ref.next_ref, bf16[8448,128]{1,0:T(8,128)(2,1)S(1)} %constant_dynamic-update-slice_fusion.10.main_ref.next_ref, bf16[64,128]{1,0:T(8,128)(2,1)S(1)} %slice.46.parts_ref, ...), custom_call_target="tpu_custom_call" | custom-call | flops 2147483648 | bytes 10551296 | tf_op jit(solution)/shard_map/row_spectra/pallas_call | solution.py:410
  105.2 4.3 %row_products.3 = (s16[16,272,256]{2,1,0:T(8,128)(2,1)}, bf16[16,128]{1,0:T(8,128)(2,1)}) custom-call(bf16[16,8,256,128]{3,2,1,0:T(8,128)(2,1)S(1)} %copy-done.1, bf16[16,1024,256]{2,1,0:T(8,128)(2,1)S(1)} %row_spectra.2.left_ref, bf16[16,128]{1,0:T(8,128)(2,1)S(1)} %get-tuple-element.16.refs_0_), custom_call_target="tpu_custom_call" | custom-call | flops 2147483648 | bytes 16777216 | tf_op jit(solution)/shard_map/row_products/pallas_call | solution.py:452
  109.5 38.3 %all-to-all-done.1.coded_ref = s16[16,272,256]{2,1,0:T(8,128)(2,1)} async-done(((s16[16,272,256]{2,1,0:T(8,128)(2,1)}), s16[16,272,256]{2,1,0:T(8,128)(2,1)}, u32[]{:S(2)}, u32[]{:S(2)}) %all-to-all-start.1) | async-done | bytes 2228256 | tf_op jit(solution)/shard_map/all_to_all | solution.py:560
  147.8 5.0 %all-to-all-start = ((s16[16,272,256]{2,1,0:T(8,128)(2,1)}), s16[16,272,256]{2,1,0:T(8,128)(2,1)S(1)}, u32[]{:S(2)}, u32[]{:S(2)}) async-start(s16[16,272,256]{2,1,0:T(8,128)(2,1)} %get-tuple-element.17), calls=%async_computation | async-start | bytes 4456448 | tf_op jit(solution)/shard_map/all_to_all | solution.py:560
  152.8 9.0 %finish.2.refs_0_ = f32[256,64,128]{2,1,0:T(8,128)} custom-call(s32[4096]{0:T(1024)S(1)} %copy-done.5, s16[16,272,256]{2,1,0:T(8,128)(2,1)} %all-to-all-done.1.coded_ref), custom_call_target="tpu_custom_call" | custom-call | tf_op jit(solution)/shard_map/finish/pallas_call | solution.py:508
  161.8 41.2 %all-to-all-done.coded_ref = s16[16,272,256]{2,1,0:T(8,128)(2,1)S(1)} async-done(((s16[16,272,256]{2,1,0:T(8,128)(2,1)}), s16[16,272,256]{2,1,0:T(8,128)(2,1)S(1)}, u32[]{:S(2)}, u32[]{:S(2)}) %all-to-all-start) | async-done | bytes 2228256 | tf_op jit(solution)/shard_map/all_to_all | solution.py:560
  203.1 8.1 %finish.3 = f32[256,64,128]{2,1,0:T(8,128)} custom-call(s32[4096]{0:T(1024)S(1)} %copy-done.5, s16[16,272,256]{2,1,0:T(8,128)(2,1)S(1)} %all-to-all-done.coded_ref, f32[256,64,128]{2,1,0:T(8,128)} %finish.2.refs_0_), custom_call_target="tpu_custom_call", output_to_operand_aliasing={{}: (2, {})} | custom-call | tf_op jit(solution)/shard_map/finish/pallas_call | solution.py:508
  (81 shorter events, 5.2 us)
Async XLA Ops:
  8.4 1.9 copy-start.2
  8.4 27.5 %slice-start = ((s8[8503296]{0:T(1024)(128)(4,1)}), s8[114688]{0:T(1024)(128)(4,1)S(1)}, s32[]{:S(2)}) async-start(s8[8503296]{0:T(1024)(128)(4,1)} %bitcast.15), calls=%async_computation.2 | async-start | bytes 229376
  9.5 3.3 %collective-permute-start.3 = (bf16[4224,128]{1,0:T(8,128)(2,1)}, bf16[4224,128]{1,0:T(8,128)(2,1)}, u32[]{:S(2)}, u32[]{:S(2)}) collective-permute-start(bf16[4224,128]{1,0:T(8,128)(2,1)} %constant_dynamic-slice_fusion.6), channel_id=1, source_target_pairs={{0,1},{1,0},{2,3},{3,2},{4,5},{5,4},{6,7},{7,6},{8,9},{9,8},{10,11... | collective-permute-start | bytes 3244040 | tf_op jit(solution)/shard_map/ppermute | solution.py:353
  10.3 4.7 %collective-permute-start = (bf16[4224,128]{1,0:T(8,128)(2,1)S(1)}, bf16[4224,128]{1,0:T(8,128)(2,1)}, u32[]{:S(2)}, u32[]{:S(2)}) collective-permute-start(bf16[4224,128]{1,0:T(8,128)(2,1)S(1)} %constant_dynamic-slice_fusion.9), channel_id=1, source_target_pairs={{0,1},{1,0},{2,3},{3,2},{4,5},{5,4},{6,7},{7,6},{8,9},{9,8},{10,11... | collective-permute-start | bytes 3244040 | tf_op jit(solution)/shard_map/ppermute | solution.py:353
  10.8 25.1 %slice-start.1 = ((s8[8503296]{0:T(1024)(128)(4,1)}), s8[4194304]{0:T(1024)(128)(4,1)S(1)}, s32[]{:S(2)}) async-start(s8[8503296]{0:T(1024)(128)(4,1)} %bitcast.15), calls=%async_computation.3 | async-start | bytes 8388608
  14.4 1.6 copy-start.3
  14.5 7.8 %collective-permute-start.13 = (bf16[1056,128]{1,0:T(8,128)(2,1)S(1)}, bf16[1056,128]{1,0:T(8,128)(2,1)S(1)}, u32[]{:S(2)}, u32[]{:S(2)}) collective-permute-start(bf16[1056,128]{1,0:T(8,128)(2,1)S(1)} %constant_dynamic-slice_fusion.1), channel_id=1, source_target_pairs={{0,4},{1,5},{2,6},{3,7},{4,0},{5,1},{6,2},{7,3},{8,12},{9,13},{10,... | collective-permute-start | bytes 811016 | tf_op jit(solution)/shard_map/ppermute | solution.py:353
  14.8 7.9 %collective-permute-start.4 = (bf16[1056,128]{1,0:T(8,128)(2,1)S(1)}, bf16[1056,128]{1,0:T(8,128)(2,1)S(1)}, u32[]{:S(2)}, u32[]{:S(2)}) collective-permute-start(bf16[1056,128]{1,0:T(8,128)(2,1)S(1)} %constant_dynamic-slice_fusion.5), channel_id=1, source_target_pairs={{0,2},{1,3},{2,0},{3,1},{4,6},{5,7},{6,4},{7,5},{8,10},{9,11},{10,... | collective-permute-start | bytes 811016 | tf_op jit(solution)/shard_map/ppermute | solution.py:353
  17.5 18.4 %slice-start.2 = ((s8[8503296]{0:T(1024)(128)(4,1)}), s8[4194304]{0:T(1024)(128)(4,1)S(1)}, s32[]{:S(2)}) async-start(s8[8503296]{0:T(1024)(128)(4,1)} %bitcast.15), calls=%async_computation.4 | async-start | bytes 8388608
  17.6 10.4 %collective-permute-start.1 = (bf16[1056,128]{1,0:T(8,128)(2,1)S(1)}, bf16[1056,128]{1,0:T(8,128)(2,1)S(1)}, u32[]{:S(2)}, u32[]{:S(2)}) collective-permute-start(bf16[1056,128]{1,0:T(8,128)(2,1)S(1)} %constant_dynamic-slice_fusion.8), channel_id=1, source_target_pairs={{0,2},{1,3},{2,0},{3,1},{4,6},{5,7},{6,4},{7,5},{8,10},{9,11},{10,... | collective-permute-start | bytes 811016 | tf_op jit(solution)/shard_map/ppermute | solution.py:353
  18.1 11.4 %collective-permute-start.7 = (bf16[1056,128]{1,0:T(8,128)(2,1)S(1)}, bf16[1056,128]{1,0:T(8,128)(2,1)S(1)}, u32[]{:S(2)}, u32[]{:S(2)}) collective-permute-start(bf16[1056,128]{1,0:T(8,128)(2,1)S(1)} %constant_dynamic-slice_fusion.3), channel_id=1, source_target_pairs={{0,4},{1,5},{2,6},{3,7},{4,0},{5,1},{6,2},{7,3},{8,12},{9,13},{10,... | collective-permute-start | bytes 811016 | tf_op jit(solution)/shard_map/ppermute | solution.py:353
  22.3 13.6 %copy-start.4 = (bf16[256,256]{1,0:T(8,128)(2,1)S(1)}, bf16[256,256]{1,0:T(8,128)(2,1)}, u32[]{:S(2)}) copy-start(bf16[256,256]{1,0:T(8,128)(2,1)} %constant.225.clone.weights_ref) | copy-start | bytes 393220
  22.4 30.9 %collective-permute-start.14 = (bf16[528,128]{1,0:T(8,128)(2,1)S(1)}, bf16[528,128]{1,0:T(8,128)(2,1)S(1)}, u32[]{:S(2)}, u32[]{:S(2)}) collective-permute-start(bf16[528,128]{1,0:T(8,128)(2,1)S(1)} %constant_dynamic-slice_fusion), channel_id=1, source_target_pairs={{0,2},{1,3},{2,0},{3,1},{4,6},{5,7},{6,4},{7,5},{8,10},{9,11},{10,... | collective-permute-start | bytes 405512 | tf_op jit(solution)/shard_map/ppermute | solution.py:353
  22.8 28.3 %collective-permute-start.5 = (bf16[528,128]{1,0:T(8,128)(2,1)S(1)}, bf16[528,128]{1,0:T(8,128)(2,1)S(1)}, u32[]{:S(2)}, u32[]{:S(2)}) collective-permute-start(bf16[528,128]{1,0:T(8,128)(2,1)S(1)} %constant_dynamic-slice_fusion.4), channel_id=1, source_target_pairs={{0,4},{1,5},{2,6},{3,7},{4,0},{5,1},{6,2},{7,3},{8,12},{9,13},{10,... | collective-permute-start | bytes 405512 | tf_op jit(solution)/shard_map/ppermute | solution.py:353
  28.1 4.8 %collective-permute-start.2 = (bf16[528,128]{1,0:T(8,128)(2,1)S(1)}, bf16[528,128]{1,0:T(8,128)(2,1)S(1)}, u32[]{:S(2)}, u32[]{:S(2)}) collective-permute-start(bf16[528,128]{1,0:T(8,128)(2,1)S(1)} %constant_dynamic-slice_fusion.7), channel_id=1, source_target_pairs={{0,4},{1,5},{2,6},{3,7},{4,0},{5,1},{6,2},{7,3},{8,12},{9,13},{10,... | collective-permute-start | bytes 405512 | tf_op jit(solution)/shard_map/ppermute | solution.py:353
  29.6 5.8 %collective-permute-start.8 = (bf16[528,128]{1,0:T(8,128)(2,1)S(1)}, bf16[528,128]{1,0:T(8,128)(2,1)S(1)}, u32[]{:S(2)}, u32[]{:S(2)}) collective-permute-start(bf16[528,128]{1,0:T(8,128)(2,1)S(1)} %constant_dynamic-slice_fusion.2), channel_id=1, source_target_pairs={{0,2},{1,3},{2,0},{3,1},{4,6},{5,7},{6,4},{7,5},{8,10},{9,11},{10,... | collective-permute-start | bytes 405512 | tf_op jit(solution)/shard_map/ppermute | solution.py:353
  33.0 15.2 %collective-permute-start.6 = (bf16[528,128]{1,0:T(8,128)(2,1)S(1)}, bf16[528,128]{1,0:T(8,128)(2,1)S(1)}, u32[]{:S(2)}, u32[]{:S(2)}) collective-permute-start(bf16[528,128]{1,0:T(8,128)(2,1)S(1)} %dynamic-slice_add_fusion.7.after_ref), channel_id=1, source_target_pairs={{0,8},{1,9},{2,10},{3,11},{4,12},{5,13},{6,14},{7,15},{8,0},{9,1},... | collective-permute-start | bytes 405512 | tf_op jit(solution)/shard_map/ppermute | solution.py:353
  35.4 11.4 %collective-permute-start.9 = (bf16[528,128]{1,0:T(8,128)(2,1)S(1)}, bf16[528,128]{1,0:T(8,128)(2,1)S(1)}, u32[]{:S(2)}, u32[]{:S(2)}) collective-permute-start(bf16[528,128]{1,0:T(8,128)(2,1)S(1)} %dynamic-slice_add_fusion.6), channel_id=1, source_target_pairs={{0,8},{1,9},{2,10},{3,11},{4,12},{5,13},{6,14},{7,15},{8,0},{9,1},... | collective-permute-start | bytes 405512 | tf_op jit(solution)/shard_map/ppermute | solution.py:353
  44.9 39.2 %copy-start = (bf16[16,8,256,128]{3,2,1,0:T(8,128)(2,1)}, bf16[16,8,256,128]{3,2,1,0:T(8,128)(2,1)S(1)}, u32[]{:S(2)}) copy-start(bf16[16,8,256,128]{3,2,1,0:T(8,128)(2,1)S(1)} %get-tuple-element.13.own_ref) | copy-start | bytes 25165828
  47.9 5.8 %collective-permute-start.21 = (bf16[528,128]{1,0:T(8,128)(2,1)S(1)}, bf16[528,128]{1,0:T(8,128)(2,1)S(1)}, u32[]{:S(2)}, u32[]{:S(2)}) collective-permute-start(bf16[528,128]{1,0:T(8,128)(2,1)S(1)} %get-tuple-element.22), channel_id=1, source_target_pairs={{0,2},{1,3},{2,0},{3,1},{4,6},{5,7},{6,4},{7,5},{8,10},{9,11},{10,... | collective-permute-start | bytes 405512 | tf_op jit(solution)/shard_map/ppermute | solution.py:353
  49.3 13.3 %collective-permute-start.19 = (bf16[528,128]{1,0:T(8,128)(2,1)S(1)}, bf16[528,128]{1,0:T(8,128)(2,1)S(1)}, u32[]{:S(2)}, u32[]{:S(2)}) collective-permute-start(bf16[528,128]{1,0:T(8,128)(2,1)S(1)} %get-tuple-element.20), channel_id=1, source_target_pairs={{0,4},{1,5},{2,6},{3,7},{4,0},{5,1},{6,2},{7,3},{8,12},{9,13},{10,... | collective-permute-start | bytes 405512 | tf_op jit(solution)/shard_map/ppermute | solution.py:353
  51.2 4.9 %collective-permute-start.10 = (bf16[528,128]{1,0:T(8,128)(2,1)S(1)}, bf16[528,128]{1,0:T(8,128)(2,1)S(1)}, u32[]{:S(2)}, u32[]{:S(2)}) collective-permute-start(bf16[528,128]{1,0:T(8,128)(2,1)S(1)} %add_add_fusion.2), channel_id=1, source_target_pairs={{0,8},{1,9},{2,10},{3,11},{4,12},{5,13},{6,14},{7,15},{8,0},{9,1},... | collective-permute-start | bytes 405512 | tf_op jit(solution)/shard_map/ppermute | solution.py:353
  53.3 7.7 %collective-permute-start.15 = (bf16[528,128]{1,0:T(8,128)(2,1)S(1)}, bf16[528,128]{1,0:T(8,128)(2,1)S(1)}, u32[]{:S(2)}, u32[]{:S(2)}) collective-permute-start(bf16[528,128]{1,0:T(8,128)(2,1)S(1)} %add_add_fusion), channel_id=1, source_target_pairs={{0,8},{1,9},{2,10},{3,11},{4,12},{5,13},{6,14},{7,15},{8,0},{9,1},... | collective-permute-start | bytes 405512 | tf_op jit(solution)/shard_map/ppermute | solution.py:353
  53.7 17.5 %collective-permute-start.22 = (bf16[1056,128]{1,0:T(8,128)(2,1)S(1)}, bf16[1056,128]{1,0:T(8,128)(2,1)S(1)}, u32[]{:S(2)}, u32[]{:S(2)}) collective-permute-start(bf16[1056,128]{1,0:T(8,128)(2,1)S(1)} %constant_dynamic-update-slice_fusion.4), channel_id=1, source_target_pairs={{0,4},{1,5},{2,6},{3,7},{4,0},{5,1},{6,2},{7,3},{8,12},{9,13},{10,... | collective-permute-start | bytes 811016 | tf_op jit(solution)/shard_map/ppermute | solution.py:353
  56.2 13.8 %collective-permute-start.11 = (bf16[528,128]{1,0:T(8,128)(2,1)S(1)}, bf16[528,128]{1,0:T(8,128)(2,1)S(1)}, u32[]{:S(2)}, u32[]{:S(2)}) collective-permute-start(bf16[528,128]{1,0:T(8,128)(2,1)S(1)} %get-tuple-element.24), channel_id=1, source_target_pairs={{0,4},{1,5},{2,6},{3,7},{4,0},{5,1},{6,2},{7,3},{8,12},{9,13},{10,... | collective-permute-start | bytes 405512 | tf_op jit(solution)/shard_map/ppermute | solution.py:353
  61.0 4.2 %collective-permute-start.16 = (bf16[528,128]{1,0:T(8,128)(2,1)S(1)}, bf16[528,128]{1,0:T(8,128)(2,1)S(1)}, u32[]{:S(2)}, u32[]{:S(2)}) collective-permute-start(bf16[528,128]{1,0:T(8,128)(2,1)S(1)} %get-tuple-element.26), channel_id=1, source_target_pairs={{0,2},{1,3},{2,0},{3,1},{4,6},{5,7},{6,4},{7,5},{8,10},{9,11},{10,... | collective-permute-start | bytes 405512 | tf_op jit(solution)/shard_map/ppermute | solution.py:353
  62.6 8.7 %collective-permute-start.20 = (bf16[1056,128]{1,0:T(8,128)(2,1)S(1)}, bf16[1056,128]{1,0:T(8,128)(2,1)S(1)}, u32[]{:S(2)}, u32[]{:S(2)}) collective-permute-start(bf16[1056,128]{1,0:T(8,128)(2,1)S(1)} %constant_dynamic-update-slice_fusion.8), channel_id=1, source_target_pairs={{0,2},{1,3},{2,0},{3,1},{4,6},{5,7},{6,4},{7,5},{8,10},{9,11},{10,... | collective-permute-start | bytes 811016 | tf_op jit(solution)/shard_map/ppermute | solution.py:353
  65.3 11.6 %collective-permute-start.17 = (bf16[1056,128]{1,0:T(8,128)(2,1)S(1)}, bf16[1056,128]{1,0:T(8,128)(2,1)S(1)}, u32[]{:S(2)}, u32[]{:S(2)}) collective-permute-start(bf16[1056,128]{1,0:T(8,128)(2,1)S(1)} %constant_dynamic-update-slice_fusion.14), channel_id=1, source_target_pairs={{0,4},{1,5},{2,6},{3,7},{4,0},{5,1},{6,2},{7,3},{8,12},{9,13},{10,... | collective-permute-start | bytes 811016 | tf_op jit(solution)/shard_map/ppermute | solution.py:353
  70.0 7.3 %collective-permute-start.12 = (bf16[1056,128]{1,0:T(8,128)(2,1)S(1)}, bf16[1056,128]{1,0:T(8,128)(2,1)S(1)}, u32[]{:S(2)}, u32[]{:S(2)}) collective-permute-start(bf16[1056,128]{1,0:T(8,128)(2,1)S(1)} %constant_dynamic-update-slice_fusion.18), channel_id=1, source_target_pairs={{0,2},{1,3},{2,0},{3,1},{4,6},{5,7},{6,4},{7,5},{8,10},{9,11},{10,... | collective-permute-start | bytes 811016 | tf_op jit(solution)/shard_map/ppermute | solution.py:353
  71.6 7.6 %collective-permute-start.23 = (bf16[4224,128]{1,0:T(8,128)(2,1)S(1)}, bf16[4224,128]{1,0:T(8,128)(2,1)S(1)}, u32[]{:S(2)}, u32[]{:S(2)}) collective-permute-start(bf16[4224,128]{1,0:T(8,128)(2,1)S(1)} %get-tuple-element.27), channel_id=1, source_target_pairs={{0,1},{1,0},{2,3},{3,2},{4,5},{5,4},{6,7},{7,6},{8,9},{9,8},{10,11... | collective-permute-start | bytes 3244040 | tf_op jit(solution)/shard_map/ppermute | solution.py:353
  88.5 59.3 %all-to-all-start.1 = ((s16[16,272,256]{2,1,0:T(8,128)(2,1)}), s16[16,272,256]{2,1,0:T(8,128)(2,1)}, u32[]{:S(2)}, u32[]{:S(2)}) async-start(s16[16,272,256]{2,1,0:T(8,128)(2,1)} %get-tuple-element.18), calls=%async_computation.1 | async-start | bytes 4456448 | tf_op jit(solution)/shard_map/all_to_all | solution.py:560
  97.5 2.8 %collective-permute-start.18 = (bf16[4224,128]{1,0:T(8,128)(2,1)S(1)}, bf16[4224,128]{1,0:T(8,128)(2,1)S(1)}, u32[]{:S(2)}, u32[]{:S(2)}) collective-permute-start(bf16[4224,128]{1,0:T(8,128)(2,1)S(1)} %get-tuple-element.29.refs_0_), channel_id=1, source_target_pairs={{0,1},{1,0},{2,3},{3,2},{4,5},{5,4},{6,7},{7,6},{8,9},{9,8},{10,11... | collective-permute-start | bytes 3244040 | tf_op jit(solution)/shard_map/ppermute | solution.py:353
  100.4 4.8 %copy-start.1 = (bf16[16,8,256,128]{3,2,1,0:T(8,128)(2,1)S(1)}, bf16[16,8,256,128]{3,2,1,0:T(8,128)(2,1)}, u32[]{:S(2)}) copy-start(bf16[16,8,256,128]{3,2,1,0:T(8,128)(2,1)} %copy-done) | copy-start | bytes 25165828
  147.8 5.0 %copy-start.5 = (s32[4096]{0:T(1024)S(1)}, s32[4096]{0:T(1024)}, u32[]{:S(2)}) copy-start(s32[4096]{0:T(1024)} %slot_ref.3) | copy-start | bytes 49156
  147.8 55.2 %all-to-all-start = ((s16[16,272,256]{2,1,0:T(8,128)(2,1)}), s16[16,272,256]{2,1,0:T(8,128)(2,1)S(1)}, u32[]{:S(2)}, u32[]{:S(2)}) async-start(s16[16,272,256]{2,1,0:T(8,128)(2,1)} %get-tuple-element.17), calls=%async_computation | async-start | bytes 4456448 | tf_op jit(solution)/shard_map/all_to_all | solution.py:560

commit v13 on v12

--- a/solution.py
+++ b/solution.py
@@ -201,6 +201,7 @@
 SPAN = 16
 STEPS = 8
 RANGE = 14
+EXTRA = 8
 
 
 def filter_weights(ch):
@@ -308,44 +309,46 @@
     )(words, words, gains, weights, after)
 
 
-def select_kernel(last_rows, slots_ref, words_ref, parts_ref, *outs):
+def select_kernel(last_rows, place_ref, slots_ref, words_ref, gains_ref, *outs):
     step = pl.program_id(0)
-    count, rows = words_ref.shape[1], slots_ref.shape[1]
+    count, rows = words_ref.shape[1], len(outs) * LANES
     words = words_ref[...].astype(jnp.float32).astype(jnp.bfloat16)
-    place = lax.broadcasted_iota(jnp.int32, (count, rows), 0)
-    choice = jnp.where(slots_ref[...] == place, 1.0, 0.0).astype(jnp.bfloat16)
+    place = lax.broadcasted_iota(jnp.int32, (count, rows), 0) + place_ref[0] * count
+    slots = jnp.concatenate([slots_ref[index : index + 1, :] for index in range(len(outs))], axis=1)
+    choice = jnp.where(slots == place, 1.0, 0.0).astype(jnp.bfloat16)
     taken = jnp.dot(words, choice, preferred_element_type=jnp.float32).astype(outs[0].dtype)
     for index, out_ref in enumerate(outs):
         out_ref[...] = taken[:, index * LANES : (index + 1) * LANES]
 
     @pl.when(step == pl.num_programs(0) - 1)
     def _():
-        extra = parts_ref.shape[0]
-        gains = jnp.dot(parts_ref[...], choice, preferred_element_type=jnp.float32).astype(outs[0].dtype)
+        gains = gains_ref[...]
+        parts = jnp.concatenate([gains >> 4, gains & 15], axis=0).astype(jnp.float32).astype(jnp.bfloat16)
+        extra = parts.shape[0]
+        gains = jnp.dot(parts, choice, preferred_element_type=jnp.float32).astype(outs[0].dtype)
         for index, out_ref in enumerate(outs):
             out_ref[last_rows : last_rows + extra, :] = gains[:, index * LANES : (index + 1) * LANES]
             left = out_ref.shape[0] - last_rows - extra
             out_ref[last_rows + extra :, :] = jnp.zeros((left, LANES), out_ref.dtype)
 
 
-def select_rows(words, gains, slots, total):
+def select_rows(place, words, gains, slots, rows, total):
     lines, count = words.shape
-    rows = slots.shape[1]
     block = total // STEPS
-    parts = jnp.concatenate([gains >> 4, gains & 15], axis=0).astype(jnp.bfloat16)
     return pl.pallas_call(
         functools.partial(select_kernel, lines - (STEPS - 1) * block),
         grid=(STEPS,),
         in_specs=[
-            pl.BlockSpec((1, rows), lambda i: (0, 0)),
+            pl.BlockSpec(memory_space=pltpu.SMEM),
+            pl.BlockSpec((8, LANES), lambda i: (0, 0)),
             pl.BlockSpec((block, count), lambda i: (i, 0)),
-            pl.BlockSpec(parts.shape, lambda i: (0, 0)),
+            pl.BlockSpec(gains.shape, lambda i: (0, 0)),
         ],
         out_specs=[pl.BlockSpec((block, LANES), lambda i: (i, 0))] * (rows // LANES),
         out_shape=[jax.ShapeDtypeStruct((total, LANES), jnp.bfloat16)] * (rows // LANES),
         compiler_params=pltpu.CompilerParams(vmem_limit_bytes=8 << 20),
         name="select_rows",
-    )(slots, words, parts)
+    )(place, slots, words, gains)
 
 
 def swap(value, bit):
@@ -371,22 +374,19 @@
     return lax.dynamic_update_slice_in_dim(buffer, other, (1 - side(bit)) * size, 0)
 
 
-def sum_over_feed(value, behind=None, work=None):
+def sum_over_feed(value, work=None):
     half = reduce_half(value, 1)
     size = half.shape[0] // 2
     left, right = half[:size], half[size:]
     left_1, right_1 = reduce_half(left, 2), reduce_half(right, 4)
     left_2, right_2 = reduce_half(left_1, 4), reduce_half(right_1, 2)
-    if behind is not None:
-        left_2, right_2 = left_2 + behind, right_2 + behind
     left_3, right_3 = left_2 + swap(left_2, 8), right_2 + swap(right_2, 8)
     if work is not None:
         left_3 = left_3 + work(left_2)
-    crossed = (left_3[0, 0] + right_3[0, 0]) * 0
     left_1, right_1 = gather_half(left_3, 4, left_1), gather_half(right_3, 2, right_1)
     left, right = gather_half(left_1, 2, left), gather_half(right_1, 4, right)
     half = jnp.concatenate([left, right], axis=0)
-    return half, lambda: gather_half(half, 1, value), crossed
+    return half, lambda: gather_half(half, 1, value)
 
 
 def rows_kernel(main_ref, next_ref, parts_ref, weights_ref, out_ref):
@@ -454,11 +454,11 @@
         grid=(ch // each,),
         in_specs=[pl.BlockSpec(memory_space=pltpu.VMEM)] * 2 + [pl.BlockSpec(memory_space=pl.ANY)] * len(after),
         out_specs=[
-            pl.BlockSpec((each, count + 16, columns), lambda i: (i, 0, 0)),
+            pl.BlockSpec((each, count + EXTRA, columns), lambda i: (i, 0, 0)),
             pl.BlockSpec((16, LANES), lambda i: (0, 0)),
         ],
         out_shape=[
-            pltpu.HBM((ch, count + 16, columns), jnp.int16),
+            pltpu.HBM((ch, count + EXTRA, columns), jnp.int16),
             jax.ShapeDtypeStruct((16, LANES), jnp.bfloat16),
         ],
         compiler_params=pltpu.CompilerParams(vmem_limit_bytes=10 << 20),
@@ -473,14 +473,14 @@
     out_ref, products, tile, mixed = refs[-4:]
     step = pl.program_id(0)
     sources, lines, width = coded_ref.shape
-    count = lines - 16
+    count = lines - EXTRA
     pieces = width // LANES
     together = 8 // pieces
 
     @pl.when(step == 0)
     def _():
         for source in range(sources):
-            power = coded_ref[source, count : count + 16, :][:1].astype(jnp.float32)
+            power = coded_ref[source, count:, :][:1].astype(jnp.float32)
             values = coded_ref[source, :count, :].astype(jnp.float32) * (jnp.exp2(power - RANGE) * scale)
             for piece in range(pieces):
                 products[pl.ds(source * count * pieces + piece, count, stride=pieces), :] = values[
@@ -489,20 +489,18 @@
 
     for part in range(together):
         for i in range(LANES):
-            slot = slot_ref[(step * together + part) * LANES + i]
-            tile[i * pieces : (i + 1) * pieces, :] = products[
-                pl.ds(pl.multiple_of(slot * pieces, pieces), pieces), :
-            ]
+            line = slot_ref[(step * together + part) * LANES + i]
+            tile[i * pieces : (i + 1) * pieces, :] = products[pl.ds(pl.multiple_of(line, pieces), pieces), :]
         for piece in range(pieces):
             turned = tile[pl.ds(piece, LANES, stride=pieces), :].T
             mixed[pl.ds(part * pieces + piece, LANES, stride=8), :] = turned
     out_ref[...] = mixed[...].reshape(out_ref.shape)
 
 
-def finish(coded, feed_slot, index, pieces, scale, before):
+def finish(coded, places, index, pieces, scale, before):
     sources, lines, width = coded.shape
     rows = width // 2
-    feeds = sources * (lines - 16)
+    feeds = sources * (lines - EXTRA)
     columns = 2 * (feeds // LANES)
     earlier = [] if before is None else [before]
     return pl.pallas_call(
@@ -523,7 +521,7 @@
         input_output_aliases={2: 0} if earlier else {},
         compiler_params=pltpu.CompilerParams(vmem_limit_bytes=14 << 20),
         name="finish",
-    )(feed_slot, coded, *earlier)
+    )(places, coded, *earlier)
 
 
 def through_rows(samples, gains, feed_slot):
@@ -536,8 +534,8 @@
     words = jnp.transpose(samples, (2, 1, 0)).reshape(lines, count)
     scales = gains.reshape(2 * ch, count)
     weights = jnp.asarray(filter_weights(ch))
-    slots = (feed_slot[:ROWS] - lax.axis_index("feed") * count).reshape(1, ROWS)
-    picked = select_rows(pltpu.with_memory_space_constraint(words, pltpu.HBM), scales, slots, total)
+    place = lax.axis_index("feed").reshape(1)
+    picked = select_rows(place, words, scales, feed_slot.reshape(-1, LANES), ROWS, total)
     held = []
 
     def work(after):
@@ -545,10 +543,7 @@
         held.append(own)
         return zero[0, 0]
 
-    sums, behind = [], None
-    for index, value in enumerate(picked):
-        sums.append(sum_over_feed(value, behind, None if index else work))
-        behind = sums[-1][2]
+    sums = [sum_over_feed(value, None if index else work) for index, value in enumerate(picked)]
     own = held[0]
     out, after = None, [sums[-1][0]]
     for index in range(pieces):
@@ -558,7 +553,7 @@
         coded, done = row_products(own, left, after)
         after = [done]
         moved = lax.all_to_all(coded, "feed", split_axis=0, concat_axis=0, tiled=True)
-        out = finish(moved, feed_slot, index, pieces, 1.0 / spectra, out)
+        out = finish(moved, feed_slot * 2, index, pieces, 1.0 / spectra, out)
     feeds = feed_slot.shape[0]
     out = out.reshape(ROWS, feeds // LANES, 2, LANES)
     return jnp.transpose(out, (0, 2, 1, 3)).reshape(ROWS, 2, feeds)

time: 212 us -> 208 us (0.981)
  Pallas kernels: 51.2 us -> 47.6 us
  local copies, waits for them, and re-layouts: 5.33 us -> 7.65 us
    pallas_call x1, Pallas kernels: 6.85 us -> 2.65 us  [select_rows(): pl.pallas_call(functools.partial(select_kernel, lines - (STEPS - 1) * blo...]
    unnamed x18 -> x26, local copies, waits for them, and re-layouts: 1.13 us -> 4.95 us
    ppermute x24, waiting for transfers between devices: 22.7 us -> 26.3 us  [swap(): return lax.ppermute(value, 'feed', pairs)]
    all_to_all x2, waiting for transfers between devices: 79.6 us -> 77.2 us  [through_rows(): lax.all_to_all(coded, 'feed', split_axis=0, concat_axis=0, tiled=True)]
  transfers between devices with their start and end apart: 26 -> 26, of which waited for: 14 -> 12; matrix products, arithmetic and copies ran while one was open for 4% -> 3% of each run, Pallas kernels for 13% -> 13%
where the time goes in v13:
time: 208 us; the launch traced here: 207 us
  waiting for transfers between devices  104 us (50%)
  Pallas kernels  47.6 us (23%)
  starting transfers between devices  42.6 us (20%)
  local copies, waits for them, and re-layouts  7.65 us (4%)
  other arithmetic  5.12 us (2%)
    all_to_all x2, waiting for transfers between devices, through_rows(): lax.all_to_all(coded, 'feed', split_axis=0, concat_axis=0, tiled=True)  77.2 us
    ppermute x24, starting transfers between devices, swap(): return lax.ppermute(value, 'feed', pairs)  29.3 us
    ppermute x24, waiting for transfers between devices, swap(): return lax.ppermute(value, 'feed', pairs)  26.3 us
    pallas_call x2, Pallas kernels, finish(): pl.pallas_call(functools.partial(finish_kernel, scale), grid=(columns //...  17.4 us
    all_to_all x2, starting transfers between devices, through_rows(): lax.all_to_all(coded, 'feed', split_axis=0, concat_axis=0, tiled=True)  13.3 us
    pallas_call x2, Pallas kernels, row_spectra(): pl.pallas_call(rows_kernel, grid=(spectra // (STEPS * STEP),), in_specs=[...  9.61 us
    pallas_call x1, Pallas kernels, own_spectra(): pl.pallas_call(own_kernel, grid=(steps,), in_specs=[pl.BlockSpec((main, c...  9.45 us
    pallas_call x2, Pallas kernels, row_products(): pl.pallas_call(products_kernel, grid=(ch // each,), in_specs=[pl.BlockSpe...  8.55 us
  transfers between devices with their start and end apart: 26, of which 12 were waited for; matrix products, arithmetic and copies ran while one was open for 3% of the time, Pallas kernels for 13%

profile of v13, /device:TPU:13, one launch (start us, length us, event | category | flops | bytes accessed | tf_op | source)
XLA Modules:
  0.0 207.0 jit_solution(4079247497183356563)
XLA Ops:
  0.0 3.4 %copy-done = s32[256,16,519]{0,1,2:T(8,128)S(1)} copy-done((s32[256,16,519]{0,1,2:T(8,128)S(1)}, s32[256,16,519]{0,1,2:T(8,128)}, u32[]{:S(2)}) %copy-start) | copy-done | bytes 8503320
  3.4 0.8 copy-done.6
  4.2 0.7 copy-done.8
  4.9 2.6 %select_rows.1 = (bf16[8448,128]{1,0:T(8,128)(2,1)S(1)}, bf16[8448,128]{1,0:T(8,128)(2,1)S(1)}) custom-call(s32[1]{0:T(128)} %bitcast.3.place_ref, s32[32,128]{1,0:T(8,128)S(1)} %bitcast.19, s32[8304,256]{1,0:T(8,128)S(1)} %bitcast.13, s32[32,256]{1,0:T(8,128)S(1)} %bitcast.18), custom_call_target="tpu_custom_call" | custom-call | tf_op jit(solution)/shard_map/select_rows/pallas_call | solution.py:338
  7.6 1.1 constant_dynamic-slice_fusion.9
  8.6 0.7 collective-permute-start
  9.4 0.6 collective-permute-start.3
  10.0 2.0 collective-permute-done
  12.0 1.8 dynamic-slice_add_fusion.1
  14.4 1.5 dynamic-slice_add_fusion
  16.0 1.4 collective-permute-start.4
  17.5 1.4 collective-permute-start.9
  18.9 2.9 %collective-permute-done.1 = bf16[1056,128]{1,0:T(8,128)(2,1)S(1)} collective-permute-done((bf16[1056,128]{1,0:T(8,128)(2,1)S(1)}, bf16[1056,128]{1,0:T(8,128)(2,1)S(1)}, u32[]{:S(2)}, u32[]{:S(2)}) %collective-permute-start.1) | collective-permute-done | bytes 270368 | tf_op jit(solution)/shard_map/ppermute | solution.py:356
  22.2 1.0 collective-permute-start.19
  23.1 4.4 %collective-permute-done.4 = bf16[1056,128]{1,0:T(8,128)(2,1)S(1)} collective-permute-done((bf16[1056,128]{1,0:T(8,128)(2,1)S(1)}, bf16[1056,128]{1,0:T(8,128)(2,1)S(1)}, u32[]{:S(2)}, u32[]{:S(2)}) %collective-permute-start.4) | collective-permute-done | bytes 270368 | tf_op jit(solution)/shard_map/ppermute | solution.py:356
  27.9 1.0 collective-permute-start.10
  28.9 1.5 collective-permute-done.2
  30.4 2.4 %collective-permute-start.15 = (bf16[528,128]{1,0:T(8,128)(2,1)S(1)}, bf16[528,128]{1,0:T(8,128)(2,1)S(1)}, u32[]{:S(2)}, u32[]{:S(2)}) collective-permute-start(bf16[528,128]{1,0:T(8,128)(2,1)S(1)} %dynamic-slice_add_fusion.9.after_ref), channel_id=1, source_target_pairs={{0,8},{1,9},{2,10},{3,11},{4,12},{5,13},{6,14},{7,15},{8,0},{9,1},... | collective-permute-start | bytes 405512 | tf_op jit(solution)/shard_map/ppermute | solution.py:356
  32.8 9.5 %own_spectra.1 = (bf16[16,8,256,128]{3,2,1,0:T(8,128)(2,1)S(1)}, bf16[16,128]{1,0:T(8,128)(2,1)S(1)}) custom-call(s32[8304,256]{1,0:T(8,128)S(1)} %bitcast.16, s32[8304,256]{1,0:T(8,128)S(1)} %bitcast.17, f32[32,256]{1,0:T(8,128)S(1)} %bitcast_convert_fusion.gains_ref, bf16[256,256]{1,0:T(8,128)(2,1)S(1)} %copy-done.5, ...), custom_call_target="tpu_custom_call" | custom-call | flops 4294967296 | bytes 16891904 | tf_op jit(solution)/shard_map/own_spectra/pallas_call | solution.py:281
  42.3 0.6 slice.25
  43.1 2.4 %collective-permute-start.6 = (bf16[528,128]{1,0:T(8,128)(2,1)S(1)}, bf16[528,128]{1,0:T(8,128)(2,1)S(1)}, u32[]{:S(2)}, u32[]{:S(2)}) collective-permute-start(bf16[528,128]{1,0:T(8,128)(2,1)S(1)} %dynamic-slice_add_fusion.8), channel_id=1, source_target_pairs={{0,8},{1,9},{2,10},{3,11},{4,12},{5,13},{6,14},{7,15},{8,0},{9,1},... | collective-permute-start | bytes 405512 | tf_op jit(solution)/shard_map/ppermute | solution.py:356
  45.7 0.6 constant_dynamic-update-slice_fusion.9
  46.3 0.4 collective-permute-start.16
  46.7 5.6 %collective-permute-done.20 = bf16[528,128]{1,0:T(8,128)(2,1)S(1)} collective-permute-done((bf16[528,128]{1,0:T(8,128)(2,1)S(1)}, bf16[528,128]{1,0:T(8,128)(2,1)S(1)}, u32[]{:S(2)}, u32[]{:S(2)}) %collective-permute-start.20) | collective-permute-done | bytes 135200 | tf_op jit(solution)/shard_map/ppermute | solution.py:356
  52.3 0.7 collective-permute-start.21
  53.1 3.9 %collective-permute-done.6 = bf16[528,128]{1,0:T(8,128)(2,1)S(1)} collective-permute-done((bf16[528,128]{1,0:T(8,128)(2,1)S(1)}, bf16[528,128]{1,0:T(8,128)(2,1)S(1)}, u32[]{:S(2)}, u32[]{:S(2)}) %collective-permute-start.6) | collective-permute-done | bytes 135200 | tf_op jit(solution)/shard_map/ppermute | solution.py:356
  57.1 3.2 %collective-permute-start.7 = (bf16[528,128]{1,0:T(8,128)(2,1)S(1)}, bf16[528,128]{1,0:T(8,128)(2,1)S(1)}, u32[]{:S(2)}, u32[]{:S(2)}) collective-permute-start(bf16[528,128]{1,0:T(8,128)(2,1)S(1)} %get-tuple-element.24), channel_id=1, source_target_pairs={{0,4},{1,5},{2,6},{3,7},{4,0},{5,1},{6,2},{7,3},{8,12},{9,13},{10,... | collective-permute-start | bytes 405512 | tf_op jit(solution)/shard_map/ppermute | solution.py:356
  60.3 1.2 collective-permute-start.12
  61.6 0.4 collective-permute-start.17
  62.1 2.8 %collective-permute-start.22 = (bf16[1056,128]{1,0:T(8,128)(2,1)S(1)}, bf16[1056,128]{1,0:T(8,128)(2,1)S(1)}, u32[]{:S(2)}, u32[]{:S(2)}) collective-permute-start(bf16[1056,128]{1,0:T(8,128)(2,1)S(1)} %constant_dynamic-update-slice_fusion.4), channel_id=1, source_target_pairs={{0,4},{1,5},{2,6},{3,7},{4,0},{5,1},{6,2},{7,3},{8,12},{9,13},{10,... | collective-permute-start | bytes 811016 | tf_op jit(solution)/shard_map/ppermute | solution.py:356
  65.0 1.2 collective-permute-start.8
  66.3 1.1 collective-permute-start.13
  67.5 0.8 collective-permute-done.17
  68.3 0.8 collective-permute-done.22
  69.4 6.1 %collective-permute-start.23 = (bf16[4224,128]{1,0:T(8,128)(2,1)S(1)}, bf16[4224,128]{1,0:T(8,128)(2,1)S(1)}, u32[]{:S(2)}, u32[]{:S(2)}) collective-permute-start(bf16[4224,128]{1,0:T(8,128)(2,1)S(1)} %get-tuple-element.27), channel_id=1, source_target_pairs={{0,1},{1,0},{2,3},{3,2},{4,5},{5,4},{6,7},{7,6},{8,9},{9,8},{10,11... | collective-permute-start | bytes 3244040 | tf_op jit(solution)/shard_map/ppermute | solution.py:356
  75.8 2.0 collective-permute-done.23
  78.0 4.8 %row_spectra.3.left_ref = bf16[16,1024,256]{2,1,0:T(8,128)(2,1)S(1)} custom-call(bf16[8448,128]{1,0:T(8,128)(2,1)S(1)} %constant_dynamic-update-slice_fusion.main_ref.next_ref, bf16[8448,128]{1,0:T(8,128)(2,1)S(1)} %constant_dynamic-update-slice_fusion.main_ref.next_ref, bf16[64,128]{1,0:T(8,128)(2,1)S(1)} %slice.33.parts_ref, bf16[256,256]{1,0:T(8,128)(2,1)S(1)} %copy-done.5), custom_call_target="tpu_custom_call" | custom-call | flops 2147483648 | bytes 10551296 | tf_op jit(solution)/shard_map/row_spectra/pallas_call | solution.py:410
  82.8 4.3 %row_products.2 = (s16[16,264,256]{2,1,0:T(8,128)(2,1)}, bf16[16,128]{1,0:T(8,128)(2,1)S(1)}) custom-call(bf16[16,8,256,128]{3,2,1,0:T(8,128)(2,1)S(1)} %get-tuple-element.13.own_ref, bf16[16,1024,256]{2,1,0:T(8,128)(2,1)S(1)} %row_spectra.3.left_ref, bf16[4224,128]{1,0:T(8,128)(2,1)S(1)} %get-tuple-element.31.refs_0_), custom_call_target="tpu_custom_call" | custom-call | flops 2147483648 | bytes 16777216 | tf_op jit(solution)/shard_map/row_products/pallas_call | solution.py:452
  87.2 8.3 %all-to-all-start.1 = ((s16[16,264,256]{2,1,0:T(8,128)(2,1)}), s16[16,264,256]{2,1,0:T(8,128)(2,1)}, u32[]{:S(2)}, u32[]{:S(2)}) async-start(s16[16,264,256]{2,1,0:T(8,128)(2,1)} %get-tuple-element.18), calls=%async_computation.1 | async-start | bytes 4325376 | tf_op jit(solution)/shard_map/all_to_all | solution.py:555
  95.4 0.4 collective-permute-start.14
  95.8 2.4 %collective-permute-done.14 = bf16[4224,128]{1,0:T(8,128)(2,1)S(1)} collective-permute-done((bf16[4224,128]{1,0:T(8,128)(2,1)S(1)}, bf16[4224,128]{1,0:T(8,128)(2,1)S(1)}, u32[]{:S(2)}, u32[]{:S(2)}) %collective-permute-start.14) | collective-permute-done | bytes 1081376 | tf_op jit(solution)/shard_map/ppermute | solution.py:356
  98.4 4.8 %row_spectra.2.left_ref = bf16[16,1024,256]{2,1,0:T(8,128)(2,1)S(1)} custom-call(bf16[8448,128]{1,0:T(8,128)(2,1)S(1)} %constant_dynamic-update-slice_fusion.10.main_ref.next_ref, bf16[8448,128]{1,0:T(8,128)(2,1)S(1)} %constant_dynamic-update-slice_fusion.10.main_ref.next_ref, bf16[64,128]{1,0:T(8,128)(2,1)S(1)} %slice.31.parts_ref, ...), custom_call_target="tpu_custom_call" | custom-call | flops 2147483648 | bytes 10551296 | tf_op jit(solution)/shard_map/row_spectra/pallas_call | solution.py:410
  103.2 4.2 %row_products.3 = (s16[16,264,256]{2,1,0:T(8,128)(2,1)}, bf16[16,128]{1,0:T(8,128)(2,1)}) custom-call(bf16[16,8,256,128]{3,2,1,0:T(8,128)(2,1)S(1)} %copy-done.2, bf16[16,1024,256]{2,1,0:T(8,128)(2,1)S(1)} %row_spectra.2.left_ref, bf16[16,128]{1,0:T(8,128)(2,1)S(1)} %get-tuple-element.16.refs_0_), custom_call_target="tpu_custom_call" | custom-call | flops 2147483648 | bytes 16777216 | tf_op jit(solution)/shard_map/row_products/pallas_call | solution.py:452
  107.4 37.0 %all-to-all-done.1.coded_ref = s16[16,264,256]{2,1,0:T(8,128)(2,1)} async-done(((s16[16,264,256]{2,1,0:T(8,128)(2,1)}), s16[16,264,256]{2,1,0:T(8,128)(2,1)}, u32[]{:S(2)}, u32[]{:S(2)}) %all-to-all-start.1) | async-done | bytes 2162720 | tf_op jit(solution)/shard_map/all_to_all | solution.py:555
  144.4 5.0 %all-to-all-start = ((s16[16,264,256]{2,1,0:T(8,128)(2,1)}), s16[16,264,256]{2,1,0:T(8,128)(2,1)}, u32[]{:S(2)}, u32[]{:S(2)}) async-start(s16[16,264,256]{2,1,0:T(8,128)(2,1)} %get-tuple-element.17), calls=%async_computation | async-start | bytes 4325376 | tf_op jit(solution)/shard_map/all_to_all | solution.py:555
  149.4 8.7 %finish.2.refs_0_ = f32[256,64,128]{2,1,0:T(8,128)} custom-call(s32[4096]{0:T(1024)S(1)} %broadcast_multiply_fusion.slot_ref, s16[16,264,256]{2,1,0:T(8,128)(2,1)} %all-to-all-done.1.coded_ref), custom_call_target="tpu_custom_call" | custom-call | tf_op jit(solution)/shard_map/finish/pallas_call | solution.py:506
  158.1 40.2 %all-to-all-done.coded_ref = s16[16,264,256]{2,1,0:T(8,128)(2,1)} async-done(((s16[16,264,256]{2,1,0:T(8,128)(2,1)}), s16[16,264,256]{2,1,0:T(8,128)(2,1)}, u32[]{:S(2)}, u32[]{:S(2)}) %all-to-all-start) | async-done | bytes 2162720 | tf_op jit(solution)/shard_map/all_to_all | solution.py:555
  198.3 8.7 %finish.3 = f32[256,64,128]{2,1,0:T(8,128)} custom-call(s32[4096]{0:T(1024)S(1)} %broadcast_multiply_fusion.slot_ref, s16[16,264,256]{2,1,0:T(8,128)(2,1)} %all-to-all-done.coded_ref, f32[256,64,128]{2,1,0:T(8,128)} %finish.2.refs_0_), custom_call_target="tpu_custom_call", output_to_operand_aliasing={{}: (2, {})} | custom-call | tf_op jit(solution)/shard_map/finish/pallas_call | solution.py:506
  (86 shorter events, 3.3 us)
Async XLA Ops:
  0.0 3.4 %copy-start = (s32[256,16,519]{0,1,2:T(8,128)S(1)}, s32[256,16,519]{0,1,2:T(8,128)}, u32[]{:S(2)}) copy-start(s32[256,16,519]{0,1,2:T(8,128)} %param.4) | copy-start | bytes 25509892
  3.4 0.8 copy-start.6
  4.2 0.7 copy-start.8
  7.5 1.9 copy-start.3
  7.6 2.4 %copy-start.7 = (s32[2,16,256]{2,1,0:T(8,128)S(1)}, s32[2,16,256]{2,1,0:T(8,128)}, u32[]{:S(2)}) copy-start(s32[2,16,256]{2,1,0:T(8,128)} %param.5) | copy-start | bytes 98308
  7.6 25.3 %slice-start = ((s8[8503296]{0:T(1024)(128)(4,1)}), s8[114688]{0:T(1024)(128)(4,1)S(1)}, s32[]{:S(2)}) async-start(s8[8503296]{0:T(1024)(128)(4,1)} %bitcast.14), calls=%async_computation.2 | async-start | bytes 229376
  8.6 3.4 %collective-permute-start = (bf16[4224,128]{1,0:T(8,128)(2,1)}, bf16[4224,128]{1,0:T(8,128)(2,1)}, u32[]{:S(2)}, u32[]{:S(2)}) collective-permute-start(bf16[4224,128]{1,0:T(8,128)(2,1)} %constant_dynamic-slice_fusion.9), channel_id=1, source_target_pairs={{0,1},{1,0},{2,3},{3,2},{4,5},{5,4},{6,7},{7,6},{8,9},{9,8},{10,11... | collective-permute-start | bytes 3244040 | tf_op jit(solution)/shard_map/ppermute | solution.py:356
  9.4 4.9 %collective-permute-start.3 = (bf16[4224,128]{1,0:T(8,128)(2,1)S(1)}, bf16[4224,128]{1,0:T(8,128)(2,1)}, u32[]{:S(2)}, u32[]{:S(2)}) collective-permute-start(bf16[4224,128]{1,0:T(8,128)(2,1)S(1)} %constant_dynamic-slice_fusion.6), channel_id=1, source_target_pairs={{0,1},{1,0},{2,3},{3,2},{4,5},{5,4},{6,7},{7,6},{8,9},{9,8},{10,11... | collective-permute-start | bytes 3244040 | tf_op jit(solution)/shard_map/ppermute | solution.py:356
  10.0 22.9 %slice-start.1 = ((s8[8503296]{0:T(1024)(128)(4,1)}), s8[4194304]{0:T(1024)(128)(4,1)S(1)}, s32[]{:S(2)}) async-start(s8[8503296]{0:T(1024)(128)(4,1)} %bitcast.14), calls=%async_computation.3 | async-start | bytes 8388608
  14.0 7.8 %collective-permute-start.1 = (bf16[1056,128]{1,0:T(8,128)(2,1)S(1)}, bf16[1056,128]{1,0:T(8,128)(2,1)S(1)}, u32[]{:S(2)}, u32[]{:S(2)}) collective-permute-start(bf16[1056,128]{1,0:T(8,128)(2,1)S(1)} %constant_dynamic-slice_fusion.8), channel_id=1, source_target_pairs={{0,2},{1,3},{2,0},{3,1},{4,6},{5,7},{6,4},{7,5},{8,10},{9,11},{10,... | collective-permute-start | bytes 811016 | tf_op jit(solution)/shard_map/ppermute | solution.py:356
  14.3 7.8 %collective-permute-start.18 = (bf16[1056,128]{1,0:T(8,128)(2,1)S(1)}, bf16[1056,128]{1,0:T(8,128)(2,1)S(1)}, u32[]{:S(2)}, u32[]{:S(2)}) collective-permute-start(bf16[1056,128]{1,0:T(8,128)(2,1)S(1)} %constant_dynamic-slice_fusion.1), channel_id=1, source_target_pairs={{0,4},{1,5},{2,6},{3,7},{4,0},{5,1},{6,2},{7,3},{8,12},{9,13},{10,... | collective-permute-start | bytes 811016 | tf_op jit(solution)/shard_map/ppermute | solution.py:356
  15.9 16.9 %slice-start.2 = ((s8[8503296]{0:T(1024)(128)(4,1)}), s8[4194304]{0:T(1024)(128)(4,1)S(1)}, s32[]{:S(2)}) async-start(s8[8503296]{0:T(1024)(128)(4,1)} %bitcast.14), calls=%async_computation.4 | async-start | bytes 8388608
  16.0 11.5 %collective-permute-start.4 = (bf16[1056,128]{1,0:T(8,128)(2,1)S(1)}, bf16[1056,128]{1,0:T(8,128)(2,1)S(1)}, u32[]{:S(2)}, u32[]{:S(2)}) collective-permute-start(bf16[1056,128]{1,0:T(8,128)(2,1)S(1)} %constant_dynamic-slice_fusion.5), channel_id=1, source_target_pairs={{0,2},{1,3},{2,0},{3,1},{4,6},{5,7},{6,4},{7,5},{8,10},{9,11},{10,... | collective-permute-start | bytes 811016 | tf_op jit(solution)/shard_map/ppermute | solution.py:356
  17.5 10.4 %collective-permute-start.9 = (bf16[1056,128]{1,0:T(8,128)(2,1)S(1)}, bf16[1056,128]{1,0:T(8,128)(2,1)S(1)}, u32[]{:S(2)}, u32[]{:S(2)}) collective-permute-start(bf16[1056,128]{1,0:T(8,128)(2,1)S(1)} %constant_dynamic-slice_fusion.3), channel_id=1, source_target_pairs={{0,4},{1,5},{2,6},{3,7},{4,0},{5,1},{6,2},{7,3},{8,12},{9,13},{10,... | collective-permute-start | bytes 811016 | tf_op jit(solution)/shard_map/ppermute | solution.py:356
  21.8 11.0 %copy-start.5 = (bf16[256,256]{1,0:T(8,128)(2,1)S(1)}, bf16[256,256]{1,0:T(8,128)(2,1)}, u32[]{:S(2)}) copy-start(bf16[256,256]{1,0:T(8,128)(2,1)} %constant.217.clone.weights_ref) | copy-start | bytes 393220
  21.8 8.6 %collective-permute-start.2 = (bf16[528,128]{1,0:T(8,128)(2,1)S(1)}, bf16[528,128]{1,0:T(8,128)(2,1)S(1)}, u32[]{:S(2)}, u32[]{:S(2)}) collective-permute-start(bf16[528,128]{1,0:T(8,128)(2,1)S(1)} %constant_dynamic-slice_fusion.7), channel_id=1, source_target_pairs={{0,4},{1,5},{2,6},{3,7},{4,0},{5,1},{6,2},{7,3},{8,12},{9,13},{10,... | collective-permute-start | bytes 405512 | tf_op jit(solution)/shard_map/ppermute | solution.py:356
  22.2 20.7 %collective-permute-start.19 = (bf16[528,128]{1,0:T(8,128)(2,1)S(1)}, bf16[528,128]{1,0:T(8,128)(2,1)S(1)}, u32[]{:S(2)}, u32[]{:S(2)}) collective-permute-start(bf16[528,128]{1,0:T(8,128)(2,1)S(1)} %constant_dynamic-slice_fusion), channel_id=1, source_target_pairs={{0,2},{1,3},{2,0},{3,1},{4,6},{5,7},{6,4},{7,5},{8,10},{9,11},{10,... | collective-permute-start | bytes 405512 | tf_op jit(solution)/shard_map/ppermute | solution.py:356
  27.6 15.4 %collective-permute-start.5 = (bf16[528,128]{1,0:T(8,128)(2,1)S(1)}, bf16[528,128]{1,0:T(8,128)(2,1)S(1)}, u32[]{:S(2)}, u32[]{:S(2)}) collective-permute-start(bf16[528,128]{1,0:T(8,128)(2,1)S(1)} %constant_dynamic-slice_fusion.4), channel_id=1, source_target_pairs={{0,4},{1,5},{2,6},{3,7},{4,0},{5,1},{6,2},{7,3},{8,12},{9,13},{10,... | collective-permute-start | bytes 405512 | tf_op jit(solution)/shard_map/ppermute | solution.py:356
  27.9 17.6 %collective-permute-start.10 = (bf16[528,128]{1,0:T(8,128)(2,1)S(1)}, bf16[528,128]{1,0:T(8,128)(2,1)S(1)}, u32[]{:S(2)}, u32[]{:S(2)}) collective-permute-start(bf16[528,128]{1,0:T(8,128)(2,1)S(1)} %constant_dynamic-slice_fusion.2), channel_id=1, source_target_pairs={{0,2},{1,3},{2,0},{3,1},{4,6},{5,7},{6,4},{7,5},{8,10},{9,11},{10,... | collective-permute-start | bytes 405512 | tf_op jit(solution)/shard_map/ppermute | solution.py:356
  30.4 15.2 %collective-permute-start.15 = (bf16[528,128]{1,0:T(8,128)(2,1)S(1)}, bf16[528,128]{1,0:T(8,128)(2,1)S(1)}, u32[]{:S(2)}, u32[]{:S(2)}) collective-permute-start(bf16[528,128]{1,0:T(8,128)(2,1)S(1)} %dynamic-slice_add_fusion.9.after_ref), channel_id=1, source_target_pairs={{0,8},{1,9},{2,10},{3,11},{4,12},{5,13},{6,14},{7,15},{8,0},{9,1},... | collective-permute-start | bytes 405512 | tf_op jit(solution)/shard_map/ppermute | solution.py:356
  42.3 40.5 %copy-start.1 = (bf16[16,8,256,128]{3,2,1,0:T(8,128)(2,1)}, bf16[16,8,256,128]{3,2,1,0:T(8,128)(2,1)S(1)}, u32[]{:S(2)}) copy-start(bf16[16,8,256,128]{3,2,1,0:T(8,128)(2,1)S(1)} %get-tuple-element.13.own_ref) | copy-start | bytes 25165828
  42.9 9.3 %collective-permute-start.20 = (bf16[528,128]{1,0:T(8,128)(2,1)S(1)}, bf16[528,128]{1,0:T(8,128)(2,1)S(1)}, u32[]{:S(2)}, u32[]{:S(2)}) collective-permute-start(bf16[528,128]{1,0:T(8,128)(2,1)S(1)} %dynamic-slice_add_fusion.6), channel_id=1, source_target_pairs={{0,8},{1,9},{2,10},{3,11},{4,12},{5,13},{6,14},{7,15},{8,0},{9,1},... | collective-permute-start | bytes 405512 | tf_op jit(solution)/shard_map/ppermute | solution.py:356
  43.1 13.9 %collective-permute-start.6 = (bf16[528,128]{1,0:T(8,128)(2,1)S(1)}, bf16[528,128]{1,0:T(8,128)(2,1)S(1)}, u32[]{:S(2)}, u32[]{:S(2)}) collective-permute-start(bf16[528,128]{1,0:T(8,128)(2,1)S(1)} %dynamic-slice_add_fusion.8), channel_id=1, source_target_pairs={{0,8},{1,9},{2,10},{3,11},{4,12},{5,13},{6,14},{7,15},{8,0},{9,1},... | collective-permute-start | bytes 405512 | tf_op jit(solution)/shard_map/ppermute | solution.py:356
  45.5 14.7 %collective-permute-start.11 = (bf16[528,128]{1,0:T(8,128)(2,1)S(1)}, bf16[528,128]{1,0:T(8,128)(2,1)S(1)}, u32[]{:S(2)}, u32[]{:S(2)}) collective-permute-start(bf16[528,128]{1,0:T(8,128)(2,1)S(1)} %dynamic-slice_add_fusion.7), channel_id=1, source_target_pairs={{0,8},{1,9},{2,10},{3,11},{4,12},{5,13},{6,14},{7,15},{8,0},{9,1},... | collective-permute-start | bytes 405512 | tf_op jit(solution)/shard_map/ppermute | solution.py:356
  46.3 15.3 %collective-permute-start.16 = (bf16[528,128]{1,0:T(8,128)(2,1)S(1)}, bf16[528,128]{1,0:T(8,128)(2,1)S(1)}, u32[]{:S(2)}, u32[]{:S(2)}) collective-permute-start(bf16[528,128]{1,0:T(8,128)(2,1)S(1)} %get-tuple-element.20), channel_id=1, source_target_pairs={{0,4},{1,5},{2,6},{3,7},{4,0},{5,1},{6,2},{7,3},{8,12},{9,13},{10,... | collective-permute-start | bytes 405512 | tf_op jit(solution)/shard_map/ppermute | solution.py:356
  52.3 9.7 %collective-permute-start.21 = (bf16[528,128]{1,0:T(8,128)(2,1)S(1)}, bf16[528,128]{1,0:T(8,128)(2,1)S(1)}, u32[]{:S(2)}, u32[]{:S(2)}) collective-permute-start(bf16[528,128]{1,0:T(8,128)(2,1)S(1)} %get-tuple-element.22), channel_id=1, source_target_pairs={{0,2},{1,3},{2,0},{3,1},{4,6},{5,7},{6,4},{7,5},{8,10},{9,11},{10,... | collective-permute-start | bytes 405512 | tf_op jit(solution)/shard_map/ppermute | solution.py:356
  57.1 7.8 %collective-permute-start.7 = (bf16[528,128]{1,0:T(8,128)(2,1)S(1)}, bf16[528,128]{1,0:T(8,128)(2,1)S(1)}, u32[]{:S(2)}, u32[]{:S(2)}) collective-permute-start(bf16[528,128]{1,0:T(8,128)(2,1)S(1)} %get-tuple-element.24), channel_id=1, source_target_pairs={{0,4},{1,5},{2,6},{3,7},{4,0},{5,1},{6,2},{7,3},{8,12},{9,13},{10,... | collective-permute-start | bytes 405512 | tf_op jit(solution)/shard_map/ppermute | solution.py:356
  60.3 5.9 %collective-permute-start.12 = (bf16[528,128]{1,0:T(8,128)(2,1)S(1)}, bf16[528,128]{1,0:T(8,128)(2,1)S(1)}, u32[]{:S(2)}, u32[]{:S(2)}) collective-permute-start(bf16[528,128]{1,0:T(8,128)(2,1)S(1)} %get-tuple-element.26), channel_id=1, source_target_pairs={{0,2},{1,3},{2,0},{3,1},{4,6},{5,7},{6,4},{7,5},{8,10},{9,11},{10,... | collective-permute-start | bytes 405512 | tf_op jit(solution)/shard_map/ppermute | solution.py:356
  61.6 7.6 %copy-start.4 = (bf16[8448,128]{1,0:T(8,128)(2,1)S(1)}, bf16[8448,128]{1,0:T(8,128)(2,1)}, u32[]{:S(2)}) copy-start(bf16[8448,128]{1,0:T(8,128)(2,1)} %copy-done.3) | copy-start | bytes 6488068
  61.6 6.7 %collective-permute-start.17 = (bf16[1056,128]{1,0:T(8,128)(2,1)S(1)}, bf16[1056,128]{1,0:T(8,128)(2,1)S(1)}, u32[]{:S(2)}, u32[]{:S(2)}) collective-permute-start(bf16[1056,128]{1,0:T(8,128)(2,1)S(1)} %constant_dynamic-update-slice_fusion.8), channel_id=1, source_target_pairs={{0,2},{1,3},{2,0},{3,1},{4,6},{5,7},{6,4},{7,5},{8,10},{9,11},{10,... | collective-permute-start | bytes 811016 | tf_op jit(solution)/shard_map/ppermute | solution.py:356
  62.1 7.1 %collective-permute-start.22 = (bf16[1056,128]{1,0:T(8,128)(2,1)S(1)}, bf16[1056,128]{1,0:T(8,128)(2,1)S(1)}, u32[]{:S(2)}, u32[]{:S(2)}) collective-permute-start(bf16[1056,128]{1,0:T(8,128)(2,1)S(1)} %constant_dynamic-update-slice_fusion.4), channel_id=1, source_target_pairs={{0,4},{1,5},{2,6},{3,7},{4,0},{5,1},{6,2},{7,3},{8,12},{9,13},{10,... | collective-permute-start | bytes 811016 | tf_op jit(solution)/shard_map/ppermute | solution.py:356
  65.0 10.5 %collective-permute-start.8 = (bf16[1056,128]{1,0:T(8,128)(2,1)S(1)}, bf16[1056,128]{1,0:T(8,128)(2,1)S(1)}, u32[]{:S(2)}, u32[]{:S(2)}) collective-permute-start(bf16[1056,128]{1,0:T(8,128)(2,1)S(1)} %constant_dynamic-update-slice_fusion.18), channel_id=1, source_target_pairs={{0,2},{1,3},{2,0},{3,1},{4,6},{5,7},{6,4},{7,5},{8,10},{9,11},{10,... | collective-permute-start | bytes 811016 | tf_op jit(solution)/shard_map/ppermute | solution.py:356
  66.3 9.2 %collective-permute-start.13 = (bf16[1056,128]{1,0:T(8,128)(2,1)S(1)}, bf16[1056,128]{1,0:T(8,128)(2,1)S(1)}, u32[]{:S(2)}, u32[]{:S(2)}) collective-permute-start(bf16[1056,128]{1,0:T(8,128)(2,1)S(1)} %constant_dynamic-update-slice_fusion.14), channel_id=1, source_target_pairs={{0,4},{1,5},{2,6},{3,7},{4,0},{5,1},{6,2},{7,3},{8,12},{9,13},{10,... | collective-permute-start | bytes 811016 | tf_op jit(solution)/shard_map/ppermute | solution.py:356
  69.4 8.4 %collective-permute-start.23 = (bf16[4224,128]{1,0:T(8,128)(2,1)S(1)}, bf16[4224,128]{1,0:T(8,128)(2,1)S(1)}, u32[]{:S(2)}, u32[]{:S(2)}) collective-permute-start(bf16[4224,128]{1,0:T(8,128)(2,1)S(1)} %get-tuple-element.27), channel_id=1, source_target_pairs={{0,1},{1,0},{2,3},{3,2},{4,5},{5,4},{6,7},{7,6},{8,9},{9,8},{10,11... | collective-permute-start | bytes 3244040 | tf_op jit(solution)/shard_map/ppermute | solution.py:356
  87.2 57.2 %all-to-all-start.1 = ((s16[16,264,256]{2,1,0:T(8,128)(2,1)}), s16[16,264,256]{2,1,0:T(8,128)(2,1)}, u32[]{:S(2)}, u32[]{:S(2)}) async-start(s16[16,264,256]{2,1,0:T(8,128)(2,1)} %get-tuple-element.18), calls=%async_computation.1 | async-start | bytes 4325376 | tf_op jit(solution)/shard_map/all_to_all | solution.py:555
  95.4 2.7 %collective-permute-start.14 = (bf16[4224,128]{1,0:T(8,128)(2,1)S(1)}, bf16[4224,128]{1,0:T(8,128)(2,1)S(1)}, u32[]{:S(2)}, u32[]{:S(2)}) collective-permute-start(bf16[4224,128]{1,0:T(8,128)(2,1)S(1)} %get-tuple-element.31.refs_0_), channel_id=1, source_target_pairs={{0,1},{1,0},{2,3},{3,2},{4,5},{5,4},{6,7},{7,6},{8,9},{9,8},{10,11... | collective-permute-start | bytes 3244040 | tf_op jit(solution)/shard_map/ppermute | solution.py:356
  98.3 4.8 %copy-start.2 = (bf16[16,8,256,128]{3,2,1,0:T(8,128)(2,1)S(1)}, bf16[16,8,256,128]{3,2,1,0:T(8,128)(2,1)}, u32[]{:S(2)}) copy-start(bf16[16,8,256,128]{3,2,1,0:T(8,128)(2,1)} %copy-done.1) | copy-start | bytes 25165828
  144.4 5.0 %copy-start.9 = (s32[4096]{0:T(1024)S(1)}, s32[4096]{0:T(1024)}, u32[]{:S(2)}) copy-start(s32[4096]{0:T(1024)} %param.6) | copy-start | bytes 49156
  144.4 53.9 %all-to-all-start = ((s16[16,264,256]{2,1,0:T(8,128)(2,1)}), s16[16,264,256]{2,1,0:T(8,128)(2,1)}, u32[]{:S(2)}, u32[]{:S(2)}) async-start(s16[16,264,256]{2,1,0:T(8,128)(2,1)} %get-tuple-element.17), calls=%async_computation | async-start | bytes 4325376 | tf_op jit(solution)/shard_map/all_to_all | solution.py:555

commit v14 on v13

--- a/solution.py
+++ b/solution.py
@@ -260,7 +260,8 @@
     ]
 
 
-def own_kernel(main_ref, next_ref, gains_ref, weights_ref, after_ref, out_ref, zero_ref, held):
+def own_kernel(main_ref, next_ref, gains_ref, weights_ref, *refs):
+    out_ref, zero_ref, held = refs[-3:]
     step = pl.program_id(0)
     ch = out_ref.shape[0]
     zero_ref[...] = jnp.zeros_like(zero_ref)
@@ -286,8 +287,8 @@
             pl.BlockSpec((STEP * ch, count), lambda i: ((i + 1) * STEPS, 0)),
             pl.BlockSpec(gains.shape, lambda i: (0, 0)),
             pl.BlockSpec(weights.shape, lambda i: (0, 0)),
-            pl.BlockSpec(memory_space=pl.ANY),
-        ],
+        ]
+        + [pl.BlockSpec(memory_space=pl.ANY)] * len(after),
         out_specs=[
             pl.BlockSpec(memory_space=pltpu.VMEM),
             pl.BlockSpec((16, LANES), lambda i: (0, 0)),
@@ -306,7 +307,7 @@
             transcendentals=0,
         ),
         name="own_spectra",
-    )(words, words, gains, weights, after)
+    )(words, words, gains, weights, *after)
 
 
 def select_kernel(last_rows, place_ref, slots_ref, words_ref, gains_ref, *outs):
@@ -374,19 +375,31 @@
     return lax.dynamic_update_slice_in_dim(buffer, other, (1 - side(bit)) * size, 0)
 
 
-def sum_over_feed(value, work=None):
-    half = reduce_half(value, 1)
+def quarters(half, behind):
     size = half.shape[0] // 2
+    half = half + behind
     left, right = half[:size], half[size:]
     left_1, right_1 = reduce_half(left, 2), reduce_half(right, 4)
-    left_2, right_2 = reduce_half(left_1, 4), reduce_half(right_1, 2)
-    left_3, right_3 = left_2 + swap(left_2, 8), right_2 + swap(right_2, 8)
-    if work is not None:
-        left_3 = left_3 + work(left_2)
-    left_1, right_1 = gather_half(left_3, 4, left_1), gather_half(right_3, 2, right_1)
-    left, right = gather_half(left_1, 2, left), gather_half(right_1, 4, right)
-    half = jnp.concatenate([left, right], axis=0)
-    return half, lambda: gather_half(half, 1, value)
+    return (left, right), (left_1, right_1)
+
+
+def eighths(first):
+    return reduce_half(first[0], 4), reduce_half(first[1], 2)
+
+
+def cross(second, behind):
+    second = [value + behind for value in second]
+    return [value + swap(value, 8) for value in second]
+
+
+def gathered(half, first, third):
+    left_1, right_1 = gather_half(third[0], 4, first[0]), gather_half(third[1], 2, first[1])
+    left, right = gather_half(left_1, 2, half[0]), gather_half(right_1, 4, half[1])
+    return jnp.concatenate([left, right], axis=0)
+
+
+def zero_after(values):
+    return sum(value[0, 0] for value in values) * 0
 
 
 def rows_kernel(main_ref, next_ref, parts_ref, weights_ref, out_ref):
@@ -536,21 +549,32 @@
     weights = jnp.asarray(filter_weights(ch))
     place = lax.axis_index("feed").reshape(1)
     picked = select_rows(place, words, scales, feed_slot.reshape(-1, LANES), ROWS, total)
-    held = []
-
-    def work(after):
-        own, zero = own_spectra(words, scales.astype(jnp.float32), weights, ch, spectra, after)
-        held.append(own)
-        return zero[0, 0]
-
-    sums = [sum_over_feed(value, None if index else work) for index, value in enumerate(picked)]
-    own = held[0]
-    out, after = None, [sums[-1][0]]
+    nothing = jnp.zeros((), jnp.bfloat16)
+    halves, firsts, behind = [], [], nothing
+    for value in picked:
+        half, first = quarters(reduce_half(value, 1), behind)
+        behind = zero_after(first)
+        halves.append(half)
+        firsts.append(first)
+    seconds = [eighths(first) for first in firsts]
+    own, zero = own_spectra(words, scales.astype(jnp.float32), weights, ch, spectra, sum(seconds, ()))
+    thirds, behind = [], nothing
+    for second in seconds:
+        third = cross(second, behind)
+        if not thirds:
+            third[0] = third[0] + zero[0, 0]
+        behind = zero_after(third)
+        thirds.append(third)
+    ends = [gathered(*parts) for parts in zip(halves, firsts, thirds)]
+    out, lefts = None, []
     for index in range(pieces):
-        rows = sums[index][1]()
+        end = ends[index] if not lefts else ends[index] + zero_after([lefts[-1][0]])
+        rows = gather_half(end, 1, picked[index])
         parts = rows[lines : lines + 4 * ch]
-        left = row_spectra(rows, parts, weights, ch, spectra)
-        coded, done = row_products(own, left, after)
+        lefts.append(row_spectra(rows, parts, weights, ch, spectra))
+    after = [end]
+    for index in range(pieces):
+        coded, done = row_products(own, lefts[index], after)
         after = [done]
         moved = lax.all_to_all(coded, "feed", split_axis=0, concat_axis=0, tiled=True)
         out = finish(moved, feed_slot * 2, index, pieces, 1.0 / spectra, out)

time: 208 us -> 223 us (1.072)
  local copies, waits for them, and re-layouts: 7.65 us -> 14.5 us
  waiting for transfers between devices: 104 us -> 108 us
  between operations: 0.44 us -> 3.61 us
    ppermute x24, waiting for transfers between devices: 26.3 us -> 30.5 us  [swap(): return lax.ppermute(value, 'feed', pairs)]
    unnamed x26, local copies, waits for them, and re-layouts: 4.95 us -> 8.68 us
    slice x3 -> x8, local copies, waits for them, and re-layouts: 0.73 us -> 3.87 us  [the longest x5 3.17 us: zero_after(): return sum((value[0, 0] for value in values)) * 0]
  transfers between devices with their start and end apart: 26 -> 26, of which waited for: 12 -> 13; matrix products, arithmetic and copies ran while one was open for 3% -> 5% of each run, Pallas kernels for 13% -> 12%
where the time goes in v14:
time: 223 us; the launch traced here: 222 us
  waiting for transfers between devices  108 us (48%)
  Pallas kernels  47.2 us (21%)
  starting transfers between devices  43 us (19%)
  local copies, waits for them, and re-layouts  14.5 us (7%)
  other arithmetic  6.34 us (3%)
  between operations  3.61 us (2%)
    all_to_all x2, waiting for transfers between devices, through_rows(): lax.all_to_all(coded, 'feed', split_axis=0, concat_axis=0, tiled=True)  77.2 us
    ppermute x24, waiting for transfers between devices, swap(): return lax.ppermute(value, 'feed', pairs)  30.5 us
    ppermute x24, starting transfers between devices, swap(): return lax.ppermute(value, 'feed', pairs)  28.2 us
    pallas_call x2, Pallas kernels, finish(): pl.pallas_call(functools.partial(finish_kernel, scale), grid=(columns //...  17.4 us
    all_to_all x2, starting transfers between devices, through_rows(): lax.all_to_all(coded, 'feed', split_axis=0, concat_axis=0, tiled=True)  14.8 us
    pallas_call x2, Pallas kernels, row_spectra(): pl.pallas_call(rows_kernel, grid=(spectra // (STEPS * STEP),), in_specs=[...  9.6 us
    pallas_call x1, Pallas kernels, own_spectra(): pl.pallas_call(own_kernel, grid=(steps,), in_specs=[pl.BlockSpec((main, c...  9.12 us
    unnamed x26, local copies, waits for them, and re-layouts  8.68 us
  transfers between devices with their start and end apart: 26, of which 13 were waited for; matrix products, arithmetic and copies ran while one was open for 5% of the time, Pallas kernels for 12%

profile of v14, /device:TPU:13, one launch (start us, length us, event | category | flops | bytes accessed | tf_op | source)
XLA Modules:
  0.0 222.4 jit_solution(5012217212415553198)
XLA Ops:
  0.0 3.4 %copy-done = s32[256,16,519]{0,1,2:T(8,128)S(1)} copy-done((s32[256,16,519]{0,1,2:T(8,128)S(1)}, s32[256,16,519]{0,1,2:T(8,128)}, u32[]{:S(2)}) %copy-start) | copy-done | bytes 8503320
  3.4 0.8 copy-done.7
  4.2 0.7 copy-done.9
  4.9 2.6 %select_rows.1 = (bf16[8448,128]{1,0:T(8,128)(2,1)S(1)}, bf16[8448,128]{1,0:T(8,128)(2,1)S(1)}) custom-call(s32[1]{0:T(128)} %bitcast.3.place_ref, s32[32,128]{1,0:T(8,128)S(1)} %bitcast.22, s32[8304,256]{1,0:T(8,128)S(1)} %bitcast.18, s32[32,256]{1,0:T(8,128)S(1)} %bitcast.21), custom_call_target="tpu_custom_call" | custom-call | tf_op jit(solution)/shard_map/select_rows/pallas_call | solution.py:339
  7.6 0.7 collective-permute-start
  8.4 1.1 constant_dynamic-slice_fusion.4
  9.9 0.9 collective-permute-done
  10.9 1.8 dynamic-slice_add_fusion
  13.7 7.0 %collective-permute-done.1 = bf16[1056,128]{1,0:T(8,128)(2,1)} collective-permute-done((bf16[1056,128]{1,0:T(8,128)(2,1)S(1)}, bf16[1056,128]{1,0:T(8,128)(2,1)}, u32[]{:S(2)}, u32[]{:S(2)}) %collective-permute-start.1) | collective-permute-done | bytes 270368 | tf_op jit(solution)/shard_map/ppermute | solution.py:357
  20.7 1.0 dynamic-slice_add_fusion.4
  21.7 0.6 slice.54
  24.4 1.6 add_add_fusion
  26.6 1.2 collective-permute-start.6
  27.8 1.4 collective-permute-start.8
  29.2 0.9 collective-permute-done.4
  30.1 2.4 %collective-permute-start.11 = (bf16[528,128]{1,0:T(8,128)(2,1)S(1)}, bf16[528,128]{1,0:T(8,128)(2,1)S(1)}, u32[]{:S(2)}, u32[]{:S(2)}) collective-permute-start(bf16[528,128]{1,0:T(8,128)(2,1)S(1)} %dynamic-slice_add_fusion.7.refs_1_), channel_id=1, source_target_pairs={{0,8},{1,9},{2,10},{3,11},{4,12},{5,13},{6,14},{7,15},{8,0},{9,1},... | collective-permute-start | bytes 405512 | tf_op jit(solution)/shard_map/ppermute | solution.py:357
  32.7 5.9 %collective-permute-done.11 = bf16[528,128]{1,0:T(8,128)(2,1)S(1)} collective-permute-done((bf16[528,128]{1,0:T(8,128)(2,1)S(1)}, bf16[528,128]{1,0:T(8,128)(2,1)S(1)}, u32[]{:S(2)}, u32[]{:S(2)}) %collective-permute-start.11) | collective-permute-done | bytes 135200 | tf_op jit(solution)/shard_map/ppermute | solution.py:357
  39.7 1.4 collective-permute-start.9
  41.1 3.0 %collective-permute-done.7 = bf16[528,128]{1,0:T(8,128)(2,1)S(1)} collective-permute-done((bf16[528,128]{1,0:T(8,128)(2,1)S(1)}, bf16[528,128]{1,0:T(8,128)(2,1)S(1)}, u32[]{:S(2)}, u32[]{:S(2)}) %collective-permute-start.7) | collective-permute-done | bytes 135200 | tf_op jit(solution)/shard_map/ppermute | solution.py:357
  44.1 0.7 collective-permute-done.9
  44.9 3.4 %copy-done.1 = s32[256,16,519]{0,1,2:T(8,128)S(1)} copy-done((s32[256,16,519]{0,1,2:T(8,128)S(1)}, s32[256,16,519]{0,1,2:T(8,128)}, u32[]{:S(2)}) %copy-start.1) | copy-done | bytes 8503320
  48.3 9.1 %own_spectra.1 = (bf16[16,8,256,128]{3,2,1,0:T(8,128)(2,1)S(1)}, bf16[16,128]{1,0:T(8,128)(2,1)S(1)}) custom-call(s32[8304,256]{1,0:T(8,128)S(1)} %bitcast.19, s32[8304,256]{1,0:T(8,128)S(1)} %bitcast.20, f32[32,256]{1,0:T(8,128)S(1)} %bitcast_convert_fusion.gains_ref, bf16[256,256]{1,0:T(8,128)(2,1)S(1)} %copy-done.6, ...), custom_call_target="tpu_custom_call" | custom-call | flops 4294967296 | bytes 16891904 | tf_op jit(solution)/shard_map/own_spectra/pallas_call | solution.py:282
  57.4 0.6 slice.45
  58.0 0.6 constant_dynamic-update-slice_fusion.11
  58.6 1.0 slice.58
  59.6 0.6 collective-permute-start.18
  61.5 0.9 collective-permute-start.21
  62.4 0.6 collective-permute-start.12
  63.1 1.7 collective-permute-start.15
  65.4 3.0 %collective-permute-done.12 = bf16[528,128]{1,0:T(8,128)(2,1)S(1)} collective-permute-done((bf16[528,128]{1,0:T(8,128)(2,1)S(1)}, bf16[528,128]{1,0:T(8,128)(2,1)S(1)}, u32[]{:S(2)}, u32[]{:S(2)}) %collective-permute-start.12) | collective-permute-done | bytes 135200 | tf_op jit(solution)/shard_map/ppermute | solution.py:357
  68.6 1.3 collective-permute-done.15
  70.0 1.2 collective-permute-start.16
  71.5 11.2 %collective-permute-start.22 = (bf16[4224,128]{1,0:T(8,128)(2,1)S(1)}, bf16[4224,128]{1,0:T(8,128)(2,1)S(1)}, u32[]{:S(2)}, u32[]{:S(2)}) collective-permute-start(bf16[4224,128]{1,0:T(8,128)(2,1)S(1)} %get-tuple-element.29), channel_id=1, source_target_pairs={{0,1},{1,0},{2,3},{3,2},{4,5},{5,4},{6,7},{7,6},{8,9},{9,8},{10,11... | collective-permute-start | bytes 3244040 | tf_op jit(solution)/shard_map/ppermute | solution.py:357
  82.7 1.7 collective-permute-start.17
  84.8 3.4 %collective-permute-done.17 = bf16[1056,128]{1,0:T(8,128)(2,1)S(1)} collective-permute-done((bf16[1056,128]{1,0:T(8,128)(2,1)S(1)}, bf16[1056,128]{1,0:T(8,128)(2,1)S(1)}, u32[]{:S(2)}, u32[]{:S(2)}) %collective-permute-start.17) | collective-permute-done | bytes 270368 | tf_op jit(solution)/shard_map/ppermute | solution.py:357
  88.2 1.9 collective-permute-done.14
  90.3 4.8 %row_spectra.2.left_ref = bf16[16,1024,256]{2,1,0:T(8,128)(2,1)S(1)} custom-call(bf16[8448,128]{1,0:T(8,128)(2,1)S(1)} %constant_dynamic-update-slice_fusion.2.main_ref.next_ref, bf16[8448,128]{1,0:T(8,128)(2,1)S(1)} %constant_dynamic-update-slice_fusion.2.main_ref.next_ref, bf16[64,128]{1,0:T(8,128)(2,1)S(1)} %slice.60.parts_ref, bf16[256,256]{1,0:T(8,128)(2,1)S(1)} %copy-done.6), custom_call_target="tpu_custom_call" | custom-call | flops 2147483648 | bytes 10551296 | tf_op jit(solution)/shard_map/row_spectra/pallas_call | solution.py:423
  95.2 0.6 slice.62
  96.8 4.3 %row_products.2 = (s16[16,264,256]{2,1,0:T(8,128)(2,1)}, bf16[16,128]{1,0:T(8,128)(2,1)S(1)}) custom-call(bf16[16,8,256,128]{3,2,1,0:T(8,128)(2,1)S(1)} %get-tuple-element.14.own_ref, bf16[16,1024,256]{2,1,0:T(8,128)(2,1)S(1)} %row_spectra.2.left_ref, bf16[4224,128]{1,0:T(8,128)(2,1)S(1)} %get-tuple-element.20.refs_0_), custom_call_target="tpu_custom_call" | custom-call | flops 2147483648 | bytes 16777216 | tf_op jit(solution)/shard_map/row_products/pallas_call | solution.py:465
  101.1 9.7 %all-to-all-start.1 = ((s16[16,264,256]{2,1,0:T(8,128)(2,1)}), s16[16,264,256]{2,1,0:T(8,128)(2,1)}, u32[]{:S(2)}, u32[]{:S(2)}) async-start(s16[16,264,256]{2,1,0:T(8,128)(2,1)} %get-tuple-element.18), calls=%async_computation.1 | async-start | bytes 4325376 | tf_op jit(solution)/shard_map/all_to_all | solution.py:579
  111.2 2.4 %collective-permute-done.23 = bf16[4224,128]{1,0:T(8,128)(2,1)S(1)} collective-permute-done((bf16[4224,128]{1,0:T(8,128)(2,1)S(1)}, bf16[4224,128]{1,0:T(8,128)(2,1)S(1)}, u32[]{:S(2)}, u32[]{:S(2)}) %collective-permute-start.23) | collective-permute-done | bytes 1081376 | tf_op jit(solution)/shard_map/ppermute | solution.py:357
  113.7 4.8 %row_spectra.3.left_ref = bf16[16,1024,256]{2,1,0:T(8,128)(2,1)S(1)} custom-call(bf16[8448,128]{1,0:T(8,128)(2,1)S(1)} %constant_dynamic-update-slice_fusion.main_ref.next_ref, bf16[8448,128]{1,0:T(8,128)(2,1)S(1)} %constant_dynamic-update-slice_fusion.main_ref.next_ref, bf16[64,128]{1,0:T(8,128)(2,1)S(1)} %slice.63.parts_ref, bf16[256,256]{1,0:T(8,128)(2,1)S(1)} %copy-done.6), custom_call_target="tpu_custom_call" | custom-call | flops 2147483648 | bytes 10551296 | tf_op jit(solution)/shard_map/row_spectra/pallas_call | solution.py:423
  118.5 4.2 %row_products.3 = (s16[16,264,256]{2,1,0:T(8,128)(2,1)}, bf16[16,128]{1,0:T(8,128)(2,1)}) custom-call(bf16[16,8,256,128]{3,2,1,0:T(8,128)(2,1)S(1)} %copy-done.3, bf16[16,1024,256]{2,1,0:T(8,128)(2,1)S(1)} %row_spectra.3.left_ref, bf16[16,128]{1,0:T(8,128)(2,1)S(1)} %get-tuple-element.16.refs_0_), custom_call_target="tpu_custom_call" | custom-call | flops 2147483648 | bytes 16777216 | tf_op jit(solution)/shard_map/row_products/pallas_call | solution.py:465
  122.7 37.0 %all-to-all-done.1.coded_ref = s16[16,264,256]{2,1,0:T(8,128)(2,1)} async-done(((s16[16,264,256]{2,1,0:T(8,128)(2,1)}), s16[16,264,256]{2,1,0:T(8,128)(2,1)}, u32[]{:S(2)}, u32[]{:S(2)}) %all-to-all-start.1) | async-done | bytes 2162720 | tf_op jit(solution)/shard_map/all_to_all | solution.py:579
  159.8 5.0 %all-to-all-start = ((s16[16,264,256]{2,1,0:T(8,128)(2,1)}), s16[16,264,256]{2,1,0:T(8,128)(2,1)}, u32[]{:S(2)}, u32[]{:S(2)}) async-start(s16[16,264,256]{2,1,0:T(8,128)(2,1)} %get-tuple-element.17), calls=%async_computation | async-start | bytes 4325376 | tf_op jit(solution)/shard_map/all_to_all | solution.py:579
  164.8 8.7 %finish.2.refs_0_ = f32[256,64,128]{2,1,0:T(8,128)} custom-call(s32[4096]{0:T(1024)S(1)} %broadcast_multiply_fusion.slot_ref, s16[16,264,256]{2,1,0:T(8,128)(2,1)} %all-to-all-done.1.coded_ref), custom_call_target="tpu_custom_call" | custom-call | tf_op jit(solution)/shard_map/finish/pallas_call | solution.py:519
  173.5 40.2 %all-to-all-done.coded_ref = s16[16,264,256]{2,1,0:T(8,128)(2,1)} async-done(((s16[16,264,256]{2,1,0:T(8,128)(2,1)}), s16[16,264,256]{2,1,0:T(8,128)(2,1)}, u32[]{:S(2)}, u32[]{:S(2)}) %all-to-all-start) | async-done | bytes 2162720 | tf_op jit(solution)/shard_map/all_to_all | solution.py:579
  213.7 8.7 %finish.3 = f32[256,64,128]{2,1,0:T(8,128)} custom-call(s32[4096]{0:T(1024)S(1)} %broadcast_multiply_fusion.slot_ref, s16[16,264,256]{2,1,0:T(8,128)(2,1)} %all-to-all-done.coded_ref, f32[256,64,128]{2,1,0:T(8,128)} %finish.2.refs_0_), custom_call_target="tpu_custom_call", output_to_operand_aliasing={{}: (2, {})} | custom-call | tf_op jit(solution)/shard_map/finish/pallas_call | solution.py:519
  (93 shorter events, 7.0 us)
Async XLA Ops:
  0.0 3.4 %copy-start = (s32[256,16,519]{0,1,2:T(8,128)S(1)}, s32[256,16,519]{0,1,2:T(8,128)}, u32[]{:S(2)}) copy-start(s32[256,16,519]{0,1,2:T(8,128)} %param.4) | copy-start | bytes 25509892
  3.4 0.8 copy-start.7
  4.2 0.7 copy-start.9
  7.5 1.9 copy-start.4
  7.6 3.2 %collective-permute-start = (bf16[4224,128]{1,0:T(8,128)(2,1)S(1)}, bf16[4224,128]{1,0:T(8,128)(2,1)}, u32[]{:S(2)}, u32[]{:S(2)}) collective-permute-start(bf16[4224,128]{1,0:T(8,128)(2,1)S(1)} %constant_dynamic-slice_fusion.9), channel_id=1, source_target_pairs={{0,1},{1,0},{2,3},{3,2},{4,5},{5,4},{6,7},{7,6},{8,9},{9,8},{10,11... | collective-permute-start | bytes 3244040 | tf_op jit(solution)/shard_map/ppermute | solution.py:357
  9.4 15.0 %collective-permute-start.5 = (bf16[4224,128]{1,0:T(8,128)(2,1)}, bf16[4224,128]{1,0:T(8,128)(2,1)}, u32[]{:S(2)}, u32[]{:S(2)}) collective-permute-start(bf16[4224,128]{1,0:T(8,128)(2,1)} %constant_dynamic-slice_fusion.4), channel_id=1, source_target_pairs={{0,1},{1,0},{2,3},{3,2},{4,5},{5,4},{6,7},{7,6},{8,9},{9,8},{10,11... | collective-permute-start | bytes 3244040 | tf_op jit(solution)/shard_map/ppermute | solution.py:357
  12.7 0.8 copy-start.8
  12.8 13.3 %copy-start.11 = (bf16[2112,128]{1,0:T(8,128)(2,1)}, bf16[2112,128]{1,0:T(8,128)(2,1)S(1)}, u32[]{:S(2)}) copy-start(bf16[2112,128]{1,0:T(8,128)(2,1)S(1)} %get-tuple-element.33) | copy-start | bytes 1622020
  12.8 7.9 %collective-permute-start.1 = (bf16[1056,128]{1,0:T(8,128)(2,1)S(1)}, bf16[1056,128]{1,0:T(8,128)(2,1)}, u32[]{:S(2)}, u32[]{:S(2)}) collective-permute-start(bf16[1056,128]{1,0:T(8,128)(2,1)S(1)} %constant_dynamic-slice_fusion.8), channel_id=1, source_target_pairs={{0,2},{1,3},{2,0},{3,1},{4,6},{5,7},{6,4},{7,5},{8,10},{9,11},{10,... | collective-permute-start | bytes 811016 | tf_op jit(solution)/shard_map/ppermute | solution.py:357
  13.5 9.0 %collective-permute-start.3 = (bf16[1056,128]{1,0:T(8,128)(2,1)S(1)}, bf16[1056,128]{1,0:T(8,128)(2,1)S(1)}, u32[]{:S(2)}, u32[]{:S(2)}) collective-permute-start(bf16[1056,128]{1,0:T(8,128)(2,1)S(1)} %constant_dynamic-slice_fusion.6), channel_id=1, source_target_pairs={{0,4},{1,5},{2,6},{3,7},{4,0},{5,1},{6,2},{7,3},{8,12},{9,13},{10,... | collective-permute-start | bytes 811016 | tf_op jit(solution)/shard_map/ppermute | solution.py:357
  22.3 10.2 %collective-permute-start.2 = (bf16[528,128]{1,0:T(8,128)(2,1)S(1)}, bf16[528,128]{1,0:T(8,128)(2,1)S(1)}, u32[]{:S(2)}, u32[]{:S(2)}) collective-permute-start(bf16[528,128]{1,0:T(8,128)(2,1)S(1)} %constant_dynamic-slice_fusion.7), channel_id=1, source_target_pairs={{0,4},{1,5},{2,6},{3,7},{4,0},{5,1},{6,2},{7,3},{8,12},{9,13},{10,... | collective-permute-start | bytes 405512 | tf_op jit(solution)/shard_map/ppermute | solution.py:357
  26.2 3.9 %collective-permute-start.4 = (bf16[528,128]{1,0:T(8,128)(2,1)S(1)}, bf16[528,128]{1,0:T(8,128)(2,1)S(1)}, u32[]{:S(2)}, u32[]{:S(2)}) collective-permute-start(bf16[528,128]{1,0:T(8,128)(2,1)S(1)} %constant_dynamic-slice_fusion.5), channel_id=1, source_target_pairs={{0,2},{1,3},{2,0},{3,1},{4,6},{5,7},{6,4},{7,5},{8,10},{9,11},{10,... | collective-permute-start | bytes 405512 | tf_op jit(solution)/shard_map/ppermute | solution.py:357
  26.6 12.8 %collective-permute-start.6 = (bf16[1056,128]{1,0:T(8,128)(2,1)S(1)}, bf16[1056,128]{1,0:T(8,128)(2,1)S(1)}, u32[]{:S(2)}, u32[]{:S(2)}) collective-permute-start(bf16[1056,128]{1,0:T(8,128)(2,1)S(1)} %constant_dynamic-slice_fusion.3), channel_id=1, source_target_pairs={{0,2},{1,3},{2,0},{3,1},{4,6},{5,7},{6,4},{7,5},{8,10},{9,11},{10,... | collective-permute-start | bytes 811016 | tf_op jit(solution)/shard_map/ppermute | solution.py:357
  27.8 17.1 %copy-start.6 = (bf16[256,256]{1,0:T(8,128)(2,1)S(1)}, bf16[256,256]{1,0:T(8,128)(2,1)}, u32[]{:S(2)}) copy-start(bf16[256,256]{1,0:T(8,128)(2,1)} %constant.222.clone.weights_ref) | copy-start | bytes 393220
  27.8 11.8 %collective-permute-start.8 = (bf16[1056,128]{1,0:T(8,128)(2,1)S(1)}, bf16[1056,128]{1,0:T(8,128)(2,1)S(1)}, u32[]{:S(2)}, u32[]{:S(2)}) collective-permute-start(bf16[1056,128]{1,0:T(8,128)(2,1)S(1)} %constant_dynamic-slice_fusion.1), channel_id=1, source_target_pairs={{0,4},{1,5},{2,6},{3,7},{4,0},{5,1},{6,2},{7,3},{8,12},{9,13},{10,... | collective-permute-start | bytes 811016 | tf_op jit(solution)/shard_map/ppermute | solution.py:357
  30.1 8.5 %collective-permute-start.11 = (bf16[528,128]{1,0:T(8,128)(2,1)S(1)}, bf16[528,128]{1,0:T(8,128)(2,1)S(1)}, u32[]{:S(2)}, u32[]{:S(2)}) collective-permute-start(bf16[528,128]{1,0:T(8,128)(2,1)S(1)} %dynamic-slice_add_fusion.7.refs_1_), channel_id=1, source_target_pairs={{0,8},{1,9},{2,10},{3,11},{4,12},{5,13},{6,14},{7,15},{8,0},{9,1},... | collective-permute-start | bytes 405512 | tf_op jit(solution)/shard_map/ppermute | solution.py:357
  32.6 25.4 %collective-permute-start.10 = (bf16[528,128]{1,0:T(8,128)(2,1)S(1)}, bf16[528,128]{1,0:T(8,128)(2,1)S(1)}, u32[]{:S(2)}, u32[]{:S(2)}) collective-permute-start(bf16[528,128]{1,0:T(8,128)(2,1)S(1)} %dynamic-slice_add_fusion.8.refs_0_), channel_id=1, source_target_pairs={{0,8},{1,9},{2,10},{3,11},{4,12},{5,13},{6,14},{7,15},{8,0},{9,1},... | collective-permute-start | bytes 405512 | tf_op jit(solution)/shard_map/ppermute | solution.py:357
  39.2 22.2 %collective-permute-start.20 = (bf16[528,128]{1,0:T(8,128)(2,1)S(1)}, bf16[528,128]{1,0:T(8,128)(2,1)S(1)}, u32[]{:S(2)}, u32[]{:S(2)}) collective-permute-start(bf16[528,128]{1,0:T(8,128)(2,1)S(1)} %get-tuple-element.24), channel_id=1, source_target_pairs={{0,2},{1,3},{2,0},{3,1},{4,6},{5,7},{6,4},{7,5},{8,10},{9,11},{10,... | collective-permute-start | bytes 405512 | tf_op jit(solution)/shard_map/ppermute | solution.py:357
  39.5 4.5 %collective-permute-start.7 = (bf16[528,128]{1,0:T(8,128)(2,1)S(1)}, bf16[528,128]{1,0:T(8,128)(2,1)S(1)}, u32[]{:S(2)}, u32[]{:S(2)}) collective-permute-start(bf16[528,128]{1,0:T(8,128)(2,1)S(1)} %constant_dynamic-slice_fusion.2), channel_id=1, source_target_pairs={{0,4},{1,5},{2,6},{3,7},{4,0},{5,1},{6,2},{7,3},{8,12},{9,13},{10,... | collective-permute-start | bytes 405512 | tf_op jit(solution)/shard_map/ppermute | solution.py:357
  39.7 5.1 %collective-permute-start.9 = (bf16[528,128]{1,0:T(8,128)(2,1)S(1)}, bf16[528,128]{1,0:T(8,128)(2,1)S(1)}, u32[]{:S(2)}, u32[]{:S(2)}) collective-permute-start(bf16[528,128]{1,0:T(8,128)(2,1)S(1)} %constant_dynamic-slice_fusion), channel_id=1, source_target_pairs={{0,2},{1,3},{2,0},{3,1},{4,6},{5,7},{6,4},{7,5},{8,10},{9,11},{10,... | collective-permute-start | bytes 405512 | tf_op jit(solution)/shard_map/ppermute | solution.py:357
  44.9 3.4 %copy-start.1 = (s32[256,16,519]{0,1,2:T(8,128)S(1)}, s32[256,16,519]{0,1,2:T(8,128)}, u32[]{:S(2)}) copy-start(s32[256,16,519]{0,1,2:T(8,128)} %param.4) | copy-start | bytes 25509892
  48.3 16.5 %copy-start.12 = (bf16[2112,128]{1,0:T(8,128)(2,1)S(1)}, bf16[2112,128]{1,0:T(8,128)(2,1)}, u32[]{:S(2)}) copy-start(bf16[2112,128]{1,0:T(8,128)(2,1)} %copy-done.11) | copy-start | bytes 1622020
  57.4 39.3 %copy-start.2 = (bf16[16,8,256,128]{3,2,1,0:T(8,128)(2,1)}, bf16[16,8,256,128]{3,2,1,0:T(8,128)(2,1)S(1)}, u32[]{:S(2)}) copy-start(bf16[16,8,256,128]{3,2,1,0:T(8,128)(2,1)S(1)} %get-tuple-element.14.own_ref) | copy-start | bytes 25165828
  59.6 5.2 %collective-permute-start.18 = (bf16[528,128]{1,0:T(8,128)(2,1)S(1)}, bf16[528,128]{1,0:T(8,128)(2,1)S(1)}, u32[]{:S(2)}, u32[]{:S(2)}) collective-permute-start(bf16[528,128]{1,0:T(8,128)(2,1)S(1)} %get-tuple-element.22), channel_id=1, source_target_pairs={{0,4},{1,5},{2,6},{3,7},{4,0},{5,1},{6,2},{7,3},{8,12},{9,13},{10,... | collective-permute-start | bytes 405512 | tf_op jit(solution)/shard_map/ppermute | solution.py:357
  61.4 9.9 %copy-start.5 = (bf16[8448,128]{1,0:T(8,128)(2,1)S(1)}, bf16[8448,128]{1,0:T(8,128)(2,1)}, u32[]{:S(2)}) copy-start(bf16[8448,128]{1,0:T(8,128)(2,1)} %copy-done.4) | copy-start | bytes 6488068
  61.5 9.7 %collective-permute-start.21 = (bf16[1056,128]{1,0:T(8,128)(2,1)S(1)}, bf16[1056,128]{1,0:T(8,128)(2,1)S(1)}, u32[]{:S(2)}, u32[]{:S(2)}) collective-permute-start(bf16[1056,128]{1,0:T(8,128)(2,1)S(1)} %constant_dynamic-update-slice_fusion.6), channel_id=1, source_target_pairs={{0,4},{1,5},{2,6},{3,7},{4,0},{5,1},{6,2},{7,3},{8,12},{9,13},{10,... | collective-permute-start | bytes 811016 | tf_op jit(solution)/shard_map/ppermute | solution.py:357
  62.4 6.0 %collective-permute-start.12 = (bf16[528,128]{1,0:T(8,128)(2,1)S(1)}, bf16[528,128]{1,0:T(8,128)(2,1)S(1)}, u32[]{:S(2)}, u32[]{:S(2)}) collective-permute-start(bf16[528,128]{1,0:T(8,128)(2,1)S(1)} %broadcast_add_fusion.1), channel_id=1, source_target_pairs={{0,8},{1,9},{2,10},{3,11},{4,12},{5,13},{6,14},{7,15},{8,0},{9,1},... | collective-permute-start | bytes 405512 | tf_op jit(solution)/shard_map/ppermute | solution.py:357
  63.1 6.8 %collective-permute-start.15 = (bf16[528,128]{1,0:T(8,128)(2,1)S(1)}, bf16[528,128]{1,0:T(8,128)(2,1)S(1)}, u32[]{:S(2)}, u32[]{:S(2)}) collective-permute-start(bf16[528,128]{1,0:T(8,128)(2,1)S(1)} %broadcast_add_fusion), channel_id=1, source_target_pairs={{0,8},{1,9},{2,10},{3,11},{4,12},{5,13},{6,14},{7,15},{8,0},{9,1},... | collective-permute-start | bytes 405512 | tf_op jit(solution)/shard_map/ppermute | solution.py:357
  64.9 6.3 %collective-permute-start.19 = (bf16[1056,128]{1,0:T(8,128)(2,1)S(1)}, bf16[1056,128]{1,0:T(8,128)(2,1)S(1)}, u32[]{:S(2)}, u32[]{:S(2)}) collective-permute-start(bf16[1056,128]{1,0:T(8,128)(2,1)S(1)} %constant_dynamic-update-slice_fusion.10), channel_id=1, source_target_pairs={{0,2},{1,3},{2,0},{3,1},{4,6},{5,7},{6,4},{7,5},{8,10},{9,11},{10,... | collective-permute-start | bytes 811016 | tf_op jit(solution)/shard_map/ppermute | solution.py:357
  68.5 15.8 %collective-permute-start.13 = (bf16[528,128]{1,0:T(8,128)(2,1)S(1)}, bf16[528,128]{1,0:T(8,128)(2,1)S(1)}, u32[]{:S(2)}, u32[]{:S(2)}) collective-permute-start(bf16[528,128]{1,0:T(8,128)(2,1)S(1)} %get-tuple-element.26), channel_id=1, source_target_pairs={{0,4},{1,5},{2,6},{3,7},{4,0},{5,1},{6,2},{7,3},{8,12},{9,13},{10,... | collective-permute-start | bytes 405512 | tf_op jit(solution)/shard_map/ppermute | solution.py:357
  70.0 12.7 %collective-permute-start.16 = (bf16[528,128]{1,0:T(8,128)(2,1)S(1)}, bf16[528,128]{1,0:T(8,128)(2,1)S(1)}, u32[]{:S(2)}, u32[]{:S(2)}) collective-permute-start(bf16[528,128]{1,0:T(8,128)(2,1)S(1)} %get-tuple-element.28), channel_id=1, source_target_pairs={{0,2},{1,3},{2,0},{3,1},{4,6},{5,7},{6,4},{7,5},{8,10},{9,11},{10,... | collective-permute-start | bytes 405512 | tf_op jit(solution)/shard_map/ppermute | solution.py:357
  71.5 18.6 %collective-permute-start.22 = (bf16[4224,128]{1,0:T(8,128)(2,1)S(1)}, bf16[4224,128]{1,0:T(8,128)(2,1)S(1)}, u32[]{:S(2)}, u32[]{:S(2)}) collective-permute-start(bf16[4224,128]{1,0:T(8,128)(2,1)S(1)} %get-tuple-element.29), channel_id=1, source_target_pairs={{0,1},{1,0},{2,3},{3,2},{4,5},{5,4},{6,7},{7,6},{8,9},{9,8},{10,11... | collective-permute-start | bytes 3244040 | tf_op jit(solution)/shard_map/ppermute | solution.py:357
  82.7 5.5 %collective-permute-start.17 = (bf16[1056,128]{1,0:T(8,128)(2,1)S(1)}, bf16[1056,128]{1,0:T(8,128)(2,1)S(1)}, u32[]{:S(2)}, u32[]{:S(2)}) collective-permute-start(bf16[1056,128]{1,0:T(8,128)(2,1)S(1)} %constant_dynamic-update-slice_fusion.14), channel_id=1, source_target_pairs={{0,4},{1,5},{2,6},{3,7},{4,0},{5,1},{6,2},{7,3},{8,12},{9,13},{10,... | collective-permute-start | bytes 811016 | tf_op jit(solution)/shard_map/ppermute | solution.py:357
  84.4 5.7 %collective-permute-start.14 = (bf16[1056,128]{1,0:T(8,128)(2,1)S(1)}, bf16[1056,128]{1,0:T(8,128)(2,1)S(1)}, u32[]{:S(2)}, u32[]{:S(2)}) collective-permute-start(bf16[1056,128]{1,0:T(8,128)(2,1)S(1)} %constant_dynamic-update-slice_fusion.18), channel_id=1, source_target_pairs={{0,2},{1,3},{2,0},{3,1},{4,6},{5,7},{6,4},{7,5},{8,10},{9,11},{10,... | collective-permute-start | bytes 811016 | tf_op jit(solution)/shard_map/ppermute | solution.py:357
  101.1 58.7 %all-to-all-start.1 = ((s16[16,264,256]{2,1,0:T(8,128)(2,1)}), s16[16,264,256]{2,1,0:T(8,128)(2,1)}, u32[]{:S(2)}, u32[]{:S(2)}) async-start(s16[16,264,256]{2,1,0:T(8,128)(2,1)} %get-tuple-element.18), calls=%async_computation.1 | async-start | bytes 4325376 | tf_op jit(solution)/shard_map/all_to_all | solution.py:579
  110.8 2.7 %collective-permute-start.23 = (bf16[4224,128]{1,0:T(8,128)(2,1)S(1)}, bf16[4224,128]{1,0:T(8,128)(2,1)S(1)}, u32[]{:S(2)}, u32[]{:S(2)}) collective-permute-start(bf16[4224,128]{1,0:T(8,128)(2,1)S(1)} %get-tuple-element.20.refs_0_), channel_id=1, source_target_pairs={{0,1},{1,0},{2,3},{3,2},{4,5},{5,4},{6,7},{7,6},{8,9},{9,8},{10,11... | collective-permute-start | bytes 3244040 | tf_op jit(solution)/shard_map/ppermute | solution.py:357
  113.7 4.8 %copy-start.3 = (bf16[16,8,256,128]{3,2,1,0:T(8,128)(2,1)S(1)}, bf16[16,8,256,128]{3,2,1,0:T(8,128)(2,1)}, u32[]{:S(2)}) copy-start(bf16[16,8,256,128]{3,2,1,0:T(8,128)(2,1)} %copy-done.2) | copy-start | bytes 25165828
  159.8 5.0 %copy-start.10 = (s32[4096]{0:T(1024)S(1)}, s32[4096]{0:T(1024)}, u32[]{:S(2)}) copy-start(s32[4096]{0:T(1024)} %param.6) | copy-start | bytes 49156
  159.8 53.9 %all-to-all-start = ((s16[16,264,256]{2,1,0:T(8,128)(2,1)}), s16[16,264,256]{2,1,0:T(8,128)(2,1)}, u32[]{:S(2)}, u32[]{:S(2)}) async-start(s16[16,264,256]{2,1,0:T(8,128)(2,1)} %get-tuple-element.17), calls=%async_computation | async-start | bytes 4325376 | tf_op jit(solution)/shard_map/all_to_all | solution.py:579

commit v15 on v14

--- a/solution.py
+++ b/solution.py
@@ -333,6 +333,10 @@
             out_ref[last_rows + extra :, :] = jnp.zeros((left, LANES), out_ref.dtype)
 
 
+def at_hand(value):
+    return pltpu.with_memory_space_constraint(value, pltpu.HBM)
+
+
 def select_rows(place, words, gains, slots, rows, total):
     lines, count = words.shape
     block = total // STEPS
@@ -349,7 +353,7 @@
         out_shape=[jax.ShapeDtypeStruct((total, LANES), jnp.bfloat16)] * (rows // LANES),
         compiler_params=pltpu.CompilerParams(vmem_limit_bytes=8 << 20),
         name="select_rows",
-    )(place, slots, words, gains)
+    )(place, at_hand(slots), words, at_hand(gains))
 
 
 def swap(value, bit):
@@ -375,9 +379,8 @@
     return lax.dynamic_update_slice_in_dim(buffer, other, (1 - side(bit)) * size, 0)
 
 
-def quarters(half, behind):
+def quarters(half):
     size = half.shape[0] // 2
-    half = half + behind
     left, right = half[:size], half[size:]
     left_1, right_1 = reduce_half(left, 2), reduce_half(right, 4)
     return (left, right), (left_1, right_1)
@@ -387,8 +390,7 @@
     return reduce_half(first[0], 4), reduce_half(first[1], 2)
 
 
-def cross(second, behind):
-    second = [value + behind for value in second]
+def cross(second):
     return [value + swap(value, 8) for value in second]
 
 
@@ -396,10 +398,6 @@
     left_1, right_1 = gather_half(third[0], 4, first[0]), gather_half(third[1], 2, first[1])
     left, right = gather_half(left_1, 2, half[0]), gather_half(right_1, 4, half[1])
     return jnp.concatenate([left, right], axis=0)
-
-
-def zero_after(values):
-    return sum(value[0, 0] for value in values) * 0
 
 
 def rows_kernel(main_ref, next_ref, parts_ref, weights_ref, out_ref):
@@ -549,32 +547,18 @@
     weights = jnp.asarray(filter_weights(ch))
     place = lax.axis_index("feed").reshape(1)
     picked = select_rows(place, words, scales, feed_slot.reshape(-1, LANES), ROWS, total)
-    nothing = jnp.zeros((), jnp.bfloat16)
-    halves, firsts, behind = [], [], nothing
-    for value in picked:
-        half, first = quarters(reduce_half(value, 1), behind)
-        behind = zero_after(first)
-        halves.append(half)
-        firsts.append(first)
+    halves, firsts = zip(*[quarters(reduce_half(value, 1)) for value in picked])
     seconds = [eighths(first) for first in firsts]
     own, zero = own_spectra(words, scales.astype(jnp.float32), weights, ch, spectra, sum(seconds, ()))
-    thirds, behind = [], nothing
-    for second in seconds:
-        third = cross(second, behind)
-        if not thirds:
-            third[0] = third[0] + zero[0, 0]
-        behind = zero_after(third)
-        thirds.append(third)
+    thirds = [cross(second) for second in seconds]
+    thirds[0][0] = thirds[0][0] + zero[0, 0]
     ends = [gathered(*parts) for parts in zip(halves, firsts, thirds)]
-    out, lefts = None, []
+    out, after = None, [ends[-1]]
     for index in range(pieces):
-        end = ends[index] if not lefts else ends[index] + zero_after([lefts[-1][0]])
-        rows = gather_half(end, 1, picked[index])
+        rows = gather_half(ends[index], 1, picked[index])
         parts = rows[lines : lines + 4 * ch]
-        lefts.append(row_spectra(rows, parts, weights, ch, spectra))
-    after = [end]
-    for index in range(pieces):
-        coded, done = row_products(own, lefts[index], after)
+        left = row_spectra(rows, parts, weights, ch, spectra)
+        coded, done = row_products(own, left, after)
         after = [done]
         moved = lax.all_to_all(coded, "feed", split_axis=0, concat_axis=0, tiled=True)
         out = finish(moved, feed_slot * 2, index, pieces, 1.0 / spectra, out)

time: 223 us -> 203 us (0.910)
  local copies, waits for them, and re-layouts: 14.5 us -> 6.23 us
  starting transfers between devices: 43 us -> 34.8 us
  between operations: 3.61 us -> 0.41 us
    ppermute x24, starting transfers between devices: 28.2 us -> 21.5 us  [swap(): return lax.ppermute(value, 'feed', pairs)]
    unnamed x26 -> x22, local copies, waits for them, and re-layouts: 8.68 us -> 3.47 us
    slice x6 -> x1, local copies, waits for them, and re-layouts: 3.72 us -> 0.54 us  [through_rows(): thirds[0][0] = thirds[0][0] + zero[0, 0]]
  transfers between devices with their start and end apart: 26 -> 26, of which waited for: 13 -> 17; matrix products, arithmetic and copies ran while one was open for 5% -> 3% of each run, Pallas kernels for 12% -> 13%
where the time goes in v15:
time: 203 us
  waiting for transfers between devices  109 us (54%)
  Pallas kernels  47.2 us (23%)
  starting transfers between devices  34.8 us (17%)
  local copies, waits for them, and re-layouts  6.23 us (3%)
  other arithmetic  5.2 us (3%)
    all_to_all x2, waiting for transfers between devices, through_rows(): lax.all_to_all(coded, 'feed', split_axis=0, concat_axis=0, tiled=True)  77 us
    ppermute x24, waiting for transfers between devices, swap(): return lax.ppermute(value, 'feed', pairs)  31.8 us
    ppermute x24, starting transfers between devices, swap(): return lax.ppermute(value, 'feed', pairs)  21.5 us
    pallas_call x2, Pallas kernels, finish(): pl.pallas_call(functools.partial(finish_kernel, scale), grid=(columns //...  16.5 us
    all_to_all x2, starting transfers between devices, through_rows(): lax.all_to_all(coded, 'feed', split_axis=0, concat_axis=0, tiled=True)  13.2 us
    pallas_call x2, Pallas kernels, row_spectra(): pl.pallas_call(rows_kernel, grid=(spectra // (STEPS * STEP),), in_specs=[...  9.59 us
    pallas_call x1, Pallas kernels, own_spectra(): pl.pallas_call(own_kernel, grid=(steps,), in_specs=[pl.BlockSpec((main, c...  8.99 us
    pallas_call x2, Pallas kernels, row_products(): pl.pallas_call(products_kernel, grid=(ch // each,), in_specs=[pl.BlockSpe...  8.61 us
  transfers between devices with their start and end apart: 26, of which 17 were waited for; matrix products, arithmetic and copies ran while one was open for 3% of the time, Pallas kernels for 13%

profile of v15, /device:TPU:13, one launch (start us, length us, event | category | flops | bytes accessed | tf_op | source)
XLA Modules:
  0.0 202.6 jit_solution(18109898693873473581)
XLA Ops:
  0.0 3.4 %copy-done = s32[256,16,519]{0,1,2:T(8,128)S(1)} copy-done((s32[256,16,519]{0,1,2:T(8,128)S(1)}, s32[256,16,519]{0,1,2:T(8,128)}, u32[]{:S(2)}) %copy-start) | copy-done | bytes 8503320
  3.4 3.5 %select_rows.1 = (bf16[8448,128]{1,0:T(8,128)(2,1)S(1)}, bf16[8448,128]{1,0:T(8,128)(2,1)S(1)}) custom-call(s32[1]{0:T(128)} %bitcast.3.place_ref, s32[32,128]{1,0:T(8,128)} %bitcast.19, s32[8304,256]{1,0:T(8,128)S(1)} %bitcast.13, s32[32,256]{1,0:T(8,128)} %bitcast.18), custom_call_target="tpu_custom_call" | custom-call | tf_op jit(solution)/shard_map/select_rows/pallas_call | solution.py:343
  6.9 1.2 constant_dynamic-slice_fusion.4
  8.1 0.7 collective-permute-start.5
  8.8 0.4 collective-permute-start
  9.3 2.2 %collective-permute-done.5 = bf16[4224,128]{1,0:T(8,128)(2,1)} collective-permute-done((bf16[4224,128]{1,0:T(8,128)(2,1)}, bf16[4224,128]{1,0:T(8,128)(2,1)}, u32[]{:S(2)}, u32[]{:S(2)}) %collective-permute-start.5) | collective-permute-done | bytes 1081376 | tf_op jit(solution)/shard_map/ppermute | solution.py:361
  11.4 1.7 dynamic-slice_add_fusion
  13.6 1.8 dynamic-slice_add_fusion.1
  15.5 1.2 collective-permute-start.3
  16.8 1.3 collective-permute-start.1
  18.1 2.9 %collective-permute-done.8 = bf16[1056,128]{1,0:T(8,128)(2,1)S(1)} collective-permute-done((bf16[1056,128]{1,0:T(8,128)(2,1)S(1)}, bf16[1056,128]{1,0:T(8,128)(2,1)S(1)}, u32[]{:S(2)}, u32[]{:S(2)}) %collective-permute-start.8) | collective-permute-done | bytes 270368 | tf_op jit(solution)/shard_map/ppermute | solution.py:361
  21.5 0.9 collective-permute-start.7
  22.4 4.3 %collective-permute-done.1 = bf16[1056,128]{1,0:T(8,128)(2,1)S(1)} collective-permute-done((bf16[1056,128]{1,0:T(8,128)(2,1)S(1)}, bf16[1056,128]{1,0:T(8,128)(2,1)S(1)}, u32[]{:S(2)}, u32[]{:S(2)}) %collective-permute-start.1) | collective-permute-done | bytes 270368 | tf_op jit(solution)/shard_map/ppermute | solution.py:361
  26.8 1.4 collective-permute-start.2
  28.6 3.1 %collective-permute-done.2 = bf16[528,128]{1,0:T(8,128)(2,1)S(1)} collective-permute-done((bf16[528,128]{1,0:T(8,128)(2,1)S(1)}, bf16[528,128]{1,0:T(8,128)(2,1)S(1)}, u32[]{:S(2)}, u32[]{:S(2)}) %collective-permute-start.2) | collective-permute-done | bytes 135200 | tf_op jit(solution)/shard_map/ppermute | solution.py:361
  31.7 2.4 %collective-permute-start.17 = (bf16[528,128]{1,0:T(8,128)(2,1)S(1)}, bf16[528,128]{1,0:T(8,128)(2,1)S(1)}, u32[]{:S(2)}, u32[]{:S(2)}) collective-permute-start(bf16[528,128]{1,0:T(8,128)(2,1)S(1)} %dynamic-slice_add_fusion.9.refs_0_), channel_id=1, source_target_pairs={{0,8},{1,9},{2,10},{3,11},{4,12},{5,13},{6,14},{7,15},{8,0},{9,1},... | collective-permute-start | bytes 405512 | tf_op jit(solution)/shard_map/ppermute | solution.py:361
  34.1 0.5 collective-permute-start.20
  34.7 2.0 collective-permute-start.10
  36.7 0.5 collective-permute-start.13
  37.3 9.0 %own_spectra.1 = (bf16[16,8,256,128]{3,2,1,0:T(8,128)(2,1)S(1)}, bf16[16,128]{1,0:T(8,128)(2,1)S(1)}) custom-call(s32[8304,256]{1,0:T(8,128)S(1)} %bitcast.16, s32[8304,256]{1,0:T(8,128)S(1)} %bitcast.17, f32[32,256]{1,0:T(8,128)S(1)} %bitcast_convert_fusion.gains_ref, bf16[256,256]{1,0:T(8,128)(2,1)S(1)} %copy-done.5, ...), custom_call_target="tpu_custom_call" | custom-call | flops 4294967296 | bytes 16891904 | tf_op jit(solution)/shard_map/own_spectra/pallas_call | solution.py:282
  46.3 0.5 slice.26
  46.8 1.7 collective-permute-done.17
  48.5 0.6 constant_dynamic-update-slice_fusion.9
  49.2 2.2 %collective-permute-done.20 = bf16[528,128]{1,0:T(8,128)(2,1)S(1)} collective-permute-done((bf16[528,128]{1,0:T(8,128)(2,1)S(1)}, bf16[528,128]{1,0:T(8,128)(2,1)S(1)}, u32[]{:S(2)}, u32[]{:S(2)}) %collective-permute-start.20) | collective-permute-done | bytes 135200 | tf_op jit(solution)/shard_map/ppermute | solution.py:361
  51.5 0.3 collective-permute-start.21
  51.8 2.6 %collective-permute-done.10 = bf16[528,128]{1,0:T(8,128)(2,1)S(1)} collective-permute-done((bf16[528,128]{1,0:T(8,128)(2,1)S(1)}, bf16[528,128]{1,0:T(8,128)(2,1)S(1)}, u32[]{:S(2)}, u32[]{:S(2)}) %collective-permute-start.10) | collective-permute-done | bytes 135200 | tf_op jit(solution)/shard_map/ppermute | solution.py:361
  54.4 0.6 collective-permute-start.11
  55.0 2.3 %collective-permute-done.13 = bf16[528,128]{1,0:T(8,128)(2,1)S(1)} collective-permute-done((bf16[528,128]{1,0:T(8,128)(2,1)S(1)}, bf16[528,128]{1,0:T(8,128)(2,1)S(1)}, u32[]{:S(2)}, u32[]{:S(2)}) %collective-permute-start.13) | collective-permute-done | bytes 135200 | tf_op jit(solution)/shard_map/ppermute | solution.py:361
  57.3 0.3 collective-permute-start.14
  57.6 2.2 %collective-permute-done.18 = bf16[528,128]{1,0:T(8,128)(2,1)S(1)} collective-permute-done((bf16[528,128]{1,0:T(8,128)(2,1)S(1)}, bf16[528,128]{1,0:T(8,128)(2,1)S(1)}, u32[]{:S(2)}, u32[]{:S(2)}) %collective-permute-start.18) | collective-permute-done | bytes 135200 | tf_op jit(solution)/shard_map/ppermute | solution.py:361
  60.2 2.3 %collective-permute-start.22 = (bf16[1056,128]{1,0:T(8,128)(2,1)S(1)}, bf16[1056,128]{1,0:T(8,128)(2,1)S(1)}, u32[]{:S(2)}, u32[]{:S(2)}) collective-permute-start(bf16[1056,128]{1,0:T(8,128)(2,1)S(1)} %constant_dynamic-update-slice_fusion.4), channel_id=1, source_target_pairs={{0,4},{1,5},{2,6},{3,7},{4,0},{5,1},{6,2},{7,3},{8,12},{9,13},{10,... | collective-permute-start | bytes 811016 | tf_op jit(solution)/shard_map/ppermute | solution.py:361
  62.8 1.1 collective-permute-start.12
  64.0 1.4 collective-permute-start.15
  65.4 2.9 %collective-permute-done.19 = bf16[1056,128]{1,0:T(8,128)(2,1)S(1)} collective-permute-done((bf16[1056,128]{1,0:T(8,128)(2,1)S(1)}, bf16[1056,128]{1,0:T(8,128)(2,1)S(1)}, u32[]{:S(2)}, u32[]{:S(2)}) %collective-permute-start.19) | collective-permute-done | bytes 270368 | tf_op jit(solution)/shard_map/ppermute | solution.py:361
  68.7 2.6 %collective-permute-start.23 = (bf16[4224,128]{1,0:T(8,128)(2,1)S(1)}, bf16[4224,128]{1,0:T(8,128)(2,1)S(1)}, u32[]{:S(2)}, u32[]{:S(2)}) collective-permute-start(bf16[4224,128]{1,0:T(8,128)(2,1)S(1)} %get-tuple-element.27), channel_id=1, source_target_pairs={{0,1},{1,0},{2,3},{3,2},{4,5},{5,4},{6,7},{7,6},{8,9},{9,8},{10,11... | collective-permute-start | bytes 3244040 | tf_op jit(solution)/shard_map/ppermute | solution.py:361
  71.3 2.9 %collective-permute-done.12 = bf16[1056,128]{1,0:T(8,128)(2,1)S(1)} collective-permute-done((bf16[1056,128]{1,0:T(8,128)(2,1)S(1)}, bf16[1056,128]{1,0:T(8,128)(2,1)S(1)}, u32[]{:S(2)}, u32[]{:S(2)}) %collective-permute-start.12) | collective-permute-done | bytes 270368 | tf_op jit(solution)/shard_map/ppermute | solution.py:361
  74.7 4.8 %row_spectra.3.left_ref = bf16[16,1024,256]{2,1,0:T(8,128)(2,1)S(1)} custom-call(bf16[8448,128]{1,0:T(8,128)(2,1)S(1)} %constant_dynamic-update-slice_fusion.main_ref.next_ref, bf16[8448,128]{1,0:T(8,128)(2,1)S(1)} %constant_dynamic-update-slice_fusion.main_ref.next_ref, bf16[64,128]{1,0:T(8,128)(2,1)S(1)} %slice.33.parts_ref, bf16[256,256]{1,0:T(8,128)(2,1)S(1)} %copy-done.5), custom_call_target="tpu_custom_call" | custom-call | flops 2147483648 | bytes 10551296 | tf_op jit(solution)/shard_map/row_spectra/pallas_call | solution.py:421
  79.5 4.3 %row_products.2 = (s16[16,264,256]{2,1,0:T(8,128)(2,1)}, bf16[16,128]{1,0:T(8,128)(2,1)S(1)}) custom-call(bf16[16,8,256,128]{3,2,1,0:T(8,128)(2,1)S(1)} %get-tuple-element.14.own_ref, bf16[16,1024,256]{2,1,0:T(8,128)(2,1)S(1)} %row_spectra.3.left_ref, bf16[4224,128]{1,0:T(8,128)(2,1)S(1)} %get-tuple-element.29.refs_0_), custom_call_target="tpu_custom_call" | custom-call | flops 2147483648 | bytes 16777216 | tf_op jit(solution)/shard_map/row_products/pallas_call | solution.py:463
  83.8 8.2 %all-to-all-start.1 = ((s16[16,264,256]{2,1,0:T(8,128)(2,1)}), s16[16,264,256]{2,1,0:T(8,128)(2,1)}, u32[]{:S(2)}, u32[]{:S(2)}) async-start(s16[16,264,256]{2,1,0:T(8,128)(2,1)} %get-tuple-element.18), calls=%async_computation.1 | async-start | bytes 4325376 | tf_op jit(solution)/shard_map/all_to_all | solution.py:563
  92.0 0.4 collective-permute-start.16
  92.3 2.4 %collective-permute-done.16 = bf16[4224,128]{1,0:T(8,128)(2,1)S(1)} collective-permute-done((bf16[4224,128]{1,0:T(8,128)(2,1)S(1)}, bf16[4224,128]{1,0:T(8,128)(2,1)S(1)}, u32[]{:S(2)}, u32[]{:S(2)}) %collective-permute-start.16) | collective-permute-done | bytes 1081376 | tf_op jit(solution)/shard_map/ppermute | solution.py:361
  94.9 4.8 %row_spectra.2.left_ref = bf16[16,1024,256]{2,1,0:T(8,128)(2,1)S(1)} custom-call(bf16[8448,128]{1,0:T(8,128)(2,1)S(1)} %constant_dynamic-update-slice_fusion.10.main_ref.next_ref, bf16[8448,128]{1,0:T(8,128)(2,1)S(1)} %constant_dynamic-update-slice_fusion.10.main_ref.next_ref, bf16[64,128]{1,0:T(8,128)(2,1)S(1)} %slice.32.parts_ref, ...), custom_call_target="tpu_custom_call" | custom-call | flops 2147483648 | bytes 10551296 | tf_op jit(solution)/shard_map/row_spectra/pallas_call | solution.py:421
  99.7 4.3 %row_products.3 = (s16[16,264,256]{2,1,0:T(8,128)(2,1)}, bf16[16,128]{1,0:T(8,128)(2,1)}) custom-call(bf16[16,8,256,128]{3,2,1,0:T(8,128)(2,1)S(1)} %copy-done.2, bf16[16,1024,256]{2,1,0:T(8,128)(2,1)S(1)} %row_spectra.2.left_ref, bf16[16,128]{1,0:T(8,128)(2,1)S(1)} %get-tuple-element.16.refs_0_), custom_call_target="tpu_custom_call" | custom-call | flops 2147483648 | bytes 16777216 | tf_op jit(solution)/shard_map/row_products/pallas_call | solution.py:463
  104.0 36.9 %all-to-all-done.1.coded_ref = s16[16,264,256]{2,1,0:T(8,128)(2,1)} async-done(((s16[16,264,256]{2,1,0:T(8,128)(2,1)}), s16[16,264,256]{2,1,0:T(8,128)(2,1)}, u32[]{:S(2)}, u32[]{:S(2)}) %all-to-all-start.1) | async-done | bytes 2162720 | tf_op jit(solution)/shard_map/all_to_all | solution.py:563
  140.9 5.0 %all-to-all-start = ((s16[16,264,256]{2,1,0:T(8,128)(2,1)}), s16[16,264,256]{2,1,0:T(8,128)(2,1)S(1)}, u32[]{:S(2)}, u32[]{:S(2)}) async-start(s16[16,264,256]{2,1,0:T(8,128)(2,1)} %get-tuple-element.17), calls=%async_computation | async-start | bytes 4325376 | tf_op jit(solution)/shard_map/all_to_all | solution.py:563
  146.0 8.7 %finish.2.refs_0_ = f32[256,64,128]{2,1,0:T(8,128)} custom-call(s32[4096]{0:T(1024)S(1)} %broadcast_multiply_fusion.slot_ref, s16[16,264,256]{2,1,0:T(8,128)(2,1)} %all-to-all-done.1.coded_ref), custom_call_target="tpu_custom_call" | custom-call | tf_op jit(solution)/shard_map/finish/pallas_call | solution.py:517
  154.7 40.1 %all-to-all-done.coded_ref = s16[16,264,256]{2,1,0:T(8,128)(2,1)S(1)} async-done(((s16[16,264,256]{2,1,0:T(8,128)(2,1)}), s16[16,264,256]{2,1,0:T(8,128)(2,1)S(1)}, u32[]{:S(2)}, u32[]{:S(2)}) %all-to-all-start) | async-done | bytes 2162720 | tf_op jit(solution)/shard_map/all_to_all | solution.py:563
  194.8 7.9 %finish.3 = f32[256,64,128]{2,1,0:T(8,128)} custom-call(s32[4096]{0:T(1024)S(1)} %broadcast_multiply_fusion.slot_ref, s16[16,264,256]{2,1,0:T(8,128)(2,1)S(1)} %all-to-all-done.coded_ref, f32[256,64,128]{2,1,0:T(8,128)} %finish.2.refs_0_), custom_call_target="tpu_custom_call", output_to_operand_aliasing={{}: (2, {})} | custom-call | tf_op jit(solution)/shard_map/finish/pallas_call | solution.py:517
  (82 shorter events, 3.9 us)
Async XLA Ops:
  0.0 3.4 %copy-start = (s32[256,16,519]{0,1,2:T(8,128)S(1)}, s32[256,16,519]{0,1,2:T(8,128)}, u32[]{:S(2)}) copy-start(s32[256,16,519]{0,1,2:T(8,128)} %param.4) | copy-start | bytes 25509892
  6.9 1.9 copy-start.3
  6.9 2.4 %copy-start.6 = (s32[2,16,256]{2,1,0:T(8,128)S(1)}, s32[2,16,256]{2,1,0:T(8,128)}, u32[]{:S(2)}) copy-start(s32[2,16,256]{2,1,0:T(8,128)} %param.5) | copy-start | bytes 98308
  8.1 3.3 %collective-permute-start.5 = (bf16[4224,128]{1,0:T(8,128)(2,1)}, bf16[4224,128]{1,0:T(8,128)(2,1)}, u32[]{:S(2)}, u32[]{:S(2)}) collective-permute-start(bf16[4224,128]{1,0:T(8,128)(2,1)} %constant_dynamic-slice_fusion.4), channel_id=1, source_target_pairs={{0,1},{1,0},{2,3},{3,2},{4,5},{5,4},{6,7},{7,6},{8,9},{9,8},{10,11... | collective-permute-start | bytes 3244040 | tf_op jit(solution)/shard_map/ppermute | solution.py:361
  8.8 28.5 %slice-start = ((s8[8503296]{0:T(1024)(128)(4,1)}), s8[114688]{0:T(1024)(128)(4,1)S(1)}, s32[]{:S(2)}) async-start(s8[8503296]{0:T(1024)(128)(4,1)} %bitcast.14), calls=%async_computation.2 | async-start | bytes 229376
  8.8 4.8 %collective-permute-start = (bf16[4224,128]{1,0:T(8,128)(2,1)S(1)}, bf16[4224,128]{1,0:T(8,128)(2,1)}, u32[]{:S(2)}, u32[]{:S(2)}) collective-permute-start(bf16[4224,128]{1,0:T(8,128)(2,1)S(1)} %constant_dynamic-slice_fusion.9), channel_id=1, source_target_pairs={{0,1},{1,0},{2,3},{3,2},{4,5},{5,4},{6,7},{7,6},{8,9},{9,8},{10,11... | collective-permute-start | bytes 3244040 | tf_op jit(solution)/shard_map/ppermute | solution.py:361
  11.4 2.2 %copy-start.4 = (bf16[8448,128]{1,0:T(8,128)(2,1)S(1)}, bf16[8448,128]{1,0:T(8,128)(2,1)}, u32[]{:S(2)}) copy-start(bf16[8448,128]{1,0:T(8,128)(2,1)} %copy-done.3) | copy-start | bytes 6488068
  13.1 24.2 %slice-start.1 = ((s8[8503296]{0:T(1024)(128)(4,1)}), s8[4194304]{0:T(1024)(128)(4,1)S(1)}, s32[]{:S(2)}) async-start(s8[8503296]{0:T(1024)(128)(4,1)} %bitcast.14), calls=%async_computation.3 | async-start | bytes 8388608
  13.2 7.8 %collective-permute-start.8 = (bf16[1056,128]{1,0:T(8,128)(2,1)S(1)}, bf16[1056,128]{1,0:T(8,128)(2,1)S(1)}, u32[]{:S(2)}, u32[]{:S(2)}) collective-permute-start(bf16[1056,128]{1,0:T(8,128)(2,1)S(1)} %constant_dynamic-slice_fusion.1), channel_id=1, source_target_pairs={{0,4},{1,5},{2,6},{3,7},{4,0},{5,1},{6,2},{7,3},{8,12},{9,13},{10,... | collective-permute-start | bytes 811016 | tf_op jit(solution)/shard_map/ppermute | solution.py:361
  13.5 7.9 %collective-permute-start.6 = (bf16[1056,128]{1,0:T(8,128)(2,1)S(1)}, bf16[1056,128]{1,0:T(8,128)(2,1)S(1)}, u32[]{:S(2)}, u32[]{:S(2)}) collective-permute-start(bf16[1056,128]{1,0:T(8,128)(2,1)S(1)} %constant_dynamic-slice_fusion.3), channel_id=1, source_target_pairs={{0,2},{1,3},{2,0},{3,1},{4,6},{5,7},{6,4},{7,5},{8,10},{9,11},{10,... | collective-permute-start | bytes 811016 | tf_op jit(solution)/shard_map/ppermute | solution.py:361
  15.4 21.9 %slice-start.2 = ((s8[8503296]{0:T(1024)(128)(4,1)}), s8[4194304]{0:T(1024)(128)(4,1)S(1)}, s32[]{:S(2)}) async-start(s8[8503296]{0:T(1024)(128)(4,1)} %bitcast.14), calls=%async_computation.4 | async-start | bytes 8388608
  15.5 12.6 %collective-permute-start.3 = (bf16[1056,128]{1,0:T(8,128)(2,1)S(1)}, bf16[1056,128]{1,0:T(8,128)(2,1)S(1)}, u32[]{:S(2)}, u32[]{:S(2)}) collective-permute-start(bf16[1056,128]{1,0:T(8,128)(2,1)S(1)} %constant_dynamic-slice_fusion.6), channel_id=1, source_target_pairs={{0,4},{1,5},{2,6},{3,7},{4,0},{5,1},{6,2},{7,3},{8,12},{9,13},{10,... | collective-permute-start | bytes 811016 | tf_op jit(solution)/shard_map/ppermute | solution.py:361
  16.8 9.9 %collective-permute-start.1 = (bf16[1056,128]{1,0:T(8,128)(2,1)S(1)}, bf16[1056,128]{1,0:T(8,128)(2,1)S(1)}, u32[]{:S(2)}, u32[]{:S(2)}) collective-permute-start(bf16[1056,128]{1,0:T(8,128)(2,1)S(1)} %constant_dynamic-slice_fusion.8), channel_id=1, source_target_pairs={{0,2},{1,3},{2,0},{3,1},{4,6},{5,7},{6,4},{7,5},{8,10},{9,11},{10,... | collective-permute-start | bytes 811016 | tf_op jit(solution)/shard_map/ppermute | solution.py:361
  21.1 15.6 %collective-permute-start.9 = (bf16[528,128]{1,0:T(8,128)(2,1)S(1)}, bf16[528,128]{1,0:T(8,128)(2,1)S(1)}, u32[]{:S(2)}, u32[]{:S(2)}) collective-permute-start(bf16[528,128]{1,0:T(8,128)(2,1)S(1)} %constant_dynamic-slice_fusion), channel_id=1, source_target_pairs={{0,2},{1,3},{2,0},{3,1},{4,6},{5,7},{6,4},{7,5},{8,10},{9,11},{10,... | collective-permute-start | bytes 405512 | tf_op jit(solution)/shard_map/ppermute | solution.py:361
  21.5 15.8 %copy-start.5 = (bf16[256,256]{1,0:T(8,128)(2,1)S(1)}, bf16[256,256]{1,0:T(8,128)(2,1)}, u32[]{:S(2)}) copy-start(bf16[256,256]{1,0:T(8,128)(2,1)} %constant.217.clone.weights_ref) | copy-start | bytes 393220
  21.5 13.2 %collective-permute-start.7 = (bf16[528,128]{1,0:T(8,128)(2,1)S(1)}, bf16[528,128]{1,0:T(8,128)(2,1)S(1)}, u32[]{:S(2)}, u32[]{:S(2)}) collective-permute-start(bf16[528,128]{1,0:T(8,128)(2,1)S(1)} %constant_dynamic-slice_fusion.2), channel_id=1, source_target_pairs={{0,4},{1,5},{2,6},{3,7},{4,0},{5,1},{6,2},{7,3},{8,12},{9,13},{10,... | collective-permute-start | bytes 405512 | tf_op jit(solution)/shard_map/ppermute | solution.py:361
  26.8 4.8 %collective-permute-start.2 = (bf16[528,128]{1,0:T(8,128)(2,1)S(1)}, bf16[528,128]{1,0:T(8,128)(2,1)S(1)}, u32[]{:S(2)}, u32[]{:S(2)}) collective-permute-start(bf16[528,128]{1,0:T(8,128)(2,1)S(1)} %constant_dynamic-slice_fusion.7), channel_id=1, source_target_pairs={{0,4},{1,5},{2,6},{3,7},{4,0},{5,1},{6,2},{7,3},{8,12},{9,13},{10,... | collective-permute-start | bytes 405512 | tf_op jit(solution)/shard_map/ppermute | solution.py:361
  28.3 5.8 %collective-permute-start.4 = (bf16[528,128]{1,0:T(8,128)(2,1)S(1)}, bf16[528,128]{1,0:T(8,128)(2,1)S(1)}, u32[]{:S(2)}, u32[]{:S(2)}) collective-permute-start(bf16[528,128]{1,0:T(8,128)(2,1)S(1)} %constant_dynamic-slice_fusion.5), channel_id=1, source_target_pairs={{0,2},{1,3},{2,0},{3,1},{4,6},{5,7},{6,4},{7,5},{8,10},{9,11},{10,... | collective-permute-start | bytes 405512 | tf_op jit(solution)/shard_map/ppermute | solution.py:361
  31.7 16.8 %collective-permute-start.17 = (bf16[528,128]{1,0:T(8,128)(2,1)S(1)}, bf16[528,128]{1,0:T(8,128)(2,1)S(1)}, u32[]{:S(2)}, u32[]{:S(2)}) collective-permute-start(bf16[528,128]{1,0:T(8,128)(2,1)S(1)} %dynamic-slice_add_fusion.9.refs_0_), channel_id=1, source_target_pairs={{0,8},{1,9},{2,10},{3,11},{4,12},{5,13},{6,14},{7,15},{8,0},{9,1},... | collective-permute-start | bytes 405512 | tf_op jit(solution)/shard_map/ppermute | solution.py:361
  34.1 17.3 %collective-permute-start.20 = (bf16[528,128]{1,0:T(8,128)(2,1)S(1)}, bf16[528,128]{1,0:T(8,128)(2,1)S(1)}, u32[]{:S(2)}, u32[]{:S(2)}) collective-permute-start(bf16[528,128]{1,0:T(8,128)(2,1)S(1)} %dynamic-slice_add_fusion.8.refs_1_), channel_id=1, source_target_pairs={{0,8},{1,9},{2,10},{3,11},{4,12},{5,13},{6,14},{7,15},{8,0},{9,1},... | collective-permute-start | bytes 405512 | tf_op jit(solution)/shard_map/ppermute | solution.py:361
  34.7 19.6 %collective-permute-start.10 = (bf16[528,128]{1,0:T(8,128)(2,1)S(1)}, bf16[528,128]{1,0:T(8,128)(2,1)S(1)}, u32[]{:S(2)}, u32[]{:S(2)}) collective-permute-start(bf16[528,128]{1,0:T(8,128)(2,1)S(1)} %dynamic-slice_add_fusion.7.refs_2_), channel_id=1, source_target_pairs={{0,8},{1,9},{2,10},{3,11},{4,12},{5,13},{6,14},{7,15},{8,0},{9,1},... | collective-permute-start | bytes 405512 | tf_op jit(solution)/shard_map/ppermute | solution.py:361
  36.7 20.5 %collective-permute-start.13 = (bf16[528,128]{1,0:T(8,128)(2,1)S(1)}, bf16[528,128]{1,0:T(8,128)(2,1)S(1)}, u32[]{:S(2)}, u32[]{:S(2)}) collective-permute-start(bf16[528,128]{1,0:T(8,128)(2,1)S(1)} %dynamic-slice_add_fusion.6.refs_3_), channel_id=1, source_target_pairs={{0,8},{1,9},{2,10},{3,11},{4,12},{5,13},{6,14},{7,15},{8,0},{9,1},... | collective-permute-start | bytes 405512 | tf_op jit(solution)/shard_map/ppermute | solution.py:361
  46.3 33.2 %copy-start.1 = (bf16[16,8,256,128]{3,2,1,0:T(8,128)(2,1)}, bf16[16,8,256,128]{3,2,1,0:T(8,128)(2,1)S(1)}, u32[]{:S(2)}) copy-start(bf16[16,8,256,128]{3,2,1,0:T(8,128)(2,1)S(1)} %get-tuple-element.14.own_ref) | copy-start | bytes 25165828
  49.1 10.7 %collective-permute-start.18 = (bf16[528,128]{1,0:T(8,128)(2,1)S(1)}, bf16[528,128]{1,0:T(8,128)(2,1)S(1)}, u32[]{:S(2)}, u32[]{:S(2)}) collective-permute-start(bf16[528,128]{1,0:T(8,128)(2,1)S(1)} %get-tuple-element.20), channel_id=1, source_target_pairs={{0,4},{1,5},{2,6},{3,7},{4,0},{5,1},{6,2},{7,3},{8,12},{9,13},{10,... | collective-permute-start | bytes 405512 | tf_op jit(solution)/shard_map/ppermute | solution.py:361
  51.5 8.7 %collective-permute-start.21 = (bf16[528,128]{1,0:T(8,128)(2,1)S(1)}, bf16[528,128]{1,0:T(8,128)(2,1)S(1)}, u32[]{:S(2)}, u32[]{:S(2)}) collective-permute-start(bf16[528,128]{1,0:T(8,128)(2,1)S(1)} %get-tuple-element.22), channel_id=1, source_target_pairs={{0,2},{1,3},{2,0},{3,1},{4,6},{5,7},{6,4},{7,5},{8,10},{9,11},{10,... | collective-permute-start | bytes 405512 | tf_op jit(solution)/shard_map/ppermute | solution.py:361
  54.4 8.3 %collective-permute-start.11 = (bf16[528,128]{1,0:T(8,128)(2,1)S(1)}, bf16[528,128]{1,0:T(8,128)(2,1)S(1)}, u32[]{:S(2)}, u32[]{:S(2)}) collective-permute-start(bf16[528,128]{1,0:T(8,128)(2,1)S(1)} %get-tuple-element.24), channel_id=1, source_target_pairs={{0,4},{1,5},{2,6},{3,7},{4,0},{5,1},{6,2},{7,3},{8,12},{9,13},{10,... | collective-permute-start | bytes 405512 | tf_op jit(solution)/shard_map/ppermute | solution.py:361
  57.3 6.6 %collective-permute-start.14 = (bf16[528,128]{1,0:T(8,128)(2,1)S(1)}, bf16[528,128]{1,0:T(8,128)(2,1)S(1)}, u32[]{:S(2)}, u32[]{:S(2)}) collective-permute-start(bf16[528,128]{1,0:T(8,128)(2,1)S(1)} %get-tuple-element.26), channel_id=1, source_target_pairs={{0,2},{1,3},{2,0},{3,1},{4,6},{5,7},{6,4},{7,5},{8,10},{9,11},{10,... | collective-permute-start | bytes 405512 | tf_op jit(solution)/shard_map/ppermute | solution.py:361
  59.9 8.5 %collective-permute-start.19 = (bf16[1056,128]{1,0:T(8,128)(2,1)S(1)}, bf16[1056,128]{1,0:T(8,128)(2,1)S(1)}, u32[]{:S(2)}, u32[]{:S(2)}) collective-permute-start(bf16[1056,128]{1,0:T(8,128)(2,1)S(1)} %constant_dynamic-update-slice_fusion.8), channel_id=1, source_target_pairs={{0,2},{1,3},{2,0},{3,1},{4,6},{5,7},{6,4},{7,5},{8,10},{9,11},{10,... | collective-permute-start | bytes 811016 | tf_op jit(solution)/shard_map/ppermute | solution.py:361
  60.2 8.3 %collective-permute-start.22 = (bf16[1056,128]{1,0:T(8,128)(2,1)S(1)}, bf16[1056,128]{1,0:T(8,128)(2,1)S(1)}, u32[]{:S(2)}, u32[]{:S(2)}) collective-permute-start(bf16[1056,128]{1,0:T(8,128)(2,1)S(1)} %constant_dynamic-update-slice_fusion.4), channel_id=1, source_target_pairs={{0,4},{1,5},{2,6},{3,7},{4,0},{5,1},{6,2},{7,3},{8,12},{9,13},{10,... | collective-permute-start | bytes 811016 | tf_op jit(solution)/shard_map/ppermute | solution.py:361
  62.8 11.4 %collective-permute-start.12 = (bf16[1056,128]{1,0:T(8,128)(2,1)S(1)}, bf16[1056,128]{1,0:T(8,128)(2,1)S(1)}, u32[]{:S(2)}, u32[]{:S(2)}) collective-permute-start(bf16[1056,128]{1,0:T(8,128)(2,1)S(1)} %constant_dynamic-update-slice_fusion.18), channel_id=1, source_target_pairs={{0,2},{1,3},{2,0},{3,1},{4,6},{5,7},{6,4},{7,5},{8,10},{9,11},{10,... | collective-permute-start | bytes 811016 | tf_op jit(solution)/shard_map/ppermute | solution.py:361
  64.0 10.3 %collective-permute-start.15 = (bf16[1056,128]{1,0:T(8,128)(2,1)S(1)}, bf16[1056,128]{1,0:T(8,128)(2,1)S(1)}, u32[]{:S(2)}, u32[]{:S(2)}) collective-permute-start(bf16[1056,128]{1,0:T(8,128)(2,1)S(1)} %constant_dynamic-update-slice_fusion.14), channel_id=1, source_target_pairs={{0,4},{1,5},{2,6},{3,7},{4,0},{5,1},{6,2},{7,3},{8,12},{9,13},{10,... | collective-permute-start | bytes 811016 | tf_op jit(solution)/shard_map/ppermute | solution.py:361
  68.7 5.8 %collective-permute-start.23 = (bf16[4224,128]{1,0:T(8,128)(2,1)S(1)}, bf16[4224,128]{1,0:T(8,128)(2,1)S(1)}, u32[]{:S(2)}, u32[]{:S(2)}) collective-permute-start(bf16[4224,128]{1,0:T(8,128)(2,1)S(1)} %get-tuple-element.27), channel_id=1, source_target_pairs={{0,1},{1,0},{2,3},{3,2},{4,5},{5,4},{6,7},{7,6},{8,9},{9,8},{10,11... | collective-permute-start | bytes 3244040 | tf_op jit(solution)/shard_map/ppermute | solution.py:361
  83.8 57.1 %all-to-all-start.1 = ((s16[16,264,256]{2,1,0:T(8,128)(2,1)}), s16[16,264,256]{2,1,0:T(8,128)(2,1)}, u32[]{:S(2)}, u32[]{:S(2)}) async-start(s16[16,264,256]{2,1,0:T(8,128)(2,1)} %get-tuple-element.18), calls=%async_computation.1 | async-start | bytes 4325376 | tf_op jit(solution)/shard_map/all_to_all | solution.py:563
  92.0 2.7 %collective-permute-start.16 = (bf16[4224,128]{1,0:T(8,128)(2,1)S(1)}, bf16[4224,128]{1,0:T(8,128)(2,1)S(1)}, u32[]{:S(2)}, u32[]{:S(2)}) collective-permute-start(bf16[4224,128]{1,0:T(8,128)(2,1)S(1)} %get-tuple-element.29.refs_0_), channel_id=1, source_target_pairs={{0,1},{1,0},{2,3},{3,2},{4,5},{5,4},{6,7},{7,6},{8,9},{9,8},{10,11... | collective-permute-start | bytes 3244040 | tf_op jit(solution)/shard_map/ppermute | solution.py:361
  94.9 4.8 %copy-start.2 = (bf16[16,8,256,128]{3,2,1,0:T(8,128)(2,1)S(1)}, bf16[16,8,256,128]{3,2,1,0:T(8,128)(2,1)}, u32[]{:S(2)}) copy-start(bf16[16,8,256,128]{3,2,1,0:T(8,128)(2,1)} %copy-done.1) | copy-start | bytes 25165828
  140.9 5.0 %copy-start.7 = (s32[4096]{0:T(1024)S(1)}, s32[4096]{0:T(1024)}, u32[]{:S(2)}) copy-start(s32[4096]{0:T(1024)} %param.6) | copy-start | bytes 49156
  140.9 53.9 %all-to-all-start = ((s16[16,264,256]{2,1,0:T(8,128)(2,1)}), s16[16,264,256]{2,1,0:T(8,128)(2,1)S(1)}, u32[]{:S(2)}, u32[]{:S(2)}) async-start(s16[16,264,256]{2,1,0:T(8,128)(2,1)} %get-tuple-element.17), calls=%async_computation | async-start | bytes 4325376 | tf_op jit(solution)/shard_map/all_to_all | solution.py:563

commit v16 on v15

--- a/solution.py
+++ b/solution.py
@@ -310,27 +310,27 @@
     )(words, words, gains, weights, *after)
 
 
-def select_kernel(last_rows, place_ref, slots_ref, words_ref, gains_ref, *outs):
-    step = pl.program_id(0)
-    count, rows = words_ref.shape[1], len(outs) * LANES
-    words = words_ref[...].astype(jnp.float32).astype(jnp.bfloat16)
+def select_kernel(block, place_ref, slots_ref, words_ref, gains_ref, *outs):
+    lines, count = words_ref.shape
+    rows = len(outs) * LANES
     place = lax.broadcasted_iota(jnp.int32, (count, rows), 0) + place_ref[0] * count
     slots = jnp.concatenate([slots_ref[index : index + 1, :] for index in range(len(outs))], axis=1)
     choice = jnp.where(slots == place, 1.0, 0.0).astype(jnp.bfloat16)
-    taken = jnp.dot(words, choice, preferred_element_type=jnp.float32).astype(outs[0].dtype)
-    for index, out_ref in enumerate(outs):
-        out_ref[...] = taken[:, index * LANES : (index + 1) * LANES]
-
-    @pl.when(step == pl.num_programs(0) - 1)
-    def _():
-        gains = gains_ref[...]
-        parts = jnp.concatenate([gains >> 4, gains & 15], axis=0).astype(jnp.float32).astype(jnp.bfloat16)
-        extra = parts.shape[0]
-        gains = jnp.dot(parts, choice, preferred_element_type=jnp.float32).astype(outs[0].dtype)
+
+    def put(first, values):
+        size = values.shape[0]
+        values = values.astype(jnp.float32).astype(jnp.bfloat16)
+        taken = jnp.dot(values, choice, preferred_element_type=jnp.float32).astype(outs[0].dtype)
         for index, out_ref in enumerate(outs):
-            out_ref[last_rows : last_rows + extra, :] = gains[:, index * LANES : (index + 1) * LANES]
-            left = out_ref.shape[0] - last_rows - extra
-            out_ref[last_rows + extra :, :] = jnp.zeros((left, LANES), out_ref.dtype)
+            out_ref[first : first + size, :] = taken[:, index * LANES : (index + 1) * LANES]
+
+    for first in range(0, lines, block):
+        put(first, words_ref[first : min(first + block, lines), :])
+    gains = gains_ref[...]
+    put(lines, jnp.concatenate([gains >> 4, gains & 15], axis=0))
+    first = lines + 2 * gains.shape[0]
+    for out_ref in outs:
+        out_ref[first:, :] = jnp.zeros((out_ref.shape[0] - first, LANES), out_ref.dtype)
 
 
 def at_hand(value):
@@ -338,20 +338,18 @@
 
 
 def select_rows(place, words, gains, slots, rows, total):
-    lines, count = words.shape
-    block = total // STEPS
     return pl.pallas_call(
-        functools.partial(select_kernel, lines - (STEPS - 1) * block),
-        grid=(STEPS,),
+        functools.partial(select_kernel, total // STEPS),
+        grid=(1,),
         in_specs=[
             pl.BlockSpec(memory_space=pltpu.SMEM),
             pl.BlockSpec((8, LANES), lambda i: (0, 0)),
-            pl.BlockSpec((block, count), lambda i: (i, 0)),
+            pl.BlockSpec(memory_space=pltpu.VMEM),
             pl.BlockSpec(gains.shape, lambda i: (0, 0)),
         ],
-        out_specs=[pl.BlockSpec((block, LANES), lambda i: (i, 0))] * (rows // LANES),
+        out_specs=[pl.BlockSpec(memory_space=pltpu.VMEM)] * (rows // LANES),
         out_shape=[jax.ShapeDtypeStruct((total, LANES), jnp.bfloat16)] * (rows // LANES),
-        compiler_params=pltpu.CompilerParams(vmem_limit_bytes=8 << 20),
+        compiler_params=pltpu.CompilerParams(vmem_limit_bytes=12 << 20),
         name="select_rows",
     )(place, at_hand(slots), words, at_hand(gains))
 
@@ -400,30 +398,33 @@
     return jnp.concatenate([left, right], axis=0)
 
 
-def rows_kernel(main_ref, next_ref, parts_ref, weights_ref, out_ref):
-    step = pl.program_id(0)
-    ch, rows = out_ref.shape[0], main_ref.shape[1]
-    words = jnp.concatenate([main_ref[...], next_ref[...]], axis=0).astype(jnp.float32).astype(jnp.int32)
+def rows_kernel(words_ref, parts_ref, weights_ref, out_ref):
+    ch, rows = out_ref.shape[0], words_ref.shape[1]
+    width = 2 * STEPS * STEP
+    main = STEPS * STEP * ch
     parts = parts_ref[...].astype(jnp.float32)
     gains = parts[: 2 * ch] * 16.0 + parts[2 * ch :]
 
-    def store(b, c, real, imag):
-        spot = pl.ds(pl.multiple_of(step * (2 * STEPS * STEP), 2 * STEPS * STEP) + b * 2 * STEP, 2 * STEP)
-        out_ref[c, spot, :rows] = jnp.concatenate([real, imag], axis=0).astype(out_ref.dtype)
-        out_ref[c, spot, rows:] = jnp.concatenate([imag, -real], axis=0).astype(out_ref.dtype)
-
-    spectra_of(weights_ref, levels_of(words), gains, ch, store)
+    @pl.loop(0, out_ref.shape[1] // width)
+    def _(step):
+        words = words_ref[pl.ds(pl.multiple_of(step * main, main), main + STEP * ch), :]
+        words = words.astype(jnp.float32).astype(jnp.int32)
+
+        def store(b, c, real, imag):
+            spot = pl.ds(pl.multiple_of(step * width, width) + b * 2 * STEP, 2 * STEP)
+            out_ref[c, spot, :rows] = jnp.concatenate([real, imag], axis=0).astype(out_ref.dtype)
+            out_ref[c, spot, rows:] = jnp.concatenate([imag, -real], axis=0).astype(out_ref.dtype)
+
+        spectra_of(weights_ref, levels_of(words), gains, ch, store)
 
 
 def row_spectra(words, parts, weights, ch, spectra):
     rows = words.shape[1]
-    main = STEPS * STEP * ch
     return pl.pallas_call(
         rows_kernel,
-        grid=(spectra // (STEPS * STEP),),
+        grid=(1,),
         in_specs=[
-            pl.BlockSpec((main, rows), lambda i: (i, 0)),
-            pl.BlockSpec((STEP * ch, rows), lambda i: ((i + 1) * STEPS, 0)),
+            pl.BlockSpec(memory_space=pltpu.VMEM),
             pl.BlockSpec(parts.shape, lambda i: (0, 0)),
             pl.BlockSpec(weights.shape, lambda i: (0, 0)),
         ],
@@ -436,7 +437,7 @@
             transcendentals=0,
         ),
         name="row_spectra",
-    )(words, words, parts, weights)
+    )(words, parts, weights)
 
 
 def products_kernel(own_ref, left_ref, *refs):
@@ -498,14 +499,18 @@
                     :, piece * LANES : (piece + 1) * LANES
                 ]
 
-    for part in range(together):
-        for i in range(LANES):
-            line = slot_ref[(step * together + part) * LANES + i]
-            tile[i * pieces : (i + 1) * pieces, :] = products[pl.ds(pl.multiple_of(line, pieces), pieces), :]
-        for piece in range(pieces):
-            turned = tile[pl.ds(piece, LANES, stride=pieces), :].T
-            mixed[pl.ds(part * pieces + piece, LANES, stride=8), :] = turned
-    out_ref[...] = mixed[...].reshape(out_ref.shape)
+    tiles = out_ref.shape[1] // 8
+
+    @pl.loop(0, tiles)
+    def _(j):
+        for part in range(together):
+            for i in range(LANES):
+                line = slot_ref[((step * tiles + j) * together + part) * LANES + i]
+                tile[i * pieces : (i + 1) * pieces, :] = products[pl.ds(pl.multiple_of(line, pieces), pieces), :]
+            for piece in range(pieces):
+                turned = tile[pl.ds(piece, LANES, stride=pieces), :].T
+                mixed[pl.ds(part * pieces + piece, LANES, stride=8), :] = turned
+        out_ref[:, pl.ds(pl.multiple_of(j * 8, 8), 8), :] = mixed[...].reshape(out_ref.shape[0], 8, LANES)
 
 
 def finish(coded, places, index, pieces, scale, before):
@@ -516,13 +521,13 @@
     earlier = [] if before is None else [before]
     return pl.pallas_call(
         functools.partial(finish_kernel, scale),
-        grid=(columns // 8,),
+        grid=(columns // 16,),
         in_specs=[
             pl.BlockSpec(memory_space=pltpu.SMEM),
             pl.BlockSpec(memory_space=pltpu.VMEM),
         ]
         + [pl.BlockSpec(memory_space=pl.ANY)] * len(earlier),
-        out_specs=pl.BlockSpec((rows, 8, LANES), lambda i: (index, i, 0)),
+        out_specs=pl.BlockSpec((rows, 16, LANES), lambda i: (index, i, 0)),
         out_shape=jax.ShapeDtypeStruct((pieces * rows, columns, LANES), jnp.float32),
         scratch_shapes=[
             pltpu.VMEM((feeds * width // LANES, LANES), jnp.float32),

time: 203 us -> 201 us (level)
  no operation moved by 1% of the time
where the time goes in v16:
time: 201 us
  waiting for transfers between devices  109 us (54%)
  Pallas kernels  45.5 us (23%)
  starting transfers between devices  34.7 us (17%)
  local copies, waits for them, and re-layouts  6.24 us (3%)
  other arithmetic  5.21 us (3%)
    all_to_all x2, waiting for transfers between devices, through_rows(): lax.all_to_all(coded, 'feed', split_axis=0, concat_axis=0, tiled=True)  77.2 us
    ppermute x24, waiting for transfers between devices, swap(): return lax.ppermute(value, 'feed', pairs)  31.8 us
    ppermute x24, starting transfers between devices, swap(): return lax.ppermute(value, 'feed', pairs)  21.6 us
    pallas_call x2, Pallas kernels, finish(): pl.pallas_call(functools.partial(finish_kernel, scale), grid=(columns //...  16.3 us
    all_to_all x2, starting transfers between devices, through_rows(): lax.all_to_all(coded, 'feed', split_axis=0, concat_axis=0, tiled=True)  13.2 us
    pallas_call x2, Pallas kernels, row_spectra(): pl.pallas_call(rows_kernel, grid=(1,), in_specs=[pl.BlockSpec(memory_spac...  9.44 us
    pallas_call x1, Pallas kernels, own_spectra(): pl.pallas_call(own_kernel, grid=(steps,), in_specs=[pl.BlockSpec((main, c...  9.05 us
    pallas_call x2, Pallas kernels, row_products(): pl.pallas_call(products_kernel, grid=(ch // each,), in_specs=[pl.BlockSpe...  8.62 us
  transfers between devices with their start and end apart: 26, of which 17 were waited for; matrix products, arithmetic and copies ran while one was open for 3% of the time, Pallas kernels for 13%

profile of v16, /device:TPU:13, one launch (start us, length us, event | category | flops | bytes accessed | tf_op | source)
XLA Modules:
  0.0 201.0 jit_solution(6430582949375269477)
XLA Ops:
  0.0 3.4 %copy-done = s32[256,16,519]{0,1,2:T(8,128)S(1)} copy-done((s32[256,16,519]{0,1,2:T(8,128)S(1)}, s32[256,16,519]{0,1,2:T(8,128)}, u32[]{:S(2)}) %copy-start) | copy-done | bytes 8503320
  3.4 2.1 %select_rows.1 = (bf16[8448,128]{1,0:T(8,128)(2,1)S(1)}, bf16[8448,128]{1,0:T(8,128)(2,1)S(1)}) custom-call(s32[1]{0:T(128)} %bitcast.3.place_ref, s32[32,128]{1,0:T(8,128)} %bitcast.19, s32[8304,256]{1,0:T(8,128)S(1)} %bitcast.13, s32[32,256]{1,0:T(8,128)} %bitcast.18), custom_call_target="tpu_custom_call" | custom-call | tf_op jit(solution)/shard_map/select_rows/pallas_call | solution.py:341
  5.5 1.2 constant_dynamic-slice_fusion.4
  6.7 0.7 collective-permute-start.5
  7.5 0.4 collective-permute-start
  7.9 2.2 %collective-permute-done.5 = bf16[4224,128]{1,0:T(8,128)(2,1)} collective-permute-done((bf16[4224,128]{1,0:T(8,128)(2,1)}, bf16[4224,128]{1,0:T(8,128)(2,1)}, u32[]{:S(2)}, u32[]{:S(2)}) %collective-permute-start.5) | collective-permute-done | bytes 1081376 | tf_op jit(solution)/shard_map/ppermute | solution.py:359
  10.0 1.7 dynamic-slice_add_fusion
  12.3 1.8 dynamic-slice_add_fusion.1
  14.2 1.2 collective-permute-start.3
  15.4 1.3 collective-permute-start.1
  16.7 2.9 %collective-permute-done.8 = bf16[1056,128]{1,0:T(8,128)(2,1)S(1)} collective-permute-done((bf16[1056,128]{1,0:T(8,128)(2,1)S(1)}, bf16[1056,128]{1,0:T(8,128)(2,1)S(1)}, u32[]{:S(2)}, u32[]{:S(2)}) %collective-permute-start.8) | collective-permute-done | bytes 270368 | tf_op jit(solution)/shard_map/ppermute | solution.py:359
  19.7 0.3 collective-permute-start.9
  20.1 0.9 collective-permute-start.7
  21.0 4.3 %collective-permute-done.1 = bf16[1056,128]{1,0:T(8,128)(2,1)S(1)} collective-permute-done((bf16[1056,128]{1,0:T(8,128)(2,1)S(1)}, bf16[1056,128]{1,0:T(8,128)(2,1)S(1)}, u32[]{:S(2)}, u32[]{:S(2)}) %collective-permute-start.1) | collective-permute-done | bytes 270368 | tf_op jit(solution)/shard_map/ppermute | solution.py:359
  25.4 1.4 collective-permute-start.2
  26.9 0.3 collective-permute-start.4
  27.2 3.1 %collective-permute-done.2 = bf16[528,128]{1,0:T(8,128)(2,1)S(1)} collective-permute-done((bf16[528,128]{1,0:T(8,128)(2,1)S(1)}, bf16[528,128]{1,0:T(8,128)(2,1)S(1)}, u32[]{:S(2)}, u32[]{:S(2)}) %collective-permute-start.2) | collective-permute-done | bytes 135200 | tf_op jit(solution)/shard_map/ppermute | solution.py:359
  30.3 2.4 %collective-permute-start.17 = (bf16[528,128]{1,0:T(8,128)(2,1)S(1)}, bf16[528,128]{1,0:T(8,128)(2,1)S(1)}, u32[]{:S(2)}, u32[]{:S(2)}) collective-permute-start(bf16[528,128]{1,0:T(8,128)(2,1)S(1)} %dynamic-slice_add_fusion.9.refs_0_), channel_id=1, source_target_pairs={{0,8},{1,9},{2,10},{3,11},{4,12},{5,13},{6,14},{7,15},{8,0},{9,1},... | collective-permute-start | bytes 405512 | tf_op jit(solution)/shard_map/ppermute | solution.py:359
  32.7 0.5 collective-permute-start.20
  33.3 2.0 collective-permute-start.10
  35.3 0.5 collective-permute-start.13
  35.9 9.1 %own_spectra.1 = (bf16[16,8,256,128]{3,2,1,0:T(8,128)(2,1)S(1)}, bf16[16,128]{1,0:T(8,128)(2,1)S(1)}) custom-call(s32[8304,256]{1,0:T(8,128)S(1)} %bitcast.16, s32[8304,256]{1,0:T(8,128)S(1)} %bitcast.17, f32[32,256]{1,0:T(8,128)S(1)} %bitcast_convert_fusion.gains_ref, bf16[256,256]{1,0:T(8,128)(2,1)S(1)} %copy-done.5, ...), custom_call_target="tpu_custom_call" | custom-call | flops 4294967296 | bytes 16891904 | tf_op jit(solution)/shard_map/own_spectra/pallas_call | solution.py:282
  44.9 0.5 slice.26
  45.5 1.6 collective-permute-done.17
  47.1 0.6 constant_dynamic-update-slice_fusion.9
  47.8 2.2 %collective-permute-done.20 = bf16[528,128]{1,0:T(8,128)(2,1)S(1)} collective-permute-done((bf16[528,128]{1,0:T(8,128)(2,1)S(1)}, bf16[528,128]{1,0:T(8,128)(2,1)S(1)}, u32[]{:S(2)}, u32[]{:S(2)}) %collective-permute-start.20) | collective-permute-done | bytes 135200 | tf_op jit(solution)/shard_map/ppermute | solution.py:359
  50.3 2.6 %collective-permute-done.10 = bf16[528,128]{1,0:T(8,128)(2,1)S(1)} collective-permute-done((bf16[528,128]{1,0:T(8,128)(2,1)S(1)}, bf16[528,128]{1,0:T(8,128)(2,1)S(1)}, u32[]{:S(2)}, u32[]{:S(2)}) %collective-permute-start.10) | collective-permute-done | bytes 135200 | tf_op jit(solution)/shard_map/ppermute | solution.py:359
  53.0 0.6 collective-permute-start.11
  53.6 2.2 %collective-permute-done.13 = bf16[528,128]{1,0:T(8,128)(2,1)S(1)} collective-permute-done((bf16[528,128]{1,0:T(8,128)(2,1)S(1)}, bf16[528,128]{1,0:T(8,128)(2,1)S(1)}, u32[]{:S(2)}, u32[]{:S(2)}) %collective-permute-start.13) | collective-permute-done | bytes 135200 | tf_op jit(solution)/shard_map/ppermute | solution.py:359
  56.2 2.3 %collective-permute-done.18 = bf16[528,128]{1,0:T(8,128)(2,1)S(1)} collective-permute-done((bf16[528,128]{1,0:T(8,128)(2,1)S(1)}, bf16[528,128]{1,0:T(8,128)(2,1)S(1)}, u32[]{:S(2)}, u32[]{:S(2)}) %collective-permute-start.18) | collective-permute-done | bytes 135200 | tf_op jit(solution)/shard_map/ppermute | solution.py:359
  58.8 2.3 %collective-permute-start.22 = (bf16[1056,128]{1,0:T(8,128)(2,1)S(1)}, bf16[1056,128]{1,0:T(8,128)(2,1)S(1)}, u32[]{:S(2)}, u32[]{:S(2)}) collective-permute-start(bf16[1056,128]{1,0:T(8,128)(2,1)S(1)} %constant_dynamic-update-slice_fusion.4), channel_id=1, source_target_pairs={{0,4},{1,5},{2,6},{3,7},{4,0},{5,1},{6,2},{7,3},{8,12},{9,13},{10,... | collective-permute-start | bytes 811016 | tf_op jit(solution)/shard_map/ppermute | solution.py:359
  61.4 1.1 collective-permute-start.12
  62.6 1.4 collective-permute-start.15
  64.1 2.9 %collective-permute-done.19 = bf16[1056,128]{1,0:T(8,128)(2,1)S(1)} collective-permute-done((bf16[1056,128]{1,0:T(8,128)(2,1)S(1)}, bf16[1056,128]{1,0:T(8,128)(2,1)S(1)}, u32[]{:S(2)}, u32[]{:S(2)}) %collective-permute-start.19) | collective-permute-done | bytes 270368 | tf_op jit(solution)/shard_map/ppermute | solution.py:359
  67.4 2.6 %collective-permute-start.23 = (bf16[4224,128]{1,0:T(8,128)(2,1)S(1)}, bf16[4224,128]{1,0:T(8,128)(2,1)S(1)}, u32[]{:S(2)}, u32[]{:S(2)}) collective-permute-start(bf16[4224,128]{1,0:T(8,128)(2,1)S(1)} %get-tuple-element.27), channel_id=1, source_target_pairs={{0,1},{1,0},{2,3},{3,2},{4,5},{5,4},{6,7},{7,6},{8,9},{9,8},{10,11... | collective-permute-start | bytes 3244040 | tf_op jit(solution)/shard_map/ppermute | solution.py:359
  69.9 2.8 %collective-permute-done.12 = bf16[1056,128]{1,0:T(8,128)(2,1)S(1)} collective-permute-done((bf16[1056,128]{1,0:T(8,128)(2,1)S(1)}, bf16[1056,128]{1,0:T(8,128)(2,1)S(1)}, u32[]{:S(2)}, u32[]{:S(2)}) %collective-permute-start.12) | collective-permute-done | bytes 270368 | tf_op jit(solution)/shard_map/ppermute | solution.py:359
  73.3 4.7 %row_spectra.3.left_ref = bf16[16,1024,256]{2,1,0:T(8,128)(2,1)S(1)} custom-call(bf16[8448,128]{1,0:T(8,128)(2,1)S(1)} %constant_dynamic-update-slice_fusion.words_ref, bf16[64,128]{1,0:T(8,128)(2,1)S(1)} %slice.33.parts_ref, bf16[256,256]{1,0:T(8,128)(2,1)S(1)} %copy-done.5), custom_call_target="tpu_custom_call" | custom-call | flops 2147483648 | bytes 10551296 | tf_op jit(solution)/shard_map/row_spectra/pallas_call | solution.py:423
  78.1 4.3 %row_products.2 = (s16[16,264,256]{2,1,0:T(8,128)(2,1)}, bf16[16,128]{1,0:T(8,128)(2,1)S(1)}) custom-call(bf16[16,8,256,128]{3,2,1,0:T(8,128)(2,1)S(1)} %get-tuple-element.14.own_ref, bf16[16,1024,256]{2,1,0:T(8,128)(2,1)S(1)} %row_spectra.3.left_ref, bf16[4224,128]{1,0:T(8,128)(2,1)S(1)} %get-tuple-element.29.refs_0_), custom_call_target="tpu_custom_call" | custom-call | flops 2147483648 | bytes 16777216 | tf_op jit(solution)/shard_map/row_products/pallas_call | solution.py:464
  82.4 8.1 %all-to-all-start.1 = ((s16[16,264,256]{2,1,0:T(8,128)(2,1)}), s16[16,264,256]{2,1,0:T(8,128)(2,1)}, u32[]{:S(2)}, u32[]{:S(2)}) async-start(s16[16,264,256]{2,1,0:T(8,128)(2,1)} %get-tuple-element.18), calls=%async_computation.1 | async-start | bytes 4325376 | tf_op jit(solution)/shard_map/all_to_all | solution.py:568
  90.5 0.4 collective-permute-start.16
  90.9 2.4 %collective-permute-done.16 = bf16[4224,128]{1,0:T(8,128)(2,1)S(1)} collective-permute-done((bf16[4224,128]{1,0:T(8,128)(2,1)S(1)}, bf16[4224,128]{1,0:T(8,128)(2,1)S(1)}, u32[]{:S(2)}, u32[]{:S(2)}) %collective-permute-start.16) | collective-permute-done | bytes 1081376 | tf_op jit(solution)/shard_map/ppermute | solution.py:359
  93.4 4.7 %row_spectra.2.left_ref = bf16[16,1024,256]{2,1,0:T(8,128)(2,1)S(1)} custom-call(bf16[8448,128]{1,0:T(8,128)(2,1)S(1)} %constant_dynamic-update-slice_fusion.10.words_ref, bf16[64,128]{1,0:T(8,128)(2,1)S(1)} %slice.32.parts_ref, bf16[256,256]{1,0:T(8,128)(2,1)S(1)} %copy-done.5), custom_call_target="tpu_custom_call" | custom-call | flops 2147483648 | bytes 10551296 | tf_op jit(solution)/shard_map/row_spectra/pallas_call | solution.py:423
  98.2 4.3 %row_products.3 = (s16[16,264,256]{2,1,0:T(8,128)(2,1)}, bf16[16,128]{1,0:T(8,128)(2,1)}) custom-call(bf16[16,8,256,128]{3,2,1,0:T(8,128)(2,1)S(1)} %copy-done.2, bf16[16,1024,256]{2,1,0:T(8,128)(2,1)S(1)} %row_spectra.2.left_ref, bf16[16,128]{1,0:T(8,128)(2,1)S(1)} %get-tuple-element.16.refs_0_), custom_call_target="tpu_custom_call" | custom-call | flops 2147483648 | bytes 16777216 | tf_op jit(solution)/shard_map/row_products/pallas_call | solution.py:464
  102.5 36.9 %all-to-all-done.1.coded_ref = s16[16,264,256]{2,1,0:T(8,128)(2,1)} async-done(((s16[16,264,256]{2,1,0:T(8,128)(2,1)}), s16[16,264,256]{2,1,0:T(8,128)(2,1)}, u32[]{:S(2)}, u32[]{:S(2)}) %all-to-all-start.1) | async-done | bytes 2162720 | tf_op jit(solution)/shard_map/all_to_all | solution.py:568
  139.4 5.0 %all-to-all-start = ((s16[16,264,256]{2,1,0:T(8,128)(2,1)}), s16[16,264,256]{2,1,0:T(8,128)(2,1)S(1)}, u32[]{:S(2)}, u32[]{:S(2)}) async-start(s16[16,264,256]{2,1,0:T(8,128)(2,1)} %get-tuple-element.17), calls=%async_computation | async-start | bytes 4325376 | tf_op jit(solution)/shard_map/all_to_all | solution.py:568
  144.5 8.6 %finish.2.refs_0_ = f32[256,64,128]{2,1,0:T(8,128)} custom-call(s32[4096]{0:T(1024)S(1)} %broadcast_multiply_fusion.slot_ref, s16[16,264,256]{2,1,0:T(8,128)(2,1)} %all-to-all-done.1.coded_ref), custom_call_target="tpu_custom_call" | custom-call | tf_op jit(solution)/shard_map/finish/pallas_call | solution.py:522
  153.1 40.2 %all-to-all-done.coded_ref = s16[16,264,256]{2,1,0:T(8,128)(2,1)S(1)} async-done(((s16[16,264,256]{2,1,0:T(8,128)(2,1)}), s16[16,264,256]{2,1,0:T(8,128)(2,1)S(1)}, u32[]{:S(2)}, u32[]{:S(2)}) %all-to-all-start) | async-done | bytes 2162720 | tf_op jit(solution)/shard_map/all_to_all | solution.py:568
  193.3 7.7 %finish.3 = f32[256,64,128]{2,1,0:T(8,128)} custom-call(s32[4096]{0:T(1024)S(1)} %broadcast_multiply_fusion.slot_ref, s16[16,264,256]{2,1,0:T(8,128)(2,1)S(1)} %all-to-all-done.coded_ref, f32[256,64,128]{2,1,0:T(8,128)} %finish.2.refs_0_), custom_call_target="tpu_custom_call", output_to_operand_aliasing={{}: (2, {})} | custom-call | tf_op jit(solution)/shard_map/finish/pallas_call | solution.py:522
  (82 shorter events, 3.9 us)
Async XLA Ops:
  0.0 3.4 %copy-start = (s32[256,16,519]{0,1,2:T(8,128)S(1)}, s32[256,16,519]{0,1,2:T(8,128)}, u32[]{:S(2)}) copy-start(s32[256,16,519]{0,1,2:T(8,128)} %param.4) | copy-start | bytes 25509892
  5.5 2.0 copy-start.3
  5.5 2.4 %copy-start.6 = (s32[2,16,256]{2,1,0:T(8,128)S(1)}, s32[2,16,256]{2,1,0:T(8,128)}, u32[]{:S(2)}) copy-start(s32[2,16,256]{2,1,0:T(8,128)} %param.5) | copy-start | bytes 98308
  6.7 3.4 %collective-permute-start.5 = (bf16[4224,128]{1,0:T(8,128)(2,1)}, bf16[4224,128]{1,0:T(8,128)(2,1)}, u32[]{:S(2)}, u32[]{:S(2)}) collective-permute-start(bf16[4224,128]{1,0:T(8,128)(2,1)} %constant_dynamic-slice_fusion.4), channel_id=1, source_target_pairs={{0,1},{1,0},{2,3},{3,2},{4,5},{5,4},{6,7},{7,6},{8,9},{9,8},{10,11... | collective-permute-start | bytes 3244040 | tf_op jit(solution)/shard_map/ppermute | solution.py:359
  7.4 28.5 %slice-start = ((s8[8503296]{0:T(1024)(128)(4,1)}), s8[114688]{0:T(1024)(128)(4,1)S(1)}, s32[]{:S(2)}) async-start(s8[8503296]{0:T(1024)(128)(4,1)} %bitcast.14), calls=%async_computation.2 | async-start | bytes 229376
  7.5 4.8 %collective-permute-start = (bf16[4224,128]{1,0:T(8,128)(2,1)S(1)}, bf16[4224,128]{1,0:T(8,128)(2,1)}, u32[]{:S(2)}, u32[]{:S(2)}) collective-permute-start(bf16[4224,128]{1,0:T(8,128)(2,1)S(1)} %constant_dynamic-slice_fusion.9), channel_id=1, source_target_pairs={{0,1},{1,0},{2,3},{3,2},{4,5},{5,4},{6,7},{7,6},{8,9},{9,8},{10,11... | collective-permute-start | bytes 3244040 | tf_op jit(solution)/shard_map/ppermute | solution.py:359
  10.0 2.2 %copy-start.4 = (bf16[8448,128]{1,0:T(8,128)(2,1)S(1)}, bf16[8448,128]{1,0:T(8,128)(2,1)}, u32[]{:S(2)}) copy-start(bf16[8448,128]{1,0:T(8,128)(2,1)} %copy-done.3) | copy-start | bytes 6488068
  11.7 24.1 %slice-start.1 = ((s8[8503296]{0:T(1024)(128)(4,1)}), s8[4194304]{0:T(1024)(128)(4,1)S(1)}, s32[]{:S(2)}) async-start(s8[8503296]{0:T(1024)(128)(4,1)} %bitcast.14), calls=%async_computation.3 | async-start | bytes 8388608
  11.8 7.8 %collective-permute-start.8 = (bf16[1056,128]{1,0:T(8,128)(2,1)S(1)}, bf16[1056,128]{1,0:T(8,128)(2,1)S(1)}, u32[]{:S(2)}, u32[]{:S(2)}) collective-permute-start(bf16[1056,128]{1,0:T(8,128)(2,1)S(1)} %constant_dynamic-slice_fusion.1), channel_id=1, source_target_pairs={{0,4},{1,5},{2,6},{3,7},{4,0},{5,1},{6,2},{7,3},{8,12},{9,13},{10,... | collective-permute-start | bytes 811016 | tf_op jit(solution)/shard_map/ppermute | solution.py:359
  12.1 7.9 %collective-permute-start.6 = (bf16[1056,128]{1,0:T(8,128)(2,1)S(1)}, bf16[1056,128]{1,0:T(8,128)(2,1)S(1)}, u32[]{:S(2)}, u32[]{:S(2)}) collective-permute-start(bf16[1056,128]{1,0:T(8,128)(2,1)S(1)} %constant_dynamic-slice_fusion.3), channel_id=1, source_target_pairs={{0,2},{1,3},{2,0},{3,1},{4,6},{5,7},{6,4},{7,5},{8,10},{9,11},{10,... | collective-permute-start | bytes 811016 | tf_op jit(solution)/shard_map/ppermute | solution.py:359
  14.0 21.8 %slice-start.2 = ((s8[8503296]{0:T(1024)(128)(4,1)}), s8[4194304]{0:T(1024)(128)(4,1)S(1)}, s32[]{:S(2)}) async-start(s8[8503296]{0:T(1024)(128)(4,1)} %bitcast.14), calls=%async_computation.4 | async-start | bytes 8388608
  14.2 12.6 %collective-permute-start.3 = (bf16[1056,128]{1,0:T(8,128)(2,1)S(1)}, bf16[1056,128]{1,0:T(8,128)(2,1)S(1)}, u32[]{:S(2)}, u32[]{:S(2)}) collective-permute-start(bf16[1056,128]{1,0:T(8,128)(2,1)S(1)} %constant_dynamic-slice_fusion.6), channel_id=1, source_target_pairs={{0,4},{1,5},{2,6},{3,7},{4,0},{5,1},{6,2},{7,3},{8,12},{9,13},{10,... | collective-permute-start | bytes 811016 | tf_op jit(solution)/shard_map/ppermute | solution.py:359
  15.4 9.9 %collective-permute-start.1 = (bf16[1056,128]{1,0:T(8,128)(2,1)S(1)}, bf16[1056,128]{1,0:T(8,128)(2,1)S(1)}, u32[]{:S(2)}, u32[]{:S(2)}) collective-permute-start(bf16[1056,128]{1,0:T(8,128)(2,1)S(1)} %constant_dynamic-slice_fusion.8), channel_id=1, source_target_pairs={{0,2},{1,3},{2,0},{3,1},{4,6},{5,7},{6,4},{7,5},{8,10},{9,11},{10,... | collective-permute-start | bytes 811016 | tf_op jit(solution)/shard_map/ppermute | solution.py:359
  19.7 15.6 %collective-permute-start.9 = (bf16[528,128]{1,0:T(8,128)(2,1)S(1)}, bf16[528,128]{1,0:T(8,128)(2,1)S(1)}, u32[]{:S(2)}, u32[]{:S(2)}) collective-permute-start(bf16[528,128]{1,0:T(8,128)(2,1)S(1)} %constant_dynamic-slice_fusion), channel_id=1, source_target_pairs={{0,2},{1,3},{2,0},{3,1},{4,6},{5,7},{6,4},{7,5},{8,10},{9,11},{10,... | collective-permute-start | bytes 405512 | tf_op jit(solution)/shard_map/ppermute | solution.py:359
  20.1 15.8 %copy-start.5 = (bf16[256,256]{1,0:T(8,128)(2,1)S(1)}, bf16[256,256]{1,0:T(8,128)(2,1)}, u32[]{:S(2)}) copy-start(bf16[256,256]{1,0:T(8,128)(2,1)} %constant.217.clone.weights_ref) | copy-start | bytes 393220
  20.1 13.1 %collective-permute-start.7 = (bf16[528,128]{1,0:T(8,128)(2,1)S(1)}, bf16[528,128]{1,0:T(8,128)(2,1)S(1)}, u32[]{:S(2)}, u32[]{:S(2)}) collective-permute-start(bf16[528,128]{1,0:T(8,128)(2,1)S(1)} %constant_dynamic-slice_fusion.2), channel_id=1, source_target_pairs={{0,4},{1,5},{2,6},{3,7},{4,0},{5,1},{6,2},{7,3},{8,12},{9,13},{10,... | collective-permute-start | bytes 405512 | tf_op jit(solution)/shard_map/ppermute | solution.py:359
  25.4 4.8 %collective-permute-start.2 = (bf16[528,128]{1,0:T(8,128)(2,1)S(1)}, bf16[528,128]{1,0:T(8,128)(2,1)S(1)}, u32[]{:S(2)}, u32[]{:S(2)}) collective-permute-start(bf16[528,128]{1,0:T(8,128)(2,1)S(1)} %constant_dynamic-slice_fusion.7), channel_id=1, source_target_pairs={{0,4},{1,5},{2,6},{3,7},{4,0},{5,1},{6,2},{7,3},{8,12},{9,13},{10,... | collective-permute-start | bytes 405512 | tf_op jit(solution)/shard_map/ppermute | solution.py:359
  26.9 5.8 %collective-permute-start.4 = (bf16[528,128]{1,0:T(8,128)(2,1)S(1)}, bf16[528,128]{1,0:T(8,128)(2,1)S(1)}, u32[]{:S(2)}, u32[]{:S(2)}) collective-permute-start(bf16[528,128]{1,0:T(8,128)(2,1)S(1)} %constant_dynamic-slice_fusion.5), channel_id=1, source_target_pairs={{0,2},{1,3},{2,0},{3,1},{4,6},{5,7},{6,4},{7,5},{8,10},{9,11},{10,... | collective-permute-start | bytes 405512 | tf_op jit(solution)/shard_map/ppermute | solution.py:359
  30.3 16.8 %collective-permute-start.17 = (bf16[528,128]{1,0:T(8,128)(2,1)S(1)}, bf16[528,128]{1,0:T(8,128)(2,1)S(1)}, u32[]{:S(2)}, u32[]{:S(2)}) collective-permute-start(bf16[528,128]{1,0:T(8,128)(2,1)S(1)} %dynamic-slice_add_fusion.9.refs_0_), channel_id=1, source_target_pairs={{0,8},{1,9},{2,10},{3,11},{4,12},{5,13},{6,14},{7,15},{8,0},{9,1},... | collective-permute-start | bytes 405512 | tf_op jit(solution)/shard_map/ppermute | solution.py:359
  32.7 17.3 %collective-permute-start.20 = (bf16[528,128]{1,0:T(8,128)(2,1)S(1)}, bf16[528,128]{1,0:T(8,128)(2,1)S(1)}, u32[]{:S(2)}, u32[]{:S(2)}) collective-permute-start(bf16[528,128]{1,0:T(8,128)(2,1)S(1)} %dynamic-slice_add_fusion.8.refs_1_), channel_id=1, source_target_pairs={{0,8},{1,9},{2,10},{3,11},{4,12},{5,13},{6,14},{7,15},{8,0},{9,1},... | collective-permute-start | bytes 405512 | tf_op jit(solution)/shard_map/ppermute | solution.py:359
  33.3 19.6 %collective-permute-start.10 = (bf16[528,128]{1,0:T(8,128)(2,1)S(1)}, bf16[528,128]{1,0:T(8,128)(2,1)S(1)}, u32[]{:S(2)}, u32[]{:S(2)}) collective-permute-start(bf16[528,128]{1,0:T(8,128)(2,1)S(1)} %dynamic-slice_add_fusion.7.refs_2_), channel_id=1, source_target_pairs={{0,8},{1,9},{2,10},{3,11},{4,12},{5,13},{6,14},{7,15},{8,0},{9,1},... | collective-permute-start | bytes 405512 | tf_op jit(solution)/shard_map/ppermute | solution.py:359
  35.3 20.5 %collective-permute-start.13 = (bf16[528,128]{1,0:T(8,128)(2,1)S(1)}, bf16[528,128]{1,0:T(8,128)(2,1)S(1)}, u32[]{:S(2)}, u32[]{:S(2)}) collective-permute-start(bf16[528,128]{1,0:T(8,128)(2,1)S(1)} %dynamic-slice_add_fusion.6.refs_3_), channel_id=1, source_target_pairs={{0,8},{1,9},{2,10},{3,11},{4,12},{5,13},{6,14},{7,15},{8,0},{9,1},... | collective-permute-start | bytes 405512 | tf_op jit(solution)/shard_map/ppermute | solution.py:359
  44.9 33.1 %copy-start.1 = (bf16[16,8,256,128]{3,2,1,0:T(8,128)(2,1)}, bf16[16,8,256,128]{3,2,1,0:T(8,128)(2,1)S(1)}, u32[]{:S(2)}) copy-start(bf16[16,8,256,128]{3,2,1,0:T(8,128)(2,1)S(1)} %get-tuple-element.14.own_ref) | copy-start | bytes 25165828
  47.7 10.7 %collective-permute-start.18 = (bf16[528,128]{1,0:T(8,128)(2,1)S(1)}, bf16[528,128]{1,0:T(8,128)(2,1)S(1)}, u32[]{:S(2)}, u32[]{:S(2)}) collective-permute-start(bf16[528,128]{1,0:T(8,128)(2,1)S(1)} %get-tuple-element.20), channel_id=1, source_target_pairs={{0,4},{1,5},{2,6},{3,7},{4,0},{5,1},{6,2},{7,3},{8,12},{9,13},{10,... | collective-permute-start | bytes 405512 | tf_op jit(solution)/shard_map/ppermute | solution.py:359
  50.0 8.8 %collective-permute-start.21 = (bf16[528,128]{1,0:T(8,128)(2,1)S(1)}, bf16[528,128]{1,0:T(8,128)(2,1)S(1)}, u32[]{:S(2)}, u32[]{:S(2)}) collective-permute-start(bf16[528,128]{1,0:T(8,128)(2,1)S(1)} %get-tuple-element.22), channel_id=1, source_target_pairs={{0,2},{1,3},{2,0},{3,1},{4,6},{5,7},{6,4},{7,5},{8,10},{9,11},{10,... | collective-permute-start | bytes 405512 | tf_op jit(solution)/shard_map/ppermute | solution.py:359
  53.0 8.4 %collective-permute-start.11 = (bf16[528,128]{1,0:T(8,128)(2,1)S(1)}, bf16[528,128]{1,0:T(8,128)(2,1)S(1)}, u32[]{:S(2)}, u32[]{:S(2)}) collective-permute-start(bf16[528,128]{1,0:T(8,128)(2,1)S(1)} %get-tuple-element.24), channel_id=1, source_target_pairs={{0,4},{1,5},{2,6},{3,7},{4,0},{5,1},{6,2},{7,3},{8,12},{9,13},{10,... | collective-permute-start | bytes 405512 | tf_op jit(solution)/shard_map/ppermute | solution.py:359
  55.9 6.7 %collective-permute-start.14 = (bf16[528,128]{1,0:T(8,128)(2,1)S(1)}, bf16[528,128]{1,0:T(8,128)(2,1)S(1)}, u32[]{:S(2)}, u32[]{:S(2)}) collective-permute-start(bf16[528,128]{1,0:T(8,128)(2,1)S(1)} %get-tuple-element.26), channel_id=1, source_target_pairs={{0,2},{1,3},{2,0},{3,1},{4,6},{5,7},{6,4},{7,5},{8,10},{9,11},{10,... | collective-permute-start | bytes 405512 | tf_op jit(solution)/shard_map/ppermute | solution.py:359
  58.5 8.5 %collective-permute-start.19 = (bf16[1056,128]{1,0:T(8,128)(2,1)S(1)}, bf16[1056,128]{1,0:T(8,128)(2,1)S(1)}, u32[]{:S(2)}, u32[]{:S(2)}) collective-permute-start(bf16[1056,128]{1,0:T(8,128)(2,1)S(1)} %constant_dynamic-update-slice_fusion.8), channel_id=1, source_target_pairs={{0,2},{1,3},{2,0},{3,1},{4,6},{5,7},{6,4},{7,5},{8,10},{9,11},{10,... | collective-permute-start | bytes 811016 | tf_op jit(solution)/shard_map/ppermute | solution.py:359
  58.8 8.3 %collective-permute-start.22 = (bf16[1056,128]{1,0:T(8,128)(2,1)S(1)}, bf16[1056,128]{1,0:T(8,128)(2,1)S(1)}, u32[]{:S(2)}, u32[]{:S(2)}) collective-permute-start(bf16[1056,128]{1,0:T(8,128)(2,1)S(1)} %constant_dynamic-update-slice_fusion.4), channel_id=1, source_target_pairs={{0,4},{1,5},{2,6},{3,7},{4,0},{5,1},{6,2},{7,3},{8,12},{9,13},{10,... | collective-permute-start | bytes 811016 | tf_op jit(solution)/shard_map/ppermute | solution.py:359
  61.4 11.4 %collective-permute-start.12 = (bf16[1056,128]{1,0:T(8,128)(2,1)S(1)}, bf16[1056,128]{1,0:T(8,128)(2,1)S(1)}, u32[]{:S(2)}, u32[]{:S(2)}) collective-permute-start(bf16[1056,128]{1,0:T(8,128)(2,1)S(1)} %constant_dynamic-update-slice_fusion.18), channel_id=1, source_target_pairs={{0,2},{1,3},{2,0},{3,1},{4,6},{5,7},{6,4},{7,5},{8,10},{9,11},{10,... | collective-permute-start | bytes 811016 | tf_op jit(solution)/shard_map/ppermute | solution.py:359
  62.6 10.3 %collective-permute-start.15 = (bf16[1056,128]{1,0:T(8,128)(2,1)S(1)}, bf16[1056,128]{1,0:T(8,128)(2,1)S(1)}, u32[]{:S(2)}, u32[]{:S(2)}) collective-permute-start(bf16[1056,128]{1,0:T(8,128)(2,1)S(1)} %constant_dynamic-update-slice_fusion.14), channel_id=1, source_target_pairs={{0,4},{1,5},{2,6},{3,7},{4,0},{5,1},{6,2},{7,3},{8,12},{9,13},{10,... | collective-permute-start | bytes 811016 | tf_op jit(solution)/shard_map/ppermute | solution.py:359
  67.4 5.8 %collective-permute-start.23 = (bf16[4224,128]{1,0:T(8,128)(2,1)S(1)}, bf16[4224,128]{1,0:T(8,128)(2,1)S(1)}, u32[]{:S(2)}, u32[]{:S(2)}) collective-permute-start(bf16[4224,128]{1,0:T(8,128)(2,1)S(1)} %get-tuple-element.27), channel_id=1, source_target_pairs={{0,1},{1,0},{2,3},{3,2},{4,5},{5,4},{6,7},{7,6},{8,9},{9,8},{10,11... | collective-permute-start | bytes 3244040 | tf_op jit(solution)/shard_map/ppermute | solution.py:359
  82.4 57.1 %all-to-all-start.1 = ((s16[16,264,256]{2,1,0:T(8,128)(2,1)}), s16[16,264,256]{2,1,0:T(8,128)(2,1)}, u32[]{:S(2)}, u32[]{:S(2)}) async-start(s16[16,264,256]{2,1,0:T(8,128)(2,1)} %get-tuple-element.18), calls=%async_computation.1 | async-start | bytes 4325376 | tf_op jit(solution)/shard_map/all_to_all | solution.py:568
  90.5 2.7 %collective-permute-start.16 = (bf16[4224,128]{1,0:T(8,128)(2,1)S(1)}, bf16[4224,128]{1,0:T(8,128)(2,1)S(1)}, u32[]{:S(2)}, u32[]{:S(2)}) collective-permute-start(bf16[4224,128]{1,0:T(8,128)(2,1)S(1)} %get-tuple-element.29.refs_0_), channel_id=1, source_target_pairs={{0,1},{1,0},{2,3},{3,2},{4,5},{5,4},{6,7},{7,6},{8,9},{9,8},{10,11... | collective-permute-start | bytes 3244040 | tf_op jit(solution)/shard_map/ppermute | solution.py:359
  93.4 4.7 %copy-start.2 = (bf16[16,8,256,128]{3,2,1,0:T(8,128)(2,1)S(1)}, bf16[16,8,256,128]{3,2,1,0:T(8,128)(2,1)}, u32[]{:S(2)}) copy-start(bf16[16,8,256,128]{3,2,1,0:T(8,128)(2,1)} %copy-done.1) | copy-start | bytes 25165828
  139.4 5.0 %copy-start.7 = (s32[4096]{0:T(1024)S(1)}, s32[4096]{0:T(1024)}, u32[]{:S(2)}) copy-start(s32[4096]{0:T(1024)} %param.6) | copy-start | bytes 49156
  139.4 53.9 %all-to-all-start = ((s16[16,264,256]{2,1,0:T(8,128)(2,1)}), s16[16,264,256]{2,1,0:T(8,128)(2,1)S(1)}, u32[]{:S(2)}, u32[]{:S(2)}) async-start(s16[16,264,256]{2,1,0:T(8,128)(2,1)} %get-tuple-element.17), calls=%async_computation | async-start | bytes 4325376 | tf_op jit(solution)/shard_map/all_to_all | solution.py:568

commit v17 on v16

--- a/solution.py
+++ b/solution.py
@@ -201,6 +201,7 @@
 SPAN = 16
 STEPS = 8
 RANGE = 14
+FIT = 1.0 - 2.0**-15
 EXTRA = 8
 
 
@@ -310,27 +311,38 @@
     )(words, words, gains, weights, *after)
 
 
-def select_kernel(block, place_ref, slots_ref, words_ref, gains_ref, *outs):
+def select_kernel(blocks, place_ref, slots_ref, words_ref, gains_ref, *outs):
     lines, count = words_ref.shape
-    rows = len(outs) * LANES
+    pieces = len(outs) // 2
+    rows = pieces * LANES
+    size = outs[0].shape[0]
     place = lax.broadcasted_iota(jnp.int32, (count, rows), 0) + place_ref[0] * count
-    slots = jnp.concatenate([slots_ref[index : index + 1, :] for index in range(len(outs))], axis=1)
+    slots = jnp.concatenate([slots_ref[index : index + 1, :] for index in range(pieces)], axis=1)
     choice = jnp.where(slots == place, 1.0, 0.0).astype(jnp.bfloat16)
-
-    def put(first, values):
-        size = values.shape[0]
+    gains = gains_ref[...]
+    parts = jnp.concatenate([gains >> 4, gains & 15], axis=0)
+
+    def put(refs, first, values):
         values = values.astype(jnp.float32).astype(jnp.bfloat16)
         taken = jnp.dot(values, choice, preferred_element_type=jnp.float32).astype(outs[0].dtype)
-        for index, out_ref in enumerate(outs):
-            out_ref[first : first + size, :] = taken[:, index * LANES : (index + 1) * LANES]
-
-    for first in range(0, lines, block):
-        put(first, words_ref[first : min(first + block, lines), :])
-    gains = gains_ref[...]
-    put(lines, jnp.concatenate([gains >> 4, gains & 15], axis=0))
-    first = lines + 2 * gains.shape[0]
-    for out_ref in outs:
-        out_ref[first:, :] = jnp.zeros((out_ref.shape[0] - first, LANES), out_ref.dtype)
+        for index, out_ref in enumerate(refs):
+            out_ref[first : first + values.shape[0], :] = taken[:, index * LANES : (index + 1) * LANES]
+
+    for side in range(2):
+
+        @pl.when(place_ref[0] % 2 == side)
+        def _():
+            for half in range(2):
+                refs = outs[:pieces] if half == side else outs[pieces:]
+                end = min((half + 1) * size, lines)
+                for first in range(half * size, end, size // blocks):
+                    last = min(first + size // blocks, end)
+                    put(refs, first - half * size, words_ref[first:last, :])
+            first = lines - size
+            put(refs, first, parts)
+            first += parts.shape[0]
+            for out_ref in refs:
+                out_ref[first:, :] = jnp.zeros((size - first, LANES), out_ref.dtype)
 
 
 def at_hand(value):
@@ -338,8 +350,9 @@
 
 
 def select_rows(place, words, gains, slots, rows, total):
-    return pl.pallas_call(
-        functools.partial(select_kernel, total // STEPS),
+    pieces = rows // LANES
+    outs = pl.pallas_call(
+        functools.partial(select_kernel, STEPS // 2),
         grid=(1,),
         in_specs=[
             pl.BlockSpec(memory_space=pltpu.SMEM),
@@ -347,11 +360,12 @@
             pl.BlockSpec(memory_space=pltpu.VMEM),
             pl.BlockSpec(gains.shape, lambda i: (0, 0)),
         ],
-        out_specs=[pl.BlockSpec(memory_space=pltpu.VMEM)] * (rows // LANES),
-        out_shape=[jax.ShapeDtypeStruct((total, LANES), jnp.bfloat16)] * (rows // LANES),
+        out_specs=[pl.BlockSpec(memory_space=pltpu.VMEM)] * (2 * pieces),
+        out_shape=[jax.ShapeDtypeStruct((total // 2, LANES), jnp.bfloat16)] * (2 * pieces),
         compiler_params=pltpu.CompilerParams(vmem_limit_bytes=12 << 20),
         name="select_rows",
     )(place, at_hand(slots), words, at_hand(gains))
+    return outs[:pieces], outs[pieces:]
 
 
 def swap(value, bit):
@@ -375,6 +389,11 @@
     other = swap(value, bit)
     buffer = lax.dynamic_update_slice_in_dim(buffer, value, side(bit) * size, 0)
     return lax.dynamic_update_slice_in_dim(buffer, other, (1 - side(bit)) * size, 0)
+
+
+def both_halves(half):
+    other, first = swap(half, 1), side(1) == 0
+    return jnp.concatenate([jnp.where(first, half, other), jnp.where(first, other, half)], axis=0)
 
 
 def quarters(half):
@@ -451,7 +470,7 @@
         count = products.shape[0]
         largest = jnp.maximum(jnp.max(jnp.abs(products), axis=0, keepdims=True), 2.0**-60)
         power = jnp.floor(jnp.log2(largest))
-        coded = jnp.clip(jnp.round(products * jnp.exp2(RANGE - power)), -32767.0, 32767.0)
+        coded = jnp.round(products * (jnp.exp2(RANGE - power) * FIT))
         out_ref[index, :count, :] = coded.astype(jnp.int32).astype(jnp.int16)
         line = jnp.broadcast_to(power, (out_ref.shape[1] - count, power.shape[1]))
         out_ref[index, count:, :] = line.astype(jnp.int32).astype(jnp.int16)
@@ -493,7 +512,7 @@
     def _():
         for source in range(sources):
             power = coded_ref[source, count:, :][:1].astype(jnp.float32)
-            values = coded_ref[source, :count, :].astype(jnp.float32) * (jnp.exp2(power - RANGE) * scale)
+            values = coded_ref[source, :count, :].astype(jnp.float32) * (jnp.exp2(power - RANGE) * (scale / FIT))
             for piece in range(pieces):
                 products[pl.ds(source * count * pieces + piece, count, stride=pieces), :] = values[
                     :, piece * LANES : (piece + 1) * LANES
@@ -551,8 +570,8 @@
     scales = gains.reshape(2 * ch, count)
     weights = jnp.asarray(filter_weights(ch))
     place = lax.axis_index("feed").reshape(1)
-    picked = select_rows(place, words, scales, feed_slot.reshape(-1, LANES), ROWS, total)
-    halves, firsts = zip(*[quarters(reduce_half(value, 1)) for value in picked])
+    kept, sent = select_rows(place, words, scales, feed_slot.reshape(-1, LANES), ROWS, total)
+    halves, firsts = zip(*[quarters(keep + swap(send, 1)) for keep, send in zip(kept, sent)])
     seconds = [eighths(first) for first in firsts]
     own, zero = own_spectra(words, scales.astype(jnp.float32), weights, ch, spectra, sum(seconds, ()))
     thirds = [cross(second) for second in seconds]
@@ -560,7 +579,7 @@
     ends = [gathered(*parts) for parts in zip(halves, firsts, thirds)]
     out, after = None, [ends[-1]]
     for index in range(pieces):
-        rows = gather_half(ends[index], 1, picked[index])
+        rows = both_halves(ends[index])
         parts = rows[lines : lines + 4 * ch]
         left = row_spectra(rows, parts, weights, ch, spectra)
         coded, done = row_products(own, left, after)

time: 201 us -> 212 us (1.055)
  other arithmetic: 5.21 us -> 22.2 us
  waiting for transfers between devices: 109 us -> 102 us
    concatenate x0 -> x2, other arithmetic: none -> 15.1 us  [both_halves(): jnp.concatenate([jnp.where(first, half, other), jnp.where(first, other, h...]
    all_to_all x2, waiting for transfers between devices: 77.2 us -> 68.9 us  [through_rows(): lax.all_to_all(coded, 'feed', split_axis=0, concat_axis=0, tiled=True)]
    add x10 -> x8, other arithmetic: 3.91 us -> 0.46 us  [reduce_half(): return keep + swap(send, bit)]
    add x0 -> x2, other arithmetic: none -> 3.33 us  [through_rows(): keep + swap(send, 1)]
    select_n x0 -> x2, other arithmetic: none -> 2.21 us  [both_halves(): jnp.where(first, half, other)]
    unnamed x22 -> x24, local copies, waits for them, and re-layouts: 3.47 us -> 4.45 us
  transfers between devices with their start and end apart: 26 -> 26, of which waited for: 17 -> 17; matrix products, arithmetic and copies ran while one was open for 3% -> 7% of each run, Pallas kernels for 13% -> 12%
where the time goes in v17:
time: 212 us
  waiting for transfers between devices  102 us (48%)
  Pallas kernels  46.3 us (22%)
  starting transfers between devices  34.4 us (16%)
  other arithmetic  22.2 us (10%)
  local copies, waits for them, and re-layouts  5.79 us (3%)
    all_to_all x2, waiting for transfers between devices, through_rows(): lax.all_to_all(coded, 'feed', split_axis=0, concat_axis=0, tiled=True)  68.9 us
    ppermute x24, waiting for transfers between devices, swap(): return lax.ppermute(value, 'feed', pairs)  33.6 us
    ppermute x24, starting transfers between devices, swap(): return lax.ppermute(value, 'feed', pairs)  21.5 us
    pallas_call x2, Pallas kernels, finish(): pl.pallas_call(functools.partial(finish_kernel, scale), grid=(columns //...  16.3 us
    concatenate x2, other arithmetic, both_halves(): jnp.concatenate([jnp.where(first, half, other), jnp.where(first, other, h...  15.1 us
    all_to_all x2, starting transfers between devices, through_rows(): lax.all_to_all(coded, 'feed', split_axis=0, concat_axis=0, tiled=True)  12.9 us
    pallas_call x2, Pallas kernels, row_spectra(): pl.pallas_call(rows_kernel, grid=(1,), in_specs=[pl.BlockSpec(memory_spac...  9.42 us
    pallas_call x1, Pallas kernels, own_spectra(): pl.pallas_call(own_kernel, grid=(steps,), in_specs=[pl.BlockSpec((main, c...  8.99 us
  transfers between devices with their start and end apart: 26, of which 17 were waited for; matrix products, arithmetic and copies ran while one was open for 7% of the time, Pallas kernels for 12%

profile of v17, /device:TPU:13, one launch (start us, length us, event | category | flops | bytes accessed | tf_op | source)
XLA Modules:
  0.0 211.6 jit_solution(1083994449209210665)
XLA Ops:
  0.0 3.4 %copy-done = s32[256,16,519]{0,1,2:T(8,128)S(1)} copy-done((s32[256,16,519]{0,1,2:T(8,128)S(1)}, s32[256,16,519]{0,1,2:T(8,128)}, u32[]{:S(2)}) %copy-start) | copy-done | bytes 8503320
  3.4 3.3 %select_rows.1 = (bf16[4224,128]{1,0:T(8,128)(2,1)S(1)}, bf16[4224,128]{1,0:T(8,128)(2,1)S(1)}, bf16[4224,128]{1,0:T(8,128)(2,1)S(1)}, bf16[4224,128]{1,0:T(8,128)(2,1)}) custom-call(s32[1]{0:T(128)} %bitcast.3.place_ref, s32[32,128]{1,0:T(8,128)} %bitcast.21, s32[8304,256]{1,0:T(8,128)S(1)} %bitcast.13, s32[32,256]{1,0:T(8,128)} %bitcast.20), custom_call_target="tpu_custom_call" | custom-call | tf_op jit(solution)/shard_map/select_rows/pallas_call | solution.py:354
  6.7 0.7 collective-permute-start.5
  7.4 4.2 %collective-permute-done.5 = bf16[4224,128]{1,0:T(8,128)(2,1)} collective-permute-done((bf16[4224,128]{1,0:T(8,128)(2,1)}, bf16[4224,128]{1,0:T(8,128)(2,1)}, u32[]{:S(2)}, u32[]{:S(2)}) %collective-permute-start.5) | collective-permute-done | bytes 1081376 | tf_op jit(solution)/shard_map/ppermute | solution.py:373
  11.6 1.7 add.155
  13.8 1.7 add.140
  15.6 1.5 collective-permute-start.3
  17.1 1.3 collective-permute-start.1
  18.4 2.7 %collective-permute-done.8 = bf16[1056,128]{1,0:T(8,128)(2,1)S(1)} collective-permute-done((bf16[1056,128]{1,0:T(8,128)(2,1)S(1)}, bf16[1056,128]{1,0:T(8,128)(2,1)S(1)}, u32[]{:S(2)}, u32[]{:S(2)}) %collective-permute-start.8) | collective-permute-done | bytes 270368 | tf_op jit(solution)/shard_map/ppermute | solution.py:373
  21.6 0.9 collective-permute-start.7
  22.5 4.3 %collective-permute-done.1 = bf16[1056,128]{1,0:T(8,128)(2,1)S(1)} collective-permute-done((bf16[1056,128]{1,0:T(8,128)(2,1)S(1)}, bf16[1056,128]{1,0:T(8,128)(2,1)S(1)}, u32[]{:S(2)}, u32[]{:S(2)}) %collective-permute-start.1) | collective-permute-done | bytes 270368 | tf_op jit(solution)/shard_map/ppermute | solution.py:373
  27.0 1.4 collective-permute-start.2
  28.7 3.0 %collective-permute-done.2 = bf16[528,128]{1,0:T(8,128)(2,1)S(1)} collective-permute-done((bf16[528,128]{1,0:T(8,128)(2,1)S(1)}, bf16[528,128]{1,0:T(8,128)(2,1)S(1)}, u32[]{:S(2)}, u32[]{:S(2)}) %collective-permute-start.2) | collective-permute-done | bytes 135200 | tf_op jit(solution)/shard_map/ppermute | solution.py:373
  31.8 2.4 %collective-permute-start.17 = (bf16[528,128]{1,0:T(8,128)(2,1)S(1)}, bf16[528,128]{1,0:T(8,128)(2,1)S(1)}, u32[]{:S(2)}, u32[]{:S(2)}) collective-permute-start(bf16[528,128]{1,0:T(8,128)(2,1)S(1)} %dynamic-slice_add_fusion.7.refs_0_), channel_id=1, source_target_pairs={{0,8},{1,9},{2,10},{3,11},{4,12},{5,13},{6,14},{7,15},{8,0},{9,1},... | collective-permute-start | bytes 405512 | tf_op jit(solution)/shard_map/ppermute | solution.py:373
  34.3 0.5 collective-permute-start.20
  34.9 1.9 collective-permute-start.10
  36.8 0.5 collective-permute-start.13
  37.4 9.0 %own_spectra.1 = (bf16[16,8,256,128]{3,2,1,0:T(8,128)(2,1)S(1)}, bf16[16,128]{1,0:T(8,128)(2,1)S(1)}) custom-call(s32[8304,256]{1,0:T(8,128)S(1)} %bitcast.16, s32[8304,256]{1,0:T(8,128)S(1)} %bitcast.17, f32[32,256]{1,0:T(8,128)S(1)} %bitcast_convert_fusion.gains_ref, bf16[256,256]{1,0:T(8,128)(2,1)S(1)} %copy-done.2, ...), custom_call_target="tpu_custom_call" | custom-call | flops 4294967296 | bytes 16891904 | tf_op jit(solution)/shard_map/own_spectra/pallas_call | solution.py:283
  46.4 0.6 slice.26
  47.1 1.5 collective-permute-done.17
  48.6 0.8 constant_dynamic-update-slice_fusion.7
  49.4 2.1 collective-permute-done.20
  51.9 2.6 %collective-permute-done.10 = bf16[528,128]{1,0:T(8,128)(2,1)S(1)} collective-permute-done((bf16[528,128]{1,0:T(8,128)(2,1)S(1)}, bf16[528,128]{1,0:T(8,128)(2,1)S(1)}, u32[]{:S(2)}, u32[]{:S(2)}) %collective-permute-start.10) | collective-permute-done | bytes 135200 | tf_op jit(solution)/shard_map/ppermute | solution.py:373
  54.5 0.6 collective-permute-start.11
  55.1 2.2 %collective-permute-done.13 = bf16[528,128]{1,0:T(8,128)(2,1)S(1)} collective-permute-done((bf16[528,128]{1,0:T(8,128)(2,1)S(1)}, bf16[528,128]{1,0:T(8,128)(2,1)S(1)}, u32[]{:S(2)}, u32[]{:S(2)}) %collective-permute-start.13) | collective-permute-done | bytes 135200 | tf_op jit(solution)/shard_map/ppermute | solution.py:373
  57.7 2.3 %collective-permute-done.18 = bf16[528,128]{1,0:T(8,128)(2,1)S(1)} collective-permute-done((bf16[528,128]{1,0:T(8,128)(2,1)S(1)}, bf16[528,128]{1,0:T(8,128)(2,1)S(1)}, u32[]{:S(2)}, u32[]{:S(2)}) %collective-permute-start.18) | collective-permute-done | bytes 135200 | tf_op jit(solution)/shard_map/ppermute | solution.py:373
  60.4 2.3 %collective-permute-start.22 = (bf16[1056,128]{1,0:T(8,128)(2,1)S(1)}, bf16[1056,128]{1,0:T(8,128)(2,1)S(1)}, u32[]{:S(2)}, u32[]{:S(2)}) collective-permute-start(bf16[1056,128]{1,0:T(8,128)(2,1)S(1)} %constant_dynamic-update-slice_fusion.2), channel_id=1, source_target_pairs={{0,4},{1,5},{2,6},{3,7},{4,0},{5,1},{6,2},{7,3},{8,12},{9,13},{10,... | collective-permute-start | bytes 811016 | tf_op jit(solution)/shard_map/ppermute | solution.py:373
  62.9 1.1 collective-permute-start.12
  64.1 1.4 collective-permute-start.15
  65.5 3.0 %collective-permute-done.19 = bf16[1056,128]{1,0:T(8,128)(2,1)S(1)} collective-permute-done((bf16[1056,128]{1,0:T(8,128)(2,1)S(1)}, bf16[1056,128]{1,0:T(8,128)(2,1)S(1)}, u32[]{:S(2)}, u32[]{:S(2)}) %collective-permute-start.19) | collective-permute-done | bytes 270368 | tf_op jit(solution)/shard_map/ppermute | solution.py:373
  68.7 2.6 %collective-permute-start.23 = (bf16[4224,128]{1,0:T(8,128)(2,1)S(1)}, bf16[4224,128]{1,0:T(8,128)(2,1)S(1)}, u32[]{:S(2)}, u32[]{:S(2)}) collective-permute-start(bf16[4224,128]{1,0:T(8,128)(2,1)S(1)} %pad_maximum_fusion.3), channel_id=1, source_target_pairs={{0,1},{1,0},{2,3},{3,2},{4,5},{5,4},{6,7},{7,6},{8,9},{9,8},{10,11... | collective-permute-start | bytes 3244040 | tf_op jit(solution)/shard_map/ppermute | solution.py:373
  71.4 3.0 %collective-permute-done.12 = bf16[1056,128]{1,0:T(8,128)(2,1)S(1)} collective-permute-done((bf16[1056,128]{1,0:T(8,128)(2,1)S(1)}, bf16[1056,128]{1,0:T(8,128)(2,1)S(1)}, u32[]{:S(2)}, u32[]{:S(2)}) %collective-permute-start.12) | collective-permute-done | bytes 270368 | tf_op jit(solution)/shard_map/ppermute | solution.py:373
  74.5 0.7 copy-done.4
  75.3 0.4 broadcast_select_fusion.1
  76.0 7.5 %pad_maximum_fusion.1.words_ref = bf16[8448,128]{1,0:T(8,128)(2,1)S(1)} fusion(bf16[4224,128]{1,0:T(8,128)(2,1)S(1)} %get-tuple-element.32, bf16[4224,128]{1,0:T(8,128)(2,1)S(1)} %get-tuple-element.31), kind=kLoop, calls=%fused_computation.1 | loop fusion | flops 4325376 | bytes 4325376 | tf_op jit(solution)/shard_map/concatenate | solution.py:396
  83.5 4.7 %row_spectra.3.left_ref = bf16[16,1024,256]{2,1,0:T(8,128)(2,1)S(1)} custom-call(bf16[8448,128]{1,0:T(8,128)(2,1)S(1)} %pad_maximum_fusion.1.words_ref, bf16[64,128]{1,0:T(8,128)(2,1)S(1)} %slice.33.parts_ref, bf16[256,256]{1,0:T(8,128)(2,1)S(1)} %copy-done.2), custom_call_target="tpu_custom_call" | custom-call | flops 2147483648 | bytes 10551296 | tf_op jit(solution)/shard_map/row_spectra/pallas_call | solution.py:442
  88.3 4.1 %row_products.2 = (s16[16,264,256]{2,1,0:T(8,128)(2,1)}, bf16[16,128]{1,0:T(8,128)(2,1)S(1)}) custom-call(bf16[16,8,256,128]{3,2,1,0:T(8,128)(2,1)S(1)} %get-tuple-element.18.own_ref, bf16[16,1024,256]{2,1,0:T(8,128)(2,1)S(1)} %row_spectra.3.left_ref, bf16[4224,128]{1,0:T(8,128)(2,1)S(1)} %pad_maximum_fusion.2.refs_0_), custom_call_target="tpu_custom_call" | custom-call | flops 2147483648 | bytes 16777216 | tf_op jit(solution)/shard_map/row_products/pallas_call | solution.py:483
  92.4 7.8 %all-to-all-start.1 = ((s16[16,264,256]{2,1,0:T(8,128)(2,1)}), s16[16,264,256]{2,1,0:T(8,128)(2,1)S(1)}, u32[]{:S(2)}, u32[]{:S(2)}) async-start(s16[16,264,256]{2,1,0:T(8,128)(2,1)} %get-tuple-element.22), calls=%async_computation.1 | async-start | bytes 4325376 | tf_op jit(solution)/shard_map/all_to_all | solution.py:587
  100.7 2.3 %collective-permute-done.16 = bf16[4224,128]{1,0:T(8,128)(2,1)S(1)} collective-permute-done((bf16[4224,128]{1,0:T(8,128)(2,1)S(1)}, bf16[4224,128]{1,0:T(8,128)(2,1)S(1)}, u32[]{:S(2)}, u32[]{:S(2)}) %collective-permute-start.16) | collective-permute-done | bytes 1081376 | tf_op jit(solution)/shard_map/ppermute | solution.py:373
  103.0 1.8 broadcast_select_fusion.3
  104.8 7.6 %pad_maximum_fusion.words_ref = bf16[8448,128]{1,0:T(8,128)(2,1)S(1)} fusion(bf16[4224,128]{1,0:T(8,128)(2,1)S(1)} %get-tuple-element.34, bf16[4224,128]{1,0:T(8,128)(2,1)S(1)} %get-tuple-element.33), kind=kLoop, calls=%fused_computation | loop fusion | flops 4325376 | bytes 4325376 | tf_op jit(solution)/shard_map/concatenate | solution.py:396
  112.4 4.7 %row_spectra.2.left_ref = bf16[16,1024,256]{2,1,0:T(8,128)(2,1)S(1)} custom-call(bf16[8448,128]{1,0:T(8,128)(2,1)S(1)} %pad_maximum_fusion.words_ref, bf16[64,128]{1,0:T(8,128)(2,1)S(1)} %slice.32.parts_ref, bf16[256,256]{1,0:T(8,128)(2,1)S(1)} %copy-done.2), custom_call_target="tpu_custom_call" | custom-call | flops 2147483648 | bytes 10551296 | tf_op jit(solution)/shard_map/row_spectra/pallas_call | solution.py:442
  117.2 4.2 %row_products.3 = (s16[16,264,256]{2,1,0:T(8,128)(2,1)}, bf16[16,128]{1,0:T(8,128)(2,1)}) custom-call(bf16[16,8,256,128]{3,2,1,0:T(8,128)(2,1)S(1)} %bitcast.19, bf16[16,1024,256]{2,1,0:T(8,128)(2,1)S(1)} %row_spectra.2.left_ref, bf16[16,128]{1,0:T(8,128)(2,1)S(1)} %get-tuple-element.20.refs_0_), custom_call_target="tpu_custom_call" | custom-call | flops 2147483648 | bytes 16777216 | tf_op jit(solution)/shard_map/row_products/pallas_call | solution.py:483
  121.3 27.7 %all-to-all-done.1.coded_ref = s16[16,264,256]{2,1,0:T(8,128)(2,1)S(1)} async-done(((s16[16,264,256]{2,1,0:T(8,128)(2,1)}), s16[16,264,256]{2,1,0:T(8,128)(2,1)S(1)}, u32[]{:S(2)}, u32[]{:S(2)}) %all-to-all-start.1) | async-done | bytes 2162720 | tf_op jit(solution)/shard_map/all_to_all | solution.py:587
  149.1 5.0 %all-to-all-start = ((s16[16,264,256]{2,1,0:T(8,128)(2,1)}), s16[16,264,256]{2,1,0:T(8,128)(2,1)}, u32[]{:S(2)}, u32[]{:S(2)}) async-start(s16[16,264,256]{2,1,0:T(8,128)(2,1)} %get-tuple-element.21), calls=%async_computation | async-start | bytes 4325376 | tf_op jit(solution)/shard_map/all_to_all | solution.py:587
  154.1 7.7 %finish.2.refs_0_ = f32[256,64,128]{2,1,0:T(8,128)} custom-call(s32[4096]{0:T(1024)S(1)} %broadcast_multiply_fusion.slot_ref, s16[16,264,256]{2,1,0:T(8,128)(2,1)S(1)} %all-to-all-done.1.coded_ref), custom_call_target="tpu_custom_call" | custom-call | tf_op jit(solution)/shard_map/finish/pallas_call | solution.py:541
  161.9 41.2 %all-to-all-done.coded_ref = s16[16,264,256]{2,1,0:T(8,128)(2,1)} async-done(((s16[16,264,256]{2,1,0:T(8,128)(2,1)}), s16[16,264,256]{2,1,0:T(8,128)(2,1)}, u32[]{:S(2)}, u32[]{:S(2)}) %all-to-all-start) | async-done | bytes 2162720 | tf_op jit(solution)/shard_map/all_to_all | solution.py:587
  203.0 8.5 %finish.3 = f32[256,64,128]{2,1,0:T(8,128)} custom-call(s32[4096]{0:T(1024)S(1)} %broadcast_multiply_fusion.slot_ref, s16[16,264,256]{2,1,0:T(8,128)(2,1)} %all-to-all-done.coded_ref, f32[256,64,128]{2,1,0:T(8,128)} %finish.2.refs_0_), custom_call_target="tpu_custom_call", output_to_operand_aliasing={{}: (2, {})} | custom-call | tf_op jit(solution)/shard_map/finish/pallas_call | solution.py:541
  (85 shorter events, 4.5 us)
Async XLA Ops:
  0.0 3.4 %copy-start = (s32[256,16,519]{0,1,2:T(8,128)S(1)}, s32[256,16,519]{0,1,2:T(8,128)}, u32[]{:S(2)}) copy-start(s32[256,16,519]{0,1,2:T(8,128)} %param.4) | copy-start | bytes 25509892
  3.4 4.0 %copy-start.5 = (s32[2,16,256]{2,1,0:T(8,128)S(1)}, s32[2,16,256]{2,1,0:T(8,128)}, u32[]{:S(2)}) copy-start(s32[2,16,256]{2,1,0:T(8,128)} %param.5) | copy-start | bytes 98308
  3.4 34.0 %slice-start = ((s8[8503296]{0:T(1024)(128)(4,1)}), s8[114688]{0:T(1024)(128)(4,1)S(1)}, s32[]{:S(2)}) async-start(s8[8503296]{0:T(1024)(128)(4,1)} %bitcast.14), calls=%async_computation.2 | async-start | bytes 229376
  6.7 4.9 %collective-permute-start.5 = (bf16[4224,128]{1,0:T(8,128)(2,1)}, bf16[4224,128]{1,0:T(8,128)(2,1)}, u32[]{:S(2)}, u32[]{:S(2)}) collective-permute-start(bf16[4224,128]{1,0:T(8,128)(2,1)} %get-tuple-element.17), channel_id=1, source_target_pairs={{0,1},{1,0},{2,3},{3,2},{4,5},{5,4},{6,7},{7,6},{8,9},{9,8},{10,11... | collective-permute-start | bytes 3244040 | tf_op jit(solution)/shard_map/ppermute | solution.py:373
  7.4 6.4 %collective-permute-start = (bf16[4224,128]{1,0:T(8,128)(2,1)S(1)}, bf16[4224,128]{1,0:T(8,128)(2,1)}, u32[]{:S(2)}, u32[]{:S(2)}) collective-permute-start(bf16[4224,128]{1,0:T(8,128)(2,1)S(1)} %get-tuple-element.15), channel_id=1, source_target_pairs={{0,1},{1,0},{2,3},{3,2},{4,5},{5,4},{6,7},{7,6},{8,9},{9,8},{10,11... | collective-permute-start | bytes 3244040 | tf_op jit(solution)/shard_map/ppermute | solution.py:373
  11.6 25.8 %slice-start.1 = ((s8[8503296]{0:T(1024)(128)(4,1)}), s8[4194304]{0:T(1024)(128)(4,1)S(1)}, s32[]{:S(2)}) async-start(s8[8503296]{0:T(1024)(128)(4,1)} %bitcast.14), calls=%async_computation.3 | async-start | bytes 8388608
  13.4 7.8 %collective-permute-start.8 = (bf16[1056,128]{1,0:T(8,128)(2,1)S(1)}, bf16[1056,128]{1,0:T(8,128)(2,1)S(1)}, u32[]{:S(2)}, u32[]{:S(2)}) collective-permute-start(bf16[1056,128]{1,0:T(8,128)(2,1)S(1)} %constant_dynamic-slice_fusion.1), channel_id=1, source_target_pairs={{0,4},{1,5},{2,6},{3,7},{4,0},{5,1},{6,2},{7,3},{8,12},{9,13},{10,... | collective-permute-start | bytes 811016 | tf_op jit(solution)/shard_map/ppermute | solution.py:373
  13.6 7.9 %collective-permute-start.6 = (bf16[1056,128]{1,0:T(8,128)(2,1)S(1)}, bf16[1056,128]{1,0:T(8,128)(2,1)S(1)}, u32[]{:S(2)}, u32[]{:S(2)}) collective-permute-start(bf16[1056,128]{1,0:T(8,128)(2,1)S(1)} %constant_dynamic-slice_fusion.3), channel_id=1, source_target_pairs={{0,2},{1,3},{2,0},{3,1},{4,6},{5,7},{6,4},{7,5},{8,10},{9,11},{10,... | collective-permute-start | bytes 811016 | tf_op jit(solution)/shard_map/ppermute | solution.py:373
  13.8 23.6 %slice-start.2 = ((s8[8503296]{0:T(1024)(128)(4,1)}), s8[4194304]{0:T(1024)(128)(4,1)S(1)}, s32[]{:S(2)}) async-start(s8[8503296]{0:T(1024)(128)(4,1)} %bitcast.14), calls=%async_computation.4 | async-start | bytes 8388608
  15.6 12.8 %collective-permute-start.3 = (bf16[1056,128]{1,0:T(8,128)(2,1)S(1)}, bf16[1056,128]{1,0:T(8,128)(2,1)S(1)}, u32[]{:S(2)}, u32[]{:S(2)}) collective-permute-start(bf16[1056,128]{1,0:T(8,128)(2,1)S(1)} %constant_dynamic-slice_fusion.5), channel_id=1, source_target_pairs={{0,4},{1,5},{2,6},{3,7},{4,0},{5,1},{6,2},{7,3},{8,12},{9,13},{10,... | collective-permute-start | bytes 811016 | tf_op jit(solution)/shard_map/ppermute | solution.py:373
  17.1 9.8 %collective-permute-start.1 = (bf16[1056,128]{1,0:T(8,128)(2,1)S(1)}, bf16[1056,128]{1,0:T(8,128)(2,1)S(1)}, u32[]{:S(2)}, u32[]{:S(2)}) collective-permute-start(bf16[1056,128]{1,0:T(8,128)(2,1)S(1)} %constant_dynamic-slice_fusion.7), channel_id=1, source_target_pairs={{0,2},{1,3},{2,0},{3,1},{4,6},{5,7},{6,4},{7,5},{8,10},{9,11},{10,... | collective-permute-start | bytes 811016 | tf_op jit(solution)/shard_map/ppermute | solution.py:373
  21.2 15.6 %collective-permute-start.9 = (bf16[528,128]{1,0:T(8,128)(2,1)S(1)}, bf16[528,128]{1,0:T(8,128)(2,1)S(1)}, u32[]{:S(2)}, u32[]{:S(2)}) collective-permute-start(bf16[528,128]{1,0:T(8,128)(2,1)S(1)} %constant_dynamic-slice_fusion), channel_id=1, source_target_pairs={{0,2},{1,3},{2,0},{3,1},{4,6},{5,7},{6,4},{7,5},{8,10},{9,11},{10,... | collective-permute-start | bytes 405512 | tf_op jit(solution)/shard_map/ppermute | solution.py:373
  21.6 13.2 %collective-permute-start.7 = (bf16[528,128]{1,0:T(8,128)(2,1)S(1)}, bf16[528,128]{1,0:T(8,128)(2,1)S(1)}, u32[]{:S(2)}, u32[]{:S(2)}) collective-permute-start(bf16[528,128]{1,0:T(8,128)(2,1)S(1)} %constant_dynamic-slice_fusion.2), channel_id=1, source_target_pairs={{0,4},{1,5},{2,6},{3,7},{4,0},{5,1},{6,2},{7,3},{8,12},{9,13},{10,... | collective-permute-start | bytes 405512 | tf_op jit(solution)/shard_map/ppermute | solution.py:373
  27.0 4.8 %collective-permute-start.2 = (bf16[528,128]{1,0:T(8,128)(2,1)S(1)}, bf16[528,128]{1,0:T(8,128)(2,1)S(1)}, u32[]{:S(2)}, u32[]{:S(2)}) collective-permute-start(bf16[528,128]{1,0:T(8,128)(2,1)S(1)} %constant_dynamic-slice_fusion.6), channel_id=1, source_target_pairs={{0,4},{1,5},{2,6},{3,7},{4,0},{5,1},{6,2},{7,3},{8,12},{9,13},{10,... | collective-permute-start | bytes 405512 | tf_op jit(solution)/shard_map/ppermute | solution.py:373
  28.4 9.0 %copy-start.2 = (bf16[256,256]{1,0:T(8,128)(2,1)S(1)}, bf16[256,256]{1,0:T(8,128)(2,1)}, u32[]{:S(2)}) copy-start(bf16[256,256]{1,0:T(8,128)(2,1)} %constant.189.clone.weights_ref) | copy-start | bytes 393220
  28.5 5.8 %collective-permute-start.4 = (bf16[528,128]{1,0:T(8,128)(2,1)S(1)}, bf16[528,128]{1,0:T(8,128)(2,1)S(1)}, u32[]{:S(2)}, u32[]{:S(2)}) collective-permute-start(bf16[528,128]{1,0:T(8,128)(2,1)S(1)} %constant_dynamic-slice_fusion.4), channel_id=1, source_target_pairs={{0,2},{1,3},{2,0},{3,1},{4,6},{5,7},{6,4},{7,5},{8,10},{9,11},{10,... | collective-permute-start | bytes 405512 | tf_op jit(solution)/shard_map/ppermute | solution.py:373
  31.8 16.8 %collective-permute-start.17 = (bf16[528,128]{1,0:T(8,128)(2,1)S(1)}, bf16[528,128]{1,0:T(8,128)(2,1)S(1)}, u32[]{:S(2)}, u32[]{:S(2)}) collective-permute-start(bf16[528,128]{1,0:T(8,128)(2,1)S(1)} %dynamic-slice_add_fusion.7.refs_0_), channel_id=1, source_target_pairs={{0,8},{1,9},{2,10},{3,11},{4,12},{5,13},{6,14},{7,15},{8,0},{9,1},... | collective-permute-start | bytes 405512 | tf_op jit(solution)/shard_map/ppermute | solution.py:373
  34.3 17.3 %collective-permute-start.20 = (bf16[528,128]{1,0:T(8,128)(2,1)S(1)}, bf16[528,128]{1,0:T(8,128)(2,1)S(1)}, u32[]{:S(2)}, u32[]{:S(2)}) collective-permute-start(bf16[528,128]{1,0:T(8,128)(2,1)S(1)} %dynamic-slice_add_fusion.6.refs_1_), channel_id=1, source_target_pairs={{0,8},{1,9},{2,10},{3,11},{4,12},{5,13},{6,14},{7,15},{8,0},{9,1},... | collective-permute-start | bytes 405512 | tf_op jit(solution)/shard_map/ppermute | solution.py:373
  34.9 19.6 %collective-permute-start.10 = (bf16[528,128]{1,0:T(8,128)(2,1)S(1)}, bf16[528,128]{1,0:T(8,128)(2,1)S(1)}, u32[]{:S(2)}, u32[]{:S(2)}) collective-permute-start(bf16[528,128]{1,0:T(8,128)(2,1)S(1)} %dynamic-slice_add_fusion.5.refs_2_), channel_id=1, source_target_pairs={{0,8},{1,9},{2,10},{3,11},{4,12},{5,13},{6,14},{7,15},{8,0},{9,1},... | collective-permute-start | bytes 405512 | tf_op jit(solution)/shard_map/ppermute | solution.py:373
  36.8 20.5 %collective-permute-start.13 = (bf16[528,128]{1,0:T(8,128)(2,1)S(1)}, bf16[528,128]{1,0:T(8,128)(2,1)S(1)}, u32[]{:S(2)}, u32[]{:S(2)}) collective-permute-start(bf16[528,128]{1,0:T(8,128)(2,1)S(1)} %dynamic-slice_add_fusion.4.refs_3_), channel_id=1, source_target_pairs={{0,8},{1,9},{2,10},{3,11},{4,12},{5,13},{6,14},{7,15},{8,0},{9,1},... | collective-permute-start | bytes 405512 | tf_op jit(solution)/shard_map/ppermute | solution.py:373
  46.4 41.8 %copy-start.1 = (bf16[16,8,256,128]{3,2,1,0:T(8,128)(2,1)}, bf16[16,8,256,128]{3,2,1,0:T(8,128)(2,1)S(1)}, u32[]{:S(2)}) copy-start(bf16[16,8,256,128]{3,2,1,0:T(8,128)(2,1)S(1)} %get-tuple-element.18.own_ref) | copy-start | bytes 25165828
  49.4 10.6 %collective-permute-start.18 = (bf16[528,128]{1,0:T(8,128)(2,1)S(1)}, bf16[528,128]{1,0:T(8,128)(2,1)S(1)}, u32[]{:S(2)}, u32[]{:S(2)}) collective-permute-start(bf16[528,128]{1,0:T(8,128)(2,1)S(1)} %get-tuple-element.24), channel_id=1, source_target_pairs={{0,4},{1,5},{2,6},{3,7},{4,0},{5,1},{6,2},{7,3},{8,12},{9,13},{10,... | collective-permute-start | bytes 405512 | tf_op jit(solution)/shard_map/ppermute | solution.py:373
  51.6 8.8 %collective-permute-start.21 = (bf16[528,128]{1,0:T(8,128)(2,1)S(1)}, bf16[528,128]{1,0:T(8,128)(2,1)S(1)}, u32[]{:S(2)}, u32[]{:S(2)}) collective-permute-start(bf16[528,128]{1,0:T(8,128)(2,1)S(1)} %get-tuple-element.26), channel_id=1, source_target_pairs={{0,2},{1,3},{2,0},{3,1},{4,6},{5,7},{6,4},{7,5},{8,10},{9,11},{10,... | collective-permute-start | bytes 405512 | tf_op jit(solution)/shard_map/ppermute | solution.py:373
  54.5 8.4 %collective-permute-start.11 = (bf16[528,128]{1,0:T(8,128)(2,1)S(1)}, bf16[528,128]{1,0:T(8,128)(2,1)S(1)}, u32[]{:S(2)}, u32[]{:S(2)}) collective-permute-start(bf16[528,128]{1,0:T(8,128)(2,1)S(1)} %get-tuple-element.28), channel_id=1, source_target_pairs={{0,4},{1,5},{2,6},{3,7},{4,0},{5,1},{6,2},{7,3},{8,12},{9,13},{10,... | collective-permute-start | bytes 405512 | tf_op jit(solution)/shard_map/ppermute | solution.py:373
  57.4 6.7 %collective-permute-start.14 = (bf16[528,128]{1,0:T(8,128)(2,1)S(1)}, bf16[528,128]{1,0:T(8,128)(2,1)S(1)}, u32[]{:S(2)}, u32[]{:S(2)}) collective-permute-start(bf16[528,128]{1,0:T(8,128)(2,1)S(1)} %get-tuple-element.30), channel_id=1, source_target_pairs={{0,2},{1,3},{2,0},{3,1},{4,6},{5,7},{6,4},{7,5},{8,10},{9,11},{10,... | collective-permute-start | bytes 405512 | tf_op jit(solution)/shard_map/ppermute | solution.py:373
  60.0 8.5 %collective-permute-start.19 = (bf16[1056,128]{1,0:T(8,128)(2,1)S(1)}, bf16[1056,128]{1,0:T(8,128)(2,1)S(1)}, u32[]{:S(2)}, u32[]{:S(2)}) collective-permute-start(bf16[1056,128]{1,0:T(8,128)(2,1)S(1)} %constant_dynamic-update-slice_fusion.6), channel_id=1, source_target_pairs={{0,2},{1,3},{2,0},{3,1},{4,6},{5,7},{6,4},{7,5},{8,10},{9,11},{10,... | collective-permute-start | bytes 811016 | tf_op jit(solution)/shard_map/ppermute | solution.py:373
  60.4 8.3 %collective-permute-start.22 = (bf16[1056,128]{1,0:T(8,128)(2,1)S(1)}, bf16[1056,128]{1,0:T(8,128)(2,1)S(1)}, u32[]{:S(2)}, u32[]{:S(2)}) collective-permute-start(bf16[1056,128]{1,0:T(8,128)(2,1)S(1)} %constant_dynamic-update-slice_fusion.2), channel_id=1, source_target_pairs={{0,4},{1,5},{2,6},{3,7},{4,0},{5,1},{6,2},{7,3},{8,12},{9,13},{10,... | collective-permute-start | bytes 811016 | tf_op jit(solution)/shard_map/ppermute | solution.py:373
  62.9 11.4 %collective-permute-start.12 = (bf16[1056,128]{1,0:T(8,128)(2,1)S(1)}, bf16[1056,128]{1,0:T(8,128)(2,1)S(1)}, u32[]{:S(2)}, u32[]{:S(2)}) collective-permute-start(bf16[1056,128]{1,0:T(8,128)(2,1)S(1)} %constant_dynamic-update-slice_fusion.14), channel_id=1, source_target_pairs={{0,2},{1,3},{2,0},{3,1},{4,6},{5,7},{6,4},{7,5},{8,10},{9,11},{10,... | collective-permute-start | bytes 811016 | tf_op jit(solution)/shard_map/ppermute | solution.py:373
  64.1 10.3 %collective-permute-start.15 = (bf16[1056,128]{1,0:T(8,128)(2,1)S(1)}, bf16[1056,128]{1,0:T(8,128)(2,1)S(1)}, u32[]{:S(2)}, u32[]{:S(2)}) collective-permute-start(bf16[1056,128]{1,0:T(8,128)(2,1)S(1)} %constant_dynamic-update-slice_fusion.10), channel_id=1, source_target_pairs={{0,4},{1,5},{2,6},{3,7},{4,0},{5,1},{6,2},{7,3},{8,12},{9,13},{10,... | collective-permute-start | bytes 811016 | tf_op jit(solution)/shard_map/ppermute | solution.py:373
  68.7 6.5 %collective-permute-start.23 = (bf16[4224,128]{1,0:T(8,128)(2,1)S(1)}, bf16[4224,128]{1,0:T(8,128)(2,1)S(1)}, u32[]{:S(2)}, u32[]{:S(2)}) collective-permute-start(bf16[4224,128]{1,0:T(8,128)(2,1)S(1)} %pad_maximum_fusion.3), channel_id=1, source_target_pairs={{0,1},{1,0},{2,3},{3,2},{4,5},{5,4},{6,7},{7,6},{8,9},{9,8},{10,11... | collective-permute-start | bytes 3244040 | tf_op jit(solution)/shard_map/ppermute | solution.py:373
  74.3 0.8 copy-start.4
  75.2 0.8 copy-start.3
  92.4 56.7 %all-to-all-start.1 = ((s16[16,264,256]{2,1,0:T(8,128)(2,1)}), s16[16,264,256]{2,1,0:T(8,128)(2,1)S(1)}, u32[]{:S(2)}, u32[]{:S(2)}) async-start(s16[16,264,256]{2,1,0:T(8,128)(2,1)} %get-tuple-element.22), calls=%async_computation.1 | async-start | bytes 4325376 | tf_op jit(solution)/shard_map/all_to_all | solution.py:587
  100.2 2.8 %collective-permute-start.16 = (bf16[4224,128]{1,0:T(8,128)(2,1)S(1)}, bf16[4224,128]{1,0:T(8,128)(2,1)S(1)}, u32[]{:S(2)}, u32[]{:S(2)}) collective-permute-start(bf16[4224,128]{1,0:T(8,128)(2,1)S(1)} %pad_maximum_fusion.2.refs_0_), channel_id=1, source_target_pairs={{0,1},{1,0},{2,3},{3,2},{4,5},{5,4},{6,7},{7,6},{8,9},{9,8},{10,11... | collective-permute-start | bytes 3244040 | tf_op jit(solution)/shard_map/ppermute | solution.py:373
  103.0 14.1 %slice-start.3 = ((s8[8388608]{0:T(1024)(128)(4,1)}), s8[4194304]{0:T(1024)(128)(4,1)S(1)}, s32[]{:S(2)}) async-start(s8[8388608]{0:T(1024)(128)(4,1)} %bitcast.18), calls=%async_computation.5 | async-start | bytes 8388608
  112.4 4.8 %slice-start.4 = ((s8[8388608]{0:T(1024)(128)(4,1)}), s8[4194304]{0:T(1024)(128)(4,1)S(1)}, s32[]{:S(2)}) async-start(s8[8388608]{0:T(1024)(128)(4,1)} %bitcast.18), calls=%async_computation.6 | async-start | bytes 8388608
  149.1 5.0 %copy-start.6 = (s32[4096]{0:T(1024)S(1)}, s32[4096]{0:T(1024)}, u32[]{:S(2)}) copy-start(s32[4096]{0:T(1024)} %param.6) | copy-start | bytes 49156
  149.1 54.0 %all-to-all-start = ((s16[16,264,256]{2,1,0:T(8,128)(2,1)}), s16[16,264,256]{2,1,0:T(8,128)(2,1)}, u32[]{:S(2)}, u32[]{:S(2)}) async-start(s16[16,264,256]{2,1,0:T(8,128)(2,1)} %get-tuple-element.21), calls=%async_computation | async-start | bytes 4325376 | tf_op jit(solution)/shard_map/all_to_all | solution.py:587

commit v18 on v16

--- a/solution.py
+++ b/solution.py
@@ -201,6 +201,7 @@
 SPAN = 16
 STEPS = 8
 RANGE = 14
+FIT = 1.0 - 2.0**-15
 EXTRA = 8
 
 
@@ -370,6 +371,32 @@
     return keep + swap(send, bit)
 
 
+def add_kernel(place_ref, value_ref, other_ref, out_ref):
+    size = out_ref.shape[0]
+    block = size // STEPS
+    start = place_ref[0] % 2 * size
+
+    @pl.loop(0, STEPS)
+    def _(step):
+        mine = value_ref[pl.ds(pl.multiple_of(start + step * block, 16), block), :]
+        spot = pl.ds(pl.multiple_of(step * block, 16), block)
+        out_ref[spot, :] = mine + other_ref[spot, :]
+
+
+def reduce_core(place, value):
+    size = value.shape[0] // 2
+    send = lax.dynamic_slice_in_dim(value, (1 - side(1)) * size, size, 0)
+    return pl.pallas_call(
+        add_kernel,
+        grid=(1,),
+        in_specs=[pl.BlockSpec(memory_space=pltpu.SMEM)] + [pl.BlockSpec(memory_space=pltpu.VMEM)] * 2,
+        out_specs=pl.BlockSpec(memory_space=pltpu.VMEM),
+        out_shape=jax.ShapeDtypeStruct((size, value.shape[1]), value.dtype),
+        compiler_params=pltpu.CompilerParams(vmem_limit_bytes=4 << 20),
+        name="add_halves",
+    )(place, value, swap(send, 1))
+
+
 def gather_half(value, bit, buffer):
     size = value.shape[0]
     other = swap(value, bit)
@@ -451,7 +478,7 @@
         count = products.shape[0]
         largest = jnp.maximum(jnp.max(jnp.abs(products), axis=0, keepdims=True), 2.0**-60)
         power = jnp.floor(jnp.log2(largest))
-        coded = jnp.clip(jnp.round(products * jnp.exp2(RANGE - power)), -32767.0, 32767.0)
+        coded = jnp.round(products * (jnp.exp2(RANGE - power) * FIT))
         out_ref[index, :count, :] = coded.astype(jnp.int32).astype(jnp.int16)
         line = jnp.broadcast_to(power, (out_ref.shape[1] - count, power.shape[1]))
         out_ref[index, count:, :] = line.astype(jnp.int32).astype(jnp.int16)
@@ -493,7 +520,7 @@
     def _():
         for source in range(sources):
             power = coded_ref[source, count:, :][:1].astype(jnp.float32)
-            values = coded_ref[source, :count, :].astype(jnp.float32) * (jnp.exp2(power - RANGE) * scale)
+            values = coded_ref[source, :count, :].astype(jnp.float32) * (jnp.exp2(power - RANGE) * (scale / FIT))
             for piece in range(pieces):
                 products[pl.ds(source * count * pieces + piece, count, stride=pieces), :] = values[
                     :, piece * LANES : (piece + 1) * LANES
@@ -552,7 +579,7 @@
     weights = jnp.asarray(filter_weights(ch))
     place = lax.axis_index("feed").reshape(1)
     picked = select_rows(place, words, scales, feed_slot.reshape(-1, LANES), ROWS, total)
-    halves, firsts = zip(*[quarters(reduce_half(value, 1)) for value in picked])
+    halves, firsts = zip(*[quarters(reduce_core(place, value)) for value in picked])
     seconds = [eighths(first) for first in firsts]
     own, zero = own_spectra(words, scales.astype(jnp.float32), weights, ch, spectra, sum(seconds, ()))
     thirds = [cross(second) for second in seconds]

time: 201 us -> 201 us (level)
  other arithmetic: 5.21 us -> 1.75 us
    add x10 -> x8, other arithmetic: 3.91 us -> 0.46 us  [reduce_half(): return keep + swap(send, bit)]
    dynamic_slice x0 -> x2, local copies, waits for them, and re-layouts: none -> 2.26 us  [reduce_core(): send = lax.dynamic_slice_in_dim(value, (1 - side(1)) * size, size, 0)]
  transfers between devices with their start and end apart: 26 -> 26, of which waited for: 17 -> 17; matrix products, arithmetic and copies ran while one was open for 3% -> 2% of each run, Pallas kernels for 13% -> 14%
where the time goes in v18:
time: 201 us
  waiting for transfers between devices  110 us (55%)
  Pallas kernels  47 us (23%)
  starting transfers between devices  34.6 us (17%)
  local copies, waits for them, and re-layouts  7.25 us (4%)
    all_to_all x2, waiting for transfers between devices, through_rows(): lax.all_to_all(coded, 'feed', split_axis=0, concat_axis=0, tiled=True)  77.4 us
    ppermute x24, waiting for transfers between devices, swap(): return lax.ppermute(value, 'feed', pairs)  32.4 us
    ppermute x24, starting transfers between devices, swap(): return lax.ppermute(value, 'feed', pairs)  21.4 us
    pallas_call x2, Pallas kernels, finish(): pl.pallas_call(functools.partial(finish_kernel, scale), grid=(columns //...  16.3 us
    all_to_all x2, starting transfers between devices, through_rows(): lax.all_to_all(coded, 'feed', split_axis=0, concat_axis=0, tiled=True)  13.2 us
    pallas_call x2, Pallas kernels, row_spectra(): pl.pallas_call(rows_kernel, grid=(1,), in_specs=[pl.BlockSpec(memory_spac...  9.42 us
    pallas_call x1, Pallas kernels, own_spectra(): pl.pallas_call(own_kernel, grid=(steps,), in_specs=[pl.BlockSpec((main, c...  9.05 us
    pallas_call x2, Pallas kernels, row_products(): pl.pallas_call(products_kernel, grid=(ch // each,), in_specs=[pl.BlockSpe...  8.32 us
  transfers between devices with their start and end apart: 26, of which 17 were waited for; matrix products, arithmetic and copies ran while one was open for 2% of the time, Pallas kernels for 14%

profile of v18, /device:TPU:13, one launch (start us, length us, event | category | flops | bytes accessed | tf_op | source)
XLA Modules:
  0.0 200.8 jit_solution(15126150941864275805)
XLA Ops:
  0.0 3.4 %copy-done = s32[256,16,519]{0,1,2:T(8,128)S(1)} copy-done((s32[256,16,519]{0,1,2:T(8,128)S(1)}, s32[256,16,519]{0,1,2:T(8,128)}, u32[]{:S(2)}) %copy-start) | copy-done | bytes 8503320
  3.4 2.1 %select_rows.1 = (bf16[8448,128]{1,0:T(8,128)(2,1)S(1)}, bf16[8448,128]{1,0:T(8,128)(2,1)S(1)}) custom-call(s32[1]{0:T(128)} %bitcast.3.place_ref, s32[32,128]{1,0:T(8,128)} %bitcast.19, s32[8304,256]{1,0:T(8,128)S(1)} %bitcast.13, s32[32,256]{1,0:T(8,128)} %bitcast.18), custom_call_target="tpu_custom_call" | custom-call | tf_op jit(solution)/shard_map/select_rows/pallas_call | solution.py:342
  5.5 1.2 constant_dynamic-slice_fusion.4
  6.7 0.7 collective-permute-start.5
  7.4 1.1 constant_dynamic-slice_fusion.9
  8.5 1.6 collective-permute-done.5.other_ref
  10.0 1.6 add_halves.3
  12.6 1.5 collective-permute-start.3
  14.2 1.3 collective-permute-start.1
  15.5 4.1 %collective-permute-done.8 = bf16[1056,128]{1,0:T(8,128)(2,1)S(1)} collective-permute-done((bf16[1056,128]{1,0:T(8,128)(2,1)S(1)}, bf16[1056,128]{1,0:T(8,128)(2,1)S(1)}, u32[]{:S(2)}, u32[]{:S(2)}) %collective-permute-start.8) | collective-permute-done | bytes 270368 | tf_op jit(solution)/shard_map/ppermute | solution.py:360
  19.7 0.3 collective-permute-start.9
  20.1 0.9 collective-permute-start.7
  21.0 4.3 %collective-permute-done.1 = bf16[1056,128]{1,0:T(8,128)(2,1)S(1)} collective-permute-done((bf16[1056,128]{1,0:T(8,128)(2,1)S(1)}, bf16[1056,128]{1,0:T(8,128)(2,1)S(1)}, u32[]{:S(2)}, u32[]{:S(2)}) %collective-permute-start.1) | collective-permute-done | bytes 270368 | tf_op jit(solution)/shard_map/ppermute | solution.py:360
  25.4 1.4 collective-permute-start.2
  26.9 0.3 collective-permute-start.4
  27.2 3.1 %collective-permute-done.2 = bf16[528,128]{1,0:T(8,128)(2,1)S(1)} collective-permute-done((bf16[528,128]{1,0:T(8,128)(2,1)S(1)}, bf16[528,128]{1,0:T(8,128)(2,1)S(1)}, u32[]{:S(2)}, u32[]{:S(2)}) %collective-permute-start.2) | collective-permute-done | bytes 135200 | tf_op jit(solution)/shard_map/ppermute | solution.py:360
  30.3 2.4 %collective-permute-start.17 = (bf16[528,128]{1,0:T(8,128)(2,1)S(1)}, bf16[528,128]{1,0:T(8,128)(2,1)S(1)}, u32[]{:S(2)}, u32[]{:S(2)}) collective-permute-start(bf16[528,128]{1,0:T(8,128)(2,1)S(1)} %dynamic-slice_add_fusion.7.refs_0_), channel_id=1, source_target_pairs={{0,8},{1,9},{2,10},{3,11},{4,12},{5,13},{6,14},{7,15},{8,0},{9,1},... | collective-permute-start | bytes 405512 | tf_op jit(solution)/shard_map/ppermute | solution.py:360
  32.7 0.5 collective-permute-start.20
  33.3 2.0 collective-permute-start.10
  35.3 0.5 collective-permute-start.13
  35.9 9.1 %own_spectra.1 = (bf16[16,8,256,128]{3,2,1,0:T(8,128)(2,1)S(1)}, bf16[16,128]{1,0:T(8,128)(2,1)S(1)}) custom-call(s32[8304,256]{1,0:T(8,128)S(1)} %bitcast.16, s32[8304,256]{1,0:T(8,128)S(1)} %bitcast.17, f32[32,256]{1,0:T(8,128)S(1)} %bitcast_convert_fusion.gains_ref, bf16[256,256]{1,0:T(8,128)(2,1)S(1)} %copy-done.5, ...), custom_call_target="tpu_custom_call" | custom-call | flops 4294967296 | bytes 16891904 | tf_op jit(solution)/shard_map/own_spectra/pallas_call | solution.py:283
  44.9 0.5 slice.26
  45.5 1.6 collective-permute-done.17
  47.1 0.6 constant_dynamic-update-slice_fusion.9
  47.8 2.2 %collective-permute-done.20 = bf16[528,128]{1,0:T(8,128)(2,1)S(1)} collective-permute-done((bf16[528,128]{1,0:T(8,128)(2,1)S(1)}, bf16[528,128]{1,0:T(8,128)(2,1)S(1)}, u32[]{:S(2)}, u32[]{:S(2)}) %collective-permute-start.20) | collective-permute-done | bytes 135200 | tf_op jit(solution)/shard_map/ppermute | solution.py:360
  50.0 0.3 collective-permute-start.21
  50.3 2.6 %collective-permute-done.10 = bf16[528,128]{1,0:T(8,128)(2,1)S(1)} collective-permute-done((bf16[528,128]{1,0:T(8,128)(2,1)S(1)}, bf16[528,128]{1,0:T(8,128)(2,1)S(1)}, u32[]{:S(2)}, u32[]{:S(2)}) %collective-permute-start.10) | collective-permute-done | bytes 135200 | tf_op jit(solution)/shard_map/ppermute | solution.py:360
  53.0 0.6 collective-permute-start.11
  53.6 2.2 %collective-permute-done.13 = bf16[528,128]{1,0:T(8,128)(2,1)S(1)} collective-permute-done((bf16[528,128]{1,0:T(8,128)(2,1)S(1)}, bf16[528,128]{1,0:T(8,128)(2,1)S(1)}, u32[]{:S(2)}, u32[]{:S(2)}) %collective-permute-start.13) | collective-permute-done | bytes 135200 | tf_op jit(solution)/shard_map/ppermute | solution.py:360
  56.2 2.3 %collective-permute-done.18 = bf16[528,128]{1,0:T(8,128)(2,1)S(1)} collective-permute-done((bf16[528,128]{1,0:T(8,128)(2,1)S(1)}, bf16[528,128]{1,0:T(8,128)(2,1)S(1)}, u32[]{:S(2)}, u32[]{:S(2)}) %collective-permute-start.18) | collective-permute-done | bytes 135200 | tf_op jit(solution)/shard_map/ppermute | solution.py:360
  58.8 2.3 %collective-permute-start.22 = (bf16[1056,128]{1,0:T(8,128)(2,1)S(1)}, bf16[1056,128]{1,0:T(8,128)(2,1)S(1)}, u32[]{:S(2)}, u32[]{:S(2)}) collective-permute-start(bf16[1056,128]{1,0:T(8,128)(2,1)S(1)} %constant_dynamic-update-slice_fusion.4), channel_id=1, source_target_pairs={{0,4},{1,5},{2,6},{3,7},{4,0},{5,1},{6,2},{7,3},{8,12},{9,13},{10,... | collective-permute-start | bytes 811016 | tf_op jit(solution)/shard_map/ppermute | solution.py:360
  61.4 1.1 collective-permute-start.12
  62.6 1.4 collective-permute-start.15
  64.0 2.9 %collective-permute-done.19 = bf16[1056,128]{1,0:T(8,128)(2,1)S(1)} collective-permute-done((bf16[1056,128]{1,0:T(8,128)(2,1)S(1)}, bf16[1056,128]{1,0:T(8,128)(2,1)S(1)}, u32[]{:S(2)}, u32[]{:S(2)}) %collective-permute-start.19) | collective-permute-done | bytes 270368 | tf_op jit(solution)/shard_map/ppermute | solution.py:360
  67.3 2.6 %collective-permute-start.23 = (bf16[4224,128]{1,0:T(8,128)(2,1)S(1)}, bf16[4224,128]{1,0:T(8,128)(2,1)S(1)}, u32[]{:S(2)}, u32[]{:S(2)}) collective-permute-start(bf16[4224,128]{1,0:T(8,128)(2,1)S(1)} %get-tuple-element.27), channel_id=1, source_target_pairs={{0,1},{1,0},{2,3},{3,2},{4,5},{5,4},{6,7},{7,6},{8,9},{9,8},{10,11... | collective-permute-start | bytes 3244040 | tf_op jit(solution)/shard_map/ppermute | solution.py:360
  69.9 2.8 %collective-permute-done.12 = bf16[1056,128]{1,0:T(8,128)(2,1)S(1)} collective-permute-done((bf16[1056,128]{1,0:T(8,128)(2,1)S(1)}, bf16[1056,128]{1,0:T(8,128)(2,1)S(1)}, u32[]{:S(2)}, u32[]{:S(2)}) %collective-permute-start.12) | collective-permute-done | bytes 270368 | tf_op jit(solution)/shard_map/ppermute | solution.py:360
  73.3 4.7 %row_spectra.3.left_ref = bf16[16,1024,256]{2,1,0:T(8,128)(2,1)S(1)} custom-call(bf16[8448,128]{1,0:T(8,128)(2,1)S(1)} %constant_dynamic-update-slice_fusion.words_ref, bf16[64,128]{1,0:T(8,128)(2,1)S(1)} %slice.33.parts_ref, bf16[256,256]{1,0:T(8,128)(2,1)S(1)} %copy-done.5), custom_call_target="tpu_custom_call" | custom-call | flops 2147483648 | bytes 10551296 | tf_op jit(solution)/shard_map/row_spectra/pallas_call | solution.py:450
  78.1 4.1 %row_products.2 = (s16[16,264,256]{2,1,0:T(8,128)(2,1)}, bf16[16,128]{1,0:T(8,128)(2,1)S(1)}) custom-call(bf16[16,8,256,128]{3,2,1,0:T(8,128)(2,1)S(1)} %get-tuple-element.14.own_ref, bf16[16,1024,256]{2,1,0:T(8,128)(2,1)S(1)} %row_spectra.3.left_ref, bf16[4224,128]{1,0:T(8,128)(2,1)S(1)} %get-tuple-element.29.refs_0_), custom_call_target="tpu_custom_call" | custom-call | flops 2147483648 | bytes 16777216 | tf_op jit(solution)/shard_map/row_products/pallas_call | solution.py:491
  82.2 8.1 %all-to-all-start.1 = ((s16[16,264,256]{2,1,0:T(8,128)(2,1)}), s16[16,264,256]{2,1,0:T(8,128)(2,1)}, u32[]{:S(2)}, u32[]{:S(2)}) async-start(s16[16,264,256]{2,1,0:T(8,128)(2,1)} %get-tuple-element.18), calls=%async_computation.1 | async-start | bytes 4325376 | tf_op jit(solution)/shard_map/all_to_all | solution.py:595
  90.3 0.4 collective-permute-start.16
  90.7 2.4 %collective-permute-done.16 = bf16[4224,128]{1,0:T(8,128)(2,1)S(1)} collective-permute-done((bf16[4224,128]{1,0:T(8,128)(2,1)S(1)}, bf16[4224,128]{1,0:T(8,128)(2,1)S(1)}, u32[]{:S(2)}, u32[]{:S(2)}) %collective-permute-start.16) | collective-permute-done | bytes 1081376 | tf_op jit(solution)/shard_map/ppermute | solution.py:360
  93.3 4.7 %row_spectra.2.left_ref = bf16[16,1024,256]{2,1,0:T(8,128)(2,1)S(1)} custom-call(bf16[8448,128]{1,0:T(8,128)(2,1)S(1)} %constant_dynamic-update-slice_fusion.10.words_ref, bf16[64,128]{1,0:T(8,128)(2,1)S(1)} %slice.32.parts_ref, bf16[256,256]{1,0:T(8,128)(2,1)S(1)} %copy-done.5), custom_call_target="tpu_custom_call" | custom-call | flops 2147483648 | bytes 10551296 | tf_op jit(solution)/shard_map/row_spectra/pallas_call | solution.py:450
  98.0 4.2 %row_products.3 = (s16[16,264,256]{2,1,0:T(8,128)(2,1)}, bf16[16,128]{1,0:T(8,128)(2,1)}) custom-call(bf16[16,8,256,128]{3,2,1,0:T(8,128)(2,1)S(1)} %copy-done.2, bf16[16,1024,256]{2,1,0:T(8,128)(2,1)S(1)} %row_spectra.2.left_ref, bf16[16,128]{1,0:T(8,128)(2,1)S(1)} %get-tuple-element.16.refs_0_), custom_call_target="tpu_custom_call" | custom-call | flops 2147483648 | bytes 16777216 | tf_op jit(solution)/shard_map/row_products/pallas_call | solution.py:491
  102.2 37.1 %all-to-all-done.1.coded_ref = s16[16,264,256]{2,1,0:T(8,128)(2,1)} async-done(((s16[16,264,256]{2,1,0:T(8,128)(2,1)}), s16[16,264,256]{2,1,0:T(8,128)(2,1)}, u32[]{:S(2)}, u32[]{:S(2)}) %all-to-all-start.1) | async-done | bytes 2162720 | tf_op jit(solution)/shard_map/all_to_all | solution.py:595
  139.3 5.0 %all-to-all-start = ((s16[16,264,256]{2,1,0:T(8,128)(2,1)}), s16[16,264,256]{2,1,0:T(8,128)(2,1)S(1)}, u32[]{:S(2)}, u32[]{:S(2)}) async-start(s16[16,264,256]{2,1,0:T(8,128)(2,1)} %get-tuple-element.17), calls=%async_computation | async-start | bytes 4325376 | tf_op jit(solution)/shard_map/all_to_all | solution.py:595
  144.3 8.6 %finish.2.refs_0_ = f32[256,64,128]{2,1,0:T(8,128)} custom-call(s32[4096]{0:T(1024)S(1)} %broadcast_multiply_fusion.slot_ref, s16[16,264,256]{2,1,0:T(8,128)(2,1)} %all-to-all-done.1.coded_ref), custom_call_target="tpu_custom_call" | custom-call | tf_op jit(solution)/shard_map/finish/pallas_call | solution.py:549
  152.9 40.2 %all-to-all-done.coded_ref = s16[16,264,256]{2,1,0:T(8,128)(2,1)S(1)} async-done(((s16[16,264,256]{2,1,0:T(8,128)(2,1)}), s16[16,264,256]{2,1,0:T(8,128)(2,1)S(1)}, u32[]{:S(2)}, u32[]{:S(2)}) %all-to-all-start) | async-done | bytes 2162720 | tf_op jit(solution)/shard_map/all_to_all | solution.py:595
  193.1 7.7 %finish.3 = f32[256,64,128]{2,1,0:T(8,128)} custom-call(s32[4096]{0:T(1024)S(1)} %broadcast_multiply_fusion.slot_ref, s16[16,264,256]{2,1,0:T(8,128)(2,1)S(1)} %all-to-all-done.coded_ref, f32[256,64,128]{2,1,0:T(8,128)} %finish.2.refs_0_), custom_call_target="tpu_custom_call", output_to_operand_aliasing={{}: (2, {})} | custom-call | tf_op jit(solution)/shard_map/finish/pallas_call | solution.py:549
  (82 shorter events, 3.8 us)
Async XLA Ops:
  0.0 3.4 %copy-start = (s32[256,16,519]{0,1,2:T(8,128)S(1)}, s32[256,16,519]{0,1,2:T(8,128)}, u32[]{:S(2)}) copy-start(s32[256,16,519]{0,1,2:T(8,128)} %param.4) | copy-start | bytes 25509892
  5.5 3.0 %copy-start.3 = (bf16[8448,128]{1,0:T(8,128)(2,1)}, bf16[8448,128]{1,0:T(8,128)(2,1)S(1)}, u32[]{:S(2)}) copy-start(bf16[8448,128]{1,0:T(8,128)(2,1)S(1)} %get-tuple-element.12.value_ref) | copy-start | bytes 6488068
  5.5 3.0 %copy-start.6 = (s32[2,16,256]{2,1,0:T(8,128)S(1)}, s32[2,16,256]{2,1,0:T(8,128)}, u32[]{:S(2)}) copy-start(s32[2,16,256]{2,1,0:T(8,128)} %param.5) | copy-start | bytes 98308
  6.7 3.4 %collective-permute-start.5 = (bf16[4224,128]{1,0:T(8,128)(2,1)}, bf16[4224,128]{1,0:T(8,128)(2,1)}, u32[]{:S(2)}, u32[]{:S(2)}) collective-permute-start(bf16[4224,128]{1,0:T(8,128)(2,1)} %constant_dynamic-slice_fusion.4), channel_id=1, source_target_pairs={{0,1},{1,0},{2,3},{3,2},{4,5},{5,4},{6,7},{7,6},{8,9},{9,8},{10,11... | collective-permute-start | bytes 3244040 | tf_op jit(solution)/shard_map/ppermute | solution.py:360
  7.4 28.5 %slice-start = ((s8[8503296]{0:T(1024)(128)(4,1)}), s8[114688]{0:T(1024)(128)(4,1)S(1)}, s32[]{:S(2)}) async-start(s8[8503296]{0:T(1024)(128)(4,1)} %bitcast.14), calls=%async_computation.2 | async-start | bytes 229376
  8.5 3.8 %collective-permute-start = (bf16[4224,128]{1,0:T(8,128)(2,1)}, bf16[4224,128]{1,0:T(8,128)(2,1)S(1)}, u32[]{:S(2)}, u32[]{:S(2)}) collective-permute-start(bf16[4224,128]{1,0:T(8,128)(2,1)} %constant_dynamic-slice_fusion.9), channel_id=1, source_target_pairs={{0,1},{1,0},{2,3},{3,2},{4,5},{5,4},{6,7},{7,6},{8,9},{9,8},{10,11... | collective-permute-start | bytes 3244040 | tf_op jit(solution)/shard_map/ppermute | solution.py:360
  10.0 2.2 %copy-start.4 = (bf16[8448,128]{1,0:T(8,128)(2,1)S(1)}, bf16[8448,128]{1,0:T(8,128)(2,1)}, u32[]{:S(2)}) copy-start(bf16[8448,128]{1,0:T(8,128)(2,1)} %copy-done.3) | copy-start | bytes 6488068
  11.7 24.1 %slice-start.1 = ((s8[8503296]{0:T(1024)(128)(4,1)}), s8[4194304]{0:T(1024)(128)(4,1)S(1)}, s32[]{:S(2)}) async-start(s8[8503296]{0:T(1024)(128)(4,1)} %bitcast.14), calls=%async_computation.3 | async-start | bytes 8388608
  11.8 7.8 %collective-permute-start.8 = (bf16[1056,128]{1,0:T(8,128)(2,1)S(1)}, bf16[1056,128]{1,0:T(8,128)(2,1)S(1)}, u32[]{:S(2)}, u32[]{:S(2)}) collective-permute-start(bf16[1056,128]{1,0:T(8,128)(2,1)S(1)} %constant_dynamic-slice_fusion.1), channel_id=1, source_target_pairs={{0,4},{1,5},{2,6},{3,7},{4,0},{5,1},{6,2},{7,3},{8,12},{9,13},{10,... | collective-permute-start | bytes 811016 | tf_op jit(solution)/shard_map/ppermute | solution.py:360
  12.1 7.9 %collective-permute-start.6 = (bf16[1056,128]{1,0:T(8,128)(2,1)S(1)}, bf16[1056,128]{1,0:T(8,128)(2,1)S(1)}, u32[]{:S(2)}, u32[]{:S(2)}) collective-permute-start(bf16[1056,128]{1,0:T(8,128)(2,1)S(1)} %constant_dynamic-slice_fusion.3), channel_id=1, source_target_pairs={{0,2},{1,3},{2,0},{3,1},{4,6},{5,7},{6,4},{7,5},{8,10},{9,11},{10,... | collective-permute-start | bytes 811016 | tf_op jit(solution)/shard_map/ppermute | solution.py:360
  12.5 23.3 %slice-start.2 = ((s8[8503296]{0:T(1024)(128)(4,1)}), s8[4194304]{0:T(1024)(128)(4,1)S(1)}, s32[]{:S(2)}) async-start(s8[8503296]{0:T(1024)(128)(4,1)} %bitcast.14), calls=%async_computation.4 | async-start | bytes 8388608
  12.6 14.1 %collective-permute-start.3 = (bf16[1056,128]{1,0:T(8,128)(2,1)S(1)}, bf16[1056,128]{1,0:T(8,128)(2,1)S(1)}, u32[]{:S(2)}, u32[]{:S(2)}) collective-permute-start(bf16[1056,128]{1,0:T(8,128)(2,1)S(1)} %constant_dynamic-slice_fusion.6), channel_id=1, source_target_pairs={{0,4},{1,5},{2,6},{3,7},{4,0},{5,1},{6,2},{7,3},{8,12},{9,13},{10,... | collective-permute-start | bytes 811016 | tf_op jit(solution)/shard_map/ppermute | solution.py:360
  14.2 11.2 %collective-permute-start.1 = (bf16[1056,128]{1,0:T(8,128)(2,1)S(1)}, bf16[1056,128]{1,0:T(8,128)(2,1)S(1)}, u32[]{:S(2)}, u32[]{:S(2)}) collective-permute-start(bf16[1056,128]{1,0:T(8,128)(2,1)S(1)} %constant_dynamic-slice_fusion.8), channel_id=1, source_target_pairs={{0,2},{1,3},{2,0},{3,1},{4,6},{5,7},{6,4},{7,5},{8,10},{9,11},{10,... | collective-permute-start | bytes 811016 | tf_op jit(solution)/shard_map/ppermute | solution.py:360
  19.7 15.6 %collective-permute-start.9 = (bf16[528,128]{1,0:T(8,128)(2,1)S(1)}, bf16[528,128]{1,0:T(8,128)(2,1)S(1)}, u32[]{:S(2)}, u32[]{:S(2)}) collective-permute-start(bf16[528,128]{1,0:T(8,128)(2,1)S(1)} %constant_dynamic-slice_fusion), channel_id=1, source_target_pairs={{0,2},{1,3},{2,0},{3,1},{4,6},{5,7},{6,4},{7,5},{8,10},{9,11},{10,... | collective-permute-start | bytes 405512 | tf_op jit(solution)/shard_map/ppermute | solution.py:360
  20.1 15.8 %copy-start.5 = (bf16[256,256]{1,0:T(8,128)(2,1)S(1)}, bf16[256,256]{1,0:T(8,128)(2,1)}, u32[]{:S(2)}) copy-start(bf16[256,256]{1,0:T(8,128)(2,1)} %constant.209.clone.weights_ref) | copy-start | bytes 393220
  20.1 13.1 %collective-permute-start.7 = (bf16[528,128]{1,0:T(8,128)(2,1)S(1)}, bf16[528,128]{1,0:T(8,128)(2,1)S(1)}, u32[]{:S(2)}, u32[]{:S(2)}) collective-permute-start(bf16[528,128]{1,0:T(8,128)(2,1)S(1)} %constant_dynamic-slice_fusion.2), channel_id=1, source_target_pairs={{0,4},{1,5},{2,6},{3,7},{4,0},{5,1},{6,2},{7,3},{8,12},{9,13},{10,... | collective-permute-start | bytes 405512 | tf_op jit(solution)/shard_map/ppermute | solution.py:360
  25.4 4.8 %collective-permute-start.2 = (bf16[528,128]{1,0:T(8,128)(2,1)S(1)}, bf16[528,128]{1,0:T(8,128)(2,1)S(1)}, u32[]{:S(2)}, u32[]{:S(2)}) collective-permute-start(bf16[528,128]{1,0:T(8,128)(2,1)S(1)} %constant_dynamic-slice_fusion.7), channel_id=1, source_target_pairs={{0,4},{1,5},{2,6},{3,7},{4,0},{5,1},{6,2},{7,3},{8,12},{9,13},{10,... | collective-permute-start | bytes 405512 | tf_op jit(solution)/shard_map/ppermute | solution.py:360
  26.9 5.8 %collective-permute-start.4 = (bf16[528,128]{1,0:T(8,128)(2,1)S(1)}, bf16[528,128]{1,0:T(8,128)(2,1)S(1)}, u32[]{:S(2)}, u32[]{:S(2)}) collective-permute-start(bf16[528,128]{1,0:T(8,128)(2,1)S(1)} %constant_dynamic-slice_fusion.5), channel_id=1, source_target_pairs={{0,2},{1,3},{2,0},{3,1},{4,6},{5,7},{6,4},{7,5},{8,10},{9,11},{10,... | collective-permute-start | bytes 405512 | tf_op jit(solution)/shard_map/ppermute | solution.py:360
  30.3 16.8 %collective-permute-start.17 = (bf16[528,128]{1,0:T(8,128)(2,1)S(1)}, bf16[528,128]{1,0:T(8,128)(2,1)S(1)}, u32[]{:S(2)}, u32[]{:S(2)}) collective-permute-start(bf16[528,128]{1,0:T(8,128)(2,1)S(1)} %dynamic-slice_add_fusion.7.refs_0_), channel_id=1, source_target_pairs={{0,8},{1,9},{2,10},{3,11},{4,12},{5,13},{6,14},{7,15},{8,0},{9,1},... | collective-permute-start | bytes 405512 | tf_op jit(solution)/shard_map/ppermute | solution.py:360
  32.7 17.3 %collective-permute-start.20 = (bf16[528,128]{1,0:T(8,128)(2,1)S(1)}, bf16[528,128]{1,0:T(8,128)(2,1)S(1)}, u32[]{:S(2)}, u32[]{:S(2)}) collective-permute-start(bf16[528,128]{1,0:T(8,128)(2,1)S(1)} %dynamic-slice_add_fusion.6.refs_1_), channel_id=1, source_target_pairs={{0,8},{1,9},{2,10},{3,11},{4,12},{5,13},{6,14},{7,15},{8,0},{9,1},... | collective-permute-start | bytes 405512 | tf_op jit(solution)/shard_map/ppermute | solution.py:360
  33.3 19.6 %collective-permute-start.10 = (bf16[528,128]{1,0:T(8,128)(2,1)S(1)}, bf16[528,128]{1,0:T(8,128)(2,1)S(1)}, u32[]{:S(2)}, u32[]{:S(2)}) collective-permute-start(bf16[528,128]{1,0:T(8,128)(2,1)S(1)} %dynamic-slice_add_fusion.5.refs_2_), channel_id=1, source_target_pairs={{0,8},{1,9},{2,10},{3,11},{4,12},{5,13},{6,14},{7,15},{8,0},{9,1},... | collective-permute-start | bytes 405512 | tf_op jit(solution)/shard_map/ppermute | solution.py:360
  35.3 20.5 %collective-permute-start.13 = (bf16[528,128]{1,0:T(8,128)(2,1)S(1)}, bf16[528,128]{1,0:T(8,128)(2,1)S(1)}, u32[]{:S(2)}, u32[]{:S(2)}) collective-permute-start(bf16[528,128]{1,0:T(8,128)(2,1)S(1)} %dynamic-slice_add_fusion.4.refs_3_), channel_id=1, source_target_pairs={{0,8},{1,9},{2,10},{3,11},{4,12},{5,13},{6,14},{7,15},{8,0},{9,1},... | collective-permute-start | bytes 405512 | tf_op jit(solution)/shard_map/ppermute | solution.py:360
  44.9 33.1 %copy-start.1 = (bf16[16,8,256,128]{3,2,1,0:T(8,128)(2,1)}, bf16[16,8,256,128]{3,2,1,0:T(8,128)(2,1)S(1)}, u32[]{:S(2)}) copy-start(bf16[16,8,256,128]{3,2,1,0:T(8,128)(2,1)S(1)} %get-tuple-element.14.own_ref) | copy-start | bytes 25165828
  47.7 10.7 %collective-permute-start.18 = (bf16[528,128]{1,0:T(8,128)(2,1)S(1)}, bf16[528,128]{1,0:T(8,128)(2,1)S(1)}, u32[]{:S(2)}, u32[]{:S(2)}) collective-permute-start(bf16[528,128]{1,0:T(8,128)(2,1)S(1)} %get-tuple-element.20), channel_id=1, source_target_pairs={{0,4},{1,5},{2,6},{3,7},{4,0},{5,1},{6,2},{7,3},{8,12},{9,13},{10,... | collective-permute-start | bytes 405512 | tf_op jit(solution)/shard_map/ppermute | solution.py:360
  50.0 8.8 %collective-permute-start.21 = (bf16[528,128]{1,0:T(8,128)(2,1)S(1)}, bf16[528,128]{1,0:T(8,128)(2,1)S(1)}, u32[]{:S(2)}, u32[]{:S(2)}) collective-permute-start(bf16[528,128]{1,0:T(8,128)(2,1)S(1)} %get-tuple-element.22), channel_id=1, source_target_pairs={{0,2},{1,3},{2,0},{3,1},{4,6},{5,7},{6,4},{7,5},{8,10},{9,11},{10,... | collective-permute-start | bytes 405512 | tf_op jit(solution)/shard_map/ppermute | solution.py:360
  53.0 8.4 %collective-permute-start.11 = (bf16[528,128]{1,0:T(8,128)(2,1)S(1)}, bf16[528,128]{1,0:T(8,128)(2,1)S(1)}, u32[]{:S(2)}, u32[]{:S(2)}) collective-permute-start(bf16[528,128]{1,0:T(8,128)(2,1)S(1)} %get-tuple-element.24), channel_id=1, source_target_pairs={{0,4},{1,5},{2,6},{3,7},{4,0},{5,1},{6,2},{7,3},{8,12},{9,13},{10,... | collective-permute-start | bytes 405512 | tf_op jit(solution)/shard_map/ppermute | solution.py:360
  55.9 6.7 %collective-permute-start.14 = (bf16[528,128]{1,0:T(8,128)(2,1)S(1)}, bf16[528,128]{1,0:T(8,128)(2,1)S(1)}, u32[]{:S(2)}, u32[]{:S(2)}) collective-permute-start(bf16[528,128]{1,0:T(8,128)(2,1)S(1)} %get-tuple-element.26), channel_id=1, source_target_pairs={{0,2},{1,3},{2,0},{3,1},{4,6},{5,7},{6,4},{7,5},{8,10},{9,11},{10,... | collective-permute-start | bytes 405512 | tf_op jit(solution)/shard_map/ppermute | solution.py:360
  58.5 8.5 %collective-permute-start.19 = (bf16[1056,128]{1,0:T(8,128)(2,1)S(1)}, bf16[1056,128]{1,0:T(8,128)(2,1)S(1)}, u32[]{:S(2)}, u32[]{:S(2)}) collective-permute-start(bf16[1056,128]{1,0:T(8,128)(2,1)S(1)} %constant_dynamic-update-slice_fusion.8), channel_id=1, source_target_pairs={{0,2},{1,3},{2,0},{3,1},{4,6},{5,7},{6,4},{7,5},{8,10},{9,11},{10,... | collective-permute-start | bytes 811016 | tf_op jit(solution)/shard_map/ppermute | solution.py:360
  58.8 8.3 %collective-permute-start.22 = (bf16[1056,128]{1,0:T(8,128)(2,1)S(1)}, bf16[1056,128]{1,0:T(8,128)(2,1)S(1)}, u32[]{:S(2)}, u32[]{:S(2)}) collective-permute-start(bf16[1056,128]{1,0:T(8,128)(2,1)S(1)} %constant_dynamic-update-slice_fusion.4), channel_id=1, source_target_pairs={{0,4},{1,5},{2,6},{3,7},{4,0},{5,1},{6,2},{7,3},{8,12},{9,13},{10,... | collective-permute-start | bytes 811016 | tf_op jit(solution)/shard_map/ppermute | solution.py:360
  61.4 11.4 %collective-permute-start.12 = (bf16[1056,128]{1,0:T(8,128)(2,1)S(1)}, bf16[1056,128]{1,0:T(8,128)(2,1)S(1)}, u32[]{:S(2)}, u32[]{:S(2)}) collective-permute-start(bf16[1056,128]{1,0:T(8,128)(2,1)S(1)} %constant_dynamic-update-slice_fusion.18), channel_id=1, source_target_pairs={{0,2},{1,3},{2,0},{3,1},{4,6},{5,7},{6,4},{7,5},{8,10},{9,11},{10,... | collective-permute-start | bytes 811016 | tf_op jit(solution)/shard_map/ppermute | solution.py:360
  62.6 10.3 %collective-permute-start.15 = (bf16[1056,128]{1,0:T(8,128)(2,1)S(1)}, bf16[1056,128]{1,0:T(8,128)(2,1)S(1)}, u32[]{:S(2)}, u32[]{:S(2)}) collective-permute-start(bf16[1056,128]{1,0:T(8,128)(2,1)S(1)} %constant_dynamic-update-slice_fusion.14), channel_id=1, source_target_pairs={{0,4},{1,5},{2,6},{3,7},{4,0},{5,1},{6,2},{7,3},{8,12},{9,13},{10,... | collective-permute-start | bytes 811016 | tf_op jit(solution)/shard_map/ppermute | solution.py:360
  67.3 5.8 %collective-permute-start.23 = (bf16[4224,128]{1,0:T(8,128)(2,1)S(1)}, bf16[4224,128]{1,0:T(8,128)(2,1)S(1)}, u32[]{:S(2)}, u32[]{:S(2)}) collective-permute-start(bf16[4224,128]{1,0:T(8,128)(2,1)S(1)} %get-tuple-element.27), channel_id=1, source_target_pairs={{0,1},{1,0},{2,3},{3,2},{4,5},{5,4},{6,7},{7,6},{8,9},{9,8},{10,11... | collective-permute-start | bytes 3244040 | tf_op jit(solution)/shard_map/ppermute | solution.py:360
  82.2 57.1 %all-to-all-start.1 = ((s16[16,264,256]{2,1,0:T(8,128)(2,1)}), s16[16,264,256]{2,1,0:T(8,128)(2,1)}, u32[]{:S(2)}, u32[]{:S(2)}) async-start(s16[16,264,256]{2,1,0:T(8,128)(2,1)} %get-tuple-element.18), calls=%async_computation.1 | async-start | bytes 4325376 | tf_op jit(solution)/shard_map/all_to_all | solution.py:595
  90.3 2.7 %collective-permute-start.16 = (bf16[4224,128]{1,0:T(8,128)(2,1)S(1)}, bf16[4224,128]{1,0:T(8,128)(2,1)S(1)}, u32[]{:S(2)}, u32[]{:S(2)}) collective-permute-start(bf16[4224,128]{1,0:T(8,128)(2,1)S(1)} %get-tuple-element.29.refs_0_), channel_id=1, source_target_pairs={{0,1},{1,0},{2,3},{3,2},{4,5},{5,4},{6,7},{7,6},{8,9},{9,8},{10,11... | collective-permute-start | bytes 3244040 | tf_op jit(solution)/shard_map/ppermute | solution.py:360
  93.2 4.7 %copy-start.2 = (bf16[16,8,256,128]{3,2,1,0:T(8,128)(2,1)S(1)}, bf16[16,8,256,128]{3,2,1,0:T(8,128)(2,1)}, u32[]{:S(2)}) copy-start(bf16[16,8,256,128]{3,2,1,0:T(8,128)(2,1)} %copy-done.1) | copy-start | bytes 25165828
  139.3 5.0 %copy-start.7 = (s32[4096]{0:T(1024)S(1)}, s32[4096]{0:T(1024)}, u32[]{:S(2)}) copy-start(s32[4096]{0:T(1024)} %param.6) | copy-start | bytes 49156
  139.3 53.9 %all-to-all-start = ((s16[16,264,256]{2,1,0:T(8,128)(2,1)}), s16[16,264,256]{2,1,0:T(8,128)(2,1)S(1)}, u32[]{:S(2)}, u32[]{:S(2)}) async-start(s16[16,264,256]{2,1,0:T(8,128)(2,1)} %get-tuple-element.17), calls=%async_computation | async-start | bytes 4325376 | tf_op jit(solution)/shard_map/all_to_all | solution.py:595

commit v19 on v18

--- a/solution.py
+++ b/solution.py
@@ -311,27 +311,35 @@
     )(words, words, gains, weights, *after)
 
 
-def select_kernel(block, place_ref, slots_ref, words_ref, gains_ref, *outs):
+def select_kernel(block, place_ref, slots_ref, words_ref, gains_ref, *refs):
     lines, count = words_ref.shape
-    rows = len(outs) * LANES
+    outs, sends = refs[: len(refs) // 2], refs[len(refs) // 2 :]
+    rows, size = len(outs) * LANES, sends[0].shape[0]
     place = lax.broadcasted_iota(jnp.int32, (count, rows), 0) + place_ref[0] * count
     slots = jnp.concatenate([slots_ref[index : index + 1, :] for index in range(len(outs))], axis=1)
     choice = jnp.where(slots == place, 1.0, 0.0).astype(jnp.bfloat16)
 
+    def store(first, taken):
+        half = first // size
+        spot = slice(first - half * size, first - half * size + taken.shape[0])
+        for index, out_ref in enumerate(outs):
+            out_ref[first : first + taken.shape[0], :] = taken[:, index * LANES : (index + 1) * LANES]
+
+        @pl.when(place_ref[0] % 2 != half)
+        def _():
+            for index, send_ref in enumerate(sends):
+                send_ref[spot, :] = taken[:, index * LANES : (index + 1) * LANES]
+
     def put(first, values):
-        size = values.shape[0]
         values = values.astype(jnp.float32).astype(jnp.bfloat16)
-        taken = jnp.dot(values, choice, preferred_element_type=jnp.float32).astype(outs[0].dtype)
-        for index, out_ref in enumerate(outs):
-            out_ref[first : first + size, :] = taken[:, index * LANES : (index + 1) * LANES]
+        store(first, jnp.dot(values, choice, preferred_element_type=jnp.float32).astype(outs[0].dtype))
 
     for first in range(0, lines, block):
         put(first, words_ref[first : min(first + block, lines), :])
     gains = gains_ref[...]
     put(lines, jnp.concatenate([gains >> 4, gains & 15], axis=0))
     first = lines + 2 * gains.shape[0]
-    for out_ref in outs:
-        out_ref[first:, :] = jnp.zeros((out_ref.shape[0] - first, LANES), out_ref.dtype)
+    store(first, jnp.zeros((2 * size - first, rows), outs[0].dtype))
 
 
 def at_hand(value):
@@ -339,7 +347,8 @@
 
 
 def select_rows(place, words, gains, slots, rows, total):
-    return pl.pallas_call(
+    pieces = rows // LANES
+    outs = pl.pallas_call(
         functools.partial(select_kernel, total // STEPS),
         grid=(1,),
         in_specs=[
@@ -348,11 +357,13 @@
             pl.BlockSpec(memory_space=pltpu.VMEM),
             pl.BlockSpec(gains.shape, lambda i: (0, 0)),
         ],
-        out_specs=[pl.BlockSpec(memory_space=pltpu.VMEM)] * (rows // LANES),
-        out_shape=[jax.ShapeDtypeStruct((total, LANES), jnp.bfloat16)] * (rows // LANES),
+        out_specs=[pl.BlockSpec(memory_space=pltpu.VMEM)] * (2 * pieces),
+        out_shape=[jax.ShapeDtypeStruct((total, LANES), jnp.bfloat16)] * pieces
+        + [jax.ShapeDtypeStruct((total // 2, LANES), jnp.bfloat16)] * pieces,
         compiler_params=pltpu.CompilerParams(vmem_limit_bytes=12 << 20),
         name="select_rows",
     )(place, at_hand(slots), words, at_hand(gains))
+    return outs[:pieces], outs[pieces:]
 
 
 def swap(value, bit):
@@ -383,15 +394,13 @@
         out_ref[spot, :] = mine + other_ref[spot, :]
 
 
-def reduce_core(place, value):
-    size = value.shape[0] // 2
-    send = lax.dynamic_slice_in_dim(value, (1 - side(1)) * size, size, 0)
+def reduce_core(place, value, send):
     return pl.pallas_call(
         add_kernel,
         grid=(1,),
         in_specs=[pl.BlockSpec(memory_space=pltpu.SMEM)] + [pl.BlockSpec(memory_space=pltpu.VMEM)] * 2,
         out_specs=pl.BlockSpec(memory_space=pltpu.VMEM),
-        out_shape=jax.ShapeDtypeStruct((size, value.shape[1]), value.dtype),
+        out_shape=jax.ShapeDtypeStruct(send.shape, value.dtype),
         compiler_params=pltpu.CompilerParams(vmem_limit_bytes=4 << 20),
         name="add_halves",
     )(place, value, swap(send, 1))
@@ -578,8 +587,8 @@
     scales = gains.reshape(2 * ch, count)
     weights = jnp.asarray(filter_weights(ch))
     place = lax.axis_index("feed").reshape(1)
-    picked = select_rows(place, words, scales, feed_slot.reshape(-1, LANES), ROWS, total)
-    halves, firsts = zip(*[quarters(reduce_core(place, value)) for value in picked])
+    picked, sent = select_rows(place, words, scales, feed_slot.reshape(-1, LANES), ROWS, total)
+    halves, firsts = zip(*[quarters(reduce_core(place, *pair)) for pair in zip(picked, sent)])
     seconds = [eighths(first) for first in firsts]
     own, zero = own_spectra(words, scales.astype(jnp.float32), weights, ch, spectra, sum(seconds, ()))
     thirds = [cross(second) for second in seconds]

time: 201 us -> 207 us (1.030)
  Pallas kernels: 47 us -> 50.8 us
    pallas_call x1, Pallas kernels: 2.07 us -> 5.91 us  [select_rows(): pl.pallas_call(functools.partial(select_kernel, total // STEPS), grid=(1,...]
    ppermute x24, waiting for transfers between devices: 32.4 us -> 35 us  [swap(): return lax.ppermute(value, 'feed', pairs)]
    unnamed x22, local copies, waits for them, and re-layouts: 3.47 us -> 5.88 us
    dynamic_slice x2 -> x0, local copies, waits for them, and re-layouts: 2.26 us -> none  [reduce_core(): send = lax.dynamic_slice_in_dim(value, (1 - side(1)) * size, size, 0)]
where the time goes in v19:
time: 207 us; the launch traced here: 206 us
  waiting for transfers between devices  112 us (54%)
  Pallas kernels  50.8 us (25%)
  starting transfers between devices  33.5 us (16%)
  local copies, waits for them, and re-layouts  7.4 us (4%)
    all_to_all x2, waiting for transfers between devices, through_rows(): lax.all_to_all(coded, 'feed', split_axis=0, concat_axis=0, tiled=True)  77.5 us
    ppermute x24, waiting for transfers between devices, swap(): return lax.ppermute(value, 'feed', pairs)  35 us
    ppermute x24, starting transfers between devices, swap(): return lax.ppermute(value, 'feed', pairs)  20.3 us
    pallas_call x2, Pallas kernels, finish(): pl.pallas_call(functools.partial(finish_kernel, scale), grid=(columns //...  16.3 us
    all_to_all x2, starting transfers between devices, through_rows(): lax.all_to_all(coded, 'feed', split_axis=0, concat_axis=0, tiled=True)  13.2 us
    pallas_call x2, Pallas kernels, row_spectra(): pl.pallas_call(rows_kernel, grid=(1,), in_specs=[pl.BlockSpec(memory_spac...  9.41 us
    pallas_call x1, Pallas kernels, own_spectra(): pl.pallas_call(own_kernel, grid=(steps,), in_specs=[pl.BlockSpec((main, c...  9.05 us
    pallas_call x2, Pallas kernels, row_products(): pl.pallas_call(products_kernel, grid=(ch // each,), in_specs=[pl.BlockSpe...  8.23 us
  transfers between devices with their start and end apart: 26, of which 17 were waited for; matrix products, arithmetic and copies ran while one was open for 2% of the time, Pallas kernels for 14%

profile of v19, /device:TPU:13, one launch (start us, length us, event | category | flops | bytes accessed | tf_op | source)
XLA Modules:
  0.0 206.3 jit_solution(11290000658359804988)
XLA Ops:
  0.0 3.4 %copy-done = s32[256,16,519]{0,1,2:T(8,128)S(1)} copy-done((s32[256,16,519]{0,1,2:T(8,128)S(1)}, s32[256,16,519]{0,1,2:T(8,128)}, u32[]{:S(2)}) %copy-start) | copy-done | bytes 8503320
  3.4 5.9 %select_rows.1 = (bf16[8448,128]{1,0:T(8,128)(2,1)S(1)}, bf16[8448,128]{1,0:T(8,128)(2,1)S(1)}, bf16[4224,128]{1,0:T(8,128)(2,1)}, bf16[4224,128]{1,0:T(8,128)(2,1)}) custom-call(s32[1]{0:T(128)} %bitcast.3.place_ref, s32[32,128]{1,0:T(8,128)} %bitcast.19, s32[8304,256]{1,0:T(8,128)S(1)} %bitcast.13, s32[32,256]{1,0:T(8,128)} %bitcast.18), custom_call_target="tpu_custom_call" | custom-call | tf_op jit(solution)/shard_map/select_rows/pallas_call | solution.py:351
  9.3 1.3 copy-done.3
  10.7 0.7 collective-permute-start.5
  11.4 4.2 %collective-permute-done.5.other_ref = bf16[4224,128]{1,0:T(8,128)(2,1)} collective-permute-done((bf16[4224,128]{1,0:T(8,128)(2,1)}, bf16[4224,128]{1,0:T(8,128)(2,1)}, u32[]{:S(2)}, u32[]{:S(2)}) %collective-permute-start.5) | collective-permute-done | bytes 1081376 | tf_op jit(solution)/shard_map/ppermute | solution.py:371
  15.5 1.6 add_halves.3
  17.7 1.1 copy-done.4
  19.2 0.4 collective-permute-start.3
  19.7 1.3 collective-permute-start.1
  21.0 4.1 %collective-permute-done.8 = bf16[1056,128]{1,0:T(8,128)(2,1)S(1)} collective-permute-done((bf16[1056,128]{1,0:T(8,128)(2,1)S(1)}, bf16[1056,128]{1,0:T(8,128)(2,1)S(1)}, u32[]{:S(2)}, u32[]{:S(2)}) %collective-permute-start.8) | collective-permute-done | bytes 270368 | tf_op jit(solution)/shard_map/ppermute | solution.py:371
  25.2 0.3 collective-permute-start.9
  25.6 0.9 collective-permute-start.7
  26.5 4.3 %collective-permute-done.1 = bf16[1056,128]{1,0:T(8,128)(2,1)S(1)} collective-permute-done((bf16[1056,128]{1,0:T(8,128)(2,1)S(1)}, bf16[1056,128]{1,0:T(8,128)(2,1)S(1)}, u32[]{:S(2)}, u32[]{:S(2)}) %collective-permute-start.1) | collective-permute-done | bytes 270368 | tf_op jit(solution)/shard_map/ppermute | solution.py:371
  30.9 1.4 collective-permute-start.2
  32.7 3.1 %collective-permute-done.2 = bf16[528,128]{1,0:T(8,128)(2,1)S(1)} collective-permute-done((bf16[528,128]{1,0:T(8,128)(2,1)S(1)}, bf16[528,128]{1,0:T(8,128)(2,1)S(1)}, u32[]{:S(2)}, u32[]{:S(2)}) %collective-permute-start.2) | collective-permute-done | bytes 135200 | tf_op jit(solution)/shard_map/ppermute | solution.py:371
  35.8 2.4 %collective-permute-start.17 = (bf16[528,128]{1,0:T(8,128)(2,1)S(1)}, bf16[528,128]{1,0:T(8,128)(2,1)S(1)}, u32[]{:S(2)}, u32[]{:S(2)}) collective-permute-start(bf16[528,128]{1,0:T(8,128)(2,1)S(1)} %dynamic-slice_add_fusion.7.refs_0_), channel_id=1, source_target_pairs={{0,8},{1,9},{2,10},{3,11},{4,12},{5,13},{6,14},{7,15},{8,0},{9,1},... | collective-permute-start | bytes 405512 | tf_op jit(solution)/shard_map/ppermute | solution.py:371
  38.2 0.5 collective-permute-start.20
  38.8 2.0 collective-permute-start.10
  40.8 0.5 collective-permute-start.13
  41.3 9.1 %own_spectra.1 = (bf16[16,8,256,128]{3,2,1,0:T(8,128)(2,1)S(1)}, bf16[16,128]{1,0:T(8,128)(2,1)S(1)}) custom-call(s32[8304,256]{1,0:T(8,128)S(1)} %bitcast.16, s32[8304,256]{1,0:T(8,128)S(1)} %bitcast.17, f32[32,256]{1,0:T(8,128)S(1)} %bitcast_convert_fusion.gains_ref, bf16[256,256]{1,0:T(8,128)(2,1)S(1)} %copy-done.5, ...), custom_call_target="tpu_custom_call" | custom-call | flops 4294967296 | bytes 16891904 | tf_op jit(solution)/shard_map/own_spectra/pallas_call | solution.py:283
  50.4 0.5 slice.26
  50.9 1.6 collective-permute-done.17
  52.5 0.6 constant_dynamic-update-slice_fusion.9
  53.3 2.2 %collective-permute-done.20 = bf16[528,128]{1,0:T(8,128)(2,1)S(1)} collective-permute-done((bf16[528,128]{1,0:T(8,128)(2,1)S(1)}, bf16[528,128]{1,0:T(8,128)(2,1)S(1)}, u32[]{:S(2)}, u32[]{:S(2)}) %collective-permute-start.20) | collective-permute-done | bytes 135200 | tf_op jit(solution)/shard_map/ppermute | solution.py:371
  55.5 0.3 collective-permute-start.21
  55.8 2.6 %collective-permute-done.10 = bf16[528,128]{1,0:T(8,128)(2,1)S(1)} collective-permute-done((bf16[528,128]{1,0:T(8,128)(2,1)S(1)}, bf16[528,128]{1,0:T(8,128)(2,1)S(1)}, u32[]{:S(2)}, u32[]{:S(2)}) %collective-permute-start.10) | collective-permute-done | bytes 135200 | tf_op jit(solution)/shard_map/ppermute | solution.py:371
  58.5 0.6 collective-permute-start.11
  59.1 2.2 %collective-permute-done.13 = bf16[528,128]{1,0:T(8,128)(2,1)S(1)} collective-permute-done((bf16[528,128]{1,0:T(8,128)(2,1)S(1)}, bf16[528,128]{1,0:T(8,128)(2,1)S(1)}, u32[]{:S(2)}, u32[]{:S(2)}) %collective-permute-start.13) | collective-permute-done | bytes 135200 | tf_op jit(solution)/shard_map/ppermute | solution.py:371
  61.4 0.3 collective-permute-start.14
  61.6 2.3 %collective-permute-done.18 = bf16[528,128]{1,0:T(8,128)(2,1)S(1)} collective-permute-done((bf16[528,128]{1,0:T(8,128)(2,1)S(1)}, bf16[528,128]{1,0:T(8,128)(2,1)S(1)}, u32[]{:S(2)}, u32[]{:S(2)}) %collective-permute-start.18) | collective-permute-done | bytes 135200 | tf_op jit(solution)/shard_map/ppermute | solution.py:371
  64.3 2.3 %collective-permute-start.22 = (bf16[1056,128]{1,0:T(8,128)(2,1)S(1)}, bf16[1056,128]{1,0:T(8,128)(2,1)S(1)}, u32[]{:S(2)}, u32[]{:S(2)}) collective-permute-start(bf16[1056,128]{1,0:T(8,128)(2,1)S(1)} %constant_dynamic-update-slice_fusion.4), channel_id=1, source_target_pairs={{0,4},{1,5},{2,6},{3,7},{4,0},{5,1},{6,2},{7,3},{8,12},{9,13},{10,... | collective-permute-start | bytes 811016 | tf_op jit(solution)/shard_map/ppermute | solution.py:371
  66.8 1.1 collective-permute-start.12
  68.1 1.4 collective-permute-start.15
  69.5 2.9 %collective-permute-done.19 = bf16[1056,128]{1,0:T(8,128)(2,1)S(1)} collective-permute-done((bf16[1056,128]{1,0:T(8,128)(2,1)S(1)}, bf16[1056,128]{1,0:T(8,128)(2,1)S(1)}, u32[]{:S(2)}, u32[]{:S(2)}) %collective-permute-start.19) | collective-permute-done | bytes 270368 | tf_op jit(solution)/shard_map/ppermute | solution.py:371
  72.8 2.6 %collective-permute-start.23 = (bf16[4224,128]{1,0:T(8,128)(2,1)S(1)}, bf16[4224,128]{1,0:T(8,128)(2,1)S(1)}, u32[]{:S(2)}, u32[]{:S(2)}) collective-permute-start(bf16[4224,128]{1,0:T(8,128)(2,1)S(1)} %get-tuple-element.31), channel_id=1, source_target_pairs={{0,1},{1,0},{2,3},{3,2},{4,5},{5,4},{6,7},{7,6},{8,9},{9,8},{10,11... | collective-permute-start | bytes 3244040 | tf_op jit(solution)/shard_map/ppermute | solution.py:371
  75.4 2.9 %collective-permute-done.12 = bf16[1056,128]{1,0:T(8,128)(2,1)S(1)} collective-permute-done((bf16[1056,128]{1,0:T(8,128)(2,1)S(1)}, bf16[1056,128]{1,0:T(8,128)(2,1)S(1)}, u32[]{:S(2)}, u32[]{:S(2)}) %collective-permute-start.12) | collective-permute-done | bytes 270368 | tf_op jit(solution)/shard_map/ppermute | solution.py:371
  78.8 4.7 %row_spectra.3.left_ref = bf16[16,1024,256]{2,1,0:T(8,128)(2,1)S(1)} custom-call(bf16[8448,128]{1,0:T(8,128)(2,1)S(1)} %constant_dynamic-update-slice_fusion.words_ref, bf16[64,128]{1,0:T(8,128)(2,1)S(1)} %slice.33.parts_ref, bf16[256,256]{1,0:T(8,128)(2,1)S(1)} %copy-done.5), custom_call_target="tpu_custom_call" | custom-call | flops 2147483648 | bytes 10551296 | tf_op jit(solution)/shard_map/row_spectra/pallas_call | solution.py:459
  83.5 4.2 %row_products.2 = (s16[16,264,256]{2,1,0:T(8,128)(2,1)}, bf16[16,128]{1,0:T(8,128)(2,1)S(1)}) custom-call(bf16[16,8,256,128]{3,2,1,0:T(8,128)(2,1)S(1)} %get-tuple-element.18.own_ref, bf16[16,1024,256]{2,1,0:T(8,128)(2,1)S(1)} %row_spectra.3.left_ref, bf16[4224,128]{1,0:T(8,128)(2,1)S(1)} %get-tuple-element.33.refs_0_), custom_call_target="tpu_custom_call" | custom-call | flops 2147483648 | bytes 16777216 | tf_op jit(solution)/shard_map/row_products/pallas_call | solution.py:500
  87.7 8.1 %all-to-all-start.1 = ((s16[16,264,256]{2,1,0:T(8,128)(2,1)}), s16[16,264,256]{2,1,0:T(8,128)(2,1)}, u32[]{:S(2)}, u32[]{:S(2)}) async-start(s16[16,264,256]{2,1,0:T(8,128)(2,1)} %get-tuple-element.22), calls=%async_computation.1 | async-start | bytes 4325376 | tf_op jit(solution)/shard_map/all_to_all | solution.py:604
  95.8 0.4 collective-permute-start.16
  96.2 2.4 %collective-permute-done.16 = bf16[4224,128]{1,0:T(8,128)(2,1)S(1)} collective-permute-done((bf16[4224,128]{1,0:T(8,128)(2,1)S(1)}, bf16[4224,128]{1,0:T(8,128)(2,1)S(1)}, u32[]{:S(2)}, u32[]{:S(2)}) %collective-permute-start.16) | collective-permute-done | bytes 1081376 | tf_op jit(solution)/shard_map/ppermute | solution.py:371
  98.7 4.7 %row_spectra.2.left_ref = bf16[16,1024,256]{2,1,0:T(8,128)(2,1)S(1)} custom-call(bf16[8448,128]{1,0:T(8,128)(2,1)S(1)} %constant_dynamic-update-slice_fusion.10.words_ref, bf16[64,128]{1,0:T(8,128)(2,1)S(1)} %slice.32.parts_ref, bf16[256,256]{1,0:T(8,128)(2,1)S(1)} %copy-done.5), custom_call_target="tpu_custom_call" | custom-call | flops 2147483648 | bytes 10551296 | tf_op jit(solution)/shard_map/row_spectra/pallas_call | solution.py:459
  103.5 4.1 %row_products.3 = (s16[16,264,256]{2,1,0:T(8,128)(2,1)}, bf16[16,128]{1,0:T(8,128)(2,1)}) custom-call(bf16[16,8,256,128]{3,2,1,0:T(8,128)(2,1)S(1)} %copy-done.2, bf16[16,1024,256]{2,1,0:T(8,128)(2,1)S(1)} %row_spectra.2.left_ref, bf16[16,128]{1,0:T(8,128)(2,1)S(1)} %get-tuple-element.20.refs_0_), custom_call_target="tpu_custom_call" | custom-call | flops 2147483648 | bytes 16777216 | tf_op jit(solution)/shard_map/row_products/pallas_call | solution.py:500
  107.5 37.2 %all-to-all-done.1.coded_ref = s16[16,264,256]{2,1,0:T(8,128)(2,1)} async-done(((s16[16,264,256]{2,1,0:T(8,128)(2,1)}), s16[16,264,256]{2,1,0:T(8,128)(2,1)}, u32[]{:S(2)}, u32[]{:S(2)}) %all-to-all-start.1) | async-done | bytes 2162720 | tf_op jit(solution)/shard_map/all_to_all | solution.py:604
  144.8 5.0 %all-to-all-start = ((s16[16,264,256]{2,1,0:T(8,128)(2,1)}), s16[16,264,256]{2,1,0:T(8,128)(2,1)S(1)}, u32[]{:S(2)}, u32[]{:S(2)}) async-start(s16[16,264,256]{2,1,0:T(8,128)(2,1)} %get-tuple-element.21), calls=%async_computation | async-start | bytes 4325376 | tf_op jit(solution)/shard_map/all_to_all | solution.py:604
  149.8 8.6 %finish.2.refs_0_ = f32[256,64,128]{2,1,0:T(8,128)} custom-call(s32[4096]{0:T(1024)S(1)} %broadcast_multiply_fusion.slot_ref, s16[16,264,256]{2,1,0:T(8,128)(2,1)} %all-to-all-done.1.coded_ref), custom_call_target="tpu_custom_call" | custom-call | tf_op jit(solution)/shard_map/finish/pallas_call | solution.py:558
  158.4 40.2 %all-to-all-done.coded_ref = s16[16,264,256]{2,1,0:T(8,128)(2,1)S(1)} async-done(((s16[16,264,256]{2,1,0:T(8,128)(2,1)}), s16[16,264,256]{2,1,0:T(8,128)(2,1)S(1)}, u32[]{:S(2)}, u32[]{:S(2)}) %all-to-all-start) | async-done | bytes 2162720 | tf_op jit(solution)/shard_map/all_to_all | solution.py:604
  198.6 7.7 %finish.3 = f32[256,64,128]{2,1,0:T(8,128)} custom-call(s32[4096]{0:T(1024)S(1)} %broadcast_multiply_fusion.slot_ref, s16[16,264,256]{2,1,0:T(8,128)(2,1)S(1)} %all-to-all-done.coded_ref, f32[256,64,128]{2,1,0:T(8,128)} %finish.2.refs_0_), custom_call_target="tpu_custom_call", output_to_operand_aliasing={{}: (2, {})} | custom-call | tf_op jit(solution)/shard_map/finish/pallas_call | solution.py:558
  (80 shorter events, 3.8 us)
Async XLA Ops:
  0.0 3.4 %copy-start = (s32[256,16,519]{0,1,2:T(8,128)S(1)}, s32[256,16,519]{0,1,2:T(8,128)}, u32[]{:S(2)}) copy-start(s32[256,16,519]{0,1,2:T(8,128)} %param.4) | copy-start | bytes 25509892
  3.4 7.9 %copy-start.6 = (s32[2,16,256]{2,1,0:T(8,128)S(1)}, s32[2,16,256]{2,1,0:T(8,128)}, u32[]{:S(2)}) copy-start(s32[2,16,256]{2,1,0:T(8,128)} %param.5) | copy-start | bytes 98308
  3.4 37.9 %slice-start = ((s8[8503296]{0:T(1024)(128)(4,1)}), s8[114688]{0:T(1024)(128)(4,1)S(1)}, s32[]{:S(2)}) async-start(s8[8503296]{0:T(1024)(128)(4,1)} %bitcast.14), calls=%async_computation.2 | async-start | bytes 229376
  9.3 1.3 copy-start.3
  10.7 4.9 %collective-permute-start.5 = (bf16[4224,128]{1,0:T(8,128)(2,1)}, bf16[4224,128]{1,0:T(8,128)(2,1)}, u32[]{:S(2)}, u32[]{:S(2)}) collective-permute-start(bf16[4224,128]{1,0:T(8,128)(2,1)} %get-tuple-element.17), channel_id=1, source_target_pairs={{0,1},{1,0},{2,3},{3,2},{4,5},{5,4},{6,7},{7,6},{8,9},{9,8},{10,11... | collective-permute-start | bytes 3244040 | tf_op jit(solution)/shard_map/ppermute | solution.py:371
  11.3 6.4 %collective-permute-start = (bf16[4224,128]{1,0:T(8,128)(2,1)}, bf16[4224,128]{1,0:T(8,128)(2,1)S(1)}, u32[]{:S(2)}, u32[]{:S(2)}) collective-permute-start(bf16[4224,128]{1,0:T(8,128)(2,1)} %get-tuple-element.15), channel_id=1, source_target_pairs={{0,1},{1,0},{2,3},{3,2},{4,5},{5,4},{6,7},{7,6},{8,9},{9,8},{10,11... | collective-permute-start | bytes 3244040 | tf_op jit(solution)/shard_map/ppermute | solution.py:371
  15.5 25.8 %slice-start.1 = ((s8[8503296]{0:T(1024)(128)(4,1)}), s8[4194304]{0:T(1024)(128)(4,1)S(1)}, s32[]{:S(2)}) async-start(s8[8503296]{0:T(1024)(128)(4,1)} %bitcast.14), calls=%async_computation.3 | async-start | bytes 8388608
  17.2 1.6 copy-start.4
  17.3 7.8 %collective-permute-start.8 = (bf16[1056,128]{1,0:T(8,128)(2,1)S(1)}, bf16[1056,128]{1,0:T(8,128)(2,1)S(1)}, u32[]{:S(2)}, u32[]{:S(2)}) collective-permute-start(bf16[1056,128]{1,0:T(8,128)(2,1)S(1)} %constant_dynamic-slice_fusion.1), channel_id=1, source_target_pairs={{0,4},{1,5},{2,6},{3,7},{4,0},{5,1},{6,2},{7,3},{8,12},{9,13},{10,... | collective-permute-start | bytes 811016 | tf_op jit(solution)/shard_map/ppermute | solution.py:371
  17.6 7.9 %collective-permute-start.6 = (bf16[1056,128]{1,0:T(8,128)(2,1)S(1)}, bf16[1056,128]{1,0:T(8,128)(2,1)S(1)}, u32[]{:S(2)}, u32[]{:S(2)}) collective-permute-start(bf16[1056,128]{1,0:T(8,128)(2,1)S(1)} %constant_dynamic-slice_fusion.3), channel_id=1, source_target_pairs={{0,2},{1,3},{2,0},{3,1},{4,6},{5,7},{6,4},{7,5},{8,10},{9,11},{10,... | collective-permute-start | bytes 811016 | tf_op jit(solution)/shard_map/ppermute | solution.py:371
  18.8 22.5 %slice-start.2 = ((s8[8503296]{0:T(1024)(128)(4,1)}), s8[4194304]{0:T(1024)(128)(4,1)S(1)}, s32[]{:S(2)}) async-start(s8[8503296]{0:T(1024)(128)(4,1)} %bitcast.14), calls=%async_computation.4 | async-start | bytes 8388608
  19.2 13.1 %collective-permute-start.3 = (bf16[1056,128]{1,0:T(8,128)(2,1)S(1)}, bf16[1056,128]{1,0:T(8,128)(2,1)S(1)}, u32[]{:S(2)}, u32[]{:S(2)}) collective-permute-start(bf16[1056,128]{1,0:T(8,128)(2,1)S(1)} %constant_dynamic-slice_fusion.5), channel_id=1, source_target_pairs={{0,4},{1,5},{2,6},{3,7},{4,0},{5,1},{6,2},{7,3},{8,12},{9,13},{10,... | collective-permute-start | bytes 811016 | tf_op jit(solution)/shard_map/ppermute | solution.py:371
  19.7 11.2 %collective-permute-start.1 = (bf16[1056,128]{1,0:T(8,128)(2,1)S(1)}, bf16[1056,128]{1,0:T(8,128)(2,1)S(1)}, u32[]{:S(2)}, u32[]{:S(2)}) collective-permute-start(bf16[1056,128]{1,0:T(8,128)(2,1)S(1)} %constant_dynamic-slice_fusion.7), channel_id=1, source_target_pairs={{0,2},{1,3},{2,0},{3,1},{4,6},{5,7},{6,4},{7,5},{8,10},{9,11},{10,... | collective-permute-start | bytes 811016 | tf_op jit(solution)/shard_map/ppermute | solution.py:371
  25.2 15.5 %collective-permute-start.9 = (bf16[528,128]{1,0:T(8,128)(2,1)S(1)}, bf16[528,128]{1,0:T(8,128)(2,1)S(1)}, u32[]{:S(2)}, u32[]{:S(2)}) collective-permute-start(bf16[528,128]{1,0:T(8,128)(2,1)S(1)} %constant_dynamic-slice_fusion), channel_id=1, source_target_pairs={{0,2},{1,3},{2,0},{3,1},{4,6},{5,7},{6,4},{7,5},{8,10},{9,11},{10,... | collective-permute-start | bytes 405512 | tf_op jit(solution)/shard_map/ppermute | solution.py:371
  25.6 15.8 %copy-start.5 = (bf16[256,256]{1,0:T(8,128)(2,1)S(1)}, bf16[256,256]{1,0:T(8,128)(2,1)}, u32[]{:S(2)}) copy-start(bf16[256,256]{1,0:T(8,128)(2,1)} %constant.201.clone.weights_ref) | copy-start | bytes 393220
  25.6 13.1 %collective-permute-start.7 = (bf16[528,128]{1,0:T(8,128)(2,1)S(1)}, bf16[528,128]{1,0:T(8,128)(2,1)S(1)}, u32[]{:S(2)}, u32[]{:S(2)}) collective-permute-start(bf16[528,128]{1,0:T(8,128)(2,1)S(1)} %constant_dynamic-slice_fusion.2), channel_id=1, source_target_pairs={{0,4},{1,5},{2,6},{3,7},{4,0},{5,1},{6,2},{7,3},{8,12},{9,13},{10,... | collective-permute-start | bytes 405512 | tf_op jit(solution)/shard_map/ppermute | solution.py:371
  30.9 4.8 %collective-permute-start.2 = (bf16[528,128]{1,0:T(8,128)(2,1)S(1)}, bf16[528,128]{1,0:T(8,128)(2,1)S(1)}, u32[]{:S(2)}, u32[]{:S(2)}) collective-permute-start(bf16[528,128]{1,0:T(8,128)(2,1)S(1)} %constant_dynamic-slice_fusion.6), channel_id=1, source_target_pairs={{0,4},{1,5},{2,6},{3,7},{4,0},{5,1},{6,2},{7,3},{8,12},{9,13},{10,... | collective-permute-start | bytes 405512 | tf_op jit(solution)/shard_map/ppermute | solution.py:371
  32.4 5.8 %collective-permute-start.4 = (bf16[528,128]{1,0:T(8,128)(2,1)S(1)}, bf16[528,128]{1,0:T(8,128)(2,1)S(1)}, u32[]{:S(2)}, u32[]{:S(2)}) collective-permute-start(bf16[528,128]{1,0:T(8,128)(2,1)S(1)} %constant_dynamic-slice_fusion.4), channel_id=1, source_target_pairs={{0,2},{1,3},{2,0},{3,1},{4,6},{5,7},{6,4},{7,5},{8,10},{9,11},{10,... | collective-permute-start | bytes 405512 | tf_op jit(solution)/shard_map/ppermute | solution.py:371
  35.8 16.8 %collective-permute-start.17 = (bf16[528,128]{1,0:T(8,128)(2,1)S(1)}, bf16[528,128]{1,0:T(8,128)(2,1)S(1)}, u32[]{:S(2)}, u32[]{:S(2)}) collective-permute-start(bf16[528,128]{1,0:T(8,128)(2,1)S(1)} %dynamic-slice_add_fusion.7.refs_0_), channel_id=1, source_target_pairs={{0,8},{1,9},{2,10},{3,11},{4,12},{5,13},{6,14},{7,15},{8,0},{9,1},... | collective-permute-start | bytes 405512 | tf_op jit(solution)/shard_map/ppermute | solution.py:371
  38.2 17.3 %collective-permute-start.20 = (bf16[528,128]{1,0:T(8,128)(2,1)S(1)}, bf16[528,128]{1,0:T(8,128)(2,1)S(1)}, u32[]{:S(2)}, u32[]{:S(2)}) collective-permute-start(bf16[528,128]{1,0:T(8,128)(2,1)S(1)} %dynamic-slice_add_fusion.6.refs_1_), channel_id=1, source_target_pairs={{0,8},{1,9},{2,10},{3,11},{4,12},{5,13},{6,14},{7,15},{8,0},{9,1},... | collective-permute-start | bytes 405512 | tf_op jit(solution)/shard_map/ppermute | solution.py:371
  38.8 19.6 %collective-permute-start.10 = (bf16[528,128]{1,0:T(8,128)(2,1)S(1)}, bf16[528,128]{1,0:T(8,128)(2,1)S(1)}, u32[]{:S(2)}, u32[]{:S(2)}) collective-permute-start(bf16[528,128]{1,0:T(8,128)(2,1)S(1)} %dynamic-slice_add_fusion.5.refs_2_), channel_id=1, source_target_pairs={{0,8},{1,9},{2,10},{3,11},{4,12},{5,13},{6,14},{7,15},{8,0},{9,1},... | collective-permute-start | bytes 405512 | tf_op jit(solution)/shard_map/ppermute | solution.py:371
  40.8 20.5 %collective-permute-start.13 = (bf16[528,128]{1,0:T(8,128)(2,1)S(1)}, bf16[528,128]{1,0:T(8,128)(2,1)S(1)}, u32[]{:S(2)}, u32[]{:S(2)}) collective-permute-start(bf16[528,128]{1,0:T(8,128)(2,1)S(1)} %dynamic-slice_add_fusion.4.refs_3_), channel_id=1, source_target_pairs={{0,8},{1,9},{2,10},{3,11},{4,12},{5,13},{6,14},{7,15},{8,0},{9,1},... | collective-permute-start | bytes 405512 | tf_op jit(solution)/shard_map/ppermute | solution.py:371
  50.4 33.1 %copy-start.1 = (bf16[16,8,256,128]{3,2,1,0:T(8,128)(2,1)}, bf16[16,8,256,128]{3,2,1,0:T(8,128)(2,1)S(1)}, u32[]{:S(2)}) copy-start(bf16[16,8,256,128]{3,2,1,0:T(8,128)(2,1)S(1)} %get-tuple-element.18.own_ref) | copy-start | bytes 25165828
  53.2 10.7 %collective-permute-start.18 = (bf16[528,128]{1,0:T(8,128)(2,1)S(1)}, bf16[528,128]{1,0:T(8,128)(2,1)S(1)}, u32[]{:S(2)}, u32[]{:S(2)}) collective-permute-start(bf16[528,128]{1,0:T(8,128)(2,1)S(1)} %get-tuple-element.24), channel_id=1, source_target_pairs={{0,4},{1,5},{2,6},{3,7},{4,0},{5,1},{6,2},{7,3},{8,12},{9,13},{10,... | collective-permute-start | bytes 405512 | tf_op jit(solution)/shard_map/ppermute | solution.py:371
  55.5 8.8 %collective-permute-start.21 = (bf16[528,128]{1,0:T(8,128)(2,1)S(1)}, bf16[528,128]{1,0:T(8,128)(2,1)S(1)}, u32[]{:S(2)}, u32[]{:S(2)}) collective-permute-start(bf16[528,128]{1,0:T(8,128)(2,1)S(1)} %get-tuple-element.26), channel_id=1, source_target_pairs={{0,2},{1,3},{2,0},{3,1},{4,6},{5,7},{6,4},{7,5},{8,10},{9,11},{10,... | collective-permute-start | bytes 405512 | tf_op jit(solution)/shard_map/ppermute | solution.py:371
  58.5 8.4 %collective-permute-start.11 = (bf16[528,128]{1,0:T(8,128)(2,1)S(1)}, bf16[528,128]{1,0:T(8,128)(2,1)S(1)}, u32[]{:S(2)}, u32[]{:S(2)}) collective-permute-start(bf16[528,128]{1,0:T(8,128)(2,1)S(1)} %get-tuple-element.28), channel_id=1, source_target_pairs={{0,4},{1,5},{2,6},{3,7},{4,0},{5,1},{6,2},{7,3},{8,12},{9,13},{10,... | collective-permute-start | bytes 405512 | tf_op jit(solution)/shard_map/ppermute | solution.py:371
  61.4 6.7 %collective-permute-start.14 = (bf16[528,128]{1,0:T(8,128)(2,1)S(1)}, bf16[528,128]{1,0:T(8,128)(2,1)S(1)}, u32[]{:S(2)}, u32[]{:S(2)}) collective-permute-start(bf16[528,128]{1,0:T(8,128)(2,1)S(1)} %get-tuple-element.30), channel_id=1, source_target_pairs={{0,2},{1,3},{2,0},{3,1},{4,6},{5,7},{6,4},{7,5},{8,10},{9,11},{10,... | collective-permute-start | bytes 405512 | tf_op jit(solution)/shard_map/ppermute | solution.py:371
  63.9 8.5 %collective-permute-start.19 = (bf16[1056,128]{1,0:T(8,128)(2,1)S(1)}, bf16[1056,128]{1,0:T(8,128)(2,1)S(1)}, u32[]{:S(2)}, u32[]{:S(2)}) collective-permute-start(bf16[1056,128]{1,0:T(8,128)(2,1)S(1)} %constant_dynamic-update-slice_fusion.8), channel_id=1, source_target_pairs={{0,2},{1,3},{2,0},{3,1},{4,6},{5,7},{6,4},{7,5},{8,10},{9,11},{10,... | collective-permute-start | bytes 811016 | tf_op jit(solution)/shard_map/ppermute | solution.py:371
  64.3 8.3 %collective-permute-start.22 = (bf16[1056,128]{1,0:T(8,128)(2,1)S(1)}, bf16[1056,128]{1,0:T(8,128)(2,1)S(1)}, u32[]{:S(2)}, u32[]{:S(2)}) collective-permute-start(bf16[1056,128]{1,0:T(8,128)(2,1)S(1)} %constant_dynamic-update-slice_fusion.4), channel_id=1, source_target_pairs={{0,4},{1,5},{2,6},{3,7},{4,0},{5,1},{6,2},{7,3},{8,12},{9,13},{10,... | collective-permute-start | bytes 811016 | tf_op jit(solution)/shard_map/ppermute | solution.py:371
  66.8 11.4 %collective-permute-start.12 = (bf16[1056,128]{1,0:T(8,128)(2,1)S(1)}, bf16[1056,128]{1,0:T(8,128)(2,1)S(1)}, u32[]{:S(2)}, u32[]{:S(2)}) collective-permute-start(bf16[1056,128]{1,0:T(8,128)(2,1)S(1)} %constant_dynamic-update-slice_fusion.18), channel_id=1, source_target_pairs={{0,2},{1,3},{2,0},{3,1},{4,6},{5,7},{6,4},{7,5},{8,10},{9,11},{10,... | collective-permute-start | bytes 811016 | tf_op jit(solution)/shard_map/ppermute | solution.py:371
  68.1 10.3 %collective-permute-start.15 = (bf16[1056,128]{1,0:T(8,128)(2,1)S(1)}, bf16[1056,128]{1,0:T(8,128)(2,1)S(1)}, u32[]{:S(2)}, u32[]{:S(2)}) collective-permute-start(bf16[1056,128]{1,0:T(8,128)(2,1)S(1)} %constant_dynamic-update-slice_fusion.14), channel_id=1, source_target_pairs={{0,4},{1,5},{2,6},{3,7},{4,0},{5,1},{6,2},{7,3},{8,12},{9,13},{10,... | collective-permute-start | bytes 811016 | tf_op jit(solution)/shard_map/ppermute | solution.py:371
  72.8 5.8 %collective-permute-start.23 = (bf16[4224,128]{1,0:T(8,128)(2,1)S(1)}, bf16[4224,128]{1,0:T(8,128)(2,1)S(1)}, u32[]{:S(2)}, u32[]{:S(2)}) collective-permute-start(bf16[4224,128]{1,0:T(8,128)(2,1)S(1)} %get-tuple-element.31), channel_id=1, source_target_pairs={{0,1},{1,0},{2,3},{3,2},{4,5},{5,4},{6,7},{7,6},{8,9},{9,8},{10,11... | collective-permute-start | bytes 3244040 | tf_op jit(solution)/shard_map/ppermute | solution.py:371
  87.7 57.1 %all-to-all-start.1 = ((s16[16,264,256]{2,1,0:T(8,128)(2,1)}), s16[16,264,256]{2,1,0:T(8,128)(2,1)}, u32[]{:S(2)}, u32[]{:S(2)}) async-start(s16[16,264,256]{2,1,0:T(8,128)(2,1)} %get-tuple-element.22), calls=%async_computation.1 | async-start | bytes 4325376 | tf_op jit(solution)/shard_map/all_to_all | solution.py:604
  95.8 2.7 %collective-permute-start.16 = (bf16[4224,128]{1,0:T(8,128)(2,1)S(1)}, bf16[4224,128]{1,0:T(8,128)(2,1)S(1)}, u32[]{:S(2)}, u32[]{:S(2)}) collective-permute-start(bf16[4224,128]{1,0:T(8,128)(2,1)S(1)} %get-tuple-element.33.refs_0_), channel_id=1, source_target_pairs={{0,1},{1,0},{2,3},{3,2},{4,5},{5,4},{6,7},{7,6},{8,9},{9,8},{10,11... | collective-permute-start | bytes 3244040 | tf_op jit(solution)/shard_map/ppermute | solution.py:371
  98.7 4.7 %copy-start.2 = (bf16[16,8,256,128]{3,2,1,0:T(8,128)(2,1)S(1)}, bf16[16,8,256,128]{3,2,1,0:T(8,128)(2,1)}, u32[]{:S(2)}) copy-start(bf16[16,8,256,128]{3,2,1,0:T(8,128)(2,1)} %copy-done.1) | copy-start | bytes 25165828
  144.8 5.0 %copy-start.7 = (s32[4096]{0:T(1024)S(1)}, s32[4096]{0:T(1024)}, u32[]{:S(2)}) copy-start(s32[4096]{0:T(1024)} %param.6) | copy-start | bytes 49156
  144.8 53.9 %all-to-all-start = ((s16[16,264,256]{2,1,0:T(8,128)(2,1)}), s16[16,264,256]{2,1,0:T(8,128)(2,1)S(1)}, u32[]{:S(2)}, u32[]{:S(2)}) async-start(s16[16,264,256]{2,1,0:T(8,128)(2,1)} %get-tuple-element.21), calls=%async_computation | async-start | bytes 4325376 | tf_op jit(solution)/shard_map/all_to_all | solution.py:604
